TPU v7x, 32 devices: a whole 2x2x4 slice. The times are simulated.
32 devices in a mesh: grp: 2 (over y), wide: 8 (over z, x), narrow: 2 (over core).
Axes of the slice: x: 2, y: 2, z: 4, core: 2. Of those that a mesh axis runs over, the one named last changes fastest.
Arguments:
- inputs: bfloat16 [1024, 28672], P(('grp', 'wide'), 'narrow'), parts along dimension 0, may hold values from -6 to 6
- deltas: bfloat16 [1024, 8192], P('grp', 'wide'), parts along dimension 0, may hold values from -0.375 to 0.375
- basis_in: bfloat16 [57344, 14336], P(('grp', 'narrow'), 'wide'), parts along dimension 0, may hold values from -0.03125 to 0.03125
- basis_out: bfloat16 [16384, 4096], P(('grp', 'wide'), 'narrow'), parts along dimension 0, may hold values from -0.0625 to 0.0625
Outputs:
- corrections: float32 [28672, 4096], P(('grp', 'wide'), 'narrow'), parts along dimension 0
There are 2 independent parts, one for each index of `grp`. A program takes and returns all parts, laid end to end along the dimension named above; each array names one. Nothing has to cross between parts.
All inputs are finite; a program needn't handle non-finite values.
Results may differ from a plain program's by a relative error of at most 0.0041.
Values may be sent and summed in bfloat16 or wider, within the bound.
No kernel may reach another device: no remote copies, remote signals or barrier semaphores. Data moves between devices by JAX's collectives and lax.ppermute only.
A program may use at most 192 MiB of HBM per device.

v0:
```python
import jax
import jax.numpy as jnp
from jax import lax
from jax.sharding import PartitionSpec as P

EX = 2
SEQ = 256


def local(inputs, deltas, basis_in, basis_out):
    partial_in = jnp.dot(
        lax.all_gather(inputs, "wide", axis=0, tiled=True),
        basis_in,
        preferred_element_type=jnp.float32,
    )
    rotated_in = lax.psum(partial_in, "narrow").astype(jnp.bfloat16)
    partial_out = jnp.dot(deltas, basis_out, preferred_element_type=jnp.float32)
    rotated_out = lax.psum(partial_out, "wide").astype(jnp.bfloat16)
    blocks_in = rotated_in.reshape(EX, SEQ, rotated_in.shape[1])
    blocks_out = rotated_out.reshape(EX, SEQ, rotated_out.shape[1])
    grads = jnp.einsum("eta,ets->eas", blocks_in, blocks_out, preferred_element_type=jnp.float32)
    return jnp.sum(grads * grads, axis=0) / EX


def solution(mesh):
    return jax.shard_map(
        local,
        mesh=mesh,
        in_specs=(
            P(("grp", "wide"), "narrow"),
            P("grp", "wide"),
            P(("grp", "narrow"), "wide"),
            P(("grp", "wide"), "narrow"),
        ),
        out_specs=P(("grp", "wide"), "narrow"),
        check_vma=False,
    )
```

profile of v0, /device:TPU:0, one launch (start us, length us, event | category | flops | bytes accessed | tf_op | source)
XLA Modules:
  0.0 411.8 jit_solution(16737871436244678951)
XLA Ops:
  6.5 0.0 copy-start
  6.5 0.0 all-gather.2.cloned.1.call-start
  6.5 0.7 all-gather.2.cloned.1.call-update
  7.3 0.5 copy-done
  7.8 6.5 %fusion.1 = f32[512,2048]{1,0:T(8,128)} fusion(bf16[512,1024]{1,0:T(8,128)(2,1)S(1)} %copy-done, bf16[1024,2048]{1,0:T(8,128)(2,1)} %param.7), kind=kOutput, calls=%fused_computation.3 | convolution fusion | flops 2147483648 | bytes 9437184 | tf_op jit(solution)/shard_map/dot_general | solution.py:17
  14.3 228.2 %all-reduce.3 = bf16[512,2048]{1,0:T(8,128)(2,1)S(1)} all-reduce(f32[512,2048]{1,0:T(8,128)} %fusion.1), channel_id=1, replica_groups=mesh['grp'=2,'wide'=8,'narrow'=2] {'wide'}, use_global_device_ids=true, to_apply=%region_1.0 | all-reduce | flops 1048576 | bytes 6291456 | tf_op jit(solution)/shard_map/psum | solution.py:18
  242.5 87.1 %all-gather.2.cloned.1.call-done = bf16[512,14336]{1,0:T(8,128)(2,1)} async-done(((bf16[64,14336]{1,0:T(8,128)(2,1)}), bf16[512,14336]{1,0:T(8,128)(2,1)}) %all-gather.2.cloned.1.call-update) | async-done | bytes 14680080 | tf_op jit(solution)/shard_map/all_gather | solution.py:12
  329.6 34.8 %fusion = f32[512,1792]{1,0:T(8,128)} fusion(bf16[512,14336]{1,0:T(8,128)(2,1)} %all-gather.2.cloned.1.call-done, bf16[14336,1792]{1,0:T(8,128)(2,1)} %param.6), kind=kOutput, calls=%fused_computation.2 | convolution fusion | flops 26306674688 | bytes 69730304 | tf_op jit(solution)/shard_map/dot_general | solution.py:11
  364.4 13.8 %all-reduce.2 = bf16[512,1792]{1,0:T(8,128)(2,1)} all-reduce(f32[512,1792]{1,0:T(8,128)} %fusion), channel_id=1, replica_groups=mesh['grp'=2,'wide'=8,'narrow'=2] {'narrow'}, use_global_device_ids=true, to_apply=%region_0.0 | all-reduce | flops 917504 | bytes 5505024 | tf_op jit(solution)/shard_map/psum | solution.py:16
  378.1 12.8 %multiply_reduce_fusion = f32[1792,2048]{1,0:T(8,128)} fusion(bf16[2,256,1792]{2,1,0:T(8,128)(2,1)} %bitcast.9, bf16[2,256,2048]{2,1,0:T(8,128)(2,1)S(1)} %bitcast.8), kind=kOutput, calls=%fused_computation | convolution fusion | flops 3769106432 | bytes 18612224 | tf_op jit(solution)/shard_map/eta,ets->eas/dot_general | solution.py:21
  390.9 0.0 copy-start.1
  390.9 14.0 %broadcast_multiply_fusion = f32[1792,2048]{1,0:T(8,128)} fusion(f32[1792,2048]{1,0:T(8,128)} %multiply_reduce_fusion), kind=kLoop, calls=%fused_computation.1 | loop fusion | flops 3670016 | bytes 29360128 | tf_op jit(solution)/shard_map/div | solution.py:22
  404.9 0.0 copy-done.1
Async XLA Ops:
  6.5 1.2 copy-start
  6.5 323.0 %all-gather.2.cloned.1.call-start = ((), (), s32[]{:S(2)}) async-start(), calls=%async_computation | async-start | bytes 16515072 | tf_op jit(solution)/shard_map/all_gather | solution.py:12
  390.9 14.0 %copy-start.1 = (bf16[512,1024]{1,0:T(8,128)(2,1)S(1)}, bf16[512,1024]{1,0:T(8,128)(2,1)}, u32[]{:S(2)}) copy-start(bf16[512,1024]{1,0:T(8,128)(2,1)} %param.5) | copy-start | bytes 3145732
Sparse Core Ops, SparseCore 0:
  9.5 319.9 all-gather.1
where the time goes:
time: 412 us
  blocking collectives  242 us (59%)
  waiting for transfers between devices  87.8 us (21%)
  matrix products  54.1 us (13%)
  other arithmetic  14 us (3%)
  between operations  13.4 us (3%)
    psum x1, blocking collectives, local(): rotated_out = lax.psum(partial_out, 'wide').astype(jnp.bfloat16)  228 us
    all_gather x1, waiting for transfers between devices, local(): lax.all_gather(inputs, 'wide', axis=0, tiled=True)  87.1 us
    dot_general x1, matrix products, local(): jnp.dot(lax.all_gather(inputs, 'wide', axis=0, tiled=True), basis_in, pre...  34.8 us
    div x1, other arithmetic, local(): return jnp.sum(grads * grads, axis=0) / EX  14 us
    psum x1, blocking collectives, local(): rotated_in = lax.psum(partial_in, 'narrow').astype(jnp.bfloat16)  13.8 us
    dot_general x1, matrix products, local(): jnp.einsum('eta,ets->eas', blocks_in, blocks_out, preferred_element_type=...  12.8 us
  transfers between devices with their start and end apart: 1, of which 1 were waited for; matrix products, arithmetic and copies ran while one was open for 2% of the time, Pallas kernels for 0%

commit v1 on v0

v1 whole, which is shorter than its diff:
```python
import functools

import jax
import jax.numpy as jnp
from jax import lax
from jax.experimental import pallas as pl
from jax.experimental.pallas import tpu as pltpu
from jax.sharding import PartitionSpec as P

EX = 2
LINE, PAIR = 4, 2
BF16, F32 = jnp.bfloat16, jnp.float32


def dot(a, b):
    return jnp.dot(a, b, preferred_element_type=F32)


def fit_kernel(order_ref, mine_ref, other_ref, out_ref, fit_ref, rot_ref):
    rows, blocks = mine_ref.shape[0], order_ref.shape[0]
    size, seq = rows // blocks, rows // EX
    for slot in range(blocks):
        here = pl.ds(slot * size, size)
        there = pl.ds(pl.multiple_of(order_ref[slot] * size, size), size)
        rot_ref[there, :] = mine_ref[here, :] + other_ref[here, :]
    total = None
    for e in range(EX):
        here = pl.ds(e * seq, seq)
        grad = lax.dot_general(
            rot_ref[here, :].astype(BF16),
            out_ref[here, :],
            (((0,), (0,)), ((), ())),
            preferred_element_type=F32,
        )
        total = grad * grad if total is None else total + grad * grad
    fit_ref[...] = total * (1.0 / EX)


def fit(order, mine, other, rotated_out):
    rows, ka = mine.shape
    ks = rotated_out.shape[1]
    tile = 256 if ka % 256 == 0 else ka
    return pl.pallas_call(
        fit_kernel,
        out_shape=jax.ShapeDtypeStruct((ka, ks), F32),
        grid_spec=pltpu.PrefetchScalarGridSpec(
            num_scalar_prefetch=1,
            grid=(ka // tile,),
            in_specs=[
                pl.BlockSpec((rows, tile), lambda i, o: (0, i)),
                pl.BlockSpec((rows, tile), lambda i, o: (0, i)),
                pl.BlockSpec((rows, ks), lambda i, o: (0, 0)),
            ],
            out_specs=pl.BlockSpec((tile, ks), lambda i, o: (i, 0)),
            scratch_shapes=[pltpu.VMEM((rows, tile), F32)],
        ),
        compiler_params=pltpu.CompilerParams(vmem_limit_bytes=48 << 20),
        cost_estimate=pl.CostEstimate(
            flops=2 * rows * ka * ks,
            bytes_accessed=8 * rows * ka + 2 * rows * ks + 4 * ka * ks,
            transcendentals=0,
        ),
        name="fit",
    )(order, mine, other, rotated_out)


def swap_narrow(a):
    return lax.ppermute(a, "narrow", [(0, 1), (1, 0)])


def general(wide, inputs, deltas, basis_in, basis_out):
    partial_in = dot(lax.all_gather(inputs, "wide", axis=0, tiled=True), basis_in)
    rotated_out = lax.psum(dot(deltas, basis_out), "wide").astype(BF16)
    order = jnp.arange(EX, dtype=jnp.int32)
    return fit(order, partial_in, swap_narrow(partial_in), rotated_out)


def pairs(step, where=lambda z: True):
    out = []
    for z in range(LINE):
        for x in range(PAIR):
            if where(z):
                tz, tx = step(z, x)
                out.append((z * PAIR + x, tz * PAIR + tx))
    return out


def corner(z):
    return z in (0, LINE - 1)


ENDS = pairs(lambda z, x: (z ^ 1, x))
TO_ENDS = pairs(lambda z, x: (z ^ 1, x), lambda z: not corner(z))
MIDDLE = pairs(lambda z, x: (3 - z, x), lambda z: not corner(z))
ACROSS = pairs(lambda z, x: (z, 1 - x))
ACROSS_ENDS = pairs(lambda z, x: (z, 1 - x), corner)


def gather(block, at_end):
    send = lambda a, perm: lax.ppermute(a, "wide", perm)
    pick = lambda a, b: jnp.where(at_end, a, b)
    a1 = send(block, ENDS)
    x1 = send(block, ACROSS)
    m1 = send(block, MIDDLE)
    m2 = send(a1, MIDDLE)
    a2 = send(pick(x1, m1), ENDS)
    x2 = send(pick(a1, m1), ACROSS)
    a3 = send(m2, TO_ENDS)
    x3 = send(pick(a2, m2), ACROSS)
    x4 = send(a3, ACROSS_ENDS)
    return jnp.concatenate(
        [block, a1, pick(a2, m1), pick(a3, m2), x1, pick(x2, a2), pick(x3, x2), pick(x4, x3)], axis=0
    )


def slots(w):
    z, x = w // PAIR, w % PAIR
    flip = jnp.where(z >= 2, 3, 0)
    end = (z == 0) | (z == LINE - 1)
    mine = [jnp.where(end, a, b) ^ flip for a, b in ((0, 1), (1, 0), (2, 2), (3, 3))]
    return jnp.stack([q * PAIR + x for q in mine] + [q * PAIR + 1 - x for q in mine]).astype(jnp.int32)


def scheduled(inputs, deltas, basis_in, basis_out):
    w = lax.axis_index("wide")
    z = w // PAIR
    at_end = (z == 0) | (z == LINE - 1)
    deep = inputs.shape[1]
    chunks = 4
    width = deep // chunks

    partial_out = dot(deltas, basis_out)
    mine_out = lax.psum_scatter(partial_out, "wide", scatter_dimension=0, tiled=True).astype(BF16)
    rotated_out = lax.all_gather(mine_out, "wide", axis=0, tiled=True)

    total = None
    for c in range(chunks):
        here = slice(c * width, (c + 1) * width)
        term = dot(gather(inputs[:, here], at_end), basis_in[here])
        total = term if total is None else total + term
    return fit(slots(w), total, swap_narrow(total), rotated_out)


def solution(mesh):
    wide = mesh.shape["wide"]
    local = scheduled if wide == LINE * PAIR else functools.partial(general, wide)
    return jax.shard_map(
        local,
        mesh=mesh,
        in_specs=(
            P(("grp", "wide"), "narrow"),
            P("grp", "wide"),
            P(("grp", "narrow"), "wide"),
            P(("grp", "wide"), "narrow"),
        ),
        out_specs=P(("grp", "wide"), "narrow"),
        check_vma=False,
    )
```

time: 412 us -> 389 us (0.944)
  blocking collectives: 242 us -> 0 us
  waiting for transfers between devices: 87.8 us -> 214 us
  starting transfers between devices: 0.01 us -> 83.3 us
  Pallas kernels: 0 us -> 12.4 us
  other arithmetic: 14 us -> 5.52 us
  local copies, waits for them, and re-layouts: 0.51 us -> 6.95 us
    psum x2 -> x0, blocking collectives: 242 us -> none  [the longest x1 228 us: local(): rotated_out = lax.psum(partial_out, 'wide').astype(jnp.bfloat16)]
    ppermute x0 -> x37, waiting for transfers between devices: none -> 170 us  [the longest x36 165 us: gather(): send = lambda a, perm: lax.ppermute(a, 'wide', perm)]
    ppermute x0 -> x37, starting transfers between devices: none -> 83.2 us  [the longest x36 83.2 us: gather(): send = lambda a, perm: lax.ppermute(a, 'wide', perm)]
    all_gather x1, waiting for transfers between devices: 87.1 us -> 44.1 us  [scheduled(): rotated_out = lax.all_gather(mine_out, 'wide', axis=0, tiled=True)]
    div x1 -> x0, other arithmetic: 14 us -> none  [local(): return jnp.sum(grads * grads, axis=0) / EX]
    pallas_call x0 -> x1, Pallas kernels: none -> 12.4 us  [fit(): pl.pallas_call(fit_kernel, out_shape=jax.ShapeDtypeStruct((ka, ks), F32),...]
    dot_general x3 -> x5, matrix products: 54.1 us -> 51.9 us  [dot(): return jnp.dot(a, b, preferred_element_type=F32)]
  transfers between devices with their start and end apart: 1 -> 39, of which waited for: 1 -> 18; matrix products, arithmetic and copies ran while one was open for 2% -> 15% of each run, Pallas kernels for 0% -> 0%
where the time goes in v1:
time: 389 us; the launch traced here: 388 us
  waiting for transfers between devices  214 us (55%)
  starting transfers between devices  83.3 us (21%)
  matrix products  51.9 us (13%)
  between operations  14 us (4%)
  Pallas kernels  12.4 us (3%)
  local copies, waits for them, and re-layouts  6.95 us (2%)
  other arithmetic  5.52 us (1%)
    ppermute x36, waiting for transfers between devices, gather(): send = lambda a, perm: lax.ppermute(a, 'wide', perm)  165 us
    ppermute x36, starting transfers between devices, gather(): send = lambda a, perm: lax.ppermute(a, 'wide', perm)  83.2 us
    dot_general x5, matrix products, dot(): return jnp.dot(a, b, preferred_element_type=F32)  51.9 us
    all_gather x1, waiting for transfers between devices, scheduled(): rotated_out = lax.all_gather(mine_out, 'wide', axis=0, tiled=True)  44.1 us
    pallas_call x1, Pallas kernels, fit(): pl.pallas_call(fit_kernel, out_shape=jax.ShapeDtypeStruct((ka, ks), F32),...  12.4 us
  transfers between devices with their start and end apart: 39, of which 18 were waited for; matrix products, arithmetic and copies ran while one was open for 15% of the time, Pallas kernels for 0%

profile of v1, /device:TPU:0, one launch (start us, length us, event | category | flops | bytes accessed | tf_op | source)
XLA Modules:
  0.0 388.4 jit_solution(16200963895048177997)
XLA Ops:
  6.5 3.4 fusion.8
  10.0 2.9 collective-permute-start.28
  13.6 4.4 %collective-permute-start.27 = (bf16[64,3584]{1,0:T(8,128)(2,1)}, bf16[64,3584]{1,0:T(8,128)(2,1)S(1)}, u32[]{:S(2)}, u32[]{:S(2)}) collective-permute-start(bf16[64,3584]{1,0:T(8,128)(2,1)} %get-tuple-element.11), channel_id=1, source_target_pairs={{0,4},{2,6},{4,0},{6,2},{8,12},{10,14},{12,8},{14,10},{1,5},{3,7},... | collective-permute-start | bytes 1376264 | tf_op jit(solution)/shard_map/ppermute | solution.py:100
  19.3 4.4 %fusion.9 = f32[512,2048]{1,0:T(8,128)} fusion(bf16[512,1024]{1,0:T(8,128)(2,1)S(1)} %copy-done, bf16[1024,2048]{1,0:T(8,128)(2,1)S(1)} %copy-done.7), kind=kOutput, calls=%fused_computation.54 | convolution fusion | flops 2147483648 | bytes 9437184 | tf_op jit(solution)/shard_map/dot_general | solution.py:16
  28.2 8.3 %collective-permute-done.10 = bf16[64,3584]{1,0:T(8,128)(2,1)S(1)} collective-permute-done((bf16[64,3584]{1,0:T(8,128)(2,1)}, bf16[64,3584]{1,0:T(8,128)(2,1)S(1)}, u32[]{:S(2)}, u32[]{:S(2)}) %collective-permute-start.10) | collective-permute-done | bytes 458784 | tf_op jit(solution)/shard_map/ppermute | solution.py:100
  37.2 11.7 %collective-permute-start = (bf16[64,3584]{1,0:T(8,128)(2,1)}, bf16[64,3584]{1,0:T(8,128)(2,1)S(1)}, u32[]{:S(2)}, u32[]{:S(2)}) collective-permute-start(bf16[64,3584]{1,0:T(8,128)(2,1)} %get-tuple-element.10), channel_id=1, source_target_pairs={{0,4},{2,6},{4,0},{6,2},{8,12},{10,14},{12,8},{14,10},{1,5},{3,7},... | collective-permute-start | bytes 1376264 | tf_op jit(solution)/shard_map/ppermute | solution.py:100
  51.4 13.5 %collective-permute-done.19 = bf16[64,3584]{1,0:T(8,128)(2,1)S(1)} collective-permute-done((bf16[64,3584]{1,0:T(8,128)(2,1)}, bf16[64,3584]{1,0:T(8,128)(2,1)S(1)}, u32[]{:S(2)}, u32[]{:S(2)}) %collective-permute-start.19) | collective-permute-done | bytes 458784 | tf_op jit(solution)/shard_map/ppermute | solution.py:100
  64.9 10.1 %collective-permute-start.18 = (bf16[64,3584]{1,0:T(8,128)(2,1)}, bf16[64,3584]{1,0:T(8,128)(2,1)S(1)}, u32[]{:S(2)}, u32[]{:S(2)}) collective-permute-start(bf16[64,3584]{1,0:T(8,128)(2,1)} %get-tuple-element.12), channel_id=1, source_target_pairs={{0,4},{2,6},{4,0},{6,2},{8,12},{10,14},{12,8},{14,10},{1,5},{3,7},... | collective-permute-start | bytes 1376264 | tf_op jit(solution)/shard_map/ppermute | solution.py:100
  75.0 16.7 %collective-permute-start.30 = (bf16[64,3584]{1,0:T(8,128)(2,1)S(1)}, bf16[64,3584]{1,0:T(8,128)(2,1)S(1)}, u32[]{:S(2)}, u32[]{:S(2)}) collective-permute-start(bf16[64,3584]{1,0:T(8,128)(2,1)S(1)} %broadcast_select_fusion.2), channel_id=1, source_target_pairs={{0,4},{2,6},{4,0},{6,2},{8,12},{10,14},{12,8},{14,10},{1,5},{3,7},... | collective-permute-start | bytes 1376264 | tf_op jit(solution)/shard_map/ppermute | solution.py:100
  96.5 6.7 %collective-permute-done.30 = bf16[64,3584]{1,0:T(8,128)(2,1)S(1)} collective-permute-done((bf16[64,3584]{1,0:T(8,128)(2,1)S(1)}, bf16[64,3584]{1,0:T(8,128)(2,1)S(1)}, u32[]{:S(2)}, u32[]{:S(2)}) %collective-permute-start.30) | collective-permute-done | bytes 458784 | tf_op jit(solution)/shard_map/ppermute | solution.py:100
  104.9 8.2 %collective-permute-done.12 = bf16[64,3584]{1,0:T(8,128)(2,1)S(1)} collective-permute-done((bf16[64,3584]{1,0:T(8,128)(2,1)S(1)}, bf16[64,3584]{1,0:T(8,128)(2,1)S(1)}, u32[]{:S(2)}, u32[]{:S(2)}) %collective-permute-start.12) | collective-permute-done | bytes 458784 | tf_op jit(solution)/shard_map/ppermute | solution.py:100
  113.9 21.9 %collective-permute-done.3 = bf16[64,3584]{1,0:T(8,128)(2,1)S(1)} collective-permute-done((bf16[64,3584]{1,0:T(8,128)(2,1)S(1)}, bf16[64,3584]{1,0:T(8,128)(2,1)S(1)}, u32[]{:S(2)}, u32[]{:S(2)}) %collective-permute-start.3) | collective-permute-done | bytes 458784 | tf_op jit(solution)/shard_map/ppermute | solution.py:100
  136.8 10.8 %collective-permute-done.21 = bf16[64,3584]{1,0:T(8,128)(2,1)S(1)} collective-permute-done((bf16[64,3584]{1,0:T(8,128)(2,1)S(1)}, bf16[64,3584]{1,0:T(8,128)(2,1)S(1)}, u32[]{:S(2)}, u32[]{:S(2)}) %collective-permute-start.21) | collective-permute-done | bytes 458784 | tf_op jit(solution)/shard_map/ppermute | solution.py:100
  149.9 10.3 %collective-permute-done.32 = bf16[64,3584]{1,0:T(8,128)(2,1)S(1)} collective-permute-done((bf16[64,3584]{1,0:T(8,128)(2,1)S(1)}, bf16[64,3584]{1,0:T(8,128)(2,1)S(1)}, u32[]{:S(2)}, u32[]{:S(2)}) %collective-permute-start.32) | collective-permute-done | bytes 458784 | tf_op jit(solution)/shard_map/ppermute | solution.py:100
  161.7 10.1 %collective-permute-done.14 = bf16[64,3584]{1,0:T(8,128)(2,1)S(1)} collective-permute-done((bf16[64,3584]{1,0:T(8,128)(2,1)S(1)}, bf16[64,3584]{1,0:T(8,128)(2,1)S(1)}, u32[]{:S(2)}, u32[]{:S(2)}) %collective-permute-start.14) | collective-permute-done | bytes 458784 | tf_op jit(solution)/shard_map/ppermute | solution.py:100
  176.8 12.3 %collective-permute-done.5 = bf16[64,3584]{1,0:T(8,128)(2,1)S(1)} collective-permute-done((bf16[64,3584]{1,0:T(8,128)(2,1)S(1)}, bf16[64,3584]{1,0:T(8,128)(2,1)S(1)}, u32[]{:S(2)}, u32[]{:S(2)}) %collective-permute-start.5) | collective-permute-done | bytes 458784 | tf_op jit(solution)/shard_map/ppermute | solution.py:100
  196.5 2.9 collective-permute-start.35
  199.6 5.3 %collective-permute-done.34 = bf16[64,3584]{1,0:T(8,128)(2,1)S(1)} collective-permute-done((bf16[64,3584]{1,0:T(8,128)(2,1)S(1)}, bf16[64,3584]{1,0:T(8,128)(2,1)S(1)}, u32[]{:S(2)}, u32[]{:S(2)}) %collective-permute-start.34) | collective-permute-done | bytes 458784 | tf_op jit(solution)/shard_map/ppermute | solution.py:100
  204.9 2.8 collective-permute-start.17
  207.8 36.4 %collective-permute-done.35 = bf16[64,3584]{1,0:T(8,128)(2,1)S(1)} collective-permute-done((bf16[64,3584]{1,0:T(8,128)(2,1)S(1)}, bf16[64,3584]{1,0:T(8,128)(2,1)S(1)}, u32[]{:S(2)}, u32[]{:S(2)}) %collective-permute-start.35) | collective-permute-done | bytes 458784 | tf_op jit(solution)/shard_map/ppermute | solution.py:100
  244.2 2.8 collective-permute-start.8
  247.2 3.0 collective-permute-start.26
  250.3 3.7 collective-permute-done.17
  254.3 9.6 %collective-permute-done.8 = bf16[64,3584]{1,0:T(8,128)(2,1)S(1)} collective-permute-done((bf16[64,3584]{1,0:T(8,128)(2,1)S(1)}, bf16[64,3584]{1,0:T(8,128)(2,1)S(1)}, u32[]{:S(2)}, u32[]{:S(2)}) %collective-permute-start.8) | collective-permute-done | bytes 458784 | tf_op jit(solution)/shard_map/ppermute | solution.py:100
  264.1 4.9 %collective-permute-done.26 = bf16[64,3584]{1,0:T(8,128)(2,1)S(1)} collective-permute-done((bf16[64,3584]{1,0:T(8,128)(2,1)S(1)}, bf16[64,3584]{1,0:T(8,128)(2,1)S(1)}, u32[]{:S(2)}, u32[]{:S(2)}) %collective-permute-start.26) | collective-permute-done | bytes 458784 | tf_op jit(solution)/shard_map/ppermute | solution.py:100
  269.2 10.1 %fusion.4 = f32[512,1792]{1,0:T(8,128)S(1)} fusion(bf16[512,3584]{1,0:T(8,128)(2,1)S(1)} %select_dynamic-update-slice_fusion.10, bf16[14336,1792]{1,0:T(8,128)(2,1)} %param.6), kind=kOutput, calls=%fused_computation.4 | convolution fusion | flops 6576668672 | bytes 20185088 | tf_op jit(solution)/shard_map/dot_general | solution.py:16
  279.2 11.6 %fusion.6 = f32[512,1792]{1,0:T(8,128)} fusion(bf16[512,3584]{1,0:T(8,128)(2,1)S(1)} %select_dynamic-update-slice_fusion.15, bf16[14336,1792]{1,0:T(8,128)(2,1)} %param.6), kind=kOutput, calls=%fused_computation.6 | convolution fusion | flops 6576668672 | bytes 20185088 | tf_op jit(solution)/shard_map/dot_general | solution.py:16
  290.8 11.6 %fusion.2 = f32[512,1792]{1,0:T(8,128)} fusion(bf16[512,3584]{1,0:T(8,128)(2,1)S(1)} %select_dynamic-update-slice_fusion.5, bf16[14336,1792]{1,0:T(8,128)(2,1)} %param.6), kind=kOutput, calls=%fused_computation.2 | convolution fusion | flops 6576668672 | bytes 20185088 | tf_op jit(solution)/shard_map/dot_general | solution.py:16
  302.4 14.3 %add_add_fusion.mine_ref = f32[512,1792]{1,0:T(8,128)} fusion(f32[512,1792]{1,0:T(8,128)} %fusion.2, f32[512,1792]{1,0:T(8,128)} %fusion.6, f32[512,1792]{1,0:T(8,128)S(1)} %fusion.4, bf16[512,3584]{1,0:T(8,128)(2,1)S(1)} %select_dynamic-update-slice_fusion, bf16[14336,1792]{1,0:T(8,128)(2,1)} %param.6), kind=kOutput, calls=%fused_computation.8 | convolution fusion | flops 6579421184 | bytes 31195136 | tf_op jit(solution)/shard_map/dot_general | solution.py:16
  318.6 4.8 %collective-permute-done.36.other_ref = f32[512,1792]{1,0:T(8,128)} collective-permute-done((f32[512,1792]{1,0:T(8,128)}, f32[512,1792]{1,0:T(8,128)}, u32[]{:S(2)}, u32[]{:S(2)}) %collective-permute-start.36) | collective-permute-done | bytes 3670048 | tf_op jit(solution)/shard_map/ppermute | solution.py:68
  323.4 44.1 %all-gather.2.cloned.1.call-done.out_ref = bf16[512,2048]{1,0:T(8,128)(2,1)} async-done(((bf16[64,2048]{1,0:T(8,128)(2,1)}), bf16[512,2048]{1,0:T(8,128)(2,1)}) %all-gather.2.cloned.1.call-update) | async-done | bytes 2097168 | tf_op jit(solution)/shard_map/all_gather | solution.py:134
  369.1 12.4 %fit.1 = f32[1792,2048]{1,0:T(8,128)} custom-call(s32[8]{0:T(128)S(1)} %stack.35.order_ref, f32[512,1792]{1,0:T(8,128)} %add_add_fusion.mine_ref, f32[512,1792]{1,0:T(8,128)} %collective-permute-done.36.other_ref, bf16[512,2048]{1,0:T(8,128)(2,1)S(1)} %copy-done.2), custom_call_target="tpu_custom_call" | custom-call | flops 3758096384 | bytes 24117248 | tf_op jit(solution)/shard_map/fit/pallas_call | solution.py:43
  (105 shorter events, 38.1 us)
Async XLA Ops:
  6.5 310.2 %reduce-scatter.2.cloned.1.call-start = ((), (), s32[]{:S(2)}) async-start(), calls=%async_computation.1 | async-start | bytes 4718592 | tf_op jit(solution)/shard_map/reduce_scatter | solution.py:133
  13.6 78.2 %collective-permute-start.27 = (bf16[64,3584]{1,0:T(8,128)(2,1)}, bf16[64,3584]{1,0:T(8,128)(2,1)S(1)}, u32[]{:S(2)}, u32[]{:S(2)}) collective-permute-start(bf16[64,3584]{1,0:T(8,128)(2,1)} %get-tuple-element.11), channel_id=1, source_target_pairs={{0,4},{2,6},{4,0},{6,2},{8,12},{10,14},{12,8},{14,10},{1,5},{3,7},... | collective-permute-start | bytes 1376264 | tf_op jit(solution)/shard_map/ppermute | solution.py:100
  18.0 18.5 %collective-permute-start.10 = (bf16[64,3584]{1,0:T(8,128)(2,1)}, bf16[64,3584]{1,0:T(8,128)(2,1)S(1)}, u32[]{:S(2)}, u32[]{:S(2)}) collective-permute-start(bf16[64,3584]{1,0:T(8,128)(2,1)} %get-tuple-element.5), channel_id=1, source_target_pairs={{0,2},{2,0},{4,6},{6,4},{8,10},{10,8},{12,14},{14,12},{1,3},{3,1},... | collective-permute-start | bytes 1376264 | tf_op jit(solution)/shard_map/ppermute | solution.py:100
  18.6 18.6 %collective-permute-start.11 = (bf16[64,3584]{1,0:T(8,128)(2,1)}, bf16[64,3584]{1,0:T(8,128)(2,1)S(1)}, u32[]{:S(2)}, u32[]{:S(2)}) collective-permute-start(bf16[64,3584]{1,0:T(8,128)(2,1)} %get-tuple-element.5), channel_id=1, source_target_pairs={{4,8},{6,10},{8,4},{10,6},{5,9},{7,11},{9,5},{11,7},{20,24},{22,26... | collective-permute-start | bytes 1376264 | tf_op jit(solution)/shard_map/ppermute | solution.py:100
  23.7 343.8 %all-gather.2.cloned.1.call-start = ((), (), s32[]{:S(2)}) async-start(), calls=%async_computation.2 | async-start | bytes 2359296 | tf_op jit(solution)/shard_map/all_gather | solution.py:134
  24.5 68.2 %collective-permute-start.9 = (bf16[64,3584]{1,0:T(8,128)(2,1)}, bf16[64,3584]{1,0:T(8,128)(2,1)S(1)}, u32[]{:S(2)}, u32[]{:S(2)}) collective-permute-start(bf16[64,3584]{1,0:T(8,128)(2,1)} %get-tuple-element.5), channel_id=1, source_target_pairs={{0,4},{2,6},{4,0},{6,2},{8,12},{10,14},{12,8},{14,10},{1,5},{3,7},... | collective-permute-start | bytes 1376264 | tf_op jit(solution)/shard_map/ppermute | solution.py:100
  26.6 22.3 %collective-permute-start.1 = (bf16[64,3584]{1,0:T(8,128)(2,1)}, bf16[64,3584]{1,0:T(8,128)(2,1)S(1)}, u32[]{:S(2)}, u32[]{:S(2)}) collective-permute-start(bf16[64,3584]{1,0:T(8,128)(2,1)} %get-tuple-element.10), channel_id=1, source_target_pairs={{0,2},{2,0},{4,6},{6,4},{8,10},{10,8},{12,14},{14,12},{1,3},{3,1},... | collective-permute-start | bytes 1376264 | tf_op jit(solution)/shard_map/ppermute | solution.py:100
  37.2 58.3 %collective-permute-start = (bf16[64,3584]{1,0:T(8,128)(2,1)}, bf16[64,3584]{1,0:T(8,128)(2,1)S(1)}, u32[]{:S(2)}, u32[]{:S(2)}) collective-permute-start(bf16[64,3584]{1,0:T(8,128)(2,1)} %get-tuple-element.10), channel_id=1, source_target_pairs={{0,4},{2,6},{4,0},{6,2},{8,12},{10,14},{12,8},{14,10},{1,5},{3,7},... | collective-permute-start | bytes 1376264 | tf_op jit(solution)/shard_map/ppermute | solution.py:100
  48.9 16.0 %collective-permute-start.19 = (bf16[64,3584]{1,0:T(8,128)(2,1)}, bf16[64,3584]{1,0:T(8,128)(2,1)S(1)}, u32[]{:S(2)}, u32[]{:S(2)}) collective-permute-start(bf16[64,3584]{1,0:T(8,128)(2,1)} %get-tuple-element.12), channel_id=1, source_target_pairs={{0,2},{2,0},{4,6},{6,4},{8,10},{10,8},{12,14},{14,12},{1,3},{3,1},... | collective-permute-start | bytes 1376264 | tf_op jit(solution)/shard_map/ppermute | solution.py:100
  50.7 24.3 %collective-permute-start.20 = (bf16[64,3584]{1,0:T(8,128)(2,1)}, bf16[64,3584]{1,0:T(8,128)(2,1)S(1)}, u32[]{:S(2)}, u32[]{:S(2)}) collective-permute-start(bf16[64,3584]{1,0:T(8,128)(2,1)} %get-tuple-element.12), channel_id=1, source_target_pairs={{4,8},{6,10},{8,4},{10,6},{5,9},{7,11},{9,5},{11,7},{20,24},{22,26... | collective-permute-start | bytes 1376264 | tf_op jit(solution)/shard_map/ppermute | solution.py:100
  64.9 30.7 %collective-permute-start.18 = (bf16[64,3584]{1,0:T(8,128)(2,1)}, bf16[64,3584]{1,0:T(8,128)(2,1)S(1)}, u32[]{:S(2)}, u32[]{:S(2)}) collective-permute-start(bf16[64,3584]{1,0:T(8,128)(2,1)} %get-tuple-element.12), channel_id=1, source_target_pairs={{0,4},{2,6},{4,0},{6,2},{8,12},{10,14},{12,8},{14,10},{1,5},{3,7},... | collective-permute-start | bytes 1376264 | tf_op jit(solution)/shard_map/ppermute | solution.py:100
  75.0 28.2 %collective-permute-start.30 = (bf16[64,3584]{1,0:T(8,128)(2,1)S(1)}, bf16[64,3584]{1,0:T(8,128)(2,1)S(1)}, u32[]{:S(2)}, u32[]{:S(2)}) collective-permute-start(bf16[64,3584]{1,0:T(8,128)(2,1)S(1)} %broadcast_select_fusion.2), channel_id=1, source_target_pairs={{0,4},{2,6},{4,0},{6,2},{8,12},{10,14},{12,8},{14,10},{1,5},{3,7},... | collective-permute-start | bytes 1376264 | tf_op jit(solution)/shard_map/ppermute | solution.py:100
  91.8 21.2 %collective-permute-start.12 = (bf16[64,3584]{1,0:T(8,128)(2,1)S(1)}, bf16[64,3584]{1,0:T(8,128)(2,1)S(1)}, u32[]{:S(2)}, u32[]{:S(2)}) collective-permute-start(bf16[64,3584]{1,0:T(8,128)(2,1)S(1)} %broadcast_select_fusion.8), channel_id=1, source_target_pairs={{0,4},{2,6},{4,0},{6,2},{8,12},{10,14},{12,8},{14,10},{1,5},{3,7},... | collective-permute-start | bytes 1376264 | tf_op jit(solution)/shard_map/ppermute | solution.py:100
  92.7 43.1 %collective-permute-start.3 = (bf16[64,3584]{1,0:T(8,128)(2,1)S(1)}, bf16[64,3584]{1,0:T(8,128)(2,1)S(1)}, u32[]{:S(2)}, u32[]{:S(2)}) collective-permute-start(bf16[64,3584]{1,0:T(8,128)(2,1)S(1)} %broadcast_select_fusion.11), channel_id=1, source_target_pairs={{0,4},{2,6},{4,0},{6,2},{8,12},{10,14},{12,8},{14,10},{1,5},{3,7},... | collective-permute-start | bytes 1376264 | tf_op jit(solution)/shard_map/ppermute | solution.py:100
  95.5 52.1 %collective-permute-start.21 = (bf16[64,3584]{1,0:T(8,128)(2,1)S(1)}, bf16[64,3584]{1,0:T(8,128)(2,1)S(1)}, u32[]{:S(2)}, u32[]{:S(2)}) collective-permute-start(bf16[64,3584]{1,0:T(8,128)(2,1)S(1)} %broadcast_select_fusion.5), channel_id=1, source_target_pairs={{0,4},{2,6},{4,0},{6,2},{8,12},{10,14},{12,8},{14,10},{1,5},{3,7},... | collective-permute-start | bytes 1376264 | tf_op jit(solution)/shard_map/ppermute | solution.py:100
  95.6 41.1 %collective-permute-start.31 = (bf16[64,3584]{1,0:T(8,128)(2,1)S(1)}, bf16[64,3584]{1,0:T(8,128)(2,1)S(1)}, u32[]{:S(2)}, u32[]{:S(2)}) collective-permute-start(bf16[64,3584]{1,0:T(8,128)(2,1)S(1)} %collective-permute-done.27), channel_id=1, source_target_pairs={{4,8},{6,10},{8,4},{10,6},{5,9},{7,11},{9,5},{11,7},{20,24},{22,26... | collective-permute-start | bytes 1376264 | tf_op jit(solution)/shard_map/ppermute | solution.py:100
  103.2 45.9 %collective-permute-start.13 = (bf16[64,3584]{1,0:T(8,128)(2,1)S(1)}, bf16[64,3584]{1,0:T(8,128)(2,1)S(1)}, u32[]{:S(2)}, u32[]{:S(2)}) collective-permute-start(bf16[64,3584]{1,0:T(8,128)(2,1)S(1)} %collective-permute-done.9), channel_id=1, source_target_pairs={{4,8},{6,10},{8,4},{10,6},{5,9},{7,11},{9,5},{11,7},{20,24},{22,26... | collective-permute-start | bytes 1376264 | tf_op jit(solution)/shard_map/ppermute | solution.py:100
  113.0 59.9 %collective-permute-start.4 = (bf16[64,3584]{1,0:T(8,128)(2,1)S(1)}, bf16[64,3584]{1,0:T(8,128)(2,1)S(1)}, u32[]{:S(2)}, u32[]{:S(2)}) collective-permute-start(bf16[64,3584]{1,0:T(8,128)(2,1)S(1)} %collective-permute-done), channel_id=1, source_target_pairs={{4,8},{6,10},{8,4},{10,6},{5,9},{7,11},{9,5},{11,7},{20,24},{22,26... | collective-permute-start | bytes 1376264 | tf_op jit(solution)/shard_map/ppermute | solution.py:100
  135.8 38.3 %collective-permute-start.22 = (bf16[64,3584]{1,0:T(8,128)(2,1)S(1)}, bf16[64,3584]{1,0:T(8,128)(2,1)S(1)}, u32[]{:S(2)}, u32[]{:S(2)}) collective-permute-start(bf16[64,3584]{1,0:T(8,128)(2,1)S(1)} %collective-permute-done.18), channel_id=1, source_target_pairs={{4,8},{6,10},{8,4},{10,6},{5,9},{7,11},{9,5},{11,7},{20,24},{22,26... | collective-permute-start | bytes 1376264 | tf_op jit(solution)/shard_map/ppermute | solution.py:100
  136.7 38.7 %collective-permute-start.33 = (bf16[64,3584]{1,0:T(8,128)(2,1)S(1)}, bf16[64,3584]{1,0:T(8,128)(2,1)S(1)}, u32[]{:S(2)}, u32[]{:S(2)}) collective-permute-start(bf16[64,3584]{1,0:T(8,128)(2,1)S(1)} %get-tuple-element.27), channel_id=1, source_target_pairs={{0,2},{2,0},{4,6},{6,4},{8,10},{10,8},{12,14},{14,12},{1,3},{3,1},... | collective-permute-start | bytes 1376264 | tf_op jit(solution)/shard_map/ppermute | solution.py:100
  149.1 41.3 %collective-permute-start.15 = (bf16[64,3584]{1,0:T(8,128)(2,1)S(1)}, bf16[64,3584]{1,0:T(8,128)(2,1)S(1)}, u32[]{:S(2)}, u32[]{:S(2)}) collective-permute-start(bf16[64,3584]{1,0:T(8,128)(2,1)S(1)} %get-tuple-element.15), channel_id=1, source_target_pairs={{0,2},{2,0},{4,6},{6,4},{8,10},{10,8},{12,14},{14,12},{1,3},{3,1},... | collective-permute-start | bytes 1376264 | tf_op jit(solution)/shard_map/ppermute | solution.py:100
  171.8 23.5 %collective-permute-start.6 = (bf16[64,3584]{1,0:T(8,128)(2,1)S(1)}, bf16[64,3584]{1,0:T(8,128)(2,1)S(1)}, u32[]{:S(2)}, u32[]{:S(2)}) collective-permute-start(bf16[64,3584]{1,0:T(8,128)(2,1)S(1)} %get-tuple-element.19), channel_id=1, source_target_pairs={{0,2},{2,0},{4,6},{6,4},{8,10},{10,8},{12,14},{14,12},{1,3},{3,1},... | collective-permute-start | bytes 1376264 | tf_op jit(solution)/shard_map/ppermute | solution.py:100
  172.9 23.6 %collective-permute-start.24 = (bf16[64,3584]{1,0:T(8,128)(2,1)S(1)}, bf16[64,3584]{1,0:T(8,128)(2,1)S(1)}, u32[]{:S(2)}, u32[]{:S(2)}) collective-permute-start(bf16[64,3584]{1,0:T(8,128)(2,1)S(1)} %get-tuple-element.23), channel_id=1, source_target_pairs={{0,2},{2,0},{4,6},{6,4},{8,10},{10,8},{12,14},{14,12},{1,3},{3,1},... | collective-permute-start | bytes 1376264 | tf_op jit(solution)/shard_map/ppermute | solution.py:100
  175.4 18.7 %collective-permute-start.23 = (bf16[64,3584]{1,0:T(8,128)(2,1)S(1)}, bf16[64,3584]{1,0:T(8,128)(2,1)S(1)}, u32[]{:S(2)}, u32[]{:S(2)}) collective-permute-start(bf16[64,3584]{1,0:T(8,128)(2,1)S(1)} %collective-permute-done.22), channel_id=1, source_target_pairs={{4,0},{6,2},{8,12},{10,14},{5,1},{7,3},{9,13},{11,15},{20,16},{22,... | collective-permute-start | bytes 1376264 | tf_op jit(solution)/shard_map/ppermute | solution.py:100
  189.1 15.8 %collective-permute-start.34 = (bf16[64,3584]{1,0:T(8,128)(2,1)S(1)}, bf16[64,3584]{1,0:T(8,128)(2,1)S(1)}, u32[]{:S(2)}, u32[]{:S(2)}) collective-permute-start(bf16[64,3584]{1,0:T(8,128)(2,1)S(1)} %get-tuple-element.25), channel_id=1, source_target_pairs={{0,2},{2,0},{4,6},{6,4},{8,10},{10,8},{12,14},{14,12},{1,3},{3,1},... | collective-permute-start | bytes 1376264 | tf_op jit(solution)/shard_map/ppermute | solution.py:100
  190.4 56.7 %collective-permute-start.16 = (bf16[64,3584]{1,0:T(8,128)(2,1)S(1)}, bf16[64,3584]{1,0:T(8,128)(2,1)S(1)}, u32[]{:S(2)}, u32[]{:S(2)}) collective-permute-start(bf16[64,3584]{1,0:T(8,128)(2,1)S(1)} %get-tuple-element.13), channel_id=1, source_target_pairs={{0,2},{2,0},{4,6},{6,4},{8,10},{10,8},{12,14},{14,12},{1,3},{3,1},... | collective-permute-start | bytes 1376264 | tf_op jit(solution)/shard_map/ppermute | solution.py:100
  194.1 60.1 %collective-permute-start.7 = (bf16[64,3584]{1,0:T(8,128)(2,1)S(1)}, bf16[64,3584]{1,0:T(8,128)(2,1)S(1)}, u32[]{:S(2)}, u32[]{:S(2)}) collective-permute-start(bf16[64,3584]{1,0:T(8,128)(2,1)S(1)} %get-tuple-element.17), channel_id=1, source_target_pairs={{0,2},{2,0},{4,6},{6,4},{8,10},{10,8},{12,14},{14,12},{1,3},{3,1},... | collective-permute-start | bytes 1376264 | tf_op jit(solution)/shard_map/ppermute | solution.py:100
  195.3 68.7 %collective-permute-start.25 = (bf16[64,3584]{1,0:T(8,128)(2,1)S(1)}, bf16[64,3584]{1,0:T(8,128)(2,1)S(1)}, u32[]{:S(2)}, u32[]{:S(2)}) collective-permute-start(bf16[64,3584]{1,0:T(8,128)(2,1)S(1)} %get-tuple-element.21), channel_id=1, source_target_pairs={{0,2},{2,0},{4,6},{6,4},{8,10},{10,8},{12,14},{14,12},{1,3},{3,1},... | collective-permute-start | bytes 1376264 | tf_op jit(solution)/shard_map/ppermute | solution.py:100
  196.5 47.7 %collective-permute-start.35 = (bf16[64,3584]{1,0:T(8,128)(2,1)S(1)}, bf16[64,3584]{1,0:T(8,128)(2,1)S(1)}, u32[]{:S(2)}, u32[]{:S(2)}) collective-permute-start(bf16[64,3584]{1,0:T(8,128)(2,1)S(1)} %collective-permute-done.32), channel_id=1, source_target_pairs={{0,2},{2,0},{12,14},{14,12},{1,3},{3,1},{13,15},{15,13},{16,18},{1... | collective-permute-start | bytes 1376264 | tf_op jit(solution)/shard_map/ppermute | solution.py:100
  204.9 49.2 %collective-permute-start.17 = (bf16[64,3584]{1,0:T(8,128)(2,1)S(1)}, bf16[64,3584]{1,0:T(8,128)(2,1)S(1)}, u32[]{:S(2)}, u32[]{:S(2)}) collective-permute-start(bf16[64,3584]{1,0:T(8,128)(2,1)S(1)} %collective-permute-done.14), channel_id=1, source_target_pairs={{0,2},{2,0},{12,14},{14,12},{1,3},{3,1},{13,15},{15,13},{16,18},{1... | collective-permute-start | bytes 1376264 | tf_op jit(solution)/shard_map/ppermute | solution.py:100
  244.2 19.7 %collective-permute-start.8 = (bf16[64,3584]{1,0:T(8,128)(2,1)S(1)}, bf16[64,3584]{1,0:T(8,128)(2,1)S(1)}, u32[]{:S(2)}, u32[]{:S(2)}) collective-permute-start(bf16[64,3584]{1,0:T(8,128)(2,1)S(1)} %collective-permute-done.5), channel_id=1, source_target_pairs={{0,2},{2,0},{12,14},{14,12},{1,3},{3,1},{13,15},{15,13},{16,18},{1... | collective-permute-start | bytes 1376264 | tf_op jit(solution)/shard_map/ppermute | solution.py:100
  247.2 21.9 %collective-permute-start.26 = (bf16[64,3584]{1,0:T(8,128)(2,1)S(1)}, bf16[64,3584]{1,0:T(8,128)(2,1)S(1)}, u32[]{:S(2)}, u32[]{:S(2)}) collective-permute-start(bf16[64,3584]{1,0:T(8,128)(2,1)S(1)} %collective-permute-done.23), channel_id=1, source_target_pairs={{0,2},{2,0},{12,14},{14,12},{1,3},{3,1},{13,15},{15,13},{16,18},{1... | collective-permute-start | bytes 1376264 | tf_op jit(solution)/shard_map/ppermute | solution.py:100
  (15 other events, 339.7 us)
Sparse Core Ops, SparseCore 0:
  23.8 123.3 reduce-scatter.1
  318.6 48.8 all-gather.1

commit v2 on v1

--- a/solution.py
+++ b/solution.py
@@ -96,20 +96,30 @@
 ACROSS_ENDS = pairs(lambda z, x: (z, 1 - x), corner)
 
 
-def gather(block, at_end):
-    send = lambda a, perm: lax.ppermute(a, "wide", perm)
-    pick = lambda a, b: jnp.where(at_end, a, b)
-    a1 = send(block, ENDS)
-    x1 = send(block, ACROSS)
-    m1 = send(block, MIDDLE)
-    m2 = send(a1, MIDDLE)
-    a2 = send(pick(x1, m1), ENDS)
-    x2 = send(pick(a1, m1), ACROSS)
-    a3 = send(m2, TO_ENDS)
-    x3 = send(pick(a2, m2), ACROSS)
-    x4 = send(a3, ACROSS_ENDS)
+def send(a, perm):
+    return lax.ppermute(a, "wide", perm)
+
+
+def stage(step, got, at_end):
+    pick = lambda a, b: jnp.where(at_end, got[a], got[b])
+    if step == 0:
+        return {"a1": send(got["own"], ENDS), "x1": send(got["own"], ACROSS), "m1": send(got["own"], MIDDLE)}
+    if step == 1:
+        return {
+            "m2": send(got["a1"], MIDDLE),
+            "x2": send(pick("a1", "m1"), ACROSS),
+            "a2": send(pick("x1", "m1"), ENDS),
+        }
+    if step == 2:
+        return {"a3": send(got["m2"], TO_ENDS), "x3": send(pick("a2", "m2"), ACROSS)}
+    return {"x4": send(got["a3"], ACROSS_ENDS)}
+
+
+def assemble(got, at_end):
+    pick = lambda a, b: jnp.where(at_end, got[a], got[b])
     return jnp.concatenate(
-        [block, a1, pick(a2, m1), pick(a3, m2), x1, pick(x2, a2), pick(x3, x2), pick(x4, x3)], axis=0
+        [got["own"], got["a1"], pick("a2", "m1"), pick("a3", "m2"), got["x1"], pick("x2", "a2"), pick("x3", "x2"),
+         pick("x4", "x3")], axis=0
     )
 
 
@@ -126,18 +136,51 @@
     z = w // PAIR
     at_end = (z == 0) | (z == LINE - 1)
     deep = inputs.shape[1]
-    chunks = 4
+    chunks, steps, lag = 8, 4, 2
     width = deep // chunks
 
+    def fence(names, arrays):
+        return dict(zip(names, lax.optimization_barrier(tuple(arrays))))
+
     partial_out = dot(deltas, basis_out)
-    mine_out = lax.psum_scatter(partial_out, "wide", scatter_dimension=0, tiled=True).astype(BF16)
-    rotated_out = lax.all_gather(mine_out, "wide", axis=0, tiled=True)
-
+    sums = lax.psum_scatter(partial_out, "wide", scatter_dimension=0, tiled=True)
+    rotated_out = None
+
+    got = [{"own": inputs[:, c * width : (c + 1) * width]} for c in range(chunks)]
+    fresh = {}
     total = None
-    for c in range(chunks):
-        here = slice(c * width, (c + 1) * width)
-        term = dot(gather(inputs[:, here], at_end), basis_in[here])
-        total = term if total is None else total + term
+    last = chunks + lag * (steps - 1)
+    for slot in range(last + lag):
+        names = fresh.get(slot - lag, [])
+        if slot < chunks:
+            names = names + [(slot, "own")]
+        arrays = [got[c][n] for c, n in names]
+        if total is not None:
+            names, arrays = names + ["total"], arrays + [total]
+        if slot == 9:
+            names, arrays = names + ["sums"], arrays + [sums]
+        if slot == 14:
+            names, arrays = names + ["rotated_out"], arrays + [rotated_out]
+        for name, value in fence(names, arrays).items():
+            if name == "total":
+                total = value
+            elif name == "sums":
+                rotated_out = lax.all_gather(value.astype(BF16), "wide", axis=0, tiled=True)
+            elif name == "rotated_out":
+                rotated_out = value
+            else:
+                got[name[0]][name[1]] = value
+        fresh[slot] = []
+        for step in range(steps):
+            c = slot - lag * step
+            if 0 <= c < chunks:
+                new = stage(step, got[c], at_end)
+                got[c].update(new)
+                fresh[slot] += [(c, n) for n in new]
+        c = slot - lag * steps
+        if 0 <= c < chunks:
+            term = dot(assemble(got[c], at_end), basis_in[c * width : (c + 1) * width])
+            total = term if total is None else total + term
     return fit(slots(w), total, swap_narrow(total), rotated_out)
 
 

time: 389 us -> 375 us (0.964); the launches traced: 388 us -> 370 us
  waiting for transfers between devices: 214 us -> 112 us
  other arithmetic: 5.52 us -> 43 us
  starting transfers between devices: 83.3 us -> 115 us
  matrix products: 51.9 us -> 62.3 us
  local copies, waits for them, and re-layouts: 6.95 us -> 11 us
    ppermute x36 -> x72, waiting for transfers between devices: 165 us -> 105 us  [send(): return lax.ppermute(a, 'wide', perm)]
    all_gather x1, waiting for transfers between devices: 44.1 us -> 0.01 us  [scheduled(): rotated_out = lax.all_gather(value.astype(BF16), 'wide', axis=0, tiled=True)]
    ppermute x36 -> x72, starting transfers between devices: 83.2 us -> 115 us  [send(): return lax.ppermute(a, 'wide', perm)]
    unnamed x8 -> x38, other arithmetic: 0.87 us -> 25.1 us
    add x0 -> x7, other arithmetic: none -> 10.7 us  [scheduled(): total = term if total is None else total + term]
    dot_general x5 -> x9, matrix products: 51.9 us -> 62.3 us  [dot(): return jnp.dot(a, b, preferred_element_type=F32)]
    unnamed x24 -> x82, local copies, waits for them, and re-layouts: 3.43 us -> 9.17 us
    concatenate x4 -> x7, other arithmetic: 0.43 us -> 4.63 us  [assemble(): jnp.concatenate([got['own'], got['a1'], pick('a2', 'm1'), pick('a3', 'm2'...]
  transfers between devices with their start and end apart: 39 -> 75, of which waited for: 18 -> 21; matrix products, arithmetic and copies ran while one was open for 15% -> 28% of each run, Pallas kernels for 0% -> 0%
where the time goes in v2:
time: 375 us; the launch traced here: 370 us
  starting transfers between devices  115 us (31%)
  waiting for transfers between devices  112 us (30%)
  matrix products  62.3 us (17%)
  other arithmetic  43 us (11%)
  between operations  14.5 us (4%)
  Pallas kernels  12.4 us (3%)
  local copies, waits for them, and re-layouts  11 us (3%)
    ppermute x72, starting transfers between devices, send(): return lax.ppermute(a, 'wide', perm)  115 us
    ppermute x72, waiting for transfers between devices, send(): return lax.ppermute(a, 'wide', perm)  105 us
    dot_general x9, matrix products, dot(): return jnp.dot(a, b, preferred_element_type=F32)  62.3 us
    unnamed x38, other arithmetic  25.1 us
    pallas_call x1, Pallas kernels, fit(): pl.pallas_call(fit_kernel, out_shape=jax.ShapeDtypeStruct((ka, ks), F32),...  12.4 us
    add x7, other arithmetic, scheduled(): total = term if total is None else total + term  10.7 us
    unnamed x82, local copies, waits for them, and re-layouts  9.17 us
  transfers between devices with their start and end apart: 75, of which 21 were waited for; matrix products, arithmetic and copies ran while one was open for 28% of the time, Pallas kernels for 0%

profile of v2, /device:TPU:0, one launch (start us, length us, event | category | flops | bytes accessed | tf_op | source)
XLA Modules:
  0.0 370.1 jit_solution(18232690271665528378)
XLA Ops:
  8.3 3.1 collective-permute-start.26
  14.2 3.8 %collective-permute-start = (bf16[64,1792]{1,0:T(8,128)(2,1)S(1)}, bf16[64,1792]{1,0:T(8,128)(2,1)}, u32[]{:S(2)}, u32[]{:S(2)}) collective-permute-start(bf16[64,1792]{1,0:T(8,128)(2,1)S(1)} %get-tuple-element.185), channel_id=1, source_target_pairs={{0,4},{2,6},{4,0},{6,2},{8,12},{10,14},{12,8},{14,10},{1,5},{3,7},... | collective-permute-start | bytes 688136 | tf_op jit(solution)/shard_map/ppermute | solution.py:100
  18.5 6.5 %fusion.17 = f32[512,2048]{1,0:T(8,128)} fusion(bf16[512,1024]{1,0:T(8,128)(2,1)S(1)} %copy-done, bf16[1024,2048]{1,0:T(8,128)(2,1)} %param.7), kind=kOutput, calls=%fused_computation.105 | convolution fusion | flops 2147483648 | bytes 9437184 | tf_op jit(solution)/shard_map/dot_general | solution.py:16
  34.5 10.1 %collective-permute-done.33 = bf16[64,1792]{1,0:T(8,128)(2,1)S(1)} collective-permute-done((bf16[64,1792]{1,0:T(8,128)(2,1)S(1)}, bf16[64,1792]{1,0:T(8,128)(2,1)S(1)}, u32[]{:S(2)}, u32[]{:S(2)}) %collective-permute-start.33) | collective-permute-done | bytes 229408 | tf_op jit(solution)/shard_map/ppermute | solution.py:100
  45.3 12.8 %collective-permute-done.34 = bf16[64,1792]{1,0:T(8,128)(2,1)S(1)} collective-permute-done((bf16[64,1792]{1,0:T(8,128)(2,1)S(1)}, bf16[64,1792]{1,0:T(8,128)(2,1)S(1)}, u32[]{:S(2)}, u32[]{:S(2)}) %collective-permute-start.34) | collective-permute-done | bytes 229408 | tf_op jit(solution)/shard_map/ppermute | solution.py:100
  58.1 3.0 collective-permute-start.4
  62.7 9.8 %collective-permute-done.7 = bf16[64,1792]{1,0:T(8,128)(2,1)S(1)} collective-permute-done((bf16[64,1792]{1,0:T(8,128)(2,1)S(1)}, bf16[64,1792]{1,0:T(8,128)(2,1)S(1)}, u32[]{:S(2)}, u32[]{:S(2)}) %collective-permute-start.7) | collective-permute-done | bytes 229408 | tf_op jit(solution)/shard_map/ppermute | solution.py:100
  75.2 8.5 %collective-permute-done.8 = bf16[64,1792]{1,0:T(8,128)(2,1)S(1)} collective-permute-done((bf16[64,1792]{1,0:T(8,128)(2,1)S(1)}, bf16[64,1792]{1,0:T(8,128)(2,1)S(1)}, u32[]{:S(2)}, u32[]{:S(2)}) %collective-permute-start.8) | collective-permute-done | bytes 229408 | tf_op jit(solution)/shard_map/ppermute | solution.py:100
  90.3 14.1 %collective-permute-done.39 = bf16[64,1792]{1,0:T(8,128)(2,1)S(1)} collective-permute-done((bf16[64,1792]{1,0:T(8,128)(2,1)S(1)}, bf16[64,1792]{1,0:T(8,128)(2,1)S(1)}, u32[]{:S(2)}, u32[]{:S(2)}) %collective-permute-start.39) | collective-permute-done | bytes 229408 | tf_op jit(solution)/shard_map/ppermute | solution.py:100
  116.2 4.0 %collective-permute-start.14 = (bf16[64,1792]{1,0:T(8,128)(2,1)S(1)}, bf16[64,1792]{1,0:T(8,128)(2,1)S(1)}, u32[]{:S(2)}, u32[]{:S(2)}) collective-permute-start(bf16[64,1792]{1,0:T(8,128)(2,1)S(1)} %get-tuple-element.211), channel_id=1, source_target_pairs={{0,4},{2,6},{4,0},{6,2},{8,12},{10,14},{12,8},{14,10},{1,5},{3,7},... | collective-permute-start | bytes 688136 | tf_op jit(solution)/shard_map/ppermute | solution.py:100
  120.4 6.9 %collective-permute-done.16 = bf16[64,1792]{1,0:T(8,128)(2,1)S(1)} collective-permute-done((bf16[64,1792]{1,0:T(8,128)(2,1)S(1)}, bf16[64,1792]{1,0:T(8,128)(2,1)S(1)}, u32[]{:S(2)}, u32[]{:S(2)}) %collective-permute-start.16) | collective-permute-done | bytes 229408 | tf_op jit(solution)/shard_map/ppermute | solution.py:100
  131.9 4.7 %collective-permute-start.9 = (bf16[64,1792]{1,0:T(8,128)(2,1)S(1)}, bf16[64,1792]{1,0:T(8,128)(2,1)S(1)}, u32[]{:S(2)}, u32[]{:S(2)}) collective-permute-start(bf16[64,1792]{1,0:T(8,128)(2,1)S(1)} %get-tuple-element.96), channel_id=1, source_target_pairs={{0,4},{2,6},{4,0},{6,2},{8,12},{10,14},{12,8},{14,10},{1,5},{3,7},... | collective-permute-start | bytes 688136 | tf_op jit(solution)/shard_map/ppermute | solution.py:100
  138.8 6.3 %collective-permute-done.15 = bf16[64,1792]{1,0:T(8,128)(2,1)S(1)} collective-permute-done((bf16[64,1792]{1,0:T(8,128)(2,1)S(1)}, bf16[64,1792]{1,0:T(8,128)(2,1)S(1)}, u32[]{:S(2)}, u32[]{:S(2)}) %collective-permute-start.15) | collective-permute-done | bytes 229408 | tf_op jit(solution)/shard_map/ppermute | solution.py:100
  145.7 4.3 %collective-permute-done.9 = bf16[64,1792]{1,0:T(8,128)(2,1)S(1)} collective-permute-done((bf16[64,1792]{1,0:T(8,128)(2,1)S(1)}, bf16[64,1792]{1,0:T(8,128)(2,1)S(1)}, u32[]{:S(2)}, u32[]{:S(2)}) %collective-permute-start.9) | collective-permute-done | bytes 229408 | tf_op jit(solution)/shard_map/ppermute | solution.py:100
  154.5 4.6 %collective-permute-done.48 = bf16[64,1792]{1,0:T(8,128)(2,1)S(1)} collective-permute-done((bf16[64,1792]{1,0:T(8,128)(2,1)S(1)}, bf16[64,1792]{1,0:T(8,128)(2,1)S(1)}, u32[]{:S(2)}, u32[]{:S(2)}) %collective-permute-start.48) | collective-permute-done | bytes 229408 | tf_op jit(solution)/shard_map/ppermute | solution.py:100
  175.0 8.2 %fusion.14 = f32[512,1792]{1,0:T(8,128)} fusion(bf16[512,1792]{1,0:T(8,128)(2,1)S(1)} %select_dynamic-update-slice_fusion.35, bf16[14336,1792]{1,0:T(8,128)(2,1)} %param.6), kind=kOutput, calls=%fused_computation.14 | convolution fusion | flops 3288334336 | bytes 11927552 | tf_op jit(solution)/shard_map/dot_general | solution.py:16
  186.5 3.1 collective-permute-start.25
  192.4 3.0 collective-permute-start.63
  202.0 7.0 %fusion.12 = f32[512,1792]{1,0:T(8,128)S(1)} fusion(bf16[512,1792]{1,0:T(8,128)(2,1)} %select_dynamic-update-slice_fusion.30, bf16[14336,1792]{1,0:T(8,128)(2,1)} %param.6), kind=kOutput, calls=%fused_computation.12 | convolution fusion | flops 3288334336 | bytes 11927552 | tf_op jit(solution)/shard_map/dot_general | solution.py:16
  220.1 8.2 %fusion.10 = f32[512,1792]{1,0:T(8,128)} fusion(bf16[512,1792]{1,0:T(8,128)(2,1)S(1)} %select_dynamic-update-slice_fusion.25, bf16[14336,1792]{1,0:T(8,128)(2,1)} %param.6), kind=kOutput, calls=%fused_computation.10 | convolution fusion | flops 3288334336 | bytes 11927552 | tf_op jit(solution)/shard_map/dot_general | solution.py:16
  243.0 7.1 %collective-permute-start.54 = (bf16[64,1792]{1,0:T(8,128)(2,1)}, bf16[64,1792]{1,0:T(8,128)(2,1)S(1)}, u32[]{:S(2)}, u32[]{:S(2)}) collective-permute-start(bf16[64,1792]{1,0:T(8,128)(2,1)} %get-tuple-element.191), channel_id=1, source_target_pairs={{0,4},{2,6},{4,0},{6,2},{8,12},{10,14},{12,8},{14,10},{1,5},{3,7},... | collective-permute-start | bytes 688136 | tf_op jit(solution)/shard_map/ppermute | solution.py:100
  255.8 6.2 %collective-permute-done.54 = bf16[64,1792]{1,0:T(8,128)(2,1)S(1)} collective-permute-done((bf16[64,1792]{1,0:T(8,128)(2,1)}, bf16[64,1792]{1,0:T(8,128)(2,1)S(1)}, u32[]{:S(2)}, u32[]{:S(2)}) %collective-permute-start.54) | collective-permute-done | bytes 229408 | tf_op jit(solution)/shard_map/ppermute | solution.py:100
  266.9 6.3 %fusion.8 = f32[512,1792]{1,0:T(8,128)S(1)} fusion(bf16[512,1792]{1,0:T(8,128)(2,1)S(1)} %select_dynamic-update-slice_fusion.20, bf16[14336,1792]{1,0:T(8,128)(2,1)} %param.6), kind=kOutput, calls=%fused_computation.8 | convolution fusion | flops 3288334336 | bytes 11927552 | tf_op jit(solution)/shard_map/dot_general | solution.py:16
  273.7 4.1 %collective-permute-done.68 = bf16[64,1792]{1,0:T(8,128)(2,1)S(1)} collective-permute-done((bf16[64,1792]{1,0:T(8,128)(2,1)S(1)}, bf16[64,1792]{1,0:T(8,128)(2,1)S(1)}, u32[]{:S(2)}, u32[]{:S(2)}) %collective-permute-start.68) | collective-permute-done | bytes 229408 | tf_op jit(solution)/shard_map/ppermute | solution.py:100
  281.8 13.4 %collective-permute-start.66 = (bf16[64,1792]{1,0:T(8,128)(2,1)}, bf16[64,1792]{1,0:T(8,128)(2,1)S(1)}, u32[]{:S(2)}, u32[]{:S(2)}) collective-permute-start(bf16[64,1792]{1,0:T(8,128)(2,1)} %collective-permute-done.55), channel_id=1, source_target_pairs={{0,2},{2,0},{12,14},{14,12},{1,3},{3,1},{13,15},{15,13},{16,18},{1... | collective-permute-start | bytes 688136 | tf_op jit(solution)/shard_map/ppermute | solution.py:100
  296.3 6.3 %fusion.6 = f32[512,1792]{1,0:T(8,128)S(1)} fusion(bf16[512,1792]{1,0:T(8,128)(2,1)S(1)} %select_dynamic-update-slice_fusion.15, bf16[14336,1792]{1,0:T(8,128)(2,1)} %param.6), kind=kOutput, calls=%fused_computation.6 | convolution fusion | flops 3288334336 | bytes 11927552 | tf_op jit(solution)/shard_map/dot_general | solution.py:16
  307.4 3.4 collective-permute-done.65
  317.3 6.3 %fusion.4 = f32[512,1792]{1,0:T(8,128)S(1)} fusion(bf16[512,1792]{1,0:T(8,128)(2,1)S(1)} %get-tuple-element.228, bf16[14336,1792]{1,0:T(8,128)(2,1)} %param.6), kind=kOutput, calls=%fused_computation.4 | convolution fusion | flops 3288334336 | bytes 11927552 | tf_op jit(solution)/shard_map/dot_general | solution.py:16
  326.7 7.0 %fusion.2 = f32[512,1792]{1,0:T(8,128)S(1)} fusion(bf16[512,1792]{1,0:T(8,128)(2,1)} %select_dynamic-update-slice_fusion.5, bf16[14336,1792]{1,0:T(8,128)(2,1)} %param.6), kind=kOutput, calls=%fused_computation.2 | convolution fusion | flops 3288334336 | bytes 11927552 | tf_op jit(solution)/shard_map/dot_general | solution.py:16
  335.2 6.3 %fusion = f32[512,1792]{1,0:T(8,128)S(1)} fusion(bf16[512,1792]{1,0:T(8,128)(2,1)S(1)} %select_dynamic-update-slice_fusion, bf16[14336,1792]{1,0:T(8,128)(2,1)} %param.6), kind=kOutput, calls=%fused_computation | convolution fusion | flops 3288334336 | bytes 11927552 | tf_op jit(solution)/shard_map/dot_general | solution.py:16
  344.0 6.7 %collective-permute-done.72.other_ref = f32[512,1792]{1,0:T(8,128)} collective-permute-done((f32[512,1792]{1,0:T(8,128)}, f32[512,1792]{1,0:T(8,128)}, u32[]{:S(2)}, u32[]{:S(2)}) %collective-permute-start.72) | collective-permute-done | bytes 3670048 | tf_op jit(solution)/shard_map/ppermute | solution.py:68
  350.6 12.4 %fit.1 = f32[1792,2048]{1,0:T(8,128)} custom-call(s32[8]{0:T(128)S(1)} %stack.35.order_ref, f32[512,1792]{1,0:T(8,128)} %add.67.mine_ref, f32[512,1792]{1,0:T(8,128)} %collective-permute-done.72.other_ref, bf16[512,2048]{1,0:T(8,128)(2,1)S(1)} %copy-done.2), custom_call_target="tpu_custom_call" | custom-call | flops 3758096384 | bytes 24117248 | tf_op jit(solution)/shard_map/fit/pallas_call | solution.py:43
  (269 shorter events, 137.9 us)
Async XLA Ops:
  6.5 193.7 %reduce-scatter.2.cloned.1.call-start = ((), (), s32[]{:S(2)}) async-start(), calls=%async_computation.1 | async-start | bytes 4718592 | tf_op jit(solution)/shard_map/reduce_scatter | solution.py:146
  25.1 300.8 %all-gather.2.cloned.1.call-start = ((), (), s32[]{:S(2)}) async-start(), calls=%async_computation.2 | async-start | bytes 2359296 | tf_op jit(solution)/shard_map/all_gather | solution.py:168
  26.6 31.5 %collective-permute-start.29 = (bf16[64,1792]{1,0:T(8,128)(2,1)S(1)}, bf16[64,1792]{1,0:T(8,128)(2,1)S(1)}, u32[]{:S(2)}, u32[]{:S(2)}) collective-permute-start(bf16[64,1792]{1,0:T(8,128)(2,1)S(1)} %get-tuple-element.110), channel_id=1, source_target_pairs={{0,4},{2,6},{4,0},{6,2},{8,12},{10,14},{12,8},{14,10},{1,5},{3,7},... | collective-permute-start | bytes 688136 | tf_op jit(solution)/shard_map/ppermute | solution.py:100
  28.0 33.1 %collective-permute-start.30 = (bf16[64,1792]{1,0:T(8,128)(2,1)S(1)}, bf16[64,1792]{1,0:T(8,128)(2,1)S(1)}, u32[]{:S(2)}, u32[]{:S(2)}) collective-permute-start(bf16[64,1792]{1,0:T(8,128)(2,1)S(1)} %get-tuple-element.110), channel_id=1, source_target_pairs={{0,2},{2,0},{4,6},{6,4},{8,10},{10,8},{12,14},{14,12},{1,3},{3,1},... | collective-permute-start | bytes 688136 | tf_op jit(solution)/shard_map/ppermute | solution.py:100
  31.3 30.5 %collective-permute-start.31 = (bf16[64,1792]{1,0:T(8,128)(2,1)S(1)}, bf16[64,1792]{1,0:T(8,128)(2,1)S(1)}, u32[]{:S(2)}, u32[]{:S(2)}) collective-permute-start(bf16[64,1792]{1,0:T(8,128)(2,1)S(1)} %get-tuple-element.110), channel_id=1, source_target_pairs={{4,8},{6,10},{8,4},{10,6},{5,9},{7,11},{9,5},{11,7},{20,24},{22,26... | collective-permute-start | bytes 688136 | tf_op jit(solution)/shard_map/ppermute | solution.py:100
  32.0 30.5 %collective-permute-start.32 = (bf16[64,1792]{1,0:T(8,128)(2,1)}, bf16[64,1792]{1,0:T(8,128)(2,1)S(1)}, u32[]{:S(2)}, u32[]{:S(2)}) collective-permute-start(bf16[64,1792]{1,0:T(8,128)(2,1)} %collective-permute-done.26), channel_id=1, source_target_pairs={{4,8},{6,10},{8,4},{10,6},{5,9},{7,11},{9,5},{11,7},{20,24},{22,26... | collective-permute-start | bytes 688136 | tf_op jit(solution)/shard_map/ppermute | solution.py:100
  58.1 27.3 %collective-permute-start.3 = (bf16[64,1792]{1,0:T(8,128)(2,1)S(1)}, bf16[64,1792]{1,0:T(8,128)(2,1)S(1)}, u32[]{:S(2)}, u32[]{:S(2)}) collective-permute-start(bf16[64,1792]{1,0:T(8,128)(2,1)S(1)} %get-tuple-element.92), channel_id=1, source_target_pairs={{0,4},{2,6},{4,0},{6,2},{8,12},{10,14},{12,8},{14,10},{1,5},{3,7},... | collective-permute-start | bytes 688136 | tf_op jit(solution)/shard_map/ppermute | solution.py:100
  58.1 28.8 %collective-permute-start.4 = (bf16[64,1792]{1,0:T(8,128)(2,1)S(1)}, bf16[64,1792]{1,0:T(8,128)(2,1)S(1)}, u32[]{:S(2)}, u32[]{:S(2)}) collective-permute-start(bf16[64,1792]{1,0:T(8,128)(2,1)S(1)} %get-tuple-element.92), channel_id=1, source_target_pairs={{0,2},{2,0},{4,6},{6,4},{8,10},{10,8},{12,14},{14,12},{1,3},{3,1},... | collective-permute-start | bytes 688136 | tf_op jit(solution)/shard_map/ppermute | solution.py:100
  61.1 26.3 %collective-permute-start.5 = (bf16[64,1792]{1,0:T(8,128)(2,1)S(1)}, bf16[64,1792]{1,0:T(8,128)(2,1)S(1)}, u32[]{:S(2)}, u32[]{:S(2)}) collective-permute-start(bf16[64,1792]{1,0:T(8,128)(2,1)S(1)} %get-tuple-element.92), channel_id=1, source_target_pairs={{4,8},{6,10},{8,4},{10,6},{5,9},{7,11},{9,5},{11,7},{20,24},{22,26... | collective-permute-start | bytes 688136 | tf_op jit(solution)/shard_map/ppermute | solution.py:100
  61.8 26.3 %collective-permute-start.6 = (bf16[64,1792]{1,0:T(8,128)(2,1)}, bf16[64,1792]{1,0:T(8,128)(2,1)S(1)}, u32[]{:S(2)}, u32[]{:S(2)}) collective-permute-start(bf16[64,1792]{1,0:T(8,128)(2,1)} %collective-permute-done), channel_id=1, source_target_pairs={{4,8},{6,10},{8,4},{10,6},{5,9},{7,11},{9,5},{11,7},{20,24},{22,26... | collective-permute-start | bytes 688136 | tf_op jit(solution)/shard_map/ppermute | solution.py:100
  83.7 25.7 %collective-permute-start.35 = (bf16[64,1792]{1,0:T(8,128)(2,1)S(1)}, bf16[64,1792]{1,0:T(8,128)(2,1)S(1)}, u32[]{:S(2)}, u32[]{:S(2)}) collective-permute-start(bf16[64,1792]{1,0:T(8,128)(2,1)S(1)} %get-tuple-element.114), channel_id=1, source_target_pairs={{0,4},{2,6},{4,0},{6,2},{8,12},{10,14},{12,8},{14,10},{1,5},{3,7},... | collective-permute-start | bytes 688136 | tf_op jit(solution)/shard_map/ppermute | solution.py:100
  85.4 25.1 %collective-permute-start.36 = (bf16[64,1792]{1,0:T(8,128)(2,1)S(1)}, bf16[64,1792]{1,0:T(8,128)(2,1)S(1)}, u32[]{:S(2)}, u32[]{:S(2)}) collective-permute-start(bf16[64,1792]{1,0:T(8,128)(2,1)S(1)} %get-tuple-element.114), channel_id=1, source_target_pairs={{0,2},{2,0},{4,6},{6,4},{8,10},{10,8},{12,14},{14,12},{1,3},{3,1},... | collective-permute-start | bytes 688136 | tf_op jit(solution)/shard_map/ppermute | solution.py:100
  88.2 19.3 %collective-permute-start.42 = (bf16[64,1792]{1,0:T(8,128)(2,1)S(1)}, bf16[64,1792]{1,0:T(8,128)(2,1)S(1)}, u32[]{:S(2)}, u32[]{:S(2)}) collective-permute-start(bf16[64,1792]{1,0:T(8,128)(2,1)S(1)} %get-tuple-element.222), channel_id=1, source_target_pairs={{0,2},{2,0},{4,6},{6,4},{8,10},{10,8},{12,14},{14,12},{1,3},{3,1},... | collective-permute-start | bytes 688136 | tf_op jit(solution)/shard_map/ppermute | solution.py:100
  109.4 27.2 %collective-permute-start.10 = (bf16[64,1792]{1,0:T(8,128)(2,1)S(1)}, bf16[64,1792]{1,0:T(8,128)(2,1)S(1)}, u32[]{:S(2)}, u32[]{:S(2)}) collective-permute-start(bf16[64,1792]{1,0:T(8,128)(2,1)S(1)} %get-tuple-element.96), channel_id=1, source_target_pairs={{0,2},{2,0},{4,6},{6,4},{8,10},{10,8},{12,14},{14,12},{1,3},{3,1},... | collective-permute-start | bytes 688136 | tf_op jit(solution)/shard_map/ppermute | solution.py:100
  110.5 26.3 %collective-permute-start.11 = (bf16[64,1792]{1,0:T(8,128)(2,1)S(1)}, bf16[64,1792]{1,0:T(8,128)(2,1)S(1)}, u32[]{:S(2)}, u32[]{:S(2)}) collective-permute-start(bf16[64,1792]{1,0:T(8,128)(2,1)S(1)} %get-tuple-element.96), channel_id=1, source_target_pairs={{4,8},{6,10},{8,4},{10,6},{5,9},{7,11},{9,5},{11,7},{20,24},{22,26... | collective-permute-start | bytes 688136 | tf_op jit(solution)/shard_map/ppermute | solution.py:100
  112.2 18.4 %collective-permute-start.13 = (bf16[64,1792]{1,0:T(8,128)(2,1)S(1)}, bf16[64,1792]{1,0:T(8,128)(2,1)S(1)}, u32[]{:S(2)}, u32[]{:S(2)}) collective-permute-start(bf16[64,1792]{1,0:T(8,128)(2,1)S(1)} %get-tuple-element.210), channel_id=1, source_target_pairs={{0,2},{2,0},{4,6},{6,4},{8,10},{10,8},{12,14},{14,12},{1,3},{3,1},... | collective-permute-start | bytes 688136 | tf_op jit(solution)/shard_map/ppermute | solution.py:100
  136.6 23.7 %collective-permute-start.43 = (bf16[64,1792]{1,0:T(8,128)(2,1)S(1)}, bf16[64,1792]{1,0:T(8,128)(2,1)S(1)}, u32[]{:S(2)}, u32[]{:S(2)}) collective-permute-start(bf16[64,1792]{1,0:T(8,128)(2,1)S(1)} %get-tuple-element.122), channel_id=1, source_target_pairs={{0,4},{2,6},{4,0},{6,2},{8,12},{10,14},{12,8},{14,10},{1,5},{3,7},... | collective-permute-start | bytes 688136 | tf_op jit(solution)/shard_map/ppermute | solution.py:100
  136.7 27.2 %collective-permute-start.44 = (bf16[64,1792]{1,0:T(8,128)(2,1)S(1)}, bf16[64,1792]{1,0:T(8,128)(2,1)S(1)}, u32[]{:S(2)}, u32[]{:S(2)}) collective-permute-start(bf16[64,1792]{1,0:T(8,128)(2,1)S(1)} %get-tuple-element.122), channel_id=1, source_target_pairs={{0,2},{2,0},{4,6},{6,4},{8,10},{10,8},{12,14},{14,12},{1,3},{3,1},... | collective-permute-start | bytes 688136 | tf_op jit(solution)/shard_map/ppermute | solution.py:100
  163.9 22.6 %collective-permute-start.17 = (bf16[64,1792]{1,0:T(8,128)(2,1)S(1)}, bf16[64,1792]{1,0:T(8,128)(2,1)}, u32[]{:S(2)}, u32[]{:S(2)}) collective-permute-start(bf16[64,1792]{1,0:T(8,128)(2,1)S(1)} %get-tuple-element.102), channel_id=1, source_target_pairs={{0,4},{2,6},{4,0},{6,2},{8,12},{10,14},{12,8},{14,10},{1,5},{3,7},... | collective-permute-start | bytes 688136 | tf_op jit(solution)/shard_map/ppermute | solution.py:100
  165.1 24.6 %collective-permute-start.18 = (bf16[64,1792]{1,0:T(8,128)(2,1)S(1)}, bf16[64,1792]{1,0:T(8,128)(2,1)S(1)}, u32[]{:S(2)}, u32[]{:S(2)}) collective-permute-start(bf16[64,1792]{1,0:T(8,128)(2,1)S(1)} %get-tuple-element.102), channel_id=1, source_target_pairs={{0,2},{2,0},{4,6},{6,4},{8,10},{10,8},{12,14},{14,12},{1,3},{3,1},... | collective-permute-start | bytes 688136 | tf_op jit(solution)/shard_map/ppermute | solution.py:100
  189.7 29.4 %collective-permute-start.58 = (bf16[64,1792]{1,0:T(8,128)(2,1)S(1)}, bf16[64,1792]{1,0:T(8,128)(2,1)}, u32[]{:S(2)}, u32[]{:S(2)}) collective-permute-start(bf16[64,1792]{1,0:T(8,128)(2,1)S(1)} %collective-permute-done.43), channel_id=1, source_target_pairs={{4,8},{6,10},{8,4},{10,6},{5,9},{7,11},{9,5},{11,7},{20,24},{22,26... | collective-permute-start | bytes 688136 | tf_op jit(solution)/shard_map/ppermute | solution.py:100
  191.1 28.0 %collective-permute-start.61 = (bf16[64,1792]{1,0:T(8,128)(2,1)}, bf16[64,1792]{1,0:T(8,128)(2,1)}, u32[]{:S(2)}, u32[]{:S(2)}) collective-permute-start(bf16[64,1792]{1,0:T(8,128)(2,1)} %collective-permute-done.46), channel_id=1, source_target_pairs={{4,0},{6,2},{8,12},{10,14},{5,1},{7,3},{9,13},{11,15},{20,16},{22,... | collective-permute-start | bytes 688136 | tf_op jit(solution)/shard_map/ppermute | solution.py:100
  192.4 26.7 %collective-permute-start.63 = (bf16[64,1792]{1,0:T(8,128)(2,1)}, bf16[64,1792]{1,0:T(8,128)(2,1)}, u32[]{:S(2)}, u32[]{:S(2)}) collective-permute-start(bf16[64,1792]{1,0:T(8,128)(2,1)} %collective-permute-done.49), channel_id=1, source_target_pairs={{0,2},{2,0},{12,14},{14,12},{1,3},{3,1},{13,15},{15,13},{16,18},{1... | collective-permute-start | bytes 688136 | tf_op jit(solution)/shard_map/ppermute | solution.py:100
  215.0 51.0 %collective-permute-start.57 = (bf16[64,1792]{1,0:T(8,128)(2,1)}, bf16[64,1792]{1,0:T(8,128)(2,1)}, u32[]{:S(2)}, u32[]{:S(2)}) collective-permute-start(bf16[64,1792]{1,0:T(8,128)(2,1)} %collective-permute-done.23), channel_id=1, source_target_pairs={{0,2},{2,0},{12,14},{14,12},{1,3},{3,1},{13,15},{15,13},{16,18},{1... | collective-permute-start | bytes 688136 | tf_op jit(solution)/shard_map/ppermute | solution.py:100
  228.4 37.6 %collective-permute-start.55 = (bf16[64,1792]{1,0:T(8,128)(2,1)}, bf16[64,1792]{1,0:T(8,128)(2,1)}, u32[]{:S(2)}, u32[]{:S(2)}) collective-permute-start(bf16[64,1792]{1,0:T(8,128)(2,1)} %collective-permute-done.20), channel_id=1, source_target_pairs={{4,0},{6,2},{8,12},{10,14},{5,1},{7,3},{9,13},{11,15},{20,16},{22,... | collective-permute-start | bytes 688136 | tf_op jit(solution)/shard_map/ppermute | solution.py:100
  231.3 32.5 %collective-permute-start.52 = (bf16[64,1792]{1,0:T(8,128)(2,1)}, bf16[64,1792]{1,0:T(8,128)(2,1)}, u32[]{:S(2)}, u32[]{:S(2)}) collective-permute-start(bf16[64,1792]{1,0:T(8,128)(2,1)} %collective-permute-done.17), channel_id=1, source_target_pairs={{4,8},{6,10},{8,4},{10,6},{5,9},{7,11},{9,5},{11,7},{20,24},{22,26... | collective-permute-start | bytes 688136 | tf_op jit(solution)/shard_map/ppermute | solution.py:100
  234.5 19.9 %collective-permute-start.53 = (bf16[64,1792]{1,0:T(8,128)(2,1)}, bf16[64,1792]{1,0:T(8,128)(2,1)S(1)}, u32[]{:S(2)}, u32[]{:S(2)}) collective-permute-start(bf16[64,1792]{1,0:T(8,128)(2,1)} %get-tuple-element.190), channel_id=1, source_target_pairs={{0,2},{2,0},{4,6},{6,4},{8,10},{10,8},{12,14},{14,12},{1,3},{3,1},... | collective-permute-start | bytes 688136 | tf_op jit(solution)/shard_map/ppermute | solution.py:100
  243.0 19.0 %collective-permute-start.54 = (bf16[64,1792]{1,0:T(8,128)(2,1)}, bf16[64,1792]{1,0:T(8,128)(2,1)S(1)}, u32[]{:S(2)}, u32[]{:S(2)}) collective-permute-start(bf16[64,1792]{1,0:T(8,128)(2,1)} %get-tuple-element.191), channel_id=1, source_target_pairs={{0,4},{2,6},{4,0},{6,2},{8,12},{10,14},{12,8},{14,10},{1,5},{3,7},... | collective-permute-start | bytes 688136 | tf_op jit(solution)/shard_map/ppermute | solution.py:100
  254.5 23.4 %collective-permute-start.67 = (bf16[64,1792]{1,0:T(8,128)(2,1)}, bf16[64,1792]{1,0:T(8,128)(2,1)S(1)}, u32[]{:S(2)}, u32[]{:S(2)}) collective-permute-start(bf16[64,1792]{1,0:T(8,128)(2,1)} %collective-permute-done.58), channel_id=1, source_target_pairs={{4,0},{6,2},{8,12},{10,14},{5,1},{7,3},{9,13},{11,15},{20,16},{22,... | collective-permute-start | bytes 688136 | tf_op jit(solution)/shard_map/ppermute | solution.py:100
  277.9 48.0 %collective-permute-start.71 = (bf16[64,1792]{1,0:T(8,128)(2,1)S(1)}, bf16[64,1792]{1,0:T(8,128)(2,1)S(1)}, u32[]{:S(2)}, u32[]{:S(2)}) collective-permute-start(bf16[64,1792]{1,0:T(8,128)(2,1)S(1)} %collective-permute-done.67), channel_id=1, source_target_pairs={{0,2},{2,0},{12,14},{14,12},{1,3},{3,1},{13,15},{15,13},{16,18},{1... | collective-permute-start | bytes 688136 | tf_op jit(solution)/shard_map/ppermute | solution.py:100
  281.8 29.1 %collective-permute-start.66 = (bf16[64,1792]{1,0:T(8,128)(2,1)}, bf16[64,1792]{1,0:T(8,128)(2,1)S(1)}, u32[]{:S(2)}, u32[]{:S(2)}) collective-permute-start(bf16[64,1792]{1,0:T(8,128)(2,1)} %collective-permute-done.55), channel_id=1, source_target_pairs={{0,2},{2,0},{12,14},{14,12},{1,3},{3,1},{13,15},{15,13},{16,18},{1... | collective-permute-start | bytes 688136 | tf_op jit(solution)/shard_map/ppermute | solution.py:100
  310.9 23.2 %collective-permute-start.70 = (bf16[64,1792]{1,0:T(8,128)(2,1)}, bf16[64,1792]{1,0:T(8,128)(2,1)S(1)}, u32[]{:S(2)}, u32[]{:S(2)}) collective-permute-start(bf16[64,1792]{1,0:T(8,128)(2,1)} %collective-permute-done.64), channel_id=1, source_target_pairs={{0,2},{2,0},{12,14},{14,12},{1,3},{3,1},{13,15},{15,13},{16,18},{1... | collective-permute-start | bytes 688136 | tf_op jit(solution)/shard_map/ppermute | solution.py:100
  (76 other events, 971.8 us)
Sparse Core Ops, SparseCore 0:
  25.2 118.5 reduce-scatter.1
  239.1 55.1 all-gather.1

commit v3 on v1

v3 whole, which is shorter than its diff:
```python
import jax
import jax.numpy as jnp
from jax import lax
from jax.experimental import pallas as pl
from jax.experimental.pallas import tpu as pltpu
from jax.sharding import Mesh
from jax.sharding import PartitionSpec as P

EX = 2
BF16, F32 = jnp.bfloat16, jnp.float32


def dot(a, b):
    return jnp.dot(a, b, preferred_element_type=F32)


def fit_kernel(order_ref, mine_ref, other_ref, out_ref, fit_ref, rot_ref):
    rows, blocks = mine_ref.shape[0], order_ref.shape[0]
    size, seq = rows // blocks, rows // EX
    for slot in range(blocks):
        here = pl.ds(slot * size, size)
        there = pl.ds(pl.multiple_of(order_ref[slot] * size, size), size)
        rot_ref[there, :] = mine_ref[here, :] + other_ref[here, :]
    total = None
    for e in range(EX):
        here = pl.ds(e * seq, seq)
        grad = lax.dot_general(
            rot_ref[here, :].astype(BF16),
            out_ref[here, :],
            (((0,), (0,)), ((), ())),
            preferred_element_type=F32,
        )
        total = grad * grad if total is None else total + grad * grad
    fit_ref[...] = total * (1.0 / EX)


def fit(order, mine, other, rotated_out):
    rows, ka = mine.shape
    ks = rotated_out.shape[1]
    tile = 256 if ka % 256 == 0 else ka
    return pl.pallas_call(
        fit_kernel,
        out_shape=jax.ShapeDtypeStruct((ka, ks), F32),
        grid_spec=pltpu.PrefetchScalarGridSpec(
            num_scalar_prefetch=1,
            grid=(ka // tile,),
            in_specs=[
                pl.BlockSpec((rows, tile), lambda i, o: (0, i)),
                pl.BlockSpec((rows, tile), lambda i, o: (0, i)),
                pl.BlockSpec((rows, ks), lambda i, o: (0, 0)),
            ],
            out_specs=pl.BlockSpec((tile, ks), lambda i, o: (i, 0)),
            scratch_shapes=[pltpu.VMEM((rows, tile), F32)],
        ),
        compiler_params=pltpu.CompilerParams(vmem_limit_bytes=48 << 20),
        cost_estimate=pl.CostEstimate(
            flops=2 * rows * ka * ks,
            bytes_accessed=8 * rows * ka + 2 * rows * ks + 4 * ka * ks,
            transcendentals=0,
        ),
        name="fit",
    )(order, mine, other, rotated_out)


def swap_narrow(a):
    return lax.ppermute(a, "narrow", [(0, 1), (1, 0)])


def rotate_kernel(*refs):
    mine_ref, other_ref, basis_ref, total_ref, sum_ref = refs if len(refs) == 5 else (*refs[:3], None, refs[3])
    half = mine_ref.shape[0]
    for at, ref in ((0, mine_ref), (half, other_ref)):
        here = pl.ds(at, half)
        term = dot(ref[...], basis_ref[...])
        sum_ref[here, :] = term if total_ref is None else total_ref[here, :] + term


def rotate(total, mine, other, basis, chunk):
    half, width = mine.shape
    ka = basis.shape[1]
    tile = 256 if ka % 256 == 0 else ka
    rows = pl.BlockSpec((half, width), lambda j: (0, 0))
    sums = pl.BlockSpec((2 * half, tile), lambda j: (0, j))
    arrays = [mine, other, basis] + ([] if total is None else [total])
    return pl.pallas_call(
        rotate_kernel,
        out_shape=jax.ShapeDtypeStruct((2 * half, ka), F32),
        grid=(ka // tile,),
        in_specs=[rows, rows, pl.BlockSpec((width, tile), lambda j: (chunk, j)), sums][: len(arrays)],
        out_specs=sums,
        input_output_aliases={} if total is None else {3: 0},
        compiler_params=pltpu.CompilerParams(vmem_limit_bytes=40 << 20),
        cost_estimate=pl.CostEstimate(
            flops=4 * half * width * ka, bytes_accessed=4 * half * width + 2 * width * ka + 16 * half * ka, transcendentals=0
        ),
        name="rotate",
    )(*arrays)


def general(inputs, deltas, basis_in, basis_out):
    wide = ("line", "pair")
    partial_in = dot(lax.all_gather(inputs, wide, axis=0, tiled=True), basis_in)
    rotated_out = lax.psum(dot(deltas, basis_out), wide).astype(BF16)
    order = jnp.arange(EX, dtype=jnp.int32)
    return fit(order, partial_in, swap_narrow(partial_in), rotated_out)


def swap_pair(a):
    return lax.ppermute(a, "pair", [(0, 1), (1, 0)])


def gather_line(a):
    return lax.all_gather(a, "line", axis=0, tiled=True)


CHUNKS = 8
PAIR_FIRST = (0, 1)
ORDER = (2, 3, 0, 4, 1, 5, 6, 7)


def scheduled(inputs, deltas, basis_in, basis_out):
    lines = lax.axis_size("line")
    x = lax.axis_index("pair")
    width = inputs.shape[1] // CHUNKS
    own = [inputs[:, c * width : (c + 1) * width] for c in range(CHUNKS)]

    partial_out = dot(deltas, basis_out)
    ks = partial_out.shape[1] // 2
    keep = lax.dynamic_slice_in_dim(partial_out, x * ks, ks, 1)
    give = lax.dynamic_slice_in_dim(partial_out, (1 - x) * ks, ks, 1)
    crossed = {c: swap_pair(own[c]) for c in PAIR_FIRST}
    sums = keep + swap_pair(give)

    mine, other, total, out = {}, {}, None, None
    for i, c in enumerate(ORDER):
        mine[c] = gather_line(own[c])
        if c in PAIR_FIRST:
            other[c] = gather_line(crossed[c])
        if i == 4:
            sums = lax.psum_scatter(sums, "line", scatter_dimension=0, tiled=True).astype(BF16)
        if i == 6:
            sums = gather_line(sums)
    for i, c in enumerate(ORDER):
        before = ORDER[i - 2] if i >= 2 else None
        held = [mine[c]] + ([other[before]] if i >= 2 else []) + ([total] if i >= 3 else [])
        held = lax.optimization_barrier(tuple(held))
        mine[c] = held[0]
        if i >= 2:
            other[before] = held[1]
        if i >= 3:
            total = held[2]
        if c not in PAIR_FIRST:
            other[c] = swap_pair(mine[c])
        if i >= 2:
            total = rotate(total, mine[before], other[before], basis_in, before)
    sums, total = lax.optimization_barrier((sums, total))
    far = swap_pair(sums)
    for c in ORDER[-2:]:
        total = rotate(total, mine[c], other[c], basis_in, c)
    rotated_out = jnp.where(x == 0, jnp.concatenate([sums, far], 1), jnp.concatenate([far, sums], 1))
    order = jnp.concatenate([2 * jnp.arange(lines) + x, 2 * jnp.arange(lines) + 1 - x]).astype(jnp.int32)
    return fit(order, total, swap_narrow(total), rotated_out)


def solution(mesh):
    grp, wide, narrow = (mesh.shape[name] for name in ("grp", "wide", "narrow"))
    devices = mesh.devices.reshape(grp, wide, narrow)
    columns = len({getattr(d, "coords", (i % 2,))[0] for i, d in enumerate(devices[0, :, 0])})
    grid = Mesh(devices.reshape(grp, wide // columns, columns, narrow), ("grp", "line", "pair", "narrow"))
    wide = ("line", "pair")
    return jax.shard_map(
        scheduled if columns == 2 else general,
        mesh=grid,
        in_specs=(
            P(("grp", *wide), "narrow"),
            P("grp", wide),
            P(("grp", "narrow"), wide),
            P(("grp", *wide), "narrow"),
        ),
        out_specs=P(("grp", *wide), "narrow"),
        check_vma=False,
    )
```

time: 389 us -> 431 us (1.11)
  blocking collectives: 0 us -> 224 us
  waiting for transfers between devices: 214 us -> 69.7 us
  Pallas kernels: 12.4 us -> 88.5 us
  starting transfers between devices: 83.3 us -> 13.5 us
  matrix products: 51.9 us -> 4.52 us
    all_gather x0 -> x10, blocking collectives: none -> 224 us  [gather_line(): return lax.all_gather(a, 'line', axis=0, tiled=True)]
    ppermute x36 -> x10, waiting for transfers between devices: 165 us -> 69.7 us  [swap_pair(): return lax.ppermute(a, 'pair', [(0, 1), (1, 0)])]
    pallas_call x0 -> x8, Pallas kernels: none -> 76.1 us  [rotate(): pl.pallas_call(rotate_kernel, out_shape=jax.ShapeDtypeStruct((2 * half, k...]
    ppermute x36 -> x10, starting transfers between devices: 83.2 us -> 13.4 us  [swap_pair(): return lax.ppermute(a, 'pair', [(0, 1), (1, 0)])]
    dot_general x5 -> x1, matrix products: 51.9 us -> 4.52 us  [dot(): return jnp.dot(a, b, preferred_element_type=F32)]
    all_gather x1, waiting for transfers between devices: 44.1 us -> 0.01 us  [gather_line(): return lax.all_gather(a, 'line', axis=0, tiled=True)]
    ppermute x1, waiting for transfers between devices: 4.83 us -> 0.01 us  [swap_narrow(): return lax.ppermute(a, 'narrow', [(0, 1), (1, 0)])]
  transfers between devices with their start and end apart: 39 -> 13, of which waited for: 18 -> 2; matrix products, arithmetic and copies ran while one was open for 15% -> 1% of each run, Pallas kernels for 0% -> 15%
where the time goes in v3:
time: 431 us; the launch traced here: 429 us
  blocking collectives  224 us (52%)
  Pallas kernels  88.5 us (21%)
  waiting for transfers between devices  69.7 us (16%)
  starting transfers between devices  13.5 us (3%)
  between operations  13.5 us (3%)
  local copies, waits for them, and re-layouts  8.76 us (2%)
  other arithmetic  6.01 us (1%)
  matrix products  4.52 us (1%)
    all_gather x10, blocking collectives, gather_line(): return lax.all_gather(a, 'line', axis=0, tiled=True)  224 us
    pallas_call x8, Pallas kernels, rotate(): pl.pallas_call(rotate_kernel, out_shape=jax.ShapeDtypeStruct((2 * half, k...  76.1 us
    ppermute x10, waiting for transfers between devices, swap_pair(): return lax.ppermute(a, 'pair', [(0, 1), (1, 0)])  69.7 us
    ppermute x10, starting transfers between devices, swap_pair(): return lax.ppermute(a, 'pair', [(0, 1), (1, 0)])  13.4 us
    pallas_call x1, Pallas kernels, fit(): pl.pallas_call(fit_kernel, out_shape=jax.ShapeDtypeStruct((ka, ks), F32),...  12.5 us
  transfers between devices with their start and end apart: 13, of which 2 were waited for; matrix products, arithmetic and copies ran while one was open for 1% of the time, Pallas kernels for 15%

profile of v3, /device:TPU:0, one launch (start us, length us, event | category | flops | bytes accessed | tf_op | source)
XLA Modules:
  0.0 428.6 jit_solution(16587687246881302592)
XLA Ops:
  7.8 4.5 %fusion.2 = f32[512,2048]{1,0:T(8,128)S(1)} fusion(bf16[512,1024]{1,0:T(8,128)(2,1)S(1)} %copy-done, bf16[1024,2048]{1,0:T(8,128)(2,1)} %param.7), kind=kOutput, calls=%fused_computation.8 | convolution fusion | flops 2147483648 | bytes 9437184 | tf_op jit(solution)/shard_map/dot_general | solution.py:14
  12.3 2.0 copy-done.5
  14.3 1.5 constant_dynamic-slice_fusion
  15.8 2.9 collective-permute-start.8
  18.7 45.8 %collective-permute-done.8 = f32[512,1024]{1,0:T(8,128)S(1)} collective-permute-done((f32[512,1024]{1,0:T(8,128)}, f32[512,1024]{1,0:T(8,128)S(1)}, u32[]{:S(2)}, u32[]{:S(2)}) %collective-permute-start.8) | collective-permute-done | bytes 2097184 | tf_op jit(solution)/shard_map/ppermute | solution.py:109
  64.5 3.4 dynamic-slice_add_fusion
  68.0 1.7 fusion.1
  69.7 1.8 collective-permute-start.3
  71.8 33.8 %all_gather.36.refs_0_ = bf16[256,1792]{1,0:T(8,128)(2,1)S(1)} all-gather(bf16[64,1792]{1,0:T(8,128)(2,1)S(1)} %get-tuple-element.46), channel_id=1, replica_groups=mesh['grp'=2,'line'=4,'pair'=2,'narrow'=2] {'line'}, dimensions={0}, use_global_device_ids=true | all-gather | bytes 1146880 | tf_op jit(solution)/shard_map/all_gather | solution.py:113
  106.8 32.1 %all_gather.37.refs_0_ = bf16[256,1792]{1,0:T(8,128)(2,1)S(1)} all-gather(bf16[64,1792]{1,0:T(8,128)(2,1)S(1)} %get-tuple-element.45), channel_id=1, replica_groups=mesh['grp'=2,'line'=4,'pair'=2,'narrow'=2] {'line'}, dimensions={0}, use_global_device_ids=true | all-gather | bytes 1146880 | tf_op jit(solution)/shard_map/all_gather | solution.py:113
  140.4 20.5 %all_gather.38.refs_0_ = bf16[256,1792]{1,0:T(8,128)(2,1)} all-gather(bf16[64,1792]{1,0:T(8,128)(2,1)S(1)} %get-tuple-element.44), channel_id=1, replica_groups=mesh['grp'=2,'line'=4,'pair'=2,'narrow'=2] {'line'}, dimensions={0}, use_global_device_ids=true | all-gather | bytes 1146880 | tf_op jit(solution)/shard_map/all_gather | solution.py:113
  160.9 19.4 %all_gather.39.refs_0_ = bf16[256,1792]{1,0:T(8,128)(2,1)} all-gather(bf16[64,1792]{1,0:T(8,128)(2,1)S(1)} %get-tuple-element.50), channel_id=1, replica_groups=mesh['grp'=2,'line'=4,'pair'=2,'narrow'=2] {'line'}, dimensions={0}, use_global_device_ids=true | all-gather | bytes 1146880 | tf_op jit(solution)/shard_map/all_gather | solution.py:113
  180.3 19.0 %all_gather.41.refs_0_ = bf16[256,1792]{1,0:T(8,128)(2,1)S(1)} all-gather(bf16[64,1792]{1,0:T(8,128)(2,1)S(1)} %get-tuple-element.43), channel_id=1, replica_groups=mesh['grp'=2,'line'=4,'pair'=2,'narrow'=2] {'line'}, dimensions={0}, use_global_device_ids=true | all-gather | bytes 1146880 | tf_op jit(solution)/shard_map/all_gather | solution.py:113
  199.4 20.3 %all_gather.35.refs_0_ = bf16[256,1792]{1,0:T(8,128)(2,1)} all-gather(bf16[64,1792]{1,0:T(8,128)(2,1)S(1)} %get-tuple-element.47), channel_id=1, replica_groups=mesh['grp'=2,'line'=4,'pair'=2,'narrow'=2] {'line'}, dimensions={0}, use_global_device_ids=true | all-gather | bytes 1146880 | tf_op jit(solution)/shard_map/all_gather | solution.py:113
  219.6 20.2 %all_gather.34.refs_0_ = bf16[256,1792]{1,0:T(8,128)(2,1)S(1)} all-gather(bf16[64,1792]{1,0:T(8,128)(2,1)S(1)} %get-tuple-element.48), channel_id=1, replica_groups=mesh['grp'=2,'line'=4,'pair'=2,'narrow'=2] {'line'}, dimensions={0}, use_global_device_ids=true | all-gather | bytes 1146880 | tf_op jit(solution)/shard_map/all_gather | solution.py:113
  239.8 18.4 %all_gather.33.refs_0_ = bf16[256,1792]{1,0:T(8,128)(2,1)S(1)} all-gather(bf16[64,1792]{1,0:T(8,128)(2,1)S(1)} %get-tuple-element.49), channel_id=1, replica_groups=mesh['grp'=2,'line'=4,'pair'=2,'narrow'=2] {'line'}, dimensions={0}, use_global_device_ids=true | all-gather | bytes 1146880 | tf_op jit(solution)/shard_map/all_gather | solution.py:113
  258.2 8.7 %rotate.8.refs_3_ = f32[512,1792]{1,0:T(8,128)} custom-call(bf16[256,1792]{1,0:T(8,128)(2,1)S(1)} %all_gather.37.refs_0_, bf16[256,1792]{1,0:T(8,128)(2,1)S(1)} %collective-permute-done.1.refs_1_, bf16[14336,1792]{1,0:T(8,128)(2,1)} %refs_2_.15), custom_call_target="tpu_custom_call" | custom-call | flops 3288334336 | bytes 15597568 | tf_op jit(solution)/shard_map/rotate/pallas_call | solution.py:85
  267.2 16.9 %all_gather.40.refs_1_ = bf16[256,1792]{1,0:T(8,128)(2,1)} all-gather(bf16[64,1792]{1,0:T(8,128)(2,1)S(1)} %collective-permute-done.3), channel_id=1, replica_groups=mesh['grp'=2,'line'=4,'pair'=2,'narrow'=2] {'line'}, dimensions={0}, use_global_device_ids=true | all-gather | bytes 1146880 | tf_op jit(solution)/shard_map/all_gather | solution.py:113
  284.2 9.4 %rotate.9.refs_3_ = f32[512,1792]{1,0:T(8,128)} custom-call(bf16[256,1792]{1,0:T(8,128)(2,1)S(1)} %all_gather.36.refs_0_, bf16[256,1792]{1,0:T(8,128)(2,1)S(1)} %collective-permute-done.refs_1_, bf16[14336,1792]{1,0:T(8,128)(2,1)} %refs_2_.15, f32[512,1792]{1,0:T(8,128)} %rotate.8.refs_3_), custom_call_target="tpu_custom_call", output_to_operand_aliasing={{}: (3, {})} | custom-call | flops 3288334336 | bytes 15597568 | tf_op jit(solution)/shard_map/rotate/pallas_call | solution.py:85
  293.6 1.8 convert_element_type.3
  297.7 9.4 %rotate.10.refs_3_ = f32[512,1792]{1,0:T(8,128)} custom-call(bf16[256,1792]{1,0:T(8,128)(2,1)S(1)} %copy-done.3, bf16[256,1792]{1,0:T(8,128)(2,1)S(1)} %copy-done.4, bf16[14336,1792]{1,0:T(8,128)(2,1)} %refs_2_.15, f32[512,1792]{1,0:T(8,128)} %rotate.9.refs_3_), custom_call_target="tpu_custom_call", output_to_operand_aliasing={{}: (3, {})} | custom-call | flops 3288334336 | bytes 15597568 | tf_op jit(solution)/shard_map/rotate/pallas_call | solution.py:85
  307.2 1.8 collective-permute-start.4
  309.0 23.4 %all_gather.42.refs_1_ = bf16[256,1792]{1,0:T(8,128)(2,1)S(1)} all-gather(bf16[64,1792]{1,0:T(8,128)(2,1)S(1)} %collective-permute-done.5), channel_id=1, replica_groups=mesh['grp'=2,'line'=4,'pair'=2,'narrow'=2] {'line'}, dimensions={0}, use_global_device_ids=true | all-gather | bytes 1146880 | tf_op jit(solution)/shard_map/all_gather | solution.py:113
  332.4 10.1 %rotate.11.refs_3_ = f32[512,1792]{1,0:T(8,128)} custom-call(bf16[256,1792]{1,0:T(8,128)(2,1)} %all_gather.35.refs_0_, bf16[256,1792]{1,0:T(8,128)(2,1)} %collective-permute-done.2.refs_1_, bf16[14336,1792]{1,0:T(8,128)(2,1)} %refs_2_.15, f32[512,1792]{1,0:T(8,128)} %rotate.10.refs_3_), custom_call_target="tpu_custom_call", output_to_operand_aliasing={{}: (3, {})} | custom-call | flops 3288334336 | bytes 15597568 | tf_op jit(solution)/shard_map/rotate/pallas_call | solution.py:85
  342.5 1.6 collective-permute-start.7
  344.1 9.4 %rotate.12.refs_3_ = f32[512,1792]{1,0:T(8,128)} custom-call(bf16[256,1792]{1,0:T(8,128)(2,1)S(1)} %copy-done.2, bf16[256,1792]{1,0:T(8,128)(2,1)S(1)} %all_gather.42.refs_1_, bf16[14336,1792]{1,0:T(8,128)(2,1)} %refs_2_.15, f32[512,1792]{1,0:T(8,128)} %rotate.11.refs_3_), custom_call_target="tpu_custom_call", output_to_operand_aliasing={{}: (3, {})} | custom-call | flops 3288334336 | bytes 15597568 | tf_op jit(solution)/shard_map/rotate/pallas_call | solution.py:85
  353.9 9.4 %rotate.13.refs_3_ = f32[512,1792]{1,0:T(8,128)} custom-call(bf16[256,1792]{1,0:T(8,128)(2,1)S(1)} %all_gather.34.refs_0_, bf16[256,1792]{1,0:T(8,128)(2,1)S(1)} %collective-permute-done.4.refs_1_, bf16[14336,1792]{1,0:T(8,128)(2,1)} %refs_2_.15, f32[512,1792]{1,0:T(8,128)} %rotate.12.refs_3_), custom_call_target="tpu_custom_call", output_to_operand_aliasing={{}: (3, {})} | custom-call | flops 3288334336 | bytes 15597568 | tf_op jit(solution)/shard_map/rotate/pallas_call | solution.py:85
  363.4 9.7 %rotate.14.refs_3_ = f32[512,1792]{1,0:T(8,128)} custom-call(bf16[256,1792]{1,0:T(8,128)(2,1)S(1)} %all_gather.41.refs_0_, bf16[256,1792]{1,0:T(8,128)(2,1)} %collective-permute-done.7.refs_1_, bf16[14336,1792]{1,0:T(8,128)(2,1)} %refs_2_.15, f32[512,1792]{1,0:T(8,128)} %rotate.13.refs_3_), custom_call_target="tpu_custom_call", output_to_operand_aliasing={{}: (3, {})} | custom-call | flops 3288334336 | bytes 15597568 | tf_op jit(solution)/shard_map/rotate/pallas_call | solution.py:85
  373.1 9.8 %rotate.15.mine_ref = f32[512,1792]{1,0:T(8,128)} custom-call(bf16[256,1792]{1,0:T(8,128)(2,1)S(1)} %all_gather.33.refs_0_, bf16[256,1792]{1,0:T(8,128)(2,1)} %collective-permute-done.6.refs_1_, bf16[14336,1792]{1,0:T(8,128)(2,1)} %refs_2_.15, f32[512,1792]{1,0:T(8,128)} %rotate.14.refs_3_), custom_call_target="tpu_custom_call", output_to_operand_aliasing={{}: (3, {})} | custom-call | flops 3288334336 | bytes 15597568 | tf_op jit(solution)/shard_map/rotate/pallas_call | solution.py:85
  382.9 1.7 collective-permute-start.10
  384.7 23.8 %collective-permute-done.10 = bf16[512,1024]{1,0:T(8,128)(2,1)S(1)} collective-permute-done((bf16[512,1024]{1,0:T(8,128)(2,1)S(1)}, bf16[512,1024]{1,0:T(8,128)(2,1)S(1)}, u32[]{:S(2)}, u32[]{:S(2)}) %collective-permute-start.10) | collective-permute-done | bytes 1048608 | tf_op jit(solution)/shard_map/ppermute | solution.py:109
  409.3 12.5 %fit.1 = f32[1792,2048]{1,0:T(8,128)} custom-call(s32[8]{0:T(128)S(1)} %pad_add_fusion.order_ref, f32[512,1792]{1,0:T(8,128)} %rotate.15.mine_ref, f32[512,1792]{1,0:T(8,128)} %collective-permute-done.9.other_ref, bf16[512,2048]{1,0:T(8,128)(2,1)S(1)} %maximum_select_fusion.out_ref), custom_call_target="tpu_custom_call" | custom-call | flops 3758096384 | bytes 24117248 | tf_op jit(solution)/shard_map/fit/pallas_call | solution.py:41
  (37 shorter events, 8.3 us)
Async XLA Ops:
  6.5 1.2 copy-start
  6.5 287.0 %reduce-scatter.2.cloned.1.call-start = ((), (), s32[]{:S(2)}) async-start(), calls=%async_computation.1 | async-start | bytes 2621440 | tf_op jit(solution)/shard_map/reduce_scatter | solution.py:140
  12.3 2.0 copy-start.5
  15.8 48.8 %collective-permute-start.8 = (f32[512,1024]{1,0:T(8,128)}, f32[512,1024]{1,0:T(8,128)S(1)}, u32[]{:S(2)}, u32[]{:S(2)}) collective-permute-start(f32[512,1024]{1,0:T(8,128)} %constant_dynamic-slice_fusion), channel_id=1, source_target_pairs={{0,2},{2,0},{1,3},{3,1},{4,6},{6,4},{5,7},{7,5},{8,10},{10,8},{9,1... | collective-permute-start | bytes 6291464 | tf_op jit(solution)/shard_map/ppermute | solution.py:109
  67.9 295.4 %all-gather.2.cloned.1.call-start = ((), (), s32[]{:S(2)}) async-start(), calls=%async_computation.2 | async-start | bytes 1310720 | tf_op jit(solution)/shard_map/all_gather | solution.py:113
  69.7 197.6 %collective-permute-start.3 = (bf16[64,1792]{1,0:T(8,128)(2,1)S(1)}, bf16[64,1792]{1,0:T(8,128)(2,1)S(1)}, u32[]{:S(2)}, u32[]{:S(2)}) collective-permute-start(bf16[64,1792]{1,0:T(8,128)(2,1)S(1)} %get-tuple-element.44), channel_id=1, source_target_pairs={{0,2},{2,0},{1,3},{3,1},{4,6},{6,4},{5,7},{7,5},{8,10},{10,8},{9,1... | collective-permute-start | bytes 688136 | tf_op jit(solution)/shard_map/ppermute | solution.py:109
  71.5 237.4 %collective-permute-start.5 = (bf16[64,1792]{1,0:T(8,128)(2,1)S(1)}, bf16[64,1792]{1,0:T(8,128)(2,1)S(1)}, u32[]{:S(2)}, u32[]{:S(2)}) collective-permute-start(bf16[64,1792]{1,0:T(8,128)(2,1)S(1)} %get-tuple-element.50), channel_id=1, source_target_pairs={{0,2},{2,0},{1,3},{3,1},{4,6},{6,4},{5,7},{7,5},{8,10},{10,8},{9,1... | collective-permute-start | bytes 688136 | tf_op jit(solution)/shard_map/ppermute | solution.py:109
  105.6 161.4 %collective-permute-start = (bf16[256,1792]{1,0:T(8,128)(2,1)S(1)}, bf16[256,1792]{1,0:T(8,128)(2,1)S(1)}, u32[]{:S(2)}, u32[]{:S(2)}) collective-permute-start(bf16[256,1792]{1,0:T(8,128)(2,1)S(1)} %all_gather.36.refs_0_), channel_id=1, source_target_pairs={{0,2},{2,0},{1,3},{3,1},{4,6},{6,4},{5,7},{7,5},{8,10},{10,8},{9,1... | collective-permute-start | bytes 2752520 | tf_op jit(solution)/shard_map/ppermute | solution.py:109
  138.9 119.3 %collective-permute-start.1 = (bf16[256,1792]{1,0:T(8,128)(2,1)S(1)}, bf16[256,1792]{1,0:T(8,128)(2,1)S(1)}, u32[]{:S(2)}, u32[]{:S(2)}) collective-permute-start(bf16[256,1792]{1,0:T(8,128)(2,1)S(1)} %all_gather.37.refs_0_), channel_id=1, source_target_pairs={{0,2},{2,0},{1,3},{3,1},{4,6},{6,4},{5,7},{7,5},{8,10},{10,8},{9,1... | collective-permute-start | bytes 2752520 | tf_op jit(solution)/shard_map/ppermute | solution.py:109
  267.0 40.2 %collective-permute-start.2 = (bf16[256,1792]{1,0:T(8,128)(2,1)}, bf16[256,1792]{1,0:T(8,128)(2,1)}, u32[]{:S(2)}, u32[]{:S(2)}) collective-permute-start(bf16[256,1792]{1,0:T(8,128)(2,1)} %all_gather.35.refs_0_), channel_id=1, source_target_pairs={{0,2},{2,0},{1,3},{3,1},{4,6},{6,4},{5,7},{7,5},{8,10},{10,8},{9,1... | collective-permute-start | bytes 2752520 | tf_op jit(solution)/shard_map/ppermute | solution.py:109
  295.4 1.2 copy-start.3
  296.6 1.2 copy-start.4
  307.2 46.3 %collective-permute-start.4 = (bf16[256,1792]{1,0:T(8,128)(2,1)S(1)}, bf16[256,1792]{1,0:T(8,128)(2,1)S(1)}, u32[]{:S(2)}, u32[]{:S(2)}) collective-permute-start(bf16[256,1792]{1,0:T(8,128)(2,1)S(1)} %all_gather.34.refs_0_), channel_id=1, source_target_pairs={{0,2},{2,0},{1,3},{3,1},{4,6},{6,4},{5,7},{7,5},{8,10},{10,8},{9,1... | collective-permute-start | bytes 2752520 | tf_op jit(solution)/shard_map/ppermute | solution.py:109
  332.4 11.7 %copy-start.2 = (bf16[256,1792]{1,0:T(8,128)(2,1)S(1)}, bf16[256,1792]{1,0:T(8,128)(2,1)}, u32[]{:S(2)}) copy-start(bf16[256,1792]{1,0:T(8,128)(2,1)} %all_gather.39.refs_0_) | copy-start | bytes 2752516
  342.5 20.9 %collective-permute-start.7 = (bf16[256,1792]{1,0:T(8,128)(2,1)S(1)}, bf16[256,1792]{1,0:T(8,128)(2,1)}, u32[]{:S(2)}, u32[]{:S(2)}) collective-permute-start(bf16[256,1792]{1,0:T(8,128)(2,1)S(1)} %all_gather.41.refs_0_), channel_id=1, source_target_pairs={{0,2},{2,0},{1,3},{3,1},{4,6},{6,4},{5,7},{7,5},{8,10},{10,8},{9,1... | collective-permute-start | bytes 2752520 | tf_op jit(solution)/shard_map/ppermute | solution.py:109
  353.5 19.6 %collective-permute-start.6 = (bf16[256,1792]{1,0:T(8,128)(2,1)S(1)}, bf16[256,1792]{1,0:T(8,128)(2,1)}, u32[]{:S(2)}, u32[]{:S(2)}) collective-permute-start(bf16[256,1792]{1,0:T(8,128)(2,1)S(1)} %all_gather.33.refs_0_), channel_id=1, source_target_pairs={{0,2},{2,0},{1,3},{3,1},{4,6},{6,4},{5,7},{7,5},{8,10},{10,8},{9,1... | collective-permute-start | bytes 2752520 | tf_op jit(solution)/shard_map/ppermute | solution.py:109
  373.1 9.8 %copy-start.6 = (bf16[512,1024]{1,0:T(8,128)(2,1)S(1)}, bf16[512,1024]{1,0:T(8,128)(2,1)}, u32[]{:S(2)}) copy-start(bf16[512,1024]{1,0:T(8,128)(2,1)} %all-gather.2.cloned.1.call-done) | copy-start | bytes 3145732
  382.9 26.4 %collective-permute-start.9 = (f32[512,1792]{1,0:T(8,128)}, f32[512,1792]{1,0:T(8,128)}, u32[]{:S(2)}, u32[]{:S(2)}) collective-permute-start(f32[512,1792]{1,0:T(8,128)} %rotate.15.mine_ref), channel_id=1, source_target_pairs={{0,1},{1,0},{2,3},{3,2},{4,5},{5,4},{6,7},{7,6},{8,9},{9,8},{10,11... | collective-permute-start | bytes 11010056 | tf_op jit(solution)/shard_map/ppermute | solution.py:66
  382.9 25.6 %collective-permute-start.10 = (bf16[512,1024]{1,0:T(8,128)(2,1)S(1)}, bf16[512,1024]{1,0:T(8,128)(2,1)S(1)}, u32[]{:S(2)}, u32[]{:S(2)}) collective-permute-start(bf16[512,1024]{1,0:T(8,128)(2,1)S(1)} %copy-done.6), channel_id=1, source_target_pairs={{0,2},{2,0},{1,3},{3,1},{4,6},{6,4},{5,7},{7,5},{8,10},{10,8},{9,1... | collective-permute-start | bytes 3145736 | tf_op jit(solution)/shard_map/ppermute | solution.py:109
  409.3 12.5 %copy-start.1 = (bf16[512,1024]{1,0:T(8,128)(2,1)S(1)}, bf16[512,1024]{1,0:T(8,128)(2,1)}, u32[]{:S(2)}) copy-start(bf16[512,1024]{1,0:T(8,128)(2,1)} %param.5) | copy-start | bytes 3145732
Sparse Core Ops, SparseCore 0:
  68.1 70.5 reduce-scatter.1
  295.5 34.0 all-gather.1

commit v4 on v0

v4 whole, which is shorter than its diff:
```python
import jax
import jax.numpy as jnp
from jax import lax
from jax.experimental import pallas as pl
from jax.experimental.pallas import tpu as pltpu
from jax.sharding import PartitionSpec as P

EX = 2
LINE, PAIR = 4, 2
DEEP = 1024
BF16, F32 = jnp.bfloat16, jnp.float32


def dot(a, b):
    return jnp.dot(a, b, preferred_element_type=F32)


def fit_kernel(order_ref, flip_ref, *refs):
    *sum_refs, out_ref, fit_ref, rot_ref = refs
    rows, blocks = rot_ref.shape[0], order_ref.shape[0]
    size, seq = rows // blocks, rows // EX

    @pl.when(pl.program_id(1) == 0)
    def _():
        slot = 0
        for mine_ref, other_ref in zip(sum_refs[::2], sum_refs[1::2]):
            for at in range(0, mine_ref.shape[0], size):
                here = pl.ds(at, size)
                there = pl.ds(pl.multiple_of(order_ref[slot] * size, size), size)
                rot_ref[there, :] = mine_ref[here, :] + other_ref[here, :]
                slot += 1

    total = None
    for e in range(EX):
        here = pl.ds(e * seq, seq)
        grad = lax.dot_general(
            rot_ref[here, :].astype(BF16),
            out_ref[here, :],
            (((0,), (0,)), ((), ())),
            preferred_element_type=F32,
        )
        total = grad * grad if total is None else total + grad * grad
    fit_ref[...] = total * (1.0 / EX)


def fit(order, flip, sums, rotated_out):
    rows = sum(mine.shape[0] for mine, _ in sums)
    ka, ks = sums[0][0].shape[1], rotated_out.shape[1]
    tile = 256 if ka % 256 == 0 else ka
    part = ks // 2
    flat = [a for pair in sums for a in pair]
    return pl.pallas_call(
        fit_kernel,
        out_shape=jax.ShapeDtypeStruct((ka, ks), F32),
        grid_spec=pltpu.PrefetchScalarGridSpec(
            num_scalar_prefetch=2,
            grid=(ka // tile, 2),
            in_specs=[pl.BlockSpec((a.shape[0], tile), lambda i, j, o, f: (0, i)) for a in flat]
            + [pl.BlockSpec((rows, part), lambda i, j, o, f: (0, j))],
            out_specs=pl.BlockSpec((tile, part), lambda i, j, o, f: (i, j ^ f[0])),
            scratch_shapes=[pltpu.VMEM((rows, tile), F32)],
        ),
        compiler_params=pltpu.CompilerParams(vmem_limit_bytes=40 << 20),
        cost_estimate=pl.CostEstimate(
            flops=2 * rows * ka * ks, bytes_accessed=8 * rows * ka + 2 * rows * ks + 4 * ka * ks, transcendentals=0
        ),
        name="fit",
    )(order, flip, *flat, rotated_out)


def rotate_kernel(choices, end_ref, *refs):
    blocks = refs[: sum(choices)]
    basis_ref, *before, sum_ref, rows_ref = refs[sum(choices) :]
    size = blocks[0].shape[0]
    at = 0
    for i, choice in enumerate(choices):
        here = pl.ds(i * size, size)
        if choice == 1:
            rows_ref[here, :] = blocks[at][...]
        else:
            rows_ref[here, :] = jnp.where(end_ref[0] == 1, blocks[at][...], blocks[at + 1][...])
        at += choice

    @pl.when(pl.program_id(0) == 0)
    def _():
        sum_ref[...] = before[0][...] if before else jnp.zeros_like(sum_ref)

    sum_ref[...] += dot(rows_ref[...], basis_ref[...])


def rotate(before, end, blocks, basis, first, steps):
    flat = [pair for block in blocks for pair in block]
    size, ka = flat[0][0].shape[0], basis.shape[1]
    rows = size * len(blocks)
    specs = []
    for block in blocks:
        for which, (_, skip) in enumerate(block):
            used = lambda e, which=which, n=len(block): 1 if n == 1 else jnp.where(e[0] == 1, 1 - which, which)
            specs.append(
                pl.BlockSpec((size, DEEP), lambda k, e, used=used, skip=skip: (0, (k + skip) * used(e)))
            )
    whole = pl.BlockSpec((rows, ka), lambda k, e: (0, 0))
    arrays = [a for a, _ in flat] + [basis] + ([] if before is None else [before])
    return pl.pallas_call(
        lambda *refs: rotate_kernel([len(block) for block in blocks], *refs),
        out_shape=jax.ShapeDtypeStruct((rows, ka), F32),
        grid_spec=pltpu.PrefetchScalarGridSpec(
            num_scalar_prefetch=1,
            grid=(steps,),
            in_specs=specs
            + [pl.BlockSpec((DEEP, ka), lambda k, e: (first + k, 0))]
            + ([] if before is None else [whole]),
            out_specs=whole,
            scratch_shapes=[pltpu.VMEM((rows, DEEP), BF16)],
        ),
        compiler_params=pltpu.CompilerParams(vmem_limit_bytes=40 << 20),
        cost_estimate=pl.CostEstimate(
            flops=2 * rows * steps * DEEP * ka, bytes_accessed=2 * steps * DEEP * (rows + ka) + 8 * rows * ka, transcendentals=0
        ),
        name="rotate",
    )(end, *arrays)


def swap_narrow(a):
    return lax.ppermute(a, "narrow", [(0, 1), (1, 0)])


def general(inputs, deltas, basis_in, basis_out):
    partial_in = dot(lax.all_gather(inputs, "wide", axis=0, tiled=True), basis_in)
    rotated_out = lax.psum(dot(deltas, basis_out), "wide").astype(BF16)
    order = jnp.arange(EX, dtype=jnp.int32)
    return fit(order, jnp.zeros((1,), jnp.int32), [(partial_in, swap_narrow(partial_in))], rotated_out)


def pairs(step, where=lambda z: True):
    out = []
    for z in range(LINE):
        for x in range(PAIR):
            if where(z):
                tz, tx = step(z, x)
                out.append((z * PAIR + x, tz * PAIR + tx))
    return out


def corner(z):
    return z in (0, LINE - 1)


def middle(z):
    return not corner(z)


ENDS = pairs(lambda z, x: (z ^ 1, x))
TO_ENDS = pairs(lambda z, x: (z ^ 1, x), middle)
FROM_ENDS = pairs(lambda z, x: (z ^ 1, x), corner)
MIDDLE = pairs(lambda z, x: (3 - z, x), middle)
ACROSS = pairs(lambda z, x: (z, 1 - x))
ACROSS_ENDS = pairs(lambda z, x: (z, 1 - x), corner)
ACROSS_MIDDLE = pairs(lambda z, x: (z, 1 - x), middle)


def send(a, perm):
    return lax.ppermute(a, "wide", perm)


def scheduled(inputs, deltas, basis_in, basis_out):
    w = lax.axis_index("wide")
    z, x = w // PAIR, w % PAIR
    at_end = (z == 0) | (z == LINE - 1)
    end = at_end.astype(jnp.int32).reshape(1)
    half = (z >= 2).astype(jnp.int32)
    steps = inputs.shape[1] // DEEP
    size = [steps - steps // 2, steps // 2]
    late = size[1] - 2
    got = {}

    def fence(*names):
        got.update(zip(names, lax.optimization_barrier(tuple(got[n] for n in names))))

    def pick(a, b):
        return jnp.where(at_end, got[a], got[b])

    for c in range(2):
        got["own", c] = inputs[:, c * size[0] * DEEP : (c * size[0] + size[c]) * DEEP]

    def first(c):
        got["x1", c] = send(got["own", c], ACROSS)
        got["a1", c] = send(got["own", c], ENDS)
        got["m1", c] = send(got["own", c], MIDDLE)

    def second(c):
        got["x2", c] = send(pick(("a1", c), ("m1", c)), ACROSS)
        got["a2", c] = send(got["m1", c], TO_ENDS)
        got["m2", c] = send(got["a1", c], MIDDLE)

    def third(c):
        got["x3", c] = send(pick(("a2", c), ("m2", c)), ACROSS)
        got["a3", c] = send(got["m2", c], TO_ENDS)

    def early(before, c):
        blocks = [[("own", c)], [("a1", c)], [("x1", c)], [("a2", c), ("m1", c)]]
        return rotate(before, end, [[(got[n], 0) for n in b] for b in blocks], basis_in, c * size[0], size[c])

    def tail(before, c, x4, skip, count):
        blocks = [[("a3", c), ("m2", c)], [("x2", c), ("e", c)], [("x3", c), ("x2", c)]]
        blocks = [[(got[n], skip) for n in b] for b in blocks] + [[(got[x4], 0), (got["x3", c], skip)]]
        return rotate(before, end, blocks, basis_in, c * size[0] + skip, count)

    part = basis_out.shape[1] // 4

    def columns(a, h, p):
        return lax.dynamic_slice_in_dim(a, (2 * h + p) * part, part, 1)

    first(0)
    got["out"] = dot(deltas, basis_out)
    got["out16"] = got["out"].astype(BF16)
    fence("out", "out16", ("own", 1))
    got["r1"] = send(got["out16"], FROM_ENDS)
    first(1)
    fence(("x1", 0), ("a1", 0), ("m1", 0))
    second(0)
    fence(("x1", 1), ("a1", 1), ("m1", 1))
    second(1)
    fence(("x2", 0), ("a2", 0), ("m2", 0), "r1")
    third(0)
    here = got["out"] + got["r1"].astype(F32)
    for p in range(2):
        got["keep", p] = columns(here, half, p)
        got["m3", p] = send(columns(here, 1 - half, p), MIDDLE)
    got["early"] = early(None, 0)
    fence(("x2", 1), ("a2", 1), ("m2", 1), ("m3", 0), "early")
    third(1)
    got["keep", 0] += got["m3", 0]
    got["x5", 0] = send(got["keep", 0].astype(BF16), ACROSS_MIDDLE)
    got["early"] = early(got["early"], 1)
    fence(("x3", 0), ("a3", 0), ("m3", 1), "early")
    got["x4", 0] = send(got["a3", 0], ACROSS_ENDS)
    got["e", 0] = send(got["x1", 0], FROM_ENDS)
    got["keep", 1] += got["m3", 1]
    got["x5", 1] = send(got["keep", 1].astype(BF16), ACROSS_MIDDLE)
    got["early2"] = swap_narrow(got["early"])
    fence(("x3", 1), ("a3", 1), ("x5", 0))
    got["x4", 1] = send(got["a3", 1][:, : late * DEEP], ACROSS_ENDS)
    got["x4", 2] = send(got["a3", 1][:, late * DEEP :], ACROSS_ENDS)
    got["e", 1] = send(got["x1", 1], FROM_ENDS)

    def settle(p):
        got["sum", p] = (got["keep", p] + got["x5", p].astype(F32)).astype(BF16)
        got["m4", p] = send(got["sum", p], MIDDLE)
        got["n1", p] = send(got["sum", p], TO_ENDS)

    settle(0)
    fence(("x4", 0), ("e", 0), ("x5", 1), ("m4", 0))
    got["n2", 0] = send(got["m4", 0], TO_ENDS)
    settle(1)
    got["late"] = tail(None, 0, ("x4", 0), 0, size[0])
    fence(("x4", 1), ("e", 1), ("m4", 1), "late", "early2")
    got["n2", 1] = send(got["m4", 1], TO_ENDS)
    got["late"] = tail(got["late"], 1, ("x4", 1), 0, late)
    fence(("x4", 2), "late")
    got["late"] = tail(got["late"], 1, ("x4", 2), late, size[1] - late)
    late2 = swap_narrow(got["late"])
    rotated_out = jnp.concatenate(
        [pick(("n1", 0), ("sum", 0)), pick(("n1", 1), ("sum", 1)), pick(("n2", 0), ("m4", 0)), pick(("n2", 1), ("m4", 1))],
        axis=1,
    )
    turn = jnp.where(z >= 2, 3, 0)
    near = [jnp.where(at_end, a, b) ^ turn for a, b in ((0, 1), (1, 0), (2, 2), (3, 3))]
    mine = [q * PAIR + x for q in near]
    other = [q * PAIR + 1 - x for q in near]
    order = jnp.stack(mine[:2] + [other[0], mine[2], mine[3]] + other[1:]).astype(jnp.int32)
    sums = [(got["early"], got["early2"]), (got["late"], late2)]
    return fit(order, half.reshape(1), sums, rotated_out)


def solution(mesh):
    return jax.shard_map(
        scheduled if mesh.shape["wide"] == LINE * PAIR else general,
        mesh=mesh,
        in_specs=(
            P(("grp", "wide"), "narrow"),
            P("grp", "wide"),
            P(("grp", "narrow"), "wide"),
            P(("grp", "wide"), "narrow"),
        ),
        out_specs=P(("grp", "wide"), "narrow"),
        check_vma=False,
    )
```

time: 412 us -> 280 us (0.68)
  blocking collectives: 242 us -> 0 us
  Pallas kernels: 0 us -> 74.8 us
  starting transfers between devices: 0.01 us -> 68.5 us
  matrix products: 54.1 us -> 7.25 us
  waiting for transfers between devices: 87.8 us -> 108 us
  between operations: 13.4 us -> 0.63 us
  local copies, waits for them, and re-layouts: 0.51 us -> 6.68 us
    psum x2 -> x0, blocking collectives: 242 us -> none  [the longest x1 228 us: local(): rotated_out = lax.psum(partial_out, 'wide').astype(jnp.bfloat16)]
    ppermute x0 -> x34, waiting for transfers between devices: none -> 108 us  [the longest x32 108 us: send(): return lax.ppermute(a, 'wide', perm)]
    all_gather x1 -> x0, waiting for transfers between devices: 87.1 us -> none  [local(): lax.all_gather(inputs, 'wide', axis=0, tiled=True)]
    pallas_call x0 -> x6, Pallas kernels: none -> 74.8 us  [the longest x5 58.7 us: rotate(): pl.pallas_call(lambda *refs: rotate_kernel([len(block) for block in block...]
    ppermute x0 -> x34, starting transfers between devices: none -> 68.5 us  [the longest x32 68.5 us: send(): return lax.ppermute(a, 'wide', perm)]
    dot_general x3 -> x1, matrix products: 54.1 us -> 7.25 us  [dot(): return jnp.dot(a, b, preferred_element_type=F32)]
    div x1 -> x0, other arithmetic: 14 us -> none  [local(): return jnp.sum(grads * grads, axis=0) / EX]
    select_n x0 -> x8, other arithmetic: none -> 6.03 us  [pick(): return jnp.where(at_end, got[a], got[b])]
  transfers between devices with their start and end apart: 1 -> 34, of which waited for: 1 -> 8; matrix products, arithmetic and copies ran while one was open for 2% -> 8% of each run, Pallas kernels for 0% -> 21%
where the time goes in v4:
time: 280 us; the launch traced here: 279 us
  waiting for transfers between devices  108 us (39%)
  Pallas kernels  74.8 us (27%)
  starting transfers between devices  68.5 us (24%)
  other arithmetic  12.7 us (5%)
  matrix products  7.25 us (3%)
  local copies, waits for them, and re-layouts  6.68 us (2%)
    ppermute x32, waiting for transfers between devices, send(): return lax.ppermute(a, 'wide', perm)  108 us
    ppermute x32, starting transfers between devices, send(): return lax.ppermute(a, 'wide', perm)  68.5 us
    pallas_call x5, Pallas kernels, rotate(): pl.pallas_call(lambda *refs: rotate_kernel([len(block) for block in block...  58.7 us
    pallas_call x1, Pallas kernels, fit(): pl.pallas_call(fit_kernel, out_shape=jax.ShapeDtypeStruct((ka, ks), F32),...  16.1 us
    dot_general x1, matrix products, dot(): return jnp.dot(a, b, preferred_element_type=F32)  7.25 us
    select_n x8, other arithmetic, pick(): return jnp.where(at_end, got[a], got[b])  6.03 us
  transfers between devices with their start and end apart: 34, of which 8 were waited for; matrix products, arithmetic and copies ran while one was open for 8% of the time, Pallas kernels for 21%

profile of v4, /device:TPU:0, one launch (start us, length us, event | category | flops | bytes accessed | tf_op | source)
XLA Modules:
  0.0 278.8 jit_solution(1849937630869936834)
XLA Ops:
  0.0 1.7 fusion.2
  1.7 1.6 collective-permute-start.2
  3.3 5.0 %collective-permute-start.1 = (bf16[64,7168]{1,0:T(8,128)(2,1)S(1)}, bf16[64,7168]{1,0:T(8,128)(2,1)}, u32[]{:S(2)}, u32[]{:S(2)}) collective-permute-start(bf16[64,7168]{1,0:T(8,128)(2,1)S(1)} %get-tuple-element.82.refs_1_), channel_id=1, source_target_pairs={{0,4},{2,6},{4,0},{6,2},{8,12},{10,14},{12,8},{14,10},{1,5},{3,7},... | collective-permute-start | bytes 2752520 | tf_op jit(solution)/shard_map/ppermute | solution.py:163
  8.3 1.5 collective-permute-start
  9.8 7.3 %fusion.3 = (bf16[512,2048]{1,0:T(8,128)(2,1)}, f32[512,2048]{1,0:T(8,128)}) fusion(bf16[512,1024]{1,0:T(8,128)(2,1)S(1)} %copy-done, bf16[1024,2048]{1,0:T(8,128)(2,1)} %param.7), kind=kOutput, calls=%fused_computation.19 | convolution fusion | flops 2148532224 | bytes 11534336 | tf_op jit(solution)/shard_map/dot_general | solution.py:15
  17.0 1.6 collective-permute-start.12
  18.7 1.6 collective-permute-start.11
  20.8 8.8 %collective-permute-done.1.refs_2_ = bf16[64,7168]{1,0:T(8,128)(2,1)} collective-permute-done((bf16[64,7168]{1,0:T(8,128)(2,1)S(1)}, bf16[64,7168]{1,0:T(8,128)(2,1)}, u32[]{:S(2)}, u32[]{:S(2)}) %collective-permute-start.1) | collective-permute-done | bytes 917536 | tf_op jit(solution)/shard_map/ppermute | solution.py:163
  29.6 4.1 %collective-permute-start.6 = (bf16[512,2048]{1,0:T(8,128)(2,1)}, bf16[512,2048]{1,0:T(8,128)(2,1)S(1)}, u32[]{:S(2)}, u32[]{:S(2)}) collective-permute-start(bf16[512,2048]{1,0:T(8,128)(2,1)} %get-tuple-element.43), channel_id=1, source_target_pairs={{0,4},{2,6},{12,8},{14,10},{1,5},{3,7},{13,9},{15,11},{16,20},{18,... | collective-permute-start | bytes 6291464 | tf_op jit(solution)/shard_map/ppermute | solution.py:163
  37.0 11.7 %collective-permute-done.11.refs_2_ = bf16[64,7168]{1,0:T(8,128)(2,1)} collective-permute-done((bf16[64,7168]{1,0:T(8,128)(2,1)S(1)}, bf16[64,7168]{1,0:T(8,128)(2,1)}, u32[]{:S(2)}, u32[]{:S(2)}) %collective-permute-start.11) | collective-permute-done | bytes 917536 | tf_op jit(solution)/shard_map/ppermute | solution.py:163
  48.7 1.5 collective-permute-start.3
  52.2 17.1 %collective-permute-done.3.refs_3_.refs_6_ = bf16[64,7168]{1,0:T(8,128)(2,1)S(1)} collective-permute-done((bf16[64,7168]{1,0:T(8,128)(2,1)S(1)}, bf16[64,7168]{1,0:T(8,128)(2,1)S(1)}, u32[]{:S(2)}, u32[]{:S(2)}) %collective-permute-start.3) | collective-permute-done | bytes 917536 | tf_op jit(solution)/shard_map/ppermute | solution.py:163
  71.6 1.6 collective-permute-start.13
  73.1 19.2 %collective-permute-done.6 = bf16[512,2048]{1,0:T(8,128)(2,1)S(1)} collective-permute-done((bf16[512,2048]{1,0:T(8,128)(2,1)}, bf16[512,2048]{1,0:T(8,128)(2,1)S(1)}, u32[]{:S(2)}, u32[]{:S(2)}) %collective-permute-start.6) | collective-permute-done | bytes 2097184 | tf_op jit(solution)/shard_map/ppermute | solution.py:163
  96.1 13.7 %rotate.5.refs_7_ = f32[256,1792]{1,0:T(8,128)S(1)} custom-call(s32[1]{0:T(128)} %bitcast.9.refs_0_, bf16[64,7168]{1,0:T(8,128)(2,1)S(1)} %copy-done.9, bf16[64,7168]{1,0:T(8,128)(2,1)} %collective-permute-done.1.refs_2_, bf16[64,7168]{1,0:T(8,128)(2,1)} %collective-permute-done.refs_3_, bf16[64,7168]{1,0:T(8,128)(2,1)S(1)} %collective-permute-done.4.refs_4_, ...), custom_call_target="tpu_custom_call" | custom-call | flops 6576668672 | bytes 33030144 | tf_op jit(solution)/shard_map/rotate/pallas_call | solution.py:104
  109.9 1.6 collective-permute-start.7
  115.3 17.9 %collective-permute-done.7.refs_5_.refs_8_ = bf16[64,7168]{1,0:T(8,128)(2,1)S(1)} collective-permute-done((bf16[64,7168]{1,0:T(8,128)(2,1)S(1)}, bf16[64,7168]{1,0:T(8,128)(2,1)S(1)}, u32[]{:S(2)}, u32[]{:S(2)}) %collective-permute-start.7) | collective-permute-done | bytes 917536 | tf_op jit(solution)/shard_map/ppermute | solution.py:163
  133.2 7.5 %collective-permute-start.23 = (bf16[64,7168]{1,0:T(8,128)(2,1)}, bf16[64,7168]{1,0:T(8,128)(2,1)}, u32[]{:S(2)}, u32[]{:S(2)}) collective-permute-start(bf16[64,7168]{1,0:T(8,128)(2,1)} %collective-permute-done.refs_3_), channel_id=1, source_target_pairs={{0,4},{2,6},{12,8},{14,10},{1,5},{3,7},{13,9},{15,11},{16,20},{18,... | collective-permute-start | bytes 2752520 | tf_op jit(solution)/shard_map/ppermute | solution.py:163
  142.2 14.8 %rotate.6.refs_0_ = f32[256,1792]{1,0:T(8,128)} custom-call(s32[1]{0:T(128)} %bitcast.9.refs_0_, bf16[64,7168]{1,0:T(8,128)(2,1)S(1)} %copy-done.7, bf16[64,7168]{1,0:T(8,128)(2,1)} %collective-permute-done.11.refs_2_, bf16[64,7168]{1,0:T(8,128)(2,1)S(1)} %collective-permute-done.10.refs_3_, bf16[64,7168]{1,0:T(8,128)(2,1)S(1)} %collective-permute-done.14.refs_4_, ...), custom_call_target="tpu_custom_call" | custom-call | flops 6576668672 | bytes 33030144 | tf_op jit(solution)/shard_map/rotate/pallas_call | solution.py:104
  158.0 3.4 %collective-permute-start.22 = (bf16[64,7168]{1,0:T(8,128)(2,1)}, bf16[64,7168]{1,0:T(8,128)(2,1)}, u32[]{:S(2)}, u32[]{:S(2)}) collective-permute-start(bf16[64,7168]{1,0:T(8,128)(2,1)} %collective-permute-done.8.refs_1_), channel_id=1, source_target_pairs={{0,2},{2,0},{12,14},{14,12},{1,3},{3,1},{13,15},{15,13},{16,18},{1... | collective-permute-start | bytes 2752520 | tf_op jit(solution)/shard_map/ppermute | solution.py:163
  161.4 3.1 %add_convert_fusion.1 = (bf16[512,512]{1,0:T(8,128)(2,1)S(1)}, bf16[512,512]{1,0:T(8,128)(2,1)S(1)}) fusion(bf16[512,512]{1,0:T(8,128)(2,1)} %collective-permute-done.19, f32[512,512]{1,0:T(8,128)} %copy-done.16, f32[512,2048]{1,0:T(8,128)} %copy-done.14, s32[]{:T(128)S(6)} %select_n.87, f32[512,512]{1,0:T(8,128)} %copy-done.17, s32[]{:T(128)S(6)} %select_n.88), kind=kLoop, calls=%fused_computation.3 | loop fusion | flops 1572864 | bytes 5767176 | tf_op jit(solution)/shard_map/convert_element_type | solution.py:248
  166.7 12.9 %collective-permute-start.21 = (bf16[64,7168]{1,0:T(8,128)(2,1)S(1)}, bf16[64,7168]{1,0:T(8,128)(2,1)S(1)}, u32[]{:S(2)}, u32[]{:S(2)}) collective-permute-start(bf16[64,7168]{1,0:T(8,128)(2,1)S(1)} %copy-done.13), channel_id=1, source_target_pairs={{0,4},{2,6},{12,8},{14,10},{1,5},{3,7},{13,9},{15,11},{16,20},{18,... | collective-permute-start | bytes 2752520 | tf_op jit(solution)/shard_map/ppermute | solution.py:163
  181.7 2.4 collective-permute-start.28
  184.2 3.4 %collective-permute-start.20 = (bf16[64,5120]{1,0:T(8,128)(2,1)S(1)}, bf16[64,5120]{1,0:T(8,128)(2,1)S(1)}, u32[]{:S(2)}, u32[]{:S(2)}) collective-permute-start(bf16[64,5120]{1,0:T(8,128)(2,1)S(1)} %slice.14), channel_id=1, source_target_pairs={{0,2},{2,0},{12,14},{14,12},{1,3},{3,1},{13,15},{15,13},{16,18},{1... | collective-permute-start | bytes 1966088 | tf_op jit(solution)/shard_map/ppermute | solution.py:163
  187.6 2.3 add_convert_fusion
  190.6 13.9 %rotate.7.refs_10_ = f32[256,1792]{1,0:T(8,128)S(1)} custom-call(s32[1]{0:T(128)} %bitcast.9.refs_0_, bf16[64,7168]{1,0:T(8,128)(2,1)} %collective-permute-done.8.refs_1_, bf16[64,7168]{1,0:T(8,128)(2,1)S(1)} %copy-done.11, bf16[64,7168]{1,0:T(8,128)(2,1)S(1)} %copy-done.3, bf16[64,7168]{1,0:T(8,128)(2,1)} %collective-permute-done.23.refs_4_, ...), custom_call_target="tpu_custom_call" | custom-call | flops 6576668672 | bytes 33030144 | tf_op jit(solution)/shard_map/rotate/pallas_call | solution.py:104
  206.1 10.4 %rotate.8.refs_10_ = f32[256,1792]{1,0:T(8,128)S(1)} custom-call(s32[1]{0:T(128)} %bitcast.9.refs_0_, bf16[64,7168]{1,0:T(8,128)(2,1)} %collective-permute-done.18.refs_1_, bf16[64,7168]{1,0:T(8,128)(2,1)S(1)} %collective-permute-done.15.refs_2_, bf16[64,7168]{1,0:T(8,128)(2,1)S(1)} %collective-permute-done.13.refs_3_.refs_6_, ...), custom_call_target="tpu_custom_call" | custom-call | flops 4697620480 | bytes 24641536 | tf_op jit(solution)/shard_map/rotate/pallas_call | solution.py:104
  216.5 6.0 %rotate.9.refs_2_ = f32[256,1792]{1,0:T(8,128)} custom-call(s32[1]{0:T(128)} %bitcast.9.refs_0_, bf16[64,7168]{1,0:T(8,128)(2,1)} %collective-permute-done.18.refs_1_, bf16[64,7168]{1,0:T(8,128)(2,1)S(1)} %collective-permute-done.15.refs_2_, bf16[64,7168]{1,0:T(8,128)(2,1)S(1)} %collective-permute-done.13.refs_3_.refs_6_, ...), custom_call_target="tpu_custom_call" | custom-call | flops 1879048192 | bytes 12058624 | tf_op jit(solution)/shard_map/rotate/pallas_call | solution.py:104
  227.6 12.5 %collective-permute-done.31 = bf16[512,512]{1,0:T(8,128)(2,1)} collective-permute-done((bf16[512,512]{1,0:T(8,128)(2,1)}, bf16[512,512]{1,0:T(8,128)(2,1)}, u32[]{:S(2)}, u32[]{:S(2)}) %collective-permute-start.31) | collective-permute-done | bytes 524320 | tf_op jit(solution)/shard_map/ppermute | solution.py:163
  241.2 10.0 %collective-permute-done.32 = bf16[512,512]{1,0:T(8,128)(2,1)S(1)} collective-permute-done((bf16[512,512]{1,0:T(8,128)(2,1)}, bf16[512,512]{1,0:T(8,128)(2,1)S(1)}, u32[]{:S(2)}, u32[]{:S(2)}) %collective-permute-start.32) | collective-permute-done | bytes 524320 | tf_op jit(solution)/shard_map/ppermute | solution.py:163
  251.3 11.0 %collective-permute-done.33 = bf16[512,512]{1,0:T(8,128)(2,1)S(1)} collective-permute-done((bf16[512,512]{1,0:T(8,128)(2,1)}, bf16[512,512]{1,0:T(8,128)(2,1)S(1)}, u32[]{:S(2)}, u32[]{:S(2)}) %collective-permute-start.33) | collective-permute-done | bytes 524320 | tf_op jit(solution)/shard_map/ppermute | solution.py:163
  262.7 16.1 %fit.1 = f32[1792,2048]{1,0:T(8,128)} custom-call(s32[8]{0:T(128)S(1)} %stack.35.order_ref, s32[1]{0:T(128)} %bitcast.8.flip_ref, f32[256,1792]{1,0:T(8,128)} %rotate.6.refs_0_, f32[256,1792]{1,0:T(8,128)} %collective-permute-done.27.refs_1_, f32[256,1792]{1,0:T(8,128)} %rotate.9.refs_2_, f32[256,1792]{1,0:T(8,128)S(1)} %collective-permute-done.29.refs_3_, ...), custom_call_target="tpu_custom_call" | custom-call | flops 3758096384 | bytes 24117248 | tf_op jit(solution)/shard_map/fit/pallas_call | solution.py:52
  (101 shorter events, 31.3 us)
Async XLA Ops:
  1.7 18.5 %collective-permute-start.2 = (bf16[64,7168]{1,0:T(8,128)(2,1)S(1)}, bf16[64,7168]{1,0:T(8,128)(2,1)}, u32[]{:S(2)}, u32[]{:S(2)}) collective-permute-start(bf16[64,7168]{1,0:T(8,128)(2,1)S(1)} %get-tuple-element.82.refs_1_), channel_id=1, source_target_pairs={{4,8},{6,10},{8,4},{10,6},{5,9},{7,11},{9,5},{11,7},{20,24},{22,26... | collective-permute-start | bytes 2752520 | tf_op jit(solution)/shard_map/ppermute | solution.py:163
  3.3 26.3 %collective-permute-start.1 = (bf16[64,7168]{1,0:T(8,128)(2,1)S(1)}, bf16[64,7168]{1,0:T(8,128)(2,1)}, u32[]{:S(2)}, u32[]{:S(2)}) collective-permute-start(bf16[64,7168]{1,0:T(8,128)(2,1)S(1)} %get-tuple-element.82.refs_1_), channel_id=1, source_target_pairs={{0,4},{2,6},{4,0},{6,2},{8,12},{10,14},{12,8},{14,10},{1,5},{3,7},... | collective-permute-start | bytes 2752520 | tf_op jit(solution)/shard_map/ppermute | solution.py:163
  8.3 25.4 %collective-permute-start = (bf16[64,7168]{1,0:T(8,128)(2,1)S(1)}, bf16[64,7168]{1,0:T(8,128)(2,1)}, u32[]{:S(2)}, u32[]{:S(2)}) collective-permute-start(bf16[64,7168]{1,0:T(8,128)(2,1)S(1)} %get-tuple-element.82.refs_1_), channel_id=1, source_target_pairs={{0,2},{2,0},{4,6},{6,4},{8,10},{10,8},{12,14},{14,12},{1,3},{3,1},... | collective-permute-start | bytes 2752520 | tf_op jit(solution)/shard_map/ppermute | solution.py:163
  17.0 18.7 %collective-permute-start.12 = (bf16[64,7168]{1,0:T(8,128)(2,1)S(1)}, bf16[64,7168]{1,0:T(8,128)(2,1)}, u32[]{:S(2)}, u32[]{:S(2)}) collective-permute-start(bf16[64,7168]{1,0:T(8,128)(2,1)S(1)} %get-tuple-element.48.refs_1_), channel_id=1, source_target_pairs={{4,8},{6,10},{8,4},{10,6},{5,9},{7,11},{9,5},{11,7},{20,24},{22,26... | collective-permute-start | bytes 2752520 | tf_op jit(solution)/shard_map/ppermute | solution.py:163
  18.7 30.1 %collective-permute-start.11 = (bf16[64,7168]{1,0:T(8,128)(2,1)S(1)}, bf16[64,7168]{1,0:T(8,128)(2,1)}, u32[]{:S(2)}, u32[]{:S(2)}) collective-permute-start(bf16[64,7168]{1,0:T(8,128)(2,1)S(1)} %get-tuple-element.48.refs_1_), channel_id=1, source_target_pairs={{0,4},{2,6},{4,0},{6,2},{8,12},{10,14},{12,8},{14,10},{1,5},{3,7},... | collective-permute-start | bytes 2752520 | tf_op jit(solution)/shard_map/ppermute | solution.py:163
  20.2 30.0 %collective-permute-start.10 = (bf16[64,7168]{1,0:T(8,128)(2,1)S(1)}, bf16[64,7168]{1,0:T(8,128)(2,1)S(1)}, u32[]{:S(2)}, u32[]{:S(2)}) collective-permute-start(bf16[64,7168]{1,0:T(8,128)(2,1)S(1)} %get-tuple-element.48.refs_1_), channel_id=1, source_target_pairs={{0,2},{2,0},{4,6},{6,4},{8,10},{10,8},{12,14},{14,12},{1,3},{3,1},... | collective-permute-start | bytes 2752520 | tf_op jit(solution)/shard_map/ppermute | solution.py:163
  29.6 62.7 %collective-permute-start.6 = (bf16[512,2048]{1,0:T(8,128)(2,1)}, bf16[512,2048]{1,0:T(8,128)(2,1)S(1)}, u32[]{:S(2)}, u32[]{:S(2)}) collective-permute-start(bf16[512,2048]{1,0:T(8,128)(2,1)} %get-tuple-element.43), channel_id=1, source_target_pairs={{0,4},{2,6},{12,8},{14,10},{1,5},{3,7},{13,9},{15,11},{16,20},{18,... | collective-permute-start | bytes 6291464 | tf_op jit(solution)/shard_map/ppermute | solution.py:163
  33.7 37.9 %collective-permute-start.5 = (bf16[64,7168]{1,0:T(8,128)(2,1)}, bf16[64,7168]{1,0:T(8,128)(2,1)S(1)}, u32[]{:S(2)}, u32[]{:S(2)}) collective-permute-start(bf16[64,7168]{1,0:T(8,128)(2,1)} %collective-permute-done.1.refs_2_), channel_id=1, source_target_pairs={{4,8},{6,10},{8,4},{10,6},{5,9},{7,11},{9,5},{11,7},{20,24},{22,26... | collective-permute-start | bytes 2752520 | tf_op jit(solution)/shard_map/ppermute | solution.py:163
  35.7 37.4 %collective-permute-start.4 = (bf16[64,7168]{1,0:T(8,128)(2,1)}, bf16[64,7168]{1,0:T(8,128)(2,1)S(1)}, u32[]{:S(2)}, u32[]{:S(2)}) collective-permute-start(bf16[64,7168]{1,0:T(8,128)(2,1)} %collective-permute-done.2.refs_5_), channel_id=1, source_target_pairs={{4,0},{6,2},{8,12},{10,14},{5,1},{7,3},{9,13},{11,15},{20,16},{22,... | collective-permute-start | bytes 2752520 | tf_op jit(solution)/shard_map/ppermute | solution.py:163
  48.7 20.6 %collective-permute-start.3 = (bf16[64,7168]{1,0:T(8,128)(2,1)S(1)}, bf16[64,7168]{1,0:T(8,128)(2,1)S(1)}, u32[]{:S(2)}, u32[]{:S(2)}) collective-permute-start(bf16[64,7168]{1,0:T(8,128)(2,1)S(1)} %broadcast_select_fusion.3), channel_id=1, source_target_pairs={{0,2},{2,0},{4,6},{6,4},{8,10},{10,8},{12,14},{14,12},{1,3},{3,1},... | collective-permute-start | bytes 2752520 | tf_op jit(solution)/shard_map/ppermute | solution.py:163
  50.2 61.2 %collective-permute-start.15 = (bf16[64,7168]{1,0:T(8,128)(2,1)}, bf16[64,7168]{1,0:T(8,128)(2,1)S(1)}, u32[]{:S(2)}, u32[]{:S(2)}) collective-permute-start(bf16[64,7168]{1,0:T(8,128)(2,1)} %collective-permute-done.11.refs_2_), channel_id=1, source_target_pairs={{4,8},{6,10},{8,4},{10,6},{5,9},{7,11},{9,5},{11,7},{20,24},{22,26... | collective-permute-start | bytes 2752520 | tf_op jit(solution)/shard_map/ppermute | solution.py:163
  70.3 41.2 %collective-permute-start.14 = (bf16[64,7168]{1,0:T(8,128)(2,1)}, bf16[64,7168]{1,0:T(8,128)(2,1)S(1)}, u32[]{:S(2)}, u32[]{:S(2)}) collective-permute-start(bf16[64,7168]{1,0:T(8,128)(2,1)} %collective-permute-done.12.refs_5_), channel_id=1, source_target_pairs={{4,0},{6,2},{8,12},{10,14},{5,1},{7,3},{9,13},{11,15},{20,16},{22,... | collective-permute-start | bytes 2752520 | tf_op jit(solution)/shard_map/ppermute | solution.py:163
  71.6 38.3 %collective-permute-start.13 = (bf16[64,7168]{1,0:T(8,128)(2,1)S(1)}, bf16[64,7168]{1,0:T(8,128)(2,1)S(1)}, u32[]{:S(2)}, u32[]{:S(2)}) collective-permute-start(bf16[64,7168]{1,0:T(8,128)(2,1)S(1)} %broadcast_select_fusion.1), channel_id=1, source_target_pairs={{0,2},{2,0},{4,6},{6,4},{8,10},{10,8},{12,14},{14,12},{1,3},{3,1},... | collective-permute-start | bytes 2752520 | tf_op jit(solution)/shard_map/ppermute | solution.py:163
  92.3 48.4 %collective-permute-start.8 = (bf16[64,7168]{1,0:T(8,128)(2,1)S(1)}, bf16[64,7168]{1,0:T(8,128)(2,1)}, u32[]{:S(2)}, u32[]{:S(2)}) collective-permute-start(bf16[64,7168]{1,0:T(8,128)(2,1)S(1)} %collective-permute-done.5.refs_2_), channel_id=1, source_target_pairs={{4,0},{6,2},{8,12},{10,14},{5,1},{7,3},{9,13},{11,15},{20,16},{22,... | collective-permute-start | bytes 2752520 | tf_op jit(solution)/shard_map/ppermute | solution.py:163
  109.9 23.4 %collective-permute-start.7 = (bf16[64,7168]{1,0:T(8,128)(2,1)S(1)}, bf16[64,7168]{1,0:T(8,128)(2,1)S(1)}, u32[]{:S(2)}, u32[]{:S(2)}) collective-permute-start(bf16[64,7168]{1,0:T(8,128)(2,1)S(1)} %broadcast_select_fusion.2), channel_id=1, source_target_pairs={{0,2},{2,0},{4,6},{6,4},{8,10},{10,8},{12,14},{14,12},{1,3},{3,1},... | collective-permute-start | bytes 2752520 | tf_op jit(solution)/shard_map/ppermute | solution.py:163
  111.7 45.3 %collective-permute-start.9 = (f32[512,512]{1,0:T(8,128)S(1)}, f32[512,512]{1,0:T(8,128)S(1)}, u32[]{:S(2)}, u32[]{:S(2)}) collective-permute-start(f32[512,512]{1,0:T(8,128)S(1)} %get-tuple-element.80), channel_id=1, source_target_pairs={{4,8},{6,10},{8,4},{10,6},{5,9},{7,11},{9,5},{11,7},{20,24},{22,26... | collective-permute-start | bytes 3145736 | tf_op jit(solution)/shard_map/ppermute | solution.py:163
  113.5 47.9 %collective-permute-start.17 = (bf16[64,7168]{1,0:T(8,128)(2,1)}, bf16[64,7168]{1,0:T(8,128)(2,1)S(1)}, u32[]{:S(2)}, u32[]{:S(2)}) collective-permute-start(bf16[64,7168]{1,0:T(8,128)(2,1)} %broadcast_select_fusion), channel_id=1, source_target_pairs={{0,2},{2,0},{4,6},{6,4},{8,10},{10,8},{12,14},{14,12},{1,3},{3,1},... | collective-permute-start | bytes 2752520 | tf_op jit(solution)/shard_map/ppermute | solution.py:163
  114.0 47.4 %collective-permute-start.18 = (bf16[64,7168]{1,0:T(8,128)(2,1)S(1)}, bf16[64,7168]{1,0:T(8,128)(2,1)}, u32[]{:S(2)}, u32[]{:S(2)}) collective-permute-start(bf16[64,7168]{1,0:T(8,128)(2,1)S(1)} %collective-permute-done.15.refs_2_), channel_id=1, source_target_pairs={{4,0},{6,2},{8,12},{10,14},{5,1},{7,3},{9,13},{11,15},{20,16},{22,... | collective-permute-start | bytes 2752520 | tf_op jit(solution)/shard_map/ppermute | solution.py:163
  133.2 33.5 %collective-permute-start.23 = (bf16[64,7168]{1,0:T(8,128)(2,1)}, bf16[64,7168]{1,0:T(8,128)(2,1)}, u32[]{:S(2)}, u32[]{:S(2)}) collective-permute-start(bf16[64,7168]{1,0:T(8,128)(2,1)} %collective-permute-done.refs_3_), channel_id=1, source_target_pairs={{0,4},{2,6},{12,8},{14,10},{1,5},{3,7},{13,9},{15,11},{16,20},{18,... | collective-permute-start | bytes 2752520 | tf_op jit(solution)/shard_map/ppermute | solution.py:163
  140.7 17.2 %collective-permute-start.19 = (bf16[512,512]{1,0:T(8,128)(2,1)S(1)}, bf16[512,512]{1,0:T(8,128)(2,1)}, u32[]{:S(2)}, u32[]{:S(2)}) collective-permute-start(bf16[512,512]{1,0:T(8,128)(2,1)S(1)} %get-tuple-element.79), channel_id=1, source_target_pairs={{4,6},{6,4},{8,10},{10,8},{5,7},{7,5},{9,11},{11,9},{20,22},{22,20... | collective-permute-start | bytes 1572872 | tf_op jit(solution)/shard_map/ppermute | solution.py:163
  157.9 48.1 %collective-permute-start.27 = (f32[256,1792]{1,0:T(8,128)}, f32[256,1792]{1,0:T(8,128)}, u32[]{:S(2)}, u32[]{:S(2)}) collective-permute-start(f32[256,1792]{1,0:T(8,128)} %rotate.6.refs_0_), channel_id=1, source_target_pairs={{0,1},{1,0},{2,3},{3,2},{4,5},{5,4},{6,7},{7,6},{8,9},{9,8},{10,11... | collective-permute-start | bytes 5505032 | tf_op jit(solution)/shard_map/ppermute | solution.py:125
  158.0 29.6 %collective-permute-start.22 = (bf16[64,7168]{1,0:T(8,128)(2,1)}, bf16[64,7168]{1,0:T(8,128)(2,1)}, u32[]{:S(2)}, u32[]{:S(2)}) collective-permute-start(bf16[64,7168]{1,0:T(8,128)(2,1)} %collective-permute-done.8.refs_1_), channel_id=1, source_target_pairs={{0,2},{2,0},{12,14},{14,12},{1,3},{3,1},{13,15},{15,13},{16,18},{1... | collective-permute-start | bytes 2752520 | tf_op jit(solution)/shard_map/ppermute | solution.py:163
  164.5 17.2 %collective-permute-start.24 = (bf16[512,512]{1,0:T(8,128)(2,1)S(1)}, bf16[512,512]{1,0:T(8,128)(2,1)S(1)}, u32[]{:S(2)}, u32[]{:S(2)}) collective-permute-start(bf16[512,512]{1,0:T(8,128)(2,1)S(1)} %get-tuple-element.78), channel_id=1, source_target_pairs={{4,6},{6,4},{8,10},{10,8},{5,7},{7,5},{9,11},{11,9},{20,22},{22,20... | collective-permute-start | bytes 1572872 | tf_op jit(solution)/shard_map/ppermute | solution.py:163
  165.2 18.9 %collective-permute-start.25 = (bf16[512,512]{1,0:T(8,128)(2,1)S(1)}, bf16[512,512]{1,0:T(8,128)(2,1)}, u32[]{:S(2)}, u32[]{:S(2)}) collective-permute-start(bf16[512,512]{1,0:T(8,128)(2,1)S(1)} %get-tuple-element.77), channel_id=1, source_target_pairs={{4,8},{6,10},{8,4},{10,6},{5,9},{7,11},{9,5},{11,7},{20,24},{22,26... | collective-permute-start | bytes 1572872 | tf_op jit(solution)/shard_map/ppermute | solution.py:163
  166.7 37.9 %collective-permute-start.21 = (bf16[64,7168]{1,0:T(8,128)(2,1)S(1)}, bf16[64,7168]{1,0:T(8,128)(2,1)S(1)}, u32[]{:S(2)}, u32[]{:S(2)}) collective-permute-start(bf16[64,7168]{1,0:T(8,128)(2,1)S(1)} %copy-done.13), channel_id=1, source_target_pairs={{0,4},{2,6},{12,8},{14,10},{1,5},{3,7},{13,9},{15,11},{16,20},{18,... | collective-permute-start | bytes 2752520 | tf_op jit(solution)/shard_map/ppermute | solution.py:163
  181.7 34.8 %collective-permute-start.28 = (bf16[64,2048]{1,0:T(8,128)(2,1)S(1)}, bf16[64,2048]{1,0:T(8,128)(2,1)S(1)}, u32[]{:S(2)}, u32[]{:S(2)}) collective-permute-start(bf16[64,2048]{1,0:T(8,128)(2,1)S(1)} %slice.15), channel_id=1, source_target_pairs={{0,2},{2,0},{12,14},{14,12},{1,3},{3,1},{13,15},{15,13},{16,18},{1... | collective-permute-start | bytes 786440 | tf_op jit(solution)/shard_map/ppermute | solution.py:163
  184.2 21.9 %collective-permute-start.20 = (bf16[64,5120]{1,0:T(8,128)(2,1)S(1)}, bf16[64,5120]{1,0:T(8,128)(2,1)S(1)}, u32[]{:S(2)}, u32[]{:S(2)}) collective-permute-start(bf16[64,5120]{1,0:T(8,128)(2,1)S(1)} %slice.14), channel_id=1, source_target_pairs={{0,2},{2,0},{12,14},{14,12},{1,3},{3,1},{13,15},{15,13},{16,18},{1... | collective-permute-start | bytes 1966088 | tf_op jit(solution)/shard_map/ppermute | solution.py:163
  204.6 20.6 %collective-permute-start.30 = (bf16[512,512]{1,0:T(8,128)(2,1)S(1)}, bf16[512,512]{1,0:T(8,128)(2,1)}, u32[]{:S(2)}, u32[]{:S(2)}) collective-permute-start(bf16[512,512]{1,0:T(8,128)(2,1)S(1)} %get-tuple-element.77), channel_id=1, source_target_pairs={{4,0},{6,2},{8,12},{10,14},{5,1},{7,3},{9,13},{11,15},{20,16},{22,... | collective-permute-start | bytes 1572872 | tf_op jit(solution)/shard_map/ppermute | solution.py:163
  222.5 40.2 %collective-permute-start.29 = (f32[256,1792]{1,0:T(8,128)}, f32[256,1792]{1,0:T(8,128)S(1)}, u32[]{:S(2)}, u32[]{:S(2)}) collective-permute-start(f32[256,1792]{1,0:T(8,128)} %rotate.9.refs_2_), channel_id=1, source_target_pairs={{0,1},{1,0},{2,3},{3,2},{4,5},{5,4},{6,7},{7,6},{8,9},{9,8},{10,11... | collective-permute-start | bytes 5505032 | tf_op jit(solution)/shard_map/ppermute | solution.py:125
  222.5 17.6 %collective-permute-start.31 = (bf16[512,512]{1,0:T(8,128)(2,1)}, bf16[512,512]{1,0:T(8,128)(2,1)}, u32[]{:S(2)}, u32[]{:S(2)}) collective-permute-start(bf16[512,512]{1,0:T(8,128)(2,1)} %add_convert_fusion), channel_id=1, source_target_pairs={{4,0},{6,2},{8,12},{10,14},{5,1},{7,3},{9,13},{11,15},{20,16},{22,... | collective-permute-start | bytes 1572872 | tf_op jit(solution)/shard_map/ppermute | solution.py:163
  223.9 27.3 %collective-permute-start.32 = (bf16[512,512]{1,0:T(8,128)(2,1)}, bf16[512,512]{1,0:T(8,128)(2,1)S(1)}, u32[]{:S(2)}, u32[]{:S(2)}) collective-permute-start(bf16[512,512]{1,0:T(8,128)(2,1)} %collective-permute-done.25), channel_id=1, source_target_pairs={{4,0},{6,2},{8,12},{10,14},{5,1},{7,3},{9,13},{11,15},{20,16},{22,... | collective-permute-start | bytes 1572872 | tf_op jit(solution)/shard_map/ppermute | solution.py:163
  226.3 36.0 %collective-permute-start.33 = (bf16[512,512]{1,0:T(8,128)(2,1)}, bf16[512,512]{1,0:T(8,128)(2,1)S(1)}, u32[]{:S(2)}, u32[]{:S(2)}) collective-permute-start(bf16[512,512]{1,0:T(8,128)(2,1)} %copy-done.19), channel_id=1, source_target_pairs={{4,0},{6,2},{8,12},{10,14},{5,1},{7,3},{9,13},{11,15},{20,16},{22,... | collective-permute-start | bytes 1572872 | tf_op jit(solution)/shard_map/ppermute | solution.py:163
  (22 other events, 534.1 us)

commit v5 on v4

v5 whole, which is shorter than its diff:
```python
import jax
import jax.numpy as jnp
from jax import lax
from jax.experimental import pallas as pl
from jax.experimental.pallas import tpu as pltpu
from jax.sharding import PartitionSpec as P

EX = 2
LINE, PAIR = 4, 2
DEEP = 1024
BF16, F32 = jnp.bfloat16, jnp.float32


def dot(a, b):
    return jnp.dot(a, b, preferred_element_type=F32)


def fit_kernel(sizes, choices, order_ref, end_ref, place_ref, *refs):
    sum_refs, refs = refs[: 2 * len(sizes)], refs[2 * len(sizes) :]
    piece_refs, (fit_ref, out_ref, turned_ref, rot_ref) = refs[:-4], refs[-4:]
    rows, ks = out_ref.shape
    size, seq = rows // order_ref.shape[0], rows // EX

    @pl.when(pl.program_id(0) == 0)
    def _():
        at = 0
        for piece, choice in enumerate(choices):
            width = piece_refs[at].shape[1]
            there = pl.ds(pl.multiple_of(place_ref[piece] * width, width), width)
            if choice == 1:
                out_ref[:, there] = piece_refs[at][...]
            else:
                out_ref[:, there] = jnp.where(end_ref[0] == 1, piece_refs[at][...], piece_refs[at + 1][...])
            at += choice

    slot = 0
    for mine_ref, other_ref in zip(sum_refs[::2], sum_refs[1::2]):
        for at in range(0, mine_ref.shape[0], size):
            here = pl.ds(at, size)
            there = pl.ds(pl.multiple_of(order_ref[slot] * size, size), size)
            rot_ref[there, :] = mine_ref[here, :] + other_ref[here, :]
            slot += 1
    turned_ref[...] = rot_ref[...].T.astype(BF16)
    step = min(512, ks)
    for at in range(0, ks, step):
        total = None
        for e in range(EX):
            here = pl.ds(e * seq, seq)
            grad = dot(turned_ref[:, here], out_ref[here, pl.ds(at, step)])
            total = grad * grad if total is None else total + grad * grad
        fit_ref[:, pl.ds(at, step)] = total * (1.0 / EX)


def fit(order, end, sums, pieces, places):
    rows = sum(mine.shape[0] for mine, _ in sums)
    ka = sums[0][0].shape[1]
    ks = sum(piece[0].shape[1] for piece in pieces)
    tile = 256 if ka % 256 == 0 else ka
    flat = [a for pair in sums for a in pair]
    outs = [a for piece in pieces for a in piece]
    return pl.pallas_call(
        lambda *refs: fit_kernel([pair[0].shape[0] for pair in sums], [len(piece) for piece in pieces], *refs),
        out_shape=jax.ShapeDtypeStruct((ka, ks), F32),
        grid_spec=pltpu.PrefetchScalarGridSpec(
            num_scalar_prefetch=3,
            grid=(ka // tile,),
            in_specs=[pl.BlockSpec((a.shape[0], tile), lambda i, *_: (0, i)) for a in flat]
            + [pl.BlockSpec(a.shape, lambda i, *_: (0, 0)) for a in outs],
            out_specs=pl.BlockSpec((tile, ks), lambda i, *_: (i, 0)),
            scratch_shapes=[
                pltpu.VMEM((rows, ks), BF16),
                pltpu.VMEM((tile, rows), BF16),
                pltpu.VMEM((rows, tile), F32),
            ],
        ),
        compiler_params=pltpu.CompilerParams(vmem_limit_bytes=40 << 20),
        cost_estimate=pl.CostEstimate(
            flops=2 * rows * ka * ks, bytes_accessed=8 * rows * ka + 2 * rows * ks + 4 * ka * ks, transcendentals=0
        ),
        name="fit",
    )(order, end, places, *flat, *outs)


def rotate_kernel(choices, end_ref, *refs):
    blocks = refs[: sum(choices)]
    basis_ref, *before, sum_ref, rows_ref = refs[sum(choices) :]
    size = blocks[0].shape[0]
    at = 0
    for i, choice in enumerate(choices):
        here = pl.ds(i * size, size)
        if choice == 1:
            rows_ref[here, :] = blocks[at][...]
        else:
            rows_ref[here, :] = jnp.where(end_ref[0] == 1, blocks[at][...], blocks[at + 1][...])
        at += choice

    @pl.when(pl.program_id(0) == 0)
    def _():
        sum_ref[...] = before[0][...] if before else jnp.zeros_like(sum_ref)

    sum_ref[...] += dot(rows_ref[...], basis_ref[...])


def rotate(before, end, blocks, basis, first, steps):
    flat = [pair for block in blocks for pair in block]
    size, ka = flat[0][0].shape[0], basis.shape[1]
    rows = size * len(blocks)
    specs = []
    for block in blocks:
        for which, (_, skip) in enumerate(block):
            used = lambda e, which=which, n=len(block): 1 if n == 1 else jnp.where(e[0] == 1, 1 - which, which)
            specs.append(
                pl.BlockSpec((size, DEEP), lambda k, e, used=used, skip=skip: (0, (k + skip) * used(e)))
            )
    whole = pl.BlockSpec((rows, ka), lambda k, e: (0, 0))
    arrays = [a for a, _ in flat] + [basis] + ([] if before is None else [before])
    return pl.pallas_call(
        lambda *refs: rotate_kernel([len(block) for block in blocks], *refs),
        out_shape=jax.ShapeDtypeStruct((rows, ka), F32),
        grid_spec=pltpu.PrefetchScalarGridSpec(
            num_scalar_prefetch=1,
            grid=(steps,),
            in_specs=specs
            + [pl.BlockSpec((DEEP, ka), lambda k, e: (first + k, 0))]
            + ([] if before is None else [whole]),
            out_specs=whole,
            scratch_shapes=[pltpu.VMEM((rows, DEEP), BF16)],
        ),
        compiler_params=pltpu.CompilerParams(vmem_limit_bytes=40 << 20),
        cost_estimate=pl.CostEstimate(
            flops=rows * ka, bytes_accessed=4 * rows * ka, transcendentals=0
        ),
        name="rotate",
    )(end, *arrays)


def swap_narrow(a):
    return lax.ppermute(a, "narrow", [(0, 1), (1, 0)])


def general(inputs, deltas, basis_in, basis_out):
    partial_in = dot(lax.all_gather(inputs, "wide", axis=0, tiled=True), basis_in)
    rotated_out = lax.psum(dot(deltas, basis_out), "wide").astype(BF16)
    order, zero = jnp.arange(EX, dtype=jnp.int32), jnp.zeros((1,), jnp.int32)
    return fit(order, zero, [(partial_in, swap_narrow(partial_in))], [[rotated_out]], zero)


def pairs(step, where=lambda z: True):
    out = []
    for z in range(LINE):
        for x in range(PAIR):
            if where(z):
                tz, tx = step(z, x)
                out.append((z * PAIR + x, tz * PAIR + tx))
    return out


def corner(z):
    return z in (0, LINE - 1)


def middle(z):
    return not corner(z)


ENDS = pairs(lambda z, x: (z ^ 1, x))
TO_ENDS = pairs(lambda z, x: (z ^ 1, x), middle)
FROM_ENDS = pairs(lambda z, x: (z ^ 1, x), corner)
MIDDLE = pairs(lambda z, x: (3 - z, x), middle)
ACROSS = pairs(lambda z, x: (z, 1 - x))
ACROSS_ENDS = pairs(lambda z, x: (z, 1 - x), corner)
ACROSS_MIDDLE = pairs(lambda z, x: (z, 1 - x), middle)


def send(a, perm):
    return lax.ppermute(a, "wide", perm)


def scheduled(inputs, deltas, basis_in, basis_out):
    w = lax.axis_index("wide")
    z, x = w // PAIR, w % PAIR
    at_end = (z == 0) | (z == LINE - 1)
    end = at_end.astype(jnp.int32).reshape(1)
    half = (z >= 2).astype(jnp.int32)
    steps = inputs.shape[1] // DEEP
    some = steps // 2
    cuts = [0, 4 * steps // 14, 8 * steps // 14, 12 * steps // 14, steps]
    part = basis_out.shape[1] // 4
    got = {"own": inputs}

    def fence(*names):
        got.update(zip(names, lax.optimization_barrier(tuple(got[n] for n in names))))

    def pick(a, b):
        return jnp.where(at_end, got[a], got[b])

    def columns(a, h, p):
        return lax.dynamic_slice_in_dim(a, (2 * h + p) * part, part, 1)

    def turn(before, blocks, first, count):
        return rotate(before, end, [[(got[n], first) for n in block] for block in blocks], basis_in, first, count)

    def settle(p):
        got["sum", p] = (got["keep", p] + got["x5", p].astype(F32)).astype(BF16)
        got["m4", p] = send(got["sum", p], MIDDLE)
        got["n1", p] = send(got["sum", p], TO_ENDS)

    got["x1"] = send(got["own"], ACROSS)
    got["a1"] = send(got["own"], ENDS)
    got["m1"] = send(got["own"], MIDDLE)
    got["out"] = dot(deltas, basis_out)
    got["out16"] = got["out"].astype(BF16)
    fence("x1", "a1", "m1", "out", "out16")
    got["x2"] = send(pick("a1", "m1"), ACROSS)
    got["a2"] = send(got["m1"], TO_ENDS)
    got["m2"] = send(got["a1"], MIDDLE)
    got["r1"] = send(got["out16"], FROM_ENDS)
    got["A"] = turn(None, [["own"], ["a1"], ["x1"]], 0, steps)
    fence("x2", "a2", "m2", "r1", "A")
    got["x3"] = send(pick("a2", "m2"), ACROSS)
    got["a3"] = send(got["m2"], TO_ENDS)
    here = got["out"] + got["r1"].astype(F32)
    for p in range(2):
        got["keep", p], got["give", p] = columns(here, half, p), columns(here, 1 - half, p)
    got["m3", 0] = send(got["give", 0], MIDDLE)
    got["e"] = send(got["x1"], FROM_ENDS)
    got["B"] = turn(None, [["a2", "m1"], ["x2"]], 0, some)
    fence(("m3", 0), ("give", 1), "B")
    got["m3", 1] = send(got["give", 1], MIDDLE)
    got["keep", 0] += got["m3", 0]
    got["x5", 0] = send(got["keep", 0].astype(BF16), ACROSS_MIDDLE)
    got["B"] = turn(got["B"], [["a2", "m1"], ["x2"]], some, steps - some)
    fence("x3", "a3", "e", ("x5", 0), "B")
    def x4(piece):
        got["x4", piece] = send(got["a3"][:, cuts[piece] * DEEP : cuts[piece + 1] * DEEP], ACROSS_ENDS)

    def last(piece):
        first = cuts[piece]
        blocks = [[(got["x4", piece], 0), (got["e"], first)]]
        got["D"] = rotate(got.get("D"), end, blocks, basis_in, first, cuts[piece + 1] - first)

    x4(0)
    settle(0)
    got["C"] = turn(None, [["a3", "m2"], ["x3"]], 0, some)
    fence(("x4", 0), ("m3", 1), ("m4", 0), ("n1", 0), "A", "C", "a3")
    x4(1)
    got["keep", 1] += got["m3", 1]
    got["x5", 1] = send(got["keep", 1].astype(BF16), ACROSS_MIDDLE)
    got["n2", 0] = send(got["m4", 0], TO_ENDS)
    got["A2"] = swap_narrow(got["A"])
    got["C"] = turn(got["C"], [["a3", "m2"], ["x3"]], some, steps - some)
    fence(("x4", 1), ("x5", 1), ("n2", 0), "A2", "B", "C", "a3")
    x4(2)
    settle(1)
    got["B2"] = swap_narrow(got["B"])
    last(0)
    last(1)
    fence(("x4", 2), ("m4", 1), ("n1", 1), "B2", "C", "D", "a3")
    x4(3)
    got["n2", 1] = send(got["m4", 1], TO_ENDS)
    got["C2"] = swap_narrow(got["C"])
    last(2)
    fence(("x4", 3), "D")
    last(3)
    got["D2"] = swap_narrow(got["D"])

    flip = jnp.where(z >= 2, 3, 0)
    line = lambda a, b: jnp.where(at_end, a, b) ^ flip
    mine, other = (lambda a, b: line(a, b) * PAIR + x), (lambda a, b: line(a, b) * PAIR + 1 - x)
    order = [mine(0, 1), mine(1, 0), other(0, 1), mine(2, 2), other(1, 2), mine(3, 3), other(2, 3), other(3, 0)]
    pieces = [[got["n1", p], got["sum", p]] for p in range(2)] + [[got["n2", p], got["m4", p]] for p in range(2)]
    places = [2 * half, 2 * half + 1, 2 - 2 * half, 3 - 2 * half]
    sums = [(got[n], got[n + "2"]) for n in "ABCD"]
    return fit(jnp.stack(order).astype(jnp.int32), end, sums, pieces, jnp.stack(places).astype(jnp.int32))


def solution(mesh):
    return jax.shard_map(
        scheduled if mesh.shape["wide"] == LINE * PAIR else general,
        mesh=mesh,
        in_specs=(
            P(("grp", "wide"), "narrow"),
            P("grp", "wide"),
            P(("grp", "narrow"), "wide"),
            P(("grp", "wide"), "narrow"),
        ),
        out_specs=P(("grp", "wide"), "narrow"),
        check_vma=False,
    )
```

time: 280 us -> 271 us (0.968)
  waiting for transfers between devices: 108 us -> 61.4 us
  Pallas kernels: 74.8 us -> 111 us
  starting transfers between devices: 68.5 us -> 51.4 us
  local copies, waits for them, and re-layouts: 6.68 us -> 23.2 us
    ppermute x32 -> x24, waiting for transfers between devices: 108 us -> 61.4 us  [send(): return lax.ppermute(a, 'wide', perm)]
    pallas_call x5 -> x9, Pallas kernels: 58.7 us -> 98.8 us  [rotate(): pl.pallas_call(lambda *refs: rotate_kernel([len(block) for block in block...]
    ppermute x32 -> x24, starting transfers between devices: 68.5 us -> 51.1 us  [send(): return lax.ppermute(a, 'wide', perm)]
    unnamed x40 -> x62, local copies, waits for them, and re-layouts: 2.73 us -> 17 us
    pallas_call x1, Pallas kernels: 16.1 us -> 11.7 us  [fit(): pl.pallas_call(lambda *refs: fit_kernel([pair[0].shape[0] for pair in sum...]
    select_n x8 -> x2, other arithmetic: 6.03 us -> 5.86 us  [pick(): return jnp.where(at_end, got[a], got[b])]
  transfers between devices with their start and end apart: 34 -> 28, of which waited for: 8 -> 8; matrix products, arithmetic and copies ran while one was open for 8% -> 11% of each run, Pallas kernels for 21% -> 37%
where the time goes in v5:
time: 271 us; the launch traced here: 269 us
  Pallas kernels  111 us (41%)
  waiting for transfers between devices  61.4 us (23%)
  starting transfers between devices  51.4 us (19%)
  local copies, waits for them, and re-layouts  23.2 us (9%)
  other arithmetic  14.8 us (5%)
  matrix products  7.25 us (3%)
    pallas_call x9, Pallas kernels, rotate(): pl.pallas_call(lambda *refs: rotate_kernel([len(block) for block in block...  98.8 us
    ppermute x24, waiting for transfers between devices, send(): return lax.ppermute(a, 'wide', perm)  61.4 us
    ppermute x24, starting transfers between devices, send(): return lax.ppermute(a, 'wide', perm)  51.1 us
    unnamed x62, local copies, waits for them, and re-layouts  17 us
    pallas_call x1, Pallas kernels, fit(): pl.pallas_call(lambda *refs: fit_kernel([pair[0].shape[0] for pair in sum...  11.7 us
    dot_general x1, matrix products, dot(): return jnp.dot(a, b, preferred_element_type=F32)  7.25 us
    select_n x2, other arithmetic, pick(): return jnp.where(at_end, got[a], got[b])  5.86 us
  transfers between devices with their start and end apart: 28, of which 8 were waited for; matrix products, arithmetic and copies ran while one was open for 11% of the time, Pallas kernels for 37%

profile of v5, /device:TPU:0, one launch (start us, length us, event | category | flops | bytes accessed | tf_op | source)
XLA Modules:
  0.0 269.1 jit_solution(16185294503414887744)
XLA Ops:
  0.0 3.0 %collective-permute-start.1 = (bf16[64,14336]{1,0:T(8,128)(2,1)}, bf16[64,14336]{1,0:T(8,128)(2,1)}, u32[]{:S(2)}, u32[]{:S(2)}) collective-permute-start(bf16[64,14336]{1,0:T(8,128)(2,1)} %refs_1_.1), channel_id=1, source_target_pairs={{0,4},{2,6},{4,0},{6,2},{8,12},{10,14},{12,8},{14,10},{1,5},{3,7},... | collective-permute-start | bytes 5505032 | tf_op jit(solution)/shard_map/ppermute | solution.py:176
  4.5 1.9 collective-permute-start.2
  6.5 7.3 %fusion.2 = (bf16[512,2048]{1,0:T(8,128)(2,1)}, f32[512,2048]{1,0:T(8,128)}) fusion(bf16[512,1024]{1,0:T(8,128)(2,1)S(1)} %copy-done, bf16[1024,2048]{1,0:T(8,128)(2,1)} %param.7), kind=kOutput, calls=%fused_computation.12 | convolution fusion | flops 2148532224 | bytes 11534336 | tf_op jit(solution)/shard_map/dot_general | solution.py:15
  13.7 29.6 %collective-permute-done.1.refs_2_ = bf16[64,14336]{1,0:T(8,128)(2,1)} collective-permute-done((bf16[64,14336]{1,0:T(8,128)(2,1)}, bf16[64,14336]{1,0:T(8,128)(2,1)}, u32[]{:S(2)}, u32[]{:S(2)}) %collective-permute-start.1) | collective-permute-done | bytes 1835040 | tf_op jit(solution)/shard_map/ppermute | solution.py:176
  44.7 7.9 %collective-permute-start.6 = (bf16[512,2048]{1,0:T(8,128)(2,1)}, bf16[512,2048]{1,0:T(8,128)(2,1)}, u32[]{:S(2)}, u32[]{:S(2)}) collective-permute-start(bf16[512,2048]{1,0:T(8,128)(2,1)} %get-tuple-element.48), channel_id=1, source_target_pairs={{0,4},{2,6},{12,8},{14,10},{1,5},{3,7},{13,9},{15,11},{16,20},{18,... | collective-permute-start | bytes 6291464 | tf_op jit(solution)/shard_map/ppermute | solution.py:176
  52.6 2.9 %broadcast_select_fusion.1 = bf16[64,14336]{1,0:T(8,128)(2,1)} fusion(bf16[64,14336]{1,0:T(8,128)(2,1)} %collective-permute-done.1.refs_2_, bf16[64,14336]{1,0:T(8,128)(2,1)} %collective-permute-done.2.refs_2_, pred[]{:T(512)S(6)} %or.3), kind=kLoop, calls=%fused_computation.2 | loop fusion | flops 917504 | bytes 5505025 | tf_op jit(solution)/shard_map/jit(_where)/select_n | solution.py:195
  56.1 2.0 collective-permute-start.5
  59.3 5.9 %collective-permute-start.9 = (bf16[64,14336]{1,0:T(8,128)(2,1)}, bf16[64,14336]{1,0:T(8,128)(2,1)S(1)}, u32[]{:S(2)}, u32[]{:S(2)}) collective-permute-start(bf16[64,14336]{1,0:T(8,128)(2,1)} %copy-done.12), channel_id=1, source_target_pairs={{0,4},{2,6},{12,8},{14,10},{1,5},{3,7},{13,9},{15,11},{16,20},{18,... | collective-permute-start | bytes 5505032 | tf_op jit(solution)/shard_map/ppermute | solution.py:176
  68.2 23.8 %rotate.9.refs_3_ = f32[192,1792]{1,0:T(8,128)S(1)} custom-call(s32[1]{0:T(128)} %bitcast.8.refs_0_.refs_1_, bf16[64,14336]{1,0:T(8,128)(2,1)S(1)} %copy-done.11, bf16[64,14336]{1,0:T(8,128)(2,1)} %collective-permute-done.1.refs_2_, bf16[64,14336]{1,0:T(8,128)(2,1)S(1)} %copy-done.13, bf16[14336,1792]{1,0:T(8,128)(2,1)} %refs_3_.7), custom_call_target="tpu_custom_call" | custom-call | flops 344064 | bytes 1376256 | tf_op jit(solution)/shard_map/rotate/pallas_call | solution.py:117
  92.0 4.1 %collective-permute-done.3.refs_3_ = bf16[64,14336]{1,0:T(8,128)(2,1)} collective-permute-done((bf16[64,14336]{1,0:T(8,128)(2,1)}, bf16[64,14336]{1,0:T(8,128)(2,1)}, u32[]{:S(2)}, u32[]{:S(2)}) %collective-permute-start.3) | collective-permute-done | bytes 1835040 | tf_op jit(solution)/shard_map/ppermute | solution.py:176
  96.1 4.1 %collective-permute-done.4.refs_1_ = bf16[64,14336]{1,0:T(8,128)(2,1)} collective-permute-done((bf16[64,14336]{1,0:T(8,128)(2,1)}, bf16[64,14336]{1,0:T(8,128)(2,1)}, u32[]{:S(2)}, u32[]{:S(2)}) %collective-permute-start.4) | collective-permute-done | bytes 1835040 | tf_op jit(solution)/shard_map/ppermute | solution.py:176
  100.2 2.3 convert_add_fusion
  102.5 2.0 copy-done.27
  107.7 2.9 %broadcast_select_fusion = bf16[64,14336]{1,0:T(8,128)(2,1)} fusion(bf16[64,14336]{1,0:T(8,128)(2,1)} %collective-permute-done.4.refs_1_, bf16[64,14336]{1,0:T(8,128)(2,1)} %collective-permute-done.5.refs_2_, pred[]{:T(512)S(6)} %or.3), kind=kLoop, calls=%fused_computation.1 | loop fusion | flops 917504 | bytes 5505025 | tf_op jit(solution)/shard_map/jit(_where)/select_n | solution.py:195
  113.4 12.2 %rotate.10.refs_5_ = f32[128,1792]{1,0:T(8,128)S(1)} custom-call(s32[1]{0:T(128)} %bitcast.8.refs_0_.refs_1_, bf16[64,14336]{1,0:T(8,128)(2,1)} %collective-permute-done.4.refs_1_, bf16[64,14336]{1,0:T(8,128)(2,1)} %collective-permute-done.2.refs_2_, bf16[64,14336]{1,0:T(8,128)(2,1)} %collective-permute-done.3.refs_3_, bf16[14336,1792]{1,0:T(8,128)(2,1)} %refs_3_.7), custom_call_target="tpu_custom_call" | custom-call | flops 229376 | bytes 917504 | tf_op jit(solution)/shard_map/rotate/pallas_call | solution.py:117
  129.5 11.9 %rotate.11.refs_5_ = f32[128,1792]{1,0:T(8,128)S(1)} custom-call(s32[1]{0:T(128)} %bitcast.8.refs_0_.refs_1_, bf16[64,14336]{1,0:T(8,128)(2,1)} %collective-permute-done.4.refs_1_, bf16[64,14336]{1,0:T(8,128)(2,1)} %collective-permute-done.2.refs_2_, bf16[64,14336]{1,0:T(8,128)(2,1)} %collective-permute-done.3.refs_3_, bf16[14336,1792]{1,0:T(8,128)(2,1)} %refs_3_.7, ...), custom_call_target="tpu_custom_call" | custom-call | flops 229376 | bytes 917504 | tf_op jit(solution)/shard_map/rotate/pallas_call | solution.py:117
  141.5 8.5 %collective-permute-done.7.refs_3_ = bf16[64,14336]{1,0:T(8,128)(2,1)} collective-permute-done((bf16[64,14336]{1,0:T(8,128)(2,1)}, bf16[64,14336]{1,0:T(8,128)(2,1)}, u32[]{:S(2)}, u32[]{:S(2)}) %collective-permute-start.7) | collective-permute-done | bytes 1835040 | tf_op jit(solution)/shard_map/ppermute | solution.py:176
  150.0 3.1 %collective-permute-done.8.refs_1_ = bf16[64,14336]{1,0:T(8,128)(2,1)} collective-permute-done((bf16[64,14336]{1,0:T(8,128)(2,1)}, bf16[64,14336]{1,0:T(8,128)(2,1)}, u32[]{:S(2)}, u32[]{:S(2)}) %collective-permute-start.8) | collective-permute-done | bytes 1835040 | tf_op jit(solution)/shard_map/ppermute | solution.py:176
  155.8 2.4 collective-permute-start.12
  160.2 11.9 %rotate.12.refs_5_ = f32[128,1792]{1,0:T(8,128)S(1)} custom-call(s32[1]{0:T(128)} %bitcast.8.refs_0_.refs_1_, bf16[64,14336]{1,0:T(8,128)(2,1)} %collective-permute-done.8.refs_1_, bf16[64,14336]{1,0:T(8,128)(2,1)} %collective-permute-done.5.refs_2_, bf16[64,14336]{1,0:T(8,128)(2,1)} %collective-permute-done.7.refs_3_, bf16[14336,1792]{1,0:T(8,128)(2,1)} %refs_3_.7), custom_call_target="tpu_custom_call" | custom-call | flops 229376 | bytes 917504 | tf_op jit(solution)/shard_map/rotate/pallas_call | solution.py:117
  176.7 3.7 %collective-permute-start.16 = (bf16[64,4096]{1,0:T(8,128)(2,1)S(1)}, bf16[64,4096]{1,0:T(8,128)(2,1)S(1)}, u32[]{:S(2)}, u32[]{:S(2)}) collective-permute-start(bf16[64,4096]{1,0:T(8,128)(2,1)S(1)} %slice.13), channel_id=1, source_target_pairs={{0,2},{2,0},{12,14},{14,12},{1,3},{3,1},{13,15},{15,13},{16,18},{1... | collective-permute-start | bytes 1572872 | tf_op jit(solution)/shard_map/ppermute | solution.py:176
  184.3 12.8 %rotate.13.refs_7_ = f32[128,1792]{1,0:T(8,128)} custom-call(s32[1]{0:T(128)} %bitcast.8.refs_0_.refs_1_, bf16[64,14336]{1,0:T(8,128)(2,1)} %collective-permute-done.8.refs_1_, bf16[64,14336]{1,0:T(8,128)(2,1)} %collective-permute-done.5.refs_2_, bf16[64,14336]{1,0:T(8,128)(2,1)} %collective-permute-done.7.refs_3_, bf16[14336,1792]{1,0:T(8,128)(2,1)} %refs_3_.7, ...), custom_call_target="tpu_custom_call" | custom-call | flops 229376 | bytes 917504 | tf_op jit(solution)/shard_map/rotate/pallas_call | solution.py:117
  197.1 8.2 %collective-permute-done.18.refs_15_ = bf16[512,512]{1,0:T(8,128)(2,1)S(1)} collective-permute-done((bf16[512,512]{1,0:T(8,128)(2,1)S(1)}, bf16[512,512]{1,0:T(8,128)(2,1)S(1)}, u32[]{:S(2)}, u32[]{:S(2)}) %collective-permute-start.18) | collective-permute-done | bytes 524320 | tf_op jit(solution)/shard_map/ppermute | solution.py:176
  206.6 1.9 add_convert_fusion.refs_14_
  208.5 2.5 collective-permute-start.20
  213.8 7.1 %rotate.14.refs_4_ = f32[64,1792]{1,0:T(8,128)S(1)} custom-call(s32[1]{0:T(128)} %bitcast.8.refs_0_.refs_1_, bf16[64,4096]{1,0:T(8,128)(2,1)S(1)} %copy-done.17, bf16[64,14336]{1,0:T(8,128)(2,1)S(1)} %collective-permute-done.9.refs_2_, bf16[14336,1792]{1,0:T(8,128)(2,1)} %refs_3_.7), custom_call_target="tpu_custom_call" | custom-call | flops 114688 | bytes 458752 | tf_op jit(solution)/shard_map/rotate/pallas_call | solution.py:117
  220.8 7.1 %rotate.15.refs_4_ = f32[64,1792]{1,0:T(8,128)S(1)} custom-call(s32[1]{0:T(128)} %bitcast.8.refs_0_.refs_1_, bf16[64,4096]{1,0:T(8,128)(2,1)S(1)} %collective-permute-done.16.refs_1_, bf16[64,14336]{1,0:T(8,128)(2,1)S(1)} %collective-permute-done.9.refs_2_, bf16[14336,1792]{1,0:T(8,128)(2,1)} %refs_3_.7, f32[64,1792]{1,0:T(8,128)S(1)} %rotate.14.refs_4_), custom_call_target="tpu_custom_call" | custom-call | flops 114688 | bytes 458752 | tf_op jit(solution)/shard_map/rotate/pallas_call | solution.py:117
  229.3 3.4 %collective-permute-start.25 = (bf16[64,2048]{1,0:T(8,128)(2,1)S(1)}, bf16[64,2048]{1,0:T(8,128)(2,1)S(1)}, u32[]{:S(2)}, u32[]{:S(2)}) collective-permute-start(bf16[64,2048]{1,0:T(8,128)(2,1)S(1)} %slice.15), channel_id=1, source_target_pairs={{0,2},{2,0},{12,14},{14,12},{1,3},{3,1},{13,15},{15,13},{16,18},{1... | collective-permute-start | bytes 786440 | tf_op jit(solution)/shard_map/ppermute | solution.py:176
  234.2 7.1 %rotate.16.refs_4_ = f32[64,1792]{1,0:T(8,128)S(1)} custom-call(s32[1]{0:T(128)} %bitcast.8.refs_0_.refs_1_, bf16[64,4096]{1,0:T(8,128)(2,1)S(1)} %collective-permute-done.20.refs_1_, bf16[64,14336]{1,0:T(8,128)(2,1)S(1)} %collective-permute-done.9.refs_2_, bf16[14336,1792]{1,0:T(8,128)(2,1)} %refs_3_.7, f32[64,1792]{1,0:T(8,128)S(1)} %rotate.15.refs_4_), custom_call_target="tpu_custom_call" | custom-call | flops 114688 | bytes 458752 | tf_op jit(solution)/shard_map/rotate/pallas_call | solution.py:117
  241.4 4.8 %rotate.17.refs_9_ = f32[64,1792]{1,0:T(8,128)} custom-call(s32[1]{0:T(128)} %bitcast.8.refs_0_.refs_1_, bf16[64,2048]{1,0:T(8,128)(2,1)S(1)} %collective-permute-done.25.refs_1_, bf16[64,14336]{1,0:T(8,128)(2,1)S(1)} %collective-permute-done.9.refs_2_, bf16[14336,1792]{1,0:T(8,128)(2,1)} %refs_3_.7, f32[64,1792]{1,0:T(8,128)S(1)} %rotate.16.refs_4_), custom_call_target="tpu_custom_call" | custom-call | flops 114688 | bytes 458752 | tf_op jit(solution)/shard_map/rotate/pallas_call | solution.py:117
  246.4 2.4 collective-permute-done.27.refs_17_
  257.4 11.7 %fit.1 = f32[1792,2048]{1,0:T(8,128)} custom-call(s32[8]{0:T(128)S(1)} %stack.50.refs_0_, s32[1]{0:T(128)} %bitcast.8.refs_0_.refs_1_, s32[4]{0:T(128)S(1)} %pad_add_fusion.refs_2_, f32[192,1792]{1,0:T(8,128)S(1)} %rotate.9.refs_3_, f32[192,1792]{1,0:T(8,128)} %collective-permute-done.19.refs_4_, f32[128,1792]{1,0:T(8,128)S(1)} %copy-done.6, ...), custom_call_target="tpu_custom_call" | custom-call | flops 3758096384 | bytes 24117248 | tf_op jit(solution)/shard_map/fit/pallas_call | solution.py:61
  (111 shorter events, 46.1 us)
Async XLA Ops:
  0.0 43.3 %collective-permute-start.1 = (bf16[64,14336]{1,0:T(8,128)(2,1)}, bf16[64,14336]{1,0:T(8,128)(2,1)}, u32[]{:S(2)}, u32[]{:S(2)}) collective-permute-start(bf16[64,14336]{1,0:T(8,128)(2,1)} %refs_1_.1), channel_id=1, source_target_pairs={{0,4},{2,6},{4,0},{6,2},{8,12},{10,14},{12,8},{14,10},{1,5},{3,7},... | collective-permute-start | bytes 5505032 | tf_op jit(solution)/shard_map/ppermute | solution.py:176
  3.0 41.7 %collective-permute-start = (bf16[64,14336]{1,0:T(8,128)(2,1)}, bf16[64,14336]{1,0:T(8,128)(2,1)S(1)}, u32[]{:S(2)}, u32[]{:S(2)}) collective-permute-start(bf16[64,14336]{1,0:T(8,128)(2,1)} %refs_1_.1), channel_id=1, source_target_pairs={{0,2},{2,0},{4,6},{6,4},{8,10},{10,8},{12,14},{14,12},{1,3},{3,1},... | collective-permute-start | bytes 5505032 | tf_op jit(solution)/shard_map/ppermute | solution.py:176
  4.5 40.2 %collective-permute-start.2 = (bf16[64,14336]{1,0:T(8,128)(2,1)}, bf16[64,14336]{1,0:T(8,128)(2,1)}, u32[]{:S(2)}, u32[]{:S(2)}) collective-permute-start(bf16[64,14336]{1,0:T(8,128)(2,1)} %refs_1_.1), channel_id=1, source_target_pairs={{4,8},{6,10},{8,4},{10,6},{5,9},{7,11},{9,5},{11,7},{20,24},{22,26... | collective-permute-start | bytes 5505032 | tf_op jit(solution)/shard_map/ppermute | solution.py:176
  44.7 55.5 %collective-permute-start.6 = (bf16[512,2048]{1,0:T(8,128)(2,1)}, bf16[512,2048]{1,0:T(8,128)(2,1)}, u32[]{:S(2)}, u32[]{:S(2)}) collective-permute-start(bf16[512,2048]{1,0:T(8,128)(2,1)} %get-tuple-element.48), channel_id=1, source_target_pairs={{0,4},{2,6},{12,8},{14,10},{1,5},{3,7},{13,9},{15,11},{16,20},{18,... | collective-permute-start | bytes 6291464 | tf_op jit(solution)/shard_map/ppermute | solution.py:176
  55.5 40.6 %collective-permute-start.3 = (bf16[64,14336]{1,0:T(8,128)(2,1)}, bf16[64,14336]{1,0:T(8,128)(2,1)}, u32[]{:S(2)}, u32[]{:S(2)}) collective-permute-start(bf16[64,14336]{1,0:T(8,128)(2,1)} %broadcast_select_fusion.1), channel_id=1, source_target_pairs={{0,2},{2,0},{4,6},{6,4},{8,10},{10,8},{12,14},{14,12},{1,3},{3,1},... | collective-permute-start | bytes 5505032 | tf_op jit(solution)/shard_map/ppermute | solution.py:176
  56.1 40.1 %collective-permute-start.5 = (bf16[64,14336]{1,0:T(8,128)(2,1)}, bf16[64,14336]{1,0:T(8,128)(2,1)}, u32[]{:S(2)}, u32[]{:S(2)}) collective-permute-start(bf16[64,14336]{1,0:T(8,128)(2,1)} %collective-permute-done.1.refs_2_), channel_id=1, source_target_pairs={{4,8},{6,10},{8,4},{10,6},{5,9},{7,11},{9,5},{11,7},{20,24},{22,26... | collective-permute-start | bytes 5505032 | tf_op jit(solution)/shard_map/ppermute | solution.py:176
  58.0 42.2 %collective-permute-start.4 = (bf16[64,14336]{1,0:T(8,128)(2,1)}, bf16[64,14336]{1,0:T(8,128)(2,1)}, u32[]{:S(2)}, u32[]{:S(2)}) collective-permute-start(bf16[64,14336]{1,0:T(8,128)(2,1)} %collective-permute-done.2.refs_2_), channel_id=1, source_target_pairs={{4,0},{6,2},{8,12},{10,14},{5,1},{7,3},{9,13},{11,15},{20,16},{22,... | collective-permute-start | bytes 5505032 | tf_op jit(solution)/shard_map/ppermute | solution.py:176
  59.3 82.1 %collective-permute-start.9 = (bf16[64,14336]{1,0:T(8,128)(2,1)}, bf16[64,14336]{1,0:T(8,128)(2,1)S(1)}, u32[]{:S(2)}, u32[]{:S(2)}) collective-permute-start(bf16[64,14336]{1,0:T(8,128)(2,1)} %copy-done.12), channel_id=1, source_target_pairs={{0,4},{2,6},{12,8},{14,10},{1,5},{3,7},{13,9},{15,11},{16,20},{18,... | collective-permute-start | bytes 5505032 | tf_op jit(solution)/shard_map/ppermute | solution.py:176
  68.2 32.0 %copy-start.29 = (f32[512,2048]{1,0:T(8,128)S(1)}, f32[512,2048]{1,0:T(8,128)}, u32[]{:S(2)}) copy-start(f32[512,2048]{1,0:T(8,128)} %get-tuple-element.52) | copy-start | bytes 12582916
  106.0 19.6 %collective-permute-start.10 = (f32[512,512]{1,0:T(8,128)}, f32[512,512]{1,0:T(8,128)}, u32[]{:S(2)}, u32[]{:S(2)}) collective-permute-start(f32[512,512]{1,0:T(8,128)} %get-tuple-element.88), channel_id=1, source_target_pairs={{4,8},{6,10},{8,4},{10,6},{5,9},{7,11},{9,5},{11,7},{20,24},{22,26... | collective-permute-start | bytes 3145736 | tf_op jit(solution)/shard_map/ppermute | solution.py:176
  110.6 39.4 %collective-permute-start.7 = (bf16[64,14336]{1,0:T(8,128)(2,1)}, bf16[64,14336]{1,0:T(8,128)(2,1)}, u32[]{:S(2)}, u32[]{:S(2)}) collective-permute-start(bf16[64,14336]{1,0:T(8,128)(2,1)} %broadcast_select_fusion), channel_id=1, source_target_pairs={{0,2},{2,0},{4,6},{6,4},{8,10},{10,8},{12,14},{14,12},{1,3},{3,1},... | collective-permute-start | bytes 5505032 | tf_op jit(solution)/shard_map/ppermute | solution.py:176
  112.1 41.0 %collective-permute-start.8 = (bf16[64,14336]{1,0:T(8,128)(2,1)}, bf16[64,14336]{1,0:T(8,128)(2,1)}, u32[]{:S(2)}, u32[]{:S(2)}) collective-permute-start(bf16[64,14336]{1,0:T(8,128)(2,1)} %collective-permute-done.5.refs_2_), channel_id=1, source_target_pairs={{4,0},{6,2},{8,12},{10,14},{5,1},{7,3},{9,13},{11,15},{20,16},{22,... | collective-permute-start | bytes 5505032 | tf_op jit(solution)/shard_map/ppermute | solution.py:176
  127.1 14.3 %collective-permute-start.11 = (bf16[512,512]{1,0:T(8,128)(2,1)S(1)}, bf16[512,512]{1,0:T(8,128)(2,1)S(1)}, u32[]{:S(2)}, u32[]{:S(2)}) collective-permute-start(bf16[512,512]{1,0:T(8,128)(2,1)S(1)} %fusion), channel_id=1, source_target_pairs={{4,6},{6,4},{8,10},{10,8},{5,7},{7,5},{9,11},{11,9},{20,22},{22,20... | collective-permute-start | bytes 1572872 | tf_op jit(solution)/shard_map/ppermute | solution.py:176
  127.9 45.2 %collective-permute-start.13 = (f32[512,512]{1,0:T(8,128)S(1)}, f32[512,512]{1,0:T(8,128)}, u32[]{:S(2)}, u32[]{:S(2)}) collective-permute-start(f32[512,512]{1,0:T(8,128)S(1)} %copy-done.30), channel_id=1, source_target_pairs={{4,8},{6,10},{8,4},{10,6},{5,9},{7,11},{9,5},{11,7},{20,24},{22,26... | collective-permute-start | bytes 3145736 | tf_op jit(solution)/shard_map/ppermute | solution.py:176
  155.8 16.4 %copy-start.7 = (bf16[512,512]{1,0:T(8,128)(2,1)}, bf16[512,512]{1,0:T(8,128)(2,1)S(1)}, u32[]{:S(2)}) copy-start(bf16[512,512]{1,0:T(8,128)(2,1)S(1)} %add_convert_fusion.1.refs_12_) | copy-start | bytes 1572868
  155.8 17.3 %collective-permute-start.12 = (bf16[64,4096]{1,0:T(8,128)(2,1)S(1)}, bf16[64,4096]{1,0:T(8,128)(2,1)S(1)}, u32[]{:S(2)}, u32[]{:S(2)}) collective-permute-start(bf16[64,4096]{1,0:T(8,128)(2,1)S(1)} %slice.12), channel_id=1, source_target_pairs={{0,2},{2,0},{12,14},{14,12},{1,3},{3,1},{13,15},{15,13},{16,18},{1... | collective-permute-start | bytes 1572872 | tf_op jit(solution)/shard_map/ppermute | solution.py:176
  158.2 15.7 %collective-permute-start.15 = (bf16[512,512]{1,0:T(8,128)(2,1)S(1)}, bf16[512,512]{1,0:T(8,128)(2,1)S(1)}, u32[]{:S(2)}, u32[]{:S(2)}) collective-permute-start(bf16[512,512]{1,0:T(8,128)(2,1)S(1)} %add_convert_fusion.1.refs_12_), channel_id=1, source_target_pairs={{4,0},{6,2},{8,12},{10,14},{5,1},{7,3},{9,13},{11,15},{20,16},{22,... | collective-permute-start | bytes 1572872 | tf_op jit(solution)/shard_map/ppermute | solution.py:176
  159.5 15.2 %collective-permute-start.14 = (bf16[512,512]{1,0:T(8,128)(2,1)S(1)}, bf16[512,512]{1,0:T(8,128)(2,1)S(1)}, u32[]{:S(2)}, u32[]{:S(2)}) collective-permute-start(bf16[512,512]{1,0:T(8,128)(2,1)S(1)} %add_convert_fusion.1.refs_12_), channel_id=1, source_target_pairs={{4,8},{6,10},{8,4},{10,6},{5,9},{7,11},{9,5},{11,7},{20,24},{22,26... | collective-permute-start | bytes 1572872 | tf_op jit(solution)/shard_map/ppermute | solution.py:176
  175.5 29.8 %collective-permute-start.19 = (f32[192,1792]{1,0:T(8,128)S(1)}, f32[192,1792]{1,0:T(8,128)}, u32[]{:S(2)}, u32[]{:S(2)}) collective-permute-start(f32[192,1792]{1,0:T(8,128)S(1)} %rotate.9.refs_3_), channel_id=1, source_target_pairs={{0,1},{1,0},{2,3},{3,2},{4,5},{5,4},{6,7},{7,6},{8,9},{9,8},{10,11... | collective-permute-start | bytes 4128776 | tf_op jit(solution)/shard_map/ppermute | solution.py:138
  176.7 20.4 %collective-permute-start.16 = (bf16[64,4096]{1,0:T(8,128)(2,1)S(1)}, bf16[64,4096]{1,0:T(8,128)(2,1)S(1)}, u32[]{:S(2)}, u32[]{:S(2)}) collective-permute-start(bf16[64,4096]{1,0:T(8,128)(2,1)S(1)} %slice.13), channel_id=1, source_target_pairs={{0,2},{2,0},{12,14},{14,12},{1,3},{3,1},{13,15},{15,13},{16,18},{1... | collective-permute-start | bytes 1572872 | tf_op jit(solution)/shard_map/ppermute | solution.py:176
  182.1 23.2 %copy-start.5 = (f32[128,1792]{1,0:T(8,128)S(1)}, f32[128,1792]{1,0:T(8,128)}, u32[]{:S(2)}) copy-start(f32[128,1792]{1,0:T(8,128)} %copy-done.4) | copy-start | bytes 2752516
  182.1 15.0 %collective-permute-start.17 = (bf16[512,512]{1,0:T(8,128)(2,1)S(1)}, bf16[512,512]{1,0:T(8,128)(2,1)S(1)}, u32[]{:S(2)}, u32[]{:S(2)}) collective-permute-start(bf16[512,512]{1,0:T(8,128)(2,1)S(1)} %fusion.1), channel_id=1, source_target_pairs={{4,6},{6,4},{8,10},{10,8},{5,7},{7,5},{9,11},{11,9},{20,22},{22,20... | collective-permute-start | bytes 1572872 | tf_op jit(solution)/shard_map/ppermute | solution.py:176
  183.0 22.4 %collective-permute-start.18 = (bf16[512,512]{1,0:T(8,128)(2,1)S(1)}, bf16[512,512]{1,0:T(8,128)(2,1)S(1)}, u32[]{:S(2)}, u32[]{:S(2)}) collective-permute-start(bf16[512,512]{1,0:T(8,128)(2,1)S(1)} %copy-done.21), channel_id=1, source_target_pairs={{4,0},{6,2},{8,12},{10,14},{5,1},{7,3},{9,13},{11,15},{20,16},{22,... | collective-permute-start | bytes 1572872 | tf_op jit(solution)/shard_map/ppermute | solution.py:176
  197.1 16.7 %copy-start.17 = (bf16[64,4096]{1,0:T(8,128)(2,1)S(1)}, bf16[64,4096]{1,0:T(8,128)(2,1)}, u32[]{:S(2)}) copy-start(bf16[64,4096]{1,0:T(8,128)(2,1)} %copy-done.16) | copy-start | bytes 1572868
  205.3 22.7 %collective-permute-start.23 = (f32[128,1792]{1,0:T(8,128)S(1)}, f32[128,1792]{1,0:T(8,128)S(1)}, u32[]{:S(2)}, u32[]{:S(2)}) collective-permute-start(f32[128,1792]{1,0:T(8,128)S(1)} %copy-done.5), channel_id=1, source_target_pairs={{0,1},{1,0},{2,3},{3,2},{4,5},{5,4},{6,7},{7,6},{8,9},{9,8},{10,11... | collective-permute-start | bytes 2752520 | tf_op jit(solution)/shard_map/ppermute | solution.py:138
  208.5 19.5 %collective-permute-start.20 = (bf16[64,4096]{1,0:T(8,128)(2,1)S(1)}, bf16[64,4096]{1,0:T(8,128)(2,1)S(1)}, u32[]{:S(2)}, u32[]{:S(2)}) collective-permute-start(bf16[64,4096]{1,0:T(8,128)(2,1)S(1)} %slice.14), channel_id=1, source_target_pairs={{0,2},{2,0},{12,14},{14,12},{1,3},{3,1},{13,15},{15,13},{16,18},{1... | collective-permute-start | bytes 1572872 | tf_op jit(solution)/shard_map/ppermute | solution.py:176
  211.0 17.0 %collective-permute-start.22 = (bf16[512,512]{1,0:T(8,128)(2,1)S(1)}, bf16[512,512]{1,0:T(8,128)(2,1)S(1)}, u32[]{:S(2)}, u32[]{:S(2)}) collective-permute-start(bf16[512,512]{1,0:T(8,128)(2,1)S(1)} %add_convert_fusion.refs_14_), channel_id=1, source_target_pairs={{4,0},{6,2},{8,12},{10,14},{5,1},{7,3},{9,13},{11,15},{20,16},{22,... | collective-permute-start | bytes 1572872 | tf_op jit(solution)/shard_map/ppermute | solution.py:176
  212.3 15.7 %collective-permute-start.21 = (bf16[512,512]{1,0:T(8,128)(2,1)S(1)}, bf16[512,512]{1,0:T(8,128)(2,1)}, u32[]{:S(2)}, u32[]{:S(2)}) collective-permute-start(bf16[512,512]{1,0:T(8,128)(2,1)S(1)} %add_convert_fusion.refs_14_), channel_id=1, source_target_pairs={{4,8},{6,10},{8,4},{10,6},{5,9},{7,11},{9,5},{11,7},{20,24},{22,26... | collective-permute-start | bytes 1572872 | tf_op jit(solution)/shard_map/ppermute | solution.py:176
  228.0 20.7 %collective-permute-start.24 = (f32[128,1792]{1,0:T(8,128)}, f32[128,1792]{1,0:T(8,128)}, u32[]{:S(2)}, u32[]{:S(2)}) collective-permute-start(f32[128,1792]{1,0:T(8,128)} %rotate.13.refs_7_), channel_id=1, source_target_pairs={{0,1},{1,0},{2,3},{3,2},{4,5},{5,4},{6,7},{7,6},{8,9},{9,8},{10,11... | collective-permute-start | bytes 2752520 | tf_op jit(solution)/shard_map/ppermute | solution.py:138
  229.3 12.0 %collective-permute-start.25 = (bf16[64,2048]{1,0:T(8,128)(2,1)S(1)}, bf16[64,2048]{1,0:T(8,128)(2,1)S(1)}, u32[]{:S(2)}, u32[]{:S(2)}) collective-permute-start(bf16[64,2048]{1,0:T(8,128)(2,1)S(1)} %slice.15), channel_id=1, source_target_pairs={{0,2},{2,0},{12,14},{14,12},{1,3},{3,1},{13,15},{15,13},{16,18},{1... | collective-permute-start | bytes 786440 | tf_op jit(solution)/shard_map/ppermute | solution.py:176
  232.8 16.0 %collective-permute-start.27 = (bf16[512,512]{1,0:T(8,128)(2,1)}, bf16[512,512]{1,0:T(8,128)(2,1)}, u32[]{:S(2)}, u32[]{:S(2)}) collective-permute-start(bf16[512,512]{1,0:T(8,128)(2,1)} %collective-permute-done.21.refs_18_), channel_id=1, source_target_pairs={{4,0},{6,2},{8,12},{10,14},{5,1},{7,3},{9,13},{11,15},{20,16},{22,... | collective-permute-start | bytes 1572872 | tf_op jit(solution)/shard_map/ppermute | solution.py:176
  246.2 2.5 collective-permute-start.26
  (27 other events, 136.9 us)

commit v6 on v5

--- a/solution.py
+++ b/solution.py
@@ -8,6 +8,7 @@
 EX = 2
 LINE, PAIR = 4, 2
 DEEP = 1024
+VMEM = 20 << 20
 BF16, F32 = jnp.bfloat16, jnp.float32
 
 
@@ -73,7 +74,7 @@
                 pltpu.VMEM((rows, tile), F32),
             ],
         ),
-        compiler_params=pltpu.CompilerParams(vmem_limit_bytes=40 << 20),
+        compiler_params=pltpu.CompilerParams(vmem_limit_bytes=VMEM),
         cost_estimate=pl.CostEstimate(
             flops=2 * rows * ka * ks, bytes_accessed=8 * rows * ka + 2 * rows * ks + 4 * ka * ks, transcendentals=0
         ),
@@ -126,7 +127,7 @@
             out_specs=whole,
             scratch_shapes=[pltpu.VMEM((rows, DEEP), BF16)],
         ),
-        compiler_params=pltpu.CompilerParams(vmem_limit_bytes=40 << 20),
+        compiler_params=pltpu.CompilerParams(vmem_limit_bytes=VMEM),
         cost_estimate=pl.CostEstimate(
             flops=rows * ka, bytes_accessed=4 * rows * ka, transcendentals=0
         ),
@@ -183,7 +184,6 @@
     end = at_end.astype(jnp.int32).reshape(1)
     half = (z >= 2).astype(jnp.int32)
     steps = inputs.shape[1] // DEEP
-    some = steps // 2
     cuts = [0, 4 * steps // 14, 8 * steps // 14, 12 * steps // 14, steps]
     part = basis_out.shape[1] // 4
     got = {"own": inputs}
@@ -211,56 +211,58 @@
     got["out"] = dot(deltas, basis_out)
     got["out16"] = got["out"].astype(BF16)
     fence("x1", "a1", "m1", "out", "out16")
-    got["x2"] = send(pick("a1", "m1"), ACROSS)
+    got["pick"] = pick("a1", "m1")
+    fence("pick", "a1", "m1", "out16")
+    got["x2"] = send(got["pick"], ACROSS)
     got["a2"] = send(got["m1"], TO_ENDS)
     got["m2"] = send(got["a1"], MIDDLE)
     got["r1"] = send(got["out16"], FROM_ENDS)
     got["A"] = turn(None, [["own"], ["a1"], ["x1"]], 0, steps)
-    fence("x2", "a2", "m2", "r1", "A")
-    got["x3"] = send(pick("a2", "m2"), ACROSS)
+    fence("x1", "x2", "a2", "m2", "r1", "A")
+    got["pick"] = pick("a2", "m2")
+    fence("pick", "m2", "x1", "out")
+    got["x3"] = send(got["pick"], ACROSS)
     got["a3"] = send(got["m2"], TO_ENDS)
     here = got["out"] + got["r1"].astype(F32)
     for p in range(2):
-        got["keep", p], got["give", p] = columns(here, half, p), columns(here, 1 - half, p)
-    got["m3", 0] = send(got["give", 0], MIDDLE)
+        got["keep", p] = columns(here, half, p)
+        got["m3", p] = send(columns(here, 1 - half, p), MIDDLE)
     got["e"] = send(got["x1"], FROM_ENDS)
-    got["B"] = turn(None, [["a2", "m1"], ["x2"]], 0, some)
-    fence(("m3", 0), ("give", 1), "B")
-    got["m3", 1] = send(got["give", 1], MIDDLE)
-    got["keep", 0] += got["m3", 0]
-    got["x5", 0] = send(got["keep", 0].astype(BF16), ACROSS_MIDDLE)
-    got["B"] = turn(got["B"], [["a2", "m1"], ["x2"]], some, steps - some)
-    fence("x3", "a3", "e", ("x5", 0), "B")
+    got["B"] = turn(None, [["a2", "m1"], ["x2"]], 0, steps)
+    fence("x3", "a3", "e", "B")
+
     def x4(piece):
         got["x4", piece] = send(got["a3"][:, cuts[piece] * DEEP : cuts[piece + 1] * DEEP], ACROSS_ENDS)
 
     def last(piece):
         first = cuts[piece]
-        blocks = [[(got["x4", piece], 0), (got["e"], first)]]
+        blocks = [[(got["a3"], first), (got["m2"], first)], [(got["x3"], first)], [(got["x4", piece], 0), (got["e"], first)]]
         got["D"] = rotate(got.get("D"), end, blocks, basis_in, first, cuts[piece + 1] - first)
 
+    def cross(p):
+        got["keep", p] += got["m3", p]
+        got["x5", p] = send(got["keep", p].astype(BF16), ACROSS_MIDDLE)
+
     x4(0)
+    fence(("m3", 0), ("m3", 1), "a3")
+    cross(0)
+    cross(1)
+    fence(("x4", 0), ("x5", 0), "a3")
+    x4(1)
     settle(0)
-    got["C"] = turn(None, [["a3", "m2"], ["x3"]], 0, some)
-    fence(("x4", 0), ("m3", 1), ("m4", 0), ("n1", 0), "A", "C", "a3")
-    x4(1)
-    got["keep", 1] += got["m3", 1]
-    got["x5", 1] = send(got["keep", 1].astype(BF16), ACROSS_MIDDLE)
+    last(0)
+    fence(("x4", 1), ("x5", 1), ("m4", 0), ("n1", 0), "D", "a3")
+    x4(2)
     got["n2", 0] = send(got["m4", 0], TO_ENDS)
-    got["A2"] = swap_narrow(got["A"])
-    got["C"] = turn(got["C"], [["a3", "m2"], ["x3"]], some, steps - some)
-    fence(("x4", 1), ("x5", 1), ("n2", 0), "A2", "B", "C", "a3")
-    x4(2)
     settle(1)
-    got["B2"] = swap_narrow(got["B"])
-    last(0)
     last(1)
-    fence(("x4", 2), ("m4", 1), ("n1", 1), "B2", "C", "D", "a3")
+    fence(("x4", 2), ("m4", 1), ("n1", 1), ("n2", 0), "A", "B", "D", "a3")
     x4(3)
     got["n2", 1] = send(got["m4", 1], TO_ENDS)
-    got["C2"] = swap_narrow(got["C"])
+    got["A2"] = swap_narrow(got["A"])
+    got["B2"] = swap_narrow(got["B"])
     last(2)
-    fence(("x4", 3), "D")
+    fence(("x4", 3), ("n2", 1), "A2", "B2", "D")
     last(3)
     got["D2"] = swap_narrow(got["D"])
 
@@ -270,7 +272,7 @@
     order = [mine(0, 1), mine(1, 0), other(0, 1), mine(2, 2), other(1, 2), mine(3, 3), other(2, 3), other(3, 0)]
     pieces = [[got["n1", p], got["sum", p]] for p in range(2)] + [[got["n2", p], got["m4", p]] for p in range(2)]
     places = [2 * half, 2 * half + 1, 2 - 2 * half, 3 - 2 * half]
-    sums = [(got[n], got[n + "2"]) for n in "ABCD"]
+    sums = [(got[n], got[n + "2"]) for n in "ABD"]
     return fit(jnp.stack(order).astype(jnp.int32), end, sums, pieces, jnp.stack(places).astype(jnp.int32))
 
 

time: 271 us -> 274 us (1.011)
  waiting for transfers between devices: 61.4 us -> 88.2 us
  Pallas kernels: 111 us -> 86.4 us
    ppermute x24, waiting for transfers between devices: 61.4 us -> 85 us  [send(): return lax.ppermute(a, 'wide', perm)]
    pallas_call x9 -> x6, Pallas kernels: 98.8 us -> 75.7 us  [rotate(): pl.pallas_call(lambda *refs: rotate_kernel([len(block) for block in block...]
    ppermute x4 -> x3, waiting for transfers between devices: 0.01 us -> 3.13 us  [swap_narrow(): return lax.ppermute(a, 'narrow', [(0, 1), (1, 0)])]
    unnamed x62 -> x68, local copies, waits for them, and re-layouts: 17 us -> 18 us
  transfers between devices with their start and end apart: 28 -> 27, of which waited for: 8 -> 12; matrix products, arithmetic and copies ran while one was open for 11% -> 7% of each run, Pallas kernels for 37% -> 25%
where the time goes in v6:
time: 274 us; the launch traced here: 272 us
  waiting for transfers between devices  88.2 us (32%)
  Pallas kernels  86.4 us (32%)
  starting transfers between devices  51 us (19%)
  local copies, waits for them, and re-layouts  24.1 us (9%)
  other arithmetic  14.6 us (5%)
  matrix products  7.28 us (3%)
    ppermute x24, waiting for transfers between devices, send(): return lax.ppermute(a, 'wide', perm)  85 us
    pallas_call x6, Pallas kernels, rotate(): pl.pallas_call(lambda *refs: rotate_kernel([len(block) for block in block...  75.7 us
    ppermute x24, starting transfers between devices, send(): return lax.ppermute(a, 'wide', perm)  50.4 us
    unnamed x68, local copies, waits for them, and re-layouts  18 us
    pallas_call x1, Pallas kernels, fit(): pl.pallas_call(lambda *refs: fit_kernel([pair[0].shape[0] for pair in sum...  10.7 us
    dot_general x1, matrix products, dot(): return jnp.dot(a, b, preferred_element_type=F32)  7.28 us
  transfers between devices with their start and end apart: 27, of which 12 were waited for; matrix products, arithmetic and copies ran while one was open for 7% of the time, Pallas kernels for 25%

profile of v6, /device:TPU:0, one launch (start us, length us, event | category | flops | bytes accessed | tf_op | source)
XLA Modules:
  0.0 272.1 jit_solution(11798426230399303348)
XLA Ops:
  0.0 3.0 %collective-permute-start.1 = (bf16[64,14336]{1,0:T(8,128)(2,1)}, bf16[64,14336]{1,0:T(8,128)(2,1)S(1)}, u32[]{:S(2)}, u32[]{:S(2)}) collective-permute-start(bf16[64,14336]{1,0:T(8,128)(2,1)} %refs_1_.1), channel_id=1, source_target_pairs={{0,4},{2,6},{4,0},{6,2},{8,12},{10,14},{12,8},{14,10},{1,5},{3,7},... | collective-permute-start | bytes 5505032 | tf_op jit(solution)/shard_map/ppermute | solution.py:177
  4.5 1.9 collective-permute-start.2
  6.4 7.3 %fusion.2 = (bf16[512,2048]{1,0:T(8,128)(2,1)}, f32[512,2048]{1,0:T(8,128)}) fusion(bf16[512,1024]{1,0:T(8,128)(2,1)S(1)} %copy-done, bf16[1024,2048]{1,0:T(8,128)(2,1)} %param.7), kind=kOutput, calls=%fused_computation.12 | convolution fusion | flops 2148532224 | bytes 11534336 | tf_op jit(solution)/shard_map/dot_general | solution.py:16
  13.7 29.6 %collective-permute-done.1.refs_2_ = bf16[64,14336]{1,0:T(8,128)(2,1)S(1)} collective-permute-done((bf16[64,14336]{1,0:T(8,128)(2,1)}, bf16[64,14336]{1,0:T(8,128)(2,1)S(1)}, u32[]{:S(2)}, u32[]{:S(2)}) %collective-permute-start.1) | collective-permute-done | bytes 1835040 | tf_op jit(solution)/shard_map/ppermute | solution.py:177
  46.2 9.3 %collective-permute-start.6 = (bf16[512,2048]{1,0:T(8,128)(2,1)}, bf16[512,2048]{1,0:T(8,128)(2,1)}, u32[]{:S(2)}, u32[]{:S(2)}) collective-permute-start(bf16[512,2048]{1,0:T(8,128)(2,1)} %get-tuple-element.60), channel_id=1, source_target_pairs={{0,4},{2,6},{12,8},{14,10},{1,5},{3,7},{13,9},{15,11},{16,20},{18,... | collective-permute-start | bytes 6291464 | tf_op jit(solution)/shard_map/ppermute | solution.py:177
  61.1 23.7 %rotate.6.refs_3_ = f32[192,1792]{1,0:T(8,128)S(1)} custom-call(s32[1]{0:T(128)} %bitcast.8.refs_0_.refs_1_, bf16[64,14336]{1,0:T(8,128)(2,1)S(1)} %copy-done.12, bf16[64,14336]{1,0:T(8,128)(2,1)S(1)} %copy-done.3, bf16[64,14336]{1,0:T(8,128)(2,1)} %collective-permute-done.refs_3_, bf16[14336,1792]{1,0:T(8,128)(2,1)} %refs_6_.7), custom_call_target="tpu_custom_call" | custom-call | flops 344064 | bytes 1376256 | tf_op jit(solution)/shard_map/rotate/pallas_call | solution.py:118
  84.8 11.3 %collective-permute-done.3.refs_3_ = bf16[64,14336]{1,0:T(8,128)(2,1)} collective-permute-done((bf16[64,14336]{1,0:T(8,128)(2,1)}, bf16[64,14336]{1,0:T(8,128)(2,1)}, u32[]{:S(2)}, u32[]{:S(2)}) %collective-permute-start.3) | collective-permute-done | bytes 1835040 | tf_op jit(solution)/shard_map/ppermute | solution.py:177
  96.1 2.1 collective-permute-done.4.refs_1_
  98.3 2.9 %broadcast_select_fusion = bf16[64,14336]{1,0:T(8,128)(2,1)} fusion(bf16[64,14336]{1,0:T(8,128)(2,1)} %collective-permute-done.4.refs_1_, bf16[64,14336]{1,0:T(8,128)(2,1)S(1)} %collective-permute-done.5.refs_2_, pred[]{:T(512)S(6)} %or.3), kind=kLoop, calls=%fused_computation.1 | loop fusion | flops 917504 | bytes 5505025 | tf_op jit(solution)/shard_map/jit(_where)/select_n | solution.py:195
  102.7 6.5 %collective-permute-start.9 = (bf16[64,14336]{1,0:T(8,128)(2,1)}, bf16[64,14336]{1,0:T(8,128)(2,1)}, u32[]{:S(2)}, u32[]{:S(2)}) collective-permute-start(bf16[64,14336]{1,0:T(8,128)(2,1)} %collective-permute-done.refs_3_), channel_id=1, source_target_pairs={{0,4},{2,6},{12,8},{14,10},{1,5},{3,7},{13,9},{15,11},{16,20},{18,... | collective-permute-start | bytes 5505032 | tf_op jit(solution)/shard_map/ppermute | solution.py:177
  110.5 2.5 convert_add_fusion
  118.9 22.4 %rotate.7.refs_5_ = f32[128,1792]{1,0:T(8,128)S(1)} custom-call(s32[1]{0:T(128)} %bitcast.8.refs_0_.refs_1_, bf16[64,14336]{1,0:T(8,128)(2,1)} %collective-permute-done.4.refs_1_, bf16[64,14336]{1,0:T(8,128)(2,1)} %collective-permute-done.2.refs_2_, bf16[64,14336]{1,0:T(8,128)(2,1)} %collective-permute-done.3.refs_3_, bf16[14336,1792]{1,0:T(8,128)(2,1)} %refs_6_.7), custom_call_target="tpu_custom_call" | custom-call | flops 229376 | bytes 917504 | tf_op jit(solution)/shard_map/rotate/pallas_call | solution.py:118
  141.3 2.9 %collective-permute-done.9.refs_5_ = bf16[64,14336]{1,0:T(8,128)(2,1)} collective-permute-done((bf16[64,14336]{1,0:T(8,128)(2,1)}, bf16[64,14336]{1,0:T(8,128)(2,1)}, u32[]{:S(2)}, u32[]{:S(2)}) %collective-permute-start.9) | collective-permute-done | bytes 1835040 | tf_op jit(solution)/shard_map/ppermute | solution.py:177
  144.2 5.2 %collective-permute-done.8.refs_1_ = bf16[64,14336]{1,0:T(8,128)(2,1)} collective-permute-done((bf16[64,14336]{1,0:T(8,128)(2,1)S(1)}, bf16[64,14336]{1,0:T(8,128)(2,1)}, u32[]{:S(2)}, u32[]{:S(2)}) %collective-permute-start.8) | collective-permute-done | bytes 1835040 | tf_op jit(solution)/shard_map/ppermute | solution.py:177
  150.5 2.5 collective-permute-start.10
  153.1 2.5 fusion
  156.3 5.3 %collective-permute-done.10.refs_4_ = bf16[64,4096]{1,0:T(8,128)(2,1)S(1)} collective-permute-done((bf16[64,4096]{1,0:T(8,128)(2,1)S(1)}, bf16[64,4096]{1,0:T(8,128)(2,1)S(1)}, u32[]{:S(2)}, u32[]{:S(2)}) %collective-permute-start.10) | collective-permute-done | bytes 524320 | tf_op jit(solution)/shard_map/ppermute | solution.py:177
  163.5 2.7 collective-permute-start.14
  166.2 3.0 %add_convert_fusion.1 = (bf16[512,512]{1,0:T(8,128)(2,1)S(1)}, bf16[512,512]{1,0:T(8,128)(2,1)S(1)}) fusion(bf16[512,512]{1,0:T(8,128)(2,1)} %copy-done.33, f32[512,512]{1,0:T(8,128)} %collective-permute-done.11, f32[512,2048]{1,0:T(8,128)} %copy-done.31, s32[]{:T(128)S(6)} %select_n.68, f32[512,512]{1,0:T(8,128)} %collective-permute-done.12, s32[]{:T(128)S(6)} %select_n.71), kind=kLoop, calls=%fused_computation.4 | loop fusion | flops 1572864 | bytes 5767176 | tf_op jit(solution)/shard_map/convert_element_type | solution.py:204
  171.9 7.7 %rotate.8.refs_7_ = f32[192,1792]{1,0:T(8,128)S(1)} custom-call(s32[1]{0:T(128)} %bitcast.8.refs_0_.refs_1_, bf16[64,14336]{1,0:T(8,128)(2,1)} %collective-permute-done.8.refs_1_, bf16[64,14336]{1,0:T(8,128)(2,1)S(1)} %collective-permute-done.5.refs_2_, bf16[64,14336]{1,0:T(8,128)(2,1)} %collective-permute-done.7.refs_3_, bf16[64,4096]{1,0:T(8,128)(2,1)S(1)} %copy-done.18, ...), custom_call_target="tpu_custom_call" | custom-call | flops 344064 | bytes 1376256 | tf_op jit(solution)/shard_map/rotate/pallas_call | solution.py:118
  179.7 15.9 %collective-permute-done.17.refs_9_ = bf16[512,512]{1,0:T(8,128)(2,1)S(1)} collective-permute-done((bf16[512,512]{1,0:T(8,128)(2,1)S(1)}, bf16[512,512]{1,0:T(8,128)(2,1)S(1)}, u32[]{:S(2)}, u32[]{:S(2)}) %collective-permute-start.17) | collective-permute-done | bytes 524320 | tf_op jit(solution)/shard_map/ppermute | solution.py:177
  195.6 2.2 add_convert_fusion.refs_12_
  199.2 3.4 %collective-permute-start.18 = (bf16[64,4096]{1,0:T(8,128)(2,1)S(1)}, bf16[64,4096]{1,0:T(8,128)(2,1)S(1)}, u32[]{:S(2)}, u32[]{:S(2)}) collective-permute-start(bf16[64,4096]{1,0:T(8,128)(2,1)S(1)} %slice.14), channel_id=1, source_target_pairs={{0,2},{2,0},{12,14},{14,12},{1,3},{3,1},{13,15},{15,13},{16,18},{1... | collective-permute-start | bytes 1572872 | tf_op jit(solution)/shard_map/ppermute | solution.py:177
  205.9 7.7 %rotate.9.refs_7_ = f32[192,1792]{1,0:T(8,128)S(1)} custom-call(s32[1]{0:T(128)} %bitcast.8.refs_0_.refs_1_, bf16[64,14336]{1,0:T(8,128)(2,1)} %collective-permute-done.8.refs_1_, bf16[64,14336]{1,0:T(8,128)(2,1)S(1)} %collective-permute-done.5.refs_2_, bf16[64,14336]{1,0:T(8,128)(2,1)} %collective-permute-done.7.refs_3_, ...), custom_call_target="tpu_custom_call" | custom-call | flops 344064 | bytes 1376256 | tf_op jit(solution)/shard_map/rotate/pallas_call | solution.py:118
  213.7 2.8 %collective-permute-done.20.refs_11_ = bf16[512,512]{1,0:T(8,128)(2,1)S(1)} collective-permute-done((bf16[512,512]{1,0:T(8,128)(2,1)S(1)}, bf16[512,512]{1,0:T(8,128)(2,1)S(1)}, u32[]{:S(2)}, u32[]{:S(2)}) %collective-permute-start.20) | collective-permute-done | bytes 524320 | tf_op jit(solution)/shard_map/ppermute | solution.py:177
  216.5 5.6 %collective-permute-done.21.refs_13_ = bf16[512,512]{1,0:T(8,128)(2,1)S(1)} collective-permute-done((bf16[512,512]{1,0:T(8,128)(2,1)S(1)}, bf16[512,512]{1,0:T(8,128)(2,1)S(1)}, u32[]{:S(2)}, u32[]{:S(2)}) %collective-permute-start.21) | collective-permute-done | bytes 524320 | tf_op jit(solution)/shard_map/ppermute | solution.py:177
  225.7 3.0 %collective-permute-start.22 = (bf16[64,2048]{1,0:T(8,128)(2,1)S(1)}, bf16[64,2048]{1,0:T(8,128)(2,1)S(1)}, u32[]{:S(2)}, u32[]{:S(2)}) collective-permute-start(bf16[64,2048]{1,0:T(8,128)(2,1)S(1)} %slice.15), channel_id=1, source_target_pairs={{0,2},{2,0},{12,14},{14,12},{1,3},{3,1},{13,15},{15,13},{16,18},{1... | collective-permute-start | bytes 786440 | tf_op jit(solution)/shard_map/ppermute | solution.py:177
  228.7 7.7 %rotate.10.refs_7_ = f32[192,1792]{1,0:T(8,128)S(1)} custom-call(s32[1]{0:T(128)} %bitcast.8.refs_0_.refs_1_, bf16[64,14336]{1,0:T(8,128)(2,1)} %collective-permute-done.8.refs_1_, bf16[64,14336]{1,0:T(8,128)(2,1)S(1)} %collective-permute-done.5.refs_2_, bf16[64,14336]{1,0:T(8,128)(2,1)} %collective-permute-done.7.refs_3_, ...), custom_call_target="tpu_custom_call" | custom-call | flops 344064 | bytes 1376256 | tf_op jit(solution)/shard_map/rotate/pallas_call | solution.py:118
  236.5 2.7 collective-permute-done.23.refs_15_
  239.2 6.4 %rotate.11.refs_7_ = f32[192,1792]{1,0:T(8,128)} custom-call(s32[1]{0:T(128)} %bitcast.8.refs_0_.refs_1_, bf16[64,14336]{1,0:T(8,128)(2,1)} %collective-permute-done.8.refs_1_, bf16[64,14336]{1,0:T(8,128)(2,1)S(1)} %collective-permute-done.5.refs_2_, bf16[64,14336]{1,0:T(8,128)(2,1)} %collective-permute-done.7.refs_3_, ...), custom_call_target="tpu_custom_call" | custom-call | flops 344064 | bytes 1376256 | tf_op jit(solution)/shard_map/rotate/pallas_call | solution.py:118
  246.0 3.1 %collective-permute-done.26.refs_8_ = f32[192,1792]{1,0:T(8,128)S(1)} collective-permute-done((f32[192,1792]{1,0:T(8,128)}, f32[192,1792]{1,0:T(8,128)S(1)}, u32[]{:S(2)}, u32[]{:S(2)}) %collective-permute-start.26) | collective-permute-done | bytes 1376288 | tf_op jit(solution)/shard_map/ppermute | solution.py:139
  261.4 10.7 %fit.1 = f32[1792,2048]{1,0:T(8,128)} custom-call(s32[8]{0:T(128)S(1)} %stack.50.refs_0_, s32[1]{0:T(128)} %bitcast.8.refs_0_.refs_1_, s32[4]{0:T(128)S(1)} %pad_add_fusion.refs_2_, f32[192,1792]{1,0:T(8,128)S(1)} %copy-done.6, f32[192,1792]{1,0:T(8,128)S(1)} %copy-done.14, f32[128,1792]{1,0:T(8,128)S(1)} %copy-done.9, f32[128,1792]{1,0:T(8,128)S(1)} %copy-done.16, ...), custom_call_target="tpu_custom_call" | custom-call | flops 3758096384 | bytes 24117248 | tf_op jit(solution)/shard_map/fit/pallas_call | solution.py:62
  (111 shorter events, 45.9 us)
Async XLA Ops:
  0.0 43.2 %collective-permute-start.1 = (bf16[64,14336]{1,0:T(8,128)(2,1)}, bf16[64,14336]{1,0:T(8,128)(2,1)S(1)}, u32[]{:S(2)}, u32[]{:S(2)}) collective-permute-start(bf16[64,14336]{1,0:T(8,128)(2,1)} %refs_1_.1), channel_id=1, source_target_pairs={{0,4},{2,6},{4,0},{6,2},{8,12},{10,14},{12,8},{14,10},{1,5},{3,7},... | collective-permute-start | bytes 5505032 | tf_op jit(solution)/shard_map/ppermute | solution.py:177
  3.0 41.8 %collective-permute-start = (bf16[64,14336]{1,0:T(8,128)(2,1)}, bf16[64,14336]{1,0:T(8,128)(2,1)}, u32[]{:S(2)}, u32[]{:S(2)}) collective-permute-start(bf16[64,14336]{1,0:T(8,128)(2,1)} %refs_1_.1), channel_id=1, source_target_pairs={{0,2},{2,0},{4,6},{6,4},{8,10},{10,8},{12,14},{14,12},{1,3},{3,1},... | collective-permute-start | bytes 5505032 | tf_op jit(solution)/shard_map/ppermute | solution.py:177
  4.5 40.3 %collective-permute-start.2 = (bf16[64,14336]{1,0:T(8,128)(2,1)}, bf16[64,14336]{1,0:T(8,128)(2,1)}, u32[]{:S(2)}, u32[]{:S(2)}) collective-permute-start(bf16[64,14336]{1,0:T(8,128)(2,1)} %refs_1_.1), channel_id=1, source_target_pairs={{4,8},{6,10},{8,4},{10,6},{5,9},{7,11},{9,5},{11,7},{20,24},{22,26... | collective-permute-start | bytes 5505032 | tf_op jit(solution)/shard_map/ppermute | solution.py:177
  46.2 52.0 %collective-permute-start.6 = (bf16[512,2048]{1,0:T(8,128)(2,1)}, bf16[512,2048]{1,0:T(8,128)(2,1)}, u32[]{:S(2)}, u32[]{:S(2)}) collective-permute-start(bf16[512,2048]{1,0:T(8,128)(2,1)} %get-tuple-element.60), channel_id=1, source_target_pairs={{0,4},{2,6},{12,8},{14,10},{1,5},{3,7},{13,9},{15,11},{16,20},{18,... | collective-permute-start | bytes 6291464 | tf_op jit(solution)/shard_map/ppermute | solution.py:177
  55.5 40.6 %collective-permute-start.3 = (bf16[64,14336]{1,0:T(8,128)(2,1)}, bf16[64,14336]{1,0:T(8,128)(2,1)}, u32[]{:S(2)}, u32[]{:S(2)}) collective-permute-start(bf16[64,14336]{1,0:T(8,128)(2,1)} %broadcast_select_fusion.1), channel_id=1, source_target_pairs={{0,2},{2,0},{4,6},{6,4},{8,10},{10,8},{12,14},{14,12},{1,3},{3,1},... | collective-permute-start | bytes 5505032 | tf_op jit(solution)/shard_map/ppermute | solution.py:177
  56.0 42.2 %collective-permute-start.4 = (bf16[64,14336]{1,0:T(8,128)(2,1)}, bf16[64,14336]{1,0:T(8,128)(2,1)}, u32[]{:S(2)}, u32[]{:S(2)}) collective-permute-start(bf16[64,14336]{1,0:T(8,128)(2,1)} %collective-permute-done.2.refs_2_), channel_id=1, source_target_pairs={{4,0},{6,2},{8,12},{10,14},{5,1},{7,3},{9,13},{11,15},{20,16},{22,... | collective-permute-start | bytes 5505032 | tf_op jit(solution)/shard_map/ppermute | solution.py:177
  57.3 40.9 %collective-permute-start.5 = (bf16[64,14336]{1,0:T(8,128)(2,1)}, bf16[64,14336]{1,0:T(8,128)(2,1)S(1)}, u32[]{:S(2)}, u32[]{:S(2)}) collective-permute-start(bf16[64,14336]{1,0:T(8,128)(2,1)} %copy-done.2), channel_id=1, source_target_pairs={{4,8},{6,10},{8,4},{10,6},{5,9},{7,11},{9,5},{11,7},{20,24},{22,26... | collective-permute-start | bytes 5505032 | tf_op jit(solution)/shard_map/ppermute | solution.py:177
  84.8 25.6 %copy-start.32 = (f32[512,2048]{1,0:T(8,128)S(1)}, f32[512,2048]{1,0:T(8,128)}, u32[]{:S(2)}) copy-start(f32[512,2048]{1,0:T(8,128)} %get-tuple-element.70) | copy-start | bytes 12582916
  101.2 40.1 %collective-permute-start.7 = (bf16[64,14336]{1,0:T(8,128)(2,1)}, bf16[64,14336]{1,0:T(8,128)(2,1)}, u32[]{:S(2)}, u32[]{:S(2)}) collective-permute-start(bf16[64,14336]{1,0:T(8,128)(2,1)} %broadcast_select_fusion), channel_id=1, source_target_pairs={{0,2},{2,0},{4,6},{6,4},{8,10},{10,8},{12,14},{14,12},{1,3},{3,1},... | collective-permute-start | bytes 5505032 | tf_op jit(solution)/shard_map/ppermute | solution.py:177
  102.7 41.6 %collective-permute-start.9 = (bf16[64,14336]{1,0:T(8,128)(2,1)}, bf16[64,14336]{1,0:T(8,128)(2,1)}, u32[]{:S(2)}, u32[]{:S(2)}) collective-permute-start(bf16[64,14336]{1,0:T(8,128)(2,1)} %collective-permute-done.refs_3_), channel_id=1, source_target_pairs={{0,4},{2,6},{12,8},{14,10},{1,5},{3,7},{13,9},{15,11},{16,20},{18,... | collective-permute-start | bytes 5505032 | tf_op jit(solution)/shard_map/ppermute | solution.py:177
  109.2 40.2 %collective-permute-start.8 = (bf16[64,14336]{1,0:T(8,128)(2,1)S(1)}, bf16[64,14336]{1,0:T(8,128)(2,1)}, u32[]{:S(2)}, u32[]{:S(2)}) collective-permute-start(bf16[64,14336]{1,0:T(8,128)(2,1)S(1)} %collective-permute-done.5.refs_2_), channel_id=1, source_target_pairs={{4,0},{6,2},{8,12},{10,14},{5,1},{7,3},{9,13},{11,15},{20,16},{22,... | collective-permute-start | bytes 5505032 | tf_op jit(solution)/shard_map/ppermute | solution.py:177
  115.6 37.4 %collective-permute-start.12 = (f32[512,512]{1,0:T(8,128)}, f32[512,512]{1,0:T(8,128)}, u32[]{:S(2)}, u32[]{:S(2)}) collective-permute-start(f32[512,512]{1,0:T(8,128)} %get-tuple-element.103), channel_id=1, source_target_pairs={{4,8},{6,10},{8,4},{10,6},{5,9},{7,11},{9,5},{11,7},{20,24},{22,26... | collective-permute-start | bytes 3145736 | tf_op jit(solution)/shard_map/ppermute | solution.py:177
  117.3 35.7 %collective-permute-start.11 = (f32[512,512]{1,0:T(8,128)}, f32[512,512]{1,0:T(8,128)}, u32[]{:S(2)}, u32[]{:S(2)}) collective-permute-start(f32[512,512]{1,0:T(8,128)} %get-tuple-element.104), channel_id=1, source_target_pairs={{4,8},{6,10},{8,4},{10,6},{5,9},{7,11},{9,5},{11,7},{20,24},{22,26... | collective-permute-start | bytes 3145736 | tf_op jit(solution)/shard_map/ppermute | solution.py:177
  150.5 11.1 %collective-permute-start.10 = (bf16[64,4096]{1,0:T(8,128)(2,1)S(1)}, bf16[64,4096]{1,0:T(8,128)(2,1)S(1)}, u32[]{:S(2)}, u32[]{:S(2)}) collective-permute-start(bf16[64,4096]{1,0:T(8,128)(2,1)S(1)} %slice.12), channel_id=1, source_target_pairs={{0,2},{2,0},{12,14},{14,12},{1,3},{3,1},{13,15},{15,13},{16,18},{1... | collective-permute-start | bytes 1572872 | tf_op jit(solution)/shard_map/ppermute | solution.py:177
  155.6 6.0 %collective-permute-start.13 = (bf16[512,512]{1,0:T(8,128)(2,1)}, bf16[512,512]{1,0:T(8,128)(2,1)S(1)}, u32[]{:S(2)}, u32[]{:S(2)}) collective-permute-start(bf16[512,512]{1,0:T(8,128)(2,1)} %fusion), channel_id=1, source_target_pairs={{4,6},{6,4},{8,10},{10,8},{5,7},{7,5},{9,11},{11,9},{20,22},{22,20... | collective-permute-start | bytes 1572872 | tf_op jit(solution)/shard_map/ppermute | solution.py:177
  163.5 16.1 %collective-permute-start.14 = (bf16[64,4096]{1,0:T(8,128)(2,1)S(1)}, bf16[64,4096]{1,0:T(8,128)(2,1)S(1)}, u32[]{:S(2)}, u32[]{:S(2)}) collective-permute-start(bf16[64,4096]{1,0:T(8,128)(2,1)S(1)} %slice.13), channel_id=1, source_target_pairs={{0,2},{2,0},{12,14},{14,12},{1,3},{3,1},{13,15},{15,13},{16,18},{1... | collective-permute-start | bytes 1572872 | tf_op jit(solution)/shard_map/ppermute | solution.py:177
  169.2 10.5 %collective-permute-start.15 = (bf16[512,512]{1,0:T(8,128)(2,1)S(1)}, bf16[512,512]{1,0:T(8,128)(2,1)S(1)}, u32[]{:S(2)}, u32[]{:S(2)}) collective-permute-start(bf16[512,512]{1,0:T(8,128)(2,1)S(1)} %get-tuple-element.102), channel_id=1, source_target_pairs={{4,6},{6,4},{8,10},{10,8},{5,7},{7,5},{9,11},{11,9},{20,22},{22,20... | collective-permute-start | bytes 1572872 | tf_op jit(solution)/shard_map/ppermute | solution.py:177
  169.9 25.7 %collective-permute-start.17 = (bf16[512,512]{1,0:T(8,128)(2,1)S(1)}, bf16[512,512]{1,0:T(8,128)(2,1)S(1)}, u32[]{:S(2)}, u32[]{:S(2)}) collective-permute-start(bf16[512,512]{1,0:T(8,128)(2,1)S(1)} %get-tuple-element.101.refs_10_), channel_id=1, source_target_pairs={{4,0},{6,2},{8,12},{10,14},{5,1},{7,3},{9,13},{11,15},{20,16},{22,... | collective-permute-start | bytes 1572872 | tf_op jit(solution)/shard_map/ppermute | solution.py:177
  171.2 24.4 %collective-permute-start.16 = (bf16[512,512]{1,0:T(8,128)(2,1)S(1)}, bf16[512,512]{1,0:T(8,128)(2,1)S(1)}, u32[]{:S(2)}, u32[]{:S(2)}) collective-permute-start(bf16[512,512]{1,0:T(8,128)(2,1)S(1)} %get-tuple-element.101.refs_10_), channel_id=1, source_target_pairs={{4,8},{6,10},{8,4},{10,6},{5,9},{7,11},{9,5},{11,7},{20,24},{22,26... | collective-permute-start | bytes 1572872 | tf_op jit(solution)/shard_map/ppermute | solution.py:177
  199.2 23.7 %copy-start.5 = (f32[192,1792]{1,0:T(8,128)S(1)}, f32[192,1792]{1,0:T(8,128)}, u32[]{:S(2)}) copy-start(f32[192,1792]{1,0:T(8,128)} %copy-done.4) | copy-start | bytes 4128772
  199.2 23.7 %copy-start.8 = (f32[128,1792]{1,0:T(8,128)S(1)}, f32[128,1792]{1,0:T(8,128)}, u32[]{:S(2)}) copy-start(f32[128,1792]{1,0:T(8,128)} %copy-done.7) | copy-start | bytes 2752516
  199.2 14.5 %collective-permute-start.18 = (bf16[64,4096]{1,0:T(8,128)(2,1)S(1)}, bf16[64,4096]{1,0:T(8,128)(2,1)S(1)}, u32[]{:S(2)}, u32[]{:S(2)}) collective-permute-start(bf16[64,4096]{1,0:T(8,128)(2,1)S(1)} %slice.14), channel_id=1, source_target_pairs={{0,2},{2,0},{12,14},{14,12},{1,3},{3,1},{13,15},{15,13},{16,18},{1... | collective-permute-start | bytes 1572872 | tf_op jit(solution)/shard_map/ppermute | solution.py:177
  202.6 13.9 %collective-permute-start.20 = (bf16[512,512]{1,0:T(8,128)(2,1)S(1)}, bf16[512,512]{1,0:T(8,128)(2,1)S(1)}, u32[]{:S(2)}, u32[]{:S(2)}) collective-permute-start(bf16[512,512]{1,0:T(8,128)(2,1)S(1)} %add_convert_fusion.refs_12_), channel_id=1, source_target_pairs={{4,0},{6,2},{8,12},{10,14},{5,1},{7,3},{9,13},{11,15},{20,16},{22,... | collective-permute-start | bytes 1572872 | tf_op jit(solution)/shard_map/ppermute | solution.py:177
  203.9 12.6 %collective-permute-start.19 = (bf16[512,512]{1,0:T(8,128)(2,1)S(1)}, bf16[512,512]{1,0:T(8,128)(2,1)S(1)}, u32[]{:S(2)}, u32[]{:S(2)}) collective-permute-start(bf16[512,512]{1,0:T(8,128)(2,1)S(1)} %add_convert_fusion.refs_12_), channel_id=1, source_target_pairs={{4,8},{6,10},{8,4},{10,6},{5,9},{7,11},{9,5},{11,7},{20,24},{22,26... | collective-permute-start | bytes 1572872 | tf_op jit(solution)/shard_map/ppermute | solution.py:177
  204.6 17.5 %collective-permute-start.21 = (bf16[512,512]{1,0:T(8,128)(2,1)S(1)}, bf16[512,512]{1,0:T(8,128)(2,1)S(1)}, u32[]{:S(2)}, u32[]{:S(2)}) collective-permute-start(bf16[512,512]{1,0:T(8,128)(2,1)S(1)} %collective-permute-done.16.refs_14_), channel_id=1, source_target_pairs={{4,0},{6,2},{8,12},{10,14},{5,1},{7,3},{9,13},{11,15},{20,16},{22,... | collective-permute-start | bytes 1572872 | tf_op jit(solution)/shard_map/ppermute | solution.py:177
  216.5 20.0 %copy-start.23 = (bf16[512,512]{1,0:T(8,128)(2,1)}, bf16[512,512]{1,0:T(8,128)(2,1)S(1)}, u32[]{:S(2)}) copy-start(bf16[512,512]{1,0:T(8,128)(2,1)S(1)} %collective-permute-done.20.refs_11_) | copy-start | bytes 1572868
  216.5 20.0 %copy-start.25 = (bf16[512,512]{1,0:T(8,128)(2,1)}, bf16[512,512]{1,0:T(8,128)(2,1)S(1)}, u32[]{:S(2)}) copy-start(bf16[512,512]{1,0:T(8,128)(2,1)S(1)} %collective-permute-done.19.refs_16_) | copy-start | bytes 1572868
  222.9 16.3 %collective-permute-start.24 = (f32[192,1792]{1,0:T(8,128)S(1)}, f32[192,1792]{1,0:T(8,128)S(1)}, u32[]{:S(2)}, u32[]{:S(2)}) collective-permute-start(f32[192,1792]{1,0:T(8,128)S(1)} %copy-done.5), channel_id=1, source_target_pairs={{0,1},{1,0},{2,3},{3,2},{4,5},{5,4},{6,7},{7,6},{8,9},{9,8},{10,11... | collective-permute-start | bytes 4128776 | tf_op jit(solution)/shard_map/ppermute | solution.py:139
  222.9 16.3 %collective-permute-start.25 = (f32[128,1792]{1,0:T(8,128)S(1)}, f32[128,1792]{1,0:T(8,128)S(1)}, u32[]{:S(2)}, u32[]{:S(2)}) collective-permute-start(f32[128,1792]{1,0:T(8,128)S(1)} %copy-done.8), channel_id=1, source_target_pairs={{0,1},{1,0},{2,3},{3,2},{4,5},{5,4},{6,7},{7,6},{8,9},{9,8},{10,11... | collective-permute-start | bytes 2752520 | tf_op jit(solution)/shard_map/ppermute | solution.py:139
  223.4 15.8 %collective-permute-start.23 = (bf16[512,512]{1,0:T(8,128)(2,1)S(1)}, bf16[512,512]{1,0:T(8,128)(2,1)S(1)}, u32[]{:S(2)}, u32[]{:S(2)}) collective-permute-start(bf16[512,512]{1,0:T(8,128)(2,1)S(1)} %collective-permute-done.19.refs_16_), channel_id=1, source_target_pairs={{4,0},{6,2},{8,12},{10,14},{5,1},{7,3},{9,13},{11,15},{20,16},{22,... | collective-permute-start | bytes 1572872 | tf_op jit(solution)/shard_map/ppermute | solution.py:177
  225.7 10.8 %collective-permute-start.22 = (bf16[64,2048]{1,0:T(8,128)(2,1)S(1)}, bf16[64,2048]{1,0:T(8,128)(2,1)S(1)}, u32[]{:S(2)}, u32[]{:S(2)}) collective-permute-start(bf16[64,2048]{1,0:T(8,128)(2,1)S(1)} %slice.15), channel_id=1, source_target_pairs={{0,2},{2,0},{12,14},{14,12},{1,3},{3,1},{13,15},{15,13},{16,18},{1... | collective-permute-start | bytes 786440 | tf_op jit(solution)/shard_map/ppermute | solution.py:177
  245.7 3.4 %collective-permute-start.26 = (f32[192,1792]{1,0:T(8,128)}, f32[192,1792]{1,0:T(8,128)S(1)}, u32[]{:S(2)}, u32[]{:S(2)}) collective-permute-start(f32[192,1792]{1,0:T(8,128)} %rotate.11.refs_7_), channel_id=1, source_target_pairs={{0,1},{1,0},{2,3},{3,2},{4,5},{5,4},{6,7},{7,6},{8,9},{9,8},{10,11... | collective-permute-start | bytes 4128776 | tf_op jit(solution)/shard_map/ppermute | solution.py:139
  (29 other events, 124.4 us)

commit v7 on v6

--- a/solution.py
+++ b/solution.py
@@ -74,7 +74,7 @@
                 pltpu.VMEM((rows, tile), F32),
             ],
         ),
-        compiler_params=pltpu.CompilerParams(vmem_limit_bytes=VMEM),
+        compiler_params=pltpu.CompilerParams(vmem_limit_bytes=56 << 20),
         cost_estimate=pl.CostEstimate(
             flops=2 * rows * ka * ks, bytes_accessed=8 * rows * ka + 2 * rows * ks + 4 * ka * ks, transcendentals=0
         ),
@@ -194,8 +194,8 @@
     def pick(a, b):
         return jnp.where(at_end, got[a], got[b])
 
-    def columns(a, h, p):
-        return lax.dynamic_slice_in_dim(a, (2 * h + p) * part, part, 1)
+    def columns(a, h):
+        return lax.dynamic_slice_in_dim(a, h * 2 * part, 2 * part, 1)
 
     def turn(before, blocks, first, count):
         return rotate(before, end, [[(got[n], first) for n in block] for block in blocks], basis_in, first, count)
@@ -208,28 +208,31 @@
     got["x1"] = send(got["own"], ACROSS)
     got["a1"] = send(got["own"], ENDS)
     got["m1"] = send(got["own"], MIDDLE)
-    got["out"] = dot(deltas, basis_out)
-    got["out16"] = got["out"].astype(BF16)
-    fence("x1", "a1", "m1", "out", "out16")
+    got["give"] = dot(deltas, columns(basis_out, 1 - half))
+    got["r1", 0] = send(got["give"].astype(BF16), FROM_ENDS)
+    got["keep"] = dot(deltas, columns(basis_out, half))
+    got["r1", 1] = send(got["keep"].astype(BF16), FROM_ENDS)
+    fence("x1", "a1", "m1", "give", "keep")
     got["pick"] = pick("a1", "m1")
-    fence("pick", "a1", "m1", "out16")
+    fence("pick", "a1", "m1", "x1")
     got["x2"] = send(got["pick"], ACROSS)
     got["a2"] = send(got["m1"], TO_ENDS)
     got["m2"] = send(got["a1"], MIDDLE)
-    got["r1"] = send(got["out16"], FROM_ENDS)
-    got["A"] = turn(None, [["own"], ["a1"], ["x1"]], 0, steps)
-    fence("x1", "x2", "a2", "m2", "r1", "A")
+    some = steps // 2
+    got["A"] = turn(None, [["own"], ["a1"], ["x1"]], 0, some)
+    fence(("r1", 0), "give", "A")
+    got["give"] += got["r1", 0].astype(F32)
+    got["A"] = turn(got["A"], [["own"], ["a1"], ["x1"]], some, steps - some)
+    fence("x1", "x2", "a2", "m2", "give", "keep", ("r1", 1), "A")
+    got["m3"] = send(got["give"], MIDDLE)
     got["pick"] = pick("a2", "m2")
-    fence("pick", "m2", "x1", "out")
+    fence("pick", "m2", "x1", "keep")
     got["x3"] = send(got["pick"], ACROSS)
     got["a3"] = send(got["m2"], TO_ENDS)
-    here = got["out"] + got["r1"].astype(F32)
-    for p in range(2):
-        got["keep", p] = columns(here, half, p)
-        got["m3", p] = send(columns(here, 1 - half, p), MIDDLE)
     got["e"] = send(got["x1"], FROM_ENDS)
     got["B"] = turn(None, [["a2", "m1"], ["x2"]], 0, steps)
     fence("x3", "a3", "e", "B")
+    got["keep"] += got["r1", 1].astype(F32)
 
     def x4(piece):
         got["x4", piece] = send(got["a3"][:, cuts[piece] * DEEP : cuts[piece + 1] * DEEP], ACROSS_ENDS)
@@ -240,11 +243,12 @@
         got["D"] = rotate(got.get("D"), end, blocks, basis_in, first, cuts[piece + 1] - first)
 
     def cross(p):
-        got["keep", p] += got["m3", p]
+        here = slice(p * part, (p + 1) * part)
+        got["keep", p] = got["keep"][:, here] + got["m3"][:, here]
         got["x5", p] = send(got["keep", p].astype(BF16), ACROSS_MIDDLE)
 
     x4(0)
-    fence(("m3", 0), ("m3", 1), "a3")
+    fence("m3", "a3")
     cross(0)
     cross(1)
     fence(("x4", 0), ("x5", 0), "a3")
@@ -256,13 +260,13 @@
     got["n2", 0] = send(got["m4", 0], TO_ENDS)
     settle(1)
     last(1)
-    fence(("x4", 2), ("m4", 1), ("n1", 1), ("n2", 0), "A", "B", "D", "a3")
+    fence(("x4", 2), ("m4", 1), ("n2", 0), "A", "B", "D", "a3")
     x4(3)
     got["n2", 1] = send(got["m4", 1], TO_ENDS)
     got["A2"] = swap_narrow(got["A"])
     got["B2"] = swap_narrow(got["B"])
     last(2)
-    fence(("x4", 3), ("n2", 1), "A2", "B2", "D")
+    fence(("x4", 3), ("n1", 1), ("n2", 1), "A2", "B2", "D")
     last(3)
     got["D2"] = swap_narrow(got["D"])
 

time: 274 us -> 251 us (0.916)
  local copies, waits for them, and re-layouts: 24.1 us -> 5.87 us
  other arithmetic: 14.6 us -> 9.01 us
  waiting for transfers between devices: 88.2 us -> 83.3 us
  Pallas kernels: 86.4 us -> 90.9 us
    unnamed x68 -> x40, local copies, waits for them, and re-layouts: 18 us -> 5.11 us
    pallas_call x1, Pallas kernels: 10.7 us -> 15.5 us  [fit(): pl.pallas_call(lambda *refs: fit_kernel([pair[0].shape[0] for pair in sum...]
    convert_element_type x2, other arithmetic: 5.19 us -> 0.89 us  [settle(): got['sum', p] = (got['keep', p] + got['x5', p].astype(F32)).astype(BF16)]
    slice x4, local copies, waits for them, and re-layouts: 4.39 us -> 0.13 us  [x4(): got['a3'][:, cuts[piece] * DEEP:cuts[piece + 1] * DEEP]]
    ppermute x24, waiting for transfers between devices: 85 us -> 81.3 us  [send(): return lax.ppermute(a, 'wide', perm)]
    dot_general x1 -> x2, matrix products: 7.28 us -> 7.55 us  [dot(): return jnp.dot(a, b, preferred_element_type=F32)]
    pallas_call x6 -> x7, Pallas kernels: 75.7 us -> 75.4 us  [rotate(): pl.pallas_call(lambda *refs: rotate_kernel([len(block) for block in block...]
  transfers between devices with their start and end apart: 27 -> 27, of which waited for: 12 -> 13; matrix products, arithmetic and copies ran while one was open for 7% -> 6% of each run, Pallas kernels for 25% -> 28%
where the time goes in v7:
time: 251 us; the launch traced here: 250 us
  Pallas kernels  90.9 us (36%)
  waiting for transfers between devices  83.3 us (33%)
  starting transfers between devices  52.6 us (21%)
  other arithmetic  9.01 us (4%)
  matrix products  7.55 us (3%)
  local copies, waits for them, and re-layouts  5.87 us (2%)
    ppermute x24, waiting for transfers between devices, send(): return lax.ppermute(a, 'wide', perm)  81.3 us
    pallas_call x7, Pallas kernels, rotate(): pl.pallas_call(lambda *refs: rotate_kernel([len(block) for block in block...  75.4 us
    ppermute x24, starting transfers between devices, send(): return lax.ppermute(a, 'wide', perm)  52.1 us
    pallas_call x1, Pallas kernels, fit(): pl.pallas_call(lambda *refs: fit_kernel([pair[0].shape[0] for pair in sum...  15.5 us
    dot_general x2, matrix products, dot(): return jnp.dot(a, b, preferred_element_type=F32)  7.55 us
    unnamed x40, local copies, waits for them, and re-layouts  5.11 us
  transfers between devices with their start and end apart: 27, of which 13 were waited for; matrix products, arithmetic and copies ran while one was open for 6% of the time, Pallas kernels for 28%

profile of v7, /device:TPU:0, one launch (start us, length us, event | category | flops | bytes accessed | tf_op | source)
XLA Modules:
  0.0 249.9 jit_solution(13977866410372133623)
XLA Ops:
  0.0 2.1 collective-permute-start.2
  2.1 4.6 %collective-permute-start.1 = (bf16[64,14336]{1,0:T(8,128)(2,1)}, bf16[64,14336]{1,0:T(8,128)(2,1)S(1)}, u32[]{:S(2)}, u32[]{:S(2)}) collective-permute-start(bf16[64,14336]{1,0:T(8,128)(2,1)} %refs_1_.3), channel_id=1, source_target_pairs={{0,4},{2,6},{4,0},{6,2},{8,12},{10,14},{12,8},{14,10},{1,5},{3,7},... | collective-permute-start | bytes 5505032 | tf_op jit(solution)/shard_map/ppermute | solution.py:177
  8.2 4.6 %fusion.14 = (bf16[512,1024]{1,0:T(8,128)(2,1)}, f32[512,1024]{1,0:T(8,128)}) fusion(bf16[512,1024]{1,0:T(8,128)(2,1)S(1)} %copy-done, bf16[1024,2048]{1,0:T(8,128)(2,1)} %param.7, s32[]{:T(128)S(6)} %select_n.60), kind=kOutput, calls=%fused_computation.19 | convolution fusion | flops 1074266112 | bytes 6291460 | tf_op jit(solution)/shard_map/dot_general | solution.py:16
  12.8 2.9 %fusion.15 = (bf16[512,1024]{1,0:T(8,128)(2,1)}, f32[512,1024]{1,0:T(8,128)}) fusion(bf16[512,1024]{1,0:T(8,128)(2,1)S(1)} %copy-done, bf16[1024,2048]{1,0:T(8,128)(2,1)S(1)} %copy-done.19, s32[]{:T(128)S(6)} %select_n.61), kind=kOutput, calls=%fused_computation.20 | convolution fusion | flops 1074266112 | bytes 6291460 | tf_op jit(solution)/shard_map/dot_general | solution.py:16
  15.8 30.9 %collective-permute-done.1.refs_2_ = bf16[64,14336]{1,0:T(8,128)(2,1)S(1)} collective-permute-done((bf16[64,14336]{1,0:T(8,128)(2,1)}, bf16[64,14336]{1,0:T(8,128)(2,1)S(1)}, u32[]{:S(2)}, u32[]{:S(2)}) %collective-permute-start.1) | collective-permute-done | bytes 1835040 | tf_op jit(solution)/shard_map/ppermute | solution.py:177
  53.3 8.6 %collective-permute-start.6 = (bf16[512,1024]{1,0:T(8,128)(2,1)}, bf16[512,1024]{1,0:T(8,128)(2,1)}, u32[]{:S(2)}, u32[]{:S(2)}) collective-permute-start(bf16[512,1024]{1,0:T(8,128)(2,1)} %get-tuple-element.111), channel_id=1, source_target_pairs={{0,4},{2,6},{12,8},{14,10},{1,5},{3,7},{13,9},{15,11},{16,20},{18,... | collective-permute-start | bytes 3145736 | tf_op jit(solution)/shard_map/ppermute | solution.py:177
  61.9 2.3 collective-permute-start.7
  67.2 12.5 %rotate.7.refs_5_ = f32[192,1792]{1,0:T(8,128)S(1)} custom-call(s32[1]{0:T(128)} %bitcast.8.refs_0_.refs_1_, bf16[64,14336]{1,0:T(8,128)(2,1)S(1)} %copy-done.4, bf16[64,14336]{1,0:T(8,128)(2,1)S(1)} %copy-done.3, bf16[64,14336]{1,0:T(8,128)(2,1)} %collective-permute-done.refs_3_, bf16[14336,1792]{1,0:T(8,128)(2,1)} %refs_6_.7), custom_call_target="tpu_custom_call" | custom-call | flops 344064 | bytes 1376256 | tf_op jit(solution)/shard_map/rotate/pallas_call | solution.py:118
  79.7 5.1 %collective-permute-done.6 = bf16[512,1024]{1,0:T(8,128)(2,1)} collective-permute-done((bf16[512,1024]{1,0:T(8,128)(2,1)}, bf16[512,1024]{1,0:T(8,128)(2,1)}, u32[]{:S(2)}, u32[]{:S(2)}) %collective-permute-start.6) | collective-permute-done | bytes 1048608 | tf_op jit(solution)/shard_map/ppermute | solution.py:177
  84.9 12.5 %rotate.8.refs_3_ = f32[192,1792]{1,0:T(8,128)S(1)} custom-call(s32[1]{0:T(128)} %bitcast.8.refs_0_.refs_1_, bf16[64,14336]{1,0:T(8,128)(2,1)S(1)} %copy-done.4, bf16[64,14336]{1,0:T(8,128)(2,1)S(1)} %copy-done.3, bf16[64,14336]{1,0:T(8,128)(2,1)} %collective-permute-done.refs_3_, bf16[14336,1792]{1,0:T(8,128)(2,1)} %refs_6_.7, f32[192,1792]{1,0:T(8,128)S(1)} %rotate.7.refs_5_), custom_call_target="tpu_custom_call" | custom-call | flops 344064 | bytes 1376256 | tf_op jit(solution)/shard_map/rotate/pallas_call | solution.py:118
  97.4 2.1 convert_add_fusion.1
  99.5 4.9 %collective-permute-done.7 = bf16[512,1024]{1,0:T(8,128)(2,1)} collective-permute-done((bf16[512,1024]{1,0:T(8,128)(2,1)}, bf16[512,1024]{1,0:T(8,128)(2,1)}, u32[]{:S(2)}, u32[]{:S(2)}) %collective-permute-start.7) | collective-permute-done | bytes 1048608 | tf_op jit(solution)/shard_map/ppermute | solution.py:177
  107.5 5.4 %collective-permute-start.10 = (bf16[64,14336]{1,0:T(8,128)(2,1)}, bf16[64,14336]{1,0:T(8,128)(2,1)S(1)}, u32[]{:S(2)}, u32[]{:S(2)}) collective-permute-start(bf16[64,14336]{1,0:T(8,128)(2,1)} %collective-permute-done.refs_3_), channel_id=1, source_target_pairs={{0,4},{2,6},{12,8},{14,10},{1,5},{3,7},{13,9},{15,11},{16,20},{18,... | collective-permute-start | bytes 5505032 | tf_op jit(solution)/shard_map/ppermute | solution.py:177
  114.2 22.4 %rotate.9.refs_5_ = f32[128,1792]{1,0:T(8,128)S(1)} custom-call(s32[1]{0:T(128)} %bitcast.8.refs_0_.refs_1_, bf16[64,14336]{1,0:T(8,128)(2,1)} %collective-permute-done.4.refs_1_, bf16[64,14336]{1,0:T(8,128)(2,1)} %collective-permute-done.2.refs_2_, bf16[64,14336]{1,0:T(8,128)(2,1)} %collective-permute-done.3.refs_3_, bf16[14336,1792]{1,0:T(8,128)(2,1)} %refs_6_.7), custom_call_target="tpu_custom_call" | custom-call | flops 229376 | bytes 917504 | tf_op jit(solution)/shard_map/rotate/pallas_call | solution.py:118
  136.6 2.0 convert_add_fusion
  138.6 7.4 %collective-permute-done.8.refs_3_ = bf16[64,14336]{1,0:T(8,128)(2,1)S(1)} collective-permute-done((bf16[64,14336]{1,0:T(8,128)(2,1)S(1)}, bf16[64,14336]{1,0:T(8,128)(2,1)S(1)}, u32[]{:S(2)}, u32[]{:S(2)}) %collective-permute-start.8) | collective-permute-done | bytes 1835040 | tf_op jit(solution)/shard_map/ppermute | solution.py:177
  146.1 2.9 %collective-permute-done.10.refs_5_ = bf16[64,14336]{1,0:T(8,128)(2,1)S(1)} collective-permute-done((bf16[64,14336]{1,0:T(8,128)(2,1)}, bf16[64,14336]{1,0:T(8,128)(2,1)S(1)}, u32[]{:S(2)}, u32[]{:S(2)}) %collective-permute-start.10) | collective-permute-done | bytes 1835040 | tf_op jit(solution)/shard_map/ppermute | solution.py:177
  149.0 3.9 %collective-permute-done.9.refs_1_ = bf16[64,14336]{1,0:T(8,128)(2,1)S(1)} collective-permute-done((bf16[64,14336]{1,0:T(8,128)(2,1)S(1)}, bf16[64,14336]{1,0:T(8,128)(2,1)S(1)}, u32[]{:S(2)}, u32[]{:S(2)}) %collective-permute-start.9) | collective-permute-done | bytes 1835040 | tf_op jit(solution)/shard_map/ppermute | solution.py:177
  152.9 3.3 %collective-permute-start.11 = (bf16[64,4096]{1,0:T(8,128)(2,1)S(1)}, bf16[64,4096]{1,0:T(8,128)(2,1)S(1)}, u32[]{:S(2)}, u32[]{:S(2)}) collective-permute-start(bf16[64,4096]{1,0:T(8,128)(2,1)S(1)} %slice.24), channel_id=1, source_target_pairs={{0,2},{2,0},{12,14},{14,12},{1,3},{3,1},{13,15},{15,13},{16,18},{1... | collective-permute-start | bytes 1572872 | tf_op jit(solution)/shard_map/ppermute | solution.py:177
  157.2 6.8 %collective-permute-done.11.refs_4_ = bf16[64,4096]{1,0:T(8,128)(2,1)S(1)} collective-permute-done((bf16[64,4096]{1,0:T(8,128)(2,1)S(1)}, bf16[64,4096]{1,0:T(8,128)(2,1)S(1)}, u32[]{:S(2)}, u32[]{:S(2)}) %collective-permute-start.11) | collective-permute-done | bytes 524320 | tf_op jit(solution)/shard_map/ppermute | solution.py:177
  167.3 3.3 %collective-permute-start.14 = (bf16[64,4096]{1,0:T(8,128)(2,1)S(1)}, bf16[64,4096]{1,0:T(8,128)(2,1)S(1)}, u32[]{:S(2)}, u32[]{:S(2)}) collective-permute-start(bf16[64,4096]{1,0:T(8,128)(2,1)S(1)} %slice.27), channel_id=1, source_target_pairs={{0,2},{2,0},{12,14},{14,12},{1,3},{3,1},{13,15},{15,13},{16,18},{1... | collective-permute-start | bytes 1572872 | tf_op jit(solution)/shard_map/ppermute | solution.py:177
  170.6 7.6 %rotate.10.refs_7_ = f32[192,1792]{1,0:T(8,128)S(1)} custom-call(s32[1]{0:T(128)} %bitcast.8.refs_0_.refs_1_, bf16[64,14336]{1,0:T(8,128)(2,1)S(1)} %collective-permute-done.9.refs_1_, bf16[64,14336]{1,0:T(8,128)(2,1)S(1)} %collective-permute-done.5.refs_2_, bf16[64,14336]{1,0:T(8,128)(2,1)S(1)} %collective-permute-done.8.refs_3_, ...), custom_call_target="tpu_custom_call" | custom-call | flops 344064 | bytes 1376256 | tf_op jit(solution)/shard_map/rotate/pallas_call | solution.py:118
  179.8 4.0 %collective-permute-start.18 = (bf16[64,4096]{1,0:T(8,128)(2,1)S(1)}, bf16[64,4096]{1,0:T(8,128)(2,1)S(1)}, u32[]{:S(2)}, u32[]{:S(2)}) collective-permute-start(bf16[64,4096]{1,0:T(8,128)(2,1)S(1)} %slice.30), channel_id=1, source_target_pairs={{0,2},{2,0},{12,14},{14,12},{1,3},{3,1},{13,15},{15,13},{16,18},{1... | collective-permute-start | bytes 1572872 | tf_op jit(solution)/shard_map/ppermute | solution.py:177
  185.8 7.6 %rotate.11.refs_7_ = f32[192,1792]{1,0:T(8,128)S(1)} custom-call(s32[1]{0:T(128)} %bitcast.8.refs_0_.refs_1_, bf16[64,14336]{1,0:T(8,128)(2,1)S(1)} %collective-permute-done.9.refs_1_, bf16[64,14336]{1,0:T(8,128)(2,1)S(1)} %collective-permute-done.5.refs_2_, bf16[64,14336]{1,0:T(8,128)(2,1)S(1)} %collective-permute-done.8.refs_3_, ...), custom_call_target="tpu_custom_call" | custom-call | flops 344064 | bytes 1376256 | tf_op jit(solution)/shard_map/rotate/pallas_call | solution.py:118
  193.4 2.7 %collective-permute-done.20.refs_13_ = bf16[512,512]{1,0:T(8,128)(2,1)S(1)} collective-permute-done((bf16[512,512]{1,0:T(8,128)(2,1)S(1)}, bf16[512,512]{1,0:T(8,128)(2,1)S(1)}, u32[]{:S(2)}, u32[]{:S(2)}) %collective-permute-start.20) | collective-permute-done | bytes 524320 | tf_op jit(solution)/shard_map/ppermute | solution.py:177
  199.4 2.7 %collective-permute-start.21 = (bf16[64,2048]{1,0:T(8,128)(2,1)S(1)}, bf16[64,2048]{1,0:T(8,128)(2,1)S(1)}, u32[]{:S(2)}, u32[]{:S(2)}) collective-permute-start(bf16[64,2048]{1,0:T(8,128)(2,1)S(1)} %slice.31), channel_id=1, source_target_pairs={{0,2},{2,0},{12,14},{14,12},{1,3},{3,1},{13,15},{15,13},{16,18},{1... | collective-permute-start | bytes 786440 | tf_op jit(solution)/shard_map/ppermute | solution.py:177
  202.1 7.6 %rotate.12.refs_7_ = f32[192,1792]{1,0:T(8,128)S(1)} custom-call(s32[1]{0:T(128)} %bitcast.8.refs_0_.refs_1_, bf16[64,14336]{1,0:T(8,128)(2,1)S(1)} %collective-permute-done.9.refs_1_, bf16[64,14336]{1,0:T(8,128)(2,1)S(1)} %collective-permute-done.5.refs_2_, bf16[64,14336]{1,0:T(8,128)(2,1)S(1)} %collective-permute-done.8.refs_3_, ...), custom_call_target="tpu_custom_call" | custom-call | flops 344064 | bytes 1376256 | tf_op jit(solution)/shard_map/rotate/pallas_call | solution.py:118
  209.7 3.5 %collective-permute-done.22.refs_11_ = bf16[512,512]{1,0:T(8,128)(2,1)S(1)} collective-permute-done((bf16[512,512]{1,0:T(8,128)(2,1)S(1)}, bf16[512,512]{1,0:T(8,128)(2,1)S(1)}, u32[]{:S(2)}, u32[]{:S(2)}) %collective-permute-start.22) | collective-permute-done | bytes 524320 | tf_op jit(solution)/shard_map/ppermute | solution.py:177
  213.2 10.4 %collective-permute-done.23.refs_15_ = bf16[512,512]{1,0:T(8,128)(2,1)S(1)} collective-permute-done((bf16[512,512]{1,0:T(8,128)(2,1)S(1)}, bf16[512,512]{1,0:T(8,128)(2,1)S(1)}, u32[]{:S(2)}, u32[]{:S(2)}) %collective-permute-start.23) | collective-permute-done | bytes 524320 | tf_op jit(solution)/shard_map/ppermute | solution.py:177
  224.6 5.3 %rotate.13.refs_7_ = f32[192,1792]{1,0:T(8,128)} custom-call(s32[1]{0:T(128)} %bitcast.8.refs_0_.refs_1_, bf16[64,14336]{1,0:T(8,128)(2,1)S(1)} %collective-permute-done.9.refs_1_, bf16[64,14336]{1,0:T(8,128)(2,1)S(1)} %collective-permute-done.5.refs_2_, bf16[64,14336]{1,0:T(8,128)(2,1)S(1)} %collective-permute-done.8.refs_3_, ...), custom_call_target="tpu_custom_call" | custom-call | flops 344064 | bytes 1376256 | tf_op jit(solution)/shard_map/rotate/pallas_call | solution.py:118
  231.1 2.1 collective-permute-done.26.refs_8_
  234.3 15.5 %fit.1 = f32[1792,2048]{1,0:T(8,128)} custom-call(s32[8]{0:T(128)} %stack.50.refs_0_, s32[1]{0:T(128)} %bitcast.8.refs_0_.refs_1_, s32[4]{0:T(128)} %pad_add_fusion.refs_2_, f32[192,1792]{1,0:T(8,128)} %copy-done.5, f32[192,1792]{1,0:T(8,128)} %collective-permute-done.24.refs_4_, f32[128,1792]{1,0:T(8,128)} %copy-done.6, f32[128,1792]{1,0:T(8,128)} %copy-done.12, ...), custom_call_target="tpu_custom_call" | custom-call | flops 3758096384 | bytes 24117248 | tf_op jit(solution)/shard_map/fit/pallas_call | solution.py:62
  (85 shorter events, 29.9 us)
Async XLA Ops:
  0.0 15.8 %collective-permute-start.2 = (bf16[64,14336]{1,0:T(8,128)(2,1)}, bf16[64,14336]{1,0:T(8,128)(2,1)}, u32[]{:S(2)}, u32[]{:S(2)}) collective-permute-start(bf16[64,14336]{1,0:T(8,128)(2,1)} %refs_1_.3), channel_id=1, source_target_pairs={{4,8},{6,10},{8,4},{10,6},{5,9},{7,11},{9,5},{11,7},{20,24},{22,26... | collective-permute-start | bytes 5505032 | tf_op jit(solution)/shard_map/ppermute | solution.py:177
  2.1 44.6 %collective-permute-start.1 = (bf16[64,14336]{1,0:T(8,128)(2,1)}, bf16[64,14336]{1,0:T(8,128)(2,1)S(1)}, u32[]{:S(2)}, u32[]{:S(2)}) collective-permute-start(bf16[64,14336]{1,0:T(8,128)(2,1)} %refs_1_.3), channel_id=1, source_target_pairs={{0,4},{2,6},{4,0},{6,2},{8,12},{10,14},{12,8},{14,10},{1,5},{3,7},... | collective-permute-start | bytes 5505032 | tf_op jit(solution)/shard_map/ppermute | solution.py:177
  6.7 41.5 %collective-permute-start = (bf16[64,14336]{1,0:T(8,128)(2,1)}, bf16[64,14336]{1,0:T(8,128)(2,1)}, u32[]{:S(2)}, u32[]{:S(2)}) collective-permute-start(bf16[64,14336]{1,0:T(8,128)(2,1)} %refs_1_.3), channel_id=1, source_target_pairs={{0,2},{2,0},{4,6},{6,4},{8,10},{10,8},{12,14},{14,12},{1,3},{3,1},... | collective-permute-start | bytes 5505032 | tf_op jit(solution)/shard_map/ppermute | solution.py:177
  49.7 54.6 %collective-permute-start.3 = (bf16[64,14336]{1,0:T(8,128)(2,1)}, bf16[64,14336]{1,0:T(8,128)(2,1)}, u32[]{:S(2)}, u32[]{:S(2)}) collective-permute-start(bf16[64,14336]{1,0:T(8,128)(2,1)} %broadcast_select_fusion.1), channel_id=1, source_target_pairs={{0,2},{2,0},{4,6},{6,4},{8,10},{10,8},{12,14},{14,12},{1,3},{3,1},... | collective-permute-start | bytes 5505032 | tf_op jit(solution)/shard_map/ppermute | solution.py:177
  51.2 53.2 %collective-permute-start.4 = (bf16[64,14336]{1,0:T(8,128)(2,1)}, bf16[64,14336]{1,0:T(8,128)(2,1)}, u32[]{:S(2)}, u32[]{:S(2)}) collective-permute-start(bf16[64,14336]{1,0:T(8,128)(2,1)} %collective-permute-done.2.refs_2_), channel_id=1, source_target_pairs={{4,0},{6,2},{8,12},{10,14},{5,1},{7,3},{9,13},{11,15},{20,16},{22,... | collective-permute-start | bytes 5505032 | tf_op jit(solution)/shard_map/ppermute | solution.py:177
  52.5 51.9 %collective-permute-start.5 = (bf16[64,14336]{1,0:T(8,128)(2,1)}, bf16[64,14336]{1,0:T(8,128)(2,1)S(1)}, u32[]{:S(2)}, u32[]{:S(2)}) collective-permute-start(bf16[64,14336]{1,0:T(8,128)(2,1)} %copy-done.2), channel_id=1, source_target_pairs={{4,8},{6,10},{8,4},{10,6},{5,9},{7,11},{9,5},{11,7},{20,24},{22,26... | collective-permute-start | bytes 5505032 | tf_op jit(solution)/shard_map/ppermute | solution.py:177
  53.3 31.6 %collective-permute-start.6 = (bf16[512,1024]{1,0:T(8,128)(2,1)}, bf16[512,1024]{1,0:T(8,128)(2,1)}, u32[]{:S(2)}, u32[]{:S(2)}) collective-permute-start(bf16[512,1024]{1,0:T(8,128)(2,1)} %get-tuple-element.111), channel_id=1, source_target_pairs={{0,4},{2,6},{12,8},{14,10},{1,5},{3,7},{13,9},{15,11},{16,20},{18,... | collective-permute-start | bytes 3145736 | tf_op jit(solution)/shard_map/ppermute | solution.py:177
  61.9 42.5 %collective-permute-start.7 = (bf16[512,1024]{1,0:T(8,128)(2,1)}, bf16[512,1024]{1,0:T(8,128)(2,1)}, u32[]{:S(2)}, u32[]{:S(2)}) collective-permute-start(bf16[512,1024]{1,0:T(8,128)(2,1)} %get-tuple-element.113), channel_id=1, source_target_pairs={{0,4},{2,6},{12,8},{14,10},{1,5},{3,7},{13,9},{15,11},{16,20},{18,... | collective-permute-start | bytes 3145736 | tf_op jit(solution)/shard_map/ppermute | solution.py:177
  79.7 17.7 %copy-start.8 = (f32[512,1024]{1,0:T(8,128)S(1)}, f32[512,1024]{1,0:T(8,128)}, u32[]{:S(2)}) copy-start(f32[512,1024]{1,0:T(8,128)} %get-tuple-element.65) | copy-start | bytes 6291460
  97.4 98.6 %copy-start.5 = (f32[192,1792]{1,0:T(8,128)}, f32[192,1792]{1,0:T(8,128)S(1)}, u32[]{:S(2)}) copy-start(f32[192,1792]{1,0:T(8,128)S(1)} %rotate.8.refs_3_) | copy-start | bytes 4128772
  104.4 51.8 %collective-permute-start.12 = (f32[512,1024]{1,0:T(8,128)S(1)}, f32[512,1024]{1,0:T(8,128)S(1)}, u32[]{:S(2)}, u32[]{:S(2)}) collective-permute-start(f32[512,1024]{1,0:T(8,128)S(1)} %convert_add_fusion.1), channel_id=1, source_target_pairs={{4,8},{6,10},{8,4},{10,6},{5,9},{7,11},{9,5},{11,7},{20,24},{22,26... | collective-permute-start | bytes 6291464 | tf_op jit(solution)/shard_map/ppermute | solution.py:177
  106.9 29.7 %copy-start.7 = (f32[512,1024]{1,0:T(8,128)S(1)}, f32[512,1024]{1,0:T(8,128)}, u32[]{:S(2)}) copy-start(f32[512,1024]{1,0:T(8,128)} %get-tuple-element.78) | copy-start | bytes 6291460
  106.9 39.1 %collective-permute-start.8 = (bf16[64,14336]{1,0:T(8,128)(2,1)S(1)}, bf16[64,14336]{1,0:T(8,128)(2,1)S(1)}, u32[]{:S(2)}, u32[]{:S(2)}) collective-permute-start(bf16[64,14336]{1,0:T(8,128)(2,1)S(1)} %broadcast_select_fusion), channel_id=1, source_target_pairs={{0,2},{2,0},{4,6},{6,4},{8,10},{10,8},{12,14},{14,12},{1,3},{3,1},... | collective-permute-start | bytes 5505032 | tf_op jit(solution)/shard_map/ppermute | solution.py:177
  107.5 41.4 %collective-permute-start.10 = (bf16[64,14336]{1,0:T(8,128)(2,1)}, bf16[64,14336]{1,0:T(8,128)(2,1)S(1)}, u32[]{:S(2)}, u32[]{:S(2)}) collective-permute-start(bf16[64,14336]{1,0:T(8,128)(2,1)} %collective-permute-done.refs_3_), channel_id=1, source_target_pairs={{0,4},{2,6},{12,8},{14,10},{1,5},{3,7},{13,9},{15,11},{16,20},{18,... | collective-permute-start | bytes 5505032 | tf_op jit(solution)/shard_map/ppermute | solution.py:177
  112.9 39.9 %collective-permute-start.9 = (bf16[64,14336]{1,0:T(8,128)(2,1)S(1)}, bf16[64,14336]{1,0:T(8,128)(2,1)S(1)}, u32[]{:S(2)}, u32[]{:S(2)}) collective-permute-start(bf16[64,14336]{1,0:T(8,128)(2,1)S(1)} %collective-permute-done.5.refs_2_), channel_id=1, source_target_pairs={{4,0},{6,2},{8,12},{10,14},{5,1},{7,3},{9,13},{11,15},{20,16},{22,... | collective-permute-start | bytes 5505032 | tf_op jit(solution)/shard_map/ppermute | solution.py:177
  136.6 59.4 %copy-start.6 = (f32[128,1792]{1,0:T(8,128)}, f32[128,1792]{1,0:T(8,128)S(1)}, u32[]{:S(2)}) copy-start(f32[128,1792]{1,0:T(8,128)S(1)} %rotate.9.refs_5_) | copy-start | bytes 2752516
  152.9 11.1 %collective-permute-start.11 = (bf16[64,4096]{1,0:T(8,128)(2,1)S(1)}, bf16[64,4096]{1,0:T(8,128)(2,1)S(1)}, u32[]{:S(2)}, u32[]{:S(2)}) collective-permute-start(bf16[64,4096]{1,0:T(8,128)(2,1)S(1)} %slice.24), channel_id=1, source_target_pairs={{0,2},{2,0},{12,14},{14,12},{1,3},{3,1},{13,15},{15,13},{16,18},{1... | collective-permute-start | bytes 1572872 | tf_op jit(solution)/shard_map/ppermute | solution.py:177
  156.5 7.5 %collective-permute-start.13 = (bf16[512,512]{1,0:T(8,128)(2,1)S(1)}, bf16[512,512]{1,0:T(8,128)(2,1)S(1)}, u32[]{:S(2)}, u32[]{:S(2)}) collective-permute-start(bf16[512,512]{1,0:T(8,128)(2,1)S(1)} %fusion.10), channel_id=1, source_target_pairs={{4,6},{6,4},{8,10},{10,8},{5,7},{7,5},{9,11},{11,9},{20,22},{22,20... | collective-permute-start | bytes 1572872 | tf_op jit(solution)/shard_map/ppermute | solution.py:177
  164.6 13.6 %collective-permute-start.17 = (bf16[512,512]{1,0:T(8,128)(2,1)S(1)}, bf16[512,512]{1,0:T(8,128)(2,1)S(1)}, u32[]{:S(2)}, u32[]{:S(2)}) collective-permute-start(bf16[512,512]{1,0:T(8,128)(2,1)S(1)} %get-tuple-element.109.refs_10_), channel_id=1, source_target_pairs={{4,0},{6,2},{8,12},{10,14},{5,1},{7,3},{9,13},{11,15},{20,16},{22,... | collective-permute-start | bytes 1572872 | tf_op jit(solution)/shard_map/ppermute | solution.py:177
  165.9 12.3 %collective-permute-start.16 = (bf16[512,512]{1,0:T(8,128)(2,1)S(1)}, bf16[512,512]{1,0:T(8,128)(2,1)S(1)}, u32[]{:S(2)}, u32[]{:S(2)}) collective-permute-start(bf16[512,512]{1,0:T(8,128)(2,1)S(1)} %get-tuple-element.109.refs_10_), channel_id=1, source_target_pairs={{4,8},{6,10},{8,4},{10,6},{5,9},{7,11},{9,5},{11,7},{20,24},{22,26... | collective-permute-start | bytes 1572872 | tf_op jit(solution)/shard_map/ppermute | solution.py:177
  166.6 11.6 %collective-permute-start.15 = (bf16[512,512]{1,0:T(8,128)(2,1)S(1)}, bf16[512,512]{1,0:T(8,128)(2,1)S(1)}, u32[]{:S(2)}, u32[]{:S(2)}) collective-permute-start(bf16[512,512]{1,0:T(8,128)(2,1)S(1)} %get-tuple-element.110), channel_id=1, source_target_pairs={{4,6},{6,4},{8,10},{10,8},{5,7},{7,5},{9,11},{11,9},{20,22},{22,20... | collective-permute-start | bytes 1572872 | tf_op jit(solution)/shard_map/ppermute | solution.py:177
  167.3 12.1 %collective-permute-start.14 = (bf16[64,4096]{1,0:T(8,128)(2,1)S(1)}, bf16[64,4096]{1,0:T(8,128)(2,1)S(1)}, u32[]{:S(2)}, u32[]{:S(2)}) collective-permute-start(bf16[64,4096]{1,0:T(8,128)(2,1)S(1)} %slice.27), channel_id=1, source_target_pairs={{0,2},{2,0},{12,14},{14,12},{1,3},{3,1},{13,15},{15,13},{16,18},{1... | collective-permute-start | bytes 1572872 | tf_op jit(solution)/shard_map/ppermute | solution.py:177
  179.7 16.8 %copy-start.9 = (bf16[512,512]{1,0:T(8,128)(2,1)}, bf16[512,512]{1,0:T(8,128)(2,1)S(1)}, u32[]{:S(2)}) copy-start(bf16[512,512]{1,0:T(8,128)(2,1)S(1)} %add_convert_fusion.refs_12_) | copy-start | bytes 1572868
  179.8 13.6 %collective-permute-start.18 = (bf16[64,4096]{1,0:T(8,128)(2,1)S(1)}, bf16[64,4096]{1,0:T(8,128)(2,1)S(1)}, u32[]{:S(2)}, u32[]{:S(2)}) collective-permute-start(bf16[64,4096]{1,0:T(8,128)(2,1)S(1)} %slice.30), channel_id=1, source_target_pairs={{0,2},{2,0},{12,14},{14,12},{1,3},{3,1},{13,15},{15,13},{16,18},{1... | collective-permute-start | bytes 1572872 | tf_op jit(solution)/shard_map/ppermute | solution.py:177
  183.8 9.6 %collective-permute-start.19 = (bf16[512,512]{1,0:T(8,128)(2,1)S(1)}, bf16[512,512]{1,0:T(8,128)(2,1)S(1)}, u32[]{:S(2)}, u32[]{:S(2)}) collective-permute-start(bf16[512,512]{1,0:T(8,128)(2,1)S(1)} %add_convert_fusion.refs_12_), channel_id=1, source_target_pairs={{4,8},{6,10},{8,4},{10,6},{5,9},{7,11},{9,5},{11,7},{20,24},{22,26... | collective-permute-start | bytes 1572872 | tf_op jit(solution)/shard_map/ppermute | solution.py:177
  184.5 11.6 %collective-permute-start.20 = (bf16[512,512]{1,0:T(8,128)(2,1)S(1)}, bf16[512,512]{1,0:T(8,128)(2,1)S(1)}, u32[]{:S(2)}, u32[]{:S(2)}) collective-permute-start(bf16[512,512]{1,0:T(8,128)(2,1)S(1)} %collective-permute-done.16.refs_14_), channel_id=1, source_target_pairs={{4,0},{6,2},{8,12},{10,14},{5,1},{7,3},{9,13},{11,15},{20,16},{22,... | collective-permute-start | bytes 1572872 | tf_op jit(solution)/shard_map/ppermute | solution.py:177
  196.1 28.5 %collective-permute-start.24 = (f32[192,1792]{1,0:T(8,128)S(1)}, f32[192,1792]{1,0:T(8,128)}, u32[]{:S(2)}, u32[]{:S(2)}) collective-permute-start(f32[192,1792]{1,0:T(8,128)S(1)} %rotate.8.refs_3_), channel_id=1, source_target_pairs={{0,1},{1,0},{2,3},{3,2},{4,5},{5,4},{6,7},{7,6},{8,9},{9,8},{10,11... | collective-permute-start | bytes 4128776 | tf_op jit(solution)/shard_map/ppermute | solution.py:139
  196.1 27.5 %collective-permute-start.25 = (f32[128,1792]{1,0:T(8,128)S(1)}, f32[128,1792]{1,0:T(8,128)S(1)}, u32[]{:S(2)}, u32[]{:S(2)}) collective-permute-start(f32[128,1792]{1,0:T(8,128)S(1)} %rotate.9.refs_5_), channel_id=1, source_target_pairs={{0,1},{1,0},{2,3},{3,2},{4,5},{5,4},{6,7},{7,6},{8,9},{9,8},{10,11... | collective-permute-start | bytes 2752520 | tf_op jit(solution)/shard_map/ppermute | solution.py:139
  196.6 16.7 %collective-permute-start.22 = (bf16[512,512]{1,0:T(8,128)(2,1)S(1)}, bf16[512,512]{1,0:T(8,128)(2,1)S(1)}, u32[]{:S(2)}, u32[]{:S(2)}) collective-permute-start(bf16[512,512]{1,0:T(8,128)(2,1)S(1)} %add_convert_fusion.refs_12_), channel_id=1, source_target_pairs={{4,0},{6,2},{8,12},{10,14},{5,1},{7,3},{9,13},{11,15},{20,16},{22,... | collective-permute-start | bytes 1572872 | tf_op jit(solution)/shard_map/ppermute | solution.py:177
  197.9 25.7 %collective-permute-start.23 = (bf16[512,512]{1,0:T(8,128)(2,1)S(1)}, bf16[512,512]{1,0:T(8,128)(2,1)S(1)}, u32[]{:S(2)}, u32[]{:S(2)}) collective-permute-start(bf16[512,512]{1,0:T(8,128)(2,1)S(1)} %collective-permute-done.19.refs_16_), channel_id=1, source_target_pairs={{4,0},{6,2},{8,12},{10,14},{5,1},{7,3},{9,13},{11,15},{20,16},{22,... | collective-permute-start | bytes 1572872 | tf_op jit(solution)/shard_map/ppermute | solution.py:177
  199.4 13.9 %collective-permute-start.21 = (bf16[64,2048]{1,0:T(8,128)(2,1)S(1)}, bf16[64,2048]{1,0:T(8,128)(2,1)S(1)}, u32[]{:S(2)}, u32[]{:S(2)}) collective-permute-start(bf16[64,2048]{1,0:T(8,128)(2,1)S(1)} %slice.31), channel_id=1, source_target_pairs={{0,2},{2,0},{12,14},{14,12},{1,3},{3,1},{13,15},{15,13},{16,18},{1... | collective-permute-start | bytes 786440 | tf_op jit(solution)/shard_map/ppermute | solution.py:177
  229.8 3.3 %collective-permute-start.26 = (f32[192,1792]{1,0:T(8,128)}, f32[192,1792]{1,0:T(8,128)S(1)}, u32[]{:S(2)}, u32[]{:S(2)}) collective-permute-start(f32[192,1792]{1,0:T(8,128)} %rotate.13.refs_7_), channel_id=1, source_target_pairs={{0,1},{1,0},{2,3},{3,2},{4,5},{5,4},{6,7},{7,6},{8,9},{9,8},{10,11... | collective-permute-start | bytes 4128776 | tf_op jit(solution)/shard_map/ppermute | solution.py:139
  (15 other events, 110.5 us)

commit v8 on v7

--- a/solution.py
+++ b/solution.py
@@ -205,62 +205,74 @@
         got["m4", p] = send(got["sum", p], MIDDLE)
         got["n1", p] = send(got["sum", p], TO_ENDS)
 
+    flip = jnp.where(z >= 2, 3, 0)
+    line = lambda a, b: jnp.where(at_end, a, b) ^ flip
+    mine, other = (lambda a, b: line(a, b) * PAIR + x), (lambda a, b: line(a, b) * PAIR + 1 - x)
+    order = [mine(0, 1), mine(1, 0), other(0, 1), mine(2, 2), other(1, 2), mine(3, 3), other(2, 0), other(3, 3)]
+    got["order"] = jnp.stack(order).astype(jnp.int32)
+    places = [2 * half, 2 * half + 1, 2 - 2 * half, 3 - 2 * half]
+    got["places"] = jnp.stack(places).astype(jnp.int32)
+
     got["x1"] = send(got["own"], ACROSS)
     got["a1"] = send(got["own"], ENDS)
     got["m1"] = send(got["own"], MIDDLE)
     got["give"] = dot(deltas, columns(basis_out, 1 - half))
     got["r1", 0] = send(got["give"].astype(BF16), FROM_ENDS)
     got["keep"] = dot(deltas, columns(basis_out, half))
-    got["r1", 1] = send(got["keep"].astype(BF16), FROM_ENDS)
-    fence("x1", "a1", "m1", "give", "keep")
+    got["keep16"] = got["keep"].astype(BF16)
+    fence("x1", "a1", "m1", "give", "keep", "keep16", "order", "places")
     got["pick"] = pick("a1", "m1")
     fence("pick", "a1", "m1", "x1")
     got["x2"] = send(got["pick"], ACROSS)
     got["a2"] = send(got["m1"], TO_ENDS)
     got["m2"] = send(got["a1"], MIDDLE)
+    fence(("r1", 0), "x1", "give", "keep16")
+    got["r1", 1] = send(got["keep16"], FROM_ENDS)
+    got["give"] += got["r1", 0].astype(F32)
+    for p in range(2):
+        got["give", p] = got["give"][:, p * part : (p + 1) * part]
+    got["A"] = turn(None, [["own"], ["a1"], ["x1"]], 0, steps)
+    fence("x1", "x2", "a2", "m2", ("give", 0), ("give", 1), "keep", ("r1", 1), "A")
+    got["x3"] = send(got["a2"], ACROSS_ENDS)
+    got["a3"] = send(got["m2"], TO_ENDS)
+    for p in range(2):
+        got["m3", p] = send(got["give", p], MIDDLE)
+    got["e"] = send(got["x1"], FROM_ENDS)
+    got["keep"] += got["r1", 1].astype(F32)
     some = steps // 2
-    got["A"] = turn(None, [["own"], ["a1"], ["x1"]], 0, some)
-    fence(("r1", 0), "give", "A")
-    got["give"] += got["r1", 0].astype(F32)
-    got["A"] = turn(got["A"], [["own"], ["a1"], ["x1"]], some, steps - some)
-    fence("x1", "x2", "a2", "m2", "give", "keep", ("r1", 1), "A")
-    got["m3"] = send(got["give"], MIDDLE)
-    got["pick"] = pick("a2", "m2")
-    fence("pick", "m2", "x1", "keep")
-    got["x3"] = send(got["pick"], ACROSS)
-    got["a3"] = send(got["m2"], TO_ENDS)
-    got["e"] = send(got["x1"], FROM_ENDS)
-    got["B"] = turn(None, [["a2", "m1"], ["x2"]], 0, steps)
-    fence("x3", "a3", "e", "B")
-    got["keep"] += got["r1", 1].astype(F32)
+    got["B"] = turn(None, [["a2", "m1"], ["x2"]], 0, some)
+    fence(("m3", 0), "keep", "B")
+
+    def cross(p):
+        got["keep", p] = got["keep"][:, p * part : (p + 1) * part] + got["m3", p]
+        got["x5", p] = send(got["keep", p].astype(BF16), ACROSS_MIDDLE)
+
+    cross(0)
+    got["B"] = turn(got["B"], [["a2", "m1"], ["x2"]], some, steps - some)
+    fence("x3", "a3", "e", ("x5", 0), "B")
 
     def x4(piece):
-        got["x4", piece] = send(got["a3"][:, cuts[piece] * DEEP : cuts[piece + 1] * DEEP], ACROSS_ENDS)
+        here = slice(cuts[piece] * DEEP, cuts[piece + 1] * DEEP)
+        got["x4", piece] = send(jnp.where(at_end, got["a3"][:, here], got["m2"][:, here]), ACROSS)
 
     def last(piece):
         first = cuts[piece]
-        blocks = [[(got["a3"], first), (got["m2"], first)], [(got["x3"], first)], [(got["x4", piece], 0), (got["e"], first)]]
+        blocks = [[(got["a3"], first), (got["m2"], first)], [(got["x3"], first), (got["e"], first)], [(got["x4", piece], 0)]]
         got["D"] = rotate(got.get("D"), end, blocks, basis_in, first, cuts[piece + 1] - first)
 
-    def cross(p):
-        here = slice(p * part, (p + 1) * part)
-        got["keep", p] = got["keep"][:, here] + got["m3"][:, here]
-        got["x5", p] = send(got["keep", p].astype(BF16), ACROSS_MIDDLE)
-
     x4(0)
-    fence("m3", "a3")
-    cross(0)
+    settle(0)
+    fence(("m3", 1), "a3", "m2")
     cross(1)
-    fence(("x4", 0), ("x5", 0), "a3")
+    fence(("x4", 0), ("m4", 0), ("n1", 0), "a3", "m2")
     x4(1)
-    settle(0)
+    got["n2", 0] = send(got["m4", 0], TO_ENDS)
     last(0)
-    fence(("x4", 1), ("x5", 1), ("m4", 0), ("n1", 0), "D", "a3")
+    fence(("x4", 1), ("x5", 1), "D", "a3", "m2")
     x4(2)
-    got["n2", 0] = send(got["m4", 0], TO_ENDS)
     settle(1)
     last(1)
-    fence(("x4", 2), ("m4", 1), ("n2", 0), "A", "B", "D", "a3")
+    fence(("x4", 2), ("m4", 1), ("n2", 0), "A", "B", "D", "a3", "m2")
     x4(3)
     got["n2", 1] = send(got["m4", 1], TO_ENDS)
     got["A2"] = swap_narrow(got["A"])
@@ -270,14 +282,9 @@
     last(3)
     got["D2"] = swap_narrow(got["D"])
 
-    flip = jnp.where(z >= 2, 3, 0)
-    line = lambda a, b: jnp.where(at_end, a, b) ^ flip
-    mine, other = (lambda a, b: line(a, b) * PAIR + x), (lambda a, b: line(a, b) * PAIR + 1 - x)
-    order = [mine(0, 1), mine(1, 0), other(0, 1), mine(2, 2), other(1, 2), mine(3, 3), other(2, 3), other(3, 0)]
     pieces = [[got["n1", p], got["sum", p]] for p in range(2)] + [[got["n2", p], got["m4", p]] for p in range(2)]
-    places = [2 * half, 2 * half + 1, 2 - 2 * half, 3 - 2 * half]
     sums = [(got[n], got[n + "2"]) for n in "ABD"]
-    return fit(jnp.stack(order).astype(jnp.int32), end, sums, pieces, jnp.stack(places).astype(jnp.int32))
+    return fit(got["order"], end, sums, pieces, got["places"])
 
 
 def solution(mesh):

time: 251 us -> 250 us (level)
  starting transfers between devices: 52.6 us -> 44.2 us
  waiting for transfers between devices: 83.3 us -> 89.8 us
    ppermute x24 -> x25, starting transfers between devices: 52.1 us -> 43.7 us  [send(): return lax.ppermute(a, 'wide', perm)]
    ppermute x24 -> x25, waiting for transfers between devices: 81.3 us -> 86.6 us  [send(): return lax.ppermute(a, 'wide', perm)]
    unnamed x40 -> x42, local copies, waits for them, and re-layouts: 5.11 us -> 3.48 us
  transfers between devices with their start and end apart: 27 -> 28, of which waited for: 13 -> 11; matrix products, arithmetic and copies ran while one was open for 6% -> 8% of each run, Pallas kernels for 28% -> 28%
where the time goes in v8:
time: 250 us; the launch traced here: 249 us
  Pallas kernels  91.3 us (37%)
  waiting for transfers between devices  89.8 us (36%)
  starting transfers between devices  44.2 us (18%)
  other arithmetic  9.47 us (4%)
  matrix products  9 us (4%)
  local copies, waits for them, and re-layouts  4.29 us (2%)
    ppermute x25, waiting for transfers between devices, send(): return lax.ppermute(a, 'wide', perm)  86.6 us
    pallas_call x7, Pallas kernels, rotate(): pl.pallas_call(lambda *refs: rotate_kernel([len(block) for block in block...  75.8 us
    ppermute x25, starting transfers between devices, send(): return lax.ppermute(a, 'wide', perm)  43.7 us
    pallas_call x1, Pallas kernels, fit(): pl.pallas_call(lambda *refs: fit_kernel([pair[0].shape[0] for pair in sum...  15.5 us
    dot_general x2, matrix products, dot(): return jnp.dot(a, b, preferred_element_type=F32)  9 us
  transfers between devices with their start and end apart: 28, of which 11 were waited for; matrix products, arithmetic and copies ran while one was open for 8% of the time, Pallas kernels for 28%

profile of v8, /device:TPU:0, one launch (start us, length us, event | category | flops | bytes accessed | tf_op | source)
XLA Modules:
  0.0 248.7 jit_solution(6921613594551028703)
XLA Ops:
  0.0 3.0 %collective-permute-start.1 = (bf16[64,14336]{1,0:T(8,128)(2,1)}, bf16[64,14336]{1,0:T(8,128)(2,1)}, u32[]{:S(2)}, u32[]{:S(2)}) collective-permute-start(bf16[64,14336]{1,0:T(8,128)(2,1)} %refs_1_.1), channel_id=1, source_target_pairs={{0,4},{2,6},{4,0},{6,2},{8,12},{10,14},{12,8},{14,10},{1,5},{3,7},... | collective-permute-start | bytes 5505032 | tf_op jit(solution)/shard_map/ppermute | solution.py:177
  3.0 1.5 collective-permute-start
  5.3 4.5 %fusion.16 = (bf16[512,1024]{1,0:T(8,128)(2,1)}, f32[512,1024]{1,0:T(8,128)}) fusion(bf16[512,1024]{1,0:T(8,128)(2,1)S(1)} %copy-done, bf16[1024,2048]{1,0:T(8,128)(2,1)} %param.7, s32[]{:T(128)S(6)} %select_n.70), kind=kOutput, calls=%fused_computation.24 | convolution fusion | flops 1074266112 | bytes 6291460 | tf_op jit(solution)/shard_map/dot_general | solution.py:16
  9.9 7.2 %collective-permute-start.3 = (bf16[512,1024]{1,0:T(8,128)(2,1)}, bf16[512,1024]{1,0:T(8,128)(2,1)}, u32[]{:S(2)}, u32[]{:S(2)}) collective-permute-start(bf16[512,1024]{1,0:T(8,128)(2,1)} %get-tuple-element.131), channel_id=1, source_target_pairs={{0,4},{2,6},{12,8},{14,10},{1,5},{3,7},{13,9},{15,11},{16,20},{18,... | collective-permute-start | bytes 3145736 | tf_op jit(solution)/shard_map/ppermute | solution.py:177
  18.2 4.5 %fusion.15 = (bf16[512,1024]{1,0:T(8,128)(2,1)}, f32[512,1024]{1,0:T(8,128)}) fusion(bf16[512,1024]{1,0:T(8,128)(2,1)S(1)} %copy-done, bf16[1024,2048]{1,0:T(8,128)(2,1)} %param.7, s32[]{:T(128)S(6)} %select_n.71), kind=kOutput, calls=%fused_computation.23 | convolution fusion | flops 1074266112 | bytes 6291460 | tf_op jit(solution)/shard_map/dot_general | solution.py:16
  22.7 21.1 %collective-permute-done.1.refs_2_ = bf16[64,14336]{1,0:T(8,128)(2,1)} collective-permute-done((bf16[64,14336]{1,0:T(8,128)(2,1)}, bf16[64,14336]{1,0:T(8,128)(2,1)}, u32[]{:S(2)}, u32[]{:S(2)}) %collective-permute-start.1) | collective-permute-done | bytes 1835040 | tf_op jit(solution)/shard_map/ppermute | solution.py:177
  44.8 3.7 %broadcast_select_fusion = bf16[64,14336]{1,0:T(8,128)(2,1)} fusion(bf16[64,14336]{1,0:T(8,128)(2,1)} %collective-permute-done.1.refs_2_, bf16[64,14336]{1,0:T(8,128)(2,1)S(1)} %collective-permute-done.2.refs_2_, pred[]{:T(512)S(6)} %or.3), kind=kLoop, calls=%fused_computation.6 | loop fusion | flops 917504 | bytes 5505025 | tf_op jit(solution)/shard_map/jit(_where)/select_n | solution.py:195
  48.5 1.5 collective-permute-start.4
  52.1 13.0 %collective-permute-done.3 = bf16[512,1024]{1,0:T(8,128)(2,1)} collective-permute-done((bf16[512,1024]{1,0:T(8,128)(2,1)}, bf16[512,1024]{1,0:T(8,128)(2,1)}, u32[]{:S(2)}, u32[]{:S(2)}) %collective-permute-start.3) | collective-permute-done | bytes 1048608 | tf_op jit(solution)/shard_map/ppermute | solution.py:177
  65.1 5.4 %collective-permute-start.7 = (bf16[512,1024]{1,0:T(8,128)(2,1)}, bf16[512,1024]{1,0:T(8,128)(2,1)}, u32[]{:S(2)}, u32[]{:S(2)}) collective-permute-start(bf16[512,1024]{1,0:T(8,128)(2,1)} %get-tuple-element.80), channel_id=1, source_target_pairs={{0,4},{2,6},{12,8},{14,10},{1,5},{3,7},{13,9},{15,11},{16,20},{18,... | collective-permute-start | bytes 3145736 | tf_op jit(solution)/shard_map/ppermute | solution.py:177
  70.4 1.5 copy-done.7
  71.9 24.2 %rotate.7.refs_3_ = f32[192,1792]{1,0:T(8,128)S(1)} custom-call(s32[1]{0:T(128)} %bitcast.14.refs_0_.refs_1_, bf16[64,14336]{1,0:T(8,128)(2,1)S(1)} %copy-done.7, bf16[64,14336]{1,0:T(8,128)(2,1)} %collective-permute-done.1.refs_2_, bf16[64,14336]{1,0:T(8,128)(2,1)} %collective-permute-done.refs_3_, bf16[14336,1792]{1,0:T(8,128)(2,1)} %refs_6_.7), custom_call_target="tpu_custom_call" | custom-call | flops 344064 | bytes 1376256 | tf_op jit(solution)/shard_map/rotate/pallas_call | solution.py:118
  96.2 2.2 convert_add_fusion.1
  99.5 3.3 %collective-permute-start.10 = (bf16[64,14336]{1,0:T(8,128)(2,1)}, bf16[64,14336]{1,0:T(8,128)(2,1)S(1)}, u32[]{:S(2)}, u32[]{:S(2)}) collective-permute-start(bf16[64,14336]{1,0:T(8,128)(2,1)} %collective-permute-done.refs_3_), channel_id=1, source_target_pairs={{0,4},{2,6},{12,8},{14,10},{1,5},{3,7},{13,9},{15,11},{16,20},{18,... | collective-permute-start | bytes 5505032 | tf_op jit(solution)/shard_map/ppermute | solution.py:177
  102.8 3.4 %collective-permute-start.8 = (bf16[64,14336]{1,0:T(8,128)(2,1)}, bf16[64,14336]{1,0:T(8,128)(2,1)S(1)}, u32[]{:S(2)}, u32[]{:S(2)}) collective-permute-start(bf16[64,14336]{1,0:T(8,128)(2,1)} %collective-permute-done.5.refs_1_), channel_id=1, source_target_pairs={{0,2},{2,0},{12,14},{14,12},{1,3},{3,1},{13,15},{15,13},{16,18},{1... | collective-permute-start | bytes 5505032 | tf_op jit(solution)/shard_map/ppermute | solution.py:177
  107.5 11.9 %rotate.8.refs_5_ = f32[128,1792]{1,0:T(8,128)S(1)} custom-call(s32[1]{0:T(128)} %bitcast.14.refs_0_.refs_1_, bf16[64,14336]{1,0:T(8,128)(2,1)} %collective-permute-done.5.refs_1_, bf16[64,14336]{1,0:T(8,128)(2,1)S(1)} %copy-done.3, bf16[64,14336]{1,0:T(8,128)(2,1)} %collective-permute-done.4.refs_3_, bf16[14336,1792]{1,0:T(8,128)(2,1)} %refs_6_.7), custom_call_target="tpu_custom_call" | custom-call | flops 229376 | bytes 917504 | tf_op jit(solution)/shard_map/rotate/pallas_call | solution.py:118
  119.4 1.7 convert_add_fusion
  122.8 11.8 %rotate.9.refs_5_ = f32[128,1792]{1,0:T(8,128)S(1)} custom-call(s32[1]{0:T(128)} %bitcast.14.refs_0_.refs_1_, bf16[64,14336]{1,0:T(8,128)(2,1)} %collective-permute-done.5.refs_1_, bf16[64,14336]{1,0:T(8,128)(2,1)S(1)} %copy-done.3, bf16[64,14336]{1,0:T(8,128)(2,1)} %collective-permute-done.4.refs_3_, bf16[14336,1792]{1,0:T(8,128)(2,1)} %refs_6_.7, ...), custom_call_target="tpu_custom_call" | custom-call | flops 229376 | bytes 917504 | tf_op jit(solution)/shard_map/rotate/pallas_call | solution.py:118
  134.7 6.4 %collective-permute-done.10.refs_4_ = bf16[64,14336]{1,0:T(8,128)(2,1)S(1)} collective-permute-done((bf16[64,14336]{1,0:T(8,128)(2,1)}, bf16[64,14336]{1,0:T(8,128)(2,1)S(1)}, u32[]{:S(2)}, u32[]{:S(2)}) %collective-permute-start.10) | collective-permute-done | bytes 1835040 | tf_op jit(solution)/shard_map/ppermute | solution.py:177
  141.1 4.1 %collective-permute-done.8.refs_3_ = bf16[64,14336]{1,0:T(8,128)(2,1)S(1)} collective-permute-done((bf16[64,14336]{1,0:T(8,128)(2,1)}, bf16[64,14336]{1,0:T(8,128)(2,1)S(1)}, u32[]{:S(2)}, u32[]{:S(2)}) %collective-permute-start.8) | collective-permute-done | bytes 1835040 | tf_op jit(solution)/shard_map/ppermute | solution.py:177
  145.2 2.9 %collective-permute-done.9.refs_1_ = bf16[64,14336]{1,0:T(8,128)(2,1)S(1)} collective-permute-done((bf16[64,14336]{1,0:T(8,128)(2,1)S(1)}, bf16[64,14336]{1,0:T(8,128)(2,1)S(1)}, u32[]{:S(2)}, u32[]{:S(2)}) %collective-permute-start.9) | collective-permute-done | bytes 1835040 | tf_op jit(solution)/shard_map/ppermute | solution.py:177
  152.1 7.2 %collective-permute-done.13.refs_5_ = bf16[64,4096]{1,0:T(8,128)(2,1)S(1)} collective-permute-done((bf16[64,4096]{1,0:T(8,128)(2,1)S(1)}, bf16[64,4096]{1,0:T(8,128)(2,1)S(1)}, u32[]{:S(2)}, u32[]{:S(2)}) %collective-permute-start.13) | collective-permute-done | bytes 524320 | tf_op jit(solution)/shard_map/ppermute | solution.py:177
  159.3 3.5 %collective-permute-done.15.refs_9_ = bf16[512,512]{1,0:T(8,128)(2,1)S(1)} collective-permute-done((bf16[512,512]{1,0:T(8,128)(2,1)S(1)}, bf16[512,512]{1,0:T(8,128)(2,1)S(1)}, u32[]{:S(2)}, u32[]{:S(2)}) %collective-permute-start.15) | collective-permute-done | bytes 524320 | tf_op jit(solution)/shard_map/ppermute | solution.py:177
  165.6 7.6 %rotate.10.refs_7_ = f32[192,1792]{1,0:T(8,128)S(1)} custom-call(s32[1]{0:T(128)} %bitcast.14.refs_0_.refs_1_, bf16[64,14336]{1,0:T(8,128)(2,1)S(1)} %collective-permute-done.9.refs_1_, bf16[64,14336]{1,0:T(8,128)(2,1)S(1)} %collective-permute-done.6.refs_2_, bf16[64,14336]{1,0:T(8,128)(2,1)S(1)} %collective-permute-done.8.refs_3_, ...), custom_call_target="tpu_custom_call" | custom-call | flops 344064 | bytes 1376256 | tf_op jit(solution)/shard_map/rotate/pallas_call | solution.py:118
  173.6 2.4 collective-permute-start.19
  176.7 7.6 %rotate.11.refs_7_ = f32[192,1792]{1,0:T(8,128)S(1)} custom-call(s32[1]{0:T(128)} %bitcast.14.refs_0_.refs_1_, bf16[64,14336]{1,0:T(8,128)(2,1)S(1)} %collective-permute-done.9.refs_1_, bf16[64,14336]{1,0:T(8,128)(2,1)S(1)} %collective-permute-done.6.refs_2_, bf16[64,14336]{1,0:T(8,128)(2,1)S(1)} %collective-permute-done.8.refs_3_, ...), custom_call_target="tpu_custom_call" | custom-call | flops 344064 | bytes 1376256 | tf_op jit(solution)/shard_map/rotate/pallas_call | solution.py:118
  188.8 7.6 %rotate.12.refs_7_ = f32[192,1792]{1,0:T(8,128)S(1)} custom-call(s32[1]{0:T(128)} %bitcast.14.refs_0_.refs_1_, bf16[64,14336]{1,0:T(8,128)(2,1)S(1)} %collective-permute-done.9.refs_1_, bf16[64,14336]{1,0:T(8,128)(2,1)S(1)} %collective-permute-done.6.refs_2_, bf16[64,14336]{1,0:T(8,128)(2,1)S(1)} %collective-permute-done.8.refs_3_, ...), custom_call_target="tpu_custom_call" | custom-call | flops 344064 | bytes 1376256 | tf_op jit(solution)/shard_map/rotate/pallas_call | solution.py:118
  196.3 16.6 %collective-permute-done.23.refs_11_ = bf16[512,512]{1,0:T(8,128)(2,1)S(1)} collective-permute-done((bf16[512,512]{1,0:T(8,128)(2,1)S(1)}, bf16[512,512]{1,0:T(8,128)(2,1)S(1)}, u32[]{:S(2)}, u32[]{:S(2)}) %collective-permute-start.23) | collective-permute-done | bytes 524320 | tf_op jit(solution)/shard_map/ppermute | solution.py:177
  213.0 10.7 %collective-permute-done.24.refs_15_ = bf16[512,512]{1,0:T(8,128)(2,1)S(1)} collective-permute-done((bf16[512,512]{1,0:T(8,128)(2,1)S(1)}, bf16[512,512]{1,0:T(8,128)(2,1)S(1)}, u32[]{:S(2)}, u32[]{:S(2)}) %collective-permute-start.24) | collective-permute-done | bytes 524320 | tf_op jit(solution)/shard_map/ppermute | solution.py:177
  223.7 5.1 %rotate.13.refs_7_ = f32[192,1792]{1,0:T(8,128)S(1)} custom-call(s32[1]{0:T(128)} %bitcast.14.refs_0_.refs_1_, bf16[64,14336]{1,0:T(8,128)(2,1)S(1)} %collective-permute-done.9.refs_1_, bf16[64,14336]{1,0:T(8,128)(2,1)S(1)} %collective-permute-done.6.refs_2_, bf16[64,14336]{1,0:T(8,128)(2,1)S(1)} %collective-permute-done.8.refs_3_, ...), custom_call_target="tpu_custom_call" | custom-call | flops 344064 | bytes 1376256 | tf_op jit(solution)/shard_map/rotate/pallas_call | solution.py:118
  228.9 3.1 %collective-permute-done.27.refs_8_ = f32[192,1792]{1,0:T(8,128)S(1)} collective-permute-done((f32[192,1792]{1,0:T(8,128)S(1)}, f32[192,1792]{1,0:T(8,128)S(1)}, u32[]{:S(2)}, u32[]{:S(2)}) %collective-permute-start.27) | collective-permute-done | bytes 1376288 | tf_op jit(solution)/shard_map/ppermute | solution.py:139
  233.1 15.5 %fit.1 = f32[1792,2048]{1,0:T(8,128)} custom-call(s32[8]{0:T(128)} %stack.50.refs_0_, s32[1]{0:T(128)} %bitcast.14.refs_0_.refs_1_, s32[4]{0:T(128)} %pad_add_fusion.refs_2_, f32[192,1792]{1,0:T(8,128)} %copy-done.5, f32[192,1792]{1,0:T(8,128)} %copy-done.12, f32[128,1792]{1,0:T(8,128)} %copy-done.6, f32[128,1792]{1,0:T(8,128)} %copy-done.14, ...), custom_call_target="tpu_custom_call" | custom-call | flops 3758096384 | bytes 24117248 | tf_op jit(solution)/shard_map/fit/pallas_call | solution.py:62
  (89 shorter events, 22.4 us)
Async XLA Ops:
  0.0 43.8 %collective-permute-start.1 = (bf16[64,14336]{1,0:T(8,128)(2,1)}, bf16[64,14336]{1,0:T(8,128)(2,1)}, u32[]{:S(2)}, u32[]{:S(2)}) collective-permute-start(bf16[64,14336]{1,0:T(8,128)(2,1)} %refs_1_.1), channel_id=1, source_target_pairs={{0,4},{2,6},{4,0},{6,2},{8,12},{10,14},{12,8},{14,10},{1,5},{3,7},... | collective-permute-start | bytes 5505032 | tf_op jit(solution)/shard_map/ppermute | solution.py:177
  3.0 41.8 %collective-permute-start = (bf16[64,14336]{1,0:T(8,128)(2,1)}, bf16[64,14336]{1,0:T(8,128)(2,1)}, u32[]{:S(2)}, u32[]{:S(2)}) collective-permute-start(bf16[64,14336]{1,0:T(8,128)(2,1)} %refs_1_.1), channel_id=1, source_target_pairs={{0,2},{2,0},{4,6},{6,4},{8,10},{10,8},{12,14},{14,12},{1,3},{3,1},... | collective-permute-start | bytes 5505032 | tf_op jit(solution)/shard_map/ppermute | solution.py:177
  4.5 40.3 %collective-permute-start.2 = (bf16[64,14336]{1,0:T(8,128)(2,1)}, bf16[64,14336]{1,0:T(8,128)(2,1)S(1)}, u32[]{:S(2)}, u32[]{:S(2)}) collective-permute-start(bf16[64,14336]{1,0:T(8,128)(2,1)} %refs_1_.1), channel_id=1, source_target_pairs={{4,8},{6,10},{8,4},{10,6},{5,9},{7,11},{9,5},{11,7},{20,24},{22,26... | collective-permute-start | bytes 5505032 | tf_op jit(solution)/shard_map/ppermute | solution.py:177
  9.9 55.2 %collective-permute-start.3 = (bf16[512,1024]{1,0:T(8,128)(2,1)}, bf16[512,1024]{1,0:T(8,128)(2,1)}, u32[]{:S(2)}, u32[]{:S(2)}) collective-permute-start(bf16[512,1024]{1,0:T(8,128)(2,1)} %get-tuple-element.131), channel_id=1, source_target_pairs={{0,4},{2,6},{12,8},{14,10},{1,5},{3,7},{13,9},{15,11},{16,20},{18,... | collective-permute-start | bytes 3145736 | tf_op jit(solution)/shard_map/ppermute | solution.py:177
  48.5 50.1 %collective-permute-start.4 = (bf16[64,14336]{1,0:T(8,128)(2,1)}, bf16[64,14336]{1,0:T(8,128)(2,1)}, u32[]{:S(2)}, u32[]{:S(2)}) collective-permute-start(bf16[64,14336]{1,0:T(8,128)(2,1)} %broadcast_select_fusion), channel_id=1, source_target_pairs={{0,2},{2,0},{4,6},{6,4},{8,10},{10,8},{12,14},{14,12},{1,3},{3,1},... | collective-permute-start | bytes 5505032 | tf_op jit(solution)/shard_map/ppermute | solution.py:177
  50.0 48.6 %collective-permute-start.6 = (bf16[64,14336]{1,0:T(8,128)(2,1)}, bf16[64,14336]{1,0:T(8,128)(2,1)S(1)}, u32[]{:S(2)}, u32[]{:S(2)}) collective-permute-start(bf16[64,14336]{1,0:T(8,128)(2,1)} %collective-permute-done.1.refs_2_), channel_id=1, source_target_pairs={{4,8},{6,10},{8,4},{10,6},{5,9},{7,11},{9,5},{11,7},{20,24},{22,26... | collective-permute-start | bytes 5505032 | tf_op jit(solution)/shard_map/ppermute | solution.py:177
  50.8 47.8 %collective-permute-start.5 = (bf16[64,14336]{1,0:T(8,128)(2,1)}, bf16[64,14336]{1,0:T(8,128)(2,1)}, u32[]{:S(2)}, u32[]{:S(2)}) collective-permute-start(bf16[64,14336]{1,0:T(8,128)(2,1)} %copy-done.2), channel_id=1, source_target_pairs={{4,0},{6,2},{8,12},{10,14},{5,1},{7,3},{9,13},{11,15},{20,16},{22,... | collective-permute-start | bytes 5505032 | tf_op jit(solution)/shard_map/ppermute | solution.py:177
  65.1 33.5 %collective-permute-start.7 = (bf16[512,1024]{1,0:T(8,128)(2,1)}, bf16[512,1024]{1,0:T(8,128)(2,1)}, u32[]{:S(2)}, u32[]{:S(2)}) collective-permute-start(bf16[512,1024]{1,0:T(8,128)(2,1)} %get-tuple-element.80), channel_id=1, source_target_pairs={{0,4},{2,6},{12,8},{14,10},{1,5},{3,7},{13,9},{15,11},{16,20},{18,... | collective-permute-start | bytes 3145736 | tf_op jit(solution)/shard_map/ppermute | solution.py:177
  71.9 24.2 %copy-start.8 = (f32[512,1024]{1,0:T(8,128)S(1)}, f32[512,1024]{1,0:T(8,128)}, u32[]{:S(2)}) copy-start(f32[512,1024]{1,0:T(8,128)} %get-tuple-element.77) | copy-start | bytes 6291460
  96.2 88.2 %copy-start.5 = (f32[192,1792]{1,0:T(8,128)}, f32[192,1792]{1,0:T(8,128)S(1)}, u32[]{:S(2)}) copy-start(f32[192,1792]{1,0:T(8,128)S(1)} %rotate.7.refs_3_) | copy-start | bytes 4128772
  98.6 20.8 %copy-start.9 = (f32[512,1024]{1,0:T(8,128)S(1)}, f32[512,1024]{1,0:T(8,128)}, u32[]{:S(2)}) copy-start(f32[512,1024]{1,0:T(8,128)} %get-tuple-element.85) | copy-start | bytes 6291460
  98.6 22.5 %collective-permute-start.11 = (f32[512,512]{1,0:T(8,128)S(1)}, f32[512,512]{1,0:T(8,128)S(1)}, u32[]{:S(2)}, u32[]{:S(2)}) collective-permute-start(f32[512,512]{1,0:T(8,128)S(1)} %get-tuple-element.84), channel_id=1, source_target_pairs={{4,8},{6,10},{8,4},{10,6},{5,9},{7,11},{9,5},{11,7},{20,24},{22,26... | collective-permute-start | bytes 3145736 | tf_op jit(solution)/shard_map/ppermute | solution.py:177
  99.5 41.6 %collective-permute-start.10 = (bf16[64,14336]{1,0:T(8,128)(2,1)}, bf16[64,14336]{1,0:T(8,128)(2,1)S(1)}, u32[]{:S(2)}, u32[]{:S(2)}) collective-permute-start(bf16[64,14336]{1,0:T(8,128)(2,1)} %collective-permute-done.refs_3_), channel_id=1, source_target_pairs={{0,4},{2,6},{12,8},{14,10},{1,5},{3,7},{13,9},{15,11},{16,20},{18,... | collective-permute-start | bytes 5505032 | tf_op jit(solution)/shard_map/ppermute | solution.py:177
  102.8 42.4 %collective-permute-start.8 = (bf16[64,14336]{1,0:T(8,128)(2,1)}, bf16[64,14336]{1,0:T(8,128)(2,1)S(1)}, u32[]{:S(2)}, u32[]{:S(2)}) collective-permute-start(bf16[64,14336]{1,0:T(8,128)(2,1)} %collective-permute-done.5.refs_1_), channel_id=1, source_target_pairs={{0,2},{2,0},{12,14},{14,12},{1,3},{3,1},{13,15},{15,13},{16,18},{1... | collective-permute-start | bytes 5505032 | tf_op jit(solution)/shard_map/ppermute | solution.py:177
  106.2 41.9 %collective-permute-start.9 = (bf16[64,14336]{1,0:T(8,128)(2,1)S(1)}, bf16[64,14336]{1,0:T(8,128)(2,1)S(1)}, u32[]{:S(2)}, u32[]{:S(2)}) collective-permute-start(bf16[64,14336]{1,0:T(8,128)(2,1)S(1)} %collective-permute-done.6.refs_2_), channel_id=1, source_target_pairs={{4,0},{6,2},{8,12},{10,14},{5,1},{7,3},{9,13},{11,15},{20,16},{22,... | collective-permute-start | bytes 5505032 | tf_op jit(solution)/shard_map/ppermute | solution.py:177
  121.4 13.3 %collective-permute-start.12 = (bf16[512,512]{1,0:T(8,128)(2,1)S(1)}, bf16[512,512]{1,0:T(8,128)(2,1)S(1)}, u32[]{:S(2)}, u32[]{:S(2)}) collective-permute-start(bf16[512,512]{1,0:T(8,128)(2,1)S(1)} %fusion.10), channel_id=1, source_target_pairs={{4,6},{6,4},{8,10},{10,8},{5,7},{7,5},{9,11},{11,9},{20,22},{22,20... | collective-permute-start | bytes 1572872 | tf_op jit(solution)/shard_map/ppermute | solution.py:177
  122.1 26.1 %collective-permute-start.16 = (f32[512,512]{1,0:T(8,128)S(1)}, f32[512,512]{1,0:T(8,128)S(1)}, u32[]{:S(2)}, u32[]{:S(2)}) collective-permute-start(f32[512,512]{1,0:T(8,128)S(1)} %get-tuple-element.93), channel_id=1, source_target_pairs={{4,8},{6,10},{8,4},{10,6},{5,9},{7,11},{9,5},{11,7},{20,24},{22,26... | collective-permute-start | bytes 3145736 | tf_op jit(solution)/shard_map/ppermute | solution.py:177
  134.7 50.6 %copy-start.6 = (f32[128,1792]{1,0:T(8,128)}, f32[128,1792]{1,0:T(8,128)S(1)}, u32[]{:S(2)}) copy-start(f32[128,1792]{1,0:T(8,128)S(1)} %rotate.9.refs_5_) | copy-start | bytes 2752516
  148.2 11.1 %collective-permute-start.13 = (bf16[64,4096]{1,0:T(8,128)(2,1)S(1)}, bf16[64,4096]{1,0:T(8,128)(2,1)S(1)}, u32[]{:S(2)}, u32[]{:S(2)}) collective-permute-start(bf16[64,4096]{1,0:T(8,128)(2,1)S(1)} %slice_select_fusion.2), channel_id=1, source_target_pairs={{0,2},{2,0},{4,6},{6,4},{8,10},{10,8},{12,14},{14,12},{1,3},{3,1},... | collective-permute-start | bytes 1572872 | tf_op jit(solution)/shard_map/ppermute | solution.py:177
  149.4 13.4 %collective-permute-start.15 = (bf16[512,512]{1,0:T(8,128)(2,1)S(1)}, bf16[512,512]{1,0:T(8,128)(2,1)S(1)}, u32[]{:S(2)}, u32[]{:S(2)}) collective-permute-start(bf16[512,512]{1,0:T(8,128)(2,1)S(1)} %get-tuple-element.126.refs_10_), channel_id=1, source_target_pairs={{4,0},{6,2},{8,12},{10,14},{5,1},{7,3},{9,13},{11,15},{20,16},{22,... | collective-permute-start | bytes 1572872 | tf_op jit(solution)/shard_map/ppermute | solution.py:177
  150.7 12.1 %collective-permute-start.14 = (bf16[512,512]{1,0:T(8,128)(2,1)S(1)}, bf16[512,512]{1,0:T(8,128)(2,1)S(1)}, u32[]{:S(2)}, u32[]{:S(2)}) collective-permute-start(bf16[512,512]{1,0:T(8,128)(2,1)S(1)} %get-tuple-element.126.refs_10_), channel_id=1, source_target_pairs={{4,8},{6,10},{8,4},{10,6},{5,9},{7,11},{9,5},{11,7},{20,24},{22,26... | collective-permute-start | bytes 1572872 | tf_op jit(solution)/shard_map/ppermute | solution.py:177
  151.4 21.8 %collective-permute-start.18 = (bf16[512,512]{1,0:T(8,128)(2,1)S(1)}, bf16[512,512]{1,0:T(8,128)(2,1)S(1)}, u32[]{:S(2)}, u32[]{:S(2)}) collective-permute-start(bf16[512,512]{1,0:T(8,128)(2,1)S(1)} %get-tuple-element.125), channel_id=1, source_target_pairs={{4,6},{6,4},{8,10},{10,8},{5,7},{7,5},{9,11},{11,9},{20,22},{22,20... | collective-permute-start | bytes 1572872 | tf_op jit(solution)/shard_map/ppermute | solution.py:177
  162.9 10.3 %collective-permute-start.17 = (bf16[64,4096]{1,0:T(8,128)(2,1)S(1)}, bf16[64,4096]{1,0:T(8,128)(2,1)S(1)}, u32[]{:S(2)}, u32[]{:S(2)}) collective-permute-start(bf16[64,4096]{1,0:T(8,128)(2,1)S(1)} %slice_select_fusion.1), channel_id=1, source_target_pairs={{0,2},{2,0},{4,6},{6,4},{8,10},{10,8},{12,14},{14,12},{1,3},{3,1},... | collective-permute-start | bytes 1572872 | tf_op jit(solution)/shard_map/ppermute | solution.py:177
  164.3 20.1 %collective-permute-start.21 = (bf16[512,512]{1,0:T(8,128)(2,1)S(1)}, bf16[512,512]{1,0:T(8,128)(2,1)S(1)}, u32[]{:S(2)}, u32[]{:S(2)}) collective-permute-start(bf16[512,512]{1,0:T(8,128)(2,1)S(1)} %collective-permute-done.14.refs_14_), channel_id=1, source_target_pairs={{4,0},{6,2},{8,12},{10,14},{5,1},{7,3},{9,13},{11,15},{20,16},{22,... | collective-permute-start | bytes 1572872 | tf_op jit(solution)/shard_map/ppermute | solution.py:177
  173.6 10.8 %collective-permute-start.19 = (bf16[64,4096]{1,0:T(8,128)(2,1)S(1)}, bf16[64,4096]{1,0:T(8,128)(2,1)S(1)}, u32[]{:S(2)}, u32[]{:S(2)}) collective-permute-start(bf16[64,4096]{1,0:T(8,128)(2,1)S(1)} %slice_select_fusion), channel_id=1, source_target_pairs={{0,2},{2,0},{4,6},{6,4},{8,10},{10,8},{12,14},{14,12},{1,3},{3,1},... | collective-permute-start | bytes 1572872 | tf_op jit(solution)/shard_map/ppermute | solution.py:177
  176.1 8.3 %collective-permute-start.20 = (bf16[512,512]{1,0:T(8,128)(2,1)S(1)}, bf16[512,512]{1,0:T(8,128)(2,1)S(1)}, u32[]{:S(2)}, u32[]{:S(2)}) collective-permute-start(bf16[512,512]{1,0:T(8,128)(2,1)S(1)} %add_convert_fusion.refs_12_), channel_id=1, source_target_pairs={{4,8},{6,10},{8,4},{10,6},{5,9},{7,11},{9,5},{11,7},{20,24},{22,26... | collective-permute-start | bytes 1572872 | tf_op jit(solution)/shard_map/ppermute | solution.py:177
  185.2 38.4 %collective-permute-start.25 = (f32[192,1792]{1,0:T(8,128)S(1)}, f32[192,1792]{1,0:T(8,128)S(1)}, u32[]{:S(2)}, u32[]{:S(2)}) collective-permute-start(f32[192,1792]{1,0:T(8,128)S(1)} %rotate.7.refs_3_), channel_id=1, source_target_pairs={{0,1},{1,0},{2,3},{3,2},{4,5},{5,4},{6,7},{7,6},{8,9},{9,8},{10,11... | collective-permute-start | bytes 4128776 | tf_op jit(solution)/shard_map/ppermute | solution.py:139
  185.2 38.4 %collective-permute-start.26 = (f32[128,1792]{1,0:T(8,128)S(1)}, f32[128,1792]{1,0:T(8,128)S(1)}, u32[]{:S(2)}, u32[]{:S(2)}) collective-permute-start(f32[128,1792]{1,0:T(8,128)S(1)} %rotate.9.refs_5_), channel_id=1, source_target_pairs={{0,1},{1,0},{2,3},{3,2},{4,5},{5,4},{6,7},{7,6},{8,9},{9,8},{10,11... | collective-permute-start | bytes 2752520 | tf_op jit(solution)/shard_map/ppermute | solution.py:139
  185.8 27.2 %collective-permute-start.23 = (bf16[512,512]{1,0:T(8,128)(2,1)S(1)}, bf16[512,512]{1,0:T(8,128)(2,1)S(1)}, u32[]{:S(2)}, u32[]{:S(2)}) collective-permute-start(bf16[512,512]{1,0:T(8,128)(2,1)S(1)} %add_convert_fusion.refs_12_), channel_id=1, source_target_pairs={{4,0},{6,2},{8,12},{10,14},{5,1},{7,3},{9,13},{11,15},{20,16},{22,... | collective-permute-start | bytes 1572872 | tf_op jit(solution)/shard_map/ppermute | solution.py:177
  187.2 36.4 %collective-permute-start.24 = (bf16[512,512]{1,0:T(8,128)(2,1)S(1)}, bf16[512,512]{1,0:T(8,128)(2,1)S(1)}, u32[]{:S(2)}, u32[]{:S(2)}) collective-permute-start(bf16[512,512]{1,0:T(8,128)(2,1)S(1)} %collective-permute-done.20.refs_16_), channel_id=1, source_target_pairs={{4,0},{6,2},{8,12},{10,14},{5,1},{7,3},{9,13},{11,15},{20,16},{22,... | collective-permute-start | bytes 1572872 | tf_op jit(solution)/shard_map/ppermute | solution.py:177
  188.6 24.4 %collective-permute-start.22 = (bf16[64,2048]{1,0:T(8,128)(2,1)S(1)}, bf16[64,2048]{1,0:T(8,128)(2,1)S(1)}, u32[]{:S(2)}, u32[]{:S(2)}) collective-permute-start(bf16[64,2048]{1,0:T(8,128)(2,1)S(1)} %slice_select_fusion.3), channel_id=1, source_target_pairs={{0,2},{2,0},{4,6},{6,4},{8,10},{10,8},{12,14},{14,12},{1,3},{3,1},... | collective-permute-start | bytes 786440 | tf_op jit(solution)/shard_map/ppermute | solution.py:177
  228.8 3.2 %collective-permute-start.27 = (f32[192,1792]{1,0:T(8,128)S(1)}, f32[192,1792]{1,0:T(8,128)S(1)}, u32[]{:S(2)}, u32[]{:S(2)}) collective-permute-start(f32[192,1792]{1,0:T(8,128)S(1)} %rotate.13.refs_7_), channel_id=1, source_target_pairs={{0,1},{1,0},{2,3},{3,2},{4,5},{5,4},{6,7},{7,6},{8,9},{9,8},{10,11... | collective-permute-start | bytes 4128776 | tf_op jit(solution)/shard_map/ppermute | solution.py:139
  (17 other events, 128.9 us)

commit v9 on v8

--- a/solution.py
+++ b/solution.py
@@ -16,60 +16,62 @@
     return jnp.dot(a, b, preferred_element_type=F32)
 
 
-def fit_kernel(sizes, choices, order_ref, end_ref, place_ref, *refs):
-    sum_refs, refs = refs[: 2 * len(sizes)], refs[2 * len(sizes) :]
+def fit_kernel(count, choices, order_ref, end_ref, place_ref, *refs):
+    sum_refs, refs = refs[: 2 * count], refs[2 * count :]
     piece_refs, (fit_ref, out_ref, turned_ref, rot_ref) = refs[:-4], refs[-4:]
-    rows, ks = out_ref.shape
+    rows = rot_ref.shape[0]
     size, seq = rows // order_ref.shape[0], rows // EX
-
-    @pl.when(pl.program_id(0) == 0)
+    i, j = pl.program_id(0), pl.program_id(1)
+
+    at = 0
+    for piece, choice in enumerate(choices):
+
+        @pl.when((i == 0) & (j == piece))
+        def _(at=at, piece=piece, choice=choice):
+            if choice == 1:
+                out_ref[piece] = piece_refs[at][...]
+            else:
+                out_ref[piece] = jnp.where(end_ref[0] == 1, piece_refs[at][...], piece_refs[at + 1][...])
+
+        at += choice
+
+    @pl.when(j == 0)
     def _():
-        at = 0
-        for piece, choice in enumerate(choices):
-            width = piece_refs[at].shape[1]
-            there = pl.ds(pl.multiple_of(place_ref[piece] * width, width), width)
-            if choice == 1:
-                out_ref[:, there] = piece_refs[at][...]
-            else:
-                out_ref[:, there] = jnp.where(end_ref[0] == 1, piece_refs[at][...], piece_refs[at + 1][...])
-            at += choice
-
-    slot = 0
-    for mine_ref, other_ref in zip(sum_refs[::2], sum_refs[1::2]):
-        for at in range(0, mine_ref.shape[0], size):
-            here = pl.ds(at, size)
-            there = pl.ds(pl.multiple_of(order_ref[slot] * size, size), size)
-            rot_ref[there, :] = mine_ref[here, :] + other_ref[here, :]
-            slot += 1
-    turned_ref[...] = rot_ref[...].T.astype(BF16)
-    step = min(512, ks)
-    for at in range(0, ks, step):
-        total = None
-        for e in range(EX):
-            here = pl.ds(e * seq, seq)
-            grad = dot(turned_ref[:, here], out_ref[here, pl.ds(at, step)])
-            total = grad * grad if total is None else total + grad * grad
-        fit_ref[:, pl.ds(at, step)] = total * (1.0 / EX)
+        slot = 0
+        for mine_ref, other_ref in zip(sum_refs[::2], sum_refs[1::2]):
+            for at in range(0, mine_ref.shape[0], size):
+                here = pl.ds(at, size)
+                there = pl.ds(pl.multiple_of(order_ref[slot] * size, size), size)
+                rot_ref[there, :] = mine_ref[here, :] + other_ref[here, :]
+                slot += 1
+        turned_ref[...] = rot_ref[...].T.astype(BF16)
+
+    total = None
+    for e in range(EX):
+        here = pl.ds(e * seq, seq)
+        grad = dot(turned_ref[:, here], out_ref[j, here, :])
+        total = grad * grad if total is None else total + grad * grad
+    fit_ref[...] = total * (1.0 / EX)
 
 
 def fit(order, end, sums, pieces, places):
     rows = sum(mine.shape[0] for mine, _ in sums)
-    ka = sums[0][0].shape[1]
-    ks = sum(piece[0].shape[1] for piece in pieces)
-    tile = 256 if ka % 256 == 0 else ka
+    ka, part = sums[0][0].shape[1], pieces[0][0].shape[1]
+    ks = len(pieces) * part
+    tile = 896 if ka % 896 == 0 else ka
     flat = [a for pair in sums for a in pair]
     outs = [a for piece in pieces for a in piece]
     return pl.pallas_call(
-        lambda *refs: fit_kernel([pair[0].shape[0] for pair in sums], [len(piece) for piece in pieces], *refs),
+        lambda *refs: fit_kernel(len(sums), [len(piece) for piece in pieces], *refs),
         out_shape=jax.ShapeDtypeStruct((ka, ks), F32),
         grid_spec=pltpu.PrefetchScalarGridSpec(
             num_scalar_prefetch=3,
-            grid=(ka // tile,),
-            in_specs=[pl.BlockSpec((a.shape[0], tile), lambda i, *_: (0, i)) for a in flat]
-            + [pl.BlockSpec(a.shape, lambda i, *_: (0, 0)) for a in outs],
-            out_specs=pl.BlockSpec((tile, ks), lambda i, *_: (i, 0)),
+            grid=(ka // tile, len(pieces)),
+            in_specs=[pl.BlockSpec((a.shape[0], tile), lambda i, j, *_: (0, i)) for a in flat]
+            + [pl.BlockSpec(a.shape, lambda i, j, *_: (0, 0)) for a in outs],
+            out_specs=pl.BlockSpec((tile, part), lambda i, j, order, end, places: (i, places[j])),
             scratch_shapes=[
-                pltpu.VMEM((rows, ks), BF16),
+                pltpu.VMEM((len(pieces), rows, part), BF16),
                 pltpu.VMEM((tile, rows), BF16),
                 pltpu.VMEM((rows, tile), F32),
             ],
@@ -184,7 +186,7 @@
     end = at_end.astype(jnp.int32).reshape(1)
     half = (z >= 2).astype(jnp.int32)
     steps = inputs.shape[1] // DEEP
-    cuts = [0, 4 * steps // 14, 8 * steps // 14, 12 * steps // 14, steps]
+    cuts = [0, 6 * steps // 14, 11 * steps // 14, steps]
     part = basis_out.shape[1] // 4
     got = {"own": inputs}
 
@@ -249,7 +251,7 @@
 
     cross(0)
     got["B"] = turn(got["B"], [["a2", "m1"], ["x2"]], some, steps - some)
-    fence("x3", "a3", "e", ("x5", 0), "B")
+    fence("x3", "a3", "e", ("x5", 0), ("m3", 1), "B")
 
     def x4(piece):
         here = slice(cuts[piece] * DEEP, cuts[piece + 1] * DEEP)
@@ -260,29 +262,29 @@
         blocks = [[(got["a3"], first), (got["m2"], first)], [(got["x3"], first), (got["e"], first)], [(got["x4", piece], 0)]]
         got["D"] = rotate(got.get("D"), end, blocks, basis_in, first, cuts[piece + 1] - first)
 
+    cross(1)
+    settle(0)
     x4(0)
-    settle(0)
-    fence(("m3", 1), "a3", "m2")
-    cross(1)
-    fence(("x4", 0), ("m4", 0), ("n1", 0), "a3", "m2")
+    fence(("x5", 1), ("m4", 0), ("n1", 0), ("sum", 0))
+    settle(1)
+    got["n2", 0] = send(got["m4", 0], TO_ENDS)
+    got["R", 0] = pick(("n1", 0), ("sum", 0))
+    fence(("x4", 0), ("m4", 1), ("n1", 1), ("sum", 1), ("R", 0), "a3", "m2")
+    got["n2", 1] = send(got["m4", 1], TO_ENDS)
     x4(1)
-    got["n2", 0] = send(got["m4", 0], TO_ENDS)
+    got["R", 1] = pick(("n1", 1), ("sum", 1))
     last(0)
-    fence(("x4", 1), ("x5", 1), "D", "a3", "m2")
+    fence(("x4", 1), ("n2", 0), ("m4", 0), ("R", 1), "A", "B", "D", "a3", "m2")
     x4(2)
-    settle(1)
-    last(1)
-    fence(("x4", 2), ("m4", 1), ("n2", 0), "A", "B", "D", "a3", "m2")
-    x4(3)
-    got["n2", 1] = send(got["m4", 1], TO_ENDS)
     got["A2"] = swap_narrow(got["A"])
     got["B2"] = swap_narrow(got["B"])
+    got["R", 2] = pick(("n2", 0), ("m4", 0))
+    last(1)
+    fence(("x4", 2), ("n2", 1), ("R", 2), "A2", "B2", "D")
     last(2)
-    fence(("x4", 3), ("n1", 1), ("n2", 1), "A2", "B2", "D")
-    last(3)
     got["D2"] = swap_narrow(got["D"])
 
-    pieces = [[got["n1", p], got["sum", p]] for p in range(2)] + [[got["n2", p], got["m4", p]] for p in range(2)]
+    pieces = [[got["R", p]] for p in range(3)] + [[got["n2", 1], got["m4", 1]]]
     sums = [(got[n], got[n + "2"]) for n in "ABD"]
     return fit(got["order"], end, sums, pieces, got["places"])
 

time: 250 us -> 242 us (0.968)
  waiting for transfers between devices: 89.8 us -> 82.1 us
  other arithmetic: 9.47 us -> 12.1 us
    ppermute x25 -> x24, waiting for transfers between devices: 86.6 us -> 78.9 us  [send(): return lax.ppermute(a, 'wide', perm)]
    select_n x1 -> x4, other arithmetic: 3.68 us -> 6.28 us  [pick(): return jnp.where(at_end, got[a], got[b])]
    ppermute x25 -> x24, starting transfers between devices: 43.7 us -> 41.8 us  [send(): return lax.ppermute(a, 'wide', perm)]
    pallas_call x7 -> x6, Pallas kernels: 75.8 us -> 75.2 us  [rotate(): pl.pallas_call(lambda *refs: rotate_kernel([len(block) for block in block...]
  transfers between devices with their start and end apart: 28 -> 27, of which waited for: 11 -> 12; matrix products, arithmetic and copies ran while one was open for 8% -> 9% of each run, Pallas kernels for 28% -> 28%
where the time goes in v9:
time: 242 us; the launch traced here: 241 us
  Pallas kernels  90.2 us (37%)
  waiting for transfers between devices  82.1 us (34%)
  starting transfers between devices  42.5 us (18%)
  other arithmetic  12.1 us (5%)
  matrix products  9.03 us (4%)
  local copies, waits for them, and re-layouts  4.33 us (2%)
    ppermute x24, waiting for transfers between devices, send(): return lax.ppermute(a, 'wide', perm)  78.9 us
    pallas_call x6, Pallas kernels, rotate(): pl.pallas_call(lambda *refs: rotate_kernel([len(block) for block in block...  75.2 us
    ppermute x24, starting transfers between devices, send(): return lax.ppermute(a, 'wide', perm)  41.8 us
    pallas_call x1, Pallas kernels, fit(): pl.pallas_call(lambda *refs: fit_kernel(len(sums), [len(piece) for piece...  15.1 us
    dot_general x2, matrix products, dot(): return jnp.dot(a, b, preferred_element_type=F32)  9.03 us
    select_n x4, other arithmetic, pick(): return jnp.where(at_end, got[a], got[b])  6.28 us
  transfers between devices with their start and end apart: 27, of which 12 were waited for; matrix products, arithmetic and copies ran while one was open for 9% of the time, Pallas kernels for 28%

profile of v9, /device:TPU:0, one launch (start us, length us, event | category | flops | bytes accessed | tf_op | source)
XLA Modules:
  0.0 240.8 jit_solution(12757662487114039444)
XLA Ops:
  0.0 3.0 %collective-permute-start.1 = (bf16[64,14336]{1,0:T(8,128)(2,1)}, bf16[64,14336]{1,0:T(8,128)(2,1)}, u32[]{:S(2)}, u32[]{:S(2)}) collective-permute-start(bf16[64,14336]{1,0:T(8,128)(2,1)} %refs_1_.1), channel_id=1, source_target_pairs={{0,4},{2,6},{4,0},{6,2},{8,12},{10,14},{12,8},{14,10},{1,5},{3,7},... | collective-permute-start | bytes 5505032 | tf_op jit(solution)/shard_map/ppermute | solution.py:179
  3.0 1.5 collective-permute-start
  5.3 4.5 %fusion.16 = (bf16[512,1024]{1,0:T(8,128)(2,1)}, f32[512,1024]{1,0:T(8,128)}) fusion(bf16[512,1024]{1,0:T(8,128)(2,1)S(1)} %copy-done, bf16[1024,2048]{1,0:T(8,128)(2,1)} %param.7, s32[]{:T(128)S(6)} %select_n.86), kind=kOutput, calls=%fused_computation.26 | convolution fusion | flops 1074266112 | bytes 6291460 | tf_op jit(solution)/shard_map/dot_general | solution.py:16
  9.8 7.2 %collective-permute-start.3 = (bf16[512,1024]{1,0:T(8,128)(2,1)}, bf16[512,1024]{1,0:T(8,128)(2,1)}, u32[]{:S(2)}, u32[]{:S(2)}) collective-permute-start(bf16[512,1024]{1,0:T(8,128)(2,1)} %get-tuple-element.131), channel_id=1, source_target_pairs={{0,4},{2,6},{12,8},{14,10},{1,5},{3,7},{13,9},{15,11},{16,20},{18,... | collective-permute-start | bytes 3145736 | tf_op jit(solution)/shard_map/ppermute | solution.py:179
  18.3 4.5 %fusion.15 = (bf16[512,1024]{1,0:T(8,128)(2,1)}, f32[512,1024]{1,0:T(8,128)}) fusion(bf16[512,1024]{1,0:T(8,128)(2,1)S(1)} %copy-done, bf16[1024,2048]{1,0:T(8,128)(2,1)} %param.7, s32[]{:T(128)S(6)} %select_n.87), kind=kOutput, calls=%fused_computation.25 | convolution fusion | flops 1074266112 | bytes 6291460 | tf_op jit(solution)/shard_map/dot_general | solution.py:16
  22.8 20.9 %collective-permute-done.1.refs_2_ = bf16[64,14336]{1,0:T(8,128)(2,1)} collective-permute-done((bf16[64,14336]{1,0:T(8,128)(2,1)}, bf16[64,14336]{1,0:T(8,128)(2,1)}, u32[]{:S(2)}, u32[]{:S(2)}) %collective-permute-start.1) | collective-permute-done | bytes 1835040 | tf_op jit(solution)/shard_map/ppermute | solution.py:179
  44.8 3.7 %broadcast_select_fusion = bf16[64,14336]{1,0:T(8,128)(2,1)} fusion(bf16[64,14336]{1,0:T(8,128)(2,1)} %collective-permute-done.1.refs_2_, bf16[64,14336]{1,0:T(8,128)(2,1)S(1)} %collective-permute-done.2.refs_2_, pred[]{:T(512)S(6)} %or.3), kind=kLoop, calls=%fused_computation.6 | loop fusion | flops 917504 | bytes 5505025 | tf_op jit(solution)/shard_map/jit(_where)/select_n | solution.py:197
  48.5 1.5 collective-permute-start.4
  52.1 13.0 %collective-permute-done.3 = bf16[512,1024]{1,0:T(8,128)(2,1)} collective-permute-done((bf16[512,1024]{1,0:T(8,128)(2,1)}, bf16[512,1024]{1,0:T(8,128)(2,1)}, u32[]{:S(2)}, u32[]{:S(2)}) %collective-permute-start.3) | collective-permute-done | bytes 1048608 | tf_op jit(solution)/shard_map/ppermute | solution.py:179
  65.1 5.4 %collective-permute-start.7 = (bf16[512,1024]{1,0:T(8,128)(2,1)}, bf16[512,1024]{1,0:T(8,128)(2,1)}, u32[]{:S(2)}, u32[]{:S(2)}) collective-permute-start(bf16[512,1024]{1,0:T(8,128)(2,1)} %get-tuple-element.80), channel_id=1, source_target_pairs={{0,4},{2,6},{12,8},{14,10},{1,5},{3,7},{13,9},{15,11},{16,20},{18,... | collective-permute-start | bytes 3145736 | tf_op jit(solution)/shard_map/ppermute | solution.py:179
  70.4 1.5 copy-done.7
  71.9 24.2 %rotate.6.refs_3_ = f32[192,1792]{1,0:T(8,128)S(1)} custom-call(s32[1]{0:T(128)} %bitcast.14.refs_0_.refs_1_, bf16[64,14336]{1,0:T(8,128)(2,1)S(1)} %copy-done.7, bf16[64,14336]{1,0:T(8,128)(2,1)} %collective-permute-done.1.refs_2_, bf16[64,14336]{1,0:T(8,128)(2,1)} %collective-permute-done.refs_3_, bf16[14336,1792]{1,0:T(8,128)(2,1)} %refs_6_.5), custom_call_target="tpu_custom_call" | custom-call | flops 344064 | bytes 1376256 | tf_op jit(solution)/shard_map/rotate/pallas_call | solution.py:120
  96.2 2.2 convert_add_fusion.1
  99.5 3.3 %collective-permute-start.10 = (bf16[64,14336]{1,0:T(8,128)(2,1)}, bf16[64,14336]{1,0:T(8,128)(2,1)S(1)}, u32[]{:S(2)}, u32[]{:S(2)}) collective-permute-start(bf16[64,14336]{1,0:T(8,128)(2,1)} %collective-permute-done.refs_3_), channel_id=1, source_target_pairs={{0,4},{2,6},{12,8},{14,10},{1,5},{3,7},{13,9},{15,11},{16,20},{18,... | collective-permute-start | bytes 5505032 | tf_op jit(solution)/shard_map/ppermute | solution.py:179
  102.8 3.4 %collective-permute-start.8 = (bf16[64,14336]{1,0:T(8,128)(2,1)}, bf16[64,14336]{1,0:T(8,128)(2,1)S(1)}, u32[]{:S(2)}, u32[]{:S(2)}) collective-permute-start(bf16[64,14336]{1,0:T(8,128)(2,1)} %collective-permute-done.5.refs_1_), channel_id=1, source_target_pairs={{0,2},{2,0},{12,14},{14,12},{1,3},{3,1},{13,15},{15,13},{16,18},{1... | collective-permute-start | bytes 5505032 | tf_op jit(solution)/shard_map/ppermute | solution.py:179
  107.5 11.9 %rotate.7.refs_5_ = f32[128,1792]{1,0:T(8,128)S(1)} custom-call(s32[1]{0:T(128)} %bitcast.14.refs_0_.refs_1_, bf16[64,14336]{1,0:T(8,128)(2,1)} %collective-permute-done.5.refs_1_, bf16[64,14336]{1,0:T(8,128)(2,1)S(1)} %copy-done.3, bf16[64,14336]{1,0:T(8,128)(2,1)} %collective-permute-done.4.refs_3_, bf16[14336,1792]{1,0:T(8,128)(2,1)} %refs_6_.5), custom_call_target="tpu_custom_call" | custom-call | flops 229376 | bytes 917504 | tf_op jit(solution)/shard_map/rotate/pallas_call | solution.py:120
  120.2 1.7 convert_add_fusion
  122.8 11.8 %rotate.8.refs_5_ = f32[128,1792]{1,0:T(8,128)S(1)} custom-call(s32[1]{0:T(128)} %bitcast.14.refs_0_.refs_1_, bf16[64,14336]{1,0:T(8,128)(2,1)} %collective-permute-done.5.refs_1_, bf16[64,14336]{1,0:T(8,128)(2,1)S(1)} %copy-done.3, bf16[64,14336]{1,0:T(8,128)(2,1)} %collective-permute-done.4.refs_3_, bf16[14336,1792]{1,0:T(8,128)(2,1)} %refs_6_.5, ...), custom_call_target="tpu_custom_call" | custom-call | flops 229376 | bytes 917504 | tf_op jit(solution)/shard_map/rotate/pallas_call | solution.py:120
  134.7 6.4 %collective-permute-done.10.refs_4_ = bf16[64,14336]{1,0:T(8,128)(2,1)S(1)} collective-permute-done((bf16[64,14336]{1,0:T(8,128)(2,1)}, bf16[64,14336]{1,0:T(8,128)(2,1)S(1)}, u32[]{:S(2)}, u32[]{:S(2)}) %collective-permute-start.10) | collective-permute-done | bytes 1835040 | tf_op jit(solution)/shard_map/ppermute | solution.py:179
  141.1 4.1 %collective-permute-done.8.refs_3_ = bf16[64,14336]{1,0:T(8,128)(2,1)S(1)} collective-permute-done((bf16[64,14336]{1,0:T(8,128)(2,1)}, bf16[64,14336]{1,0:T(8,128)(2,1)S(1)}, u32[]{:S(2)}, u32[]{:S(2)}) %collective-permute-start.8) | collective-permute-done | bytes 1835040 | tf_op jit(solution)/shard_map/ppermute | solution.py:179
  145.2 2.9 %collective-permute-done.9.refs_1_ = bf16[64,14336]{1,0:T(8,128)(2,1)S(1)} collective-permute-done((bf16[64,14336]{1,0:T(8,128)(2,1)S(1)}, bf16[64,14336]{1,0:T(8,128)(2,1)S(1)}, u32[]{:S(2)}, u32[]{:S(2)}) %collective-permute-start.9) | collective-permute-done | bytes 1835040 | tf_op jit(solution)/shard_map/ppermute | solution.py:179
  152.1 9.5 %collective-permute-done.17 = bf16[512,512]{1,0:T(8,128)(2,1)S(1)} collective-permute-done((bf16[512,512]{1,0:T(8,128)(2,1)S(1)}, bf16[512,512]{1,0:T(8,128)(2,1)S(1)}, u32[]{:S(2)}, u32[]{:S(2)}) %collective-permute-start.17) | collective-permute-done | bytes 524320 | tf_op jit(solution)/shard_map/ppermute | solution.py:179
  164.8 3.4 %collective-permute-done.14.refs_5_ = bf16[64,6144]{1,0:T(8,128)(2,1)S(1)} collective-permute-done((bf16[64,6144]{1,0:T(8,128)(2,1)S(1)}, bf16[64,6144]{1,0:T(8,128)(2,1)S(1)}, u32[]{:S(2)}, u32[]{:S(2)}) %collective-permute-start.14) | collective-permute-done | bytes 786464 | tf_op jit(solution)/shard_map/ppermute | solution.py:179
  168.3 12.3 %collective-permute-done.19 = bf16[512,512]{1,0:T(8,128)(2,1)S(1)} collective-permute-done((bf16[512,512]{1,0:T(8,128)(2,1)S(1)}, bf16[512,512]{1,0:T(8,128)(2,1)S(1)}, u32[]{:S(2)}, u32[]{:S(2)}) %collective-permute-start.19) | collective-permute-done | bytes 524320 | tf_op jit(solution)/shard_map/ppermute | solution.py:179
  182.5 10.9 %rotate.9.refs_7_ = f32[192,1792]{1,0:T(8,128)S(1)} custom-call(s32[1]{0:T(128)} %bitcast.14.refs_0_.refs_1_, bf16[64,14336]{1,0:T(8,128)(2,1)S(1)} %collective-permute-done.9.refs_1_, bf16[64,14336]{1,0:T(8,128)(2,1)S(1)} %collective-permute-done.6.refs_2_, bf16[64,14336]{1,0:T(8,128)(2,1)S(1)} %collective-permute-done.8.refs_3_, ...), custom_call_target="tpu_custom_call" | custom-call | flops 344064 | bytes 1376256 | tf_op jit(solution)/shard_map/rotate/pallas_call | solution.py:120
  194.9 1.5 collective-permute-start.23
  197.0 1.6 collective-permute-start.22
  198.5 9.4 %rotate.10.refs_7_ = f32[192,1792]{1,0:T(8,128)S(1)} custom-call(s32[1]{0:T(128)} %bitcast.14.refs_0_.refs_1_, bf16[64,14336]{1,0:T(8,128)(2,1)S(1)} %collective-permute-done.9.refs_1_, bf16[64,14336]{1,0:T(8,128)(2,1)S(1)} %collective-permute-done.6.refs_2_, bf16[64,14336]{1,0:T(8,128)(2,1)S(1)} %collective-permute-done.8.refs_3_, ...), custom_call_target="tpu_custom_call" | custom-call | flops 344064 | bytes 1376256 | tf_op jit(solution)/shard_map/rotate/pallas_call | solution.py:120
  208.8 4.6 %collective-permute-done.23.refs_12_ = bf16[512,512]{1,0:T(8,128)(2,1)S(1)} collective-permute-done((bf16[512,512]{1,0:T(8,128)(2,1)S(1)}, bf16[512,512]{1,0:T(8,128)(2,1)S(1)}, u32[]{:S(2)}, u32[]{:S(2)}) %collective-permute-start.23) | collective-permute-done | bytes 524320 | tf_op jit(solution)/shard_map/ppermute | solution.py:179
  214.3 7.0 %rotate.11.refs_7_ = f32[192,1792]{1,0:T(8,128)S(1)} custom-call(s32[1]{0:T(128)} %bitcast.14.refs_0_.refs_1_, bf16[64,14336]{1,0:T(8,128)(2,1)S(1)} %collective-permute-done.9.refs_1_, bf16[64,14336]{1,0:T(8,128)(2,1)S(1)} %collective-permute-done.6.refs_2_, bf16[64,14336]{1,0:T(8,128)(2,1)S(1)} %collective-permute-done.8.refs_3_, ...), custom_call_target="tpu_custom_call" | custom-call | flops 344064 | bytes 1376256 | tf_op jit(solution)/shard_map/rotate/pallas_call | solution.py:120
  221.4 3.1 %collective-permute-done.26.refs_8_ = f32[192,1792]{1,0:T(8,128)S(1)} collective-permute-done((f32[192,1792]{1,0:T(8,128)S(1)}, f32[192,1792]{1,0:T(8,128)S(1)}, u32[]{:S(2)}, u32[]{:S(2)}) %collective-permute-start.26) | collective-permute-done | bytes 1376288 | tf_op jit(solution)/shard_map/ppermute | solution.py:141
  225.6 15.1 %fit.1 = f32[1792,2048]{1,0:T(8,128)} custom-call(s32[8]{0:T(128)} %stack.50.refs_0_, s32[1]{0:T(128)} %bitcast.14.refs_0_.refs_1_, s32[4]{0:T(128)} %pad_add_fusion.refs_2_, f32[192,1792]{1,0:T(8,128)} %copy-done.5, f32[192,1792]{1,0:T(8,128)} %copy-done.10, f32[128,1792]{1,0:T(8,128)} %copy-done.6, f32[128,1792]{1,0:T(8,128)} %copy-done.12, ...), custom_call_target="tpu_custom_call" | custom-call | flops 3758096384 | bytes 24117248 | tf_op jit(solution)/shard_map/fit/pallas_call | solution.py:64
  (76 shorter events, 23.3 us)
Async XLA Ops:
  0.0 43.8 %collective-permute-start.1 = (bf16[64,14336]{1,0:T(8,128)(2,1)}, bf16[64,14336]{1,0:T(8,128)(2,1)}, u32[]{:S(2)}, u32[]{:S(2)}) collective-permute-start(bf16[64,14336]{1,0:T(8,128)(2,1)} %refs_1_.1), channel_id=1, source_target_pairs={{0,4},{2,6},{4,0},{6,2},{8,12},{10,14},{12,8},{14,10},{1,5},{3,7},... | collective-permute-start | bytes 5505032 | tf_op jit(solution)/shard_map/ppermute | solution.py:179
  3.0 41.8 %collective-permute-start = (bf16[64,14336]{1,0:T(8,128)(2,1)}, bf16[64,14336]{1,0:T(8,128)(2,1)}, u32[]{:S(2)}, u32[]{:S(2)}) collective-permute-start(bf16[64,14336]{1,0:T(8,128)(2,1)} %refs_1_.1), channel_id=1, source_target_pairs={{0,2},{2,0},{4,6},{6,4},{8,10},{10,8},{12,14},{14,12},{1,3},{3,1},... | collective-permute-start | bytes 5505032 | tf_op jit(solution)/shard_map/ppermute | solution.py:179
  4.5 40.3 %collective-permute-start.2 = (bf16[64,14336]{1,0:T(8,128)(2,1)}, bf16[64,14336]{1,0:T(8,128)(2,1)S(1)}, u32[]{:S(2)}, u32[]{:S(2)}) collective-permute-start(bf16[64,14336]{1,0:T(8,128)(2,1)} %refs_1_.1), channel_id=1, source_target_pairs={{4,8},{6,10},{8,4},{10,6},{5,9},{7,11},{9,5},{11,7},{20,24},{22,26... | collective-permute-start | bytes 5505032 | tf_op jit(solution)/shard_map/ppermute | solution.py:179
  9.8 55.2 %collective-permute-start.3 = (bf16[512,1024]{1,0:T(8,128)(2,1)}, bf16[512,1024]{1,0:T(8,128)(2,1)}, u32[]{:S(2)}, u32[]{:S(2)}) collective-permute-start(bf16[512,1024]{1,0:T(8,128)(2,1)} %get-tuple-element.131), channel_id=1, source_target_pairs={{0,4},{2,6},{12,8},{14,10},{1,5},{3,7},{13,9},{15,11},{16,20},{18,... | collective-permute-start | bytes 3145736 | tf_op jit(solution)/shard_map/ppermute | solution.py:179
  48.5 50.0 %collective-permute-start.4 = (bf16[64,14336]{1,0:T(8,128)(2,1)}, bf16[64,14336]{1,0:T(8,128)(2,1)}, u32[]{:S(2)}, u32[]{:S(2)}) collective-permute-start(bf16[64,14336]{1,0:T(8,128)(2,1)} %broadcast_select_fusion), channel_id=1, source_target_pairs={{0,2},{2,0},{4,6},{6,4},{8,10},{10,8},{12,14},{14,12},{1,3},{3,1},... | collective-permute-start | bytes 5505032 | tf_op jit(solution)/shard_map/ppermute | solution.py:179
  50.0 48.6 %collective-permute-start.6 = (bf16[64,14336]{1,0:T(8,128)(2,1)}, bf16[64,14336]{1,0:T(8,128)(2,1)S(1)}, u32[]{:S(2)}, u32[]{:S(2)}) collective-permute-start(bf16[64,14336]{1,0:T(8,128)(2,1)} %collective-permute-done.1.refs_2_), channel_id=1, source_target_pairs={{4,8},{6,10},{8,4},{10,6},{5,9},{7,11},{9,5},{11,7},{20,24},{22,26... | collective-permute-start | bytes 5505032 | tf_op jit(solution)/shard_map/ppermute | solution.py:179
  50.8 47.8 %collective-permute-start.5 = (bf16[64,14336]{1,0:T(8,128)(2,1)}, bf16[64,14336]{1,0:T(8,128)(2,1)}, u32[]{:S(2)}, u32[]{:S(2)}) collective-permute-start(bf16[64,14336]{1,0:T(8,128)(2,1)} %copy-done.2), channel_id=1, source_target_pairs={{4,0},{6,2},{8,12},{10,14},{5,1},{7,3},{9,13},{11,15},{20,16},{22,... | collective-permute-start | bytes 5505032 | tf_op jit(solution)/shard_map/ppermute | solution.py:179
  65.1 33.5 %collective-permute-start.7 = (bf16[512,1024]{1,0:T(8,128)(2,1)}, bf16[512,1024]{1,0:T(8,128)(2,1)}, u32[]{:S(2)}, u32[]{:S(2)}) collective-permute-start(bf16[512,1024]{1,0:T(8,128)(2,1)} %get-tuple-element.80), channel_id=1, source_target_pairs={{0,4},{2,6},{12,8},{14,10},{1,5},{3,7},{13,9},{15,11},{16,20},{18,... | collective-permute-start | bytes 3145736 | tf_op jit(solution)/shard_map/ppermute | solution.py:179
  71.9 24.2 %copy-start.8 = (f32[512,1024]{1,0:T(8,128)S(1)}, f32[512,1024]{1,0:T(8,128)}, u32[]{:S(2)}) copy-start(f32[512,1024]{1,0:T(8,128)} %get-tuple-element.77) | copy-start | bytes 6291460
  96.2 98.7 %copy-start.5 = (f32[192,1792]{1,0:T(8,128)}, f32[192,1792]{1,0:T(8,128)S(1)}, u32[]{:S(2)}) copy-start(f32[192,1792]{1,0:T(8,128)S(1)} %rotate.6.refs_3_) | copy-start | bytes 4128772
  98.6 21.6 %copy-start.9 = (f32[512,1024]{1,0:T(8,128)S(1)}, f32[512,1024]{1,0:T(8,128)}, u32[]{:S(2)}) copy-start(f32[512,1024]{1,0:T(8,128)} %get-tuple-element.85) | copy-start | bytes 6291460
  98.6 23.2 %collective-permute-start.11 = (f32[512,512]{1,0:T(8,128)S(1)}, f32[512,512]{1,0:T(8,128)S(1)}, u32[]{:S(2)}, u32[]{:S(2)}) collective-permute-start(f32[512,512]{1,0:T(8,128)S(1)} %get-tuple-element.84), channel_id=1, source_target_pairs={{4,8},{6,10},{8,4},{10,6},{5,9},{7,11},{9,5},{11,7},{20,24},{22,26... | collective-permute-start | bytes 3145736 | tf_op jit(solution)/shard_map/ppermute | solution.py:179
  99.5 41.6 %collective-permute-start.10 = (bf16[64,14336]{1,0:T(8,128)(2,1)}, bf16[64,14336]{1,0:T(8,128)(2,1)S(1)}, u32[]{:S(2)}, u32[]{:S(2)}) collective-permute-start(bf16[64,14336]{1,0:T(8,128)(2,1)} %collective-permute-done.refs_3_), channel_id=1, source_target_pairs={{0,4},{2,6},{12,8},{14,10},{1,5},{3,7},{13,9},{15,11},{16,20},{18,... | collective-permute-start | bytes 5505032 | tf_op jit(solution)/shard_map/ppermute | solution.py:179
  102.8 42.4 %collective-permute-start.8 = (bf16[64,14336]{1,0:T(8,128)(2,1)}, bf16[64,14336]{1,0:T(8,128)(2,1)S(1)}, u32[]{:S(2)}, u32[]{:S(2)}) collective-permute-start(bf16[64,14336]{1,0:T(8,128)(2,1)} %collective-permute-done.5.refs_1_), channel_id=1, source_target_pairs={{0,2},{2,0},{12,14},{14,12},{1,3},{3,1},{13,15},{15,13},{16,18},{1... | collective-permute-start | bytes 5505032 | tf_op jit(solution)/shard_map/ppermute | solution.py:179
  106.2 41.9 %collective-permute-start.9 = (bf16[64,14336]{1,0:T(8,128)(2,1)S(1)}, bf16[64,14336]{1,0:T(8,128)(2,1)S(1)}, u32[]{:S(2)}, u32[]{:S(2)}) collective-permute-start(bf16[64,14336]{1,0:T(8,128)(2,1)S(1)} %collective-permute-done.6.refs_2_), channel_id=1, source_target_pairs={{4,0},{6,2},{8,12},{10,14},{5,1},{7,3},{9,13},{11,15},{20,16},{22,... | collective-permute-start | bytes 5505032 | tf_op jit(solution)/shard_map/ppermute | solution.py:179
  119.4 15.3 %collective-permute-start.13 = (f32[512,512]{1,0:T(8,128)S(1)}, f32[512,512]{1,0:T(8,128)S(1)}, u32[]{:S(2)}, u32[]{:S(2)}) collective-permute-start(f32[512,512]{1,0:T(8,128)S(1)} %get-tuple-element.90), channel_id=1, source_target_pairs={{4,8},{6,10},{8,4},{10,6},{5,9},{7,11},{9,5},{11,7},{20,24},{22,26... | collective-permute-start | bytes 3145736 | tf_op jit(solution)/shard_map/ppermute | solution.py:179
  122.1 12.6 %collective-permute-start.12 = (bf16[512,512]{1,0:T(8,128)(2,1)S(1)}, bf16[512,512]{1,0:T(8,128)(2,1)S(1)}, u32[]{:S(2)}, u32[]{:S(2)}) collective-permute-start(bf16[512,512]{1,0:T(8,128)(2,1)S(1)} %fusion.10), channel_id=1, source_target_pairs={{4,6},{6,4},{8,10},{10,8},{5,7},{7,5},{9,11},{11,9},{20,22},{22,20... | collective-permute-start | bytes 1572872 | tf_op jit(solution)/shard_map/ppermute | solution.py:179
  134.7 61.7 %copy-start.6 = (f32[128,1792]{1,0:T(8,128)}, f32[128,1792]{1,0:T(8,128)S(1)}, u32[]{:S(2)}) copy-start(f32[128,1792]{1,0:T(8,128)S(1)} %rotate.8.refs_5_) | copy-start | bytes 2752516
  148.7 12.9 %collective-permute-start.17 = (bf16[512,512]{1,0:T(8,128)(2,1)S(1)}, bf16[512,512]{1,0:T(8,128)(2,1)S(1)}, u32[]{:S(2)}, u32[]{:S(2)}) collective-permute-start(bf16[512,512]{1,0:T(8,128)(2,1)S(1)} %get-tuple-element.97), channel_id=1, source_target_pairs={{4,0},{6,2},{8,12},{10,14},{5,1},{7,3},{9,13},{11,15},{20,16},{22,... | collective-permute-start | bytes 1572872 | tf_op jit(solution)/shard_map/ppermute | solution.py:179
  150.0 11.6 %collective-permute-start.16 = (bf16[512,512]{1,0:T(8,128)(2,1)S(1)}, bf16[512,512]{1,0:T(8,128)(2,1)S(1)}, u32[]{:S(2)}, u32[]{:S(2)}) collective-permute-start(bf16[512,512]{1,0:T(8,128)(2,1)S(1)} %get-tuple-element.97), channel_id=1, source_target_pairs={{4,8},{6,10},{8,4},{10,6},{5,9},{7,11},{9,5},{11,7},{20,24},{22,26... | collective-permute-start | bytes 1572872 | tf_op jit(solution)/shard_map/ppermute | solution.py:179
  150.7 1.4 collective-permute-start.15
  151.5 16.7 %collective-permute-start.14 = (bf16[64,6144]{1,0:T(8,128)(2,1)S(1)}, bf16[64,6144]{1,0:T(8,128)(2,1)S(1)}, u32[]{:S(2)}, u32[]{:S(2)}) collective-permute-start(bf16[64,6144]{1,0:T(8,128)(2,1)S(1)} %slice_select_fusion), channel_id=1, source_target_pairs={{0,2},{2,0},{4,6},{6,4},{8,10},{10,8},{12,14},{14,12},{1,3},{3,1},... | collective-permute-start | bytes 2359304 | tf_op jit(solution)/shard_map/ppermute | solution.py:179
  162.0 18.6 %collective-permute-start.19 = (bf16[512,512]{1,0:T(8,128)(2,1)S(1)}, bf16[512,512]{1,0:T(8,128)(2,1)S(1)}, u32[]{:S(2)}, u32[]{:S(2)}) collective-permute-start(bf16[512,512]{1,0:T(8,128)(2,1)S(1)} %add_convert_fusion), channel_id=1, source_target_pairs={{4,0},{6,2},{8,12},{10,14},{5,1},{7,3},{9,13},{11,15},{20,16},{22,... | collective-permute-start | bytes 1572872 | tf_op jit(solution)/shard_map/ppermute | solution.py:179
  163.3 17.3 %collective-permute-start.18 = (bf16[512,512]{1,0:T(8,128)(2,1)S(1)}, bf16[512,512]{1,0:T(8,128)(2,1)S(1)}, u32[]{:S(2)}, u32[]{:S(2)}) collective-permute-start(bf16[512,512]{1,0:T(8,128)(2,1)S(1)} %add_convert_fusion), channel_id=1, source_target_pairs={{4,8},{6,10},{8,4},{10,6},{5,9},{7,11},{9,5},{11,7},{20,24},{22,26... | collective-permute-start | bytes 1572872 | tf_op jit(solution)/shard_map/ppermute | solution.py:179
  180.7 14.2 %collective-permute-start.20 = (bf16[64,5120]{1,0:T(8,128)(2,1)S(1)}, bf16[64,5120]{1,0:T(8,128)(2,1)S(1)}, u32[]{:S(2)}, u32[]{:S(2)}) collective-permute-start(bf16[64,5120]{1,0:T(8,128)(2,1)S(1)} %slice_select_fusion.1), channel_id=1, source_target_pairs={{0,2},{2,0},{4,6},{6,4},{8,10},{10,8},{12,14},{14,12},{1,3},{3,1},... | collective-permute-start | bytes 1966088 | tf_op jit(solution)/shard_map/ppermute | solution.py:179
  181.3 13.6 %collective-permute-start.21 = (bf16[512,512]{1,0:T(8,128)(2,1)S(1)}, bf16[512,512]{1,0:T(8,128)(2,1)S(1)}, u32[]{:S(2)}, u32[]{:S(2)}) collective-permute-start(bf16[512,512]{1,0:T(8,128)(2,1)S(1)} %collective-permute-done.16), channel_id=1, source_target_pairs={{4,0},{6,2},{8,12},{10,14},{5,1},{7,3},{9,13},{11,15},{20,16},{22,... | collective-permute-start | bytes 1572872 | tf_op jit(solution)/shard_map/ppermute | solution.py:179
  194.9 19.4 %collective-permute-start.24 = (f32[192,1792]{1,0:T(8,128)S(1)}, f32[192,1792]{1,0:T(8,128)S(1)}, u32[]{:S(2)}, u32[]{:S(2)}) collective-permute-start(f32[192,1792]{1,0:T(8,128)S(1)} %rotate.6.refs_3_), channel_id=1, source_target_pairs={{0,1},{1,0},{2,3},{3,2},{4,5},{5,4},{6,7},{7,6},{8,9},{9,8},{10,11... | collective-permute-start | bytes 4128776 | tf_op jit(solution)/shard_map/ppermute | solution.py:141
  194.9 18.5 %collective-permute-start.23 = (bf16[512,512]{1,0:T(8,128)(2,1)S(1)}, bf16[512,512]{1,0:T(8,128)(2,1)S(1)}, u32[]{:S(2)}, u32[]{:S(2)}) collective-permute-start(bf16[512,512]{1,0:T(8,128)(2,1)S(1)} %collective-permute-done.18.refs_13_), channel_id=1, source_target_pairs={{4,0},{6,2},{8,12},{10,14},{5,1},{7,3},{9,13},{11,15},{20,16},{22,... | collective-permute-start | bytes 1572872 | tf_op jit(solution)/shard_map/ppermute | solution.py:179
  196.4 17.1 %collective-permute-start.25 = (f32[128,1792]{1,0:T(8,128)S(1)}, f32[128,1792]{1,0:T(8,128)S(1)}, u32[]{:S(2)}, u32[]{:S(2)}) collective-permute-start(f32[128,1792]{1,0:T(8,128)S(1)} %rotate.8.refs_5_), channel_id=1, source_target_pairs={{0,1},{1,0},{2,3},{3,2},{4,5},{5,4},{6,7},{7,6},{8,9},{9,8},{10,11... | collective-permute-start | bytes 2752520 | tf_op jit(solution)/shard_map/ppermute | solution.py:141
  197.0 16.5 %collective-permute-start.22 = (bf16[64,3072]{1,0:T(8,128)(2,1)S(1)}, bf16[64,3072]{1,0:T(8,128)(2,1)S(1)}, u32[]{:S(2)}, u32[]{:S(2)}) collective-permute-start(bf16[64,3072]{1,0:T(8,128)(2,1)S(1)} %slice_select_fusion.2), channel_id=1, source_target_pairs={{0,2},{2,0},{4,6},{6,4},{8,10},{10,8},{12,14},{14,12},{1,3},{3,1},... | collective-permute-start | bytes 1179656 | tf_op jit(solution)/shard_map/ppermute | solution.py:179
  221.3 3.2 %collective-permute-start.26 = (f32[192,1792]{1,0:T(8,128)S(1)}, f32[192,1792]{1,0:T(8,128)S(1)}, u32[]{:S(2)}, u32[]{:S(2)}) collective-permute-start(f32[192,1792]{1,0:T(8,128)S(1)} %rotate.11.refs_7_), channel_id=1, source_target_pairs={{0,1},{1,0},{2,3},{3,2},{4,5},{5,4},{6,7},{7,6},{8,9},{9,8},{10,11... | collective-permute-start | bytes 4128776 | tf_op jit(solution)/shard_map/ppermute | solution.py:141
  225.6 15.1 %copy-start.1 = (bf16[512,1024]{1,0:T(8,128)(2,1)S(1)}, bf16[512,1024]{1,0:T(8,128)(2,1)}, u32[]{:S(2)}) copy-start(bf16[512,1024]{1,0:T(8,128)(2,1)} %param.5) | copy-start | bytes 3145732
  (10 other events, 53.1 us)

commit v10 on v8

--- a/solution.py
+++ b/solution.py
@@ -16,8 +16,8 @@
     return jnp.dot(a, b, preferred_element_type=F32)
 
 
-def fit_kernel(sizes, choices, order_ref, end_ref, place_ref, *refs):
-    sum_refs, refs = refs[: 2 * len(sizes)], refs[2 * len(sizes) :]
+def fit_kernel(counts, choices, order_ref, end_ref, place_ref, *refs):
+    sum_refs, refs = refs[: sum(counts)], refs[sum(counts) :]
     piece_refs, (fit_ref, out_ref, turned_ref, rot_ref) = refs[:-4], refs[-4:]
     rows, ks = out_ref.shape
     size, seq = rows // order_ref.shape[0], rows // EX
@@ -34,14 +34,16 @@
                 out_ref[:, there] = jnp.where(end_ref[0] == 1, piece_refs[at][...], piece_refs[at + 1][...])
             at += choice
 
-    slot = 0
-    for mine_ref, other_ref in zip(sum_refs[::2], sum_refs[1::2]):
-        for at in range(0, mine_ref.shape[0], size):
+    slot, first = 0, 0
+    for count in counts:
+        halves = sum_refs[first : first + count]
+        first += count
+        for at in range(0, halves[0].shape[0], size):
             here = pl.ds(at, size)
             there = pl.ds(pl.multiple_of(order_ref[slot] * size, size), size)
-            rot_ref[there, :] = mine_ref[here, :] + other_ref[here, :]
+            rot_ref[there, :] = sum(ref[here, :] for ref in halves).astype(BF16)
             slot += 1
-    turned_ref[...] = rot_ref[...].T.astype(BF16)
+    turned_ref[...] = rot_ref[...].T
     step = min(512, ks)
     for at in range(0, ks, step):
         total = None
@@ -53,14 +55,14 @@
 
 
 def fit(order, end, sums, pieces, places):
-    rows = sum(mine.shape[0] for mine, _ in sums)
+    rows = sum(halves[0].shape[0] for halves in sums)
     ka = sums[0][0].shape[1]
     ks = sum(piece[0].shape[1] for piece in pieces)
     tile = 256 if ka % 256 == 0 else ka
-    flat = [a for pair in sums for a in pair]
+    flat = [a for halves in sums for a in halves]
     outs = [a for piece in pieces for a in piece]
     return pl.pallas_call(
-        lambda *refs: fit_kernel([pair[0].shape[0] for pair in sums], [len(piece) for piece in pieces], *refs),
+        lambda *refs: fit_kernel([len(halves) for halves in sums], [len(piece) for piece in pieces], *refs),
         out_shape=jax.ShapeDtypeStruct((ka, ks), F32),
         grid_spec=pltpu.PrefetchScalarGridSpec(
             num_scalar_prefetch=3,
@@ -71,7 +73,7 @@
             scratch_shapes=[
                 pltpu.VMEM((rows, ks), BF16),
                 pltpu.VMEM((tile, rows), BF16),
-                pltpu.VMEM((rows, tile), F32),
+                pltpu.VMEM((rows, tile), BF16),
             ],
         ),
         compiler_params=pltpu.CompilerParams(vmem_limit_bytes=56 << 20),
@@ -84,7 +86,7 @@
 
 def rotate_kernel(choices, end_ref, *refs):
     blocks = refs[: sum(choices)]
-    basis_ref, *before, sum_ref, rows_ref = refs[sum(choices) :]
+    left_ref, right_ref, *before, sum_ref, rows_ref = refs[sum(choices) :]
     size = blocks[0].shape[0]
     at = 0
     for i, choice in enumerate(choices):
@@ -99,7 +101,9 @@
     def _():
         sum_ref[...] = before[0][...] if before else jnp.zeros_like(sum_ref)
 
-    sum_ref[...] += dot(rows_ref[...], basis_ref[...])
+    half = left_ref.shape[1]
+    sum_ref[:, :half] += dot(rows_ref[...], left_ref[...])
+    sum_ref[:, half:] += dot(rows_ref[...], right_ref[...])
 
 
 def rotate(before, end, blocks, basis, first, steps):
@@ -114,7 +118,7 @@
                 pl.BlockSpec((size, DEEP), lambda k, e, used=used, skip=skip: (0, (k + skip) * used(e)))
             )
     whole = pl.BlockSpec((rows, ka), lambda k, e: (0, 0))
-    arrays = [a for a, _ in flat] + [basis] + ([] if before is None else [before])
+    arrays = [a for a, _ in flat] + [basis, basis] + ([] if before is None else [before])
     return pl.pallas_call(
         lambda *refs: rotate_kernel([len(block) for block in blocks], *refs),
         out_shape=jax.ShapeDtypeStruct((rows, ka), F32),
@@ -122,7 +126,7 @@
             num_scalar_prefetch=1,
             grid=(steps,),
             in_specs=specs
-            + [pl.BlockSpec((DEEP, ka), lambda k, e: (first + k, 0))]
+            + [pl.BlockSpec((DEEP, ka // 2), lambda k, e, side=side: (first + k, side)) for side in range(2)]
             + ([] if before is None else [whole]),
             out_specs=whole,
             scratch_shapes=[pltpu.VMEM((rows, DEEP), BF16)],
@@ -184,7 +188,7 @@
     end = at_end.astype(jnp.int32).reshape(1)
     half = (z >= 2).astype(jnp.int32)
     steps = inputs.shape[1] // DEEP
-    cuts = [0, 4 * steps // 14, 8 * steps // 14, 12 * steps // 14, steps]
+    cuts = [0, 4 * steps // 14, 9 * steps // 14, steps]
     part = basis_out.shape[1] // 4
     got = {"own": inputs}
 
@@ -208,7 +212,7 @@
     flip = jnp.where(z >= 2, 3, 0)
     line = lambda a, b: jnp.where(at_end, a, b) ^ flip
     mine, other = (lambda a, b: line(a, b) * PAIR + x), (lambda a, b: line(a, b) * PAIR + 1 - x)
-    order = [mine(0, 1), mine(1, 0), other(0, 1), mine(2, 2), other(1, 2), mine(3, 3), other(2, 0), other(3, 3)]
+    order = [mine(0, 1), mine(1, 0), other(0, 1), mine(2, 2), other(1, 2), mine(3, 3), other(2, 3), other(3, 0)]
     got["order"] = jnp.stack(order).astype(jnp.int32)
     places = [2 * half, 2 * half + 1, 2 - 2 * half, 3 - 2 * half]
     got["places"] = jnp.stack(places).astype(jnp.int32)
@@ -221,9 +225,8 @@
     got["keep"] = dot(deltas, columns(basis_out, half))
     got["keep16"] = got["keep"].astype(BF16)
     fence("x1", "a1", "m1", "give", "keep", "keep16", "order", "places")
-    got["pick"] = pick("a1", "m1")
-    fence("pick", "a1", "m1", "x1")
-    got["x2"] = send(got["pick"], ACROSS)
+    got["x2"] = send(got["a1"], ACROSS_ENDS)
+    got["x2", "m"] = send(got["m1"], ACROSS_MIDDLE)
     got["a2"] = send(got["m1"], TO_ENDS)
     got["m2"] = send(got["a1"], MIDDLE)
     fence(("r1", 0), "x1", "give", "keep16")
@@ -231,60 +234,67 @@
     got["give"] += got["r1", 0].astype(F32)
     for p in range(2):
         got["give", p] = got["give"][:, p * part : (p + 1) * part]
+    fence(("give", 0), ("give", 1), "x1")
     got["A"] = turn(None, [["own"], ["a1"], ["x1"]], 0, steps)
-    fence("x1", "x2", "a2", "m2", ("give", 0), ("give", 1), "keep", ("r1", 1), "A")
+    fence("x1", "x2", ("x2", "m"), "a2", "m2", ("give", 0), ("give", 1), "keep", ("r1", 1), "A")
     got["x3"] = send(got["a2"], ACROSS_ENDS)
+    got["x3", "m"] = send(got["m2"], ACROSS_MIDDLE)
     got["a3"] = send(got["m2"], TO_ENDS)
-    for p in range(2):
-        got["m3", p] = send(got["give", p], MIDDLE)
+    got["m3", 0] = send(got["give", 0], MIDDLE)
     got["e"] = send(got["x1"], FROM_ENDS)
     got["keep"] += got["r1", 1].astype(F32)
     some = steps // 2
-    got["B"] = turn(None, [["a2", "m1"], ["x2"]], 0, some)
-    fence(("m3", 0), "keep", "B")
+    second = [["a2", "m1"], ["x2", ("x2", "m")]]
+    got["B"] = turn(None, second, 0, some)
+    fence(("m3", 0), ("give", 1), "keep", "B")
+    got["m3", 1] = send(got["give", 1], MIDDLE)
+    got["B"] = turn(got["B"], second, some, steps - some)
+    fence("x3", "B")
+    fence(("x3", "m"), "a3", "e", "A", "B", ("m3", 0))
+
+    def x4(piece):
+        got["x4", piece] = send(got["a3"][:, cuts[piece] * DEEP : cuts[piece + 1] * DEEP], ACROSS_ENDS)
+
+    def last(piece):
+        first = cuts[piece]
+        blocks = [["a3", "m2"], ["x3", ("x3", "m")]]
+        blocks = [[(got[n], first) for n in b] for b in blocks] + [[(got["x4", piece], 0), (got["e"], first)]]
+        got["D"] = rotate(got.get("D"), end, blocks, basis_in, first, cuts[piece + 1] - first)
 
     def cross(p):
         got["keep", p] = got["keep"][:, p * part : (p + 1) * part] + got["m3", p]
         got["x5", p] = send(got["keep", p].astype(BF16), ACROSS_MIDDLE)
 
+    x4(0)
     cross(0)
-    got["B"] = turn(got["B"], [["a2", "m1"], ["x2"]], some, steps - some)
-    fence("x3", "a3", "e", ("x5", 0), "B")
-
-    def x4(piece):
-        here = slice(cuts[piece] * DEEP, cuts[piece + 1] * DEEP)
-        got["x4", piece] = send(jnp.where(at_end, got["a3"][:, here], got["m2"][:, here]), ACROSS)
-
-    def last(piece):
-        first = cuts[piece]
-        blocks = [[(got["a3"], first), (got["m2"], first)], [(got["x3"], first), (got["e"], first)], [(got["x4", piece], 0)]]
-        got["D"] = rotate(got.get("D"), end, blocks, basis_in, first, cuts[piece + 1] - first)
-
-    x4(0)
+    fence(("m3", 1), "A", "B")
+    cross(1)
+    fence(("x4", 0), ("x5", 0), "a3")
+    x4(1)
     settle(0)
-    fence(("m3", 1), "a3", "m2")
-    cross(1)
-    fence(("x4", 0), ("m4", 0), ("n1", 0), "a3", "m2")
-    x4(1)
+    got["A2"] = swap_narrow(got["A"])
+    fence(("x5", 1), ("m4", 0), ("n1", 0), ("sum", 0), "A2", ("x4", 0))
+    settle(1)
     got["n2", 0] = send(got["m4", 0], TO_ENDS)
+    got["B2"] = swap_narrow(got["B"])
+    got["A"] = (got["A"] + got["A2"]).astype(BF16)
+    got["R", 0] = pick(("n1", 0), ("sum", 0))
     last(0)
-    fence(("x4", 1), ("x5", 1), "D", "a3", "m2")
+    fence(("x4", 1), "A", ("R", 0), "B2", "D", "a3")
     x4(2)
-    settle(1)
+    fence(("m4", 1), ("n1", 1), ("sum", 1), ("x4", 1))
+    got["B"] = (got["B"] + got["B2"]).astype(BF16)
+    got["R", 1] = pick(("n1", 1), ("sum", 1))
     last(1)
-    fence(("x4", 2), ("m4", 1), ("n2", 0), "A", "B", "D", "a3", "m2")
-    x4(3)
+    fence(("x4", 2), ("n2", 0), ("m4", 0), ("R", 1), "B", "D")
     got["n2", 1] = send(got["m4", 1], TO_ENDS)
-    got["A2"] = swap_narrow(got["A"])
-    got["B2"] = swap_narrow(got["B"])
+    got["R", 2] = pick(("n2", 0), ("m4", 0))
     last(2)
-    fence(("x4", 3), ("n1", 1), ("n2", 1), "A2", "B2", "D")
-    last(3)
+    fence(("n2", 1), ("R", 2), "D")
     got["D2"] = swap_narrow(got["D"])
 
-    pieces = [[got["n1", p], got["sum", p]] for p in range(2)] + [[got["n2", p], got["m4", p]] for p in range(2)]
-    sums = [(got[n], got[n + "2"]) for n in "ABD"]
-    return fit(got["order"], end, sums, pieces, got["places"])
+    pieces = [[got["R", p]] for p in range(3)] + [[got["n2", 1], got["m4", 1]]]
+    return fit(got["order"], end, [[got["A"]], [got["B"]], [got["D"], got["D2"]]], pieces, got["places"])
 
 
 def solution(mesh):

time: 250 us -> 241 us (0.964)
  waiting for transfers between devices: 89.8 us -> 71.6 us
  starting transfers between devices: 44.2 us -> 54 us
    ppermute x25 -> x26, waiting for transfers between devices: 86.6 us -> 68.5 us  [send(): return lax.ppermute(a, 'wide', perm)]
    ppermute x25 -> x26, starting transfers between devices: 43.7 us -> 53.8 us  [send(): return lax.ppermute(a, 'wide', perm)]
    pallas_call x1, Pallas kernels: 15.5 us -> 12.5 us  [fit(): pl.pallas_call(lambda *refs: fit_kernel([len(halves) for halves in sums],...]
    pallas_call x7 -> x6, Pallas kernels: 75.8 us -> 76.5 us  [rotate(): pl.pallas_call(lambda *refs: rotate_kernel([len(block) for block in block...]
  transfers between devices with their start and end apart: 28 -> 29, of which waited for: 11 -> 10; matrix products, arithmetic and copies ran while one was open for 8% -> 8% of each run, Pallas kernels for 28% -> 32%
where the time goes in v10:
time: 241 us; the launch traced here: 240 us
  Pallas kernels  89 us (37%)
  waiting for transfers between devices  71.6 us (30%)
  starting transfers between devices  54 us (22%)
  other arithmetic  10.3 us (4%)
  matrix products  9.03 us (4%)
  local copies, waits for them, and re-layouts  5.24 us (2%)
    pallas_call x6, Pallas kernels, rotate(): pl.pallas_call(lambda *refs: rotate_kernel([len(block) for block in block...  76.5 us
    ppermute x26, waiting for transfers between devices, send(): return lax.ppermute(a, 'wide', perm)  68.5 us
    ppermute x26, starting transfers between devices, send(): return lax.ppermute(a, 'wide', perm)  53.8 us
    pallas_call x1, Pallas kernels, fit(): pl.pallas_call(lambda *refs: fit_kernel([len(halves) for halves in sums],...  12.5 us
    dot_general x2, matrix products, dot(): return jnp.dot(a, b, preferred_element_type=F32)  9.03 us
  transfers between devices with their start and end apart: 29, of which 10 were waited for; matrix products, arithmetic and copies ran while one was open for 8% of the time, Pallas kernels for 32%

profile of v10, /device:TPU:0, one launch (start us, length us, event | category | flops | bytes accessed | tf_op | source)
XLA Modules:
  0.0 239.6 jit_solution(1082339271262900734)
XLA Ops:
  0.0 2.9 %collective-permute-start = (bf16[64,14336]{1,0:T(8,128)(2,1)}, bf16[64,14336]{1,0:T(8,128)(2,1)S(1)}, u32[]{:S(2)}, u32[]{:S(2)}) collective-permute-start(bf16[64,14336]{1,0:T(8,128)(2,1)} %refs_1_.1), channel_id=1, source_target_pairs={{0,2},{2,0},{4,6},{6,4},{8,10},{10,8},{12,14},{14,12},{1,3},{3,1},... | collective-permute-start | bytes 5505032 | tf_op jit(solution)/shard_map/ppermute | solution.py:181
  2.9 1.6 collective-permute-start.1
  4.5 1.9 collective-permute-start.2
  6.4 4.5 %fusion.16 = (bf16[512,1024]{1,0:T(8,128)(2,1)}, f32[512,1024]{1,0:T(8,128)}) fusion(bf16[512,1024]{1,0:T(8,128)(2,1)S(1)} %copy-done, bf16[1024,2048]{1,0:T(8,128)(2,1)} %param.7, s32[]{:T(128)S(6)} %select_n.56), kind=kOutput, calls=%fused_computation.24 | convolution fusion | flops 1074266112 | bytes 6291460 | tf_op jit(solution)/shard_map/dot_general | solution.py:16
  10.9 6.1 %collective-permute-start.3 = (bf16[512,1024]{1,0:T(8,128)(2,1)}, bf16[512,1024]{1,0:T(8,128)(2,1)}, u32[]{:S(2)}, u32[]{:S(2)}) collective-permute-start(bf16[512,1024]{1,0:T(8,128)(2,1)} %get-tuple-element.147), channel_id=1, source_target_pairs={{0,4},{2,6},{12,8},{14,10},{1,5},{3,7},{13,9},{15,11},{16,20},{18,... | collective-permute-start | bytes 3145736 | tf_op jit(solution)/shard_map/ppermute | solution.py:181
  18.3 4.5 %fusion.15 = (bf16[512,1024]{1,0:T(8,128)(2,1)}, f32[512,1024]{1,0:T(8,128)}) fusion(bf16[512,1024]{1,0:T(8,128)(2,1)S(1)} %copy-done, bf16[1024,2048]{1,0:T(8,128)(2,1)} %param.7, s32[]{:T(128)S(6)} %select_n.57), kind=kOutput, calls=%fused_computation.23 | convolution fusion | flops 1074266112 | bytes 6291460 | tf_op jit(solution)/shard_map/dot_general | solution.py:16
  22.8 20.4 %collective-permute-done.refs_3_ = bf16[64,14336]{1,0:T(8,128)(2,1)S(1)} collective-permute-done((bf16[64,14336]{1,0:T(8,128)(2,1)}, bf16[64,14336]{1,0:T(8,128)(2,1)S(1)}, u32[]{:S(2)}, u32[]{:S(2)}) %collective-permute-start) | collective-permute-done | bytes 1835040 | tf_op jit(solution)/shard_map/ppermute | solution.py:181
  43.2 1.3 copy-done.4
  45.3 2.8 %collective-permute-start.4 = (bf16[64,14336]{1,0:T(8,128)(2,1)}, bf16[64,14336]{1,0:T(8,128)(2,1)}, u32[]{:S(2)}, u32[]{:S(2)}) collective-permute-start(bf16[64,14336]{1,0:T(8,128)(2,1)} %collective-permute-done.1.refs_2_), channel_id=1, source_target_pairs={{0,2},{2,0},{12,14},{14,12},{1,3},{3,1},{13,15},{15,13},{16,18},{1... | collective-permute-start | bytes 5505032 | tf_op jit(solution)/shard_map/ppermute | solution.py:181
  48.1 1.9 collective-permute-start.5
  52.1 14.2 %collective-permute-done.3 = bf16[512,1024]{1,0:T(8,128)(2,1)} collective-permute-done((bf16[512,1024]{1,0:T(8,128)(2,1)}, bf16[512,1024]{1,0:T(8,128)(2,1)}, u32[]{:S(2)}, u32[]{:S(2)}) %collective-permute-start.3) | collective-permute-done | bytes 1048608 | tf_op jit(solution)/shard_map/ppermute | solution.py:181
  66.3 5.4 %collective-permute-start.8 = (bf16[512,1024]{1,0:T(8,128)(2,1)}, bf16[512,1024]{1,0:T(8,128)(2,1)}, u32[]{:S(2)}, u32[]{:S(2)}) collective-permute-start(bf16[512,1024]{1,0:T(8,128)(2,1)} %get-tuple-element.87), channel_id=1, source_target_pairs={{0,4},{2,6},{12,8},{14,10},{1,5},{3,7},{13,9},{15,11},{16,20},{18,... | collective-permute-start | bytes 3145736 | tf_op jit(solution)/shard_map/ppermute | solution.py:181
  71.7 2.3 convert_add_fusion.1
  76.0 24.4 %rotate.6 = f32[192,1792]{1,0:T(8,128)S(1)} custom-call(s32[1]{0:T(128)} %bitcast.14.refs_0_.refs_1_, bf16[64,14336]{1,0:T(8,128)(2,1)S(1)} %copy-done.3, bf16[64,14336]{1,0:T(8,128)(2,1)} %collective-permute-done.1.refs_2_, bf16[64,14336]{1,0:T(8,128)(2,1)S(1)} %copy-done.5, bf16[14336,1792]{1,0:T(8,128)(2,1)} %refs_8_.5, bf16[14336,1792]{1,0:T(8,128)(2,1)} %refs_8_.5), custom_call_target="tpu_custom_call" | custom-call | flops 344064 | bytes 1376256 | tf_op jit(solution)/shard_map/rotate/pallas_call | solution.py:122
  100.5 2.6 %collective-permute-start.12 = (bf16[64,14336]{1,0:T(8,128)(2,1)}, bf16[64,14336]{1,0:T(8,128)(2,1)S(1)}, u32[]{:S(2)}, u32[]{:S(2)}) collective-permute-start(bf16[64,14336]{1,0:T(8,128)(2,1)} %collective-permute-done.6.refs_1_), channel_id=1, source_target_pairs={{0,2},{2,0},{12,14},{14,12},{1,3},{3,1},{13,15},{15,13},{16,18},{1... | collective-permute-start | bytes 5505032 | tf_op jit(solution)/shard_map/ppermute | solution.py:181
  104.4 4.8 %collective-permute-start.11 = (bf16[64,14336]{1,0:T(8,128)(2,1)S(1)}, bf16[64,14336]{1,0:T(8,128)(2,1)S(1)}, u32[]{:S(2)}, u32[]{:S(2)}) collective-permute-start(bf16[64,14336]{1,0:T(8,128)(2,1)S(1)} %copy-done.5), channel_id=1, source_target_pairs={{0,4},{2,6},{12,8},{14,10},{1,5},{3,7},{13,9},{15,11},{16,20},{18,... | collective-permute-start | bytes 5505032 | tf_op jit(solution)/shard_map/ppermute | solution.py:181
  110.7 12.3 %rotate.7.refs_7_ = f32[128,1792]{1,0:T(8,128)S(1)} custom-call(s32[1]{0:T(128)} %bitcast.14.refs_0_.refs_1_, bf16[64,14336]{1,0:T(8,128)(2,1)} %collective-permute-done.6.refs_1_, bf16[64,14336]{1,0:T(8,128)(2,1)} %collective-permute-done.2.refs_2_, bf16[64,14336]{1,0:T(8,128)(2,1)} %collective-permute-done.4.refs_3_, ...), custom_call_target="tpu_custom_call" | custom-call | flops 229376 | bytes 917504 | tf_op jit(solution)/shard_map/rotate/pallas_call | solution.py:122
  123.1 1.7 convert_add_fusion
  125.5 12.3 %rotate.8 = f32[128,1792]{1,0:T(8,128)S(1)} custom-call(s32[1]{0:T(128)} %bitcast.14.refs_0_.refs_1_, bf16[64,14336]{1,0:T(8,128)(2,1)} %collective-permute-done.6.refs_1_, bf16[64,14336]{1,0:T(8,128)(2,1)} %collective-permute-done.2.refs_2_, bf16[64,14336]{1,0:T(8,128)(2,1)} %collective-permute-done.4.refs_3_, ...), custom_call_target="tpu_custom_call" | custom-call | flops 229376 | bytes 917504 | tf_op jit(solution)/shard_map/rotate/pallas_call | solution.py:122
  137.8 5.2 %collective-permute-done.12.refs_3_ = bf16[64,14336]{1,0:T(8,128)(2,1)S(1)} collective-permute-done((bf16[64,14336]{1,0:T(8,128)(2,1)}, bf16[64,14336]{1,0:T(8,128)(2,1)S(1)}, u32[]{:S(2)}, u32[]{:S(2)}) %collective-permute-start.12) | collective-permute-done | bytes 1835040 | tf_op jit(solution)/shard_map/ppermute | solution.py:181
  143.0 2.0 collective-permute-done.10.refs_1_
  147.3 3.4 %collective-permute-start.14 = (bf16[64,4096]{1,0:T(8,128)(2,1)S(1)}, bf16[64,4096]{1,0:T(8,128)(2,1)S(1)}, u32[]{:S(2)}, u32[]{:S(2)}) collective-permute-start(bf16[64,4096]{1,0:T(8,128)(2,1)S(1)} %slice.23), channel_id=1, source_target_pairs={{0,2},{2,0},{12,14},{14,12},{1,3},{3,1},{13,15},{15,13},{16,18},{1... | collective-permute-start | bytes 1572872 | tf_op jit(solution)/shard_map/ppermute | solution.py:181
  150.8 9.1 %collective-permute-done.14.refs_5_ = bf16[64,4096]{1,0:T(8,128)(2,1)S(1)} collective-permute-done((bf16[64,4096]{1,0:T(8,128)(2,1)S(1)}, bf16[64,4096]{1,0:T(8,128)(2,1)S(1)}, u32[]{:S(2)}, u32[]{:S(2)}) %collective-permute-start.14) | collective-permute-done | bytes 524320 | tf_op jit(solution)/shard_map/ppermute | solution.py:181
  163.3 3.4 %collective-permute-start.16 = (bf16[64,5120]{1,0:T(8,128)(2,1)S(1)}, bf16[64,5120]{1,0:T(8,128)(2,1)S(1)}, u32[]{:S(2)}, u32[]{:S(2)}) collective-permute-start(bf16[64,5120]{1,0:T(8,128)(2,1)S(1)} %slice.25), channel_id=1, source_target_pairs={{0,2},{2,0},{12,14},{14,12},{1,3},{3,1},{13,15},{15,13},{16,18},{1... | collective-permute-start | bytes 1966088 | tf_op jit(solution)/shard_map/ppermute | solution.py:181
  166.8 13.0 %collective-permute-done.20 = bf16[512,512]{1,0:T(8,128)(2,1)S(1)} collective-permute-done((bf16[512,512]{1,0:T(8,128)(2,1)S(1)}, bf16[512,512]{1,0:T(8,128)(2,1)S(1)}, u32[]{:S(2)}, u32[]{:S(2)}) %collective-permute-start.20) | collective-permute-done | bytes 524320 | tf_op jit(solution)/shard_map/ppermute | solution.py:181
  183.9 7.9 %rotate.9.refs_9_ = f32[192,1792]{1,0:T(8,128)S(1)} custom-call(s32[1]{0:T(128)} %bitcast.14.refs_0_.refs_1_, bf16[64,14336]{1,0:T(8,128)(2,1)S(1)} %collective-permute-done.10.refs_1_, bf16[64,14336]{1,0:T(8,128)(2,1)S(1)} %collective-permute-done.7.refs_2_, bf16[64,14336]{1,0:T(8,128)(2,1)S(1)} %collective-permute-done.12.refs_3_, ...), custom_call_target="tpu_custom_call" | custom-call | flops 344064 | bytes 1376256 | tf_op jit(solution)/shard_map/rotate/pallas_call | solution.py:122
  191.9 3.6 %collective-permute-start.23 = (bf16[64,5120]{1,0:T(8,128)(2,1)S(1)}, bf16[64,5120]{1,0:T(8,128)(2,1)S(1)}, u32[]{:S(2)}, u32[]{:S(2)}) collective-permute-start(bf16[64,5120]{1,0:T(8,128)(2,1)S(1)} %slice.27), channel_id=1, source_target_pairs={{0,2},{2,0},{12,14},{14,12},{1,3},{3,1},{13,15},{15,13},{16,18},{1... | collective-permute-start | bytes 1966088 | tf_op jit(solution)/shard_map/ppermute | solution.py:181
  199.0 9.8 %rotate.10.refs_9_ = f32[192,1792]{1,0:T(8,128)S(1)} custom-call(s32[1]{0:T(128)} %bitcast.14.refs_0_.refs_1_, bf16[64,14336]{1,0:T(8,128)(2,1)S(1)} %collective-permute-done.10.refs_1_, bf16[64,14336]{1,0:T(8,128)(2,1)S(1)} %collective-permute-done.7.refs_2_, bf16[64,14336]{1,0:T(8,128)(2,1)S(1)} %collective-permute-done.12.refs_3_, ...), custom_call_target="tpu_custom_call" | custom-call | flops 344064 | bytes 1376256 | tf_op jit(solution)/shard_map/rotate/pallas_call | solution.py:122
  209.7 2.6 %collective-permute-done.24 = bf16[512,512]{1,0:T(8,128)(2,1)S(1)} collective-permute-done((bf16[512,512]{1,0:T(8,128)(2,1)S(1)}, bf16[512,512]{1,0:T(8,128)(2,1)S(1)}, u32[]{:S(2)}, u32[]{:S(2)}) %collective-permute-start.24) | collective-permute-done | bytes 524320 | tf_op jit(solution)/shard_map/ppermute | solution.py:181
  212.2 9.7 %rotate.11.refs_5_ = f32[192,1792]{1,0:T(8,128)S(1)} custom-call(s32[1]{0:T(128)} %bitcast.14.refs_0_.refs_1_, bf16[64,14336]{1,0:T(8,128)(2,1)S(1)} %collective-permute-done.10.refs_1_, bf16[64,14336]{1,0:T(8,128)(2,1)S(1)} %collective-permute-done.7.refs_2_, bf16[64,14336]{1,0:T(8,128)(2,1)S(1)} %collective-permute-done.12.refs_3_, ...), custom_call_target="tpu_custom_call" | custom-call | flops 344064 | bytes 1376256 | tf_op jit(solution)/shard_map/rotate/pallas_call | solution.py:122
  222.9 3.1 %collective-permute-done.28.refs_6_ = f32[192,1792]{1,0:T(8,128)S(1)} collective-permute-done((f32[192,1792]{1,0:T(8,128)S(1)}, f32[192,1792]{1,0:T(8,128)S(1)}, u32[]{:S(2)}, u32[]{:S(2)}) %collective-permute-start.28) | collective-permute-done | bytes 1376288 | tf_op jit(solution)/shard_map/ppermute | solution.py:143
  227.1 12.5 %fit.1 = f32[1792,2048]{1,0:T(8,128)} custom-call(s32[8]{0:T(128)} %stack.50.refs_0_, s32[1]{0:T(128)} %bitcast.14.refs_0_.refs_1_, s32[4]{0:T(128)} %pad_add_fusion.refs_2_, bf16[192,1792]{1,0:T(8,128)(2,1)} %add_convert_fusion.refs_3_, bf16[128,1792]{1,0:T(8,128)(2,1)} %add_convert_fusion.3.refs_4_, f32[192,1792]{1,0:T(8,128)} %copy-done.2, ...), custom_call_target="tpu_custom_call" | custom-call | flops 3758096384 | bytes 24117248 | tf_op jit(solution)/shard_map/fit/pallas_call | solution.py:64
  (71 shorter events, 26.0 us)
Async XLA Ops:
  0.0 43.2 %collective-permute-start = (bf16[64,14336]{1,0:T(8,128)(2,1)}, bf16[64,14336]{1,0:T(8,128)(2,1)S(1)}, u32[]{:S(2)}, u32[]{:S(2)}) collective-permute-start(bf16[64,14336]{1,0:T(8,128)(2,1)} %refs_1_.1), channel_id=1, source_target_pairs={{0,2},{2,0},{4,6},{6,4},{8,10},{10,8},{12,14},{14,12},{1,3},{3,1},... | collective-permute-start | bytes 5505032 | tf_op jit(solution)/shard_map/ppermute | solution.py:181
  2.9 42.3 %collective-permute-start.1 = (bf16[64,14336]{1,0:T(8,128)(2,1)}, bf16[64,14336]{1,0:T(8,128)(2,1)}, u32[]{:S(2)}, u32[]{:S(2)}) collective-permute-start(bf16[64,14336]{1,0:T(8,128)(2,1)} %refs_1_.1), channel_id=1, source_target_pairs={{0,4},{2,6},{4,0},{6,2},{8,12},{10,14},{12,8},{14,10},{1,5},{3,7},... | collective-permute-start | bytes 5505032 | tf_op jit(solution)/shard_map/ppermute | solution.py:181
  4.5 40.8 %collective-permute-start.2 = (bf16[64,14336]{1,0:T(8,128)(2,1)}, bf16[64,14336]{1,0:T(8,128)(2,1)}, u32[]{:S(2)}, u32[]{:S(2)}) collective-permute-start(bf16[64,14336]{1,0:T(8,128)(2,1)} %refs_1_.1), channel_id=1, source_target_pairs={{4,8},{6,10},{8,4},{10,6},{5,9},{7,11},{9,5},{11,7},{20,24},{22,26... | collective-permute-start | bytes 5505032 | tf_op jit(solution)/shard_map/ppermute | solution.py:181
  10.9 55.4 %collective-permute-start.3 = (bf16[512,1024]{1,0:T(8,128)(2,1)}, bf16[512,1024]{1,0:T(8,128)(2,1)}, u32[]{:S(2)}, u32[]{:S(2)}) collective-permute-start(bf16[512,1024]{1,0:T(8,128)(2,1)} %get-tuple-element.147), channel_id=1, source_target_pairs={{0,4},{2,6},{12,8},{14,10},{1,5},{3,7},{13,9},{15,11},{16,20},{18,... | collective-permute-start | bytes 3145736 | tf_op jit(solution)/shard_map/ppermute | solution.py:181
  45.3 55.2 %collective-permute-start.4 = (bf16[64,14336]{1,0:T(8,128)(2,1)}, bf16[64,14336]{1,0:T(8,128)(2,1)}, u32[]{:S(2)}, u32[]{:S(2)}) collective-permute-start(bf16[64,14336]{1,0:T(8,128)(2,1)} %collective-permute-done.1.refs_2_), channel_id=1, source_target_pairs={{0,2},{2,0},{12,14},{14,12},{1,3},{3,1},{13,15},{15,13},{16,18},{1... | collective-permute-start | bytes 5505032 | tf_op jit(solution)/shard_map/ppermute | solution.py:181
  48.1 52.3 %collective-permute-start.5 = (bf16[64,14336]{1,0:T(8,128)(2,1)}, bf16[64,14336]{1,0:T(8,128)(2,1)}, u32[]{:S(2)}, u32[]{:S(2)}) collective-permute-start(bf16[64,14336]{1,0:T(8,128)(2,1)} %collective-permute-done.2.refs_2_), channel_id=1, source_target_pairs={{4,6},{6,4},{8,10},{10,8},{5,7},{7,5},{9,11},{11,9},{20,22},{22,20... | collective-permute-start | bytes 5505032 | tf_op jit(solution)/shard_map/ppermute | solution.py:181
  50.1 50.4 %collective-permute-start.6 = (bf16[64,14336]{1,0:T(8,128)(2,1)}, bf16[64,14336]{1,0:T(8,128)(2,1)}, u32[]{:S(2)}, u32[]{:S(2)}) collective-permute-start(bf16[64,14336]{1,0:T(8,128)(2,1)} %collective-permute-done.2.refs_2_), channel_id=1, source_target_pairs={{4,0},{6,2},{8,12},{10,14},{5,1},{7,3},{9,13},{11,15},{20,16},{22,... | collective-permute-start | bytes 5505032 | tf_op jit(solution)/shard_map/ppermute | solution.py:181
  51.3 49.2 %collective-permute-start.7 = (bf16[64,14336]{1,0:T(8,128)(2,1)}, bf16[64,14336]{1,0:T(8,128)(2,1)S(1)}, u32[]{:S(2)}, u32[]{:S(2)}) collective-permute-start(bf16[64,14336]{1,0:T(8,128)(2,1)} %collective-permute-done.1.refs_2_), channel_id=1, source_target_pairs={{4,8},{6,10},{8,4},{10,6},{5,9},{7,11},{9,5},{11,7},{20,24},{22,26... | collective-permute-start | bytes 5505032 | tf_op jit(solution)/shard_map/ppermute | solution.py:181
  66.3 34.2 %collective-permute-start.8 = (bf16[512,1024]{1,0:T(8,128)(2,1)}, bf16[512,1024]{1,0:T(8,128)(2,1)}, u32[]{:S(2)}, u32[]{:S(2)}) collective-permute-start(bf16[512,1024]{1,0:T(8,128)(2,1)} %get-tuple-element.87), channel_id=1, source_target_pairs={{0,4},{2,6},{12,8},{14,10},{1,5},{3,7},{13,9},{15,11},{16,20},{18,... | collective-permute-start | bytes 3145736 | tf_op jit(solution)/shard_map/ppermute | solution.py:181
  100.4 22.6 %copy-start.6 = (f32[512,1024]{1,0:T(8,128)S(1)}, f32[512,1024]{1,0:T(8,128)}, u32[]{:S(2)}) copy-start(f32[512,1024]{1,0:T(8,128)} %get-tuple-element.96) | copy-start | bytes 6291460
  100.5 42.5 %collective-permute-start.12 = (bf16[64,14336]{1,0:T(8,128)(2,1)}, bf16[64,14336]{1,0:T(8,128)(2,1)S(1)}, u32[]{:S(2)}, u32[]{:S(2)}) collective-permute-start(bf16[64,14336]{1,0:T(8,128)(2,1)} %collective-permute-done.6.refs_1_), channel_id=1, source_target_pairs={{0,2},{2,0},{12,14},{14,12},{1,3},{3,1},{13,15},{15,13},{16,18},{1... | collective-permute-start | bytes 5505032 | tf_op jit(solution)/shard_map/ppermute | solution.py:181
  103.1 41.9 %collective-permute-start.10 = (bf16[64,14336]{1,0:T(8,128)(2,1)S(1)}, bf16[64,14336]{1,0:T(8,128)(2,1)S(1)}, u32[]{:S(2)}, u32[]{:S(2)}) collective-permute-start(bf16[64,14336]{1,0:T(8,128)(2,1)S(1)} %collective-permute-done.7.refs_2_), channel_id=1, source_target_pairs={{4,0},{6,2},{8,12},{10,14},{5,1},{7,3},{9,13},{11,15},{20,16},{22,... | collective-permute-start | bytes 5505032 | tf_op jit(solution)/shard_map/ppermute | solution.py:181
  104.4 41.9 %collective-permute-start.11 = (bf16[64,14336]{1,0:T(8,128)(2,1)S(1)}, bf16[64,14336]{1,0:T(8,128)(2,1)S(1)}, u32[]{:S(2)}, u32[]{:S(2)}) collective-permute-start(bf16[64,14336]{1,0:T(8,128)(2,1)S(1)} %copy-done.5), channel_id=1, source_target_pairs={{0,4},{2,6},{12,8},{14,10},{1,5},{3,7},{13,9},{15,11},{16,20},{18,... | collective-permute-start | bytes 5505032 | tf_op jit(solution)/shard_map/ppermute | solution.py:181
  109.2 37.1 %collective-permute-start.9 = (bf16[64,14336]{1,0:T(8,128)(2,1)S(1)}, bf16[64,14336]{1,0:T(8,128)(2,1)S(1)}, u32[]{:S(2)}, u32[]{:S(2)}) collective-permute-start(bf16[64,14336]{1,0:T(8,128)(2,1)S(1)} %collective-permute-done.7.refs_2_), channel_id=1, source_target_pairs={{4,6},{6,4},{8,10},{10,8},{5,7},{7,5},{9,11},{11,9},{20,22},{22,20... | collective-permute-start | bytes 5505032 | tf_op jit(solution)/shard_map/ppermute | solution.py:181
  110.0 14.8 %collective-permute-start.13 = (f32[512,512]{1,0:T(8,128)S(1)}, f32[512,512]{1,0:T(8,128)S(1)}, u32[]{:S(2)}, u32[]{:S(2)}) collective-permute-start(f32[512,512]{1,0:T(8,128)S(1)} %get-tuple-element.94), channel_id=1, source_target_pairs={{4,8},{6,10},{8,4},{10,6},{5,9},{7,11},{9,5},{11,7},{20,24},{22,26... | collective-permute-start | bytes 3145736 | tf_op jit(solution)/shard_map/ppermute | solution.py:181
  124.7 26.0 %collective-permute-start.17 = (f32[512,512]{1,0:T(8,128)S(1)}, f32[512,512]{1,0:T(8,128)S(1)}, u32[]{:S(2)}, u32[]{:S(2)}) collective-permute-start(f32[512,512]{1,0:T(8,128)S(1)} %get-tuple-element.105), channel_id=1, source_target_pairs={{4,8},{6,10},{8,4},{10,6},{5,9},{7,11},{9,5},{11,7},{20,24},{22,26... | collective-permute-start | bytes 3145736 | tf_op jit(solution)/shard_map/ppermute | solution.py:181
  146.5 4.2 %collective-permute-start.15 = (bf16[512,512]{1,0:T(8,128)(2,1)S(1)}, bf16[512,512]{1,0:T(8,128)(2,1)S(1)}, u32[]{:S(2)}, u32[]{:S(2)}) collective-permute-start(bf16[512,512]{1,0:T(8,128)(2,1)S(1)} %fusion.10), channel_id=1, source_target_pairs={{4,6},{6,4},{8,10},{10,8},{5,7},{7,5},{9,11},{11,9},{20,22},{22,20... | collective-permute-start | bytes 1572872 | tf_op jit(solution)/shard_map/ppermute | solution.py:181
  147.3 12.6 %collective-permute-start.14 = (bf16[64,4096]{1,0:T(8,128)(2,1)S(1)}, bf16[64,4096]{1,0:T(8,128)(2,1)S(1)}, u32[]{:S(2)}, u32[]{:S(2)}) collective-permute-start(bf16[64,4096]{1,0:T(8,128)(2,1)S(1)} %slice.23), channel_id=1, source_target_pairs={{0,2},{2,0},{12,14},{14,12},{1,3},{3,1},{13,15},{15,13},{16,18},{1... | collective-permute-start | bytes 1572872 | tf_op jit(solution)/shard_map/ppermute | solution.py:181
  150.7 29.1 %collective-permute-start.21 = (f32[192,1792]{1,0:T(8,128)S(1)}, f32[192,1792]{1,0:T(8,128)S(1)}, u32[]{:S(2)}, u32[]{:S(2)}) collective-permute-start(f32[192,1792]{1,0:T(8,128)S(1)} %rotate.6), channel_id=1, source_target_pairs={{0,1},{1,0},{2,3},{3,2},{4,5},{5,4},{6,7},{7,6},{8,9},{9,8},{10,11... | collective-permute-start | bytes 4128776 | tf_op jit(solution)/shard_map/ppermute | solution.py:143
  160.5 2.8 %collective-permute-start.18 = (bf16[512,512]{1,0:T(8,128)(2,1)S(1)}, bf16[512,512]{1,0:T(8,128)(2,1)S(1)}, u32[]{:S(2)}, u32[]{:S(2)}) collective-permute-start(bf16[512,512]{1,0:T(8,128)(2,1)S(1)} %get-tuple-element.142), channel_id=1, source_target_pairs={{4,6},{6,4},{8,10},{10,8},{5,7},{7,5},{9,11},{11,9},{20,22},{22,20... | collective-permute-start | bytes 1572872 | tf_op jit(solution)/shard_map/ppermute | solution.py:181
  161.2 5.6 %collective-permute-start.19 = (bf16[512,512]{1,0:T(8,128)(2,1)S(1)}, bf16[512,512]{1,0:T(8,128)(2,1)S(1)}, u32[]{:S(2)}, u32[]{:S(2)}) collective-permute-start(bf16[512,512]{1,0:T(8,128)(2,1)S(1)} %get-tuple-element.114), channel_id=1, source_target_pairs={{4,8},{6,10},{8,4},{10,6},{5,9},{7,11},{9,5},{11,7},{20,24},{22,26... | collective-permute-start | bytes 1572872 | tf_op jit(solution)/shard_map/ppermute | solution.py:181
  161.9 17.9 %collective-permute-start.20 = (bf16[512,512]{1,0:T(8,128)(2,1)S(1)}, bf16[512,512]{1,0:T(8,128)(2,1)S(1)}, u32[]{:S(2)}, u32[]{:S(2)}) collective-permute-start(bf16[512,512]{1,0:T(8,128)(2,1)S(1)} %get-tuple-element.114), channel_id=1, source_target_pairs={{4,0},{6,2},{8,12},{10,14},{5,1},{7,3},{9,13},{11,15},{20,16},{22,... | collective-permute-start | bytes 1572872 | tf_op jit(solution)/shard_map/ppermute | solution.py:181
  163.2 28.6 %collective-permute-start.22 = (f32[128,1792]{1,0:T(8,128)S(1)}, f32[128,1792]{1,0:T(8,128)S(1)}, u32[]{:S(2)}, u32[]{:S(2)}) collective-permute-start(f32[128,1792]{1,0:T(8,128)S(1)} %rotate.8), channel_id=1, source_target_pairs={{0,1},{1,0},{2,3},{3,2},{4,5},{5,4},{6,7},{7,6},{8,9},{9,8},{10,11... | collective-permute-start | bytes 2752520 | tf_op jit(solution)/shard_map/ppermute | solution.py:143
  163.3 28.5 %collective-permute-start.16 = (bf16[64,5120]{1,0:T(8,128)(2,1)S(1)}, bf16[64,5120]{1,0:T(8,128)(2,1)S(1)}, u32[]{:S(2)}, u32[]{:S(2)}) collective-permute-start(bf16[64,5120]{1,0:T(8,128)(2,1)S(1)} %slice.25), channel_id=1, source_target_pairs={{0,2},{2,0},{12,14},{14,12},{1,3},{3,1},{13,15},{15,13},{16,18},{1... | collective-permute-start | bytes 1966088 | tf_op jit(solution)/shard_map/ppermute | solution.py:181
  180.1 17.6 %collective-permute-start.25 = (bf16[512,512]{1,0:T(8,128)(2,1)S(1)}, bf16[512,512]{1,0:T(8,128)(2,1)S(1)}, u32[]{:S(2)}, u32[]{:S(2)}) collective-permute-start(bf16[512,512]{1,0:T(8,128)(2,1)S(1)} %add_convert_fusion.1), channel_id=1, source_target_pairs={{4,8},{6,10},{8,4},{10,6},{5,9},{7,11},{9,5},{11,7},{20,24},{22,26... | collective-permute-start | bytes 1572872 | tf_op jit(solution)/shard_map/ppermute | solution.py:181
  180.8 16.9 %collective-permute-start.26 = (bf16[512,512]{1,0:T(8,128)(2,1)S(1)}, bf16[512,512]{1,0:T(8,128)(2,1)S(1)}, u32[]{:S(2)}, u32[]{:S(2)}) collective-permute-start(bf16[512,512]{1,0:T(8,128)(2,1)S(1)} %add_convert_fusion.1), channel_id=1, source_target_pairs={{4,0},{6,2},{8,12},{10,14},{5,1},{7,3},{9,13},{11,15},{20,16},{22,... | collective-permute-start | bytes 1572872 | tf_op jit(solution)/shard_map/ppermute | solution.py:181
  191.9 20.3 %collective-permute-start.23 = (bf16[64,5120]{1,0:T(8,128)(2,1)S(1)}, bf16[64,5120]{1,0:T(8,128)(2,1)S(1)}, u32[]{:S(2)}, u32[]{:S(2)}) collective-permute-start(bf16[64,5120]{1,0:T(8,128)(2,1)S(1)} %slice.27), channel_id=1, source_target_pairs={{0,2},{2,0},{12,14},{14,12},{1,3},{3,1},{13,15},{15,13},{16,18},{1... | collective-permute-start | bytes 1966088 | tf_op jit(solution)/shard_map/ppermute | solution.py:181
  195.5 16.8 %collective-permute-start.24 = (bf16[512,512]{1,0:T(8,128)(2,1)S(1)}, bf16[512,512]{1,0:T(8,128)(2,1)S(1)}, u32[]{:S(2)}, u32[]{:S(2)}) collective-permute-start(bf16[512,512]{1,0:T(8,128)(2,1)S(1)} %collective-permute-done.19), channel_id=1, source_target_pairs={{4,0},{6,2},{8,12},{10,14},{5,1},{7,3},{9,13},{11,15},{20,16},{22,... | collective-permute-start | bytes 1572872 | tf_op jit(solution)/shard_map/ppermute | solution.py:181
  197.7 11.1 %copy-start.8 = (bf16[512,512]{1,0:T(8,128)(2,1)}, bf16[512,512]{1,0:T(8,128)(2,1)S(1)}, u32[]{:S(2)}) copy-start(bf16[512,512]{1,0:T(8,128)(2,1)S(1)} %collective-permute-done.25.refs_11_) | copy-start | bytes 1572868
  197.7 25.2 %collective-permute-start.27 = (bf16[512,512]{1,0:T(8,128)(2,1)S(1)}, bf16[512,512]{1,0:T(8,128)(2,1)S(1)}, u32[]{:S(2)}, u32[]{:S(2)}) collective-permute-start(bf16[512,512]{1,0:T(8,128)(2,1)S(1)} %collective-permute-done.25.refs_11_), channel_id=1, source_target_pairs={{4,0},{6,2},{8,12},{10,14},{5,1},{7,3},{9,13},{11,15},{20,16},{22,... | collective-permute-start | bytes 1572872 | tf_op jit(solution)/shard_map/ppermute | solution.py:181
  222.9 3.1 %collective-permute-start.28 = (f32[192,1792]{1,0:T(8,128)S(1)}, f32[192,1792]{1,0:T(8,128)S(1)}, u32[]{:S(2)}, u32[]{:S(2)}) collective-permute-start(f32[192,1792]{1,0:T(8,128)S(1)} %rotate.11.refs_5_), channel_id=1, source_target_pairs={{0,1},{1,0},{2,3},{3,2},{4,5},{5,4},{6,7},{7,6},{8,9},{9,8},{10,11... | collective-permute-start | bytes 4128776 | tf_op jit(solution)/shard_map/ppermute | solution.py:143
  227.1 12.5 %copy-start.1 = (bf16[512,1024]{1,0:T(8,128)(2,1)S(1)}, bf16[512,1024]{1,0:T(8,128)(2,1)}, u32[]{:S(2)}) copy-start(bf16[512,1024]{1,0:T(8,128)(2,1)} %param.5) | copy-start | bytes 3145732
  (7 other events, 19.6 us)

commit v11 on v10

--- a/solution.py
+++ b/solution.py
@@ -8,7 +8,7 @@
 EX = 2
 LINE, PAIR = 4, 2
 DEEP = 1024
-VMEM = 20 << 20
+VMEM = 22 << 20
 BF16, F32 = jnp.bfloat16, jnp.float32
 
 
@@ -86,7 +86,7 @@
 
 def rotate_kernel(choices, end_ref, *refs):
     blocks = refs[: sum(choices)]
-    left_ref, right_ref, *before, sum_ref, rows_ref = refs[sum(choices) :]
+    basis_ref, *before, sum_ref, rows_ref = refs[sum(choices) :]
     size = blocks[0].shape[0]
     at = 0
     for i, choice in enumerate(choices):
@@ -99,11 +99,14 @@
 
     @pl.when(pl.program_id(0) == 0)
     def _():
-        sum_ref[...] = before[0][...] if before else jnp.zeros_like(sum_ref)
-
-    half = left_ref.shape[1]
-    sum_ref[:, :half] += dot(rows_ref[...], left_ref[...])
-    sum_ref[:, half:] += dot(rows_ref[...], right_ref[...])
+        if not before:
+            sum_ref[...] = jnp.zeros_like(sum_ref)
+        at = 0
+        for ref in before:
+            sum_ref[pl.ds(at, ref.shape[0]), :] = ref[...]
+            at += ref.shape[0]
+
+    sum_ref[...] += dot(rows_ref[...], basis_ref[...])
 
 
 def rotate(before, end, blocks, basis, first, steps):
@@ -118,7 +121,7 @@
                 pl.BlockSpec((size, DEEP), lambda k, e, used=used, skip=skip: (0, (k + skip) * used(e)))
             )
     whole = pl.BlockSpec((rows, ka), lambda k, e: (0, 0))
-    arrays = [a for a, _ in flat] + [basis, basis] + ([] if before is None else [before])
+    arrays = [a for a, _ in flat] + [basis] + before
     return pl.pallas_call(
         lambda *refs: rotate_kernel([len(block) for block in blocks], *refs),
         out_shape=jax.ShapeDtypeStruct((rows, ka), F32),
@@ -126,8 +129,8 @@
             num_scalar_prefetch=1,
             grid=(steps,),
             in_specs=specs
-            + [pl.BlockSpec((DEEP, ka // 2), lambda k, e, side=side: (first + k, side)) for side in range(2)]
-            + ([] if before is None else [whole]),
+            + [pl.BlockSpec((DEEP, ka), lambda k, e: (first + k, 0))]
+            + [pl.BlockSpec(a.shape, lambda k, e: (0, 0)) for a in before],
             out_specs=whole,
             scratch_shapes=[pltpu.VMEM((rows, DEEP), BF16)],
         ),
@@ -188,7 +191,7 @@
     end = at_end.astype(jnp.int32).reshape(1)
     half = (z >= 2).astype(jnp.int32)
     steps = inputs.shape[1] // DEEP
-    cuts = [0, 4 * steps // 14, 9 * steps // 14, steps]
+    cuts = [0, 5 * steps // 14, 9 * steps // 14, steps]
     part = basis_out.shape[1] // 4
     got = {"own": inputs}
 
@@ -225,32 +228,28 @@
     got["keep"] = dot(deltas, columns(basis_out, half))
     got["keep16"] = got["keep"].astype(BF16)
     fence("x1", "a1", "m1", "give", "keep", "keep16", "order", "places")
+    some = steps // 2
     got["x2"] = send(got["a1"], ACROSS_ENDS)
     got["x2", "m"] = send(got["m1"], ACROSS_MIDDLE)
     got["a2"] = send(got["m1"], TO_ENDS)
     got["m2"] = send(got["a1"], MIDDLE)
-    fence(("r1", 0), "x1", "give", "keep16")
+    blocks = [["own"], ["a1"], ["x1"]]
+    got["A"] = turn([], blocks, 0, some)
+    fence(("r1", 0), "x1", "give", "keep16", "A")
     got["r1", 1] = send(got["keep16"], FROM_ENDS)
     got["give"] += got["r1", 0].astype(F32)
-    for p in range(2):
-        got["give", p] = got["give"][:, p * part : (p + 1) * part]
-    fence(("give", 0), ("give", 1), "x1")
-    got["A"] = turn(None, [["own"], ["a1"], ["x1"]], 0, steps)
-    fence("x1", "x2", ("x2", "m"), "a2", "m2", ("give", 0), ("give", 1), "keep", ("r1", 1), "A")
+    fence("x1", "x2", ("x2", "m"), "a2", "m2", "give", "keep", ("r1", 1), "A")
     got["x3"] = send(got["a2"], ACROSS_ENDS)
     got["x3", "m"] = send(got["m2"], ACROSS_MIDDLE)
     got["a3"] = send(got["m2"], TO_ENDS)
-    got["m3", 0] = send(got["give", 0], MIDDLE)
+    got["m3"] = send(got["give"], MIDDLE)
     got["e"] = send(got["x1"], FROM_ENDS)
     got["keep"] += got["r1", 1].astype(F32)
-    some = steps // 2
-    second = [["a2", "m1"], ["x2", ("x2", "m")]]
-    got["B"] = turn(None, second, 0, some)
-    fence(("m3", 0), ("give", 1), "keep", "B")
-    got["m3", 1] = send(got["give", 1], MIDDLE)
-    got["B"] = turn(got["B"], second, some, steps - some)
-    fence("x3", "B")
-    fence(("x3", "m"), "a3", "e", "A", "B", ("m3", 0))
+    more = [["a2", "m1"], ["x2", ("x2", "m")]]
+    got["B"] = turn([], more, 0, some)
+    got["A"] = turn([got["A"], got["B"]], blocks + more, some, steps - some)
+    fence("x3", "A", "keep")
+    fence(("x3", "m"), "a3", "e", "A")
 
     def x4(piece):
         got["x4", piece] = send(got["a3"][:, cuts[piece] * DEEP : cuts[piece + 1] * DEEP], ACROSS_ENDS)
@@ -259,42 +258,40 @@
         first = cuts[piece]
         blocks = [["a3", "m2"], ["x3", ("x3", "m")]]
         blocks = [[(got[n], first) for n in b] for b in blocks] + [[(got["x4", piece], 0), (got["e"], first)]]
-        got["D"] = rotate(got.get("D"), end, blocks, basis_in, first, cuts[piece + 1] - first)
+        got["D"] = rotate([got["D"]] if piece else [], end, blocks, basis_in, first, cuts[piece + 1] - first)
 
     def cross(p):
-        got["keep", p] = got["keep"][:, p * part : (p + 1) * part] + got["m3", p]
+        here = slice(p * part, (p + 1) * part)
+        got["keep", p] = got["keep"][:, here] + got["m3"][:, here]
         got["x5", p] = send(got["keep", p].astype(BF16), ACROSS_MIDDLE)
 
     x4(0)
+    fence("m3", "A")
     cross(0)
-    fence(("m3", 1), "A", "B")
     cross(1)
     fence(("x4", 0), ("x5", 0), "a3")
     x4(1)
     settle(0)
-    got["A2"] = swap_narrow(got["A"])
-    fence(("x5", 1), ("m4", 0), ("n1", 0), ("sum", 0), "A2", ("x4", 0))
+    fence(("x4", 1), ("x5", 1), ("m4", 0), ("n1", 0), ("sum", 0), "A", "a3")
+    x4(2)
     settle(1)
     got["n2", 0] = send(got["m4", 0], TO_ENDS)
-    got["B2"] = swap_narrow(got["B"])
-    got["A"] = (got["A"] + got["A2"]).astype(BF16)
+    got["A2"] = swap_narrow(got["A"])
     got["R", 0] = pick(("n1", 0), ("sum", 0))
     last(0)
-    fence(("x4", 1), "A", ("R", 0), "B2", "D", "a3")
-    x4(2)
-    fence(("m4", 1), ("n1", 1), ("sum", 1), ("x4", 1))
-    got["B"] = (got["B"] + got["B2"]).astype(BF16)
+    fence(("m4", 1), ("n1", 1), ("sum", 1), "A2", ("R", 0), "D")
+    got["n2", 1] = send(got["m4", 1], TO_ENDS)
+    got["A"] = (got["A"] + got["A2"]).astype(BF16)
     got["R", 1] = pick(("n1", 1), ("sum", 1))
     last(1)
-    fence(("x4", 2), ("n2", 0), ("m4", 0), ("R", 1), "B", "D")
-    got["n2", 1] = send(got["m4", 1], TO_ENDS)
+    fence(("x4", 2), ("n2", 0), ("m4", 0), ("R", 1), "A", "D")
     got["R", 2] = pick(("n2", 0), ("m4", 0))
     last(2)
     fence(("n2", 1), ("R", 2), "D")
     got["D2"] = swap_narrow(got["D"])
 
     pieces = [[got["R", p]] for p in range(3)] + [[got["n2", 1], got["m4", 1]]]
-    return fit(got["order"], end, [[got["A"]], [got["B"]], [got["D"], got["D2"]]], pieces, got["places"])
+    return fit(got["order"], end, [[got["A"]], [got["D"], got["D2"]]], pieces, got["places"])
 
 
 def solution(mesh):

time: 241 us -> 232 us (0.963)
  Pallas kernels: 89 us -> 79.4 us
  other arithmetic: 10.3 us -> 6.56 us
  starting transfers between devices: 54 us -> 57.7 us
  waiting for transfers between devices: 71.6 us -> 74.2 us
    pallas_call x6, Pallas kernels: 76.5 us -> 66.9 us  [rotate(): pl.pallas_call(lambda *refs: rotate_kernel([len(block) for block in block...]
    ppermute x26 -> x25, starting transfers between devices: 53.8 us -> 57.7 us  [send(): return lax.ppermute(a, 'wide', perm)]
    ppermute x26 -> x25, waiting for transfers between devices: 68.5 us -> 71.1 us  [send(): return lax.ppermute(a, 'wide', perm)]
  transfers between devices with their start and end apart: 29 -> 27, of which waited for: 10 -> 14; matrix products, arithmetic and copies ran while one was open for 8% -> 7% of each run, Pallas kernels for 32% -> 29%
where the time goes in v11:
time: 232 us; the launch traced here: 231 us
  Pallas kernels  79.4 us (34%)
  waiting for transfers between devices  74.2 us (32%)
  starting transfers between devices  57.7 us (25%)
  matrix products  9.05 us (4%)
  other arithmetic  6.56 us (3%)
  local copies, waits for them, and re-layouts  3.37 us (1%)
    ppermute x25, waiting for transfers between devices, send(): return lax.ppermute(a, 'wide', perm)  71.1 us
    pallas_call x6, Pallas kernels, rotate(): pl.pallas_call(lambda *refs: rotate_kernel([len(block) for block in block...  66.9 us
    ppermute x25, starting transfers between devices, send(): return lax.ppermute(a, 'wide', perm)  57.7 us
    pallas_call x1, Pallas kernels, fit(): pl.pallas_call(lambda *refs: fit_kernel([len(halves) for halves in sums],...  12.5 us
    dot_general x2, matrix products, dot(): return jnp.dot(a, b, preferred_element_type=F32)  9.05 us
  transfers between devices with their start and end apart: 27, of which 14 were waited for; matrix products, arithmetic and copies ran while one was open for 7% of the time, Pallas kernels for 29%

profile of v11, /device:TPU:0, one launch (start us, length us, event | category | flops | bytes accessed | tf_op | source)
XLA Modules:
  0.0 230.7 jit_solution(215561605742685899)
XLA Ops:
  0.0 2.9 %collective-permute-start = (bf16[64,14336]{1,0:T(8,128)(2,1)}, bf16[64,14336]{1,0:T(8,128)(2,1)}, u32[]{:S(2)}, u32[]{:S(2)}) collective-permute-start(bf16[64,14336]{1,0:T(8,128)(2,1)} %refs_1_.3), channel_id=1, source_target_pairs={{0,2},{2,0},{4,6},{6,4},{8,10},{10,8},{12,14},{14,12},{1,3},{3,1},... | collective-permute-start | bytes 5505032 | tf_op jit(solution)/shard_map/ppermute | solution.py:184
  2.9 1.6 collective-permute-start.1
  4.5 1.9 collective-permute-start.2
  6.4 4.5 %fusion.15 = (bf16[512,1024]{1,0:T(8,128)(2,1)}, f32[512,1024]{1,0:T(8,128)}) fusion(bf16[512,1024]{1,0:T(8,128)(2,1)S(1)} %copy-done, bf16[1024,2048]{1,0:T(8,128)(2,1)} %param.7, s32[]{:T(128)S(6)} %select_n.56), kind=kOutput, calls=%fused_computation.22 | convolution fusion | flops 1074266112 | bytes 6291460 | tf_op jit(solution)/shard_map/dot_general | solution.py:16
  10.9 5.1 %collective-permute-start.3 = (bf16[512,1024]{1,0:T(8,128)(2,1)}, bf16[512,1024]{1,0:T(8,128)(2,1)S(1)}, u32[]{:S(2)}, u32[]{:S(2)}) collective-permute-start(bf16[512,1024]{1,0:T(8,128)(2,1)} %get-tuple-element.121), channel_id=1, source_target_pairs={{0,4},{2,6},{12,8},{14,10},{1,5},{3,7},{13,9},{15,11},{16,20},{18,... | collective-permute-start | bytes 3145736 | tf_op jit(solution)/shard_map/ppermute | solution.py:184
  17.4 4.5 %fusion.14 = (bf16[512,1024]{1,0:T(8,128)(2,1)}, f32[512,1024]{1,0:T(8,128)}) fusion(bf16[512,1024]{1,0:T(8,128)(2,1)S(1)} %copy-done, bf16[1024,2048]{1,0:T(8,128)(2,1)} %param.7, s32[]{:T(128)S(6)} %select_n.57), kind=kOutput, calls=%fused_computation.21 | convolution fusion | flops 1074266112 | bytes 6291460 | tf_op jit(solution)/shard_map/dot_general | solution.py:16
  21.9 21.3 %collective-permute-done.refs_3_ = bf16[64,14336]{1,0:T(8,128)(2,1)} collective-permute-done((bf16[64,14336]{1,0:T(8,128)(2,1)}, bf16[64,14336]{1,0:T(8,128)(2,1)}, u32[]{:S(2)}, u32[]{:S(2)}) %collective-permute-start) | collective-permute-done | bytes 1835040 | tf_op jit(solution)/shard_map/ppermute | solution.py:184
  43.3 2.0 collective-permute-done.1.refs_2_
  45.3 2.4 %collective-permute-start.4 = (bf16[64,14336]{1,0:T(8,128)(2,1)}, bf16[64,14336]{1,0:T(8,128)(2,1)}, u32[]{:S(2)}, u32[]{:S(2)}) collective-permute-start(bf16[64,14336]{1,0:T(8,128)(2,1)} %collective-permute-done.1.refs_2_), channel_id=1, source_target_pairs={{0,2},{2,0},{12,14},{14,12},{1,3},{3,1},{13,15},{15,13},{16,18},{1... | collective-permute-start | bytes 5505032 | tf_op jit(solution)/shard_map/ppermute | solution.py:184
  47.7 2.0 collective-permute-start.5
  51.8 1.5 copy-done.2
  53.3 12.9 %rotate.6.refs_9_ = f32[192,1792]{1,0:T(8,128)S(1)} custom-call(s32[1]{0:T(128)} %bitcast.14.refs_0_.refs_1_, bf16[64,14336]{1,0:T(8,128)(2,1)S(1)} %copy-done.2, bf16[64,14336]{1,0:T(8,128)(2,1)} %collective-permute-done.1.refs_2_, bf16[64,14336]{1,0:T(8,128)(2,1)} %collective-permute-done.refs_3_, bf16[14336,1792]{1,0:T(8,128)(2,1)} %refs_7_.5), custom_call_target="tpu_custom_call" | custom-call | flops 344064 | bytes 1376256 | tf_op jit(solution)/shard_map/rotate/pallas_call | solution.py:125
  66.3 10.0 %collective-permute-start.8 = (bf16[512,1024]{1,0:T(8,128)(2,1)S(1)}, bf16[512,1024]{1,0:T(8,128)(2,1)S(1)}, u32[]{:S(2)}, u32[]{:S(2)}) collective-permute-start(bf16[512,1024]{1,0:T(8,128)(2,1)S(1)} %copy-done.10), channel_id=1, source_target_pairs={{0,4},{2,6},{12,8},{14,10},{1,5},{3,7},{13,9},{15,11},{16,20},{18,... | collective-permute-start | bytes 3145736 | tf_op jit(solution)/shard_map/ppermute | solution.py:184
  76.8 19.8 %collective-permute-done.8 = bf16[512,1024]{1,0:T(8,128)(2,1)S(1)} collective-permute-done((bf16[512,1024]{1,0:T(8,128)(2,1)S(1)}, bf16[512,1024]{1,0:T(8,128)(2,1)S(1)}, u32[]{:S(2)}, u32[]{:S(2)}) %collective-permute-start.8) | collective-permute-done | bytes 1048608 | tf_op jit(solution)/shard_map/ppermute | solution.py:184
  97.4 3.4 %collective-permute-start.12 = (bf16[64,14336]{1,0:T(8,128)(2,1)}, bf16[64,14336]{1,0:T(8,128)(2,1)S(1)}, u32[]{:S(2)}, u32[]{:S(2)}) collective-permute-start(bf16[64,14336]{1,0:T(8,128)(2,1)} %collective-permute-done.6.refs_1_.refs_4_), channel_id=1, source_target_pairs={{0,2},{2,0},{12,14},{14,12},{1,3},{3,1},{13,15},{15,13},{16,18},{1... | collective-permute-start | bytes 5505032 | tf_op jit(solution)/shard_map/ppermute | solution.py:184
  102.1 4.8 %collective-permute-start.11 = (bf16[64,14336]{1,0:T(8,128)(2,1)}, bf16[64,14336]{1,0:T(8,128)(2,1)S(1)}, u32[]{:S(2)}, u32[]{:S(2)}) collective-permute-start(bf16[64,14336]{1,0:T(8,128)(2,1)} %collective-permute-done.refs_3_), channel_id=1, source_target_pairs={{0,4},{2,6},{12,8},{14,10},{1,5},{3,7},{13,9},{15,11},{16,20},{18,... | collective-permute-start | bytes 5505032 | tf_op jit(solution)/shard_map/ppermute | solution.py:184
  107.7 12.1 %rotate.7.refs_10_ = f32[128,1792]{1,0:T(8,128)S(1)} custom-call(s32[1]{0:T(128)} %bitcast.14.refs_0_.refs_1_, bf16[64,14336]{1,0:T(8,128)(2,1)} %collective-permute-done.6.refs_1_.refs_4_, bf16[64,14336]{1,0:T(8,128)(2,1)} %collective-permute-done.2.refs_2_.refs_5_, bf16[64,14336]{1,0:T(8,128)(2,1)} %collective-permute-done.4.refs_3_.refs_6_, ...), custom_call_target="tpu_custom_call" | custom-call | flops 229376 | bytes 917504 | tf_op jit(solution)/shard_map/rotate/pallas_call | solution.py:125
  119.8 15.5 %rotate.8 = f32[320,1792]{1,0:T(8,128)S(1)} custom-call(s32[1]{0:T(128)} %bitcast.14.refs_0_.refs_1_, bf16[64,14336]{1,0:T(8,128)(2,1)S(1)} %copy-done.3, bf16[64,14336]{1,0:T(8,128)(2,1)} %collective-permute-done.1.refs_2_, bf16[64,14336]{1,0:T(8,128)(2,1)} %collective-permute-done.refs_3_, bf16[64,14336]{1,0:T(8,128)(2,1)} %collective-permute-done.6.refs_1_.refs_4_, ...), custom_call_target="tpu_custom_call" | custom-call | flops 573440 | bytes 2293760 | tf_op jit(solution)/shard_map/rotate/pallas_call | solution.py:125
  135.6 2.7 %collective-permute-done.12.refs_3_ = bf16[64,14336]{1,0:T(8,128)(2,1)S(1)} collective-permute-done((bf16[64,14336]{1,0:T(8,128)(2,1)}, bf16[64,14336]{1,0:T(8,128)(2,1)S(1)}, u32[]{:S(2)}, u32[]{:S(2)}) %collective-permute-start.12) | collective-permute-done | bytes 1835040 | tf_op jit(solution)/shard_map/ppermute | solution.py:184
  138.3 2.9 %collective-permute-done.10.refs_1_ = bf16[64,14336]{1,0:T(8,128)(2,1)S(1)} collective-permute-done((bf16[64,14336]{1,0:T(8,128)(2,1)S(1)}, bf16[64,14336]{1,0:T(8,128)(2,1)S(1)}, u32[]{:S(2)}, u32[]{:S(2)}) %collective-permute-start.10) | collective-permute-done | bytes 1835040 | tf_op jit(solution)/shard_map/ppermute | solution.py:184
  141.2 1.6 collective-permute-done.11.refs_6_
  142.9 3.3 %collective-permute-start.13 = (bf16[64,5120]{1,0:T(8,128)(2,1)S(1)}, bf16[64,5120]{1,0:T(8,128)(2,1)S(1)}, u32[]{:S(2)}, u32[]{:S(2)}) collective-permute-start(bf16[64,5120]{1,0:T(8,128)(2,1)S(1)} %slice.21), channel_id=1, source_target_pairs={{0,2},{2,0},{12,14},{14,12},{1,3},{3,1},{13,15},{15,13},{16,18},{1... | collective-permute-start | bytes 1966088 | tf_op jit(solution)/shard_map/ppermute | solution.py:184
  147.1 9.8 %collective-permute-done.13.refs_5_ = bf16[64,5120]{1,0:T(8,128)(2,1)S(1)} collective-permute-done((bf16[64,5120]{1,0:T(8,128)(2,1)S(1)}, bf16[64,5120]{1,0:T(8,128)(2,1)S(1)}, u32[]{:S(2)}, u32[]{:S(2)}) %collective-permute-start.13) | collective-permute-done | bytes 655392 | tf_op jit(solution)/shard_map/ppermute | solution.py:184
  160.4 3.6 %collective-permute-start.16 = (bf16[64,4096]{1,0:T(8,128)(2,1)S(1)}, bf16[64,4096]{1,0:T(8,128)(2,1)S(1)}, u32[]{:S(2)}, u32[]{:S(2)}) collective-permute-start(bf16[64,4096]{1,0:T(8,128)(2,1)S(1)} %slice.24), channel_id=1, source_target_pairs={{0,2},{2,0},{12,14},{14,12},{1,3},{3,1},{13,15},{15,13},{16,18},{1... | collective-permute-start | bytes 1572872 | tf_op jit(solution)/shard_map/ppermute | solution.py:184
  164.0 6.5 %collective-permute-done.19 = bf16[512,512]{1,0:T(8,128)(2,1)S(1)} collective-permute-done((bf16[512,512]{1,0:T(8,128)(2,1)S(1)}, bf16[512,512]{1,0:T(8,128)(2,1)S(1)}, u32[]{:S(2)}, u32[]{:S(2)}) %collective-permute-start.19) | collective-permute-done | bytes 524320 | tf_op jit(solution)/shard_map/ppermute | solution.py:184
  173.8 3.6 %collective-permute-start.20 = (bf16[64,5120]{1,0:T(8,128)(2,1)S(1)}, bf16[64,5120]{1,0:T(8,128)(2,1)S(1)}, u32[]{:S(2)}, u32[]{:S(2)}) collective-permute-start(bf16[64,5120]{1,0:T(8,128)(2,1)S(1)} %slice.27), channel_id=1, source_target_pairs={{0,2},{2,0},{12,14},{14,12},{1,3},{3,1},{13,15},{15,13},{16,18},{1... | collective-permute-start | bytes 1966088 | tf_op jit(solution)/shard_map/ppermute | solution.py:184
  179.0 9.5 %rotate.9.refs_8_ = f32[192,1792]{1,0:T(8,128)S(1)} custom-call(s32[1]{0:T(128)} %bitcast.14.refs_0_.refs_1_, bf16[64,14336]{1,0:T(8,128)(2,1)S(1)} %collective-permute-done.10.refs_1_, bf16[64,14336]{1,0:T(8,128)(2,1)S(1)} %collective-permute-done.7.refs_2_, bf16[64,14336]{1,0:T(8,128)(2,1)S(1)} %collective-permute-done.12.refs_3_, ...), custom_call_target="tpu_custom_call" | custom-call | flops 344064 | bytes 1376256 | tf_op jit(solution)/shard_map/rotate/pallas_call | solution.py:125
  189.3 2.6 %collective-permute-done.23 = bf16[512,512]{1,0:T(8,128)(2,1)S(1)} collective-permute-done((bf16[512,512]{1,0:T(8,128)(2,1)S(1)}, bf16[512,512]{1,0:T(8,128)(2,1)S(1)}, u32[]{:S(2)}, u32[]{:S(2)}) %collective-permute-start.23) | collective-permute-done | bytes 524320 | tf_op jit(solution)/shard_map/ppermute | solution.py:184
  194.4 7.6 %rotate.10.refs_8_ = f32[192,1792]{1,0:T(8,128)S(1)} custom-call(s32[1]{0:T(128)} %bitcast.14.refs_0_.refs_1_, bf16[64,14336]{1,0:T(8,128)(2,1)S(1)} %collective-permute-done.10.refs_1_, bf16[64,14336]{1,0:T(8,128)(2,1)S(1)} %collective-permute-done.7.refs_2_, bf16[64,14336]{1,0:T(8,128)(2,1)S(1)} %collective-permute-done.12.refs_3_, ...), custom_call_target="tpu_custom_call" | custom-call | flops 344064 | bytes 1376256 | tf_op jit(solution)/shard_map/rotate/pallas_call | solution.py:125
  203.2 9.4 %rotate.11.refs_4_ = f32[192,1792]{1,0:T(8,128)S(1)} custom-call(s32[1]{0:T(128)} %bitcast.14.refs_0_.refs_1_, bf16[64,14336]{1,0:T(8,128)(2,1)S(1)} %collective-permute-done.10.refs_1_, bf16[64,14336]{1,0:T(8,128)(2,1)S(1)} %collective-permute-done.7.refs_2_, bf16[64,14336]{1,0:T(8,128)(2,1)S(1)} %collective-permute-done.12.refs_3_, ...), custom_call_target="tpu_custom_call" | custom-call | flops 344064 | bytes 1376256 | tf_op jit(solution)/shard_map/rotate/pallas_call | solution.py:125
  214.0 3.1 %collective-permute-done.26.refs_5_ = f32[192,1792]{1,0:T(8,128)S(1)} collective-permute-done((f32[192,1792]{1,0:T(8,128)S(1)}, f32[192,1792]{1,0:T(8,128)S(1)}, u32[]{:S(2)}, u32[]{:S(2)}) %collective-permute-start.26) | collective-permute-done | bytes 1376288 | tf_op jit(solution)/shard_map/ppermute | solution.py:146
  218.2 12.5 %fit.1 = f32[1792,2048]{1,0:T(8,128)} custom-call(s32[8]{0:T(128)} %stack.50.refs_0_, s32[1]{0:T(128)} %bitcast.14.refs_0_.refs_1_, s32[4]{0:T(128)} %pad_add_fusion.refs_2_, bf16[320,1792]{1,0:T(8,128)(2,1)} %add_convert_fusion.refs_3_, f32[192,1792]{1,0:T(8,128)} %copy-done.4, f32[192,1792]{1,0:T(8,128)} %copy-done.7, ...), custom_call_target="tpu_custom_call" | custom-call | flops 3758096384 | bytes 24117248 | tf_op jit(solution)/shard_map/fit/pallas_call | solution.py:64
  (67 shorter events, 23.2 us)
Async XLA Ops:
  0.0 43.3 %collective-permute-start = (bf16[64,14336]{1,0:T(8,128)(2,1)}, bf16[64,14336]{1,0:T(8,128)(2,1)}, u32[]{:S(2)}, u32[]{:S(2)}) collective-permute-start(bf16[64,14336]{1,0:T(8,128)(2,1)} %refs_1_.3), channel_id=1, source_target_pairs={{0,2},{2,0},{4,6},{6,4},{8,10},{10,8},{12,14},{14,12},{1,3},{3,1},... | collective-permute-start | bytes 5505032 | tf_op jit(solution)/shard_map/ppermute | solution.py:184
  2.9 42.3 %collective-permute-start.1 = (bf16[64,14336]{1,0:T(8,128)(2,1)}, bf16[64,14336]{1,0:T(8,128)(2,1)}, u32[]{:S(2)}, u32[]{:S(2)}) collective-permute-start(bf16[64,14336]{1,0:T(8,128)(2,1)} %refs_1_.3), channel_id=1, source_target_pairs={{0,4},{2,6},{4,0},{6,2},{8,12},{10,14},{12,8},{14,10},{1,5},{3,7},... | collective-permute-start | bytes 5505032 | tf_op jit(solution)/shard_map/ppermute | solution.py:184
  4.5 40.8 %collective-permute-start.2 = (bf16[64,14336]{1,0:T(8,128)(2,1)}, bf16[64,14336]{1,0:T(8,128)(2,1)}, u32[]{:S(2)}, u32[]{:S(2)}) collective-permute-start(bf16[64,14336]{1,0:T(8,128)(2,1)} %refs_1_.3), channel_id=1, source_target_pairs={{4,8},{6,10},{8,4},{10,6},{5,9},{7,11},{9,5},{11,7},{20,24},{22,26... | collective-permute-start | bytes 5505032 | tf_op jit(solution)/shard_map/ppermute | solution.py:184
  10.9 55.4 %collective-permute-start.3 = (bf16[512,1024]{1,0:T(8,128)(2,1)}, bf16[512,1024]{1,0:T(8,128)(2,1)S(1)}, u32[]{:S(2)}, u32[]{:S(2)}) collective-permute-start(bf16[512,1024]{1,0:T(8,128)(2,1)} %get-tuple-element.121), channel_id=1, source_target_pairs={{0,4},{2,6},{12,8},{14,10},{1,5},{3,7},{13,9},{15,11},{16,20},{18,... | collective-permute-start | bytes 3145736 | tf_op jit(solution)/shard_map/ppermute | solution.py:184
  45.3 51.3 %collective-permute-start.4 = (bf16[64,14336]{1,0:T(8,128)(2,1)}, bf16[64,14336]{1,0:T(8,128)(2,1)}, u32[]{:S(2)}, u32[]{:S(2)}) collective-permute-start(bf16[64,14336]{1,0:T(8,128)(2,1)} %collective-permute-done.1.refs_2_), channel_id=1, source_target_pairs={{0,2},{2,0},{12,14},{14,12},{1,3},{3,1},{13,15},{15,13},{16,18},{1... | collective-permute-start | bytes 5505032 | tf_op jit(solution)/shard_map/ppermute | solution.py:184
  47.7 48.8 %collective-permute-start.5 = (bf16[64,14336]{1,0:T(8,128)(2,1)}, bf16[64,14336]{1,0:T(8,128)(2,1)}, u32[]{:S(2)}, u32[]{:S(2)}) collective-permute-start(bf16[64,14336]{1,0:T(8,128)(2,1)} %collective-permute-done.2.refs_2_.refs_5_), channel_id=1, source_target_pairs={{4,6},{6,4},{8,10},{10,8},{5,7},{7,5},{9,11},{11,9},{20,22},{22,20... | collective-permute-start | bytes 5505032 | tf_op jit(solution)/shard_map/ppermute | solution.py:184
  49.7 46.9 %collective-permute-start.6 = (bf16[64,14336]{1,0:T(8,128)(2,1)}, bf16[64,14336]{1,0:T(8,128)(2,1)}, u32[]{:S(2)}, u32[]{:S(2)}) collective-permute-start(bf16[64,14336]{1,0:T(8,128)(2,1)} %collective-permute-done.2.refs_2_.refs_5_), channel_id=1, source_target_pairs={{4,0},{6,2},{8,12},{10,14},{5,1},{7,3},{9,13},{11,15},{20,16},{22,... | collective-permute-start | bytes 5505032 | tf_op jit(solution)/shard_map/ppermute | solution.py:184
  51.0 45.6 %collective-permute-start.7 = (bf16[64,14336]{1,0:T(8,128)(2,1)}, bf16[64,14336]{1,0:T(8,128)(2,1)S(1)}, u32[]{:S(2)}, u32[]{:S(2)}) collective-permute-start(bf16[64,14336]{1,0:T(8,128)(2,1)} %collective-permute-done.1.refs_2_), channel_id=1, source_target_pairs={{4,8},{6,10},{8,4},{10,6},{5,9},{7,11},{9,5},{11,7},{20,24},{22,26... | collective-permute-start | bytes 5505032 | tf_op jit(solution)/shard_map/ppermute | solution.py:184
  53.3 13.0 %copy-start.10 = (bf16[512,1024]{1,0:T(8,128)(2,1)S(1)}, bf16[512,1024]{1,0:T(8,128)(2,1)}, u32[]{:S(2)}) copy-start(bf16[512,1024]{1,0:T(8,128)(2,1)} %get-tuple-element.72) | copy-start | bytes 3145732
  53.3 23.0 %copy-start.5 = (f32[512,1024]{1,0:T(8,128)S(1)}, f32[512,1024]{1,0:T(8,128)}, u32[]{:S(2)}) copy-start(f32[512,1024]{1,0:T(8,128)} %get-tuple-element.69) | copy-start | bytes 6291460
  66.3 30.3 %collective-permute-start.8 = (bf16[512,1024]{1,0:T(8,128)(2,1)S(1)}, bf16[512,1024]{1,0:T(8,128)(2,1)S(1)}, u32[]{:S(2)}, u32[]{:S(2)}) collective-permute-start(bf16[512,1024]{1,0:T(8,128)(2,1)S(1)} %copy-done.10), channel_id=1, source_target_pairs={{0,4},{2,6},{12,8},{14,10},{1,5},{3,7},{13,9},{15,11},{16,20},{18,... | collective-permute-start | bytes 3145736 | tf_op jit(solution)/shard_map/ppermute | solution.py:184
  76.7 43.0 %copy-start.3 = (bf16[64,14336]{1,0:T(8,128)(2,1)S(1)}, bf16[64,14336]{1,0:T(8,128)(2,1)}, u32[]{:S(2)}) copy-start(bf16[64,14336]{1,0:T(8,128)(2,1)} %refs_1_.3) | copy-start | bytes 5505028
  96.6 49.6 %collective-permute-start.14 = (f32[512,1024]{1,0:T(8,128)S(1)}, f32[512,1024]{1,0:T(8,128)S(1)}, u32[]{:S(2)}, u32[]{:S(2)}) collective-permute-start(f32[512,1024]{1,0:T(8,128)S(1)} %convert_add_fusion.1), channel_id=1, source_target_pairs={{4,8},{6,10},{8,4},{10,6},{5,9},{7,11},{9,5},{11,7},{20,24},{22,26... | collective-permute-start | bytes 6291464 | tf_op jit(solution)/shard_map/ppermute | solution.py:184
  97.4 40.9 %collective-permute-start.12 = (bf16[64,14336]{1,0:T(8,128)(2,1)}, bf16[64,14336]{1,0:T(8,128)(2,1)S(1)}, u32[]{:S(2)}, u32[]{:S(2)}) collective-permute-start(bf16[64,14336]{1,0:T(8,128)(2,1)} %collective-permute-done.6.refs_1_.refs_4_), channel_id=1, source_target_pairs={{0,2},{2,0},{12,14},{14,12},{1,3},{3,1},{13,15},{15,13},{16,18},{1... | collective-permute-start | bytes 5505032 | tf_op jit(solution)/shard_map/ppermute | solution.py:184
  100.8 40.4 %collective-permute-start.10 = (bf16[64,14336]{1,0:T(8,128)(2,1)S(1)}, bf16[64,14336]{1,0:T(8,128)(2,1)S(1)}, u32[]{:S(2)}, u32[]{:S(2)}) collective-permute-start(bf16[64,14336]{1,0:T(8,128)(2,1)S(1)} %collective-permute-done.7.refs_2_), channel_id=1, source_target_pairs={{4,0},{6,2},{8,12},{10,14},{5,1},{7,3},{9,13},{11,15},{20,16},{22,... | collective-permute-start | bytes 5505032 | tf_op jit(solution)/shard_map/ppermute | solution.py:184
  102.1 40.7 %collective-permute-start.11 = (bf16[64,14336]{1,0:T(8,128)(2,1)}, bf16[64,14336]{1,0:T(8,128)(2,1)S(1)}, u32[]{:S(2)}, u32[]{:S(2)}) collective-permute-start(bf16[64,14336]{1,0:T(8,128)(2,1)} %collective-permute-done.refs_3_), channel_id=1, source_target_pairs={{0,4},{2,6},{12,8},{14,10},{1,5},{3,7},{13,9},{15,11},{16,20},{18,... | collective-permute-start | bytes 5505032 | tf_op jit(solution)/shard_map/ppermute | solution.py:184
  106.9 35.9 %collective-permute-start.9 = (bf16[64,14336]{1,0:T(8,128)(2,1)S(1)}, bf16[64,14336]{1,0:T(8,128)(2,1)S(1)}, u32[]{:S(2)}, u32[]{:S(2)}) collective-permute-start(bf16[64,14336]{1,0:T(8,128)(2,1)S(1)} %collective-permute-done.7.refs_2_), channel_id=1, source_target_pairs={{4,6},{6,4},{8,10},{10,8},{5,7},{7,5},{9,11},{11,9},{20,22},{22,20... | collective-permute-start | bytes 5505032 | tf_op jit(solution)/shard_map/ppermute | solution.py:184
  119.8 15.5 %copy-start.6 = (f32[512,1024]{1,0:T(8,128)S(1)}, f32[512,1024]{1,0:T(8,128)}, u32[]{:S(2)}) copy-start(f32[512,1024]{1,0:T(8,128)} %get-tuple-element.80) | copy-start | bytes 6291460
  142.9 14.1 %collective-permute-start.13 = (bf16[64,5120]{1,0:T(8,128)(2,1)S(1)}, bf16[64,5120]{1,0:T(8,128)(2,1)S(1)}, u32[]{:S(2)}, u32[]{:S(2)}) collective-permute-start(bf16[64,5120]{1,0:T(8,128)(2,1)S(1)} %slice.21), channel_id=1, source_target_pairs={{0,2},{2,0},{12,14},{14,12},{1,3},{3,1},{13,15},{15,13},{16,18},{1... | collective-permute-start | bytes 1966088 | tf_op jit(solution)/shard_map/ppermute | solution.py:184
  146.4 10.6 %collective-permute-start.15 = (bf16[512,512]{1,0:T(8,128)(2,1)S(1)}, bf16[512,512]{1,0:T(8,128)(2,1)S(1)}, u32[]{:S(2)}, u32[]{:S(2)}) collective-permute-start(bf16[512,512]{1,0:T(8,128)(2,1)S(1)} %fusion.10), channel_id=1, source_target_pairs={{4,6},{6,4},{8,10},{10,8},{5,7},{7,5},{9,11},{11,9},{20,22},{22,20... | collective-permute-start | bytes 1572872 | tf_op jit(solution)/shard_map/ppermute | solution.py:184
  157.6 6.4 %collective-permute-start.18 = (bf16[512,512]{1,0:T(8,128)(2,1)S(1)}, bf16[512,512]{1,0:T(8,128)(2,1)S(1)}, u32[]{:S(2)}, u32[]{:S(2)}) collective-permute-start(bf16[512,512]{1,0:T(8,128)(2,1)S(1)} %get-tuple-element.96), channel_id=1, source_target_pairs={{4,8},{6,10},{8,4},{10,6},{5,9},{7,11},{9,5},{11,7},{20,24},{22,26... | collective-permute-start | bytes 1572872 | tf_op jit(solution)/shard_map/ppermute | solution.py:184
  158.3 12.3 %collective-permute-start.19 = (bf16[512,512]{1,0:T(8,128)(2,1)S(1)}, bf16[512,512]{1,0:T(8,128)(2,1)S(1)}, u32[]{:S(2)}, u32[]{:S(2)}) collective-permute-start(bf16[512,512]{1,0:T(8,128)(2,1)S(1)} %get-tuple-element.96), channel_id=1, source_target_pairs={{4,0},{6,2},{8,12},{10,14},{5,1},{7,3},{9,13},{11,15},{20,16},{22,... | collective-permute-start | bytes 1572872 | tf_op jit(solution)/shard_map/ppermute | solution.py:184
  159.6 4.4 %collective-permute-start.17 = (bf16[512,512]{1,0:T(8,128)(2,1)S(1)}, bf16[512,512]{1,0:T(8,128)(2,1)S(1)}, u32[]{:S(2)}, u32[]{:S(2)}) collective-permute-start(bf16[512,512]{1,0:T(8,128)(2,1)S(1)} %get-tuple-element.118), channel_id=1, source_target_pairs={{4,6},{6,4},{8,10},{10,8},{5,7},{7,5},{9,11},{11,9},{20,22},{22,20... | collective-permute-start | bytes 1572872 | tf_op jit(solution)/shard_map/ppermute | solution.py:184
  160.4 11.1 %collective-permute-start.16 = (bf16[64,4096]{1,0:T(8,128)(2,1)S(1)}, bf16[64,4096]{1,0:T(8,128)(2,1)S(1)}, u32[]{:S(2)}, u32[]{:S(2)}) collective-permute-start(bf16[64,4096]{1,0:T(8,128)(2,1)S(1)} %slice.24), channel_id=1, source_target_pairs={{0,2},{2,0},{12,14},{14,12},{1,3},{3,1},{13,15},{15,13},{16,18},{1... | collective-permute-start | bytes 1572872 | tf_op jit(solution)/shard_map/ppermute | solution.py:184
  171.5 20.5 %collective-permute-start.24 = (f32[320,1792]{1,0:T(8,128)S(1)}, f32[320,1792]{1,0:T(8,128)S(1)}, u32[]{:S(2)}, u32[]{:S(2)}) collective-permute-start(f32[320,1792]{1,0:T(8,128)S(1)} %rotate.8), channel_id=1, source_target_pairs={{0,1},{1,0},{2,3},{3,2},{4,5},{5,4},{6,7},{7,6},{8,9},{9,8},{10,11... | collective-permute-start | bytes 6881288 | tf_op jit(solution)/shard_map/ppermute | solution.py:146
  171.8 17.5 %collective-permute-start.22 = (bf16[512,512]{1,0:T(8,128)(2,1)S(1)}, bf16[512,512]{1,0:T(8,128)(2,1)S(1)}, u32[]{:S(2)}, u32[]{:S(2)}) collective-permute-start(bf16[512,512]{1,0:T(8,128)(2,1)S(1)} %add_convert_fusion.1), channel_id=1, source_target_pairs={{4,8},{6,10},{8,4},{10,6},{5,9},{7,11},{9,5},{11,7},{20,24},{22,26... | collective-permute-start | bytes 1572872 | tf_op jit(solution)/shard_map/ppermute | solution.py:184
  172.5 19.4 %collective-permute-start.23 = (bf16[512,512]{1,0:T(8,128)(2,1)S(1)}, bf16[512,512]{1,0:T(8,128)(2,1)S(1)}, u32[]{:S(2)}, u32[]{:S(2)}) collective-permute-start(bf16[512,512]{1,0:T(8,128)(2,1)S(1)} %add_convert_fusion.1), channel_id=1, source_target_pairs={{4,0},{6,2},{8,12},{10,14},{5,1},{7,3},{9,13},{11,15},{20,16},{22,... | collective-permute-start | bytes 1572872 | tf_op jit(solution)/shard_map/ppermute | solution.py:184
  173.8 29.3 %collective-permute-start.20 = (bf16[64,5120]{1,0:T(8,128)(2,1)S(1)}, bf16[64,5120]{1,0:T(8,128)(2,1)S(1)}, u32[]{:S(2)}, u32[]{:S(2)}) collective-permute-start(bf16[64,5120]{1,0:T(8,128)(2,1)S(1)} %slice.27), channel_id=1, source_target_pairs={{0,2},{2,0},{12,14},{14,12},{1,3},{3,1},{13,15},{15,13},{16,18},{1... | collective-permute-start | bytes 1966088 | tf_op jit(solution)/shard_map/ppermute | solution.py:184
  177.5 25.7 %collective-permute-start.21 = (bf16[512,512]{1,0:T(8,128)(2,1)S(1)}, bf16[512,512]{1,0:T(8,128)(2,1)S(1)}, u32[]{:S(2)}, u32[]{:S(2)}) collective-permute-start(bf16[512,512]{1,0:T(8,128)(2,1)S(1)} %collective-permute-done.18), channel_id=1, source_target_pairs={{4,0},{6,2},{8,12},{10,14},{5,1},{7,3},{9,13},{11,15},{20,16},{22,... | collective-permute-start | bytes 1572872 | tf_op jit(solution)/shard_map/ppermute | solution.py:184
  193.1 20.9 %collective-permute-start.25 = (bf16[512,512]{1,0:T(8,128)(2,1)S(1)}, bf16[512,512]{1,0:T(8,128)(2,1)S(1)}, u32[]{:S(2)}, u32[]{:S(2)}) collective-permute-start(bf16[512,512]{1,0:T(8,128)(2,1)S(1)} %collective-permute-done.22.refs_10_), channel_id=1, source_target_pairs={{4,0},{6,2},{8,12},{10,14},{5,1},{7,3},{9,13},{11,15},{20,16},{22,... | collective-permute-start | bytes 1572872 | tf_op jit(solution)/shard_map/ppermute | solution.py:184
  214.0 3.1 %collective-permute-start.26 = (f32[192,1792]{1,0:T(8,128)S(1)}, f32[192,1792]{1,0:T(8,128)S(1)}, u32[]{:S(2)}, u32[]{:S(2)}) collective-permute-start(f32[192,1792]{1,0:T(8,128)S(1)} %rotate.11.refs_4_), channel_id=1, source_target_pairs={{0,1},{1,0},{2,3},{3,2},{4,5},{5,4},{6,7},{7,6},{8,9},{9,8},{10,11... | collective-permute-start | bytes 4128776 | tf_op jit(solution)/shard_map/ppermute | solution.py:146
  218.2 12.5 %copy-start.1 = (bf16[512,1024]{1,0:T(8,128)(2,1)S(1)}, bf16[512,1024]{1,0:T(8,128)(2,1)}, u32[]{:S(2)}) copy-start(bf16[512,1024]{1,0:T(8,128)(2,1)} %param.5) | copy-start | bytes 3145732
  (6 other events, 20.6 us)

commit v12 on v11

--- a/solution.py
+++ b/solution.py
@@ -191,7 +191,7 @@
     end = at_end.astype(jnp.int32).reshape(1)
     half = (z >= 2).astype(jnp.int32)
     steps = inputs.shape[1] // DEEP
-    cuts = [0, 5 * steps // 14, 9 * steps // 14, steps]
+    cuts = [0, 8 * steps // 14, steps]
     part = basis_out.shape[1] // 4
     got = {"own": inputs}
 
@@ -223,11 +223,9 @@
     got["x1"] = send(got["own"], ACROSS)
     got["a1"] = send(got["own"], ENDS)
     got["m1"] = send(got["own"], MIDDLE)
-    got["give"] = dot(deltas, columns(basis_out, 1 - half))
-    got["r1", 0] = send(got["give"].astype(BF16), FROM_ENDS)
-    got["keep"] = dot(deltas, columns(basis_out, half))
-    got["keep16"] = got["keep"].astype(BF16)
-    fence("x1", "a1", "m1", "give", "keep", "keep16", "order", "places")
+    got["out"] = dot(deltas, jnp.concatenate([columns(basis_out, 1 - half), columns(basis_out, half)], axis=1))
+    got["r1"] = send(got["out"].astype(BF16), FROM_ENDS)
+    fence("x1", "a1", "m1", "out", "order", "places")
     some = steps // 2
     got["x2"] = send(got["a1"], ACROSS_ENDS)
     got["x2", "m"] = send(got["m1"], ACROSS_MIDDLE)
@@ -235,16 +233,14 @@
     got["m2"] = send(got["a1"], MIDDLE)
     blocks = [["own"], ["a1"], ["x1"]]
     got["A"] = turn([], blocks, 0, some)
-    fence(("r1", 0), "x1", "give", "keep16", "A")
-    got["r1", 1] = send(got["keep16"], FROM_ENDS)
-    got["give"] += got["r1", 0].astype(F32)
-    fence("x1", "x2", ("x2", "m"), "a2", "m2", "give", "keep", ("r1", 1), "A")
+    fence("x1", "x2", ("x2", "m"), "a2", "m2", "out", "r1", "A")
     got["x3"] = send(got["a2"], ACROSS_ENDS)
     got["x3", "m"] = send(got["m2"], ACROSS_MIDDLE)
     got["a3"] = send(got["m2"], TO_ENDS)
-    got["m3"] = send(got["give"], MIDDLE)
+    cut = 2 * part
+    got["m3"] = send(got["out"][:, :cut] + got["r1"][:, :cut].astype(F32), MIDDLE)
     got["e"] = send(got["x1"], FROM_ENDS)
-    got["keep"] += got["r1", 1].astype(F32)
+    got["keep"] = got["out"][:, cut:] + got["r1"][:, cut:].astype(F32)
     more = [["a2", "m1"], ["x2", ("x2", "m")]]
     got["B"] = turn([], more, 0, some)
     got["A"] = turn([got["A"], got["B"]], blocks + more, some, steps - some)
@@ -266,27 +262,25 @@
         got["x5", p] = send(got["keep", p].astype(BF16), ACROSS_MIDDLE)
 
     x4(0)
-    fence("m3", "A")
+    got["A2"] = swap_narrow(got["A"])
+    fence("m3", "A", "A2")
     cross(0)
     cross(1)
-    fence(("x4", 0), ("x5", 0), "a3")
+    fence(("x5", 0), "a3")
+    settle(0)
+    got["A"] = (got["A"] + got["A2"]).astype(BF16)
+    fence(("x4", 0), ("x5", 1), ("m4", 0), ("n1", 0), ("sum", 0), "A", "a3")
     x4(1)
-    settle(0)
-    fence(("x4", 1), ("x5", 1), ("m4", 0), ("n1", 0), ("sum", 0), "A", "a3")
-    x4(2)
     settle(1)
     got["n2", 0] = send(got["m4", 0], TO_ENDS)
-    got["A2"] = swap_narrow(got["A"])
     got["R", 0] = pick(("n1", 0), ("sum", 0))
     last(0)
-    fence(("m4", 1), ("n1", 1), ("sum", 1), "A2", ("R", 0), "D")
+    fence(("x4", 1), ("m4", 1), ("n1", 1), ("sum", 1), ("R", 0), "D")
     got["n2", 1] = send(got["m4", 1], TO_ENDS)
-    got["A"] = (got["A"] + got["A2"]).astype(BF16)
     got["R", 1] = pick(("n1", 1), ("sum", 1))
+    fence(("n2", 0), ("m4", 0), ("R", 1), "A", "D")
+    got["R", 2] = pick(("n2", 0), ("m4", 0))
     last(1)
-    fence(("x4", 2), ("n2", 0), ("m4", 0), ("R", 1), "A", "D")
-    got["R", 2] = pick(("n2", 0), ("m4", 0))
-    last(2)
     fence(("n2", 1), ("R", 2), "D")
     got["D2"] = swap_narrow(got["D"])
 

time: 232 us -> 286 us (1.23)
  waiting for transfers between devices: 74.2 us -> 145 us
  starting transfers between devices: 57.7 us -> 43.4 us
  matrix products: 9.05 us -> 5.1 us
    ppermute x25 -> x23, waiting for transfers between devices: 71.1 us -> 138 us  [send(): return lax.ppermute(a, 'wide', perm)]
    ppermute x25 -> x23, starting transfers between devices: 57.7 us -> 43.4 us  [send(): return lax.ppermute(a, 'wide', perm)]
    dot_general x2 -> x1, matrix products: 9.05 us -> 5.1 us  [dot(): return jnp.dot(a, b, preferred_element_type=F32)]
    ppermute x2, waiting for transfers between devices: 3.13 us -> 6.76 us  [swap_narrow(): return lax.ppermute(a, 'narrow', [(0, 1), (1, 0)])]
    pallas_call x6 -> x5, Pallas kernels: 66.9 us -> 64.9 us  [rotate(): pl.pallas_call(lambda *refs: rotate_kernel([len(block) for block in block...]
  transfers between devices with their start and end apart: 27 -> 25, of which waited for: 14 -> 13; matrix products, arithmetic and copies ran while one was open for 7% -> 6% of each run, Pallas kernels for 29% -> 23%
where the time goes in v12:
time: 286 us; the launch traced here: 285 us
  waiting for transfers between devices  145 us (51%)
  Pallas kernels  77.4 us (27%)
  starting transfers between devices  43.4 us (15%)
  other arithmetic  8.26 us (3%)
  local copies, waits for them, and re-layouts  6.06 us (2%)
  matrix products  5.1 us (2%)
    ppermute x23, waiting for transfers between devices, send(): return lax.ppermute(a, 'wide', perm)  138 us
    pallas_call x5, Pallas kernels, rotate(): pl.pallas_call(lambda *refs: rotate_kernel([len(block) for block in block...  64.9 us
    ppermute x23, starting transfers between devices, send(): return lax.ppermute(a, 'wide', perm)  43.4 us
    pallas_call x1, Pallas kernels, fit(): pl.pallas_call(lambda *refs: fit_kernel([len(halves) for halves in sums],...  12.5 us
    ppermute x2, waiting for transfers between devices, swap_narrow(): return lax.ppermute(a, 'narrow', [(0, 1), (1, 0)])  6.76 us
  transfers between devices with their start and end apart: 25, of which 13 were waited for; matrix products, arithmetic and copies ran while one was open for 6% of the time, Pallas kernels for 23%

profile of v12, /device:TPU:0, one launch (start us, length us, event | category | flops | bytes accessed | tf_op | source)
XLA Modules:
  0.0 285.3 jit_solution(17987133483391738218)
XLA Ops:
  0.9 5.8 %collective-permute-start.1 = (bf16[64,14336]{1,0:T(8,128)(2,1)}, bf16[64,14336]{1,0:T(8,128)(2,1)}, u32[]{:S(2)}, u32[]{:S(2)}) collective-permute-start(bf16[64,14336]{1,0:T(8,128)(2,1)} %refs_1_.3), channel_id=1, source_target_pairs={{0,4},{2,6},{4,0},{6,2},{8,12},{10,14},{12,8},{14,10},{1,5},{3,7},... | collective-permute-start | bytes 5505032 | tf_op jit(solution)/shard_map/ppermute | solution.py:184
  6.7 1.5 collective-permute-start
  8.2 2.7 constant_dynamic-slice_fusion.1
  10.9 5.1 %fusion.10 = (bf16[512,2048]{1,0:T(8,128)(2,1)}, f32[512,2048]{1,0:T(8,128)}) fusion(bf16[512,1024]{1,0:T(8,128)(2,1)S(1)} %copy-done, bf16[1024,1024]{1,0:T(8,128)(2,1)S(1)} %get-tuple-element.104, bf16[1024,1024]{1,0:T(8,128)(2,1)S(1)} %get-tuple-element.103), kind=kOutput, calls=%fused_computation.21 | convolution fusion | flops 2156920832 | bytes 11534336 | tf_op jit(solution)/shard_map/dot_general | solution.py:16
  16.0 3.3 %collective-permute-start.7 = (bf16[512,2048]{1,0:T(8,128)(2,1)}, bf16[512,2048]{1,0:T(8,128)(2,1)}, u32[]{:S(2)}, u32[]{:S(2)}) collective-permute-start(bf16[512,2048]{1,0:T(8,128)(2,1)} %get-tuple-element.105), channel_id=1, source_target_pairs={{0,4},{2,6},{12,8},{14,10},{1,5},{3,7},{13,9},{15,11},{16,20},{18,... | collective-permute-start | bytes 6291464 | tf_op jit(solution)/shard_map/ppermute | solution.py:184
  20.6 26.8 %collective-permute-done.1.refs_2_ = bf16[64,14336]{1,0:T(8,128)(2,1)} collective-permute-done((bf16[64,14336]{1,0:T(8,128)(2,1)}, bf16[64,14336]{1,0:T(8,128)(2,1)}, u32[]{:S(2)}, u32[]{:S(2)}) %collective-permute-start.1) | collective-permute-done | bytes 1835040 | tf_op jit(solution)/shard_map/ppermute | solution.py:184
  48.2 2.0 collective-permute-start.6
  50.2 3.4 %collective-permute-start.3 = (bf16[64,14336]{1,0:T(8,128)(2,1)}, bf16[64,14336]{1,0:T(8,128)(2,1)}, u32[]{:S(2)}, u32[]{:S(2)}) collective-permute-start(bf16[64,14336]{1,0:T(8,128)(2,1)} %collective-permute-done.1.refs_2_), channel_id=1, source_target_pairs={{0,2},{2,0},{12,14},{14,12},{1,3},{3,1},{13,15},{15,13},{16,18},{1... | collective-permute-start | bytes 5505032 | tf_op jit(solution)/shard_map/ppermute | solution.py:184
  54.9 1.9 collective-permute-start.4
  56.8 1.5 copy-done.2
  58.3 12.7 %rotate.5.refs_9_ = f32[192,1792]{1,0:T(8,128)S(1)} custom-call(s32[1]{0:T(128)} %bitcast.13.refs_0_.refs_1_, bf16[64,14336]{1,0:T(8,128)(2,1)S(1)} %copy-done.2, bf16[64,14336]{1,0:T(8,128)(2,1)} %collective-permute-done.1.refs_2_, bf16[64,14336]{1,0:T(8,128)(2,1)} %collective-permute-done.refs_3_, bf16[14336,1792]{1,0:T(8,128)(2,1)} %refs_7_.3), custom_call_target="tpu_custom_call" | custom-call | flops 344064 | bytes 1376256 | tf_op jit(solution)/shard_map/rotate/pallas_call | solution.py:125
  71.0 20.0 %collective-permute-done.7 = bf16[512,2048]{1,0:T(8,128)(2,1)} collective-permute-done((bf16[512,2048]{1,0:T(8,128)(2,1)}, bf16[512,2048]{1,0:T(8,128)(2,1)}, u32[]{:S(2)}, u32[]{:S(2)}) %collective-permute-start.7) | collective-permute-done | bytes 2097184 | tf_op jit(solution)/shard_map/ppermute | solution.py:184
  91.0 1.7 collective-permute-done.3.refs_3_.refs_6_
  92.6 2.9 %collective-permute-done.5.refs_1_.refs_4_ = bf16[64,14336]{1,0:T(8,128)(2,1)} collective-permute-done((bf16[64,14336]{1,0:T(8,128)(2,1)S(1)}, bf16[64,14336]{1,0:T(8,128)(2,1)}, u32[]{:S(2)}, u32[]{:S(2)}) %collective-permute-start.5) | collective-permute-done | bytes 1835040 | tf_op jit(solution)/shard_map/ppermute | solution.py:184
  95.6 2.4 collective-permute-start.11
  98.0 5.2 %collective-permute-start.10 = (bf16[64,14336]{1,0:T(8,128)(2,1)}, bf16[64,14336]{1,0:T(8,128)(2,1)S(1)}, u32[]{:S(2)}, u32[]{:S(2)}) collective-permute-start(bf16[64,14336]{1,0:T(8,128)(2,1)} %collective-permute-done.refs_3_), channel_id=1, source_target_pairs={{0,4},{2,6},{12,8},{14,10},{1,5},{3,7},{13,9},{15,11},{16,20},{18,... | collective-permute-start | bytes 5505032 | tf_op jit(solution)/shard_map/ppermute | solution.py:184
  105.3 11.9 %rotate.6.refs_10_ = f32[128,1792]{1,0:T(8,128)S(1)} custom-call(s32[1]{0:T(128)} %bitcast.13.refs_0_.refs_1_, bf16[64,14336]{1,0:T(8,128)(2,1)} %collective-permute-done.5.refs_1_.refs_4_, bf16[64,14336]{1,0:T(8,128)(2,1)S(1)} %collective-permute-done.2.refs_2_.refs_5_, bf16[64,14336]{1,0:T(8,128)(2,1)} %collective-permute-done.3.refs_3_.refs_6_, ...), custom_call_target="tpu_custom_call" | custom-call | flops 229376 | bytes 917504 | tf_op jit(solution)/shard_map/rotate/pallas_call | solution.py:125
  117.3 15.4 %rotate.7 = f32[320,1792]{1,0:T(8,128)S(1)} custom-call(s32[1]{0:T(128)} %bitcast.13.refs_0_.refs_1_, bf16[64,14336]{1,0:T(8,128)(2,1)S(1)} %copy-done.3, bf16[64,14336]{1,0:T(8,128)(2,1)} %collective-permute-done.1.refs_2_, bf16[64,14336]{1,0:T(8,128)(2,1)} %collective-permute-done.refs_3_, bf16[64,14336]{1,0:T(8,128)(2,1)} %collective-permute-done.5.refs_1_.refs_4_, ...), custom_call_target="tpu_custom_call" | custom-call | flops 573440 | bytes 2293760 | tf_op jit(solution)/shard_map/rotate/pallas_call | solution.py:125
  132.6 2.4 convert_add_fusion
  135.0 1.7 collective-permute-done.11.refs_3_
  136.7 3.0 %collective-permute-done.10.refs_6_ = bf16[64,14336]{1,0:T(8,128)(2,1)S(1)} collective-permute-done((bf16[64,14336]{1,0:T(8,128)(2,1)}, bf16[64,14336]{1,0:T(8,128)(2,1)S(1)}, u32[]{:S(2)}, u32[]{:S(2)}) %collective-permute-start.10) | collective-permute-done | bytes 1835040 | tf_op jit(solution)/shard_map/ppermute | solution.py:184
  139.7 4.1 %collective-permute-done.9.refs_1_ = bf16[64,14336]{1,0:T(8,128)(2,1)S(1)} collective-permute-done((bf16[64,14336]{1,0:T(8,128)(2,1)}, bf16[64,14336]{1,0:T(8,128)(2,1)S(1)}, u32[]{:S(2)}, u32[]{:S(2)}) %collective-permute-start.9) | collective-permute-done | bytes 1835040 | tf_op jit(solution)/shard_map/ppermute | solution.py:184
  144.6 3.6 %collective-permute-done.14 = f32[320,1792]{1,0:T(8,128)S(1)} collective-permute-done((f32[320,1792]{1,0:T(8,128)S(1)}, f32[320,1792]{1,0:T(8,128)S(1)}, u32[]{:S(2)}, u32[]{:S(2)}) %collective-permute-start.14) | collective-permute-done | bytes 2293792 | tf_op jit(solution)/shard_map/ppermute | solution.py:146
  149.3 2.4 collective-permute-start.12
  156.4 20.0 %collective-permute-done.12.refs_5_ = bf16[64,8192]{1,0:T(8,128)(2,1)S(1)} collective-permute-done((bf16[64,8192]{1,0:T(8,128)(2,1)S(1)}, bf16[64,8192]{1,0:T(8,128)(2,1)S(1)}, u32[]{:S(2)}, u32[]{:S(2)}) %collective-permute-start.12) | collective-permute-done | bytes 1048608 | tf_op jit(solution)/shard_map/ppermute | solution.py:184
  176.4 49.7 %collective-permute-done.18 = bf16[512,512]{1,0:T(8,128)(2,1)S(1)} collective-permute-done((bf16[512,512]{1,0:T(8,128)(2,1)S(1)}, bf16[512,512]{1,0:T(8,128)(2,1)S(1)}, u32[]{:S(2)}, u32[]{:S(2)}) %collective-permute-start.18) | collective-permute-done | bytes 524320 | tf_op jit(solution)/shard_map/ppermute | solution.py:184
  226.1 2.4 collective-permute-start.20
  232.2 14.1 %rotate.8.refs_8_ = f32[192,1792]{1,0:T(8,128)S(1)} custom-call(s32[1]{0:T(128)} %bitcast.13.refs_0_.refs_1_, bf16[64,14336]{1,0:T(8,128)(2,1)S(1)} %collective-permute-done.9.refs_1_, bf16[64,14336]{1,0:T(8,128)(2,1)} %collective-permute-done.6.refs_2_, bf16[64,14336]{1,0:T(8,128)(2,1)S(1)} %collective-permute-done.11.refs_3_, ...), custom_call_target="tpu_custom_call" | custom-call | flops 344064 | bytes 1376256 | tf_op jit(solution)/shard_map/rotate/pallas_call | solution.py:125
  249.4 7.4 %collective-permute-done.19 = bf16[512,512]{1,0:T(8,128)(2,1)S(1)} collective-permute-done((bf16[512,512]{1,0:T(8,128)(2,1)S(1)}, bf16[512,512]{1,0:T(8,128)(2,1)S(1)}, u32[]{:S(2)}, u32[]{:S(2)}) %collective-permute-start.19) | collective-permute-done | bytes 524320 | tf_op jit(solution)/shard_map/ppermute | solution.py:184
  256.7 10.8 %rotate.9.refs_4_ = f32[192,1792]{1,0:T(8,128)S(1)} custom-call(s32[1]{0:T(128)} %bitcast.13.refs_0_.refs_1_, bf16[64,14336]{1,0:T(8,128)(2,1)S(1)} %collective-permute-done.9.refs_1_, bf16[64,14336]{1,0:T(8,128)(2,1)} %collective-permute-done.6.refs_2_, bf16[64,14336]{1,0:T(8,128)(2,1)S(1)} %collective-permute-done.11.refs_3_, ...), custom_call_target="tpu_custom_call" | custom-call | flops 344064 | bytes 1376256 | tf_op jit(solution)/shard_map/rotate/pallas_call | solution.py:125
  268.5 3.1 %collective-permute-done.24.refs_5_ = f32[192,1792]{1,0:T(8,128)S(1)} collective-permute-done((f32[192,1792]{1,0:T(8,128)S(1)}, f32[192,1792]{1,0:T(8,128)S(1)}, u32[]{:S(2)}, u32[]{:S(2)}) %collective-permute-start.24) | collective-permute-done | bytes 1376288 | tf_op jit(solution)/shard_map/ppermute | solution.py:146
  272.8 12.5 %fit.1 = f32[1792,2048]{1,0:T(8,128)} custom-call(s32[8]{0:T(128)} %stack.50.refs_0_, s32[1]{0:T(128)} %bitcast.13.refs_0_.refs_1_, s32[4]{0:T(128)} %pad_add_fusion.refs_2_, bf16[320,1792]{1,0:T(8,128)(2,1)} %add_convert_fusion.refs_3_, f32[192,1792]{1,0:T(8,128)} %copy-done.4, f32[192,1792]{1,0:T(8,128)} %copy-done.6, ...), custom_call_target="tpu_custom_call" | custom-call | flops 3758096384 | bytes 24117248 | tf_op jit(solution)/shard_map/fit/pallas_call | solution.py:64
  (56 shorter events, 21.5 us)
Async XLA Ops:
  0.0 10.9 %copy-start = (bf16[512,1024]{1,0:T(8,128)(2,1)S(1)}, bf16[512,1024]{1,0:T(8,128)(2,1)}, u32[]{:S(2)}) copy-start(bf16[512,1024]{1,0:T(8,128)(2,1)} %param.5) | copy-start | bytes 3145732
  0.0 20.6 %collective-permute-start.2 = (bf16[64,14336]{1,0:T(8,128)(2,1)}, bf16[64,14336]{1,0:T(8,128)(2,1)S(1)}, u32[]{:S(2)}, u32[]{:S(2)}) collective-permute-start(bf16[64,14336]{1,0:T(8,128)(2,1)} %refs_1_.3), channel_id=1, source_target_pairs={{4,8},{6,10},{8,4},{10,6},{5,9},{7,11},{9,5},{11,7},{20,24},{22,26... | collective-permute-start | bytes 5505032 | tf_op jit(solution)/shard_map/ppermute | solution.py:184
  0.9 46.6 %collective-permute-start.1 = (bf16[64,14336]{1,0:T(8,128)(2,1)}, bf16[64,14336]{1,0:T(8,128)(2,1)}, u32[]{:S(2)}, u32[]{:S(2)}) collective-permute-start(bf16[64,14336]{1,0:T(8,128)(2,1)} %refs_1_.3), channel_id=1, source_target_pairs={{0,4},{2,6},{4,0},{6,2},{8,12},{10,14},{12,8},{14,10},{1,5},{3,7},... | collective-permute-start | bytes 5505032 | tf_op jit(solution)/shard_map/ppermute | solution.py:184
  6.7 41.5 %collective-permute-start = (bf16[64,14336]{1,0:T(8,128)(2,1)}, bf16[64,14336]{1,0:T(8,128)(2,1)}, u32[]{:S(2)}, u32[]{:S(2)}) collective-permute-start(bf16[64,14336]{1,0:T(8,128)(2,1)} %refs_1_.3), channel_id=1, source_target_pairs={{0,2},{2,0},{4,6},{6,4},{8,10},{10,8},{12,14},{14,12},{1,3},{3,1},... | collective-permute-start | bytes 5505032 | tf_op jit(solution)/shard_map/ppermute | solution.py:184
  16.0 75.0 %collective-permute-start.7 = (bf16[512,2048]{1,0:T(8,128)(2,1)}, bf16[512,2048]{1,0:T(8,128)(2,1)}, u32[]{:S(2)}, u32[]{:S(2)}) collective-permute-start(bf16[512,2048]{1,0:T(8,128)(2,1)} %get-tuple-element.105), channel_id=1, source_target_pairs={{0,4},{2,6},{12,8},{14,10},{1,5},{3,7},{13,9},{15,11},{16,20},{18,... | collective-permute-start | bytes 6291464 | tf_op jit(solution)/shard_map/ppermute | solution.py:184
  48.2 42.7 %collective-permute-start.6 = (bf16[64,14336]{1,0:T(8,128)(2,1)}, bf16[64,14336]{1,0:T(8,128)(2,1)}, u32[]{:S(2)}, u32[]{:S(2)}) collective-permute-start(bf16[64,14336]{1,0:T(8,128)(2,1)} %collective-permute-done.1.refs_2_), channel_id=1, source_target_pairs={{4,8},{6,10},{8,4},{10,6},{5,9},{7,11},{9,5},{11,7},{20,24},{22,26... | collective-permute-start | bytes 5505032 | tf_op jit(solution)/shard_map/ppermute | solution.py:184
  50.2 42.5 %collective-permute-start.3 = (bf16[64,14336]{1,0:T(8,128)(2,1)}, bf16[64,14336]{1,0:T(8,128)(2,1)}, u32[]{:S(2)}, u32[]{:S(2)}) collective-permute-start(bf16[64,14336]{1,0:T(8,128)(2,1)} %collective-permute-done.1.refs_2_), channel_id=1, source_target_pairs={{0,2},{2,0},{12,14},{14,12},{1,3},{3,1},{13,15},{15,13},{16,18},{1... | collective-permute-start | bytes 5505032 | tf_op jit(solution)/shard_map/ppermute | solution.py:184
  53.6 42.0 %collective-permute-start.5 = (bf16[64,14336]{1,0:T(8,128)(2,1)S(1)}, bf16[64,14336]{1,0:T(8,128)(2,1)}, u32[]{:S(2)}, u32[]{:S(2)}) collective-permute-start(bf16[64,14336]{1,0:T(8,128)(2,1)S(1)} %collective-permute-done.2.refs_2_.refs_5_), channel_id=1, source_target_pairs={{4,0},{6,2},{8,12},{10,14},{5,1},{7,3},{9,13},{11,15},{20,16},{22,... | collective-permute-start | bytes 5505032 | tf_op jit(solution)/shard_map/ppermute | solution.py:184
  54.9 40.7 %collective-permute-start.4 = (bf16[64,14336]{1,0:T(8,128)(2,1)S(1)}, bf16[64,14336]{1,0:T(8,128)(2,1)}, u32[]{:S(2)}, u32[]{:S(2)}) collective-permute-start(bf16[64,14336]{1,0:T(8,128)(2,1)S(1)} %collective-permute-done.2.refs_2_.refs_5_), channel_id=1, source_target_pairs={{4,6},{6,4},{8,10},{10,8},{5,7},{7,5},{9,11},{11,9},{20,22},{22,20... | collective-permute-start | bytes 5505032 | tf_op jit(solution)/shard_map/ppermute | solution.py:184
  71.0 46.3 %copy-start.3 = (bf16[64,14336]{1,0:T(8,128)(2,1)S(1)}, bf16[64,14336]{1,0:T(8,128)(2,1)}, u32[]{:S(2)}) copy-start(bf16[64,14336]{1,0:T(8,128)(2,1)} %refs_1_.3) | copy-start | bytes 5505028
  95.6 41.2 %collective-permute-start.11 = (bf16[64,14336]{1,0:T(8,128)(2,1)}, bf16[64,14336]{1,0:T(8,128)(2,1)S(1)}, u32[]{:S(2)}, u32[]{:S(2)}) collective-permute-start(bf16[64,14336]{1,0:T(8,128)(2,1)} %collective-permute-done.5.refs_1_.refs_4_), channel_id=1, source_target_pairs={{0,2},{2,0},{12,14},{14,12},{1,3},{3,1},{13,15},{15,13},{16,18},{1... | collective-permute-start | bytes 5505032 | tf_op jit(solution)/shard_map/ppermute | solution.py:184
  98.0 41.7 %collective-permute-start.10 = (bf16[64,14336]{1,0:T(8,128)(2,1)}, bf16[64,14336]{1,0:T(8,128)(2,1)S(1)}, u32[]{:S(2)}, u32[]{:S(2)}) collective-permute-start(bf16[64,14336]{1,0:T(8,128)(2,1)} %collective-permute-done.refs_3_), channel_id=1, source_target_pairs={{0,4},{2,6},{12,8},{14,10},{1,5},{3,7},{13,9},{15,11},{16,20},{18,... | collective-permute-start | bytes 5505032 | tf_op jit(solution)/shard_map/ppermute | solution.py:184
  103.2 40.6 %collective-permute-start.9 = (bf16[64,14336]{1,0:T(8,128)(2,1)}, bf16[64,14336]{1,0:T(8,128)(2,1)S(1)}, u32[]{:S(2)}, u32[]{:S(2)}) collective-permute-start(bf16[64,14336]{1,0:T(8,128)(2,1)} %collective-permute-done.6.refs_2_), channel_id=1, source_target_pairs={{4,0},{6,2},{8,12},{10,14},{5,1},{7,3},{9,13},{11,15},{20,16},{22,... | collective-permute-start | bytes 5505032 | tf_op jit(solution)/shard_map/ppermute | solution.py:184
  104.5 39.3 %collective-permute-start.8 = (bf16[64,14336]{1,0:T(8,128)(2,1)}, bf16[64,14336]{1,0:T(8,128)(2,1)S(1)}, u32[]{:S(2)}, u32[]{:S(2)}) collective-permute-start(bf16[64,14336]{1,0:T(8,128)(2,1)} %collective-permute-done.6.refs_2_), channel_id=1, source_target_pairs={{4,6},{6,4},{8,10},{10,8},{5,7},{7,5},{9,11},{11,9},{20,22},{22,20... | collective-permute-start | bytes 5505032 | tf_op jit(solution)/shard_map/ppermute | solution.py:184
  117.2 15.4 %copy-start.5 = (f32[512,2048]{1,0:T(8,128)S(1)}, f32[512,2048]{1,0:T(8,128)}, u32[]{:S(2)}) copy-start(f32[512,2048]{1,0:T(8,128)} %get-tuple-element.64) | copy-start | bytes 12582916
  143.8 4.4 %collective-permute-start.14 = (f32[320,1792]{1,0:T(8,128)S(1)}, f32[320,1792]{1,0:T(8,128)S(1)}, u32[]{:S(2)}, u32[]{:S(2)}) collective-permute-start(f32[320,1792]{1,0:T(8,128)S(1)} %rotate.7), channel_id=1, source_target_pairs={{0,1},{1,0},{2,3},{3,2},{4,5},{5,4},{6,7},{7,6},{8,9},{9,8},{10,11... | collective-permute-start | bytes 6881288 | tf_op jit(solution)/shard_map/ppermute | solution.py:146
  143.8 0.8 collective-permute-start.13
  148.5 3.2 %collective-permute-start.16 = (bf16[512,512]{1,0:T(8,128)(2,1)S(1)}, bf16[512,512]{1,0:T(8,128)(2,1)S(1)}, u32[]{:S(2)}, u32[]{:S(2)}) collective-permute-start(bf16[512,512]{1,0:T(8,128)(2,1)S(1)} %fusion.8), channel_id=1, source_target_pairs={{4,6},{6,4},{8,10},{10,8},{5,7},{7,5},{9,11},{11,9},{20,22},{22,20... | collective-permute-start | bytes 1572872 | tf_op jit(solution)/shard_map/ppermute | solution.py:184
  149.3 27.1 %collective-permute-start.12 = (bf16[64,8192]{1,0:T(8,128)(2,1)S(1)}, bf16[64,8192]{1,0:T(8,128)(2,1)S(1)}, u32[]{:S(2)}, u32[]{:S(2)}) collective-permute-start(bf16[64,8192]{1,0:T(8,128)(2,1)S(1)} %slice.32), channel_id=1, source_target_pairs={{0,2},{2,0},{12,14},{14,12},{1,3},{3,1},{13,15},{15,13},{16,18},{1... | collective-permute-start | bytes 3145736 | tf_op jit(solution)/shard_map/ppermute | solution.py:184
  152.4 73.7 %collective-permute-start.18 = (bf16[512,512]{1,0:T(8,128)(2,1)S(1)}, bf16[512,512]{1,0:T(8,128)(2,1)S(1)}, u32[]{:S(2)}, u32[]{:S(2)}) collective-permute-start(bf16[512,512]{1,0:T(8,128)(2,1)S(1)} %get-tuple-element.79), channel_id=1, source_target_pairs={{4,0},{6,2},{8,12},{10,14},{5,1},{7,3},{9,13},{11,15},{20,16},{22,... | collective-permute-start | bytes 1572872 | tf_op jit(solution)/shard_map/ppermute | solution.py:184
  153.7 72.4 %collective-permute-start.17 = (bf16[512,512]{1,0:T(8,128)(2,1)S(1)}, bf16[512,512]{1,0:T(8,128)(2,1)S(1)}, u32[]{:S(2)}, u32[]{:S(2)}) collective-permute-start(bf16[512,512]{1,0:T(8,128)(2,1)S(1)} %get-tuple-element.79), channel_id=1, source_target_pairs={{4,8},{6,10},{8,4},{10,6},{5,9},{7,11},{9,5},{11,7},{20,24},{22,26... | collective-permute-start | bytes 1572872 | tf_op jit(solution)/shard_map/ppermute | solution.py:184
  154.4 22.0 %collective-permute-start.15 = (bf16[512,512]{1,0:T(8,128)(2,1)S(1)}, bf16[512,512]{1,0:T(8,128)(2,1)S(1)}, u32[]{:S(2)}, u32[]{:S(2)}) collective-permute-start(bf16[512,512]{1,0:T(8,128)(2,1)S(1)} %get-tuple-element.102), channel_id=1, source_target_pairs={{4,6},{6,4},{8,10},{10,8},{5,7},{7,5},{9,11},{11,9},{20,22},{22,20... | collective-permute-start | bytes 1572872 | tf_op jit(solution)/shard_map/ppermute | solution.py:184
  226.1 21.1 %collective-permute-start.20 = (bf16[64,6144]{1,0:T(8,128)(2,1)S(1)}, bf16[64,6144]{1,0:T(8,128)(2,1)S(1)}, u32[]{:S(2)}, u32[]{:S(2)}) collective-permute-start(bf16[64,6144]{1,0:T(8,128)(2,1)S(1)} %slice.39), channel_id=1, source_target_pairs={{0,2},{2,0},{12,14},{14,12},{1,3},{3,1},{13,15},{15,13},{16,18},{1... | collective-permute-start | bytes 2359304 | tf_op jit(solution)/shard_map/ppermute | solution.py:184
  228.9 18.3 %collective-permute-start.22 = (bf16[512,512]{1,0:T(8,128)(2,1)S(1)}, bf16[512,512]{1,0:T(8,128)(2,1)S(1)}, u32[]{:S(2)}, u32[]{:S(2)}) collective-permute-start(bf16[512,512]{1,0:T(8,128)(2,1)S(1)} %add_convert_fusion.1), channel_id=1, source_target_pairs={{4,0},{6,2},{8,12},{10,14},{5,1},{7,3},{9,13},{11,15},{20,16},{22,... | collective-permute-start | bytes 1572872 | tf_op jit(solution)/shard_map/ppermute | solution.py:184
  230.2 17.0 %collective-permute-start.21 = (bf16[512,512]{1,0:T(8,128)(2,1)S(1)}, bf16[512,512]{1,0:T(8,128)(2,1)S(1)}, u32[]{:S(2)}, u32[]{:S(2)}) collective-permute-start(bf16[512,512]{1,0:T(8,128)(2,1)S(1)} %add_convert_fusion.1), channel_id=1, source_target_pairs={{4,8},{6,10},{8,4},{10,6},{5,9},{7,11},{9,5},{11,7},{20,24},{22,26... | collective-permute-start | bytes 1572872 | tf_op jit(solution)/shard_map/ppermute | solution.py:184
  230.9 25.8 %collective-permute-start.19 = (bf16[512,512]{1,0:T(8,128)(2,1)S(1)}, bf16[512,512]{1,0:T(8,128)(2,1)S(1)}, u32[]{:S(2)}, u32[]{:S(2)}) collective-permute-start(bf16[512,512]{1,0:T(8,128)(2,1)S(1)} %collective-permute-done.17), channel_id=1, source_target_pairs={{4,0},{6,2},{8,12},{10,14},{5,1},{7,3},{9,13},{11,15},{20,16},{22,... | collective-permute-start | bytes 1572872 | tf_op jit(solution)/shard_map/ppermute | solution.py:184
  247.2 20.4 %copy-start.7 = (bf16[512,512]{1,0:T(8,128)(2,1)}, bf16[512,512]{1,0:T(8,128)(2,1)S(1)}, u32[]{:S(2)}) copy-start(bf16[512,512]{1,0:T(8,128)(2,1)S(1)} %collective-permute-done.21.refs_10_) | copy-start | bytes 1572868
  247.2 21.3 %collective-permute-start.23 = (bf16[512,512]{1,0:T(8,128)(2,1)S(1)}, bf16[512,512]{1,0:T(8,128)(2,1)S(1)}, u32[]{:S(2)}, u32[]{:S(2)}) collective-permute-start(bf16[512,512]{1,0:T(8,128)(2,1)S(1)} %collective-permute-done.21.refs_10_), channel_id=1, source_target_pairs={{4,0},{6,2},{8,12},{10,14},{5,1},{7,3},{9,13},{11,15},{20,16},{22,... | collective-permute-start | bytes 1572872 | tf_op jit(solution)/shard_map/ppermute | solution.py:184
  267.6 4.1 %copy-start.4 = (f32[192,1792]{1,0:T(8,128)}, f32[192,1792]{1,0:T(8,128)S(1)}, u32[]{:S(2)}) copy-start(f32[192,1792]{1,0:T(8,128)S(1)} %rotate.9.refs_4_) | copy-start | bytes 4128772
  268.5 3.1 %copy-start.8 = (bf16[512,512]{1,0:T(8,128)(2,1)}, bf16[512,512]{1,0:T(8,128)(2,1)S(1)}, u32[]{:S(2)}) copy-start(bf16[512,512]{1,0:T(8,128)(2,1)S(1)} %collective-permute-done.23.refs_9_) | copy-start | bytes 1572868
  268.5 3.1 %collective-permute-start.24 = (f32[192,1792]{1,0:T(8,128)S(1)}, f32[192,1792]{1,0:T(8,128)S(1)}, u32[]{:S(2)}, u32[]{:S(2)}) collective-permute-start(f32[192,1792]{1,0:T(8,128)S(1)} %rotate.9.refs_4_), channel_id=1, source_target_pairs={{0,1},{1,0},{2,3},{3,2},{4,5},{5,4},{6,7},{7,6},{8,9},{9,8},{10,11... | collective-permute-start | bytes 4128776 | tf_op jit(solution)/shard_map/ppermute | solution.py:146
  272.8 12.5 %copy-start.1 = (bf16[512,1024]{1,0:T(8,128)(2,1)S(1)}, bf16[512,1024]{1,0:T(8,128)(2,1)}, u32[]{:S(2)}) copy-start(bf16[512,1024]{1,0:T(8,128)(2,1)} %param.5) | copy-start | bytes 3145732
  (2 other events, 2.6 us)

commit v13 on v12

--- a/solution.py
+++ b/solution.py
@@ -262,21 +262,21 @@
         got["x5", p] = send(got["keep", p].astype(BF16), ACROSS_MIDDLE)
 
     x4(0)
-    got["A2"] = swap_narrow(got["A"])
-    fence("m3", "A", "A2")
+    fence("m3", "A")
     cross(0)
     cross(1)
     fence(("x5", 0), "a3")
     settle(0)
-    got["A"] = (got["A"] + got["A2"]).astype(BF16)
     fence(("x4", 0), ("x5", 1), ("m4", 0), ("n1", 0), ("sum", 0), "A", "a3")
     x4(1)
     settle(1)
     got["n2", 0] = send(got["m4", 0], TO_ENDS)
+    got["A2"] = swap_narrow(got["A"])
     got["R", 0] = pick(("n1", 0), ("sum", 0))
     last(0)
-    fence(("x4", 1), ("m4", 1), ("n1", 1), ("sum", 1), ("R", 0), "D")
+    fence(("x4", 1), ("m4", 1), ("n1", 1), ("sum", 1), ("R", 0), "A2", "D")
     got["n2", 1] = send(got["m4", 1], TO_ENDS)
+    got["A"] = (got["A"] + got["A2"]).astype(BF16)
     got["R", 1] = pick(("n1", 1), ("sum", 1))
     fence(("n2", 0), ("m4", 0), ("R", 1), "A", "D")
     got["R", 2] = pick(("n2", 0), ("m4", 0))

time: 286 us -> 237 us (0.83)
  waiting for transfers between devices: 145 us -> 92.4 us
    ppermute x23, waiting for transfers between devices: 138 us -> 89.3 us  [send(): return lax.ppermute(a, 'wide', perm)]
    ppermute x2, waiting for transfers between devices: 6.76 us -> 3.13 us  [swap_narrow(): return lax.ppermute(a, 'narrow', [(0, 1), (1, 0)])]
  transfers between devices with their start and end apart: 25 -> 25, of which waited for: 13 -> 12; matrix products, arithmetic and copies ran while one was open for 6% -> 6% of each run, Pallas kernels for 23% -> 28%
where the time goes in v13:
time: 237 us; the launch traced here: 236 us
  waiting for transfers between devices  92.4 us (39%)
  Pallas kernels  77.8 us (33%)
  starting transfers between devices  45.9 us (19%)
  other arithmetic  8.3 us (4%)
  local copies, waits for them, and re-layouts  6.06 us (3%)
  matrix products  5.12 us (2%)
    ppermute x23, waiting for transfers between devices, send(): return lax.ppermute(a, 'wide', perm)  89.3 us
    pallas_call x5, Pallas kernels, rotate(): pl.pallas_call(lambda *refs: rotate_kernel([len(block) for block in block...  65.3 us
    ppermute x23, starting transfers between devices, send(): return lax.ppermute(a, 'wide', perm)  45.9 us
    pallas_call x1, Pallas kernels, fit(): pl.pallas_call(lambda *refs: fit_kernel([len(halves) for halves in sums],...  12.5 us
    dot_general x1, matrix products, dot(): return jnp.dot(a, b, preferred_element_type=F32)  5.12 us
  transfers between devices with their start and end apart: 25, of which 12 were waited for; matrix products, arithmetic and copies ran while one was open for 6% of the time, Pallas kernels for 28%

profile of v13, /device:TPU:0, one launch (start us, length us, event | category | flops | bytes accessed | tf_op | source)
XLA Modules:
  0.0 235.9 jit_solution(16652610866392192882)
XLA Ops:
  0.9 5.8 %collective-permute-start.1 = (bf16[64,14336]{1,0:T(8,128)(2,1)}, bf16[64,14336]{1,0:T(8,128)(2,1)}, u32[]{:S(2)}, u32[]{:S(2)}) collective-permute-start(bf16[64,14336]{1,0:T(8,128)(2,1)} %refs_1_.3), channel_id=1, source_target_pairs={{0,4},{2,6},{4,0},{6,2},{8,12},{10,14},{12,8},{14,10},{1,5},{3,7},... | collective-permute-start | bytes 5505032 | tf_op jit(solution)/shard_map/ppermute | solution.py:184
  6.7 1.5 collective-permute-start
  8.2 2.7 %constant_dynamic-slice_fusion.1 = (bf16[1024,1024]{1,0:T(8,128)(2,1)S(1)}, bf16[1024,1024]{1,0:T(8,128)(2,1)S(1)}) fusion(bf16[1024,2048]{1,0:T(8,128)(2,1)} %param.7, s32[]{:T(128)S(6)} %select_n.56, s32[]{:T(128)S(6)} %select_n.57), kind=kLoop, calls=%fused_computation.19 | loop fusion | bytes 8388616 | tf_op jit(solution)/shard_map/dynamic_slice | solution.py:205
  10.9 5.1 %fusion.10 = (bf16[512,2048]{1,0:T(8,128)(2,1)}, f32[512,2048]{1,0:T(8,128)}) fusion(bf16[512,1024]{1,0:T(8,128)(2,1)S(1)} %copy-done, bf16[1024,1024]{1,0:T(8,128)(2,1)S(1)} %get-tuple-element.104, bf16[1024,1024]{1,0:T(8,128)(2,1)S(1)} %get-tuple-element.103), kind=kOutput, calls=%fused_computation.21 | convolution fusion | flops 2156920832 | bytes 11534336 | tf_op jit(solution)/shard_map/dot_general | solution.py:16
  16.0 3.3 %collective-permute-start.7 = (bf16[512,2048]{1,0:T(8,128)(2,1)}, bf16[512,2048]{1,0:T(8,128)(2,1)}, u32[]{:S(2)}, u32[]{:S(2)}) collective-permute-start(bf16[512,2048]{1,0:T(8,128)(2,1)} %get-tuple-element.105), channel_id=1, source_target_pairs={{0,4},{2,6},{12,8},{14,10},{1,5},{3,7},{13,9},{15,11},{16,20},{18,... | collective-permute-start | bytes 6291464 | tf_op jit(solution)/shard_map/ppermute | solution.py:184
  20.6 26.8 %collective-permute-done.1.refs_2_ = bf16[64,14336]{1,0:T(8,128)(2,1)} collective-permute-done((bf16[64,14336]{1,0:T(8,128)(2,1)}, bf16[64,14336]{1,0:T(8,128)(2,1)}, u32[]{:S(2)}, u32[]{:S(2)}) %collective-permute-start.1) | collective-permute-done | bytes 1835040 | tf_op jit(solution)/shard_map/ppermute | solution.py:184
  48.2 2.0 collective-permute-start.6
  50.2 3.4 %collective-permute-start.3 = (bf16[64,14336]{1,0:T(8,128)(2,1)}, bf16[64,14336]{1,0:T(8,128)(2,1)}, u32[]{:S(2)}, u32[]{:S(2)}) collective-permute-start(bf16[64,14336]{1,0:T(8,128)(2,1)} %collective-permute-done.1.refs_2_), channel_id=1, source_target_pairs={{0,2},{2,0},{12,14},{14,12},{1,3},{3,1},{13,15},{15,13},{16,18},{1... | collective-permute-start | bytes 5505032 | tf_op jit(solution)/shard_map/ppermute | solution.py:184
  53.6 1.3 collective-permute-start.5
  54.9 1.9 collective-permute-start.4
  56.8 1.5 copy-done.2
  58.3 13.1 %rotate.5.refs_9_ = f32[192,1792]{1,0:T(8,128)S(1)} custom-call(s32[1]{0:T(128)} %bitcast.13.refs_0_.refs_1_, bf16[64,14336]{1,0:T(8,128)(2,1)S(1)} %copy-done.2, bf16[64,14336]{1,0:T(8,128)(2,1)} %collective-permute-done.1.refs_2_, bf16[64,14336]{1,0:T(8,128)(2,1)} %collective-permute-done.refs_3_, bf16[14336,1792]{1,0:T(8,128)(2,1)} %refs_7_.3), custom_call_target="tpu_custom_call" | custom-call | flops 344064 | bytes 1376256 | tf_op jit(solution)/shard_map/rotate/pallas_call | solution.py:125
  71.4 19.6 %collective-permute-done.7 = bf16[512,2048]{1,0:T(8,128)(2,1)} collective-permute-done((bf16[512,2048]{1,0:T(8,128)(2,1)}, bf16[512,2048]{1,0:T(8,128)(2,1)}, u32[]{:S(2)}, u32[]{:S(2)}) %collective-permute-start.7) | collective-permute-done | bytes 2097184 | tf_op jit(solution)/shard_map/ppermute | solution.py:184
  91.0 1.7 collective-permute-done.3.refs_3_.refs_6_
  92.6 2.9 %collective-permute-done.5.refs_1_.refs_4_ = bf16[64,14336]{1,0:T(8,128)(2,1)} collective-permute-done((bf16[64,14336]{1,0:T(8,128)(2,1)S(1)}, bf16[64,14336]{1,0:T(8,128)(2,1)}, u32[]{:S(2)}, u32[]{:S(2)}) %collective-permute-start.5) | collective-permute-done | bytes 1835040 | tf_op jit(solution)/shard_map/ppermute | solution.py:184
  95.6 2.6 %convert_add_fusion = (f32[512,1024]{1,0:T(8,128)S(1)}, f32[512,1024]{1,0:T(8,128)S(1)}) fusion(f32[512,2048]{1,0:T(8,128)S(1)} %copy-done.5, bf16[512,2048]{1,0:T(8,128)(2,1)} %collective-permute-done.7), kind=kLoop, calls=%fused_computation.6 | loop fusion | flops 2097152 | bytes 10485760 | tf_op jit(solution)/shard_map/add | solution.py:241
  99.1 2.4 %collective-permute-start.11 = (bf16[64,14336]{1,0:T(8,128)(2,1)}, bf16[64,14336]{1,0:T(8,128)(2,1)S(1)}, u32[]{:S(2)}, u32[]{:S(2)}) collective-permute-start(bf16[64,14336]{1,0:T(8,128)(2,1)} %collective-permute-done.5.refs_1_.refs_4_), channel_id=1, source_target_pairs={{0,2},{2,0},{12,14},{14,12},{1,3},{3,1},{13,15},{15,13},{16,18},{1... | collective-permute-start | bytes 5505032 | tf_op jit(solution)/shard_map/ppermute | solution.py:184
  101.5 6.8 %collective-permute-start.10 = (bf16[64,14336]{1,0:T(8,128)(2,1)}, bf16[64,14336]{1,0:T(8,128)(2,1)S(1)}, u32[]{:S(2)}, u32[]{:S(2)}) collective-permute-start(bf16[64,14336]{1,0:T(8,128)(2,1)} %collective-permute-done.refs_3_), channel_id=1, source_target_pairs={{0,4},{2,6},{12,8},{14,10},{1,5},{3,7},{13,9},{15,11},{16,20},{18,... | collective-permute-start | bytes 5505032 | tf_op jit(solution)/shard_map/ppermute | solution.py:184
  110.4 11.9 %rotate.6.refs_10_ = f32[128,1792]{1,0:T(8,128)S(1)} custom-call(s32[1]{0:T(128)} %bitcast.13.refs_0_.refs_1_, bf16[64,14336]{1,0:T(8,128)(2,1)} %collective-permute-done.5.refs_1_.refs_4_, bf16[64,14336]{1,0:T(8,128)(2,1)S(1)} %collective-permute-done.2.refs_2_.refs_5_, bf16[64,14336]{1,0:T(8,128)(2,1)} %collective-permute-done.3.refs_3_.refs_6_, ...), custom_call_target="tpu_custom_call" | custom-call | flops 229376 | bytes 917504 | tf_op jit(solution)/shard_map/rotate/pallas_call | solution.py:125
  122.3 15.3 %rotate.7 = f32[320,1792]{1,0:T(8,128)S(1)} custom-call(s32[1]{0:T(128)} %bitcast.13.refs_0_.refs_1_, bf16[64,14336]{1,0:T(8,128)(2,1)S(1)} %copy-done.3, bf16[64,14336]{1,0:T(8,128)(2,1)} %collective-permute-done.1.refs_2_, bf16[64,14336]{1,0:T(8,128)(2,1)} %collective-permute-done.refs_3_, bf16[64,14336]{1,0:T(8,128)(2,1)} %collective-permute-done.5.refs_1_.refs_4_, ...), custom_call_target="tpu_custom_call" | custom-call | flops 573440 | bytes 2293760 | tf_op jit(solution)/shard_map/rotate/pallas_call | solution.py:125
  137.6 2.6 %collective-permute-done.11.refs_3_ = bf16[64,14336]{1,0:T(8,128)(2,1)S(1)} collective-permute-done((bf16[64,14336]{1,0:T(8,128)(2,1)}, bf16[64,14336]{1,0:T(8,128)(2,1)S(1)}, u32[]{:S(2)}, u32[]{:S(2)}) %collective-permute-start.11) | collective-permute-done | bytes 1835040 | tf_op jit(solution)/shard_map/ppermute | solution.py:184
  140.2 4.3 %collective-permute-done.10.refs_6_ = bf16[64,14336]{1,0:T(8,128)(2,1)S(1)} collective-permute-done((bf16[64,14336]{1,0:T(8,128)(2,1)}, bf16[64,14336]{1,0:T(8,128)(2,1)S(1)}, u32[]{:S(2)}, u32[]{:S(2)}) %collective-permute-start.10) | collective-permute-done | bytes 1835040 | tf_op jit(solution)/shard_map/ppermute | solution.py:184
  144.5 4.1 %collective-permute-done.9.refs_1_ = bf16[64,14336]{1,0:T(8,128)(2,1)S(1)} collective-permute-done((bf16[64,14336]{1,0:T(8,128)(2,1)}, bf16[64,14336]{1,0:T(8,128)(2,1)S(1)}, u32[]{:S(2)}, u32[]{:S(2)}) %collective-permute-start.9) | collective-permute-done | bytes 1835040 | tf_op jit(solution)/shard_map/ppermute | solution.py:184
  149.7 2.3 collective-permute-start.12
  155.3 16.7 %collective-permute-done.12.refs_5_ = bf16[64,8192]{1,0:T(8,128)(2,1)S(1)} collective-permute-done((bf16[64,8192]{1,0:T(8,128)(2,1)S(1)}, bf16[64,8192]{1,0:T(8,128)(2,1)S(1)}, u32[]{:S(2)}, u32[]{:S(2)}) %collective-permute-start.12) | collective-permute-done | bytes 1048608 | tf_op jit(solution)/shard_map/ppermute | solution.py:184
  172.0 4.1 %collective-permute-done.17 = bf16[512,512]{1,0:T(8,128)(2,1)S(1)} collective-permute-done((bf16[512,512]{1,0:T(8,128)(2,1)S(1)}, bf16[512,512]{1,0:T(8,128)(2,1)S(1)}, u32[]{:S(2)}, u32[]{:S(2)}) %collective-permute-start.17) | collective-permute-done | bytes 524320 | tf_op jit(solution)/shard_map/ppermute | solution.py:184
  176.2 3.4 %collective-permute-start.19 = (bf16[64,6144]{1,0:T(8,128)(2,1)S(1)}, bf16[64,6144]{1,0:T(8,128)(2,1)S(1)}, u32[]{:S(2)}, u32[]{:S(2)}) collective-permute-start(bf16[64,6144]{1,0:T(8,128)(2,1)S(1)} %slice.39), channel_id=1, source_target_pairs={{0,2},{2,0},{12,14},{14,12},{1,3},{3,1},{13,15},{15,13},{16,18},{1... | collective-permute-start | bytes 2359304 | tf_op jit(solution)/shard_map/ppermute | solution.py:184
  183.2 14.2 %rotate.8.refs_8_ = f32[192,1792]{1,0:T(8,128)S(1)} custom-call(s32[1]{0:T(128)} %bitcast.13.refs_0_.refs_1_, bf16[64,14336]{1,0:T(8,128)(2,1)S(1)} %collective-permute-done.9.refs_1_, bf16[64,14336]{1,0:T(8,128)(2,1)} %collective-permute-done.6.refs_2_, bf16[64,14336]{1,0:T(8,128)(2,1)S(1)} %collective-permute-done.11.refs_3_, ...), custom_call_target="tpu_custom_call" | custom-call | flops 344064 | bytes 1376256 | tf_op jit(solution)/shard_map/rotate/pallas_call | solution.py:125
  201.7 5.6 %collective-permute-done.18 = bf16[512,512]{1,0:T(8,128)(2,1)S(1)} collective-permute-done((bf16[512,512]{1,0:T(8,128)(2,1)S(1)}, bf16[512,512]{1,0:T(8,128)(2,1)S(1)}, u32[]{:S(2)}, u32[]{:S(2)}) %collective-permute-start.18) | collective-permute-done | bytes 524320 | tf_op jit(solution)/shard_map/ppermute | solution.py:184
  207.3 10.8 %rotate.9.refs_4_ = f32[192,1792]{1,0:T(8,128)S(1)} custom-call(s32[1]{0:T(128)} %bitcast.13.refs_0_.refs_1_, bf16[64,14336]{1,0:T(8,128)(2,1)S(1)} %collective-permute-done.9.refs_1_, bf16[64,14336]{1,0:T(8,128)(2,1)} %collective-permute-done.6.refs_2_, bf16[64,14336]{1,0:T(8,128)(2,1)S(1)} %collective-permute-done.11.refs_3_, ...), custom_call_target="tpu_custom_call" | custom-call | flops 344064 | bytes 1376256 | tf_op jit(solution)/shard_map/rotate/pallas_call | solution.py:125
  219.1 3.1 %collective-permute-done.24.refs_5_ = f32[192,1792]{1,0:T(8,128)S(1)} collective-permute-done((f32[192,1792]{1,0:T(8,128)S(1)}, f32[192,1792]{1,0:T(8,128)S(1)}, u32[]{:S(2)}, u32[]{:S(2)}) %collective-permute-start.24) | collective-permute-done | bytes 1376288 | tf_op jit(solution)/shard_map/ppermute | solution.py:146
  223.4 12.5 %fit.1 = f32[1792,2048]{1,0:T(8,128)} custom-call(s32[8]{0:T(128)} %stack.50.refs_0_, s32[1]{0:T(128)} %bitcast.13.refs_0_.refs_1_, s32[4]{0:T(128)} %pad_add_fusion.refs_2_, bf16[320,1792]{1,0:T(8,128)(2,1)} %add_convert_fusion.refs_3_, f32[192,1792]{1,0:T(8,128)} %copy-done.4, f32[192,1792]{1,0:T(8,128)} %copy-done.6, ...), custom_call_target="tpu_custom_call" | custom-call | flops 3758096384 | bytes 24117248 | tf_op jit(solution)/shard_map/fit/pallas_call | solution.py:64
  (56 shorter events, 20.2 us)
Async XLA Ops:
  0.0 10.9 %copy-start = (bf16[512,1024]{1,0:T(8,128)(2,1)S(1)}, bf16[512,1024]{1,0:T(8,128)(2,1)}, u32[]{:S(2)}) copy-start(bf16[512,1024]{1,0:T(8,128)(2,1)} %param.5) | copy-start | bytes 3145732
  0.0 20.6 %collective-permute-start.2 = (bf16[64,14336]{1,0:T(8,128)(2,1)}, bf16[64,14336]{1,0:T(8,128)(2,1)S(1)}, u32[]{:S(2)}, u32[]{:S(2)}) collective-permute-start(bf16[64,14336]{1,0:T(8,128)(2,1)} %refs_1_.3), channel_id=1, source_target_pairs={{4,8},{6,10},{8,4},{10,6},{5,9},{7,11},{9,5},{11,7},{20,24},{22,26... | collective-permute-start | bytes 5505032 | tf_op jit(solution)/shard_map/ppermute | solution.py:184
  0.9 46.6 %collective-permute-start.1 = (bf16[64,14336]{1,0:T(8,128)(2,1)}, bf16[64,14336]{1,0:T(8,128)(2,1)}, u32[]{:S(2)}, u32[]{:S(2)}) collective-permute-start(bf16[64,14336]{1,0:T(8,128)(2,1)} %refs_1_.3), channel_id=1, source_target_pairs={{0,4},{2,6},{4,0},{6,2},{8,12},{10,14},{12,8},{14,10},{1,5},{3,7},... | collective-permute-start | bytes 5505032 | tf_op jit(solution)/shard_map/ppermute | solution.py:184
  6.7 41.5 %collective-permute-start = (bf16[64,14336]{1,0:T(8,128)(2,1)}, bf16[64,14336]{1,0:T(8,128)(2,1)}, u32[]{:S(2)}, u32[]{:S(2)}) collective-permute-start(bf16[64,14336]{1,0:T(8,128)(2,1)} %refs_1_.3), channel_id=1, source_target_pairs={{0,2},{2,0},{4,6},{6,4},{8,10},{10,8},{12,14},{14,12},{1,3},{3,1},... | collective-permute-start | bytes 5505032 | tf_op jit(solution)/shard_map/ppermute | solution.py:184
  16.0 75.0 %collective-permute-start.7 = (bf16[512,2048]{1,0:T(8,128)(2,1)}, bf16[512,2048]{1,0:T(8,128)(2,1)}, u32[]{:S(2)}, u32[]{:S(2)}) collective-permute-start(bf16[512,2048]{1,0:T(8,128)(2,1)} %get-tuple-element.105), channel_id=1, source_target_pairs={{0,4},{2,6},{12,8},{14,10},{1,5},{3,7},{13,9},{15,11},{16,20},{18,... | collective-permute-start | bytes 6291464 | tf_op jit(solution)/shard_map/ppermute | solution.py:184
  48.2 42.7 %collective-permute-start.6 = (bf16[64,14336]{1,0:T(8,128)(2,1)}, bf16[64,14336]{1,0:T(8,128)(2,1)}, u32[]{:S(2)}, u32[]{:S(2)}) collective-permute-start(bf16[64,14336]{1,0:T(8,128)(2,1)} %collective-permute-done.1.refs_2_), channel_id=1, source_target_pairs={{4,8},{6,10},{8,4},{10,6},{5,9},{7,11},{9,5},{11,7},{20,24},{22,26... | collective-permute-start | bytes 5505032 | tf_op jit(solution)/shard_map/ppermute | solution.py:184
  50.2 42.5 %collective-permute-start.3 = (bf16[64,14336]{1,0:T(8,128)(2,1)}, bf16[64,14336]{1,0:T(8,128)(2,1)}, u32[]{:S(2)}, u32[]{:S(2)}) collective-permute-start(bf16[64,14336]{1,0:T(8,128)(2,1)} %collective-permute-done.1.refs_2_), channel_id=1, source_target_pairs={{0,2},{2,0},{12,14},{14,12},{1,3},{3,1},{13,15},{15,13},{16,18},{1... | collective-permute-start | bytes 5505032 | tf_op jit(solution)/shard_map/ppermute | solution.py:184
  53.6 42.0 %collective-permute-start.5 = (bf16[64,14336]{1,0:T(8,128)(2,1)S(1)}, bf16[64,14336]{1,0:T(8,128)(2,1)}, u32[]{:S(2)}, u32[]{:S(2)}) collective-permute-start(bf16[64,14336]{1,0:T(8,128)(2,1)S(1)} %collective-permute-done.2.refs_2_.refs_5_), channel_id=1, source_target_pairs={{4,0},{6,2},{8,12},{10,14},{5,1},{7,3},{9,13},{11,15},{20,16},{22,... | collective-permute-start | bytes 5505032 | tf_op jit(solution)/shard_map/ppermute | solution.py:184
  54.9 40.7 %collective-permute-start.4 = (bf16[64,14336]{1,0:T(8,128)(2,1)S(1)}, bf16[64,14336]{1,0:T(8,128)(2,1)}, u32[]{:S(2)}, u32[]{:S(2)}) collective-permute-start(bf16[64,14336]{1,0:T(8,128)(2,1)S(1)} %collective-permute-done.2.refs_2_.refs_5_), channel_id=1, source_target_pairs={{4,6},{6,4},{8,10},{10,8},{5,7},{7,5},{9,11},{11,9},{20,22},{22,20... | collective-permute-start | bytes 5505032 | tf_op jit(solution)/shard_map/ppermute | solution.py:184
  56.8 1.5 copy-start.2
  58.3 37.3 %copy-start.5 = (f32[512,2048]{1,0:T(8,128)S(1)}, f32[512,2048]{1,0:T(8,128)}, u32[]{:S(2)}) copy-start(f32[512,2048]{1,0:T(8,128)} %get-tuple-element.64) | copy-start | bytes 12582916
  98.1 24.2 %copy-start.3 = (bf16[64,14336]{1,0:T(8,128)(2,1)S(1)}, bf16[64,14336]{1,0:T(8,128)(2,1)}, u32[]{:S(2)}) copy-start(bf16[64,14336]{1,0:T(8,128)(2,1)} %refs_1_.3) | copy-start | bytes 5505028
  98.1 50.5 %collective-permute-start.13 = (f32[512,1024]{1,0:T(8,128)S(1)}, f32[512,1024]{1,0:T(8,128)S(1)}, u32[]{:S(2)}, u32[]{:S(2)}) collective-permute-start(f32[512,1024]{1,0:T(8,128)S(1)} %get-tuple-element.99), channel_id=1, source_target_pairs={{4,8},{6,10},{8,4},{10,6},{5,9},{7,11},{9,5},{11,7},{20,24},{22,26... | collective-permute-start | bytes 6291464 | tf_op jit(solution)/shard_map/ppermute | solution.py:184
  99.1 41.2 %collective-permute-start.11 = (bf16[64,14336]{1,0:T(8,128)(2,1)}, bf16[64,14336]{1,0:T(8,128)(2,1)S(1)}, u32[]{:S(2)}, u32[]{:S(2)}) collective-permute-start(bf16[64,14336]{1,0:T(8,128)(2,1)} %collective-permute-done.5.refs_1_.refs_4_), channel_id=1, source_target_pairs={{0,2},{2,0},{12,14},{14,12},{1,3},{3,1},{13,15},{15,13},{16,18},{1... | collective-permute-start | bytes 5505032 | tf_op jit(solution)/shard_map/ppermute | solution.py:184
  101.5 43.0 %collective-permute-start.10 = (bf16[64,14336]{1,0:T(8,128)(2,1)}, bf16[64,14336]{1,0:T(8,128)(2,1)S(1)}, u32[]{:S(2)}, u32[]{:S(2)}) collective-permute-start(bf16[64,14336]{1,0:T(8,128)(2,1)} %collective-permute-done.refs_3_), channel_id=1, source_target_pairs={{0,4},{2,6},{12,8},{14,10},{1,5},{3,7},{13,9},{15,11},{16,20},{18,... | collective-permute-start | bytes 5505032 | tf_op jit(solution)/shard_map/ppermute | solution.py:184
  108.3 40.3 %collective-permute-start.9 = (bf16[64,14336]{1,0:T(8,128)(2,1)}, bf16[64,14336]{1,0:T(8,128)(2,1)S(1)}, u32[]{:S(2)}, u32[]{:S(2)}) collective-permute-start(bf16[64,14336]{1,0:T(8,128)(2,1)} %collective-permute-done.6.refs_2_), channel_id=1, source_target_pairs={{4,0},{6,2},{8,12},{10,14},{5,1},{7,3},{9,13},{11,15},{20,16},{22,... | collective-permute-start | bytes 5505032 | tf_op jit(solution)/shard_map/ppermute | solution.py:184
  109.6 39.0 %collective-permute-start.8 = (bf16[64,14336]{1,0:T(8,128)(2,1)}, bf16[64,14336]{1,0:T(8,128)(2,1)S(1)}, u32[]{:S(2)}, u32[]{:S(2)}) collective-permute-start(bf16[64,14336]{1,0:T(8,128)(2,1)} %collective-permute-done.6.refs_2_), channel_id=1, source_target_pairs={{4,6},{6,4},{8,10},{10,8},{5,7},{7,5},{9,11},{11,9},{20,22},{22,20... | collective-permute-start | bytes 5505032 | tf_op jit(solution)/shard_map/ppermute | solution.py:184
  148.9 3.1 %collective-permute-start.15 = (bf16[512,512]{1,0:T(8,128)(2,1)S(1)}, bf16[512,512]{1,0:T(8,128)(2,1)S(1)}, u32[]{:S(2)}, u32[]{:S(2)}) collective-permute-start(bf16[512,512]{1,0:T(8,128)(2,1)S(1)} %fusion.8), channel_id=1, source_target_pairs={{4,6},{6,4},{8,10},{10,8},{5,7},{7,5},{9,11},{11,9},{20,22},{22,20... | collective-permute-start | bytes 1572872 | tf_op jit(solution)/shard_map/ppermute | solution.py:184
  149.7 22.3 %collective-permute-start.12 = (bf16[64,8192]{1,0:T(8,128)(2,1)S(1)}, bf16[64,8192]{1,0:T(8,128)(2,1)S(1)}, u32[]{:S(2)}, u32[]{:S(2)}) collective-permute-start(bf16[64,8192]{1,0:T(8,128)(2,1)S(1)} %slice.32), channel_id=1, source_target_pairs={{0,2},{2,0},{12,14},{14,12},{1,3},{3,1},{13,15},{15,13},{16,18},{1... | collective-permute-start | bytes 3145736 | tf_op jit(solution)/shard_map/ppermute | solution.py:184
  152.6 19.4 %collective-permute-start.14 = (bf16[512,512]{1,0:T(8,128)(2,1)S(1)}, bf16[512,512]{1,0:T(8,128)(2,1)S(1)}, u32[]{:S(2)}, u32[]{:S(2)}) collective-permute-start(bf16[512,512]{1,0:T(8,128)(2,1)S(1)} %get-tuple-element.102), channel_id=1, source_target_pairs={{4,6},{6,4},{8,10},{10,8},{5,7},{7,5},{9,11},{11,9},{20,22},{22,20... | collective-permute-start | bytes 1572872 | tf_op jit(solution)/shard_map/ppermute | solution.py:184
  153.3 22.8 %collective-permute-start.17 = (bf16[512,512]{1,0:T(8,128)(2,1)S(1)}, bf16[512,512]{1,0:T(8,128)(2,1)S(1)}, u32[]{:S(2)}, u32[]{:S(2)}) collective-permute-start(bf16[512,512]{1,0:T(8,128)(2,1)S(1)} %get-tuple-element.78), channel_id=1, source_target_pairs={{4,0},{6,2},{8,12},{10,14},{5,1},{7,3},{9,13},{11,15},{20,16},{22,... | collective-permute-start | bytes 1572872 | tf_op jit(solution)/shard_map/ppermute | solution.py:184
  154.6 21.5 %collective-permute-start.16 = (bf16[512,512]{1,0:T(8,128)(2,1)S(1)}, bf16[512,512]{1,0:T(8,128)(2,1)S(1)}, u32[]{:S(2)}, u32[]{:S(2)}) collective-permute-start(bf16[512,512]{1,0:T(8,128)(2,1)S(1)} %get-tuple-element.78), channel_id=1, source_target_pairs={{4,8},{6,10},{8,4},{10,6},{5,9},{7,11},{9,5},{11,7},{20,24},{22,26... | collective-permute-start | bytes 1572872 | tf_op jit(solution)/shard_map/ppermute | solution.py:184
  176.1 22.1 %collective-permute-start.22 = (f32[320,1792]{1,0:T(8,128)S(1)}, f32[320,1792]{1,0:T(8,128)S(1)}, u32[]{:S(2)}, u32[]{:S(2)}) collective-permute-start(f32[320,1792]{1,0:T(8,128)S(1)} %rotate.7), channel_id=1, source_target_pairs={{0,1},{1,0},{2,3},{3,2},{4,5},{5,4},{6,7},{7,6},{8,9},{9,8},{10,11... | collective-permute-start | bytes 6881288 | tf_op jit(solution)/shard_map/ppermute | solution.py:146
  176.2 22.1 %collective-permute-start.19 = (bf16[64,6144]{1,0:T(8,128)(2,1)S(1)}, bf16[64,6144]{1,0:T(8,128)(2,1)S(1)}, u32[]{:S(2)}, u32[]{:S(2)}) collective-permute-start(bf16[64,6144]{1,0:T(8,128)(2,1)S(1)} %slice.39), channel_id=1, source_target_pairs={{0,2},{2,0},{12,14},{14,12},{1,3},{3,1},{13,15},{15,13},{16,18},{1... | collective-permute-start | bytes 2359304 | tf_op jit(solution)/shard_map/ppermute | solution.py:184
  179.9 18.3 %collective-permute-start.21 = (bf16[512,512]{1,0:T(8,128)(2,1)S(1)}, bf16[512,512]{1,0:T(8,128)(2,1)S(1)}, u32[]{:S(2)}, u32[]{:S(2)}) collective-permute-start(bf16[512,512]{1,0:T(8,128)(2,1)S(1)} %add_convert_fusion.1), channel_id=1, source_target_pairs={{4,0},{6,2},{8,12},{10,14},{5,1},{7,3},{9,13},{11,15},{20,16},{22,... | collective-permute-start | bytes 1572872 | tf_op jit(solution)/shard_map/ppermute | solution.py:184
  181.2 17.0 %collective-permute-start.20 = (bf16[512,512]{1,0:T(8,128)(2,1)S(1)}, bf16[512,512]{1,0:T(8,128)(2,1)S(1)}, u32[]{:S(2)}, u32[]{:S(2)}) collective-permute-start(bf16[512,512]{1,0:T(8,128)(2,1)S(1)} %add_convert_fusion.1), channel_id=1, source_target_pairs={{4,8},{6,10},{8,4},{10,6},{5,9},{7,11},{9,5},{11,7},{20,24},{22,26... | collective-permute-start | bytes 1572872 | tf_op jit(solution)/shard_map/ppermute | solution.py:184
  181.9 25.4 %collective-permute-start.18 = (bf16[512,512]{1,0:T(8,128)(2,1)S(1)}, bf16[512,512]{1,0:T(8,128)(2,1)S(1)}, u32[]{:S(2)}, u32[]{:S(2)}) collective-permute-start(bf16[512,512]{1,0:T(8,128)(2,1)S(1)} %collective-permute-done.16), channel_id=1, source_target_pairs={{4,0},{6,2},{8,12},{10,14},{5,1},{7,3},{9,13},{11,15},{20,16},{22,... | collective-permute-start | bytes 1572872 | tf_op jit(solution)/shard_map/ppermute | solution.py:184
  199.5 19.6 %collective-permute-start.23 = (bf16[512,512]{1,0:T(8,128)(2,1)S(1)}, bf16[512,512]{1,0:T(8,128)(2,1)S(1)}, u32[]{:S(2)}, u32[]{:S(2)}) collective-permute-start(bf16[512,512]{1,0:T(8,128)(2,1)S(1)} %collective-permute-done.20.refs_10_), channel_id=1, source_target_pairs={{4,0},{6,2},{8,12},{10,14},{5,1},{7,3},{9,13},{11,15},{20,16},{22,... | collective-permute-start | bytes 1572872 | tf_op jit(solution)/shard_map/ppermute | solution.py:184
  218.2 4.1 %copy-start.4 = (f32[192,1792]{1,0:T(8,128)}, f32[192,1792]{1,0:T(8,128)S(1)}, u32[]{:S(2)}) copy-start(f32[192,1792]{1,0:T(8,128)S(1)} %rotate.9.refs_4_) | copy-start | bytes 4128772
  219.1 3.1 %copy-start.8 = (bf16[512,512]{1,0:T(8,128)(2,1)}, bf16[512,512]{1,0:T(8,128)(2,1)S(1)}, u32[]{:S(2)}) copy-start(bf16[512,512]{1,0:T(8,128)(2,1)S(1)} %collective-permute-done.23.refs_9_) | copy-start | bytes 1572868
  219.1 3.1 %collective-permute-start.24 = (f32[192,1792]{1,0:T(8,128)S(1)}, f32[192,1792]{1,0:T(8,128)S(1)}, u32[]{:S(2)}, u32[]{:S(2)}) collective-permute-start(f32[192,1792]{1,0:T(8,128)S(1)} %rotate.9.refs_4_), channel_id=1, source_target_pairs={{0,1},{1,0},{2,3},{3,2},{4,5},{5,4},{6,7},{7,6},{8,9},{9,8},{10,11... | collective-permute-start | bytes 4128776 | tf_op jit(solution)/shard_map/ppermute | solution.py:146
  223.4 12.5 %copy-start.1 = (bf16[512,1024]{1,0:T(8,128)(2,1)S(1)}, bf16[512,1024]{1,0:T(8,128)(2,1)}, u32[]{:S(2)}) copy-start(bf16[512,1024]{1,0:T(8,128)(2,1)} %param.5) | copy-start | bytes 3145732
  (2 other events, 2.4 us)

commit v14 on v13

--- a/solution.py
+++ b/solution.py
@@ -191,7 +191,7 @@
     end = at_end.astype(jnp.int32).reshape(1)
     half = (z >= 2).astype(jnp.int32)
     steps = inputs.shape[1] // DEEP
-    cuts = [0, 8 * steps // 14, steps]
+    cuts = [0, 6 * steps // 14, 11 * steps // 14, steps]
     part = basis_out.shape[1] // 4
     got = {"own": inputs}
 
@@ -233,55 +233,67 @@
     got["m2"] = send(got["a1"], MIDDLE)
     blocks = [["own"], ["a1"], ["x1"]]
     got["A"] = turn([], blocks, 0, some)
-    fence("x1", "x2", ("x2", "m"), "a2", "m2", "out", "r1", "A")
+    fence("x1", "x2", "a2", "m2", "out", "r1", "A")
+    def columns_of(p, q):
+        here = slice(p * part, q * part)
+        return got["out"][:, here] + got["r1"][:, here].astype(F32)
+
+    def cross(p):
+        here = slice(p * part, (p + 1) * part)
+        got["keep", p] = got["keep"][:, here] + got["m3", p]
+        got["x5", p] = send(got["keep", p].astype(BF16), ACROSS_MIDDLE)
+
     got["x3"] = send(got["a2"], ACROSS_ENDS)
-    got["x3", "m"] = send(got["m2"], ACROSS_MIDDLE)
+    got["m3", 0] = send(columns_of(0, 1), MIDDLE)
     got["a3"] = send(got["m2"], TO_ENDS)
-    cut = 2 * part
-    got["m3"] = send(got["out"][:, :cut] + got["r1"][:, :cut].astype(F32), MIDDLE)
     got["e"] = send(got["x1"], FROM_ENDS)
-    got["keep"] = got["out"][:, cut:] + got["r1"][:, cut:].astype(F32)
+    fence(("x2", "m"), "m2", "out", "r1")
+    got["x3m", 0] = send(got["m2"][:, : cuts[1] * DEEP], ACROSS_MIDDLE)
+    got["give"], got["keep"] = columns_of(1, 2), columns_of(2, 4)
     more = [["a2", "m1"], ["x2", ("x2", "m")]]
     got["B"] = turn([], more, 0, some)
+    fence(("m3", 0), ("x3m", 0), "give", "keep", "m2", "B")
+    cross(0)
+    got["m3", 1] = send(got["give"], MIDDLE)
     got["A"] = turn([got["A"], got["B"]], blocks + more, some, steps - some)
-    fence("x3", "A", "keep")
-    fence(("x3", "m"), "a3", "e", "A")
+    fence("x3", "A")
+    fence("a3", ("x5", 0), "A")
 
     def x4(piece):
         got["x4", piece] = send(got["a3"][:, cuts[piece] * DEEP : cuts[piece + 1] * DEEP], ACROSS_ENDS)
 
     def last(piece):
-        first = cuts[piece]
-        blocks = [["a3", "m2"], ["x3", ("x3", "m")]]
-        blocks = [[(got[n], first) for n in b] for b in blocks] + [[(got["x4", piece], 0), (got["e"], first)]]
-        got["D"] = rotate([got["D"]] if piece else [], end, blocks, basis_in, first, cuts[piece + 1] - first)
-
-    def cross(p):
-        here = slice(p * part, (p + 1) * part)
-        got["keep", p] = got["keep"][:, here] + got["m3"][:, here]
-        got["x5", p] = send(got["keep", p].astype(BF16), ACROSS_MIDDLE)
+        first, count = cuts[piece], cuts[piece + 1] - cuts[piece]
+        side = ("x3m", 0 if piece == 0 else 1)
+        blocks = [
+            [(got["a3"], first), (got["m2"], first)],
+            [(got["x3"], first), (got[side], 0 if piece == 0 else first - cuts[1])],
+            [(got["x4", piece], 0), (got["e"], first)],
+        ]
+        got["D"] = rotate([got["D"]] if piece else [], end, blocks, basis_in, first, count)
 
     x4(0)
-    fence("m3", "A")
-    cross(0)
+    settle(0)
+    fence(("m3", 1), "e", "m2")
     cross(1)
-    fence(("x5", 0), "a3")
-    settle(0)
-    fence(("x4", 0), ("x5", 1), ("m4", 0), ("n1", 0), ("sum", 0), "A", "a3")
+    got["x3m", 1] = send(got["m2"][:, cuts[1] * DEEP :], ACROSS_MIDDLE)
+    fence(("x4", 0), ("m4", 0), ("n1", 0), ("sum", 0), ("x5", 1), "A", "a3")
     x4(1)
+    got["n2", 0] = send(got["m4", 0], TO_ENDS)
     settle(1)
-    got["n2", 0] = send(got["m4", 0], TO_ENDS)
-    got["A2"] = swap_narrow(got["A"])
     got["R", 0] = pick(("n1", 0), ("sum", 0))
     last(0)
-    fence(("x4", 1), ("m4", 1), ("n1", 1), ("sum", 1), ("R", 0), "A2", "D")
+    fence(("x4", 1), ("m4", 1), ("n1", 1), ("sum", 1), ("x3m", 1), ("R", 0), "A", "D", "a3")
+    x4(2)
     got["n2", 1] = send(got["m4", 1], TO_ENDS)
+    got["A2"] = swap_narrow(got["A"])
+    got["R", 1] = pick(("n1", 1), ("sum", 1))
+    last(1)
+    fence(("x4", 2), ("n2", 0), ("m4", 0), "A2", ("R", 1), "D")
     got["A"] = (got["A"] + got["A2"]).astype(BF16)
-    got["R", 1] = pick(("n1", 1), ("sum", 1))
-    fence(("n2", 0), ("m4", 0), ("R", 1), "A", "D")
     got["R", 2] = pick(("n2", 0), ("m4", 0))
-    last(1)
-    fence(("n2", 1), ("R", 2), "D")
+    last(2)
+    fence(("n2", 1), ("R", 2), "A", "D")
     got["D2"] = swap_narrow(got["D"])
 
     pieces = [[got["R", p]] for p in range(3)] + [[got["n2", 1], got["m4", 1]]]

time: 237 us -> 229 us (0.966)
  waiting for transfers between devices: 92.4 us -> 72.7 us
  starting transfers between devices: 45.9 us -> 53.9 us
    ppermute x23 -> x26, waiting for transfers between devices: 89.3 us -> 69.6 us  [send(): return lax.ppermute(a, 'wide', perm)]
    ppermute x23 -> x26, starting transfers between devices: 45.9 us -> 53.9 us  [send(): return lax.ppermute(a, 'wide', perm)]
    pallas_call x5 -> x6, Pallas kernels: 65.3 us -> 66.9 us  [rotate(): pl.pallas_call(lambda *refs: rotate_kernel([len(block) for block in block...]
  transfers between devices with their start and end apart: 25 -> 28, of which waited for: 12 -> 11; matrix products, arithmetic and copies ran while one was open for 6% -> 8% of each run, Pallas kernels for 28% -> 29%
where the time goes in v14:
time: 229 us; the launch traced here: 227 us
  Pallas kernels  79.4 us (35%)
  waiting for transfers between devices  72.7 us (32%)
  starting transfers between devices  53.9 us (24%)
  other arithmetic  9.71 us (4%)
  local copies, waits for them, and re-layouts  6.14 us (3%)
  matrix products  5.12 us (2%)
    ppermute x26, waiting for transfers between devices, send(): return lax.ppermute(a, 'wide', perm)  69.6 us
    pallas_call x6, Pallas kernels, rotate(): pl.pallas_call(lambda *refs: rotate_kernel([len(block) for block in block...  66.9 us
    ppermute x26, starting transfers between devices, send(): return lax.ppermute(a, 'wide', perm)  53.9 us
    pallas_call x1, Pallas kernels, fit(): pl.pallas_call(lambda *refs: fit_kernel([len(halves) for halves in sums],...  12.5 us
    dot_general x1, matrix products, dot(): return jnp.dot(a, b, preferred_element_type=F32)  5.12 us
  transfers between devices with their start and end apart: 28, of which 11 were waited for; matrix products, arithmetic and copies ran while one was open for 8% of the time, Pallas kernels for 29%

profile of v14, /device:TPU:0, one launch (start us, length us, event | category | flops | bytes accessed | tf_op | source)
XLA Modules:
  0.0 227.3 jit_solution(17952622793221886727)
XLA Ops:
  0.0 2.9 %collective-permute-start = (bf16[64,14336]{1,0:T(8,128)(2,1)}, bf16[64,14336]{1,0:T(8,128)(2,1)}, u32[]{:S(2)}, u32[]{:S(2)}) collective-permute-start(bf16[64,14336]{1,0:T(8,128)(2,1)} %refs_1_.3), channel_id=1, source_target_pairs={{0,2},{2,0},{4,6},{6,4},{8,10},{10,8},{12,14},{14,12},{1,3},{3,1},... | collective-permute-start | bytes 5505032 | tf_op jit(solution)/shard_map/ppermute | solution.py:184
  2.9 1.6 collective-permute-start.1
  4.5 1.9 collective-permute-start.2
  6.5 2.7 %constant_dynamic-slice_fusion.1 = (bf16[1024,1024]{1,0:T(8,128)(2,1)S(1)}, bf16[1024,1024]{1,0:T(8,128)(2,1)S(1)}) fusion(bf16[1024,2048]{1,0:T(8,128)(2,1)} %param.7, s32[]{:T(128)S(6)} %select_n.56, s32[]{:T(128)S(6)} %select_n.57), kind=kLoop, calls=%fused_computation.20 | loop fusion | bytes 8388616 | tf_op jit(solution)/shard_map/dynamic_slice | solution.py:205
  9.1 5.1 %fusion.10 = (bf16[512,2048]{1,0:T(8,128)(2,1)}, f32[512,2048]{1,0:T(8,128)}) fusion(bf16[512,1024]{1,0:T(8,128)(2,1)S(1)} %copy-done, bf16[1024,1024]{1,0:T(8,128)(2,1)S(1)} %get-tuple-element.120, bf16[1024,1024]{1,0:T(8,128)(2,1)S(1)} %get-tuple-element.119), kind=kOutput, calls=%fused_computation.22 | convolution fusion | flops 2156920832 | bytes 11534336 | tf_op jit(solution)/shard_map/dot_general | solution.py:16
  14.3 6.4 %collective-permute-start.6 = (bf16[512,2048]{1,0:T(8,128)(2,1)}, bf16[512,2048]{1,0:T(8,128)(2,1)}, u32[]{:S(2)}, u32[]{:S(2)}) collective-permute-start(bf16[512,2048]{1,0:T(8,128)(2,1)} %get-tuple-element.123), channel_id=1, source_target_pairs={{0,4},{2,6},{12,8},{14,10},{1,5},{3,7},{13,9},{15,11},{16,20},{18,... | collective-permute-start | bytes 6291464 | tf_op jit(solution)/shard_map/ppermute | solution.py:184
  21.9 21.4 %collective-permute-done.refs_3_ = bf16[64,14336]{1,0:T(8,128)(2,1)} collective-permute-done((bf16[64,14336]{1,0:T(8,128)(2,1)}, bf16[64,14336]{1,0:T(8,128)(2,1)}, u32[]{:S(2)}, u32[]{:S(2)}) %collective-permute-start) | collective-permute-done | bytes 1835040 | tf_op jit(solution)/shard_map/ppermute | solution.py:184
  43.3 2.0 collective-permute-done.1.refs_2_
  45.3 2.4 %collective-permute-start.3 = (bf16[64,14336]{1,0:T(8,128)(2,1)}, bf16[64,14336]{1,0:T(8,128)(2,1)}, u32[]{:S(2)}, u32[]{:S(2)}) collective-permute-start(bf16[64,14336]{1,0:T(8,128)(2,1)} %collective-permute-done.1.refs_2_), channel_id=1, source_target_pairs={{0,2},{2,0},{12,14},{14,12},{1,3},{3,1},{13,15},{15,13},{16,18},{1... | collective-permute-start | bytes 5505032 | tf_op jit(solution)/shard_map/ppermute | solution.py:184
  47.7 1.3 collective-permute-start.4
  49.8 1.9 collective-permute-start.9
  51.7 1.5 copy-done.2
  53.2 13.0 %rotate.6.refs_9_ = f32[192,1792]{1,0:T(8,128)S(1)} custom-call(s32[1]{0:T(128)} %bitcast.13.refs_0_.refs_1_, bf16[64,14336]{1,0:T(8,128)(2,1)S(1)} %copy-done.2, bf16[64,14336]{1,0:T(8,128)(2,1)} %collective-permute-done.1.refs_2_, bf16[64,14336]{1,0:T(8,128)(2,1)} %collective-permute-done.refs_3_, bf16[14336,1792]{1,0:T(8,128)(2,1)} %refs_7_.5), custom_call_target="tpu_custom_call" | custom-call | flops 344064 | bytes 1376256 | tf_op jit(solution)/shard_map/rotate/pallas_call | solution.py:125
  66.3 22.5 %collective-permute-done.6 = bf16[512,2048]{1,0:T(8,128)(2,1)} collective-permute-done((bf16[512,2048]{1,0:T(8,128)(2,1)}, bf16[512,2048]{1,0:T(8,128)(2,1)}, u32[]{:S(2)}, u32[]{:S(2)}) %collective-permute-start.6) | collective-permute-done | bytes 2097184 | tf_op jit(solution)/shard_map/ppermute | solution.py:184
  88.8 2.9 %collective-permute-done.4.refs_1_.refs_4_ = bf16[64,14336]{1,0:T(8,128)(2,1)} collective-permute-done((bf16[64,14336]{1,0:T(8,128)(2,1)}, bf16[64,14336]{1,0:T(8,128)(2,1)}, u32[]{:S(2)}, u32[]{:S(2)}) %collective-permute-start.4) | collective-permute-done | bytes 1835040 | tf_op jit(solution)/shard_map/ppermute | solution.py:184
  93.7 2.4 %collective-permute-start.12 = (bf16[64,14336]{1,0:T(8,128)(2,1)}, bf16[64,14336]{1,0:T(8,128)(2,1)S(1)}, u32[]{:S(2)}, u32[]{:S(2)}) collective-permute-start(bf16[64,14336]{1,0:T(8,128)(2,1)} %collective-permute-done.4.refs_1_.refs_4_), channel_id=1, source_target_pairs={{0,2},{2,0},{12,14},{14,12},{1,3},{3,1},{13,15},{15,13},{16,18},{1... | collective-permute-start | bytes 5505032 | tf_op jit(solution)/shard_map/ppermute | solution.py:184
  98.2 9.8 %collective-permute-start.17 = (bf16[64,14336]{1,0:T(8,128)(2,1)}, bf16[64,14336]{1,0:T(8,128)(2,1)S(1)}, u32[]{:S(2)}, u32[]{:S(2)}) collective-permute-start(bf16[64,14336]{1,0:T(8,128)(2,1)} %collective-permute-done.refs_3_), channel_id=1, source_target_pairs={{0,4},{2,6},{12,8},{14,10},{1,5},{3,7},{13,9},{15,11},{16,20},{18,... | collective-permute-start | bytes 5505032 | tf_op jit(solution)/shard_map/ppermute | solution.py:184
  108.0 12.0 %rotate.7.refs_10_ = f32[128,1792]{1,0:T(8,128)S(1)} custom-call(s32[1]{0:T(128)} %bitcast.13.refs_0_.refs_1_, bf16[64,14336]{1,0:T(8,128)(2,1)} %collective-permute-done.4.refs_1_.refs_4_, bf16[64,14336]{1,0:T(8,128)(2,1)} %collective-permute-done.2.refs_2_.refs_5_, bf16[64,14336]{1,0:T(8,128)(2,1)} %collective-permute-done.3.refs_3_.refs_6_, ...), custom_call_target="tpu_custom_call" | custom-call | flops 229376 | bytes 917504 | tf_op jit(solution)/shard_map/rotate/pallas_call | solution.py:125
  121.2 1.7 convert_add_fusion
  124.8 15.3 %rotate.8 = f32[320,1792]{1,0:T(8,128)S(1)} custom-call(s32[1]{0:T(128)} %bitcast.13.refs_0_.refs_1_, bf16[64,14336]{1,0:T(8,128)(2,1)S(1)} %copy-done.3, bf16[64,14336]{1,0:T(8,128)(2,1)} %collective-permute-done.1.refs_2_, bf16[64,14336]{1,0:T(8,128)(2,1)} %collective-permute-done.refs_3_, bf16[64,14336]{1,0:T(8,128)(2,1)} %collective-permute-done.4.refs_1_.refs_4_, ...), custom_call_target="tpu_custom_call" | custom-call | flops 573440 | bytes 2293760 | tf_op jit(solution)/shard_map/rotate/pallas_call | solution.py:125
  140.6 2.8 %collective-permute-start.13 = (bf16[64,6144]{1,0:T(8,128)(2,1)S(1)}, bf16[64,6144]{1,0:T(8,128)(2,1)S(1)}, u32[]{:S(2)}, u32[]{:S(2)}) collective-permute-start(bf16[64,6144]{1,0:T(8,128)(2,1)S(1)} %slice.47), channel_id=1, source_target_pairs={{0,2},{2,0},{12,14},{14,12},{1,3},{3,1},{13,15},{15,13},{16,18},{1... | collective-permute-start | bytes 2359304 | tf_op jit(solution)/shard_map/ppermute | solution.py:184
  148.4 10.8 %collective-permute-done.15 = bf16[512,512]{1,0:T(8,128)(2,1)S(1)} collective-permute-done((bf16[512,512]{1,0:T(8,128)(2,1)S(1)}, bf16[512,512]{1,0:T(8,128)(2,1)S(1)}, u32[]{:S(2)}, u32[]{:S(2)}) %collective-permute-start.15) | collective-permute-done | bytes 524320 | tf_op jit(solution)/shard_map/ppermute | solution.py:184
  159.3 3.7 %collective-permute-start.19 = (bf16[64,5120]{1,0:T(8,128)(2,1)S(1)}, bf16[64,5120]{1,0:T(8,128)(2,1)S(1)}, u32[]{:S(2)}, u32[]{:S(2)}) collective-permute-start(bf16[64,5120]{1,0:T(8,128)(2,1)S(1)} %slice.49), channel_id=1, source_target_pairs={{0,2},{2,0},{12,14},{14,12},{1,3},{3,1},{13,15},{15,13},{16,18},{1... | collective-permute-start | bytes 1966088 | tf_op jit(solution)/shard_map/ppermute | solution.py:184
  165.4 10.8 %rotate.9.refs_8_ = f32[192,1792]{1,0:T(8,128)S(1)} custom-call(s32[1]{0:T(128)} %bitcast.13.refs_0_.refs_1_, bf16[64,14336]{1,0:T(8,128)(2,1)S(1)} %collective-permute-done.7.refs_1_, bf16[64,14336]{1,0:T(8,128)(2,1)S(1)} %collective-permute-done.5.refs_2_, bf16[64,14336]{1,0:T(8,128)(2,1)S(1)} %collective-permute-done.12.refs_3_, ...), custom_call_target="tpu_custom_call" | custom-call | flops 344064 | bytes 1376256 | tf_op jit(solution)/shard_map/rotate/pallas_call | solution.py:125
  177.1 3.6 %collective-permute-done.21 = bf16[512,512]{1,0:T(8,128)(2,1)S(1)} collective-permute-done((bf16[512,512]{1,0:T(8,128)(2,1)S(1)}, bf16[512,512]{1,0:T(8,128)(2,1)S(1)}, u32[]{:S(2)}, u32[]{:S(2)}) %collective-permute-start.21) | collective-permute-done | bytes 524320 | tf_op jit(solution)/shard_map/ppermute | solution.py:184
  182.1 3.7 %collective-permute-start.24 = (bf16[64,3072]{1,0:T(8,128)(2,1)S(1)}, bf16[64,3072]{1,0:T(8,128)(2,1)S(1)}, u32[]{:S(2)}, u32[]{:S(2)}) collective-permute-start(bf16[64,3072]{1,0:T(8,128)(2,1)S(1)} %slice.51), channel_id=1, source_target_pairs={{0,2},{2,0},{12,14},{14,12},{1,3},{3,1},{13,15},{15,13},{16,18},{1... | collective-permute-start | bytes 1179656 | tf_op jit(solution)/shard_map/ppermute | solution.py:184
  187.0 9.4 %rotate.10.refs_8_ = f32[192,1792]{1,0:T(8,128)S(1)} custom-call(s32[1]{0:T(128)} %bitcast.13.refs_0_.refs_1_, bf16[64,14336]{1,0:T(8,128)(2,1)S(1)} %collective-permute-done.7.refs_1_, bf16[64,14336]{1,0:T(8,128)(2,1)S(1)} %collective-permute-done.5.refs_2_, bf16[64,14336]{1,0:T(8,128)(2,1)S(1)} %collective-permute-done.12.refs_3_, ...), custom_call_target="tpu_custom_call" | custom-call | flops 344064 | bytes 1376256 | tf_op jit(solution)/shard_map/rotate/pallas_call | solution.py:125
  197.3 2.2 collective-permute-done.25
  199.6 6.3 %rotate.11.refs_4_ = f32[192,1792]{1,0:T(8,128)S(1)} custom-call(s32[1]{0:T(128)} %bitcast.13.refs_0_.refs_1_, bf16[64,14336]{1,0:T(8,128)(2,1)S(1)} %collective-permute-done.7.refs_1_, bf16[64,14336]{1,0:T(8,128)(2,1)S(1)} %collective-permute-done.5.refs_2_, bf16[64,14336]{1,0:T(8,128)(2,1)S(1)} %collective-permute-done.12.refs_3_, ...), custom_call_target="tpu_custom_call" | custom-call | flops 344064 | bytes 1376256 | tf_op jit(solution)/shard_map/rotate/pallas_call | solution.py:125
  208.1 2.6 %collective-permute-done.23.refs_9_ = bf16[512,512]{1,0:T(8,128)(2,1)S(1)} collective-permute-done((bf16[512,512]{1,0:T(8,128)(2,1)S(1)}, bf16[512,512]{1,0:T(8,128)(2,1)S(1)}, u32[]{:S(2)}, u32[]{:S(2)}) %collective-permute-start.23) | collective-permute-done | bytes 524320 | tf_op jit(solution)/shard_map/ppermute | solution.py:184
  210.6 3.1 %collective-permute-done.27.refs_5_ = f32[192,1792]{1,0:T(8,128)S(1)} collective-permute-done((f32[192,1792]{1,0:T(8,128)S(1)}, f32[192,1792]{1,0:T(8,128)S(1)}, u32[]{:S(2)}, u32[]{:S(2)}) %collective-permute-start.27) | collective-permute-done | bytes 1376288 | tf_op jit(solution)/shard_map/ppermute | solution.py:146
  214.8 12.5 %fit.1 = f32[1792,2048]{1,0:T(8,128)} custom-call(s32[8]{0:T(128)} %stack.50.refs_0_, s32[1]{0:T(128)} %bitcast.13.refs_0_.refs_1_, s32[4]{0:T(128)} %pad_add_fusion.refs_2_, bf16[320,1792]{1,0:T(8,128)(2,1)} %add_convert_fusion.refs_3_, f32[192,1792]{1,0:T(8,128)} %copy-done.4, f32[192,1792]{1,0:T(8,128)} %copy-done.6, ...), custom_call_target="tpu_custom_call" | custom-call | flops 3758096384 | bytes 24117248 | tf_op jit(solution)/shard_map/fit/pallas_call | solution.py:64
  (68 shorter events, 24.5 us)
Async XLA Ops:
  0.0 9.1 %copy-start = (bf16[512,1024]{1,0:T(8,128)(2,1)S(1)}, bf16[512,1024]{1,0:T(8,128)(2,1)}, u32[]{:S(2)}) copy-start(bf16[512,1024]{1,0:T(8,128)(2,1)} %param.5) | copy-start | bytes 3145732
  0.0 43.3 %collective-permute-start = (bf16[64,14336]{1,0:T(8,128)(2,1)}, bf16[64,14336]{1,0:T(8,128)(2,1)}, u32[]{:S(2)}, u32[]{:S(2)}) collective-permute-start(bf16[64,14336]{1,0:T(8,128)(2,1)} %refs_1_.3), channel_id=1, source_target_pairs={{0,2},{2,0},{4,6},{6,4},{8,10},{10,8},{12,14},{14,12},{1,3},{3,1},... | collective-permute-start | bytes 5505032 | tf_op jit(solution)/shard_map/ppermute | solution.py:184
  2.9 42.3 %collective-permute-start.1 = (bf16[64,14336]{1,0:T(8,128)(2,1)}, bf16[64,14336]{1,0:T(8,128)(2,1)}, u32[]{:S(2)}, u32[]{:S(2)}) collective-permute-start(bf16[64,14336]{1,0:T(8,128)(2,1)} %refs_1_.3), channel_id=1, source_target_pairs={{0,4},{2,6},{4,0},{6,2},{8,12},{10,14},{12,8},{14,10},{1,5},{3,7},... | collective-permute-start | bytes 5505032 | tf_op jit(solution)/shard_map/ppermute | solution.py:184
  4.5 40.8 %collective-permute-start.2 = (bf16[64,14336]{1,0:T(8,128)(2,1)}, bf16[64,14336]{1,0:T(8,128)(2,1)}, u32[]{:S(2)}, u32[]{:S(2)}) collective-permute-start(bf16[64,14336]{1,0:T(8,128)(2,1)} %refs_1_.3), channel_id=1, source_target_pairs={{4,8},{6,10},{8,4},{10,6},{5,9},{7,11},{9,5},{11,7},{20,24},{22,26... | collective-permute-start | bytes 5505032 | tf_op jit(solution)/shard_map/ppermute | solution.py:184
  14.3 74.5 %collective-permute-start.6 = (bf16[512,2048]{1,0:T(8,128)(2,1)}, bf16[512,2048]{1,0:T(8,128)(2,1)}, u32[]{:S(2)}, u32[]{:S(2)}) collective-permute-start(bf16[512,2048]{1,0:T(8,128)(2,1)} %get-tuple-element.123), channel_id=1, source_target_pairs={{0,4},{2,6},{12,8},{14,10},{1,5},{3,7},{13,9},{15,11},{16,20},{18,... | collective-permute-start | bytes 6291464 | tf_op jit(solution)/shard_map/ppermute | solution.py:184
  45.3 43.5 %collective-permute-start.3 = (bf16[64,14336]{1,0:T(8,128)(2,1)}, bf16[64,14336]{1,0:T(8,128)(2,1)}, u32[]{:S(2)}, u32[]{:S(2)}) collective-permute-start(bf16[64,14336]{1,0:T(8,128)(2,1)} %collective-permute-done.1.refs_2_), channel_id=1, source_target_pairs={{0,2},{2,0},{12,14},{14,12},{1,3},{3,1},{13,15},{15,13},{16,18},{1... | collective-permute-start | bytes 5505032 | tf_op jit(solution)/shard_map/ppermute | solution.py:184
  47.7 44.0 %collective-permute-start.4 = (bf16[64,14336]{1,0:T(8,128)(2,1)}, bf16[64,14336]{1,0:T(8,128)(2,1)}, u32[]{:S(2)}, u32[]{:S(2)}) collective-permute-start(bf16[64,14336]{1,0:T(8,128)(2,1)} %collective-permute-done.2.refs_2_.refs_5_), channel_id=1, source_target_pairs={{4,0},{6,2},{8,12},{10,14},{5,1},{7,3},{9,13},{11,15},{20,16},{22,... | collective-permute-start | bytes 5505032 | tf_op jit(solution)/shard_map/ppermute | solution.py:184
  49.0 42.7 %collective-permute-start.5 = (bf16[64,14336]{1,0:T(8,128)(2,1)}, bf16[64,14336]{1,0:T(8,128)(2,1)S(1)}, u32[]{:S(2)}, u32[]{:S(2)}) collective-permute-start(bf16[64,14336]{1,0:T(8,128)(2,1)} %collective-permute-done.1.refs_2_), channel_id=1, source_target_pairs={{4,8},{6,10},{8,4},{10,6},{5,9},{7,11},{9,5},{11,7},{20,24},{22,26... | collective-permute-start | bytes 5505032 | tf_op jit(solution)/shard_map/ppermute | solution.py:184
  49.8 47.6 %collective-permute-start.9 = (bf16[64,14336]{1,0:T(8,128)(2,1)}, bf16[64,14336]{1,0:T(8,128)(2,1)}, u32[]{:S(2)}, u32[]{:S(2)}) collective-permute-start(bf16[64,14336]{1,0:T(8,128)(2,1)} %collective-permute-done.2.refs_2_.refs_5_), channel_id=1, source_target_pairs={{4,6},{6,4},{8,10},{10,8},{5,7},{7,5},{9,11},{11,9},{20,22},{22,20... | collective-permute-start | bytes 5505032 | tf_op jit(solution)/shard_map/ppermute | solution.py:184
  53.2 38.5 %copy-start.5 = (f32[512,2048]{1,0:T(8,128)S(1)}, f32[512,2048]{1,0:T(8,128)}, u32[]{:S(2)}) copy-start(f32[512,2048]{1,0:T(8,128)} %get-tuple-element.72) | copy-start | bytes 12582916
  92.9 30.0 %collective-permute-start.8 = (f32[512,512]{1,0:T(8,128)S(1)}, f32[512,512]{1,0:T(8,128)S(1)}, u32[]{:S(2)}, u32[]{:S(2)}) collective-permute-start(f32[512,512]{1,0:T(8,128)S(1)} %convert_add_fusion.2), channel_id=1, source_target_pairs={{4,8},{6,10},{8,4},{10,6},{5,9},{7,11},{9,5},{11,7},{20,24},{22,26... | collective-permute-start | bytes 3145736 | tf_op jit(solution)/shard_map/ppermute | solution.py:184
  93.7 46.4 %collective-permute-start.12 = (bf16[64,14336]{1,0:T(8,128)(2,1)}, bf16[64,14336]{1,0:T(8,128)(2,1)S(1)}, u32[]{:S(2)}, u32[]{:S(2)}) collective-permute-start(bf16[64,14336]{1,0:T(8,128)(2,1)} %collective-permute-done.4.refs_1_.refs_4_), channel_id=1, source_target_pairs={{0,2},{2,0},{12,14},{14,12},{1,3},{3,1},{13,15},{15,13},{16,18},{1... | collective-permute-start | bytes 5505032 | tf_op jit(solution)/shard_map/ppermute | solution.py:184
  96.1 44.4 %collective-permute-start.7 = (bf16[64,14336]{1,0:T(8,128)(2,1)S(1)}, bf16[64,14336]{1,0:T(8,128)(2,1)S(1)}, u32[]{:S(2)}, u32[]{:S(2)}) collective-permute-start(bf16[64,14336]{1,0:T(8,128)(2,1)S(1)} %collective-permute-done.5.refs_2_), channel_id=1, source_target_pairs={{4,0},{6,2},{8,12},{10,14},{5,1},{7,3},{9,13},{11,15},{20,16},{22,... | collective-permute-start | bytes 5505032 | tf_op jit(solution)/shard_map/ppermute | solution.py:184
  97.5 25.4 %collective-permute-start.10 = (bf16[64,6144]{1,0:T(8,128)(2,1)S(1)}, bf16[64,6144]{1,0:T(8,128)(2,1)S(1)}, u32[]{:S(2)}, u32[]{:S(2)}) collective-permute-start(bf16[64,6144]{1,0:T(8,128)(2,1)S(1)} %slice.41), channel_id=1, source_target_pairs={{4,6},{6,4},{8,10},{10,8},{5,7},{7,5},{9,11},{11,9},{20,22},{22,20... | collective-permute-start | bytes 2359304 | tf_op jit(solution)/shard_map/ppermute | solution.py:184
  98.2 46.1 %collective-permute-start.17 = (bf16[64,14336]{1,0:T(8,128)(2,1)}, bf16[64,14336]{1,0:T(8,128)(2,1)S(1)}, u32[]{:S(2)}, u32[]{:S(2)}) collective-permute-start(bf16[64,14336]{1,0:T(8,128)(2,1)} %collective-permute-done.refs_3_), channel_id=1, source_target_pairs={{0,4},{2,6},{12,8},{14,10},{1,5},{3,7},{13,9},{15,11},{16,20},{18,... | collective-permute-start | bytes 5505032 | tf_op jit(solution)/shard_map/ppermute | solution.py:184
  123.0 21.4 %collective-permute-start.16 = (f32[512,512]{1,0:T(8,128)S(1)}, f32[512,512]{1,0:T(8,128)S(1)}, u32[]{:S(2)}, u32[]{:S(2)}) collective-permute-start(f32[512,512]{1,0:T(8,128)S(1)} %convert_add_fusion.1), channel_id=1, source_target_pairs={{4,8},{6,10},{8,4},{10,6},{5,9},{7,11},{9,5},{11,7},{20,24},{22,26... | collective-permute-start | bytes 3145736 | tf_op jit(solution)/shard_map/ppermute | solution.py:184
  124.1 16.0 %collective-permute-start.11 = (bf16[512,512]{1,0:T(8,128)(2,1)S(1)}, bf16[512,512]{1,0:T(8,128)(2,1)S(1)}, u32[]{:S(2)}, u32[]{:S(2)}) collective-permute-start(bf16[512,512]{1,0:T(8,128)(2,1)S(1)} %fusion.7), channel_id=1, source_target_pairs={{4,6},{6,4},{8,10},{10,8},{5,7},{7,5},{9,11},{11,9},{20,22},{22,20... | collective-permute-start | bytes 1572872 | tf_op jit(solution)/shard_map/ppermute | solution.py:184
  140.6 18.7 %collective-permute-start.13 = (bf16[64,6144]{1,0:T(8,128)(2,1)S(1)}, bf16[64,6144]{1,0:T(8,128)(2,1)S(1)}, u32[]{:S(2)}, u32[]{:S(2)}) collective-permute-start(bf16[64,6144]{1,0:T(8,128)(2,1)S(1)} %slice.47), channel_id=1, source_target_pairs={{0,2},{2,0},{12,14},{14,12},{1,3},{3,1},{13,15},{15,13},{16,18},{1... | collective-permute-start | bytes 2359304 | tf_op jit(solution)/shard_map/ppermute | solution.py:184
  144.9 3.5 %collective-permute-start.14 = (bf16[512,512]{1,0:T(8,128)(2,1)S(1)}, bf16[512,512]{1,0:T(8,128)(2,1)S(1)}, u32[]{:S(2)}, u32[]{:S(2)}) collective-permute-start(bf16[512,512]{1,0:T(8,128)(2,1)S(1)} %get-tuple-element.93), channel_id=1, source_target_pairs={{4,8},{6,10},{8,4},{10,6},{5,9},{7,11},{9,5},{11,7},{20,24},{22,26... | collective-permute-start | bytes 1572872 | tf_op jit(solution)/shard_map/ppermute | solution.py:184
  145.6 13.7 %collective-permute-start.15 = (bf16[512,512]{1,0:T(8,128)(2,1)S(1)}, bf16[512,512]{1,0:T(8,128)(2,1)S(1)}, u32[]{:S(2)}, u32[]{:S(2)}) collective-permute-start(bf16[512,512]{1,0:T(8,128)(2,1)S(1)} %get-tuple-element.93), channel_id=1, source_target_pairs={{4,0},{6,2},{8,12},{10,14},{5,1},{7,3},{9,13},{11,15},{20,16},{22,... | collective-permute-start | bytes 1572872 | tf_op jit(solution)/shard_map/ppermute | solution.py:184
  146.9 12.4 %collective-permute-start.18 = (bf16[512,512]{1,0:T(8,128)(2,1)S(1)}, bf16[512,512]{1,0:T(8,128)(2,1)S(1)}, u32[]{:S(2)}, u32[]{:S(2)}) collective-permute-start(bf16[512,512]{1,0:T(8,128)(2,1)S(1)} %get-tuple-element.121), channel_id=1, source_target_pairs={{4,6},{6,4},{8,10},{10,8},{5,7},{7,5},{9,11},{11,9},{20,22},{22,20... | collective-permute-start | bytes 1572872 | tf_op jit(solution)/shard_map/ppermute | solution.py:184
  147.7 33.0 %collective-permute-start.22 = (bf16[64,8192]{1,0:T(8,128)(2,1)S(1)}, bf16[64,8192]{1,0:T(8,128)(2,1)S(1)}, u32[]{:S(2)}, u32[]{:S(2)}) collective-permute-start(bf16[64,8192]{1,0:T(8,128)(2,1)S(1)} %slice.50), channel_id=1, source_target_pairs={{4,6},{6,4},{8,10},{10,8},{5,7},{7,5},{9,11},{11,9},{20,22},{22,20... | collective-permute-start | bytes 3145736 | tf_op jit(solution)/shard_map/ppermute | solution.py:184
  159.3 21.4 %collective-permute-start.19 = (bf16[64,5120]{1,0:T(8,128)(2,1)S(1)}, bf16[64,5120]{1,0:T(8,128)(2,1)S(1)}, u32[]{:S(2)}, u32[]{:S(2)}) collective-permute-start(bf16[64,5120]{1,0:T(8,128)(2,1)S(1)} %slice.49), channel_id=1, source_target_pairs={{0,2},{2,0},{12,14},{14,12},{1,3},{3,1},{13,15},{15,13},{16,18},{1... | collective-permute-start | bytes 1966088 | tf_op jit(solution)/shard_map/ppermute | solution.py:184
  163.4 13.7 %collective-permute-start.20 = (bf16[512,512]{1,0:T(8,128)(2,1)S(1)}, bf16[512,512]{1,0:T(8,128)(2,1)S(1)}, u32[]{:S(2)}, u32[]{:S(2)}) collective-permute-start(bf16[512,512]{1,0:T(8,128)(2,1)S(1)} %add_convert_fusion.1), channel_id=1, source_target_pairs={{4,8},{6,10},{8,4},{10,6},{5,9},{7,11},{9,5},{11,7},{20,24},{22,26... | collective-permute-start | bytes 1572872 | tf_op jit(solution)/shard_map/ppermute | solution.py:184
  164.1 16.7 %collective-permute-start.21 = (bf16[512,512]{1,0:T(8,128)(2,1)S(1)}, bf16[512,512]{1,0:T(8,128)(2,1)S(1)}, u32[]{:S(2)}, u32[]{:S(2)}) collective-permute-start(bf16[512,512]{1,0:T(8,128)(2,1)S(1)} %add_convert_fusion.1), channel_id=1, source_target_pairs={{4,0},{6,2},{8,12},{10,14},{5,1},{7,3},{9,13},{11,15},{20,16},{22,... | collective-permute-start | bytes 1572872 | tf_op jit(solution)/shard_map/ppermute | solution.py:184
  177.1 19.4 %copy-start.7 = (bf16[512,512]{1,0:T(8,128)(2,1)}, bf16[512,512]{1,0:T(8,128)(2,1)S(1)}, u32[]{:S(2)}) copy-start(bf16[512,512]{1,0:T(8,128)(2,1)S(1)} %collective-permute-done.20.refs_10_) | copy-start | bytes 1572868
  180.7 18.8 %collective-permute-start.26 = (f32[320,1792]{1,0:T(8,128)S(1)}, f32[320,1792]{1,0:T(8,128)S(1)}, u32[]{:S(2)}, u32[]{:S(2)}) collective-permute-start(f32[320,1792]{1,0:T(8,128)S(1)} %rotate.8), channel_id=1, source_target_pairs={{0,1},{1,0},{2,3},{3,2},{4,5},{5,4},{6,7},{7,6},{8,9},{9,8},{10,11... | collective-permute-start | bytes 6881288 | tf_op jit(solution)/shard_map/ppermute | solution.py:146
  180.7 18.8 %collective-permute-start.25 = (bf16[512,512]{1,0:T(8,128)(2,1)S(1)}, bf16[512,512]{1,0:T(8,128)(2,1)S(1)}, u32[]{:S(2)}, u32[]{:S(2)}) collective-permute-start(bf16[512,512]{1,0:T(8,128)(2,1)S(1)} %collective-permute-done.14), channel_id=1, source_target_pairs={{4,0},{6,2},{8,12},{10,14},{5,1},{7,3},{9,13},{11,15},{20,16},{22,... | collective-permute-start | bytes 1572872 | tf_op jit(solution)/shard_map/ppermute | solution.py:184
  182.1 17.5 %collective-permute-start.24 = (bf16[64,3072]{1,0:T(8,128)(2,1)S(1)}, bf16[64,3072]{1,0:T(8,128)(2,1)S(1)}, u32[]{:S(2)}, u32[]{:S(2)}) collective-permute-start(bf16[64,3072]{1,0:T(8,128)(2,1)S(1)} %slice.51), channel_id=1, source_target_pairs={{0,2},{2,0},{12,14},{14,12},{1,3},{3,1},{13,15},{15,13},{16,18},{1... | collective-permute-start | bytes 1179656 | tf_op jit(solution)/shard_map/ppermute | solution.py:184
  185.7 24.9 %collective-permute-start.23 = (bf16[512,512]{1,0:T(8,128)(2,1)S(1)}, bf16[512,512]{1,0:T(8,128)(2,1)S(1)}, u32[]{:S(2)}, u32[]{:S(2)}) collective-permute-start(bf16[512,512]{1,0:T(8,128)(2,1)S(1)} %collective-permute-done.20.refs_10_), channel_id=1, source_target_pairs={{4,0},{6,2},{8,12},{10,14},{5,1},{7,3},{9,13},{11,15},{20,16},{22,... | collective-permute-start | bytes 1572872 | tf_op jit(solution)/shard_map/ppermute | solution.py:184
  210.6 3.1 %collective-permute-start.27 = (f32[192,1792]{1,0:T(8,128)S(1)}, f32[192,1792]{1,0:T(8,128)S(1)}, u32[]{:S(2)}, u32[]{:S(2)}) collective-permute-start(f32[192,1792]{1,0:T(8,128)S(1)} %rotate.11.refs_4_), channel_id=1, source_target_pairs={{0,1},{1,0},{2,3},{3,2},{4,5},{5,4},{6,7},{7,6},{8,9},{9,8},{10,11... | collective-permute-start | bytes 4128776 | tf_op jit(solution)/shard_map/ppermute | solution.py:146
  214.8 12.5 %copy-start.1 = (bf16[512,1024]{1,0:T(8,128)(2,1)S(1)}, bf16[512,1024]{1,0:T(8,128)(2,1)}, u32[]{:S(2)}) copy-start(bf16[512,1024]{1,0:T(8,128)(2,1)} %param.5) | copy-start | bytes 3145732
  (5 other events, 12.3 us)

commit v15 on v14

--- a/solution.py
+++ b/solution.py
@@ -44,7 +44,7 @@
             rot_ref[there, :] = sum(ref[here, :] for ref in halves).astype(BF16)
             slot += 1
     turned_ref[...] = rot_ref[...].T
-    step = min(512, ks)
+    step = min(256, ks)
     for at in range(0, ks, step):
         total = None
         for e in range(EX):
@@ -191,7 +191,7 @@
     end = at_end.astype(jnp.int32).reshape(1)
     half = (z >= 2).astype(jnp.int32)
     steps = inputs.shape[1] // DEEP
-    cuts = [0, 6 * steps // 14, 11 * steps // 14, steps]
+    cuts = [0, 2 * steps // 14, 8 * steps // 14, steps]
     part = basis_out.shape[1] // 4
     got = {"own": inputs}
 
@@ -248,7 +248,7 @@
     got["a3"] = send(got["m2"], TO_ENDS)
     got["e"] = send(got["x1"], FROM_ENDS)
     fence(("x2", "m"), "m2", "out", "r1")
-    got["x3m", 0] = send(got["m2"][:, : cuts[1] * DEEP], ACROSS_MIDDLE)
+    got["x3m", 0] = send(got["m2"][:, : cuts[2] * DEEP], ACROSS_MIDDLE)
     got["give"], got["keep"] = columns_of(1, 2), columns_of(2, 4)
     more = [["a2", "m1"], ["x2", ("x2", "m")]]
     got["B"] = turn([], more, 0, some)
@@ -264,37 +264,36 @@
 
     def last(piece):
         first, count = cuts[piece], cuts[piece + 1] - cuts[piece]
-        side = ("x3m", 0 if piece == 0 else 1)
+        side = piece // 2
         blocks = [
             [(got["a3"], first), (got["m2"], first)],
-            [(got["x3"], first), (got[side], 0 if piece == 0 else first - cuts[1])],
+            [(got["x3"], first), (got["x3m", side], first - side * cuts[2])],
             [(got["x4", piece], 0), (got["e"], first)],
         ]
         got["D"] = rotate([got["D"]] if piece else [], end, blocks, basis_in, first, count)
 
     x4(0)
     settle(0)
-    fence(("m3", 1), "e", "m2")
+    fence(("x4", 0), ("m3", 1), "e", "m2", "a3", "A")
+    x4(1)
     cross(1)
-    got["x3m", 1] = send(got["m2"][:, cuts[1] * DEEP :], ACROSS_MIDDLE)
-    fence(("x4", 0), ("m4", 0), ("n1", 0), ("sum", 0), ("x5", 1), "A", "a3")
-    x4(1)
+    got["x3m", 1] = send(got["m2"][:, cuts[2] * DEEP :], ACROSS_MIDDLE)
+    last(0)
+    fence(("x4", 1), ("m4", 0), ("n1", 0), ("sum", 0), ("x5", 1), "D", "a3")
+    x4(2)
     got["n2", 0] = send(got["m4", 0], TO_ENDS)
     settle(1)
     got["R", 0] = pick(("n1", 0), ("sum", 0))
-    last(0)
-    fence(("x4", 1), ("m4", 1), ("n1", 1), ("sum", 1), ("x3m", 1), ("R", 0), "A", "D", "a3")
-    x4(2)
+    last(1)
+    fence(("x4", 2), ("m4", 1), ("n1", 1), ("sum", 1), ("n2", 0), ("m4", 0), ("x3m", 1), ("R", 0), "A", "D")
     got["n2", 1] = send(got["m4", 1], TO_ENDS)
     got["A2"] = swap_narrow(got["A"])
     got["R", 1] = pick(("n1", 1), ("sum", 1))
-    last(1)
-    fence(("x4", 2), ("n2", 0), ("m4", 0), "A2", ("R", 1), "D")
-    got["A"] = (got["A"] + got["A2"]).astype(BF16)
     got["R", 2] = pick(("n2", 0), ("m4", 0))
     last(2)
-    fence(("n2", 1), ("R", 2), "A", "D")
+    fence(("n2", 1), "A2", "D")
     got["D2"] = swap_narrow(got["D"])
+    got["A"] = (got["A"] + got["A2"]).astype(BF16)
 
     pieces = [[got["R", p]] for p in range(3)] + [[got["n2", 1], got["m4", 1]]]
     return fit(got["order"], end, [[got["A"]], [got["D"], got["D2"]]], pieces, got["places"])

time: 229 us -> 231 us (level)
    ppermute x26, waiting for transfers between devices: 69.6 us -> 73.7 us  [send(): return lax.ppermute(a, 'wide', perm)]
    ppermute x2, waiting for transfers between devices: 3.13 us -> 0.74 us  [swap_narrow(): return lax.ppermute(a, 'narrow', [(0, 1), (1, 0)])]
  transfers between devices with their start and end apart: 28 -> 28, of which waited for: 11 -> 12; matrix products, arithmetic and copies ran while one was open for 8% -> 8% of each run, Pallas kernels for 29% -> 29%
where the time goes in v15:
time: 231 us; the launch traced here: 229 us
  Pallas kernels  78.8 us (34%)
  waiting for transfers between devices  74.5 us (32%)
  starting transfers between devices  55.3 us (24%)
  other arithmetic  9.13 us (4%)
  local copies, waits for them, and re-layouts  6.15 us (3%)
  matrix products  5.11 us (2%)
    ppermute x26, waiting for transfers between devices, send(): return lax.ppermute(a, 'wide', perm)  73.7 us
    pallas_call x6, Pallas kernels, rotate(): pl.pallas_call(lambda *refs: rotate_kernel([len(block) for block in block...  66.3 us
    ppermute x26, starting transfers between devices, send(): return lax.ppermute(a, 'wide', perm)  55.3 us
    pallas_call x1, Pallas kernels, fit(): pl.pallas_call(lambda *refs: fit_kernel([len(halves) for halves in sums],...  12.5 us
    dot_general x1, matrix products, dot(): return jnp.dot(a, b, preferred_element_type=F32)  5.11 us
  transfers between devices with their start and end apart: 28, of which 12 were waited for; matrix products, arithmetic and copies ran while one was open for 8% of the time, Pallas kernels for 29%

profile of v15, /device:TPU:0, one launch (start us, length us, event | category | flops | bytes accessed | tf_op | source)
XLA Modules:
  0.0 229.4 jit_solution(2658618180576005738)
XLA Ops:
  0.0 2.9 %collective-permute-start = (bf16[64,14336]{1,0:T(8,128)(2,1)}, bf16[64,14336]{1,0:T(8,128)(2,1)}, u32[]{:S(2)}, u32[]{:S(2)}) collective-permute-start(bf16[64,14336]{1,0:T(8,128)(2,1)} %refs_1_.3), channel_id=1, source_target_pairs={{0,2},{2,0},{4,6},{6,4},{8,10},{10,8},{12,14},{14,12},{1,3},{3,1},... | collective-permute-start | bytes 5505032 | tf_op jit(solution)/shard_map/ppermute | solution.py:184
  2.9 1.6 collective-permute-start.1
  4.5 1.9 collective-permute-start.2
  6.5 2.7 %constant_dynamic-slice_fusion.1 = (bf16[1024,1024]{1,0:T(8,128)(2,1)S(1)}, bf16[1024,1024]{1,0:T(8,128)(2,1)S(1)}) fusion(bf16[1024,2048]{1,0:T(8,128)(2,1)} %param.7, s32[]{:T(128)S(6)} %select_n.56, s32[]{:T(128)S(6)} %select_n.57), kind=kLoop, calls=%fused_computation.20 | loop fusion | bytes 8388616 | tf_op jit(solution)/shard_map/dynamic_slice | solution.py:205
  9.1 5.1 %fusion.10 = (bf16[512,2048]{1,0:T(8,128)(2,1)}, f32[512,2048]{1,0:T(8,128)}) fusion(bf16[512,1024]{1,0:T(8,128)(2,1)S(1)} %copy-done, bf16[1024,1024]{1,0:T(8,128)(2,1)S(1)} %get-tuple-element.114, bf16[1024,1024]{1,0:T(8,128)(2,1)S(1)} %get-tuple-element.113), kind=kOutput, calls=%fused_computation.22 | convolution fusion | flops 2156920832 | bytes 11534336 | tf_op jit(solution)/shard_map/dot_general | solution.py:16
  14.2 6.4 %collective-permute-start.6 = (bf16[512,2048]{1,0:T(8,128)(2,1)}, bf16[512,2048]{1,0:T(8,128)(2,1)}, u32[]{:S(2)}, u32[]{:S(2)}) collective-permute-start(bf16[512,2048]{1,0:T(8,128)(2,1)} %get-tuple-element.117), channel_id=1, source_target_pairs={{0,4},{2,6},{12,8},{14,10},{1,5},{3,7},{13,9},{15,11},{16,20},{18,... | collective-permute-start | bytes 6291464 | tf_op jit(solution)/shard_map/ppermute | solution.py:184
  21.9 21.4 %collective-permute-done.refs_3_ = bf16[64,14336]{1,0:T(8,128)(2,1)} collective-permute-done((bf16[64,14336]{1,0:T(8,128)(2,1)}, bf16[64,14336]{1,0:T(8,128)(2,1)}, u32[]{:S(2)}, u32[]{:S(2)}) %collective-permute-start) | collective-permute-done | bytes 1835040 | tf_op jit(solution)/shard_map/ppermute | solution.py:184
  43.3 2.0 collective-permute-done.1.refs_2_
  45.3 2.4 %collective-permute-start.3 = (bf16[64,14336]{1,0:T(8,128)(2,1)}, bf16[64,14336]{1,0:T(8,128)(2,1)}, u32[]{:S(2)}, u32[]{:S(2)}) collective-permute-start(bf16[64,14336]{1,0:T(8,128)(2,1)} %collective-permute-done.1.refs_2_), channel_id=1, source_target_pairs={{0,2},{2,0},{12,14},{14,12},{1,3},{3,1},{13,15},{15,13},{16,18},{1... | collective-permute-start | bytes 5505032 | tf_op jit(solution)/shard_map/ppermute | solution.py:184
  49.8 1.9 collective-permute-start.9
  53.2 13.0 %rotate.6.refs_9_ = f32[192,1792]{1,0:T(8,128)S(1)} custom-call(s32[1]{0:T(128)} %bitcast.13.refs_0_.refs_1_, bf16[64,14336]{1,0:T(8,128)(2,1)S(1)} %copy-done.2, bf16[64,14336]{1,0:T(8,128)(2,1)} %collective-permute-done.1.refs_2_, bf16[64,14336]{1,0:T(8,128)(2,1)} %collective-permute-done.refs_3_, bf16[14336,1792]{1,0:T(8,128)(2,1)} %refs_7_.5), custom_call_target="tpu_custom_call" | custom-call | flops 344064 | bytes 1376256 | tf_op jit(solution)/shard_map/rotate/pallas_call | solution.py:125
  66.3 22.5 %collective-permute-done.6 = bf16[512,2048]{1,0:T(8,128)(2,1)} collective-permute-done((bf16[512,2048]{1,0:T(8,128)(2,1)}, bf16[512,2048]{1,0:T(8,128)(2,1)}, u32[]{:S(2)}, u32[]{:S(2)}) %collective-permute-start.6) | collective-permute-done | bytes 2097184 | tf_op jit(solution)/shard_map/ppermute | solution.py:184
  88.8 2.9 %collective-permute-done.4.refs_1_.refs_4_ = bf16[64,14336]{1,0:T(8,128)(2,1)} collective-permute-done((bf16[64,14336]{1,0:T(8,128)(2,1)}, bf16[64,14336]{1,0:T(8,128)(2,1)}, u32[]{:S(2)}, u32[]{:S(2)}) %collective-permute-start.4) | collective-permute-done | bytes 1835040 | tf_op jit(solution)/shard_map/ppermute | solution.py:184
  94.5 2.4 %collective-permute-start.12 = (bf16[64,14336]{1,0:T(8,128)(2,1)}, bf16[64,14336]{1,0:T(8,128)(2,1)S(1)}, u32[]{:S(2)}, u32[]{:S(2)}) collective-permute-start(bf16[64,14336]{1,0:T(8,128)(2,1)} %collective-permute-done.4.refs_1_.refs_4_), channel_id=1, source_target_pairs={{0,2},{2,0},{12,14},{14,12},{1,3},{3,1},{13,15},{15,13},{16,18},{1... | collective-permute-start | bytes 5505032 | tf_op jit(solution)/shard_map/ppermute | solution.py:184
  98.3 10.7 %collective-permute-start.15 = (bf16[64,14336]{1,0:T(8,128)(2,1)}, bf16[64,14336]{1,0:T(8,128)(2,1)S(1)}, u32[]{:S(2)}, u32[]{:S(2)}) collective-permute-start(bf16[64,14336]{1,0:T(8,128)(2,1)} %collective-permute-done.refs_3_), channel_id=1, source_target_pairs={{0,4},{2,6},{12,8},{14,10},{1,5},{3,7},{13,9},{15,11},{16,20},{18,... | collective-permute-start | bytes 5505032 | tf_op jit(solution)/shard_map/ppermute | solution.py:184
  108.9 12.0 %rotate.7.refs_10_ = f32[128,1792]{1,0:T(8,128)S(1)} custom-call(s32[1]{0:T(128)} %bitcast.13.refs_0_.refs_1_, bf16[64,14336]{1,0:T(8,128)(2,1)} %collective-permute-done.4.refs_1_.refs_4_, bf16[64,14336]{1,0:T(8,128)(2,1)} %collective-permute-done.2.refs_2_.refs_5_, bf16[64,14336]{1,0:T(8,128)(2,1)} %collective-permute-done.3.refs_3_.refs_6_, ...), custom_call_target="tpu_custom_call" | custom-call | flops 229376 | bytes 917504 | tf_op jit(solution)/shard_map/rotate/pallas_call | solution.py:125
  122.2 1.7 convert_add_fusion
  125.7 15.3 %rotate.8 = f32[320,1792]{1,0:T(8,128)S(1)} custom-call(s32[1]{0:T(128)} %bitcast.13.refs_0_.refs_1_, bf16[64,14336]{1,0:T(8,128)(2,1)S(1)} %copy-done.3, bf16[64,14336]{1,0:T(8,128)(2,1)} %collective-permute-done.1.refs_2_, bf16[64,14336]{1,0:T(8,128)(2,1)} %collective-permute-done.refs_3_, bf16[64,14336]{1,0:T(8,128)(2,1)} %collective-permute-done.4.refs_1_.refs_4_, ...), custom_call_target="tpu_custom_call" | custom-call | flops 573440 | bytes 2293760 | tf_op jit(solution)/shard_map/rotate/pallas_call | solution.py:125
  141.0 2.6 %collective-permute-done.7.refs_1_ = bf16[64,14336]{1,0:T(8,128)(2,1)S(1)} collective-permute-done((bf16[64,14336]{1,0:T(8,128)(2,1)S(1)}, bf16[64,14336]{1,0:T(8,128)(2,1)S(1)}, u32[]{:S(2)}, u32[]{:S(2)}) %collective-permute-start.7) | collective-permute-done | bytes 1835040 | tf_op jit(solution)/shard_map/ppermute | solution.py:184
  143.7 3.6 %collective-permute-start.13 = (bf16[64,2048]{1,0:T(8,128)(2,1)S(1)}, bf16[64,2048]{1,0:T(8,128)(2,1)S(1)}, u32[]{:S(2)}, u32[]{:S(2)}) collective-permute-start(bf16[64,2048]{1,0:T(8,128)(2,1)S(1)} %slice.47), channel_id=1, source_target_pairs={{0,2},{2,0},{12,14},{14,12},{1,3},{3,1},{13,15},{15,13},{16,18},{1... | collective-permute-start | bytes 786440 | tf_op jit(solution)/shard_map/ppermute | solution.py:184
  147.3 5.1 %collective-permute-done.13.refs_5_ = bf16[64,2048]{1,0:T(8,128)(2,1)S(1)} collective-permute-done((bf16[64,2048]{1,0:T(8,128)(2,1)S(1)}, bf16[64,2048]{1,0:T(8,128)(2,1)S(1)}, u32[]{:S(2)}, u32[]{:S(2)}) %collective-permute-start.13) | collective-permute-done | bytes 262176 | tf_op jit(solution)/shard_map/ppermute | solution.py:184
  152.4 3.5 %collective-permute-start.16 = (bf16[64,6144]{1,0:T(8,128)(2,1)S(1)}, bf16[64,6144]{1,0:T(8,128)(2,1)S(1)}, u32[]{:S(2)}, u32[]{:S(2)}) collective-permute-start(bf16[64,6144]{1,0:T(8,128)(2,1)S(1)} %slice.48), channel_id=1, source_target_pairs={{0,2},{2,0},{12,14},{14,12},{1,3},{3,1},{13,15},{15,13},{16,18},{1... | collective-permute-start | bytes 2359304 | tf_op jit(solution)/shard_map/ppermute | solution.py:184
  160.0 4.3 %rotate.9.refs_8_ = f32[192,1792]{1,0:T(8,128)S(1)} custom-call(s32[1]{0:T(128)} %bitcast.13.refs_0_.refs_1_, bf16[64,14336]{1,0:T(8,128)(2,1)S(1)} %collective-permute-done.7.refs_1_, bf16[64,14336]{1,0:T(8,128)(2,1)S(1)} %collective-permute-done.5.refs_2_, bf16[64,14336]{1,0:T(8,128)(2,1)S(1)} %collective-permute-done.12.refs_3_, ...), custom_call_target="tpu_custom_call" | custom-call | flops 344064 | bytes 1376256 | tf_op jit(solution)/shard_map/rotate/pallas_call | solution.py:125
  164.3 4.0 %collective-permute-done.18 = bf16[512,512]{1,0:T(8,128)(2,1)S(1)} collective-permute-done((bf16[512,512]{1,0:T(8,128)(2,1)S(1)}, bf16[512,512]{1,0:T(8,128)(2,1)S(1)}, u32[]{:S(2)}, u32[]{:S(2)}) %collective-permute-start.18) | collective-permute-done | bytes 524320 | tf_op jit(solution)/shard_map/ppermute | solution.py:184
  168.3 1.8 collective-permute-done.16.refs_5_
  170.1 3.5 %collective-permute-start.20 = (bf16[64,6144]{1,0:T(8,128)(2,1)S(1)}, bf16[64,6144]{1,0:T(8,128)(2,1)S(1)}, u32[]{:S(2)}, u32[]{:S(2)}) collective-permute-start(bf16[64,6144]{1,0:T(8,128)(2,1)S(1)} %slice.50), channel_id=1, source_target_pairs={{0,2},{2,0},{12,14},{14,12},{1,3},{3,1},{13,15},{15,13},{16,18},{1... | collective-permute-start | bytes 2359304 | tf_op jit(solution)/shard_map/ppermute | solution.py:184
  177.4 10.9 %rotate.10.refs_8_ = f32[192,1792]{1,0:T(8,128)S(1)} custom-call(s32[1]{0:T(128)} %bitcast.13.refs_0_.refs_1_, bf16[64,14336]{1,0:T(8,128)(2,1)S(1)} %collective-permute-done.7.refs_1_, bf16[64,14336]{1,0:T(8,128)(2,1)S(1)} %collective-permute-done.5.refs_2_, bf16[64,14336]{1,0:T(8,128)(2,1)S(1)} %collective-permute-done.12.refs_3_, ...), custom_call_target="tpu_custom_call" | custom-call | flops 344064 | bytes 1376256 | tf_op jit(solution)/shard_map/rotate/pallas_call | solution.py:125
  189.1 1.7 collective-permute-done.22
  190.8 5.6 %collective-permute-done.23 = bf16[512,512]{1,0:T(8,128)(2,1)S(1)} collective-permute-done((bf16[512,512]{1,0:T(8,128)(2,1)S(1)}, bf16[512,512]{1,0:T(8,128)(2,1)S(1)}, u32[]{:S(2)}, u32[]{:S(2)}) %collective-permute-start.23) | collective-permute-done | bytes 524320 | tf_op jit(solution)/shard_map/ppermute | solution.py:184
  197.7 10.9 %rotate.11.refs_4_ = f32[192,1792]{1,0:T(8,128)S(1)} custom-call(s32[1]{0:T(128)} %bitcast.13.refs_0_.refs_1_, bf16[64,14336]{1,0:T(8,128)(2,1)S(1)} %collective-permute-done.7.refs_1_, bf16[64,14336]{1,0:T(8,128)(2,1)S(1)} %collective-permute-done.5.refs_2_, bf16[64,14336]{1,0:T(8,128)(2,1)S(1)} %collective-permute-done.12.refs_3_, ...), custom_call_target="tpu_custom_call" | custom-call | flops 344064 | bytes 1376256 | tf_op jit(solution)/shard_map/rotate/pallas_call | solution.py:125
  208.6 4.0 %collective-permute-done.25.refs_9_ = bf16[512,512]{1,0:T(8,128)(2,1)S(1)} collective-permute-done((bf16[512,512]{1,0:T(8,128)(2,1)S(1)}, bf16[512,512]{1,0:T(8,128)(2,1)S(1)}, u32[]{:S(2)}, u32[]{:S(2)}) %collective-permute-start.25) | collective-permute-done | bytes 524320 | tf_op jit(solution)/shard_map/ppermute | solution.py:184
  216.9 12.5 %fit.1 = f32[1792,2048]{1,0:T(8,128)} custom-call(s32[8]{0:T(128)} %stack.50.refs_0_, s32[1]{0:T(128)} %bitcast.13.refs_0_.refs_1_, s32[4]{0:T(128)} %pad_add_fusion.refs_2_, bf16[320,1792]{1,0:T(8,128)(2,1)} %add_convert_fusion.refs_3_, f32[192,1792]{1,0:T(8,128)} %copy-done.4, f32[192,1792]{1,0:T(8,128)} %copy-done.6, ...), custom_call_target="tpu_custom_call" | custom-call | flops 3758096384 | bytes 24117248 | tf_op jit(solution)/shard_map/fit/pallas_call | solution.py:64
  (67 shorter events, 26.2 us)
Async XLA Ops:
  0.0 9.1 %copy-start = (bf16[512,1024]{1,0:T(8,128)(2,1)S(1)}, bf16[512,1024]{1,0:T(8,128)(2,1)}, u32[]{:S(2)}) copy-start(bf16[512,1024]{1,0:T(8,128)(2,1)} %param.5) | copy-start | bytes 3145732
  0.0 43.3 %collective-permute-start = (bf16[64,14336]{1,0:T(8,128)(2,1)}, bf16[64,14336]{1,0:T(8,128)(2,1)}, u32[]{:S(2)}, u32[]{:S(2)}) collective-permute-start(bf16[64,14336]{1,0:T(8,128)(2,1)} %refs_1_.3), channel_id=1, source_target_pairs={{0,2},{2,0},{4,6},{6,4},{8,10},{10,8},{12,14},{14,12},{1,3},{3,1},... | collective-permute-start | bytes 5505032 | tf_op jit(solution)/shard_map/ppermute | solution.py:184
  2.9 42.3 %collective-permute-start.1 = (bf16[64,14336]{1,0:T(8,128)(2,1)}, bf16[64,14336]{1,0:T(8,128)(2,1)}, u32[]{:S(2)}, u32[]{:S(2)}) collective-permute-start(bf16[64,14336]{1,0:T(8,128)(2,1)} %refs_1_.3), channel_id=1, source_target_pairs={{0,4},{2,6},{4,0},{6,2},{8,12},{10,14},{12,8},{14,10},{1,5},{3,7},... | collective-permute-start | bytes 5505032 | tf_op jit(solution)/shard_map/ppermute | solution.py:184
  4.5 40.8 %collective-permute-start.2 = (bf16[64,14336]{1,0:T(8,128)(2,1)}, bf16[64,14336]{1,0:T(8,128)(2,1)}, u32[]{:S(2)}, u32[]{:S(2)}) collective-permute-start(bf16[64,14336]{1,0:T(8,128)(2,1)} %refs_1_.3), channel_id=1, source_target_pairs={{4,8},{6,10},{8,4},{10,6},{5,9},{7,11},{9,5},{11,7},{20,24},{22,26... | collective-permute-start | bytes 5505032 | tf_op jit(solution)/shard_map/ppermute | solution.py:184
  14.2 74.5 %collective-permute-start.6 = (bf16[512,2048]{1,0:T(8,128)(2,1)}, bf16[512,2048]{1,0:T(8,128)(2,1)}, u32[]{:S(2)}, u32[]{:S(2)}) collective-permute-start(bf16[512,2048]{1,0:T(8,128)(2,1)} %get-tuple-element.117), channel_id=1, source_target_pairs={{0,4},{2,6},{12,8},{14,10},{1,5},{3,7},{13,9},{15,11},{16,20},{18,... | collective-permute-start | bytes 6291464 | tf_op jit(solution)/shard_map/ppermute | solution.py:184
  45.3 43.5 %collective-permute-start.3 = (bf16[64,14336]{1,0:T(8,128)(2,1)}, bf16[64,14336]{1,0:T(8,128)(2,1)}, u32[]{:S(2)}, u32[]{:S(2)}) collective-permute-start(bf16[64,14336]{1,0:T(8,128)(2,1)} %collective-permute-done.1.refs_2_), channel_id=1, source_target_pairs={{0,2},{2,0},{12,14},{14,12},{1,3},{3,1},{13,15},{15,13},{16,18},{1... | collective-permute-start | bytes 5505032 | tf_op jit(solution)/shard_map/ppermute | solution.py:184
  47.7 44.0 %collective-permute-start.4 = (bf16[64,14336]{1,0:T(8,128)(2,1)}, bf16[64,14336]{1,0:T(8,128)(2,1)}, u32[]{:S(2)}, u32[]{:S(2)}) collective-permute-start(bf16[64,14336]{1,0:T(8,128)(2,1)} %collective-permute-done.2.refs_2_.refs_5_), channel_id=1, source_target_pairs={{4,0},{6,2},{8,12},{10,14},{5,1},{7,3},{9,13},{11,15},{20,16},{22,... | collective-permute-start | bytes 5505032 | tf_op jit(solution)/shard_map/ppermute | solution.py:184
  49.0 42.7 %collective-permute-start.5 = (bf16[64,14336]{1,0:T(8,128)(2,1)}, bf16[64,14336]{1,0:T(8,128)(2,1)S(1)}, u32[]{:S(2)}, u32[]{:S(2)}) collective-permute-start(bf16[64,14336]{1,0:T(8,128)(2,1)} %collective-permute-done.1.refs_2_), channel_id=1, source_target_pairs={{4,8},{6,10},{8,4},{10,6},{5,9},{7,11},{9,5},{11,7},{20,24},{22,26... | collective-permute-start | bytes 5505032 | tf_op jit(solution)/shard_map/ppermute | solution.py:184
  49.8 43.1 %collective-permute-start.9 = (bf16[64,14336]{1,0:T(8,128)(2,1)}, bf16[64,14336]{1,0:T(8,128)(2,1)}, u32[]{:S(2)}, u32[]{:S(2)}) collective-permute-start(bf16[64,14336]{1,0:T(8,128)(2,1)} %collective-permute-done.2.refs_2_.refs_5_), channel_id=1, source_target_pairs={{4,6},{6,4},{8,10},{10,8},{5,7},{7,5},{9,11},{11,9},{20,22},{22,20... | collective-permute-start | bytes 5505032 | tf_op jit(solution)/shard_map/ppermute | solution.py:184
  53.2 38.5 %copy-start.5 = (f32[512,2048]{1,0:T(8,128)S(1)}, f32[512,2048]{1,0:T(8,128)}, u32[]{:S(2)}) copy-start(f32[512,2048]{1,0:T(8,128)} %get-tuple-element.69) | copy-start | bytes 12582916
  93.0 30.8 %collective-permute-start.10 = (bf16[64,8192]{1,0:T(8,128)(2,1)S(1)}, bf16[64,8192]{1,0:T(8,128)(2,1)S(1)}, u32[]{:S(2)}, u32[]{:S(2)}) collective-permute-start(bf16[64,8192]{1,0:T(8,128)(2,1)S(1)} %slice.41), channel_id=1, source_target_pairs={{4,6},{6,4},{8,10},{10,8},{5,7},{7,5},{9,11},{11,9},{20,22},{22,20... | collective-permute-start | bytes 3145736 | tf_op jit(solution)/shard_map/ppermute | solution.py:184
  93.8 30.1 %collective-permute-start.8 = (f32[512,512]{1,0:T(8,128)S(1)}, f32[512,512]{1,0:T(8,128)S(1)}, u32[]{:S(2)}, u32[]{:S(2)}) collective-permute-start(f32[512,512]{1,0:T(8,128)S(1)} %convert_add_fusion.2), channel_id=1, source_target_pairs={{4,8},{6,10},{8,4},{10,6},{5,9},{7,11},{9,5},{11,7},{20,24},{22,26... | collective-permute-start | bytes 3145736 | tf_op jit(solution)/shard_map/ppermute | solution.py:184
  94.5 46.5 %collective-permute-start.12 = (bf16[64,14336]{1,0:T(8,128)(2,1)}, bf16[64,14336]{1,0:T(8,128)(2,1)S(1)}, u32[]{:S(2)}, u32[]{:S(2)}) collective-permute-start(bf16[64,14336]{1,0:T(8,128)(2,1)} %collective-permute-done.4.refs_1_.refs_4_), channel_id=1, source_target_pairs={{0,2},{2,0},{12,14},{14,12},{1,3},{3,1},{13,15},{15,13},{16,18},{1... | collective-permute-start | bytes 5505032 | tf_op jit(solution)/shard_map/ppermute | solution.py:184
  97.0 46.7 %collective-permute-start.7 = (bf16[64,14336]{1,0:T(8,128)(2,1)S(1)}, bf16[64,14336]{1,0:T(8,128)(2,1)S(1)}, u32[]{:S(2)}, u32[]{:S(2)}) collective-permute-start(bf16[64,14336]{1,0:T(8,128)(2,1)S(1)} %collective-permute-done.5.refs_2_), channel_id=1, source_target_pairs={{4,0},{6,2},{8,12},{10,14},{5,1},{7,3},{9,13},{11,15},{20,16},{22,... | collective-permute-start | bytes 5505032 | tf_op jit(solution)/shard_map/ppermute | solution.py:184
  98.3 49.0 %collective-permute-start.15 = (bf16[64,14336]{1,0:T(8,128)(2,1)}, bf16[64,14336]{1,0:T(8,128)(2,1)S(1)}, u32[]{:S(2)}, u32[]{:S(2)}) collective-permute-start(bf16[64,14336]{1,0:T(8,128)(2,1)} %collective-permute-done.refs_3_), channel_id=1, source_target_pairs={{0,4},{2,6},{12,8},{14,10},{1,5},{3,7},{13,9},{15,11},{16,20},{18,... | collective-permute-start | bytes 5505032 | tf_op jit(solution)/shard_map/ppermute | solution.py:184
  123.9 28.4 %collective-permute-start.14 = (f32[512,512]{1,0:T(8,128)S(1)}, f32[512,512]{1,0:T(8,128)S(1)}, u32[]{:S(2)}, u32[]{:S(2)}) collective-permute-start(f32[512,512]{1,0:T(8,128)S(1)} %convert_add_fusion.1), channel_id=1, source_target_pairs={{4,8},{6,10},{8,4},{10,6},{5,9},{7,11},{9,5},{11,7},{20,24},{22,26... | collective-permute-start | bytes 3145736 | tf_op jit(solution)/shard_map/ppermute | solution.py:184
  125.0 16.0 %collective-permute-start.11 = (bf16[512,512]{1,0:T(8,128)(2,1)S(1)}, bf16[512,512]{1,0:T(8,128)(2,1)S(1)}, u32[]{:S(2)}, u32[]{:S(2)}) collective-permute-start(bf16[512,512]{1,0:T(8,128)(2,1)S(1)} %fusion.7), channel_id=1, source_target_pairs={{4,6},{6,4},{8,10},{10,8},{5,7},{7,5},{9,11},{11,9},{20,22},{22,20... | collective-permute-start | bytes 1572872 | tf_op jit(solution)/shard_map/ppermute | solution.py:184
  143.7 8.6 %collective-permute-start.13 = (bf16[64,2048]{1,0:T(8,128)(2,1)S(1)}, bf16[64,2048]{1,0:T(8,128)(2,1)S(1)}, u32[]{:S(2)}, u32[]{:S(2)}) collective-permute-start(bf16[64,2048]{1,0:T(8,128)(2,1)S(1)} %slice.47), channel_id=1, source_target_pairs={{0,2},{2,0},{12,14},{14,12},{1,3},{3,1},{13,15},{15,13},{16,18},{1... | collective-permute-start | bytes 786440 | tf_op jit(solution)/shard_map/ppermute | solution.py:184
  152.4 17.6 %collective-permute-start.16 = (bf16[64,6144]{1,0:T(8,128)(2,1)S(1)}, bf16[64,6144]{1,0:T(8,128)(2,1)S(1)}, u32[]{:S(2)}, u32[]{:S(2)}) collective-permute-start(bf16[64,6144]{1,0:T(8,128)(2,1)S(1)} %slice.48), channel_id=1, source_target_pairs={{0,2},{2,0},{12,14},{14,12},{1,3},{3,1},{13,15},{15,13},{16,18},{1... | collective-permute-start | bytes 2359304 | tf_op jit(solution)/shard_map/ppermute | solution.py:184
  156.5 7.8 %collective-permute-start.17 = (bf16[512,512]{1,0:T(8,128)(2,1)S(1)}, bf16[512,512]{1,0:T(8,128)(2,1)S(1)}, u32[]{:S(2)}, u32[]{:S(2)}) collective-permute-start(bf16[512,512]{1,0:T(8,128)(2,1)S(1)} %get-tuple-element.96), channel_id=1, source_target_pairs={{4,8},{6,10},{8,4},{10,6},{5,9},{7,11},{9,5},{11,7},{20,24},{22,26... | collective-permute-start | bytes 1572872 | tf_op jit(solution)/shard_map/ppermute | solution.py:184
  157.2 11.1 %collective-permute-start.18 = (bf16[512,512]{1,0:T(8,128)(2,1)S(1)}, bf16[512,512]{1,0:T(8,128)(2,1)S(1)}, u32[]{:S(2)}, u32[]{:S(2)}) collective-permute-start(bf16[512,512]{1,0:T(8,128)(2,1)S(1)} %get-tuple-element.96), channel_id=1, source_target_pairs={{4,0},{6,2},{8,12},{10,14},{5,1},{7,3},{9,13},{11,15},{20,16},{22,... | collective-permute-start | bytes 1572872 | tf_op jit(solution)/shard_map/ppermute | solution.py:184
  158.5 9.8 %collective-permute-start.19 = (bf16[512,512]{1,0:T(8,128)(2,1)S(1)}, bf16[512,512]{1,0:T(8,128)(2,1)S(1)}, u32[]{:S(2)}, u32[]{:S(2)}) collective-permute-start(bf16[512,512]{1,0:T(8,128)(2,1)S(1)} %get-tuple-element.115), channel_id=1, source_target_pairs={{4,6},{6,4},{8,10},{10,8},{5,7},{7,5},{9,11},{11,9},{20,22},{22,20... | collective-permute-start | bytes 1572872 | tf_op jit(solution)/shard_map/ppermute | solution.py:184
  159.3 29.9 %collective-permute-start.24 = (bf16[64,6144]{1,0:T(8,128)(2,1)S(1)}, bf16[64,6144]{1,0:T(8,128)(2,1)S(1)}, u32[]{:S(2)}, u32[]{:S(2)}) collective-permute-start(bf16[64,6144]{1,0:T(8,128)(2,1)S(1)} %slice.51), channel_id=1, source_target_pairs={{4,6},{6,4},{8,10},{10,8},{5,7},{7,5},{9,11},{11,9},{20,22},{22,20... | collective-permute-start | bytes 2359304 | tf_op jit(solution)/shard_map/ppermute | solution.py:184
  170.1 26.3 %collective-permute-start.20 = (bf16[64,6144]{1,0:T(8,128)(2,1)S(1)}, bf16[64,6144]{1,0:T(8,128)(2,1)S(1)}, u32[]{:S(2)}, u32[]{:S(2)}) collective-permute-start(bf16[64,6144]{1,0:T(8,128)(2,1)S(1)} %slice.50), channel_id=1, source_target_pairs={{0,2},{2,0},{12,14},{14,12},{1,3},{3,1},{13,15},{15,13},{16,18},{1... | collective-permute-start | bytes 2359304 | tf_op jit(solution)/shard_map/ppermute | solution.py:184
  173.9 15.2 %collective-permute-start.21 = (bf16[512,512]{1,0:T(8,128)(2,1)S(1)}, bf16[512,512]{1,0:T(8,128)(2,1)S(1)}, u32[]{:S(2)}, u32[]{:S(2)}) collective-permute-start(bf16[512,512]{1,0:T(8,128)(2,1)S(1)} %add_convert_fusion.1), channel_id=1, source_target_pairs={{4,8},{6,10},{8,4},{10,6},{5,9},{7,11},{9,5},{11,7},{20,24},{22,26... | collective-permute-start | bytes 1572872 | tf_op jit(solution)/shard_map/ppermute | solution.py:184
  174.6 16.2 %collective-permute-start.22 = (bf16[512,512]{1,0:T(8,128)(2,1)S(1)}, bf16[512,512]{1,0:T(8,128)(2,1)S(1)}, u32[]{:S(2)}, u32[]{:S(2)}) collective-permute-start(bf16[512,512]{1,0:T(8,128)(2,1)S(1)} %add_convert_fusion.1), channel_id=1, source_target_pairs={{4,0},{6,2},{8,12},{10,14},{5,1},{7,3},{9,13},{11,15},{20,16},{22,... | collective-permute-start | bytes 1572872 | tf_op jit(solution)/shard_map/ppermute | solution.py:184
  175.9 20.5 %collective-permute-start.23 = (bf16[512,512]{1,0:T(8,128)(2,1)S(1)}, bf16[512,512]{1,0:T(8,128)(2,1)S(1)}, u32[]{:S(2)}, u32[]{:S(2)}) collective-permute-start(bf16[512,512]{1,0:T(8,128)(2,1)S(1)} %collective-permute-done.17), channel_id=1, source_target_pairs={{4,0},{6,2},{8,12},{10,14},{5,1},{7,3},{9,13},{11,15},{20,16},{22,... | collective-permute-start | bytes 1572872 | tf_op jit(solution)/shard_map/ppermute | solution.py:184
  189.1 19.5 %copy-start.7 = (bf16[512,512]{1,0:T(8,128)(2,1)}, bf16[512,512]{1,0:T(8,128)(2,1)S(1)}, u32[]{:S(2)}) copy-start(bf16[512,512]{1,0:T(8,128)(2,1)S(1)} %collective-permute-done.21.refs_10_) | copy-start | bytes 1572868
  196.4 16.2 %collective-permute-start.26 = (f32[320,1792]{1,0:T(8,128)S(1)}, f32[320,1792]{1,0:T(8,128)S(1)}, u32[]{:S(2)}, u32[]{:S(2)}) collective-permute-start(f32[320,1792]{1,0:T(8,128)S(1)} %rotate.8), channel_id=1, source_target_pairs={{0,1},{1,0},{2,3},{3,2},{4,5},{5,4},{6,7},{7,6},{8,9},{9,8},{10,11... | collective-permute-start | bytes 6881288 | tf_op jit(solution)/shard_map/ppermute | solution.py:146
  196.4 16.2 %collective-permute-start.25 = (bf16[512,512]{1,0:T(8,128)(2,1)S(1)}, bf16[512,512]{1,0:T(8,128)(2,1)S(1)}, u32[]{:S(2)}, u32[]{:S(2)}) collective-permute-start(bf16[512,512]{1,0:T(8,128)(2,1)S(1)} %collective-permute-done.21.refs_10_), channel_id=1, source_target_pairs={{4,0},{6,2},{8,12},{10,14},{5,1},{7,3},{9,13},{11,15},{20,16},{22,... | collective-permute-start | bytes 1572872 | tf_op jit(solution)/shard_map/ppermute | solution.py:184
  212.6 3.1 %collective-permute-start.27 = (f32[192,1792]{1,0:T(8,128)S(1)}, f32[192,1792]{1,0:T(8,128)S(1)}, u32[]{:S(2)}, u32[]{:S(2)}) collective-permute-start(f32[192,1792]{1,0:T(8,128)S(1)} %rotate.11.refs_4_), channel_id=1, source_target_pairs={{0,1},{1,0},{2,3},{3,2},{4,5},{5,4},{6,7},{7,6},{8,9},{9,8},{10,11... | collective-permute-start | bytes 4128776 | tf_op jit(solution)/shard_map/ppermute | solution.py:146
  216.9 12.5 %copy-start.1 = (bf16[512,1024]{1,0:T(8,128)(2,1)S(1)}, bf16[512,1024]{1,0:T(8,128)(2,1)}, u32[]{:S(2)}) copy-start(bf16[512,1024]{1,0:T(8,128)(2,1)} %param.5) | copy-start | bytes 3145732
  (5 other events, 13.3 us)

commit v16 on v15

--- a/solution.py
+++ b/solution.py
@@ -191,7 +191,8 @@
     end = at_end.astype(jnp.int32).reshape(1)
     half = (z >= 2).astype(jnp.int32)
     steps = inputs.shape[1] // DEEP
-    cuts = [0, 2 * steps // 14, 8 * steps // 14, steps]
+    cuts = [0, 3 * steps // 14, 10 * steps // 14, steps]
+    middle = 6 * steps // 14
     part = basis_out.shape[1] // 4
     got = {"own": inputs}
 
@@ -206,11 +207,6 @@
 
     def turn(before, blocks, first, count):
         return rotate(before, end, [[(got[n], first) for n in block] for block in blocks], basis_in, first, count)
-
-    def settle(p):
-        got["sum", p] = (got["keep", p] + got["x5", p].astype(F32)).astype(BF16)
-        got["m4", p] = send(got["sum", p], MIDDLE)
-        got["n1", p] = send(got["sum", p], TO_ENDS)
 
     flip = jnp.where(z >= 2, 3, 0)
     line = lambda a, b: jnp.where(at_end, a, b) ^ flip
@@ -234,68 +230,60 @@
     blocks = [["own"], ["a1"], ["x1"]]
     got["A"] = turn([], blocks, 0, some)
     fence("x1", "x2", "a2", "m2", "out", "r1", "A")
-    def columns_of(p, q):
-        here = slice(p * part, q * part)
-        return got["out"][:, here] + got["r1"][:, here].astype(F32)
-
-    def cross(p):
-        here = slice(p * part, (p + 1) * part)
-        got["keep", p] = got["keep"][:, here] + got["m3", p]
-        got["x5", p] = send(got["keep", p].astype(BF16), ACROSS_MIDDLE)
-
+    cut = 2 * part
     got["x3"] = send(got["a2"], ACROSS_ENDS)
-    got["m3", 0] = send(columns_of(0, 1), MIDDLE)
+    got["m3"] = send((got["out"][:, :cut] + got["r1"][:, :cut].astype(F32)).astype(BF16), MIDDLE)
     got["a3"] = send(got["m2"], TO_ENDS)
     got["e"] = send(got["x1"], FROM_ENDS)
     fence(("x2", "m"), "m2", "out", "r1")
-    got["x3m", 0] = send(got["m2"][:, : cuts[2] * DEEP], ACROSS_MIDDLE)
-    got["give"], got["keep"] = columns_of(1, 2), columns_of(2, 4)
+    got["x3m", 0] = send(got["m2"][:, : middle * DEEP], ACROSS_MIDDLE)
+    got["keep"] = got["out"][:, cut:] + got["r1"][:, cut:].astype(F32)
     more = [["a2", "m1"], ["x2", ("x2", "m")]]
     got["B"] = turn([], more, 0, some)
-    fence(("m3", 0), ("x3m", 0), "give", "keep", "m2", "B")
-    cross(0)
-    got["m3", 1] = send(got["give"], MIDDLE)
+    fence("m3", ("x3m", 0), "keep", "m2", "B")
+    got["keep"] += got["m3"].astype(F32)
+    got["x5"] = send(got["keep"].astype(BF16), ACROSS_MIDDLE)
+    got["x3m", 1] = send(got["m2"][:, middle * DEEP :], ACROSS_MIDDLE)
     got["A"] = turn([got["A"], got["B"]], blocks + more, some, steps - some)
     fence("x3", "A")
-    fence("a3", ("x5", 0), "A")
+    fence("a3", "A")
 
     def x4(piece):
         got["x4", piece] = send(got["a3"][:, cuts[piece] * DEEP : cuts[piece + 1] * DEEP], ACROSS_ENDS)
 
-    def last(piece):
-        first, count = cuts[piece], cuts[piece + 1] - cuts[piece]
-        side = piece // 2
+    def last(piece, first, until):
+        side = int(first >= middle)
         blocks = [
             [(got["a3"], first), (got["m2"], first)],
-            [(got["x3"], first), (got["x3m", side], first - side * cuts[2])],
-            [(got["x4", piece], 0), (got["e"], first)],
+            [(got["x3"], first), (got["x3m", side], first - side * middle)],
+            [(got["x4", piece], first - cuts[piece]), (got["e"], first)],
         ]
-        got["D"] = rotate([got["D"]] if piece else [], end, blocks, basis_in, first, count)
+        got["D"] = rotate([got["D"]] if first else [], end, blocks, basis_in, first, until - first)
 
     x4(0)
-    settle(0)
-    fence(("x4", 0), ("m3", 1), "e", "m2", "a3", "A")
+    fence(("x4", 0), "x5", "e", "keep", "a3", "A")
+    got["sum"] = (got["keep"] + got["x5"].astype(F32)).astype(BF16)
+    got["m4"] = send(got["sum"], MIDDLE)
+    got["n1"] = send(got["sum"], TO_ENDS)
     x4(1)
-    cross(1)
-    got["x3m", 1] = send(got["m2"][:, cuts[2] * DEEP :], ACROSS_MIDDLE)
-    last(0)
-    fence(("x4", 1), ("m4", 0), ("n1", 0), ("sum", 0), ("x5", 1), "D", "a3")
+    last(0, 0, cuts[1])
+    fence("m4", "n1", "sum", ("x4", 1), ("x3m", 1), "a3", "A", "D")
+    got["n2", 0] = send(got["m4"][:, :part], TO_ENDS)
     x4(2)
-    got["n2", 0] = send(got["m4", 0], TO_ENDS)
-    settle(1)
-    got["R", 0] = pick(("n1", 0), ("sum", 0))
-    last(1)
-    fence(("x4", 2), ("m4", 1), ("n1", 1), ("sum", 1), ("n2", 0), ("m4", 0), ("x3m", 1), ("R", 0), "A", "D")
-    got["n2", 1] = send(got["m4", 1], TO_ENDS)
     got["A2"] = swap_narrow(got["A"])
-    got["R", 1] = pick(("n1", 1), ("sum", 1))
-    got["R", 2] = pick(("n2", 0), ("m4", 0))
-    last(2)
-    fence(("n2", 1), "A2", "D")
+    got["R", 0] = pick("n1", "sum")
+    last(1, cuts[1], middle)
+    last(1, middle, cuts[2])
+    fence(("x4", 2), ("n2", 0), "m4", ("R", 0), "A", "A2", "D")
+    got["n2", 1] = send(got["m4"][:, part:], TO_ENDS)
+    got["R", 1] = jnp.where(at_end, got["n2", 0], got["m4"][:, :part])
+    last(2, cuts[2], steps)
+    fence(("n2", 1), "D")
     got["D2"] = swap_narrow(got["D"])
     got["A"] = (got["A"] + got["A2"]).astype(BF16)
 
-    pieces = [[got["R", p]] for p in range(3)] + [[got["n2", 1], got["m4", 1]]]
+    pieces = [[got["R", 0][:, p * part : (p + 1) * part]] for p in range(2)]
+    pieces = pieces + [[got["R", 1]], [got["n2", 1], got["m4"][:, part:]]]
     return fit(got["order"], end, [[got["A"]], [got["D"], got["D2"]]], pieces, got["places"])
 
 

time: 231 us -> 227 us (0.983)
  starting transfers between devices: 55.3 us -> 47.3 us
  waiting for transfers between devices: 74.5 us -> 77.7 us
    ppermute x26 -> x22, starting transfers between devices: 55.3 us -> 47.3 us  [send(): return lax.ppermute(a, 'wide', perm)]
    ppermute x26 -> x22, waiting for transfers between devices: 73.7 us -> 76.9 us  [send(): return lax.ppermute(a, 'wide', perm)]
    add x3 -> x1, other arithmetic: 4.1 us -> 1.67 us  [scheduled(): got['keep'] = got['out'][:, cut:] + got['r1'][:, cut:].astype(F32)]
    pallas_call x6 -> x7, Pallas kernels: 66.3 us -> 68.1 us  [rotate(): pl.pallas_call(lambda *refs: rotate_kernel([len(block) for block in block...]
  transfers between devices with their start and end apart: 28 -> 24, of which waited for: 12 -> 12; matrix products, arithmetic and copies ran while one was open for 8% -> 7% of each run, Pallas kernels for 29% -> 30%
where the time goes in v16:
time: 227 us; the launch traced here: 226 us
  Pallas kernels  80.6 us (36%)
  waiting for transfers between devices  77.7 us (34%)
  starting transfers between devices  47.3 us (21%)
  local copies, waits for them, and re-layouts  7.51 us (3%)
  other arithmetic  7.06 us (3%)
  matrix products  5.12 us (2%)
    ppermute x22, waiting for transfers between devices, send(): return lax.ppermute(a, 'wide', perm)  76.9 us
    pallas_call x7, Pallas kernels, rotate(): pl.pallas_call(lambda *refs: rotate_kernel([len(block) for block in block...  68.1 us
    ppermute x22, starting transfers between devices, send(): return lax.ppermute(a, 'wide', perm)  47.3 us
    pallas_call x1, Pallas kernels, fit(): pl.pallas_call(lambda *refs: fit_kernel([len(halves) for halves in sums],...  12.5 us
    dot_general x1, matrix products, dot(): return jnp.dot(a, b, preferred_element_type=F32)  5.12 us
  transfers between devices with their start and end apart: 24, of which 12 were waited for; matrix products, arithmetic and copies ran while one was open for 7% of the time, Pallas kernels for 30%

profile of v16, /device:TPU:0, one launch (start us, length us, event | category | flops | bytes accessed | tf_op | source)
XLA Modules:
  0.0 225.6 jit_solution(9396701109576849309)
XLA Ops:
  0.0 2.9 %collective-permute-start = (bf16[64,14336]{1,0:T(8,128)(2,1)}, bf16[64,14336]{1,0:T(8,128)(2,1)}, u32[]{:S(2)}, u32[]{:S(2)}) collective-permute-start(bf16[64,14336]{1,0:T(8,128)(2,1)} %refs_1_.3), channel_id=1, source_target_pairs={{0,2},{2,0},{4,6},{6,4},{8,10},{10,8},{12,14},{14,12},{1,3},{3,1},... | collective-permute-start | bytes 5505032 | tf_op jit(solution)/shard_map/ppermute | solution.py:184
  2.9 1.6 collective-permute-start.1
  4.5 1.9 collective-permute-start.2
  6.5 2.7 %constant_dynamic-slice_fusion.1 = (bf16[1024,1024]{1,0:T(8,128)(2,1)S(1)}, bf16[1024,1024]{1,0:T(8,128)(2,1)S(1)}) fusion(bf16[1024,2048]{1,0:T(8,128)(2,1)} %param.7, s32[]{:T(128)S(6)} %select_n.56, s32[]{:T(128)S(6)} %select_n.57), kind=kLoop, calls=%fused_computation.14 | loop fusion | bytes 8388616 | tf_op jit(solution)/shard_map/dynamic_slice | solution.py:206
  9.1 5.1 %fusion.10 = (bf16[512,2048]{1,0:T(8,128)(2,1)}, f32[512,2048]{1,0:T(8,128)}) fusion(bf16[512,1024]{1,0:T(8,128)(2,1)S(1)} %copy-done, bf16[1024,1024]{1,0:T(8,128)(2,1)S(1)} %get-tuple-element.106, bf16[1024,1024]{1,0:T(8,128)(2,1)S(1)} %get-tuple-element.105), kind=kOutput, calls=%fused_computation.18 | convolution fusion | flops 2156920832 | bytes 11534336 | tf_op jit(solution)/shard_map/dot_general | solution.py:16
  14.3 6.4 %collective-permute-start.6 = (bf16[512,2048]{1,0:T(8,128)(2,1)}, bf16[512,2048]{1,0:T(8,128)(2,1)}, u32[]{:S(2)}, u32[]{:S(2)}) collective-permute-start(bf16[512,2048]{1,0:T(8,128)(2,1)} %get-tuple-element.111), channel_id=1, source_target_pairs={{0,4},{2,6},{12,8},{14,10},{1,5},{3,7},{13,9},{15,11},{16,20},{18,... | collective-permute-start | bytes 6291464 | tf_op jit(solution)/shard_map/ppermute | solution.py:184
  22.0 21.3 %collective-permute-done.refs_3_ = bf16[64,14336]{1,0:T(8,128)(2,1)} collective-permute-done((bf16[64,14336]{1,0:T(8,128)(2,1)}, bf16[64,14336]{1,0:T(8,128)(2,1)}, u32[]{:S(2)}, u32[]{:S(2)}) %collective-permute-start) | collective-permute-done | bytes 1835040 | tf_op jit(solution)/shard_map/ppermute | solution.py:184
  43.3 2.0 collective-permute-done.1.refs_2_
  45.3 2.4 %collective-permute-start.3 = (bf16[64,14336]{1,0:T(8,128)(2,1)}, bf16[64,14336]{1,0:T(8,128)(2,1)}, u32[]{:S(2)}, u32[]{:S(2)}) collective-permute-start(bf16[64,14336]{1,0:T(8,128)(2,1)} %collective-permute-done.1.refs_2_), channel_id=1, source_target_pairs={{0,2},{2,0},{12,14},{14,12},{1,3},{3,1},{13,15},{15,13},{16,18},{1... | collective-permute-start | bytes 5505032 | tf_op jit(solution)/shard_map/ppermute | solution.py:184
  49.8 1.9 collective-permute-start.9
  51.7 1.5 copy-done.2
  53.2 13.0 %rotate.7.refs_9_ = f32[192,1792]{1,0:T(8,128)S(1)} custom-call(s32[1]{0:T(128)} %bitcast.13.refs_0_.refs_1_, bf16[64,14336]{1,0:T(8,128)(2,1)S(1)} %copy-done.2, bf16[64,14336]{1,0:T(8,128)(2,1)} %collective-permute-done.1.refs_2_, bf16[64,14336]{1,0:T(8,128)(2,1)} %collective-permute-done.refs_3_, bf16[14336,1792]{1,0:T(8,128)(2,1)} %refs_7_.7), custom_call_target="tpu_custom_call" | custom-call | flops 344064 | bytes 1376256 | tf_op jit(solution)/shard_map/rotate/pallas_call | solution.py:125
  66.3 22.5 %collective-permute-done.6 = bf16[512,2048]{1,0:T(8,128)(2,1)} collective-permute-done((bf16[512,2048]{1,0:T(8,128)(2,1)}, bf16[512,2048]{1,0:T(8,128)(2,1)}, u32[]{:S(2)}, u32[]{:S(2)}) %collective-permute-start.6) | collective-permute-done | bytes 2097184 | tf_op jit(solution)/shard_map/ppermute | solution.py:184
  88.8 3.0 %collective-permute-done.4.refs_1_.refs_4_ = bf16[64,14336]{1,0:T(8,128)(2,1)} collective-permute-done((bf16[64,14336]{1,0:T(8,128)(2,1)}, bf16[64,14336]{1,0:T(8,128)(2,1)}, u32[]{:S(2)}, u32[]{:S(2)}) %collective-permute-start.4) | collective-permute-done | bytes 1835040 | tf_op jit(solution)/shard_map/ppermute | solution.py:184
  91.7 1.6 add_convert_fusion.2
  94.0 2.4 %collective-permute-start.8 = (bf16[64,14336]{1,0:T(8,128)(2,1)}, bf16[64,14336]{1,0:T(8,128)(2,1)S(1)}, u32[]{:S(2)}, u32[]{:S(2)}) collective-permute-start(bf16[64,14336]{1,0:T(8,128)(2,1)} %collective-permute-done.4.refs_1_.refs_4_), channel_id=1, source_target_pairs={{0,2},{2,0},{12,14},{14,12},{1,3},{3,1},{13,15},{15,13},{16,18},{1... | collective-permute-start | bytes 5505032 | tf_op jit(solution)/shard_map/ppermute | solution.py:184
  98.6 9.7 %collective-permute-start.14 = (bf16[64,14336]{1,0:T(8,128)(2,1)}, bf16[64,14336]{1,0:T(8,128)(2,1)S(1)}, u32[]{:S(2)}, u32[]{:S(2)}) collective-permute-start(bf16[64,14336]{1,0:T(8,128)(2,1)} %collective-permute-done.refs_3_), channel_id=1, source_target_pairs={{0,4},{2,6},{12,8},{14,10},{1,5},{3,7},{13,9},{15,11},{16,20},{18,... | collective-permute-start | bytes 5505032 | tf_op jit(solution)/shard_map/ppermute | solution.py:184
  108.3 12.0 %rotate.8.refs_10_ = f32[128,1792]{1,0:T(8,128)S(1)} custom-call(s32[1]{0:T(128)} %bitcast.13.refs_0_.refs_1_, bf16[64,14336]{1,0:T(8,128)(2,1)} %collective-permute-done.4.refs_1_.refs_4_, bf16[64,14336]{1,0:T(8,128)(2,1)} %collective-permute-done.2.refs_2_.refs_5_, bf16[64,14336]{1,0:T(8,128)(2,1)} %collective-permute-done.3.refs_3_.refs_6_, ...), custom_call_target="tpu_custom_call" | custom-call | flops 229376 | bytes 917504 | tf_op jit(solution)/shard_map/rotate/pallas_call | solution.py:125
  120.4 1.7 convert_add_fusion.1
  123.5 15.2 %rotate.9 = f32[320,1792]{1,0:T(8,128)S(1)} custom-call(s32[1]{0:T(128)} %bitcast.13.refs_0_.refs_1_, bf16[64,14336]{1,0:T(8,128)(2,1)S(1)} %copy-done.3, bf16[64,14336]{1,0:T(8,128)(2,1)} %collective-permute-done.1.refs_2_, bf16[64,14336]{1,0:T(8,128)(2,1)} %collective-permute-done.refs_3_, bf16[64,14336]{1,0:T(8,128)(2,1)} %collective-permute-done.4.refs_1_.refs_4_, ...), custom_call_target="tpu_custom_call" | custom-call | flops 573440 | bytes 2293760 | tf_op jit(solution)/shard_map/rotate/pallas_call | solution.py:125
  138.8 2.1 collective-permute-done.7.refs_1_
  141.0 2.3 %collective-permute-start.12 = (bf16[64,3072]{1,0:T(8,128)(2,1)S(1)}, bf16[64,3072]{1,0:T(8,128)(2,1)S(1)}, u32[]{:S(2)}, u32[]{:S(2)}) collective-permute-start(bf16[64,3072]{1,0:T(8,128)(2,1)S(1)} %slice.48), channel_id=1, source_target_pairs={{0,2},{2,0},{12,14},{14,12},{1,3},{3,1},{13,15},{15,13},{16,18},{1... | collective-permute-start | bytes 1179656 | tf_op jit(solution)/shard_map/ppermute | solution.py:184
  144.7 5.9 %collective-permute-done.12.refs_5_ = bf16[64,3072]{1,0:T(8,128)(2,1)S(1)} collective-permute-done((bf16[64,3072]{1,0:T(8,128)(2,1)S(1)}, bf16[64,3072]{1,0:T(8,128)(2,1)S(1)}, u32[]{:S(2)}, u32[]{:S(2)}) %collective-permute-start.12) | collective-permute-done | bytes 393248 | tf_op jit(solution)/shard_map/ppermute | solution.py:184
  153.1 2.3 %collective-permute-start.17 = (bf16[64,7168]{1,0:T(8,128)(2,1)S(1)}, bf16[64,7168]{1,0:T(8,128)(2,1)S(1)}, u32[]{:S(2)}, u32[]{:S(2)}) collective-permute-start(bf16[64,7168]{1,0:T(8,128)(2,1)S(1)} %slice.49), channel_id=1, source_target_pairs={{0,2},{2,0},{12,14},{14,12},{1,3},{3,1},{13,15},{15,13},{16,18},{1... | collective-permute-start | bytes 2752520 | tf_op jit(solution)/shard_map/ppermute | solution.py:184
  155.4 6.3 %rotate.10.refs_8_ = f32[192,1792]{1,0:T(8,128)S(1)} custom-call(s32[1]{0:T(128)} %bitcast.13.refs_0_.refs_1_, bf16[64,14336]{1,0:T(8,128)(2,1)S(1)} %collective-permute-done.7.refs_1_, bf16[64,14336]{1,0:T(8,128)(2,1)S(1)} %collective-permute-done.5.refs_2_, bf16[64,14336]{1,0:T(8,128)(2,1)S(1)} %collective-permute-done.8.refs_3_, ...), custom_call_target="tpu_custom_call" | custom-call | flops 344064 | bytes 1376256 | tf_op jit(solution)/shard_map/rotate/pallas_call | solution.py:125
  161.7 10.9 %collective-permute-done.17.refs_5_ = bf16[64,7168]{1,0:T(8,128)(2,1)S(1)} collective-permute-done((bf16[64,7168]{1,0:T(8,128)(2,1)S(1)}, bf16[64,7168]{1,0:T(8,128)(2,1)S(1)}, u32[]{:S(2)}, u32[]{:S(2)}) %collective-permute-start.17) | collective-permute-done | bytes 917536 | tf_op jit(solution)/shard_map/ppermute | solution.py:184
  174.2 2.2 collective-permute-start.19
  177.9 6.3 %rotate.11.refs_8_ = f32[192,1792]{1,0:T(8,128)S(1)} custom-call(s32[1]{0:T(128)} %bitcast.13.refs_0_.refs_1_, bf16[64,14336]{1,0:T(8,128)(2,1)S(1)} %collective-permute-done.7.refs_1_, bf16[64,14336]{1,0:T(8,128)(2,1)S(1)} %collective-permute-done.5.refs_2_, bf16[64,14336]{1,0:T(8,128)(2,1)S(1)} %collective-permute-done.8.refs_3_, ...), custom_call_target="tpu_custom_call" | custom-call | flops 344064 | bytes 1376256 | tf_op jit(solution)/shard_map/rotate/pallas_call | solution.py:125
  184.2 7.6 %rotate.12.refs_8_ = f32[192,1792]{1,0:T(8,128)S(1)} custom-call(s32[1]{0:T(128)} %bitcast.13.refs_0_.refs_1_, bf16[64,14336]{1,0:T(8,128)(2,1)S(1)} %collective-permute-done.7.refs_1_, bf16[64,14336]{1,0:T(8,128)(2,1)S(1)} %collective-permute-done.5.refs_2_, bf16[64,14336]{1,0:T(8,128)(2,1)S(1)} %collective-permute-done.8.refs_3_, ...), custom_call_target="tpu_custom_call" | custom-call | flops 344064 | bytes 1376256 | tf_op jit(solution)/shard_map/rotate/pallas_call | solution.py:125
  194.6 7.6 %rotate.13.refs_4_ = f32[192,1792]{1,0:T(8,128)S(1)} custom-call(s32[1]{0:T(128)} %bitcast.13.refs_0_.refs_1_, bf16[64,14336]{1,0:T(8,128)(2,1)S(1)} %collective-permute-done.7.refs_1_, bf16[64,14336]{1,0:T(8,128)(2,1)S(1)} %collective-permute-done.5.refs_2_, bf16[64,14336]{1,0:T(8,128)(2,1)S(1)} %collective-permute-done.8.refs_3_, ...), custom_call_target="tpu_custom_call" | custom-call | flops 344064 | bytes 1376256 | tf_op jit(solution)/shard_map/rotate/pallas_call | solution.py:125
  202.2 6.6 %collective-permute-done.22.refs_9_ = bf16[512,512]{1,0:T(8,128)(2,1)S(1)} collective-permute-done((bf16[512,512]{1,0:T(8,128)(2,1)S(1)}, bf16[512,512]{1,0:T(8,128)(2,1)S(1)}, u32[]{:S(2)}, u32[]{:S(2)}) %collective-permute-start.22) | collective-permute-done | bytes 524320 | tf_op jit(solution)/shard_map/ppermute | solution.py:184
  213.1 12.5 %fit.1 = f32[1792,2048]{1,0:T(8,128)} custom-call(s32[8]{0:T(128)} %stack.50.refs_0_, s32[1]{0:T(128)} %bitcast.13.refs_0_.refs_1_, s32[4]{0:T(128)} %pad_add_fusion.refs_2_, bf16[320,1792]{1,0:T(8,128)(2,1)} %add_convert_fusion.refs_3_, f32[192,1792]{1,0:T(8,128)} %copy-done.4, f32[192,1792]{1,0:T(8,128)} %copy-done.7, ...), custom_call_target="tpu_custom_call" | custom-call | flops 3758096384 | bytes 24117248 | tf_op jit(solution)/shard_map/fit/pallas_call | solution.py:64
  (60 shorter events, 21.4 us)
Async XLA Ops:
  0.0 9.1 %copy-start = (bf16[512,1024]{1,0:T(8,128)(2,1)S(1)}, bf16[512,1024]{1,0:T(8,128)(2,1)}, u32[]{:S(2)}) copy-start(bf16[512,1024]{1,0:T(8,128)(2,1)} %param.5) | copy-start | bytes 3145732
  0.0 43.3 %collective-permute-start = (bf16[64,14336]{1,0:T(8,128)(2,1)}, bf16[64,14336]{1,0:T(8,128)(2,1)}, u32[]{:S(2)}, u32[]{:S(2)}) collective-permute-start(bf16[64,14336]{1,0:T(8,128)(2,1)} %refs_1_.3), channel_id=1, source_target_pairs={{0,2},{2,0},{4,6},{6,4},{8,10},{10,8},{12,14},{14,12},{1,3},{3,1},... | collective-permute-start | bytes 5505032 | tf_op jit(solution)/shard_map/ppermute | solution.py:184
  2.9 42.3 %collective-permute-start.1 = (bf16[64,14336]{1,0:T(8,128)(2,1)}, bf16[64,14336]{1,0:T(8,128)(2,1)}, u32[]{:S(2)}, u32[]{:S(2)}) collective-permute-start(bf16[64,14336]{1,0:T(8,128)(2,1)} %refs_1_.3), channel_id=1, source_target_pairs={{0,4},{2,6},{4,0},{6,2},{8,12},{10,14},{12,8},{14,10},{1,5},{3,7},... | collective-permute-start | bytes 5505032 | tf_op jit(solution)/shard_map/ppermute | solution.py:184
  4.5 40.8 %collective-permute-start.2 = (bf16[64,14336]{1,0:T(8,128)(2,1)}, bf16[64,14336]{1,0:T(8,128)(2,1)}, u32[]{:S(2)}, u32[]{:S(2)}) collective-permute-start(bf16[64,14336]{1,0:T(8,128)(2,1)} %refs_1_.3), channel_id=1, source_target_pairs={{4,8},{6,10},{8,4},{10,6},{5,9},{7,11},{9,5},{11,7},{20,24},{22,26... | collective-permute-start | bytes 5505032 | tf_op jit(solution)/shard_map/ppermute | solution.py:184
  14.3 74.5 %collective-permute-start.6 = (bf16[512,2048]{1,0:T(8,128)(2,1)}, bf16[512,2048]{1,0:T(8,128)(2,1)}, u32[]{:S(2)}, u32[]{:S(2)}) collective-permute-start(bf16[512,2048]{1,0:T(8,128)(2,1)} %get-tuple-element.111), channel_id=1, source_target_pairs={{0,4},{2,6},{12,8},{14,10},{1,5},{3,7},{13,9},{15,11},{16,20},{18,... | collective-permute-start | bytes 6291464 | tf_op jit(solution)/shard_map/ppermute | solution.py:184
  45.3 43.5 %collective-permute-start.3 = (bf16[64,14336]{1,0:T(8,128)(2,1)}, bf16[64,14336]{1,0:T(8,128)(2,1)}, u32[]{:S(2)}, u32[]{:S(2)}) collective-permute-start(bf16[64,14336]{1,0:T(8,128)(2,1)} %collective-permute-done.1.refs_2_), channel_id=1, source_target_pairs={{0,2},{2,0},{12,14},{14,12},{1,3},{3,1},{13,15},{15,13},{16,18},{1... | collective-permute-start | bytes 5505032 | tf_op jit(solution)/shard_map/ppermute | solution.py:184
  47.7 44.0 %collective-permute-start.4 = (bf16[64,14336]{1,0:T(8,128)(2,1)}, bf16[64,14336]{1,0:T(8,128)(2,1)}, u32[]{:S(2)}, u32[]{:S(2)}) collective-permute-start(bf16[64,14336]{1,0:T(8,128)(2,1)} %collective-permute-done.2.refs_2_.refs_5_), channel_id=1, source_target_pairs={{4,0},{6,2},{8,12},{10,14},{5,1},{7,3},{9,13},{11,15},{20,16},{22,... | collective-permute-start | bytes 5505032 | tf_op jit(solution)/shard_map/ppermute | solution.py:184
  49.0 42.7 %collective-permute-start.5 = (bf16[64,14336]{1,0:T(8,128)(2,1)}, bf16[64,14336]{1,0:T(8,128)(2,1)S(1)}, u32[]{:S(2)}, u32[]{:S(2)}) collective-permute-start(bf16[64,14336]{1,0:T(8,128)(2,1)} %collective-permute-done.1.refs_2_), channel_id=1, source_target_pairs={{4,8},{6,10},{8,4},{10,6},{5,9},{7,11},{9,5},{11,7},{20,24},{22,26... | collective-permute-start | bytes 5505032 | tf_op jit(solution)/shard_map/ppermute | solution.py:184
  49.8 48.0 %collective-permute-start.9 = (bf16[64,14336]{1,0:T(8,128)(2,1)}, bf16[64,14336]{1,0:T(8,128)(2,1)}, u32[]{:S(2)}, u32[]{:S(2)}) collective-permute-start(bf16[64,14336]{1,0:T(8,128)(2,1)} %collective-permute-done.2.refs_2_.refs_5_), channel_id=1, source_target_pairs={{4,6},{6,4},{8,10},{10,8},{5,7},{7,5},{9,11},{11,9},{20,22},{22,20... | collective-permute-start | bytes 5505032 | tf_op jit(solution)/shard_map/ppermute | solution.py:184
  51.7 1.5 copy-start.2
  53.2 38.5 %copy-start.5 = (f32[512,2048]{1,0:T(8,128)S(1)}, f32[512,2048]{1,0:T(8,128)}, u32[]{:S(2)}) copy-start(f32[512,2048]{1,0:T(8,128)} %get-tuple-element.69) | copy-start | bytes 12582916
  93.3 28.8 %collective-permute-start.10 = (bf16[512,1024]{1,0:T(8,128)(2,1)S(1)}, bf16[512,1024]{1,0:T(8,128)(2,1)S(1)}, u32[]{:S(2)}, u32[]{:S(2)}) collective-permute-start(bf16[512,1024]{1,0:T(8,128)(2,1)S(1)} %add_convert_fusion.2), channel_id=1, source_target_pairs={{4,8},{6,10},{8,4},{10,6},{5,9},{7,11},{9,5},{11,7},{20,24},{22,26... | collective-permute-start | bytes 3145736 | tf_op jit(solution)/shard_map/ppermute | solution.py:184
  94.0 44.7 %collective-permute-start.8 = (bf16[64,14336]{1,0:T(8,128)(2,1)}, bf16[64,14336]{1,0:T(8,128)(2,1)S(1)}, u32[]{:S(2)}, u32[]{:S(2)}) collective-permute-start(bf16[64,14336]{1,0:T(8,128)(2,1)} %collective-permute-done.4.refs_1_.refs_4_), channel_id=1, source_target_pairs={{0,2},{2,0},{12,14},{14,12},{1,3},{3,1},{13,15},{15,13},{16,18},{1... | collective-permute-start | bytes 5505032 | tf_op jit(solution)/shard_map/ppermute | solution.py:184
  96.5 44.4 %collective-permute-start.7 = (bf16[64,14336]{1,0:T(8,128)(2,1)S(1)}, bf16[64,14336]{1,0:T(8,128)(2,1)S(1)}, u32[]{:S(2)}, u32[]{:S(2)}) collective-permute-start(bf16[64,14336]{1,0:T(8,128)(2,1)S(1)} %collective-permute-done.5.refs_2_), channel_id=1, source_target_pairs={{4,0},{6,2},{8,12},{10,14},{5,1},{7,3},{9,13},{11,15},{20,16},{22,... | collective-permute-start | bytes 5505032 | tf_op jit(solution)/shard_map/ppermute | solution.py:184
  97.9 24.2 %collective-permute-start.11 = (bf16[64,6144]{1,0:T(8,128)(2,1)S(1)}, bf16[64,6144]{1,0:T(8,128)(2,1)S(1)}, u32[]{:S(2)}, u32[]{:S(2)}) collective-permute-start(bf16[64,6144]{1,0:T(8,128)(2,1)S(1)} %slice.45), channel_id=1, source_target_pairs={{4,6},{6,4},{8,10},{10,8},{5,7},{7,5},{9,11},{11,9},{20,22},{22,20... | collective-permute-start | bytes 2359304 | tf_op jit(solution)/shard_map/ppermute | solution.py:184
  98.6 46.1 %collective-permute-start.14 = (bf16[64,14336]{1,0:T(8,128)(2,1)}, bf16[64,14336]{1,0:T(8,128)(2,1)S(1)}, u32[]{:S(2)}, u32[]{:S(2)}) collective-permute-start(bf16[64,14336]{1,0:T(8,128)(2,1)} %collective-permute-done.refs_3_), channel_id=1, source_target_pairs={{0,4},{2,6},{12,8},{14,10},{1,5},{3,7},{13,9},{15,11},{16,20},{18,... | collective-permute-start | bytes 5505032 | tf_op jit(solution)/shard_map/ppermute | solution.py:184
  122.0 1.5 copy-start.3
  122.6 22.0 %collective-permute-start.13 = (bf16[512,1024]{1,0:T(8,128)(2,1)S(1)}, bf16[512,1024]{1,0:T(8,128)(2,1)S(1)}, u32[]{:S(2)}, u32[]{:S(2)}) collective-permute-start(bf16[512,1024]{1,0:T(8,128)(2,1)S(1)} %get-tuple-element.103), channel_id=1, source_target_pairs={{4,6},{6,4},{8,10},{10,8},{5,7},{7,5},{9,11},{11,9},{20,22},{22,20... | collective-permute-start | bytes 3145736 | tf_op jit(solution)/shard_map/ppermute | solution.py:184
  141.0 9.7 %collective-permute-start.12 = (bf16[64,3072]{1,0:T(8,128)(2,1)S(1)}, bf16[64,3072]{1,0:T(8,128)(2,1)S(1)}, u32[]{:S(2)}, u32[]{:S(2)}) collective-permute-start(bf16[64,3072]{1,0:T(8,128)(2,1)S(1)} %slice.48), channel_id=1, source_target_pairs={{0,2},{2,0},{12,14},{14,12},{1,3},{3,1},{13,15},{15,13},{16,18},{1... | collective-permute-start | bytes 1179656 | tf_op jit(solution)/shard_map/ppermute | solution.py:184
  143.4 18.4 %collective-permute-start.18 = (bf16[64,8192]{1,0:T(8,128)(2,1)S(1)}, bf16[64,8192]{1,0:T(8,128)(2,1)S(1)}, u32[]{:S(2)}, u32[]{:S(2)}) collective-permute-start(bf16[64,8192]{1,0:T(8,128)(2,1)S(1)} %slice.50), channel_id=1, source_target_pairs={{4,6},{6,4},{8,10},{10,8},{5,7},{7,5},{9,11},{11,9},{20,22},{22,20... | collective-permute-start | bytes 3145736 | tf_op jit(solution)/shard_map/ppermute | solution.py:184
  151.0 21.7 %collective-permute-start.15 = (bf16[512,1024]{1,0:T(8,128)(2,1)S(1)}, bf16[512,1024]{1,0:T(8,128)(2,1)S(1)}, u32[]{:S(2)}, u32[]{:S(2)}) collective-permute-start(bf16[512,1024]{1,0:T(8,128)(2,1)S(1)} %add_convert_fusion.1), channel_id=1, source_target_pairs={{4,8},{6,10},{8,4},{10,6},{5,9},{7,11},{9,5},{11,7},{20,24},{22,26... | collective-permute-start | bytes 3145736 | tf_op jit(solution)/shard_map/ppermute | solution.py:184
  151.7 22.4 %collective-permute-start.16 = (bf16[512,1024]{1,0:T(8,128)(2,1)S(1)}, bf16[512,1024]{1,0:T(8,128)(2,1)S(1)}, u32[]{:S(2)}, u32[]{:S(2)}) collective-permute-start(bf16[512,1024]{1,0:T(8,128)(2,1)S(1)} %add_convert_fusion.1), channel_id=1, source_target_pairs={{4,0},{6,2},{8,12},{10,14},{5,1},{7,3},{9,13},{11,15},{20,16},{22,... | collective-permute-start | bytes 3145736 | tf_op jit(solution)/shard_map/ppermute | solution.py:184
  153.1 19.6 %collective-permute-start.17 = (bf16[64,7168]{1,0:T(8,128)(2,1)S(1)}, bf16[64,7168]{1,0:T(8,128)(2,1)S(1)}, u32[]{:S(2)}, u32[]{:S(2)}) collective-permute-start(bf16[64,7168]{1,0:T(8,128)(2,1)S(1)} %slice.49), channel_id=1, source_target_pairs={{0,2},{2,0},{12,14},{14,12},{1,3},{3,1},{13,15},{15,13},{16,18},{1... | collective-permute-start | bytes 2752520 | tf_op jit(solution)/shard_map/ppermute | solution.py:184
  174.1 18.2 %collective-permute-start.21 = (f32[320,1792]{1,0:T(8,128)S(1)}, f32[320,1792]{1,0:T(8,128)S(1)}, u32[]{:S(2)}, u32[]{:S(2)}) collective-permute-start(f32[320,1792]{1,0:T(8,128)S(1)} %rotate.9), channel_id=1, source_target_pairs={{0,1},{1,0},{2,3},{3,2},{4,5},{5,4},{6,7},{7,6},{8,9},{9,8},{10,11... | collective-permute-start | bytes 6881288 | tf_op jit(solution)/shard_map/ppermute | solution.py:146
  174.2 17.8 %collective-permute-start.19 = (bf16[64,4096]{1,0:T(8,128)(2,1)S(1)}, bf16[64,4096]{1,0:T(8,128)(2,1)S(1)}, u32[]{:S(2)}, u32[]{:S(2)}) collective-permute-start(bf16[64,4096]{1,0:T(8,128)(2,1)S(1)} %slice.51), channel_id=1, source_target_pairs={{0,2},{2,0},{12,14},{14,12},{1,3},{3,1},{13,15},{15,13},{16,18},{1... | collective-permute-start | bytes 1572872 | tf_op jit(solution)/shard_map/ppermute | solution.py:184
  176.4 15.9 %collective-permute-start.20 = (bf16[512,512]{1,0:T(8,128)(2,1)S(1)}, bf16[512,512]{1,0:T(8,128)(2,1)S(1)}, u32[]{:S(2)}, u32[]{:S(2)}) collective-permute-start(bf16[512,512]{1,0:T(8,128)(2,1)S(1)} %slice.52), channel_id=1, source_target_pairs={{4,0},{6,2},{8,12},{10,14},{5,1},{7,3},{9,13},{11,15},{20,16},{22,... | collective-permute-start | bytes 1572872 | tf_op jit(solution)/shard_map/ppermute | solution.py:184
  193.3 8.9 %copy-start.6 = (bf16[512,512]{1,0:T(8,128)(2,1)}, bf16[512,512]{1,0:T(8,128)(2,1)S(1)}, u32[]{:S(2)}) copy-start(bf16[512,512]{1,0:T(8,128)(2,1)S(1)} %get-tuple-element.108.refs_10_) | copy-start | bytes 1572868
  193.3 15.6 %collective-permute-start.22 = (bf16[512,512]{1,0:T(8,128)(2,1)S(1)}, bf16[512,512]{1,0:T(8,128)(2,1)S(1)}, u32[]{:S(2)}, u32[]{:S(2)}) collective-permute-start(bf16[512,512]{1,0:T(8,128)(2,1)S(1)} %get-tuple-element.108.refs_10_), channel_id=1, source_target_pairs={{4,0},{6,2},{8,12},{10,14},{5,1},{7,3},{9,13},{11,15},{20,16},{22,... | collective-permute-start | bytes 1572872 | tf_op jit(solution)/shard_map/ppermute | solution.py:184
  202.2 9.0 %copy-start.4 = (f32[192,1792]{1,0:T(8,128)}, f32[192,1792]{1,0:T(8,128)S(1)}, u32[]{:S(2)}) copy-start(f32[192,1792]{1,0:T(8,128)S(1)} %rotate.13.refs_4_) | copy-start | bytes 4128772
  208.9 2.4 %copy-start.8 = (bf16[512,512]{1,0:T(8,128)(2,1)}, bf16[512,512]{1,0:T(8,128)(2,1)S(1)}, u32[]{:S(2)}) copy-start(bf16[512,512]{1,0:T(8,128)(2,1)S(1)} %collective-permute-done.22.refs_9_) | copy-start | bytes 1572868
  208.9 3.1 %collective-permute-start.23 = (f32[192,1792]{1,0:T(8,128)S(1)}, f32[192,1792]{1,0:T(8,128)S(1)}, u32[]{:S(2)}, u32[]{:S(2)}) collective-permute-start(f32[192,1792]{1,0:T(8,128)S(1)} %rotate.13.refs_4_), channel_id=1, source_target_pairs={{0,1},{1,0},{2,3},{3,2},{4,5},{5,4},{6,7},{7,6},{8,9},{9,8},{10,11... | collective-permute-start | bytes 4128776 | tf_op jit(solution)/shard_map/ppermute | solution.py:146
  213.1 12.5 %copy-start.1 = (bf16[512,1024]{1,0:T(8,128)(2,1)S(1)}, bf16[512,1024]{1,0:T(8,128)(2,1)}, u32[]{:S(2)}) copy-start(bf16[512,1024]{1,0:T(8,128)(2,1)} %param.5) | copy-start | bytes 3145732
  (1 other events, 1.1 us)

commit v17 on v16

--- a/solution.py
+++ b/solution.py
@@ -213,8 +213,7 @@
     mine, other = (lambda a, b: line(a, b) * PAIR + x), (lambda a, b: line(a, b) * PAIR + 1 - x)
     order = [mine(0, 1), mine(1, 0), other(0, 1), mine(2, 2), other(1, 2), mine(3, 3), other(2, 3), other(3, 0)]
     got["order"] = jnp.stack(order).astype(jnp.int32)
-    places = [2 * half, 2 * half + 1, 2 - 2 * half, 3 - 2 * half]
-    got["places"] = jnp.stack(places).astype(jnp.int32)
+    got["places"] = jnp.stack([half, 1 - half])
 
     got["x1"] = send(got["own"], ACROSS)
     got["a1"] = send(got["own"], ENDS)
@@ -267,24 +266,23 @@
     got["n1"] = send(got["sum"], TO_ENDS)
     x4(1)
     last(0, 0, cuts[1])
-    fence("m4", "n1", "sum", ("x4", 1), ("x3m", 1), "a3", "A", "D")
-    got["n2", 0] = send(got["m4"][:, :part], TO_ENDS)
+    fence(("x4", 1), ("x3m", 1), "m4", "n1", "sum", "a3", "A", "D")
     x4(2)
+    got["n2"] = send(got["m4"], TO_ENDS)
     got["A2"] = swap_narrow(got["A"])
-    got["R", 0] = pick("n1", "sum")
+    got["R"] = pick("n1", "sum")
     last(1, cuts[1], middle)
     last(1, middle, cuts[2])
-    fence(("x4", 2), ("n2", 0), "m4", ("R", 0), "A", "A2", "D")
-    got["n2", 1] = send(got["m4"][:, part:], TO_ENDS)
-    got["R", 1] = jnp.where(at_end, got["n2", 0], got["m4"][:, :part])
-    last(2, cuts[2], steps)
-    fence(("n2", 1), "D")
+    fence(("x4", 2), "A", "A2", "R", "D")
+    late = (cuts[2] + steps) // 2
+    last(2, cuts[2], late)
+    fence("n2", "m4", "R", "A", "A2", "D")
+    last(2, late, steps)
     got["D2"] = swap_narrow(got["D"])
     got["A"] = (got["A"] + got["A2"]).astype(BF16)
 
-    pieces = [[got["R", 0][:, p * part : (p + 1) * part]] for p in range(2)]
-    pieces = pieces + [[got["R", 1]], [got["n2", 1], got["m4"][:, part:]]]
-    return fit(got["order"], end, [[got["A"]], [got["D"], got["D2"]]], pieces, got["places"])
+    pieces, places = [[got["R"]], [got["n2"], got["m4"]]], got["places"]
+    return fit(got["order"], end, [[got["A"]], [got["D"], got["D2"]]], pieces, places)
 
 
 def solution(mesh):

time: 227 us -> 224 us (0.987)
    ppermute x22 -> x21, waiting for transfers between devices: 76.9 us -> 74.3 us  [send(): return lax.ppermute(a, 'wide', perm)]
    ppermute x22 -> x21, starting transfers between devices: 47.3 us -> 46 us  [send(): return lax.ppermute(a, 'wide', perm)]
    pallas_call x7 -> x8, Pallas kernels: 68.1 us -> 69.2 us  [rotate(): pl.pallas_call(lambda *refs: rotate_kernel([len(block) for block in block...]
  transfers between devices with their start and end apart: 24 -> 23, of which waited for: 12 -> 11; matrix products, arithmetic and copies ran while one was open for 7% -> 7% of each run, Pallas kernels for 30% -> 29%
where the time goes in v17:
time: 224 us; the launch traced here: 223 us
  Pallas kernels  81.9 us (37%)
  waiting for transfers between devices  76.1 us (34%)
  starting transfers between devices  46.1 us (21%)
  other arithmetic  7.27 us (3%)
  local copies, waits for them, and re-layouts  6.33 us (3%)
  matrix products  5.11 us (2%)
    ppermute x21, waiting for transfers between devices, send(): return lax.ppermute(a, 'wide', perm)  74.3 us
    pallas_call x8, Pallas kernels, rotate(): pl.pallas_call(lambda *refs: rotate_kernel([len(block) for block in block...  69.2 us
    ppermute x21, starting transfers between devices, send(): return lax.ppermute(a, 'wide', perm)  46 us
    pallas_call x1, Pallas kernels, fit(): pl.pallas_call(lambda *refs: fit_kernel([len(halves) for halves in sums],...  12.7 us
    dot_general x1, matrix products, dot(): return jnp.dot(a, b, preferred_element_type=F32)  5.11 us
  transfers between devices with their start and end apart: 23, of which 11 were waited for; matrix products, arithmetic and copies ran while one was open for 7% of the time, Pallas kernels for 29%

profile of v17, /device:TPU:0, one launch (start us, length us, event | category | flops | bytes accessed | tf_op | source)
XLA Modules:
  0.0 223.1 jit_solution(5362813028775867646)
XLA Ops:
  0.0 2.9 %collective-permute-start = (bf16[64,14336]{1,0:T(8,128)(2,1)}, bf16[64,14336]{1,0:T(8,128)(2,1)}, u32[]{:S(2)}, u32[]{:S(2)}) collective-permute-start(bf16[64,14336]{1,0:T(8,128)(2,1)} %refs_1_.3), channel_id=1, source_target_pairs={{0,2},{2,0},{4,6},{6,4},{8,10},{10,8},{12,14},{14,12},{1,3},{3,1},... | collective-permute-start | bytes 5505032 | tf_op jit(solution)/shard_map/ppermute | solution.py:184
  2.9 1.6 collective-permute-start.1
  4.5 2.0 collective-permute-start.2
  6.5 2.7 %constant_dynamic-slice_fusion.1 = (bf16[1024,1024]{1,0:T(8,128)(2,1)S(1)}, bf16[1024,1024]{1,0:T(8,128)(2,1)S(1)}) fusion(bf16[1024,2048]{1,0:T(8,128)(2,1)} %param.7, s32[]{:T(128)S(6)} %select_n.48, s32[]{:T(128)S(6)} %select_n.49), kind=kLoop, calls=%fused_computation.13 | loop fusion | bytes 8388616 | tf_op jit(solution)/shard_map/dynamic_slice | solution.py:206
  9.2 5.1 %fusion.9 = (bf16[512,2048]{1,0:T(8,128)(2,1)}, f32[512,2048]{1,0:T(8,128)}) fusion(bf16[512,1024]{1,0:T(8,128)(2,1)S(1)} %copy-done, bf16[1024,1024]{1,0:T(8,128)(2,1)S(1)} %get-tuple-element.110, bf16[1024,1024]{1,0:T(8,128)(2,1)S(1)} %get-tuple-element.109), kind=kOutput, calls=%fused_computation.16 | convolution fusion | flops 2156920832 | bytes 11534336 | tf_op jit(solution)/shard_map/dot_general | solution.py:16
  14.3 6.4 %collective-permute-start.6 = (bf16[512,2048]{1,0:T(8,128)(2,1)}, bf16[512,2048]{1,0:T(8,128)(2,1)}, u32[]{:S(2)}, u32[]{:S(2)}) collective-permute-start(bf16[512,2048]{1,0:T(8,128)(2,1)} %get-tuple-element.111), channel_id=1, source_target_pairs={{0,4},{2,6},{12,8},{14,10},{1,5},{3,7},{13,9},{15,11},{16,20},{18,... | collective-permute-start | bytes 6291464 | tf_op jit(solution)/shard_map/ppermute | solution.py:184
  21.9 21.4 %collective-permute-done.refs_3_ = bf16[64,14336]{1,0:T(8,128)(2,1)} collective-permute-done((bf16[64,14336]{1,0:T(8,128)(2,1)}, bf16[64,14336]{1,0:T(8,128)(2,1)}, u32[]{:S(2)}, u32[]{:S(2)}) %collective-permute-start) | collective-permute-done | bytes 1835040 | tf_op jit(solution)/shard_map/ppermute | solution.py:184
  43.3 2.0 collective-permute-done.1.refs_2_
  45.3 2.4 %collective-permute-start.3 = (bf16[64,14336]{1,0:T(8,128)(2,1)}, bf16[64,14336]{1,0:T(8,128)(2,1)}, u32[]{:S(2)}, u32[]{:S(2)}) collective-permute-start(bf16[64,14336]{1,0:T(8,128)(2,1)} %collective-permute-done.1.refs_2_), channel_id=1, source_target_pairs={{0,2},{2,0},{12,14},{14,12},{1,3},{3,1},{13,15},{15,13},{16,18},{1... | collective-permute-start | bytes 5505032 | tf_op jit(solution)/shard_map/ppermute | solution.py:184
  49.8 1.9 collective-permute-start.9
  53.2 13.0 %rotate.8.refs_9_ = f32[192,1792]{1,0:T(8,128)S(1)} custom-call(s32[1]{0:T(128)} %bitcast.11.refs_0_.refs_1_, bf16[64,14336]{1,0:T(8,128)(2,1)S(1)} %copy-done.2, bf16[64,14336]{1,0:T(8,128)(2,1)} %collective-permute-done.1.refs_2_, bf16[64,14336]{1,0:T(8,128)(2,1)} %collective-permute-done.refs_3_, bf16[14336,1792]{1,0:T(8,128)(2,1)} %refs_7_.9), custom_call_target="tpu_custom_call" | custom-call | flops 344064 | bytes 1376256 | tf_op jit(solution)/shard_map/rotate/pallas_call | solution.py:125
  66.3 22.5 %collective-permute-done.6 = bf16[512,2048]{1,0:T(8,128)(2,1)} collective-permute-done((bf16[512,2048]{1,0:T(8,128)(2,1)}, bf16[512,2048]{1,0:T(8,128)(2,1)}, u32[]{:S(2)}, u32[]{:S(2)}) %collective-permute-start.6) | collective-permute-done | bytes 2097184 | tf_op jit(solution)/shard_map/ppermute | solution.py:184
  88.8 3.0 %collective-permute-done.4.refs_1_.refs_4_ = bf16[64,14336]{1,0:T(8,128)(2,1)} collective-permute-done((bf16[64,14336]{1,0:T(8,128)(2,1)}, bf16[64,14336]{1,0:T(8,128)(2,1)}, u32[]{:S(2)}, u32[]{:S(2)}) %collective-permute-start.4) | collective-permute-done | bytes 1835040 | tf_op jit(solution)/shard_map/ppermute | solution.py:184
  94.0 2.4 %collective-permute-start.8 = (bf16[64,14336]{1,0:T(8,128)(2,1)}, bf16[64,14336]{1,0:T(8,128)(2,1)S(1)}, u32[]{:S(2)}, u32[]{:S(2)}) collective-permute-start(bf16[64,14336]{1,0:T(8,128)(2,1)} %collective-permute-done.4.refs_1_.refs_4_), channel_id=1, source_target_pairs={{0,2},{2,0},{12,14},{14,12},{1,3},{3,1},{13,15},{15,13},{16,18},{1... | collective-permute-start | bytes 5505032 | tf_op jit(solution)/shard_map/ppermute | solution.py:184
  98.6 9.8 %collective-permute-start.14 = (bf16[64,14336]{1,0:T(8,128)(2,1)}, bf16[64,14336]{1,0:T(8,128)(2,1)S(1)}, u32[]{:S(2)}, u32[]{:S(2)}) collective-permute-start(bf16[64,14336]{1,0:T(8,128)(2,1)} %collective-permute-done.refs_3_), channel_id=1, source_target_pairs={{0,4},{2,6},{12,8},{14,10},{1,5},{3,7},{13,9},{15,11},{16,20},{18,... | collective-permute-start | bytes 5505032 | tf_op jit(solution)/shard_map/ppermute | solution.py:184
  108.3 12.0 %rotate.9.refs_10_ = f32[128,1792]{1,0:T(8,128)S(1)} custom-call(s32[1]{0:T(128)} %bitcast.11.refs_0_.refs_1_, bf16[64,14336]{1,0:T(8,128)(2,1)} %collective-permute-done.4.refs_1_.refs_4_, bf16[64,14336]{1,0:T(8,128)(2,1)} %collective-permute-done.2.refs_2_.refs_5_, bf16[64,14336]{1,0:T(8,128)(2,1)} %collective-permute-done.3.refs_3_.refs_6_, ...), custom_call_target="tpu_custom_call" | custom-call | flops 229376 | bytes 917504 | tf_op jit(solution)/shard_map/rotate/pallas_call | solution.py:125
  120.4 1.7 convert_add_fusion.1
  123.5 15.2 %rotate.10 = f32[320,1792]{1,0:T(8,128)S(1)} custom-call(s32[1]{0:T(128)} %bitcast.11.refs_0_.refs_1_, bf16[64,14336]{1,0:T(8,128)(2,1)S(1)} %copy-done.3, bf16[64,14336]{1,0:T(8,128)(2,1)} %collective-permute-done.1.refs_2_, bf16[64,14336]{1,0:T(8,128)(2,1)} %collective-permute-done.refs_3_, bf16[64,14336]{1,0:T(8,128)(2,1)} %collective-permute-done.4.refs_1_.refs_4_, ...), custom_call_target="tpu_custom_call" | custom-call | flops 573440 | bytes 2293760 | tf_op jit(solution)/shard_map/rotate/pallas_call | solution.py:125
  138.8 2.1 collective-permute-done.7.refs_1_
  141.0 2.3 %collective-permute-start.12 = (bf16[64,3072]{1,0:T(8,128)(2,1)S(1)}, bf16[64,3072]{1,0:T(8,128)(2,1)S(1)}, u32[]{:S(2)}, u32[]{:S(2)}) collective-permute-start(bf16[64,3072]{1,0:T(8,128)(2,1)S(1)} %slice.32), channel_id=1, source_target_pairs={{0,2},{2,0},{12,14},{14,12},{1,3},{3,1},{13,15},{15,13},{16,18},{1... | collective-permute-start | bytes 1179656 | tf_op jit(solution)/shard_map/ppermute | solution.py:184
  144.7 5.9 %collective-permute-done.12.refs_5_ = bf16[64,3072]{1,0:T(8,128)(2,1)S(1)} collective-permute-done((bf16[64,3072]{1,0:T(8,128)(2,1)S(1)}, bf16[64,3072]{1,0:T(8,128)(2,1)S(1)}, u32[]{:S(2)}, u32[]{:S(2)}) %collective-permute-start.12) | collective-permute-done | bytes 393248 | tf_op jit(solution)/shard_map/ppermute | solution.py:184
  153.1 2.3 %collective-permute-start.15 = (bf16[64,7168]{1,0:T(8,128)(2,1)S(1)}, bf16[64,7168]{1,0:T(8,128)(2,1)S(1)}, u32[]{:S(2)}, u32[]{:S(2)}) collective-permute-start(bf16[64,7168]{1,0:T(8,128)(2,1)S(1)} %slice.33), channel_id=1, source_target_pairs={{0,2},{2,0},{12,14},{14,12},{1,3},{3,1},{13,15},{15,13},{16,18},{1... | collective-permute-start | bytes 2752520 | tf_op jit(solution)/shard_map/ppermute | solution.py:184
  155.4 6.3 %rotate.11.refs_8_ = f32[192,1792]{1,0:T(8,128)S(1)} custom-call(s32[1]{0:T(128)} %bitcast.11.refs_0_.refs_1_, bf16[64,14336]{1,0:T(8,128)(2,1)S(1)} %collective-permute-done.7.refs_1_, bf16[64,14336]{1,0:T(8,128)(2,1)S(1)} %collective-permute-done.5.refs_2_, bf16[64,14336]{1,0:T(8,128)(2,1)S(1)} %collective-permute-done.8.refs_3_, ...), custom_call_target="tpu_custom_call" | custom-call | flops 344064 | bytes 1376256 | tf_op jit(solution)/shard_map/rotate/pallas_call | solution.py:125
  161.7 10.9 %collective-permute-done.15.refs_5_ = bf16[64,7168]{1,0:T(8,128)(2,1)S(1)} collective-permute-done((bf16[64,7168]{1,0:T(8,128)(2,1)S(1)}, bf16[64,7168]{1,0:T(8,128)(2,1)S(1)}, u32[]{:S(2)}, u32[]{:S(2)}) %collective-permute-start.15) | collective-permute-done | bytes 917536 | tf_op jit(solution)/shard_map/ppermute | solution.py:184
  175.5 2.4 %collective-permute-start.20 = (bf16[64,4096]{1,0:T(8,128)(2,1)S(1)}, bf16[64,4096]{1,0:T(8,128)(2,1)S(1)}, u32[]{:S(2)}, u32[]{:S(2)}) collective-permute-start(bf16[64,4096]{1,0:T(8,128)(2,1)S(1)} %slice.35), channel_id=1, source_target_pairs={{0,2},{2,0},{12,14},{14,12},{1,3},{3,1},{13,15},{15,13},{16,18},{1... | collective-permute-start | bytes 1572872 | tf_op jit(solution)/shard_map/ppermute | solution.py:184
  177.9 6.3 %rotate.12.refs_8_ = f32[192,1792]{1,0:T(8,128)S(1)} custom-call(s32[1]{0:T(128)} %bitcast.11.refs_0_.refs_1_, bf16[64,14336]{1,0:T(8,128)(2,1)S(1)} %collective-permute-done.7.refs_1_, bf16[64,14336]{1,0:T(8,128)(2,1)S(1)} %collective-permute-done.5.refs_2_, bf16[64,14336]{1,0:T(8,128)(2,1)S(1)} %collective-permute-done.8.refs_3_, ...), custom_call_target="tpu_custom_call" | custom-call | flops 344064 | bytes 1376256 | tf_op jit(solution)/shard_map/rotate/pallas_call | solution.py:125
  184.2 7.6 %rotate.13.refs_8_ = f32[192,1792]{1,0:T(8,128)S(1)} custom-call(s32[1]{0:T(128)} %bitcast.11.refs_0_.refs_1_, bf16[64,14336]{1,0:T(8,128)(2,1)S(1)} %collective-permute-done.7.refs_1_, bf16[64,14336]{1,0:T(8,128)(2,1)S(1)} %collective-permute-done.5.refs_2_, bf16[64,14336]{1,0:T(8,128)(2,1)S(1)} %collective-permute-done.8.refs_3_, ...), custom_call_target="tpu_custom_call" | custom-call | flops 344064 | bytes 1376256 | tf_op jit(solution)/shard_map/rotate/pallas_call | solution.py:125
  192.9 4.2 %rotate.14.refs_8_ = f32[192,1792]{1,0:T(8,128)S(1)} custom-call(s32[1]{0:T(128)} %bitcast.11.refs_0_.refs_1_, bf16[64,14336]{1,0:T(8,128)(2,1)S(1)} %collective-permute-done.7.refs_1_, bf16[64,14336]{1,0:T(8,128)(2,1)S(1)} %collective-permute-done.5.refs_2_, bf16[64,14336]{1,0:T(8,128)(2,1)S(1)} %collective-permute-done.8.refs_3_, ...), custom_call_target="tpu_custom_call" | custom-call | flops 344064 | bytes 1376256 | tf_op jit(solution)/shard_map/rotate/pallas_call | solution.py:125
  197.1 4.4 %collective-permute-done.19.refs_7_ = bf16[512,1024]{1,0:T(8,128)(2,1)S(1)} collective-permute-done((bf16[512,1024]{1,0:T(8,128)(2,1)S(1)}, bf16[512,1024]{1,0:T(8,128)(2,1)S(1)}, u32[]{:S(2)}, u32[]{:S(2)}) %collective-permute-start.19) | collective-permute-done | bytes 1048608 | tf_op jit(solution)/shard_map/ppermute | solution.py:184
  201.6 4.5 %rotate.15.refs_4_ = f32[192,1792]{1,0:T(8,128)S(1)} custom-call(s32[1]{0:T(128)} %bitcast.11.refs_0_.refs_1_, bf16[64,14336]{1,0:T(8,128)(2,1)S(1)} %collective-permute-done.7.refs_1_, bf16[64,14336]{1,0:T(8,128)(2,1)S(1)} %collective-permute-done.5.refs_2_, bf16[64,14336]{1,0:T(8,128)(2,1)S(1)} %collective-permute-done.8.refs_3_, ...), custom_call_target="tpu_custom_call" | custom-call | flops 344064 | bytes 1376256 | tf_op jit(solution)/shard_map/rotate/pallas_call | solution.py:125
  207.6 1.7 collective-permute-done.22.refs_5_
  210.4 12.7 %fit.1 = f32[1792,2048]{1,0:T(8,128)} custom-call(s32[8]{0:T(128)} %stack.44.refs_0_, s32[1]{0:T(128)} %bitcast.11.refs_0_.refs_1_, s32[2]{0:T(128)} %pad_add_fusion.refs_2_, bf16[320,1792]{1,0:T(8,128)(2,1)} %add_convert_fusion.refs_3_, f32[192,1792]{1,0:T(8,128)} %copy-done.4, f32[192,1792]{1,0:T(8,128)} %copy-done.6, ...), custom_call_target="tpu_custom_call" | custom-call | flops 3758096384 | bytes 24117248 | tf_op jit(solution)/shard_map/fit/pallas_call | solution.py:64
  (56 shorter events, 20.9 us)
Async XLA Ops:
  0.0 9.1 %copy-start = (bf16[512,1024]{1,0:T(8,128)(2,1)S(1)}, bf16[512,1024]{1,0:T(8,128)(2,1)}, u32[]{:S(2)}) copy-start(bf16[512,1024]{1,0:T(8,128)(2,1)} %param.5) | copy-start | bytes 3145732
  0.0 43.3 %collective-permute-start = (bf16[64,14336]{1,0:T(8,128)(2,1)}, bf16[64,14336]{1,0:T(8,128)(2,1)}, u32[]{:S(2)}, u32[]{:S(2)}) collective-permute-start(bf16[64,14336]{1,0:T(8,128)(2,1)} %refs_1_.3), channel_id=1, source_target_pairs={{0,2},{2,0},{4,6},{6,4},{8,10},{10,8},{12,14},{14,12},{1,3},{3,1},... | collective-permute-start | bytes 5505032 | tf_op jit(solution)/shard_map/ppermute | solution.py:184
  2.9 42.3 %collective-permute-start.1 = (bf16[64,14336]{1,0:T(8,128)(2,1)}, bf16[64,14336]{1,0:T(8,128)(2,1)}, u32[]{:S(2)}, u32[]{:S(2)}) collective-permute-start(bf16[64,14336]{1,0:T(8,128)(2,1)} %refs_1_.3), channel_id=1, source_target_pairs={{0,4},{2,6},{4,0},{6,2},{8,12},{10,14},{12,8},{14,10},{1,5},{3,7},... | collective-permute-start | bytes 5505032 | tf_op jit(solution)/shard_map/ppermute | solution.py:184
  4.5 40.8 %collective-permute-start.2 = (bf16[64,14336]{1,0:T(8,128)(2,1)}, bf16[64,14336]{1,0:T(8,128)(2,1)}, u32[]{:S(2)}, u32[]{:S(2)}) collective-permute-start(bf16[64,14336]{1,0:T(8,128)(2,1)} %refs_1_.3), channel_id=1, source_target_pairs={{4,8},{6,10},{8,4},{10,6},{5,9},{7,11},{9,5},{11,7},{20,24},{22,26... | collective-permute-start | bytes 5505032 | tf_op jit(solution)/shard_map/ppermute | solution.py:184
  14.3 74.5 %collective-permute-start.6 = (bf16[512,2048]{1,0:T(8,128)(2,1)}, bf16[512,2048]{1,0:T(8,128)(2,1)}, u32[]{:S(2)}, u32[]{:S(2)}) collective-permute-start(bf16[512,2048]{1,0:T(8,128)(2,1)} %get-tuple-element.111), channel_id=1, source_target_pairs={{0,4},{2,6},{12,8},{14,10},{1,5},{3,7},{13,9},{15,11},{16,20},{18,... | collective-permute-start | bytes 6291464 | tf_op jit(solution)/shard_map/ppermute | solution.py:184
  45.3 43.5 %collective-permute-start.3 = (bf16[64,14336]{1,0:T(8,128)(2,1)}, bf16[64,14336]{1,0:T(8,128)(2,1)}, u32[]{:S(2)}, u32[]{:S(2)}) collective-permute-start(bf16[64,14336]{1,0:T(8,128)(2,1)} %collective-permute-done.1.refs_2_), channel_id=1, source_target_pairs={{0,2},{2,0},{12,14},{14,12},{1,3},{3,1},{13,15},{15,13},{16,18},{1... | collective-permute-start | bytes 5505032 | tf_op jit(solution)/shard_map/ppermute | solution.py:184
  47.7 44.0 %collective-permute-start.4 = (bf16[64,14336]{1,0:T(8,128)(2,1)}, bf16[64,14336]{1,0:T(8,128)(2,1)}, u32[]{:S(2)}, u32[]{:S(2)}) collective-permute-start(bf16[64,14336]{1,0:T(8,128)(2,1)} %collective-permute-done.2.refs_2_.refs_5_), channel_id=1, source_target_pairs={{4,0},{6,2},{8,12},{10,14},{5,1},{7,3},{9,13},{11,15},{20,16},{22,... | collective-permute-start | bytes 5505032 | tf_op jit(solution)/shard_map/ppermute | solution.py:184
  49.0 42.7 %collective-permute-start.5 = (bf16[64,14336]{1,0:T(8,128)(2,1)}, bf16[64,14336]{1,0:T(8,128)(2,1)S(1)}, u32[]{:S(2)}, u32[]{:S(2)}) collective-permute-start(bf16[64,14336]{1,0:T(8,128)(2,1)} %collective-permute-done.1.refs_2_), channel_id=1, source_target_pairs={{4,8},{6,10},{8,4},{10,6},{5,9},{7,11},{9,5},{11,7},{20,24},{22,26... | collective-permute-start | bytes 5505032 | tf_op jit(solution)/shard_map/ppermute | solution.py:184
  49.8 48.0 %collective-permute-start.9 = (bf16[64,14336]{1,0:T(8,128)(2,1)}, bf16[64,14336]{1,0:T(8,128)(2,1)}, u32[]{:S(2)}, u32[]{:S(2)}) collective-permute-start(bf16[64,14336]{1,0:T(8,128)(2,1)} %collective-permute-done.2.refs_2_.refs_5_), channel_id=1, source_target_pairs={{4,6},{6,4},{8,10},{10,8},{5,7},{7,5},{9,11},{11,9},{20,22},{22,20... | collective-permute-start | bytes 5505032 | tf_op jit(solution)/shard_map/ppermute | solution.py:184
  51.7 1.5 copy-start.2
  53.2 38.5 %copy-start.5 = (f32[512,2048]{1,0:T(8,128)S(1)}, f32[512,2048]{1,0:T(8,128)}, u32[]{:S(2)}) copy-start(f32[512,2048]{1,0:T(8,128)} %get-tuple-element.71) | copy-start | bytes 12582916
  93.3 28.8 %collective-permute-start.10 = (bf16[512,1024]{1,0:T(8,128)(2,1)S(1)}, bf16[512,1024]{1,0:T(8,128)(2,1)S(1)}, u32[]{:S(2)}, u32[]{:S(2)}) collective-permute-start(bf16[512,1024]{1,0:T(8,128)(2,1)S(1)} %add_convert_fusion.2), channel_id=1, source_target_pairs={{4,8},{6,10},{8,4},{10,6},{5,9},{7,11},{9,5},{11,7},{20,24},{22,26... | collective-permute-start | bytes 3145736 | tf_op jit(solution)/shard_map/ppermute | solution.py:184
  94.0 44.7 %collective-permute-start.8 = (bf16[64,14336]{1,0:T(8,128)(2,1)}, bf16[64,14336]{1,0:T(8,128)(2,1)S(1)}, u32[]{:S(2)}, u32[]{:S(2)}) collective-permute-start(bf16[64,14336]{1,0:T(8,128)(2,1)} %collective-permute-done.4.refs_1_.refs_4_), channel_id=1, source_target_pairs={{0,2},{2,0},{12,14},{14,12},{1,3},{3,1},{13,15},{15,13},{16,18},{1... | collective-permute-start | bytes 5505032 | tf_op jit(solution)/shard_map/ppermute | solution.py:184
  96.5 44.4 %collective-permute-start.7 = (bf16[64,14336]{1,0:T(8,128)(2,1)S(1)}, bf16[64,14336]{1,0:T(8,128)(2,1)S(1)}, u32[]{:S(2)}, u32[]{:S(2)}) collective-permute-start(bf16[64,14336]{1,0:T(8,128)(2,1)S(1)} %collective-permute-done.5.refs_2_), channel_id=1, source_target_pairs={{4,0},{6,2},{8,12},{10,14},{5,1},{7,3},{9,13},{11,15},{20,16},{22,... | collective-permute-start | bytes 5505032 | tf_op jit(solution)/shard_map/ppermute | solution.py:184
  97.9 24.2 %collective-permute-start.11 = (bf16[64,6144]{1,0:T(8,128)(2,1)S(1)}, bf16[64,6144]{1,0:T(8,128)(2,1)S(1)}, u32[]{:S(2)}, u32[]{:S(2)}) collective-permute-start(bf16[64,6144]{1,0:T(8,128)(2,1)S(1)} %slice.29), channel_id=1, source_target_pairs={{4,6},{6,4},{8,10},{10,8},{5,7},{7,5},{9,11},{11,9},{20,22},{22,20... | collective-permute-start | bytes 2359304 | tf_op jit(solution)/shard_map/ppermute | solution.py:184
  98.6 46.1 %collective-permute-start.14 = (bf16[64,14336]{1,0:T(8,128)(2,1)}, bf16[64,14336]{1,0:T(8,128)(2,1)S(1)}, u32[]{:S(2)}, u32[]{:S(2)}) collective-permute-start(bf16[64,14336]{1,0:T(8,128)(2,1)} %collective-permute-done.refs_3_), channel_id=1, source_target_pairs={{0,4},{2,6},{12,8},{14,10},{1,5},{3,7},{13,9},{15,11},{16,20},{18,... | collective-permute-start | bytes 5505032 | tf_op jit(solution)/shard_map/ppermute | solution.py:184
  122.0 1.5 copy-start.3
  122.6 22.1 %collective-permute-start.13 = (bf16[512,1024]{1,0:T(8,128)(2,1)S(1)}, bf16[512,1024]{1,0:T(8,128)(2,1)S(1)}, u32[]{:S(2)}, u32[]{:S(2)}) collective-permute-start(bf16[512,1024]{1,0:T(8,128)(2,1)S(1)} %get-tuple-element.107), channel_id=1, source_target_pairs={{4,6},{6,4},{8,10},{10,8},{5,7},{7,5},{9,11},{11,9},{20,22},{22,20... | collective-permute-start | bytes 3145736 | tf_op jit(solution)/shard_map/ppermute | solution.py:184
  141.0 9.7 %collective-permute-start.12 = (bf16[64,3072]{1,0:T(8,128)(2,1)S(1)}, bf16[64,3072]{1,0:T(8,128)(2,1)S(1)}, u32[]{:S(2)}, u32[]{:S(2)}) collective-permute-start(bf16[64,3072]{1,0:T(8,128)(2,1)S(1)} %slice.32), channel_id=1, source_target_pairs={{0,2},{2,0},{12,14},{14,12},{1,3},{3,1},{13,15},{15,13},{16,18},{1... | collective-permute-start | bytes 1179656 | tf_op jit(solution)/shard_map/ppermute | solution.py:184
  143.4 18.4 %collective-permute-start.16 = (bf16[64,8192]{1,0:T(8,128)(2,1)S(1)}, bf16[64,8192]{1,0:T(8,128)(2,1)S(1)}, u32[]{:S(2)}, u32[]{:S(2)}) collective-permute-start(bf16[64,8192]{1,0:T(8,128)(2,1)S(1)} %slice.34), channel_id=1, source_target_pairs={{4,6},{6,4},{8,10},{10,8},{5,7},{7,5},{9,11},{11,9},{20,22},{22,20... | collective-permute-start | bytes 3145736 | tf_op jit(solution)/shard_map/ppermute | solution.py:184
  151.0 21.7 %collective-permute-start.17 = (bf16[512,1024]{1,0:T(8,128)(2,1)S(1)}, bf16[512,1024]{1,0:T(8,128)(2,1)S(1)}, u32[]{:S(2)}, u32[]{:S(2)}) collective-permute-start(bf16[512,1024]{1,0:T(8,128)(2,1)S(1)} %add_convert_fusion.1), channel_id=1, source_target_pairs={{4,8},{6,10},{8,4},{10,6},{5,9},{7,11},{9,5},{11,7},{20,24},{22,26... | collective-permute-start | bytes 3145736 | tf_op jit(solution)/shard_map/ppermute | solution.py:184
  151.7 22.4 %collective-permute-start.18 = (bf16[512,1024]{1,0:T(8,128)(2,1)S(1)}, bf16[512,1024]{1,0:T(8,128)(2,1)S(1)}, u32[]{:S(2)}, u32[]{:S(2)}) collective-permute-start(bf16[512,1024]{1,0:T(8,128)(2,1)S(1)} %add_convert_fusion.1), channel_id=1, source_target_pairs={{4,0},{6,2},{8,12},{10,14},{5,1},{7,3},{9,13},{11,15},{20,16},{22,... | collective-permute-start | bytes 3145736 | tf_op jit(solution)/shard_map/ppermute | solution.py:184
  153.1 19.6 %collective-permute-start.15 = (bf16[64,7168]{1,0:T(8,128)(2,1)S(1)}, bf16[64,7168]{1,0:T(8,128)(2,1)S(1)}, u32[]{:S(2)}, u32[]{:S(2)}) collective-permute-start(bf16[64,7168]{1,0:T(8,128)(2,1)S(1)} %slice.33), channel_id=1, source_target_pairs={{0,2},{2,0},{12,14},{14,12},{1,3},{3,1},{13,15},{15,13},{16,18},{1... | collective-permute-start | bytes 2752520 | tf_op jit(solution)/shard_map/ppermute | solution.py:184
  172.7 11.5 %copy-start.7 = (bf16[512,1024]{1,0:T(8,128)(2,1)}, bf16[512,1024]{1,0:T(8,128)(2,1)S(1)}, u32[]{:S(2)}) copy-start(bf16[512,1024]{1,0:T(8,128)(2,1)S(1)} %collective-permute-done.17.refs_8_) | copy-start | bytes 3145732
  174.1 18.8 %collective-permute-start.21 = (f32[320,1792]{1,0:T(8,128)S(1)}, f32[320,1792]{1,0:T(8,128)S(1)}, u32[]{:S(2)}, u32[]{:S(2)}) collective-permute-start(f32[320,1792]{1,0:T(8,128)S(1)} %rotate.10), channel_id=1, source_target_pairs={{0,1},{1,0},{2,3},{3,2},{4,5},{5,4},{6,7},{7,6},{8,9},{9,8},{10,11... | collective-permute-start | bytes 6881288 | tf_op jit(solution)/shard_map/ppermute | solution.py:146
  174.1 27.5 %collective-permute-start.19 = (bf16[512,1024]{1,0:T(8,128)(2,1)S(1)}, bf16[512,1024]{1,0:T(8,128)(2,1)S(1)}, u32[]{:S(2)}, u32[]{:S(2)}) collective-permute-start(bf16[512,1024]{1,0:T(8,128)(2,1)S(1)} %collective-permute-done.17.refs_8_), channel_id=1, source_target_pairs={{4,0},{6,2},{8,12},{10,14},{5,1},{7,3},{9,13},{11,15},{20,16},{22,... | collective-permute-start | bytes 3145736 | tf_op jit(solution)/shard_map/ppermute | solution.py:184
  175.5 17.4 %collective-permute-start.20 = (bf16[64,4096]{1,0:T(8,128)(2,1)S(1)}, bf16[64,4096]{1,0:T(8,128)(2,1)S(1)}, u32[]{:S(2)}, u32[]{:S(2)}) collective-permute-start(bf16[64,4096]{1,0:T(8,128)(2,1)S(1)} %slice.35), channel_id=1, source_target_pairs={{0,2},{2,0},{12,14},{14,12},{1,3},{3,1},{13,15},{15,13},{16,18},{1... | collective-permute-start | bytes 1572872 | tf_op jit(solution)/shard_map/ppermute | solution.py:184
  201.6 4.5 %copy-start.8 = (bf16[512,1024]{1,0:T(8,128)(2,1)}, bf16[512,1024]{1,0:T(8,128)(2,1)S(1)}, u32[]{:S(2)}) copy-start(bf16[512,1024]{1,0:T(8,128)(2,1)S(1)} %collective-permute-done.19.refs_7_) | copy-start | bytes 3145732
  206.1 1.5 copy-start.4
  206.1 3.2 %collective-permute-start.22 = (f32[192,1792]{1,0:T(8,128)S(1)}, f32[192,1792]{1,0:T(8,128)S(1)}, u32[]{:S(2)}, u32[]{:S(2)}) collective-permute-start(f32[192,1792]{1,0:T(8,128)S(1)} %rotate.15.refs_4_), channel_id=1, source_target_pairs={{0,1},{1,0},{2,3},{3,2},{4,5},{5,4},{6,7},{7,6},{8,9},{9,8},{10,11... | collective-permute-start | bytes 4128776 | tf_op jit(solution)/shard_map/ppermute | solution.py:146
  209.3 1.1 copy-start.6
  210.4 12.7 %copy-start.1 = (bf16[512,1024]{1,0:T(8,128)(2,1)S(1)}, bf16[512,1024]{1,0:T(8,128)(2,1)}, u32[]{:S(2)}) copy-start(bf16[512,1024]{1,0:T(8,128)(2,1)} %param.5) | copy-start | bytes 3145732

commit v18 on v17

--- a/solution.py
+++ b/solution.py
@@ -191,8 +191,7 @@
     end = at_end.astype(jnp.int32).reshape(1)
     half = (z >= 2).astype(jnp.int32)
     steps = inputs.shape[1] // DEEP
-    cuts = [0, 3 * steps // 14, 10 * steps // 14, steps]
-    middle = 6 * steps // 14
+    cuts = [0, 6 * steps // 14, 10 * steps // 14, steps]
     part = basis_out.shape[1] // 4
     got = {"own": inputs}
 
@@ -228,21 +227,24 @@
     got["m2"] = send(got["a1"], MIDDLE)
     blocks = [["own"], ["a1"], ["x1"]]
     got["A"] = turn([], blocks, 0, some)
-    fence("x1", "x2", "a2", "m2", "out", "r1", "A")
     cut = 2 * part
+    fence("r1", "out", "A")
+    got["give"] = (got["out"][:, :cut] + got["r1"][:, :cut].astype(F32)).astype(BF16)
+    fence("x1", "x2", "a2", "m2", "out", "r1", "give", "A")
     got["x3"] = send(got["a2"], ACROSS_ENDS)
-    got["m3"] = send((got["out"][:, :cut] + got["r1"][:, :cut].astype(F32)).astype(BF16), MIDDLE)
+    got["m3"] = send(got["give"], MIDDLE)
     got["a3"] = send(got["m2"], TO_ENDS)
     got["e"] = send(got["x1"], FROM_ENDS)
     fence(("x2", "m"), "m2", "out", "r1")
-    got["x3m", 0] = send(got["m2"][:, : middle * DEEP], ACROSS_MIDDLE)
+    got["x3m", 0] = send(got["m2"][:, : cuts[1] * DEEP], ACROSS_MIDDLE)
     got["keep"] = got["out"][:, cut:] + got["r1"][:, cut:].astype(F32)
+    fence("keep", ("x2", "m"))
     more = [["a2", "m1"], ["x2", ("x2", "m")]]
     got["B"] = turn([], more, 0, some)
     fence("m3", ("x3m", 0), "keep", "m2", "B")
     got["keep"] += got["m3"].astype(F32)
     got["x5"] = send(got["keep"].astype(BF16), ACROSS_MIDDLE)
-    got["x3m", 1] = send(got["m2"][:, middle * DEEP :], ACROSS_MIDDLE)
+    got["x3m", 1] = send(got["m2"][:, cuts[1] * DEEP :], ACROSS_MIDDLE)
     got["A"] = turn([got["A"], got["B"]], blocks + more, some, steps - some)
     fence("x3", "A")
     fence("a3", "A")
@@ -250,34 +252,32 @@
     def x4(piece):
         got["x4", piece] = send(got["a3"][:, cuts[piece] * DEEP : cuts[piece + 1] * DEEP], ACROSS_ENDS)
 
-    def last(piece, first, until):
-        side = int(first >= middle)
+    def last(piece):
+        first, until, side = cuts[piece], cuts[piece + 1], int(piece > 0)
         blocks = [
             [(got["a3"], first), (got["m2"], first)],
-            [(got["x3"], first), (got["x3m", side], first - side * middle)],
-            [(got["x4", piece], first - cuts[piece]), (got["e"], first)],
+            [(got["x3"], first), (got["x3m", side], first - side * cuts[1])],
+            [(got["x4", piece], 0), (got["e"], first)],
         ]
-        got["D"] = rotate([got["D"]] if first else [], end, blocks, basis_in, first, until - first)
+        got["D"] = rotate([got["D"]] if piece else [], end, blocks, basis_in, first, until - first)
 
     x4(0)
-    fence(("x4", 0), "x5", "e", "keep", "a3", "A")
+    fence("x5", "e", "keep", "A")
     got["sum"] = (got["keep"] + got["x5"].astype(F32)).astype(BF16)
     got["m4"] = send(got["sum"], MIDDLE)
     got["n1"] = send(got["sum"], TO_ENDS)
+    fence(("x4", 0), "a3", "A", "sum")
     x4(1)
-    last(0, 0, cuts[1])
+    last(0)
     fence(("x4", 1), ("x3m", 1), "m4", "n1", "sum", "a3", "A", "D")
     x4(2)
     got["n2"] = send(got["m4"], TO_ENDS)
     got["A2"] = swap_narrow(got["A"])
     got["R"] = pick("n1", "sum")
-    last(1, cuts[1], middle)
-    last(1, middle, cuts[2])
+    last(1)
     fence(("x4", 2), "A", "A2", "R", "D")
-    late = (cuts[2] + steps) // 2
-    last(2, cuts[2], late)
+    last(2)
     fence("n2", "m4", "R", "A", "A2", "D")
-    last(2, late, steps)
     got["D2"] = swap_narrow(got["D"])
     got["A"] = (got["A"] + got["A2"]).astype(BF16)
 

time: 224 us -> 219 us (0.978)
  Pallas kernels: 81.9 us -> 78.8 us
    pallas_call x8 -> x6, Pallas kernels: 69.2 us -> 66.1 us  [rotate(): pl.pallas_call(lambda *refs: rotate_kernel([len(block) for block in block...]
  transfers between devices with their start and end apart: 23 -> 23, of which waited for: 11 -> 9; matrix products, arithmetic and copies ran while one was open for 7% -> 7% of each run, Pallas kernels for 29% -> 30%
where the time goes in v18:
time: 219 us; the launch traced here: 218 us
  Pallas kernels  78.8 us (36%)
  waiting for transfers between devices  75.3 us (34%)
  starting transfers between devices  44.5 us (20%)
  other arithmetic  7.23 us (3%)
  local copies, waits for them, and re-layouts  6.2 us (3%)
  matrix products  5.09 us (2%)
    ppermute x21, waiting for transfers between devices, send(): return lax.ppermute(a, 'wide', perm)  73.5 us
    pallas_call x6, Pallas kernels, rotate(): pl.pallas_call(lambda *refs: rotate_kernel([len(block) for block in block...  66.1 us
    ppermute x21, starting transfers between devices, send(): return lax.ppermute(a, 'wide', perm)  44.4 us
    pallas_call x1, Pallas kernels, fit(): pl.pallas_call(lambda *refs: fit_kernel([len(halves) for halves in sums],...  12.7 us
    dot_general x1, matrix products, dot(): return jnp.dot(a, b, preferred_element_type=F32)  5.09 us
  transfers between devices with their start and end apart: 23, of which 9 were waited for; matrix products, arithmetic and copies ran while one was open for 7% of the time, Pallas kernels for 30%

profile of v18, /device:TPU:0, one launch (start us, length us, event | category | flops | bytes accessed | tf_op | source)
XLA Modules:
  0.0 217.6 jit_solution(9961726983096210740)
XLA Ops:
  0.9 5.8 %collective-permute-start.1 = (bf16[64,14336]{1,0:T(8,128)(2,1)}, bf16[64,14336]{1,0:T(8,128)(2,1)}, u32[]{:S(2)}, u32[]{:S(2)}) collective-permute-start(bf16[64,14336]{1,0:T(8,128)(2,1)} %refs_1_.3), channel_id=1, source_target_pairs={{0,4},{2,6},{4,0},{6,2},{8,12},{10,14},{12,8},{14,10},{1,5},{3,7},... | collective-permute-start | bytes 5505032 | tf_op jit(solution)/shard_map/ppermute | solution.py:184
  6.7 1.5 collective-permute-start
  8.2 2.7 %constant_dynamic-slice_fusion.1 = (bf16[1024,1024]{1,0:T(8,128)(2,1)S(1)}, bf16[1024,1024]{1,0:T(8,128)(2,1)S(1)}) fusion(bf16[1024,2048]{1,0:T(8,128)(2,1)} %param.7, s32[]{:T(128)S(6)} %select_n.48, s32[]{:T(128)S(6)} %select_n.49), kind=kLoop, calls=%fused_computation.13 | loop fusion | bytes 8388616 | tf_op jit(solution)/shard_map/dynamic_slice | solution.py:205
  10.9 5.1 %fusion.9 = (bf16[512,2048]{1,0:T(8,128)(2,1)}, f32[512,2048]{1,0:T(8,128)}) fusion(bf16[512,1024]{1,0:T(8,128)(2,1)S(1)} %copy-done, bf16[1024,1024]{1,0:T(8,128)(2,1)S(1)} %get-tuple-element.126, bf16[1024,1024]{1,0:T(8,128)(2,1)S(1)} %get-tuple-element.125), kind=kOutput, calls=%fused_computation.16 | convolution fusion | flops 2156920832 | bytes 11534336 | tf_op jit(solution)/shard_map/dot_general | solution.py:16
  16.0 3.3 %collective-permute-start.6 = (bf16[512,2048]{1,0:T(8,128)(2,1)}, bf16[512,2048]{1,0:T(8,128)(2,1)}, u32[]{:S(2)}, u32[]{:S(2)}) collective-permute-start(bf16[512,2048]{1,0:T(8,128)(2,1)} %get-tuple-element.127), channel_id=1, source_target_pairs={{0,4},{2,6},{12,8},{14,10},{1,5},{3,7},{13,9},{15,11},{16,20},{18,... | collective-permute-start | bytes 6291464 | tf_op jit(solution)/shard_map/ppermute | solution.py:184
  20.6 26.9 %collective-permute-done.1.refs_2_ = bf16[64,14336]{1,0:T(8,128)(2,1)} collective-permute-done((bf16[64,14336]{1,0:T(8,128)(2,1)}, bf16[64,14336]{1,0:T(8,128)(2,1)}, u32[]{:S(2)}, u32[]{:S(2)}) %collective-permute-start.1) | collective-permute-done | bytes 1835040 | tf_op jit(solution)/shard_map/ppermute | solution.py:184
  49.0 3.4 %collective-permute-start.3 = (bf16[64,14336]{1,0:T(8,128)(2,1)}, bf16[64,14336]{1,0:T(8,128)(2,1)}, u32[]{:S(2)}, u32[]{:S(2)}) collective-permute-start(bf16[64,14336]{1,0:T(8,128)(2,1)} %collective-permute-done.1.refs_2_), channel_id=1, source_target_pairs={{0,2},{2,0},{12,14},{14,12},{1,3},{3,1},{13,15},{15,13},{16,18},{1... | collective-permute-start | bytes 5505032 | tf_op jit(solution)/shard_map/ppermute | solution.py:184
  53.7 1.9 collective-permute-start.9
  55.6 1.5 copy-done.4
  57.1 13.0 %rotate.6.refs_9_ = f32[192,1792]{1,0:T(8,128)S(1)} custom-call(s32[1]{0:T(128)} %bitcast.11.refs_0_.refs_1_, bf16[64,14336]{1,0:T(8,128)(2,1)S(1)} %copy-done.4, bf16[64,14336]{1,0:T(8,128)(2,1)} %collective-permute-done.1.refs_2_, bf16[64,14336]{1,0:T(8,128)(2,1)} %collective-permute-done.refs_3_, bf16[14336,1792]{1,0:T(8,128)(2,1)} %refs_7_.5), custom_call_target="tpu_custom_call" | custom-call | flops 344064 | bytes 1376256 | tf_op jit(solution)/shard_map/rotate/pallas_call | solution.py:125
  70.1 20.8 %collective-permute-done.6 = bf16[512,2048]{1,0:T(8,128)(2,1)} collective-permute-done((bf16[512,2048]{1,0:T(8,128)(2,1)}, bf16[512,2048]{1,0:T(8,128)(2,1)}, u32[]{:S(2)}, u32[]{:S(2)}) %collective-permute-start.6) | collective-permute-done | bytes 2097184 | tf_op jit(solution)/shard_map/ppermute | solution.py:184
  91.0 1.6 add_convert_fusion.2
  92.6 2.0 collective-permute-done.4.refs_1_.refs_4_
  96.3 3.1 %collective-permute-start.8 = (bf16[64,14336]{1,0:T(8,128)(2,1)}, bf16[64,14336]{1,0:T(8,128)(2,1)S(1)}, u32[]{:S(2)}, u32[]{:S(2)}) collective-permute-start(bf16[64,14336]{1,0:T(8,128)(2,1)} %collective-permute-done.4.refs_1_.refs_4_), channel_id=1, source_target_pairs={{0,2},{2,0},{12,14},{14,12},{1,3},{3,1},{13,15},{15,13},{16,18},{1... | collective-permute-start | bytes 5505032 | tf_op jit(solution)/shard_map/ppermute | solution.py:184
  100.6 6.4 %collective-permute-start.14 = (bf16[64,14336]{1,0:T(8,128)(2,1)}, bf16[64,14336]{1,0:T(8,128)(2,1)S(1)}, u32[]{:S(2)}, u32[]{:S(2)}) collective-permute-start(bf16[64,14336]{1,0:T(8,128)(2,1)} %collective-permute-done.refs_3_), channel_id=1, source_target_pairs={{0,4},{2,6},{12,8},{14,10},{1,5},{3,7},{13,9},{15,11},{16,20},{18,... | collective-permute-start | bytes 5505032 | tf_op jit(solution)/shard_map/ppermute | solution.py:184
  107.0 1.7 convert_add_fusion.1
  108.7 11.9 %rotate.7.refs_10_ = f32[128,1792]{1,0:T(8,128)S(1)} custom-call(s32[1]{0:T(128)} %bitcast.11.refs_0_.refs_1_, bf16[64,14336]{1,0:T(8,128)(2,1)} %collective-permute-done.4.refs_1_.refs_4_, bf16[64,14336]{1,0:T(8,128)(2,1)S(1)} %copy-done.3, bf16[64,14336]{1,0:T(8,128)(2,1)} %collective-permute-done.3.refs_3_.refs_6_, ...), custom_call_target="tpu_custom_call" | custom-call | flops 229376 | bytes 917504 | tf_op jit(solution)/shard_map/rotate/pallas_call | solution.py:125
  122.9 15.2 %rotate.8 = f32[320,1792]{1,0:T(8,128)S(1)} custom-call(s32[1]{0:T(128)} %bitcast.11.refs_0_.refs_1_, bf16[64,14336]{1,0:T(8,128)(2,1)S(1)} %copy-done.5, bf16[64,14336]{1,0:T(8,128)(2,1)} %collective-permute-done.1.refs_2_, bf16[64,14336]{1,0:T(8,128)(2,1)} %collective-permute-done.refs_3_, bf16[64,14336]{1,0:T(8,128)(2,1)} %collective-permute-done.4.refs_1_.refs_4_, ...), custom_call_target="tpu_custom_call" | custom-call | flops 573440 | bytes 2293760 | tf_op jit(solution)/shard_map/rotate/pallas_call | solution.py:125
  138.1 4.0 %collective-permute-done.7.refs_1_ = bf16[64,14336]{1,0:T(8,128)(2,1)S(1)} collective-permute-done((bf16[64,14336]{1,0:T(8,128)(2,1)S(1)}, bf16[64,14336]{1,0:T(8,128)(2,1)S(1)}, u32[]{:S(2)}, u32[]{:S(2)}) %collective-permute-start.7) | collective-permute-done | bytes 1835040 | tf_op jit(solution)/shard_map/ppermute | solution.py:184
  142.2 2.3 %collective-permute-start.12 = (bf16[64,6144]{1,0:T(8,128)(2,1)S(1)}, bf16[64,6144]{1,0:T(8,128)(2,1)S(1)}, u32[]{:S(2)}, u32[]{:S(2)}) collective-permute-start(bf16[64,6144]{1,0:T(8,128)(2,1)S(1)} %slice.32), channel_id=1, source_target_pairs={{0,2},{2,0},{12,14},{14,12},{1,3},{3,1},{13,15},{15,13},{16,18},{1... | collective-permute-start | bytes 2359304 | tf_op jit(solution)/shard_map/ppermute | solution.py:184
  144.9 1.3 collective-permute-start.18
  146.9 13.0 %collective-permute-done.12.refs_5_ = bf16[64,6144]{1,0:T(8,128)(2,1)S(1)} collective-permute-done((bf16[64,6144]{1,0:T(8,128)(2,1)S(1)}, bf16[64,6144]{1,0:T(8,128)(2,1)S(1)}, u32[]{:S(2)}, u32[]{:S(2)}) %collective-permute-start.12) | collective-permute-done | bytes 786464 | tf_op jit(solution)/shard_map/ppermute | solution.py:184
  160.0 2.2 %collective-permute-start.15 = (bf16[64,4096]{1,0:T(8,128)(2,1)S(1)}, bf16[64,4096]{1,0:T(8,128)(2,1)S(1)}, u32[]{:S(2)}, u32[]{:S(2)}) collective-permute-start(bf16[64,4096]{1,0:T(8,128)(2,1)S(1)} %slice.33), channel_id=1, source_target_pairs={{0,2},{2,0},{12,14},{14,12},{1,3},{3,1},{13,15},{15,13},{16,18},{1... | collective-permute-start | bytes 1572872 | tf_op jit(solution)/shard_map/ppermute | solution.py:184
  162.2 10.8 %rotate.9.refs_8_ = f32[192,1792]{1,0:T(8,128)S(1)} custom-call(s32[1]{0:T(128)} %bitcast.11.refs_0_.refs_1_, bf16[64,14336]{1,0:T(8,128)(2,1)S(1)} %collective-permute-done.7.refs_1_, bf16[64,14336]{1,0:T(8,128)(2,1)S(1)} %collective-permute-done.5.refs_2_, bf16[64,14336]{1,0:T(8,128)(2,1)S(1)} %collective-permute-done.8.refs_3_, ...), custom_call_target="tpu_custom_call" | custom-call | flops 344064 | bytes 1376256 | tf_op jit(solution)/shard_map/rotate/pallas_call | solution.py:125
  174.5 3.8 %collective-permute-start.20 = (bf16[64,4096]{1,0:T(8,128)(2,1)S(1)}, bf16[64,4096]{1,0:T(8,128)(2,1)S(1)}, u32[]{:S(2)}, u32[]{:S(2)}) collective-permute-start(bf16[64,4096]{1,0:T(8,128)(2,1)S(1)} %slice.35), channel_id=1, source_target_pairs={{0,2},{2,0},{12,14},{14,12},{1,3},{3,1},{13,15},{15,13},{16,18},{1... | collective-permute-start | bytes 1572872 | tf_op jit(solution)/shard_map/ppermute | solution.py:184
  178.4 7.6 %rotate.10.refs_8_ = f32[192,1792]{1,0:T(8,128)S(1)} custom-call(s32[1]{0:T(128)} %bitcast.11.refs_0_.refs_1_, bf16[64,14336]{1,0:T(8,128)(2,1)S(1)} %collective-permute-done.7.refs_1_, bf16[64,14336]{1,0:T(8,128)(2,1)S(1)} %collective-permute-done.5.refs_2_, bf16[64,14336]{1,0:T(8,128)(2,1)S(1)} %collective-permute-done.8.refs_3_, ...), custom_call_target="tpu_custom_call" | custom-call | flops 344064 | bytes 1376256 | tf_op jit(solution)/shard_map/rotate/pallas_call | solution.py:125
  187.1 3.7 %collective-permute-done.20.refs_5_ = bf16[64,4096]{1,0:T(8,128)(2,1)S(1)} collective-permute-done((bf16[64,4096]{1,0:T(8,128)(2,1)S(1)}, bf16[64,4096]{1,0:T(8,128)(2,1)S(1)}, u32[]{:S(2)}, u32[]{:S(2)}) %collective-permute-start.20) | collective-permute-done | bytes 524320 | tf_op jit(solution)/shard_map/ppermute | solution.py:184
  190.7 7.6 %rotate.11.refs_4_ = f32[192,1792]{1,0:T(8,128)S(1)} custom-call(s32[1]{0:T(128)} %bitcast.11.refs_0_.refs_1_, bf16[64,14336]{1,0:T(8,128)(2,1)S(1)} %collective-permute-done.7.refs_1_, bf16[64,14336]{1,0:T(8,128)(2,1)S(1)} %collective-permute-done.5.refs_2_, bf16[64,14336]{1,0:T(8,128)(2,1)S(1)} %collective-permute-done.8.refs_3_, ...), custom_call_target="tpu_custom_call" | custom-call | flops 344064 | bytes 1376256 | tf_op jit(solution)/shard_map/rotate/pallas_call | solution.py:125
  198.3 2.3 %collective-permute-done.19.refs_7_ = bf16[512,1024]{1,0:T(8,128)(2,1)S(1)} collective-permute-done((bf16[512,1024]{1,0:T(8,128)(2,1)S(1)}, bf16[512,1024]{1,0:T(8,128)(2,1)S(1)}, u32[]{:S(2)}, u32[]{:S(2)}) %collective-permute-start.19) | collective-permute-done | bytes 1048608 | tf_op jit(solution)/shard_map/ppermute | solution.py:184
  200.6 1.3 add_convert_fusion.refs_3_
  202.0 1.8 collective-permute-done.22.refs_5_
  204.8 12.7 %fit.1 = f32[1792,2048]{1,0:T(8,128)} custom-call(s32[8]{0:T(128)} %stack.44.refs_0_, s32[1]{0:T(128)} %bitcast.11.refs_0_.refs_1_, s32[2]{0:T(128)} %pad_add_fusion.refs_2_, bf16[320,1792]{1,0:T(8,128)(2,1)} %add_convert_fusion.refs_3_, f32[192,1792]{1,0:T(8,128)} %copy-done.6, f32[192,1792]{1,0:T(8,128)} %copy-done.8, ...), custom_call_target="tpu_custom_call" | custom-call | flops 3758096384 | bytes 24117248 | tf_op jit(solution)/shard_map/fit/pallas_call | solution.py:64
  (58 shorter events, 15.0 us)
Async XLA Ops:
  0.0 10.9 %copy-start = (bf16[512,1024]{1,0:T(8,128)(2,1)S(1)}, bf16[512,1024]{1,0:T(8,128)(2,1)}, u32[]{:S(2)}) copy-start(bf16[512,1024]{1,0:T(8,128)(2,1)} %param.5) | copy-start | bytes 3145732
  0.0 20.6 %collective-permute-start.2 = (bf16[64,14336]{1,0:T(8,128)(2,1)}, bf16[64,14336]{1,0:T(8,128)(2,1)S(1)}, u32[]{:S(2)}, u32[]{:S(2)}) collective-permute-start(bf16[64,14336]{1,0:T(8,128)(2,1)} %refs_1_.3), channel_id=1, source_target_pairs={{4,8},{6,10},{8,4},{10,6},{5,9},{7,11},{9,5},{11,7},{20,24},{22,26... | collective-permute-start | bytes 5505032 | tf_op jit(solution)/shard_map/ppermute | solution.py:184
  0.9 46.6 %collective-permute-start.1 = (bf16[64,14336]{1,0:T(8,128)(2,1)}, bf16[64,14336]{1,0:T(8,128)(2,1)}, u32[]{:S(2)}, u32[]{:S(2)}) collective-permute-start(bf16[64,14336]{1,0:T(8,128)(2,1)} %refs_1_.3), channel_id=1, source_target_pairs={{0,4},{2,6},{4,0},{6,2},{8,12},{10,14},{12,8},{14,10},{1,5},{3,7},... | collective-permute-start | bytes 5505032 | tf_op jit(solution)/shard_map/ppermute | solution.py:184
  6.7 41.5 %collective-permute-start = (bf16[64,14336]{1,0:T(8,128)(2,1)}, bf16[64,14336]{1,0:T(8,128)(2,1)}, u32[]{:S(2)}, u32[]{:S(2)}) collective-permute-start(bf16[64,14336]{1,0:T(8,128)(2,1)} %refs_1_.3), channel_id=1, source_target_pairs={{0,2},{2,0},{4,6},{6,4},{8,10},{10,8},{12,14},{14,12},{1,3},{3,1},... | collective-permute-start | bytes 5505032 | tf_op jit(solution)/shard_map/ppermute | solution.py:184
  16.0 75.0 %collective-permute-start.6 = (bf16[512,2048]{1,0:T(8,128)(2,1)}, bf16[512,2048]{1,0:T(8,128)(2,1)}, u32[]{:S(2)}, u32[]{:S(2)}) collective-permute-start(bf16[512,2048]{1,0:T(8,128)(2,1)} %get-tuple-element.127), channel_id=1, source_target_pairs={{0,4},{2,6},{12,8},{14,10},{1,5},{3,7},{13,9},{15,11},{16,20},{18,... | collective-permute-start | bytes 6291464 | tf_op jit(solution)/shard_map/ppermute | solution.py:184
  20.6 27.6 %copy-start.2 = (bf16[64,14336]{1,0:T(8,128)(2,1)}, bf16[64,14336]{1,0:T(8,128)(2,1)S(1)}, u32[]{:S(2)}) copy-start(bf16[64,14336]{1,0:T(8,128)(2,1)S(1)} %collective-permute-done.2.refs_2_.refs_5_) | copy-start | bytes 5505028
  48.2 44.3 %collective-permute-start.5 = (bf16[64,14336]{1,0:T(8,128)(2,1)}, bf16[64,14336]{1,0:T(8,128)(2,1)S(1)}, u32[]{:S(2)}, u32[]{:S(2)}) collective-permute-start(bf16[64,14336]{1,0:T(8,128)(2,1)} %collective-permute-done.1.refs_2_), channel_id=1, source_target_pairs={{4,8},{6,10},{8,4},{10,6},{5,9},{7,11},{9,5},{11,7},{20,24},{22,26... | collective-permute-start | bytes 5505032 | tf_op jit(solution)/shard_map/ppermute | solution.py:184
  49.0 43.6 %collective-permute-start.3 = (bf16[64,14336]{1,0:T(8,128)(2,1)}, bf16[64,14336]{1,0:T(8,128)(2,1)}, u32[]{:S(2)}, u32[]{:S(2)}) collective-permute-start(bf16[64,14336]{1,0:T(8,128)(2,1)} %collective-permute-done.1.refs_2_), channel_id=1, source_target_pairs={{0,2},{2,0},{12,14},{14,12},{1,3},{3,1},{13,15},{15,13},{16,18},{1... | collective-permute-start | bytes 5505032 | tf_op jit(solution)/shard_map/ppermute | solution.py:184
  52.4 42.2 %collective-permute-start.4 = (bf16[64,14336]{1,0:T(8,128)(2,1)}, bf16[64,14336]{1,0:T(8,128)(2,1)}, u32[]{:S(2)}, u32[]{:S(2)}) collective-permute-start(bf16[64,14336]{1,0:T(8,128)(2,1)} %copy-done.2), channel_id=1, source_target_pairs={{4,0},{6,2},{8,12},{10,14},{5,1},{7,3},{9,13},{11,15},{20,16},{22,... | collective-permute-start | bytes 5505032 | tf_op jit(solution)/shard_map/ppermute | solution.py:184
  53.7 41.6 %collective-permute-start.9 = (bf16[64,14336]{1,0:T(8,128)(2,1)}, bf16[64,14336]{1,0:T(8,128)(2,1)}, u32[]{:S(2)}, u32[]{:S(2)}) collective-permute-start(bf16[64,14336]{1,0:T(8,128)(2,1)} %copy-done.2), channel_id=1, source_target_pairs={{4,6},{6,4},{8,10},{10,8},{5,7},{7,5},{9,11},{11,9},{20,22},{22,20... | collective-permute-start | bytes 5505032 | tf_op jit(solution)/shard_map/ppermute | solution.py:184
  55.6 1.5 copy-start.4
  57.1 33.9 %copy-start.7 = (f32[512,2048]{1,0:T(8,128)S(1)}, f32[512,2048]{1,0:T(8,128)}, u32[]{:S(2)}) copy-start(f32[512,2048]{1,0:T(8,128)} %get-tuple-element.79) | copy-start | bytes 12582916
  94.6 26.1 %collective-permute-start.10 = (bf16[512,1024]{1,0:T(8,128)(2,1)S(1)}, bf16[512,1024]{1,0:T(8,128)(2,1)S(1)}, u32[]{:S(2)}, u32[]{:S(2)}) collective-permute-start(bf16[512,1024]{1,0:T(8,128)(2,1)S(1)} %add_convert_fusion.2), channel_id=1, source_target_pairs={{4,8},{6,10},{8,4},{10,6},{5,9},{7,11},{9,5},{11,7},{20,24},{22,26... | collective-permute-start | bytes 3145736 | tf_op jit(solution)/shard_map/ppermute | solution.py:184
  95.4 13.3 %copy-start.3 = (bf16[64,14336]{1,0:T(8,128)(2,1)S(1)}, bf16[64,14336]{1,0:T(8,128)(2,1)}, u32[]{:S(2)}) copy-start(bf16[64,14336]{1,0:T(8,128)(2,1)} %copy-done.2) | copy-start | bytes 5505028
  95.4 25.2 %collective-permute-start.11 = (bf16[64,6144]{1,0:T(8,128)(2,1)S(1)}, bf16[64,6144]{1,0:T(8,128)(2,1)S(1)}, u32[]{:S(2)}, u32[]{:S(2)}) collective-permute-start(bf16[64,6144]{1,0:T(8,128)(2,1)S(1)} %slice.31), channel_id=1, source_target_pairs={{4,6},{6,4},{8,10},{10,8},{5,7},{7,5},{9,11},{11,9},{20,22},{22,20... | collective-permute-start | bytes 2359304 | tf_op jit(solution)/shard_map/ppermute | solution.py:184
  96.3 41.9 %collective-permute-start.8 = (bf16[64,14336]{1,0:T(8,128)(2,1)}, bf16[64,14336]{1,0:T(8,128)(2,1)S(1)}, u32[]{:S(2)}, u32[]{:S(2)}) collective-permute-start(bf16[64,14336]{1,0:T(8,128)(2,1)} %collective-permute-done.4.refs_1_.refs_4_), channel_id=1, source_target_pairs={{0,2},{2,0},{12,14},{14,12},{1,3},{3,1},{13,15},{15,13},{16,18},{1... | collective-permute-start | bytes 5505032 | tf_op jit(solution)/shard_map/ppermute | solution.py:184
  99.3 42.8 %collective-permute-start.7 = (bf16[64,14336]{1,0:T(8,128)(2,1)S(1)}, bf16[64,14336]{1,0:T(8,128)(2,1)S(1)}, u32[]{:S(2)}, u32[]{:S(2)}) collective-permute-start(bf16[64,14336]{1,0:T(8,128)(2,1)S(1)} %collective-permute-done.5.refs_2_), channel_id=1, source_target_pairs={{4,0},{6,2},{8,12},{10,14},{5,1},{7,3},{9,13},{11,15},{20,16},{22,... | collective-permute-start | bytes 5505032 | tf_op jit(solution)/shard_map/ppermute | solution.py:184
  100.6 43.9 %collective-permute-start.14 = (bf16[64,14336]{1,0:T(8,128)(2,1)}, bf16[64,14336]{1,0:T(8,128)(2,1)S(1)}, u32[]{:S(2)}, u32[]{:S(2)}) collective-permute-start(bf16[64,14336]{1,0:T(8,128)(2,1)} %collective-permute-done.refs_3_), channel_id=1, source_target_pairs={{0,4},{2,6},{12,8},{14,10},{1,5},{3,7},{13,9},{15,11},{16,20},{18,... | collective-permute-start | bytes 5505032 | tf_op jit(solution)/shard_map/ppermute | solution.py:184
  121.2 1.7 copy-start.5
  121.2 23.3 %collective-permute-start.13 = (bf16[512,1024]{1,0:T(8,128)(2,1)S(1)}, bf16[512,1024]{1,0:T(8,128)(2,1)S(1)}, u32[]{:S(2)}, u32[]{:S(2)}) collective-permute-start(bf16[512,1024]{1,0:T(8,128)(2,1)S(1)} %get-tuple-element.123), channel_id=1, source_target_pairs={{4,6},{6,4},{8,10},{10,8},{5,7},{7,5},{9,11},{11,9},{20,22},{22,20... | collective-permute-start | bytes 3145736 | tf_op jit(solution)/shard_map/ppermute | solution.py:184
  122.2 50.9 %collective-permute-start.16 = (bf16[64,8192]{1,0:T(8,128)(2,1)S(1)}, bf16[64,8192]{1,0:T(8,128)(2,1)S(1)}, u32[]{:S(2)}, u32[]{:S(2)}) collective-permute-start(bf16[64,8192]{1,0:T(8,128)(2,1)S(1)} %slice.34), channel_id=1, source_target_pairs={{4,6},{6,4},{8,10},{10,8},{5,7},{7,5},{9,11},{11,9},{20,22},{22,20... | collective-permute-start | bytes 3145736 | tf_op jit(solution)/shard_map/ppermute | solution.py:184
  142.2 17.8 %collective-permute-start.12 = (bf16[64,6144]{1,0:T(8,128)(2,1)S(1)}, bf16[64,6144]{1,0:T(8,128)(2,1)S(1)}, u32[]{:S(2)}, u32[]{:S(2)}) collective-permute-start(bf16[64,6144]{1,0:T(8,128)(2,1)S(1)} %slice.32), channel_id=1, source_target_pairs={{0,2},{2,0},{12,14},{14,12},{1,3},{3,1},{13,15},{15,13},{16,18},{1... | collective-permute-start | bytes 2359304 | tf_op jit(solution)/shard_map/ppermute | solution.py:184
  144.9 28.2 %collective-permute-start.18 = (bf16[512,1024]{1,0:T(8,128)(2,1)S(1)}, bf16[512,1024]{1,0:T(8,128)(2,1)S(1)}, u32[]{:S(2)}, u32[]{:S(2)}) collective-permute-start(bf16[512,1024]{1,0:T(8,128)(2,1)S(1)} %add_convert_fusion.1), channel_id=1, source_target_pairs={{4,0},{6,2},{8,12},{10,14},{5,1},{7,3},{9,13},{11,15},{20,16},{22,... | collective-permute-start | bytes 3145736 | tf_op jit(solution)/shard_map/ppermute | solution.py:184
  146.2 26.9 %collective-permute-start.17 = (bf16[512,1024]{1,0:T(8,128)(2,1)S(1)}, bf16[512,1024]{1,0:T(8,128)(2,1)S(1)}, u32[]{:S(2)}, u32[]{:S(2)}) collective-permute-start(bf16[512,1024]{1,0:T(8,128)(2,1)S(1)} %add_convert_fusion.1), channel_id=1, source_target_pairs={{4,8},{6,10},{8,4},{10,6},{5,9},{7,11},{9,5},{11,7},{20,24},{22,26... | collective-permute-start | bytes 3145736 | tf_op jit(solution)/shard_map/ppermute | solution.py:184
  160.0 13.1 %collective-permute-start.15 = (bf16[64,4096]{1,0:T(8,128)(2,1)S(1)}, bf16[64,4096]{1,0:T(8,128)(2,1)S(1)}, u32[]{:S(2)}, u32[]{:S(2)}) collective-permute-start(bf16[64,4096]{1,0:T(8,128)(2,1)S(1)} %slice.33), channel_id=1, source_target_pairs={{0,2},{2,0},{12,14},{14,12},{1,3},{3,1},{13,15},{15,13},{16,18},{1... | collective-permute-start | bytes 1572872 | tf_op jit(solution)/shard_map/ppermute | solution.py:184
  173.1 12.9 %copy-start.9 = (bf16[512,1024]{1,0:T(8,128)(2,1)}, bf16[512,1024]{1,0:T(8,128)(2,1)S(1)}, u32[]{:S(2)}) copy-start(bf16[512,1024]{1,0:T(8,128)(2,1)S(1)} %collective-permute-done.17.refs_8_) | copy-start | bytes 3145732
  173.1 17.6 %collective-permute-start.21 = (f32[320,1792]{1,0:T(8,128)S(1)}, f32[320,1792]{1,0:T(8,128)S(1)}, u32[]{:S(2)}, u32[]{:S(2)}) collective-permute-start(f32[320,1792]{1,0:T(8,128)S(1)} %rotate.8), channel_id=1, source_target_pairs={{0,1},{1,0},{2,3},{3,2},{4,5},{5,4},{6,7},{7,6},{8,9},{9,8},{10,11... | collective-permute-start | bytes 6881288 | tf_op jit(solution)/shard_map/ppermute | solution.py:146
  173.2 27.4 %collective-permute-start.19 = (bf16[512,1024]{1,0:T(8,128)(2,1)S(1)}, bf16[512,1024]{1,0:T(8,128)(2,1)S(1)}, u32[]{:S(2)}, u32[]{:S(2)}) collective-permute-start(bf16[512,1024]{1,0:T(8,128)(2,1)S(1)} %collective-permute-done.17.refs_8_), channel_id=1, source_target_pairs={{4,0},{6,2},{8,12},{10,14},{5,1},{7,3},{9,13},{11,15},{20,16},{22,... | collective-permute-start | bytes 3145736 | tf_op jit(solution)/shard_map/ppermute | solution.py:184
  174.5 16.2 %collective-permute-start.20 = (bf16[64,4096]{1,0:T(8,128)(2,1)S(1)}, bf16[64,4096]{1,0:T(8,128)(2,1)S(1)}, u32[]{:S(2)}, u32[]{:S(2)}) collective-permute-start(bf16[64,4096]{1,0:T(8,128)(2,1)S(1)} %slice.35), channel_id=1, source_target_pairs={{0,2},{2,0},{12,14},{14,12},{1,3},{3,1},{13,15},{15,13},{16,18},{1... | collective-permute-start | bytes 1572872 | tf_op jit(solution)/shard_map/ppermute | solution.py:184
  198.3 3.7 %copy-start.6 = (f32[192,1792]{1,0:T(8,128)}, f32[192,1792]{1,0:T(8,128)S(1)}, u32[]{:S(2)}) copy-start(f32[192,1792]{1,0:T(8,128)S(1)} %rotate.11.refs_4_) | copy-start | bytes 4128772
  200.6 3.1 %collective-permute-start.22 = (f32[192,1792]{1,0:T(8,128)S(1)}, f32[192,1792]{1,0:T(8,128)S(1)}, u32[]{:S(2)}, u32[]{:S(2)}) collective-permute-start(f32[192,1792]{1,0:T(8,128)S(1)} %rotate.11.refs_4_), channel_id=1, source_target_pairs={{0,1},{1,0},{2,3},{3,2},{4,5},{5,4},{6,7},{7,6},{8,9},{9,8},{10,11... | collective-permute-start | bytes 4128776 | tf_op jit(solution)/shard_map/ppermute | solution.py:146
  204.8 12.7 %copy-start.1 = (bf16[512,1024]{1,0:T(8,128)(2,1)S(1)}, bf16[512,1024]{1,0:T(8,128)(2,1)}, u32[]{:S(2)}) copy-start(bf16[512,1024]{1,0:T(8,128)(2,1)} %param.5) | copy-start | bytes 3145732
  (2 other events, 2.4 us)

commit v19 on v18

--- a/solution.py
+++ b/solution.py
@@ -76,7 +76,7 @@
                 pltpu.VMEM((rows, tile), BF16),
             ],
         ),
-        compiler_params=pltpu.CompilerParams(vmem_limit_bytes=56 << 20),
+        compiler_params=pltpu.CompilerParams(vmem_limit_bytes=32 << 20),
         cost_estimate=pl.CostEstimate(
             flops=2 * rows * ka * ks, bytes_accessed=8 * rows * ka + 2 * rows * ks + 4 * ka * ks, transcendentals=0
         ),
@@ -191,7 +191,7 @@
     end = at_end.astype(jnp.int32).reshape(1)
     half = (z >= 2).astype(jnp.int32)
     steps = inputs.shape[1] // DEEP
-    cuts = [0, 6 * steps // 14, 10 * steps // 14, steps]
+    cuts = [0, 5 * steps // 14, 9 * steps // 14, steps]
     part = basis_out.shape[1] // 4
     got = {"own": inputs}
 

time: 219 us -> 212 us (0.968)
  Pallas kernels: 78.8 us -> 76 us
  other arithmetic: 7.23 us -> 4.57 us
    pallas_call x1, Pallas kernels: 12.7 us -> 9.42 us  [fit(): pl.pallas_call(lambda *refs: fit_kernel([len(halves) for halves in sums],...]
  transfers between devices with their start and end apart: 23 -> 23, of which waited for: 9 -> 8; matrix products, arithmetic and copies ran while one was open for 7% -> 6% of each run, Pallas kernels for 30% -> 31%
where the time goes in v19:
time: 212 us; the launch traced here: 211 us
  waiting for transfers between devices  76.2 us (36%)
  Pallas kernels  76 us (36%)
  starting transfers between devices  44.5 us (21%)
  matrix products  5.11 us (2%)
  other arithmetic  4.57 us (2%)
  local copies, waits for them, and re-layouts  4.52 us (2%)
    ppermute x21, waiting for transfers between devices, send(): return lax.ppermute(a, 'wide', perm)  73.4 us
    pallas_call x6, Pallas kernels, rotate(): pl.pallas_call(lambda *refs: rotate_kernel([len(block) for block in block...  66.5 us
    ppermute x21, starting transfers between devices, send(): return lax.ppermute(a, 'wide', perm)  44.4 us
    pallas_call x1, Pallas kernels, fit(): pl.pallas_call(lambda *refs: fit_kernel([len(halves) for halves in sums],...  9.42 us
    dot_general x1, matrix products, dot(): return jnp.dot(a, b, preferred_element_type=F32)  5.11 us
  transfers between devices with their start and end apart: 23, of which 8 were waited for; matrix products, arithmetic and copies ran while one was open for 6% of the time, Pallas kernels for 31%

profile of v19, /device:TPU:0, one launch (start us, length us, event | category | flops | bytes accessed | tf_op | source)
XLA Modules:
  0.0 211.3 jit_solution(16018377355176343937)
XLA Ops:
  0.9 5.8 %collective-permute-start.1 = (bf16[64,14336]{1,0:T(8,128)(2,1)}, bf16[64,14336]{1,0:T(8,128)(2,1)}, u32[]{:S(2)}, u32[]{:S(2)}) collective-permute-start(bf16[64,14336]{1,0:T(8,128)(2,1)} %refs_1_.3), channel_id=1, source_target_pairs={{0,4},{2,6},{4,0},{6,2},{8,12},{10,14},{12,8},{14,10},{1,5},{3,7},... | collective-permute-start | bytes 5505032 | tf_op jit(solution)/shard_map/ppermute | solution.py:184
  6.7 1.5 collective-permute-start
  8.2 2.7 %constant_dynamic-slice_fusion.1 = (bf16[1024,1024]{1,0:T(8,128)(2,1)S(1)}, bf16[1024,1024]{1,0:T(8,128)(2,1)S(1)}) fusion(bf16[1024,2048]{1,0:T(8,128)(2,1)} %param.7, s32[]{:T(128)S(6)} %select_n.48, s32[]{:T(128)S(6)} %select_n.49), kind=kLoop, calls=%fused_computation.13 | loop fusion | bytes 8388616 | tf_op jit(solution)/shard_map/dynamic_slice | solution.py:205
  10.9 5.1 %fusion.9 = (bf16[512,2048]{1,0:T(8,128)(2,1)}, f32[512,2048]{1,0:T(8,128)}) fusion(bf16[512,1024]{1,0:T(8,128)(2,1)S(1)} %copy-done, bf16[1024,1024]{1,0:T(8,128)(2,1)S(1)} %get-tuple-element.126, bf16[1024,1024]{1,0:T(8,128)(2,1)S(1)} %get-tuple-element.125), kind=kOutput, calls=%fused_computation.16 | convolution fusion | flops 2156920832 | bytes 11534336 | tf_op jit(solution)/shard_map/dot_general | solution.py:16
  16.0 3.3 %collective-permute-start.6 = (bf16[512,2048]{1,0:T(8,128)(2,1)}, bf16[512,2048]{1,0:T(8,128)(2,1)}, u32[]{:S(2)}, u32[]{:S(2)}) collective-permute-start(bf16[512,2048]{1,0:T(8,128)(2,1)} %get-tuple-element.127), channel_id=1, source_target_pairs={{0,4},{2,6},{12,8},{14,10},{1,5},{3,7},{13,9},{15,11},{16,20},{18,... | collective-permute-start | bytes 6291464 | tf_op jit(solution)/shard_map/ppermute | solution.py:184
  19.5 28.0 %collective-permute-done.1.refs_2_ = bf16[64,14336]{1,0:T(8,128)(2,1)} collective-permute-done((bf16[64,14336]{1,0:T(8,128)(2,1)}, bf16[64,14336]{1,0:T(8,128)(2,1)}, u32[]{:S(2)}, u32[]{:S(2)}) %collective-permute-start.1) | collective-permute-done | bytes 1835040 | tf_op jit(solution)/shard_map/ppermute | solution.py:184
  49.0 3.4 %collective-permute-start.3 = (bf16[64,14336]{1,0:T(8,128)(2,1)}, bf16[64,14336]{1,0:T(8,128)(2,1)}, u32[]{:S(2)}, u32[]{:S(2)}) collective-permute-start(bf16[64,14336]{1,0:T(8,128)(2,1)} %collective-permute-done.1.refs_2_), channel_id=1, source_target_pairs={{0,2},{2,0},{12,14},{14,12},{1,3},{3,1},{13,15},{15,13},{16,18},{1... | collective-permute-start | bytes 5505032 | tf_op jit(solution)/shard_map/ppermute | solution.py:184
  52.4 1.3 collective-permute-start.4
  53.7 1.9 collective-permute-start.9
  55.6 1.5 copy-done.4
  57.1 13.0 %rotate.6.refs_9_ = f32[192,1792]{1,0:T(8,128)S(1)} custom-call(s32[1]{0:T(128)} %bitcast.11.refs_0_.refs_1_, bf16[64,14336]{1,0:T(8,128)(2,1)S(1)} %copy-done.4, bf16[64,14336]{1,0:T(8,128)(2,1)} %collective-permute-done.1.refs_2_, bf16[64,14336]{1,0:T(8,128)(2,1)} %collective-permute-done.refs_3_, bf16[14336,1792]{1,0:T(8,128)(2,1)} %refs_7_.5), custom_call_target="tpu_custom_call" | custom-call | flops 344064 | bytes 1376256 | tf_op jit(solution)/shard_map/rotate/pallas_call | solution.py:125
  70.1 20.8 %collective-permute-done.6 = bf16[512,2048]{1,0:T(8,128)(2,1)} collective-permute-done((bf16[512,2048]{1,0:T(8,128)(2,1)}, bf16[512,2048]{1,0:T(8,128)(2,1)}, u32[]{:S(2)}, u32[]{:S(2)}) %collective-permute-start.6) | collective-permute-done | bytes 2097184 | tf_op jit(solution)/shard_map/ppermute | solution.py:184
  91.0 1.6 add_convert_fusion.2
  92.6 2.0 collective-permute-done.4.refs_1_.refs_4_
  96.2 3.1 %collective-permute-start.8 = (bf16[64,14336]{1,0:T(8,128)(2,1)}, bf16[64,14336]{1,0:T(8,128)(2,1)S(1)}, u32[]{:S(2)}, u32[]{:S(2)}) collective-permute-start(bf16[64,14336]{1,0:T(8,128)(2,1)} %collective-permute-done.4.refs_1_.refs_4_), channel_id=1, source_target_pairs={{0,2},{2,0},{12,14},{14,12},{1,3},{3,1},{13,15},{15,13},{16,18},{1... | collective-permute-start | bytes 5505032 | tf_op jit(solution)/shard_map/ppermute | solution.py:184
  99.3 1.3 collective-permute-start.7
  100.6 6.4 %collective-permute-start.14 = (bf16[64,14336]{1,0:T(8,128)(2,1)}, bf16[64,14336]{1,0:T(8,128)(2,1)S(1)}, u32[]{:S(2)}, u32[]{:S(2)}) collective-permute-start(bf16[64,14336]{1,0:T(8,128)(2,1)} %collective-permute-done.refs_3_), channel_id=1, source_target_pairs={{0,4},{2,6},{12,8},{14,10},{1,5},{3,7},{13,9},{15,11},{16,20},{18,... | collective-permute-start | bytes 5505032 | tf_op jit(solution)/shard_map/ppermute | solution.py:184
  107.0 1.7 convert_add_fusion.1
  108.7 11.9 %rotate.7.refs_10_ = f32[128,1792]{1,0:T(8,128)S(1)} custom-call(s32[1]{0:T(128)} %bitcast.11.refs_0_.refs_1_, bf16[64,14336]{1,0:T(8,128)(2,1)} %collective-permute-done.4.refs_1_.refs_4_, bf16[64,14336]{1,0:T(8,128)(2,1)S(1)} %copy-done.3, bf16[64,14336]{1,0:T(8,128)(2,1)} %collective-permute-done.3.refs_3_.refs_6_, ...), custom_call_target="tpu_custom_call" | custom-call | flops 229376 | bytes 917504 | tf_op jit(solution)/shard_map/rotate/pallas_call | solution.py:125
  122.9 15.2 %rotate.8 = f32[320,1792]{1,0:T(8,128)S(1)} custom-call(s32[1]{0:T(128)} %bitcast.11.refs_0_.refs_1_, bf16[64,14336]{1,0:T(8,128)(2,1)S(1)} %copy-done.5, bf16[64,14336]{1,0:T(8,128)(2,1)} %collective-permute-done.1.refs_2_, bf16[64,14336]{1,0:T(8,128)(2,1)} %collective-permute-done.refs_3_, bf16[64,14336]{1,0:T(8,128)(2,1)} %collective-permute-done.4.refs_1_.refs_4_, ...), custom_call_target="tpu_custom_call" | custom-call | flops 573440 | bytes 2293760 | tf_op jit(solution)/shard_map/rotate/pallas_call | solution.py:125
  138.1 4.0 %collective-permute-done.7.refs_1_ = bf16[64,14336]{1,0:T(8,128)(2,1)S(1)} collective-permute-done((bf16[64,14336]{1,0:T(8,128)(2,1)S(1)}, bf16[64,14336]{1,0:T(8,128)(2,1)S(1)}, u32[]{:S(2)}, u32[]{:S(2)}) %collective-permute-start.7) | collective-permute-done | bytes 1835040 | tf_op jit(solution)/shard_map/ppermute | solution.py:184
  142.2 2.3 %collective-permute-start.12 = (bf16[64,5120]{1,0:T(8,128)(2,1)S(1)}, bf16[64,5120]{1,0:T(8,128)(2,1)S(1)}, u32[]{:S(2)}, u32[]{:S(2)}) collective-permute-start(bf16[64,5120]{1,0:T(8,128)(2,1)S(1)} %slice.32), channel_id=1, source_target_pairs={{0,2},{2,0},{12,14},{14,12},{1,3},{3,1},{13,15},{15,13},{16,18},{1... | collective-permute-start | bytes 1966088 | tf_op jit(solution)/shard_map/ppermute | solution.py:184
  146.9 10.3 %collective-permute-done.12.refs_5_ = bf16[64,5120]{1,0:T(8,128)(2,1)S(1)} collective-permute-done((bf16[64,5120]{1,0:T(8,128)(2,1)S(1)}, bf16[64,5120]{1,0:T(8,128)(2,1)S(1)}, u32[]{:S(2)}, u32[]{:S(2)}) %collective-permute-start.12) | collective-permute-done | bytes 655392 | tf_op jit(solution)/shard_map/ppermute | solution.py:184
  157.2 2.2 %collective-permute-start.15 = (bf16[64,4096]{1,0:T(8,128)(2,1)S(1)}, bf16[64,4096]{1,0:T(8,128)(2,1)S(1)}, u32[]{:S(2)}, u32[]{:S(2)}) collective-permute-start(bf16[64,4096]{1,0:T(8,128)(2,1)S(1)} %slice.33), channel_id=1, source_target_pairs={{0,2},{2,0},{12,14},{14,12},{1,3},{3,1},{13,15},{15,13},{16,18},{1... | collective-permute-start | bytes 1572872 | tf_op jit(solution)/shard_map/ppermute | solution.py:184
  159.4 9.4 %rotate.9.refs_8_ = f32[192,1792]{1,0:T(8,128)S(1)} custom-call(s32[1]{0:T(128)} %bitcast.11.refs_0_.refs_1_, bf16[64,14336]{1,0:T(8,128)(2,1)S(1)} %collective-permute-done.7.refs_1_, bf16[64,14336]{1,0:T(8,128)(2,1)S(1)} %collective-permute-done.5.refs_2_, bf16[64,14336]{1,0:T(8,128)(2,1)S(1)} %collective-permute-done.8.refs_3_, ...), custom_call_target="tpu_custom_call" | custom-call | flops 344064 | bytes 1376256 | tf_op jit(solution)/shard_map/rotate/pallas_call | solution.py:125
  168.9 1.3 collective-permute-start.19
  170.3 3.8 %collective-permute-start.20 = (bf16[64,5120]{1,0:T(8,128)(2,1)S(1)}, bf16[64,5120]{1,0:T(8,128)(2,1)S(1)}, u32[]{:S(2)}, u32[]{:S(2)}) collective-permute-start(bf16[64,5120]{1,0:T(8,128)(2,1)S(1)} %slice.35), channel_id=1, source_target_pairs={{0,2},{2,0},{12,14},{14,12},{1,3},{3,1},{13,15},{15,13},{16,18},{1... | collective-permute-start | bytes 1966088 | tf_op jit(solution)/shard_map/ppermute | solution.py:184
  174.1 7.6 %rotate.10.refs_8_ = f32[192,1792]{1,0:T(8,128)S(1)} custom-call(s32[1]{0:T(128)} %bitcast.11.refs_0_.refs_1_, bf16[64,14336]{1,0:T(8,128)(2,1)S(1)} %collective-permute-done.7.refs_1_, bf16[64,14336]{1,0:T(8,128)(2,1)S(1)} %collective-permute-done.5.refs_2_, bf16[64,14336]{1,0:T(8,128)(2,1)S(1)} %collective-permute-done.8.refs_3_, ...), custom_call_target="tpu_custom_call" | custom-call | flops 344064 | bytes 1376256 | tf_op jit(solution)/shard_map/rotate/pallas_call | solution.py:125
  181.8 7.5 %collective-permute-done.20.refs_5_ = bf16[64,5120]{1,0:T(8,128)(2,1)S(1)} collective-permute-done((bf16[64,5120]{1,0:T(8,128)(2,1)S(1)}, bf16[64,5120]{1,0:T(8,128)(2,1)S(1)}, u32[]{:S(2)}, u32[]{:S(2)}) %collective-permute-start.20) | collective-permute-done | bytes 655392 | tf_op jit(solution)/shard_map/ppermute | solution.py:184
  189.3 9.4 %rotate.11.refs_4_ = f32[192,1792]{1,0:T(8,128)S(1)} custom-call(s32[1]{0:T(128)} %bitcast.11.refs_0_.refs_1_, bf16[64,14336]{1,0:T(8,128)(2,1)S(1)} %collective-permute-done.7.refs_1_, bf16[64,14336]{1,0:T(8,128)(2,1)S(1)} %collective-permute-done.5.refs_2_, bf16[64,14336]{1,0:T(8,128)(2,1)S(1)} %collective-permute-done.8.refs_3_, ...), custom_call_target="tpu_custom_call" | custom-call | flops 344064 | bytes 1376256 | tf_op jit(solution)/shard_map/rotate/pallas_call | solution.py:125
  199.1 2.8 %collective-permute-done.22.refs_5_ = f32[192,1792]{1,0:T(8,128)S(1)} collective-permute-done((f32[192,1792]{1,0:T(8,128)S(1)}, f32[192,1792]{1,0:T(8,128)S(1)}, u32[]{:S(2)}, u32[]{:S(2)}) %collective-permute-start.22) | collective-permute-done | bytes 1376288 | tf_op jit(solution)/shard_map/ppermute | solution.py:146
  201.9 9.4 %fit.1 = f32[1792,2048]{1,0:T(8,128)} custom-call(s32[8]{0:T(128)S(1)} %stack.44.refs_0_, s32[1]{0:T(128)} %bitcast.11.refs_0_.refs_1_, s32[2]{0:T(128)S(1)} %pad_add_fusion.refs_2_, bf16[320,1792]{1,0:T(8,128)(2,1)S(1)} %add_convert_fusion.refs_3_, f32[192,1792]{1,0:T(8,128)S(1)} %rotate.11.refs_4_, f32[192,1792]{1,0:T(8,128)S(1)} %collective-permute-done.22.refs_5_, ...), custom_call_target="tpu_custom_call" | custom-call | flops 3758096384 | bytes 24117248 | tf_op jit(solution)/shard_map/fit/pallas_call | solution.py:64
  (50 shorter events, 9.4 us)
Async XLA Ops:
  0.0 10.9 %copy-start = (bf16[512,1024]{1,0:T(8,128)(2,1)S(1)}, bf16[512,1024]{1,0:T(8,128)(2,1)}, u32[]{:S(2)}) copy-start(bf16[512,1024]{1,0:T(8,128)(2,1)} %param.5) | copy-start | bytes 3145732
  0.0 19.5 %collective-permute-start.2 = (bf16[64,14336]{1,0:T(8,128)(2,1)}, bf16[64,14336]{1,0:T(8,128)(2,1)S(1)}, u32[]{:S(2)}, u32[]{:S(2)}) collective-permute-start(bf16[64,14336]{1,0:T(8,128)(2,1)} %refs_1_.3), channel_id=1, source_target_pairs={{4,8},{6,10},{8,4},{10,6},{5,9},{7,11},{9,5},{11,7},{20,24},{22,26... | collective-permute-start | bytes 5505032 | tf_op jit(solution)/shard_map/ppermute | solution.py:184
  0.9 46.6 %collective-permute-start.1 = (bf16[64,14336]{1,0:T(8,128)(2,1)}, bf16[64,14336]{1,0:T(8,128)(2,1)}, u32[]{:S(2)}, u32[]{:S(2)}) collective-permute-start(bf16[64,14336]{1,0:T(8,128)(2,1)} %refs_1_.3), channel_id=1, source_target_pairs={{0,4},{2,6},{4,0},{6,2},{8,12},{10,14},{12,8},{14,10},{1,5},{3,7},... | collective-permute-start | bytes 5505032 | tf_op jit(solution)/shard_map/ppermute | solution.py:184
  6.7 41.5 %collective-permute-start = (bf16[64,14336]{1,0:T(8,128)(2,1)}, bf16[64,14336]{1,0:T(8,128)(2,1)}, u32[]{:S(2)}, u32[]{:S(2)}) collective-permute-start(bf16[64,14336]{1,0:T(8,128)(2,1)} %refs_1_.3), channel_id=1, source_target_pairs={{0,2},{2,0},{4,6},{6,4},{8,10},{10,8},{12,14},{14,12},{1,3},{3,1},... | collective-permute-start | bytes 5505032 | tf_op jit(solution)/shard_map/ppermute | solution.py:184
  16.0 75.0 %collective-permute-start.6 = (bf16[512,2048]{1,0:T(8,128)(2,1)}, bf16[512,2048]{1,0:T(8,128)(2,1)}, u32[]{:S(2)}, u32[]{:S(2)}) collective-permute-start(bf16[512,2048]{1,0:T(8,128)(2,1)} %get-tuple-element.127), channel_id=1, source_target_pairs={{0,4},{2,6},{12,8},{14,10},{1,5},{3,7},{13,9},{15,11},{16,20},{18,... | collective-permute-start | bytes 6291464 | tf_op jit(solution)/shard_map/ppermute | solution.py:184
  19.5 28.8 %copy-start.2 = (bf16[64,14336]{1,0:T(8,128)(2,1)}, bf16[64,14336]{1,0:T(8,128)(2,1)S(1)}, u32[]{:S(2)}) copy-start(bf16[64,14336]{1,0:T(8,128)(2,1)S(1)} %collective-permute-done.2.refs_2_.refs_5_) | copy-start | bytes 5505028
  48.2 44.3 %collective-permute-start.5 = (bf16[64,14336]{1,0:T(8,128)(2,1)}, bf16[64,14336]{1,0:T(8,128)(2,1)S(1)}, u32[]{:S(2)}, u32[]{:S(2)}) collective-permute-start(bf16[64,14336]{1,0:T(8,128)(2,1)} %collective-permute-done.1.refs_2_), channel_id=1, source_target_pairs={{4,8},{6,10},{8,4},{10,6},{5,9},{7,11},{9,5},{11,7},{20,24},{22,26... | collective-permute-start | bytes 5505032 | tf_op jit(solution)/shard_map/ppermute | solution.py:184
  49.0 43.6 %collective-permute-start.3 = (bf16[64,14336]{1,0:T(8,128)(2,1)}, bf16[64,14336]{1,0:T(8,128)(2,1)}, u32[]{:S(2)}, u32[]{:S(2)}) collective-permute-start(bf16[64,14336]{1,0:T(8,128)(2,1)} %collective-permute-done.1.refs_2_), channel_id=1, source_target_pairs={{0,2},{2,0},{12,14},{14,12},{1,3},{3,1},{13,15},{15,13},{16,18},{1... | collective-permute-start | bytes 5505032 | tf_op jit(solution)/shard_map/ppermute | solution.py:184
  52.4 42.2 %collective-permute-start.4 = (bf16[64,14336]{1,0:T(8,128)(2,1)}, bf16[64,14336]{1,0:T(8,128)(2,1)}, u32[]{:S(2)}, u32[]{:S(2)}) collective-permute-start(bf16[64,14336]{1,0:T(8,128)(2,1)} %copy-done.2), channel_id=1, source_target_pairs={{4,0},{6,2},{8,12},{10,14},{5,1},{7,3},{9,13},{11,15},{20,16},{22,... | collective-permute-start | bytes 5505032 | tf_op jit(solution)/shard_map/ppermute | solution.py:184
  53.7 41.6 %collective-permute-start.9 = (bf16[64,14336]{1,0:T(8,128)(2,1)}, bf16[64,14336]{1,0:T(8,128)(2,1)}, u32[]{:S(2)}, u32[]{:S(2)}) collective-permute-start(bf16[64,14336]{1,0:T(8,128)(2,1)} %copy-done.2), channel_id=1, source_target_pairs={{4,6},{6,4},{8,10},{10,8},{5,7},{7,5},{9,11},{11,9},{20,22},{22,20... | collective-permute-start | bytes 5505032 | tf_op jit(solution)/shard_map/ppermute | solution.py:184
  55.6 1.5 copy-start.4
  57.1 33.9 %copy-start.6 = (f32[512,2048]{1,0:T(8,128)S(1)}, f32[512,2048]{1,0:T(8,128)}, u32[]{:S(2)}) copy-start(f32[512,2048]{1,0:T(8,128)} %get-tuple-element.79) | copy-start | bytes 12582916
  94.6 26.1 %collective-permute-start.10 = (bf16[512,1024]{1,0:T(8,128)(2,1)S(1)}, bf16[512,1024]{1,0:T(8,128)(2,1)S(1)}, u32[]{:S(2)}, u32[]{:S(2)}) collective-permute-start(bf16[512,1024]{1,0:T(8,128)(2,1)S(1)} %add_convert_fusion.2), channel_id=1, source_target_pairs={{4,8},{6,10},{8,4},{10,6},{5,9},{7,11},{9,5},{11,7},{20,24},{22,26... | collective-permute-start | bytes 3145736 | tf_op jit(solution)/shard_map/ppermute | solution.py:184
  95.4 13.3 %copy-start.3 = (bf16[64,14336]{1,0:T(8,128)(2,1)S(1)}, bf16[64,14336]{1,0:T(8,128)(2,1)}, u32[]{:S(2)}) copy-start(bf16[64,14336]{1,0:T(8,128)(2,1)} %copy-done.2) | copy-start | bytes 5505028
  95.4 25.3 %collective-permute-start.11 = (bf16[64,5120]{1,0:T(8,128)(2,1)S(1)}, bf16[64,5120]{1,0:T(8,128)(2,1)S(1)}, u32[]{:S(2)}, u32[]{:S(2)}) collective-permute-start(bf16[64,5120]{1,0:T(8,128)(2,1)S(1)} %slice.31), channel_id=1, source_target_pairs={{4,6},{6,4},{8,10},{10,8},{5,7},{7,5},{9,11},{11,9},{20,22},{22,20... | collective-permute-start | bytes 1966088 | tf_op jit(solution)/shard_map/ppermute | solution.py:184
  96.2 41.9 %collective-permute-start.8 = (bf16[64,14336]{1,0:T(8,128)(2,1)}, bf16[64,14336]{1,0:T(8,128)(2,1)S(1)}, u32[]{:S(2)}, u32[]{:S(2)}) collective-permute-start(bf16[64,14336]{1,0:T(8,128)(2,1)} %collective-permute-done.4.refs_1_.refs_4_), channel_id=1, source_target_pairs={{0,2},{2,0},{12,14},{14,12},{1,3},{3,1},{13,15},{15,13},{16,18},{1... | collective-permute-start | bytes 5505032 | tf_op jit(solution)/shard_map/ppermute | solution.py:184
  99.3 42.8 %collective-permute-start.7 = (bf16[64,14336]{1,0:T(8,128)(2,1)S(1)}, bf16[64,14336]{1,0:T(8,128)(2,1)S(1)}, u32[]{:S(2)}, u32[]{:S(2)}) collective-permute-start(bf16[64,14336]{1,0:T(8,128)(2,1)S(1)} %collective-permute-done.5.refs_2_), channel_id=1, source_target_pairs={{4,0},{6,2},{8,12},{10,14},{5,1},{7,3},{9,13},{11,15},{20,16},{22,... | collective-permute-start | bytes 5505032 | tf_op jit(solution)/shard_map/ppermute | solution.py:184
  100.6 43.9 %collective-permute-start.14 = (bf16[64,14336]{1,0:T(8,128)(2,1)}, bf16[64,14336]{1,0:T(8,128)(2,1)S(1)}, u32[]{:S(2)}, u32[]{:S(2)}) collective-permute-start(bf16[64,14336]{1,0:T(8,128)(2,1)} %collective-permute-done.refs_3_), channel_id=1, source_target_pairs={{0,4},{2,6},{12,8},{14,10},{1,5},{3,7},{13,9},{15,11},{16,20},{18,... | collective-permute-start | bytes 5505032 | tf_op jit(solution)/shard_map/ppermute | solution.py:184
  121.2 1.7 copy-start.5
  121.2 23.3 %collective-permute-start.13 = (bf16[512,1024]{1,0:T(8,128)(2,1)S(1)}, bf16[512,1024]{1,0:T(8,128)(2,1)S(1)}, u32[]{:S(2)}, u32[]{:S(2)}) collective-permute-start(bf16[512,1024]{1,0:T(8,128)(2,1)S(1)} %get-tuple-element.123), channel_id=1, source_target_pairs={{4,6},{6,4},{8,10},{10,8},{5,7},{7,5},{9,11},{11,9},{20,22},{22,20... | collective-permute-start | bytes 3145736 | tf_op jit(solution)/shard_map/ppermute | solution.py:184
  122.2 46.6 %collective-permute-start.16 = (bf16[64,9216]{1,0:T(8,128)(2,1)S(1)}, bf16[64,9216]{1,0:T(8,128)(2,1)S(1)}, u32[]{:S(2)}, u32[]{:S(2)}) collective-permute-start(bf16[64,9216]{1,0:T(8,128)(2,1)S(1)} %slice.34), channel_id=1, source_target_pairs={{4,6},{6,4},{8,10},{10,8},{5,7},{7,5},{9,11},{11,9},{20,22},{22,20... | collective-permute-start | bytes 3538952 | tf_op jit(solution)/shard_map/ppermute | solution.py:184
  142.2 15.0 %collective-permute-start.12 = (bf16[64,5120]{1,0:T(8,128)(2,1)S(1)}, bf16[64,5120]{1,0:T(8,128)(2,1)S(1)}, u32[]{:S(2)}, u32[]{:S(2)}) collective-permute-start(bf16[64,5120]{1,0:T(8,128)(2,1)S(1)} %slice.32), channel_id=1, source_target_pairs={{0,2},{2,0},{12,14},{14,12},{1,3},{3,1},{13,15},{15,13},{16,18},{1... | collective-permute-start | bytes 1966088 | tf_op jit(solution)/shard_map/ppermute | solution.py:184
  144.8 24.0 %collective-permute-start.18 = (bf16[512,1024]{1,0:T(8,128)(2,1)S(1)}, bf16[512,1024]{1,0:T(8,128)(2,1)S(1)}, u32[]{:S(2)}, u32[]{:S(2)}) collective-permute-start(bf16[512,1024]{1,0:T(8,128)(2,1)S(1)} %add_convert_fusion.1), channel_id=1, source_target_pairs={{4,0},{6,2},{8,12},{10,14},{5,1},{7,3},{9,13},{11,15},{20,16},{22,... | collective-permute-start | bytes 3145736 | tf_op jit(solution)/shard_map/ppermute | solution.py:184
  146.1 22.7 %collective-permute-start.17 = (bf16[512,1024]{1,0:T(8,128)(2,1)S(1)}, bf16[512,1024]{1,0:T(8,128)(2,1)S(1)}, u32[]{:S(2)}, u32[]{:S(2)}) collective-permute-start(bf16[512,1024]{1,0:T(8,128)(2,1)S(1)} %add_convert_fusion.1), channel_id=1, source_target_pairs={{4,8},{6,10},{8,4},{10,6},{5,9},{7,11},{9,5},{11,7},{20,24},{22,26... | collective-permute-start | bytes 3145736 | tf_op jit(solution)/shard_map/ppermute | solution.py:184
  157.2 11.6 %collective-permute-start.15 = (bf16[64,4096]{1,0:T(8,128)(2,1)S(1)}, bf16[64,4096]{1,0:T(8,128)(2,1)S(1)}, u32[]{:S(2)}, u32[]{:S(2)}) collective-permute-start(bf16[64,4096]{1,0:T(8,128)(2,1)S(1)} %slice.33), channel_id=1, source_target_pairs={{0,2},{2,0},{12,14},{14,12},{1,3},{3,1},{13,15},{15,13},{16,18},{1... | collective-permute-start | bytes 1572872 | tf_op jit(solution)/shard_map/ppermute | solution.py:184
  168.9 20.5 %collective-permute-start.21 = (f32[320,1792]{1,0:T(8,128)S(1)}, f32[320,1792]{1,0:T(8,128)S(1)}, u32[]{:S(2)}, u32[]{:S(2)}) collective-permute-start(f32[320,1792]{1,0:T(8,128)S(1)} %rotate.8), channel_id=1, source_target_pairs={{0,1},{1,0},{2,3},{3,2},{4,5},{5,4},{6,7},{7,6},{8,9},{9,8},{10,11... | collective-permute-start | bytes 6881288 | tf_op jit(solution)/shard_map/ppermute | solution.py:146
  168.9 29.8 %collective-permute-start.19 = (bf16[512,1024]{1,0:T(8,128)(2,1)S(1)}, bf16[512,1024]{1,0:T(8,128)(2,1)S(1)}, u32[]{:S(2)}, u32[]{:S(2)}) collective-permute-start(bf16[512,1024]{1,0:T(8,128)(2,1)S(1)} %collective-permute-done.17.refs_8_), channel_id=1, source_target_pairs={{4,0},{6,2},{8,12},{10,14},{5,1},{7,3},{9,13},{11,15},{20,16},{22,... | collective-permute-start | bytes 3145736 | tf_op jit(solution)/shard_map/ppermute | solution.py:184
  170.3 19.0 %collective-permute-start.20 = (bf16[64,5120]{1,0:T(8,128)(2,1)S(1)}, bf16[64,5120]{1,0:T(8,128)(2,1)S(1)}, u32[]{:S(2)}, u32[]{:S(2)}) collective-permute-start(bf16[64,5120]{1,0:T(8,128)(2,1)S(1)} %slice.35), channel_id=1, source_target_pairs={{0,2},{2,0},{12,14},{14,12},{1,3},{3,1},{13,15},{15,13},{16,18},{1... | collective-permute-start | bytes 1966088 | tf_op jit(solution)/shard_map/ppermute | solution.py:184
  198.7 3.2 %collective-permute-start.22 = (f32[192,1792]{1,0:T(8,128)S(1)}, f32[192,1792]{1,0:T(8,128)S(1)}, u32[]{:S(2)}, u32[]{:S(2)}) collective-permute-start(f32[192,1792]{1,0:T(8,128)S(1)} %rotate.11.refs_4_), channel_id=1, source_target_pairs={{0,1},{1,0},{2,3},{3,2},{4,5},{5,4},{6,7},{7,6},{8,9},{9,8},{10,11... | collective-permute-start | bytes 4128776 | tf_op jit(solution)/shard_map/ppermute | solution.py:146
  201.9 9.4 %copy-start.1 = (bf16[512,1024]{1,0:T(8,128)(2,1)S(1)}, bf16[512,1024]{1,0:T(8,128)(2,1)}, u32[]{:S(2)}) copy-start(bf16[512,1024]{1,0:T(8,128)(2,1)} %param.5) | copy-start | bytes 3145732

commit v20 on v19

--- a/solution.py
+++ b/solution.py
@@ -191,7 +191,7 @@
     end = at_end.astype(jnp.int32).reshape(1)
     half = (z >= 2).astype(jnp.int32)
     steps = inputs.shape[1] // DEEP
-    cuts = [0, 5 * steps // 14, 9 * steps // 14, steps]
+    cuts = [0, 5 * steps // 14, 9 * steps // 14, 12 * steps // 14, steps]
     part = basis_out.shape[1] // 4
     got = {"own": inputs}
 
@@ -275,8 +275,11 @@
     got["A2"] = swap_narrow(got["A"])
     got["R"] = pick("n1", "sum")
     last(1)
-    fence(("x4", 2), "A", "A2", "R", "D")
+    fence(("x4", 2), "A", "A2", "R", "D", "a3")
+    x4(3)
     last(2)
+    fence(("x4", 3), "A", "A2", "R", "D")
+    last(3)
     fence("n2", "m4", "R", "A", "A2", "D")
     got["D2"] = swap_narrow(got["D"])
     got["A"] = (got["A"] + got["A2"]).astype(BF16)

time: 212 us -> 211 us (level)
  waiting for transfers between devices: 76.2 us -> 70.6 us
  starting transfers between devices: 44.5 us -> 48.2 us
    ppermute x21 -> x22, waiting for transfers between devices: 73.4 us -> 67.7 us  [send(): return lax.ppermute(a, 'wide', perm)]
    ppermute x21 -> x22, starting transfers between devices: 44.4 us -> 48 us  [send(): return lax.ppermute(a, 'wide', perm)]
    pallas_call x6 -> x7, Pallas kernels: 66.5 us -> 67.7 us  [rotate(): pl.pallas_call(lambda *refs: rotate_kernel([len(block) for block in block...]
  transfers between devices with their start and end apart: 23 -> 24, of which waited for: 8 -> 8; matrix products, arithmetic and copies ran while one was open for 6% -> 6% of each run, Pallas kernels for 31% -> 32%
where the time goes in v20:
time: 211 us
  Pallas kernels  77.2 us (37%)
  waiting for transfers between devices  70.6 us (33%)
  starting transfers between devices  48.2 us (23%)
  matrix products  5.11 us (2%)
  other arithmetic  4.57 us (2%)
  local copies, waits for them, and re-layouts  4.52 us (2%)
    pallas_call x7, Pallas kernels, rotate(): pl.pallas_call(lambda *refs: rotate_kernel([len(block) for block in block...  67.7 us
    ppermute x22, waiting for transfers between devices, send(): return lax.ppermute(a, 'wide', perm)  67.7 us
    ppermute x22, starting transfers between devices, send(): return lax.ppermute(a, 'wide', perm)  48 us
    pallas_call x1, Pallas kernels, fit(): pl.pallas_call(lambda *refs: fit_kernel([len(halves) for halves in sums],...  9.42 us
    dot_general x1, matrix products, dot(): return jnp.dot(a, b, preferred_element_type=F32)  5.11 us
  transfers between devices with their start and end apart: 24, of which 8 were waited for; matrix products, arithmetic and copies ran while one was open for 6% of the time, Pallas kernels for 32%

profile of v20, /device:TPU:0, one launch (start us, length us, event | category | flops | bytes accessed | tf_op | source)
XLA Modules:
  0.0 210.6 jit_solution(4222331206948828783)
XLA Ops:
  0.9 5.8 %collective-permute-start.1 = (bf16[64,14336]{1,0:T(8,128)(2,1)}, bf16[64,14336]{1,0:T(8,128)(2,1)}, u32[]{:S(2)}, u32[]{:S(2)}) collective-permute-start(bf16[64,14336]{1,0:T(8,128)(2,1)} %refs_1_.3), channel_id=1, source_target_pairs={{0,4},{2,6},{4,0},{6,2},{8,12},{10,14},{12,8},{14,10},{1,5},{3,7},... | collective-permute-start | bytes 5505032 | tf_op jit(solution)/shard_map/ppermute | solution.py:184
  6.7 1.5 collective-permute-start
  8.2 2.7 %constant_dynamic-slice_fusion.1 = (bf16[1024,1024]{1,0:T(8,128)(2,1)S(1)}, bf16[1024,1024]{1,0:T(8,128)(2,1)S(1)}) fusion(bf16[1024,2048]{1,0:T(8,128)(2,1)} %param.7, s32[]{:T(128)S(6)} %select_n.48, s32[]{:T(128)S(6)} %select_n.49), kind=kLoop, calls=%fused_computation.13 | loop fusion | bytes 8388616 | tf_op jit(solution)/shard_map/dynamic_slice | solution.py:205
  10.9 5.1 %fusion.9 = (bf16[512,2048]{1,0:T(8,128)(2,1)}, f32[512,2048]{1,0:T(8,128)}) fusion(bf16[512,1024]{1,0:T(8,128)(2,1)S(1)} %copy-done, bf16[1024,1024]{1,0:T(8,128)(2,1)S(1)} %get-tuple-element.138, bf16[1024,1024]{1,0:T(8,128)(2,1)S(1)} %get-tuple-element.137), kind=kOutput, calls=%fused_computation.16 | convolution fusion | flops 2156920832 | bytes 11534336 | tf_op jit(solution)/shard_map/dot_general | solution.py:16
  16.0 3.3 %collective-permute-start.6 = (bf16[512,2048]{1,0:T(8,128)(2,1)}, bf16[512,2048]{1,0:T(8,128)(2,1)}, u32[]{:S(2)}, u32[]{:S(2)}) collective-permute-start(bf16[512,2048]{1,0:T(8,128)(2,1)} %get-tuple-element.139), channel_id=1, source_target_pairs={{0,4},{2,6},{12,8},{14,10},{1,5},{3,7},{13,9},{15,11},{16,20},{18,... | collective-permute-start | bytes 6291464 | tf_op jit(solution)/shard_map/ppermute | solution.py:184
  19.5 28.0 %collective-permute-done.1.refs_2_ = bf16[64,14336]{1,0:T(8,128)(2,1)} collective-permute-done((bf16[64,14336]{1,0:T(8,128)(2,1)}, bf16[64,14336]{1,0:T(8,128)(2,1)}, u32[]{:S(2)}, u32[]{:S(2)}) %collective-permute-start.1) | collective-permute-done | bytes 1835040 | tf_op jit(solution)/shard_map/ppermute | solution.py:184
  49.0 3.4 %collective-permute-start.3 = (bf16[64,14336]{1,0:T(8,128)(2,1)}, bf16[64,14336]{1,0:T(8,128)(2,1)}, u32[]{:S(2)}, u32[]{:S(2)}) collective-permute-start(bf16[64,14336]{1,0:T(8,128)(2,1)} %collective-permute-done.1.refs_2_), channel_id=1, source_target_pairs={{0,2},{2,0},{12,14},{14,12},{1,3},{3,1},{13,15},{15,13},{16,18},{1... | collective-permute-start | bytes 5505032 | tf_op jit(solution)/shard_map/ppermute | solution.py:184
  53.7 1.9 collective-permute-start.9
  55.6 1.5 copy-done.4
  57.1 13.0 %rotate.7.refs_9_ = f32[192,1792]{1,0:T(8,128)S(1)} custom-call(s32[1]{0:T(128)} %bitcast.11.refs_0_.refs_1_, bf16[64,14336]{1,0:T(8,128)(2,1)S(1)} %copy-done.4, bf16[64,14336]{1,0:T(8,128)(2,1)} %collective-permute-done.1.refs_2_, bf16[64,14336]{1,0:T(8,128)(2,1)} %collective-permute-done.refs_3_, bf16[14336,1792]{1,0:T(8,128)(2,1)} %refs_7_.7), custom_call_target="tpu_custom_call" | custom-call | flops 344064 | bytes 1376256 | tf_op jit(solution)/shard_map/rotate/pallas_call | solution.py:125
  70.1 20.8 %collective-permute-done.6 = bf16[512,2048]{1,0:T(8,128)(2,1)} collective-permute-done((bf16[512,2048]{1,0:T(8,128)(2,1)}, bf16[512,2048]{1,0:T(8,128)(2,1)}, u32[]{:S(2)}, u32[]{:S(2)}) %collective-permute-start.6) | collective-permute-done | bytes 2097184 | tf_op jit(solution)/shard_map/ppermute | solution.py:184
  91.0 1.6 add_convert_fusion.2
  92.6 2.0 collective-permute-done.4.refs_1_.refs_4_
  96.2 3.1 %collective-permute-start.8 = (bf16[64,14336]{1,0:T(8,128)(2,1)}, bf16[64,14336]{1,0:T(8,128)(2,1)S(1)}, u32[]{:S(2)}, u32[]{:S(2)}) collective-permute-start(bf16[64,14336]{1,0:T(8,128)(2,1)} %collective-permute-done.4.refs_1_.refs_4_), channel_id=1, source_target_pairs={{0,2},{2,0},{12,14},{14,12},{1,3},{3,1},{13,15},{15,13},{16,18},{1... | collective-permute-start | bytes 5505032 | tf_op jit(solution)/shard_map/ppermute | solution.py:184
  99.3 1.3 collective-permute-start.7
  100.6 6.4 %collective-permute-start.14 = (bf16[64,14336]{1,0:T(8,128)(2,1)}, bf16[64,14336]{1,0:T(8,128)(2,1)S(1)}, u32[]{:S(2)}, u32[]{:S(2)}) collective-permute-start(bf16[64,14336]{1,0:T(8,128)(2,1)} %collective-permute-done.refs_3_), channel_id=1, source_target_pairs={{0,4},{2,6},{12,8},{14,10},{1,5},{3,7},{13,9},{15,11},{16,20},{18,... | collective-permute-start | bytes 5505032 | tf_op jit(solution)/shard_map/ppermute | solution.py:184
  107.0 1.7 convert_add_fusion.1
  108.7 11.9 %rotate.8.refs_10_ = f32[128,1792]{1,0:T(8,128)S(1)} custom-call(s32[1]{0:T(128)} %bitcast.11.refs_0_.refs_1_, bf16[64,14336]{1,0:T(8,128)(2,1)} %collective-permute-done.4.refs_1_.refs_4_, bf16[64,14336]{1,0:T(8,128)(2,1)S(1)} %copy-done.3, bf16[64,14336]{1,0:T(8,128)(2,1)} %collective-permute-done.3.refs_3_.refs_6_, ...), custom_call_target="tpu_custom_call" | custom-call | flops 229376 | bytes 917504 | tf_op jit(solution)/shard_map/rotate/pallas_call | solution.py:125
  122.9 15.2 %rotate.9 = f32[320,1792]{1,0:T(8,128)S(1)} custom-call(s32[1]{0:T(128)} %bitcast.11.refs_0_.refs_1_, bf16[64,14336]{1,0:T(8,128)(2,1)S(1)} %copy-done.5, bf16[64,14336]{1,0:T(8,128)(2,1)} %collective-permute-done.1.refs_2_, bf16[64,14336]{1,0:T(8,128)(2,1)} %collective-permute-done.refs_3_, bf16[64,14336]{1,0:T(8,128)(2,1)} %collective-permute-done.4.refs_1_.refs_4_, ...), custom_call_target="tpu_custom_call" | custom-call | flops 573440 | bytes 2293760 | tf_op jit(solution)/shard_map/rotate/pallas_call | solution.py:125
  138.1 4.0 %collective-permute-done.7.refs_1_ = bf16[64,14336]{1,0:T(8,128)(2,1)S(1)} collective-permute-done((bf16[64,14336]{1,0:T(8,128)(2,1)S(1)}, bf16[64,14336]{1,0:T(8,128)(2,1)S(1)}, u32[]{:S(2)}, u32[]{:S(2)}) %collective-permute-start.7) | collective-permute-done | bytes 1835040 | tf_op jit(solution)/shard_map/ppermute | solution.py:184
  142.2 2.3 %collective-permute-start.12 = (bf16[64,5120]{1,0:T(8,128)(2,1)S(1)}, bf16[64,5120]{1,0:T(8,128)(2,1)S(1)}, u32[]{:S(2)}, u32[]{:S(2)}) collective-permute-start(bf16[64,5120]{1,0:T(8,128)(2,1)S(1)} %slice.35), channel_id=1, source_target_pairs={{0,2},{2,0},{12,14},{14,12},{1,3},{3,1},{13,15},{15,13},{16,18},{1... | collective-permute-start | bytes 1966088 | tf_op jit(solution)/shard_map/ppermute | solution.py:184
  146.9 10.2 %collective-permute-done.12.refs_5_ = bf16[64,5120]{1,0:T(8,128)(2,1)S(1)} collective-permute-done((bf16[64,5120]{1,0:T(8,128)(2,1)S(1)}, bf16[64,5120]{1,0:T(8,128)(2,1)S(1)}, u32[]{:S(2)}, u32[]{:S(2)}) %collective-permute-start.12) | collective-permute-done | bytes 655392 | tf_op jit(solution)/shard_map/ppermute | solution.py:184
  157.2 2.2 %collective-permute-start.15 = (bf16[64,4096]{1,0:T(8,128)(2,1)S(1)}, bf16[64,4096]{1,0:T(8,128)(2,1)S(1)}, u32[]{:S(2)}, u32[]{:S(2)}) collective-permute-start(bf16[64,4096]{1,0:T(8,128)(2,1)S(1)} %slice.36), channel_id=1, source_target_pairs={{0,2},{2,0},{12,14},{14,12},{1,3},{3,1},{13,15},{15,13},{16,18},{1... | collective-permute-start | bytes 1572872 | tf_op jit(solution)/shard_map/ppermute | solution.py:184
  159.4 9.4 %rotate.10.refs_8_ = f32[192,1792]{1,0:T(8,128)S(1)} custom-call(s32[1]{0:T(128)} %bitcast.11.refs_0_.refs_1_, bf16[64,14336]{1,0:T(8,128)(2,1)S(1)} %collective-permute-done.7.refs_1_, bf16[64,14336]{1,0:T(8,128)(2,1)S(1)} %collective-permute-done.5.refs_2_, bf16[64,14336]{1,0:T(8,128)(2,1)S(1)} %collective-permute-done.8.refs_3_, ...), custom_call_target="tpu_custom_call" | custom-call | flops 344064 | bytes 1376256 | tf_op jit(solution)/shard_map/rotate/pallas_call | solution.py:125
  170.2 3.8 %collective-permute-start.20 = (bf16[64,3072]{1,0:T(8,128)(2,1)S(1)}, bf16[64,3072]{1,0:T(8,128)(2,1)S(1)}, u32[]{:S(2)}, u32[]{:S(2)}) collective-permute-start(bf16[64,3072]{1,0:T(8,128)(2,1)S(1)} %slice.38), channel_id=1, source_target_pairs={{0,2},{2,0},{12,14},{14,12},{1,3},{3,1},{13,15},{15,13},{16,18},{1... | collective-permute-start | bytes 1179656 | tf_op jit(solution)/shard_map/ppermute | solution.py:184
  174.1 7.6 %rotate.11.refs_8_ = f32[192,1792]{1,0:T(8,128)S(1)} custom-call(s32[1]{0:T(128)} %bitcast.11.refs_0_.refs_1_, bf16[64,14336]{1,0:T(8,128)(2,1)S(1)} %collective-permute-done.7.refs_1_, bf16[64,14336]{1,0:T(8,128)(2,1)S(1)} %collective-permute-done.5.refs_2_, bf16[64,14336]{1,0:T(8,128)(2,1)S(1)} %collective-permute-done.8.refs_3_, ...), custom_call_target="tpu_custom_call" | custom-call | flops 344064 | bytes 1376256 | tf_op jit(solution)/shard_map/rotate/pallas_call | solution.py:125
  181.8 1.8 collective-permute-done.20.refs_5_
  183.7 3.6 %collective-permute-start.22 = (bf16[64,2048]{1,0:T(8,128)(2,1)S(1)}, bf16[64,2048]{1,0:T(8,128)(2,1)S(1)}, u32[]{:S(2)}, u32[]{:S(2)}) collective-permute-start(bf16[64,2048]{1,0:T(8,128)(2,1)S(1)} %slice.39), channel_id=1, source_target_pairs={{0,2},{2,0},{12,14},{14,12},{1,3},{3,1},{13,15},{15,13},{16,18},{1... | collective-permute-start | bytes 786440 | tf_op jit(solution)/shard_map/ppermute | solution.py:184
  187.3 6.3 %rotate.12.refs_8_ = f32[192,1792]{1,0:T(8,128)S(1)} custom-call(s32[1]{0:T(128)} %bitcast.11.refs_0_.refs_1_, bf16[64,14336]{1,0:T(8,128)(2,1)S(1)} %collective-permute-done.7.refs_1_, bf16[64,14336]{1,0:T(8,128)(2,1)S(1)} %collective-permute-done.5.refs_2_, bf16[64,14336]{1,0:T(8,128)(2,1)S(1)} %collective-permute-done.8.refs_3_, ...), custom_call_target="tpu_custom_call" | custom-call | flops 344064 | bytes 1376256 | tf_op jit(solution)/shard_map/rotate/pallas_call | solution.py:125
  193.6 4.3 %rotate.13.refs_4_ = f32[192,1792]{1,0:T(8,128)S(1)} custom-call(s32[1]{0:T(128)} %bitcast.11.refs_0_.refs_1_, bf16[64,14336]{1,0:T(8,128)(2,1)S(1)} %collective-permute-done.7.refs_1_, bf16[64,14336]{1,0:T(8,128)(2,1)S(1)} %collective-permute-done.5.refs_2_, bf16[64,14336]{1,0:T(8,128)(2,1)S(1)} %collective-permute-done.8.refs_3_, ...), custom_call_target="tpu_custom_call" | custom-call | flops 344064 | bytes 1376256 | tf_op jit(solution)/shard_map/rotate/pallas_call | solution.py:125
  198.3 2.8 %collective-permute-done.23.refs_5_ = f32[192,1792]{1,0:T(8,128)S(1)} collective-permute-done((f32[192,1792]{1,0:T(8,128)S(1)}, f32[192,1792]{1,0:T(8,128)S(1)}, u32[]{:S(2)}, u32[]{:S(2)}) %collective-permute-start.23) | collective-permute-done | bytes 1376288 | tf_op jit(solution)/shard_map/ppermute | solution.py:146
  201.2 9.4 %fit.1 = f32[1792,2048]{1,0:T(8,128)} custom-call(s32[8]{0:T(128)S(1)} %stack.44.refs_0_, s32[1]{0:T(128)} %bitcast.11.refs_0_.refs_1_, s32[2]{0:T(128)S(1)} %pad_add_fusion.refs_2_, bf16[320,1792]{1,0:T(8,128)(2,1)S(1)} %add_convert_fusion.refs_3_, f32[192,1792]{1,0:T(8,128)S(1)} %rotate.13.refs_4_, f32[192,1792]{1,0:T(8,128)S(1)} %collective-permute-done.23.refs_5_, ...), custom_call_target="tpu_custom_call" | custom-call | flops 3758096384 | bytes 24117248 | tf_op jit(solution)/shard_map/fit/pallas_call | solution.py:64
  (54 shorter events, 12.0 us)
Async XLA Ops:
  0.0 10.9 %copy-start = (bf16[512,1024]{1,0:T(8,128)(2,1)S(1)}, bf16[512,1024]{1,0:T(8,128)(2,1)}, u32[]{:S(2)}) copy-start(bf16[512,1024]{1,0:T(8,128)(2,1)} %param.5) | copy-start | bytes 3145732
  0.0 19.4 %collective-permute-start.2 = (bf16[64,14336]{1,0:T(8,128)(2,1)}, bf16[64,14336]{1,0:T(8,128)(2,1)S(1)}, u32[]{:S(2)}, u32[]{:S(2)}) collective-permute-start(bf16[64,14336]{1,0:T(8,128)(2,1)} %refs_1_.3), channel_id=1, source_target_pairs={{4,8},{6,10},{8,4},{10,6},{5,9},{7,11},{9,5},{11,7},{20,24},{22,26... | collective-permute-start | bytes 5505032 | tf_op jit(solution)/shard_map/ppermute | solution.py:184
  0.9 46.6 %collective-permute-start.1 = (bf16[64,14336]{1,0:T(8,128)(2,1)}, bf16[64,14336]{1,0:T(8,128)(2,1)}, u32[]{:S(2)}, u32[]{:S(2)}) collective-permute-start(bf16[64,14336]{1,0:T(8,128)(2,1)} %refs_1_.3), channel_id=1, source_target_pairs={{0,4},{2,6},{4,0},{6,2},{8,12},{10,14},{12,8},{14,10},{1,5},{3,7},... | collective-permute-start | bytes 5505032 | tf_op jit(solution)/shard_map/ppermute | solution.py:184
  6.7 41.5 %collective-permute-start = (bf16[64,14336]{1,0:T(8,128)(2,1)}, bf16[64,14336]{1,0:T(8,128)(2,1)}, u32[]{:S(2)}, u32[]{:S(2)}) collective-permute-start(bf16[64,14336]{1,0:T(8,128)(2,1)} %refs_1_.3), channel_id=1, source_target_pairs={{0,2},{2,0},{4,6},{6,4},{8,10},{10,8},{12,14},{14,12},{1,3},{3,1},... | collective-permute-start | bytes 5505032 | tf_op jit(solution)/shard_map/ppermute | solution.py:184
  16.0 75.0 %collective-permute-start.6 = (bf16[512,2048]{1,0:T(8,128)(2,1)}, bf16[512,2048]{1,0:T(8,128)(2,1)}, u32[]{:S(2)}, u32[]{:S(2)}) collective-permute-start(bf16[512,2048]{1,0:T(8,128)(2,1)} %get-tuple-element.139), channel_id=1, source_target_pairs={{0,4},{2,6},{12,8},{14,10},{1,5},{3,7},{13,9},{15,11},{16,20},{18,... | collective-permute-start | bytes 6291464 | tf_op jit(solution)/shard_map/ppermute | solution.py:184
  19.5 28.8 %copy-start.2 = (bf16[64,14336]{1,0:T(8,128)(2,1)}, bf16[64,14336]{1,0:T(8,128)(2,1)S(1)}, u32[]{:S(2)}) copy-start(bf16[64,14336]{1,0:T(8,128)(2,1)S(1)} %collective-permute-done.2.refs_2_.refs_5_) | copy-start | bytes 5505028
  48.2 44.3 %collective-permute-start.5 = (bf16[64,14336]{1,0:T(8,128)(2,1)}, bf16[64,14336]{1,0:T(8,128)(2,1)S(1)}, u32[]{:S(2)}, u32[]{:S(2)}) collective-permute-start(bf16[64,14336]{1,0:T(8,128)(2,1)} %collective-permute-done.1.refs_2_), channel_id=1, source_target_pairs={{4,8},{6,10},{8,4},{10,6},{5,9},{7,11},{9,5},{11,7},{20,24},{22,26... | collective-permute-start | bytes 5505032 | tf_op jit(solution)/shard_map/ppermute | solution.py:184
  49.0 43.6 %collective-permute-start.3 = (bf16[64,14336]{1,0:T(8,128)(2,1)}, bf16[64,14336]{1,0:T(8,128)(2,1)}, u32[]{:S(2)}, u32[]{:S(2)}) collective-permute-start(bf16[64,14336]{1,0:T(8,128)(2,1)} %collective-permute-done.1.refs_2_), channel_id=1, source_target_pairs={{0,2},{2,0},{12,14},{14,12},{1,3},{3,1},{13,15},{15,13},{16,18},{1... | collective-permute-start | bytes 5505032 | tf_op jit(solution)/shard_map/ppermute | solution.py:184
  52.4 42.2 %collective-permute-start.4 = (bf16[64,14336]{1,0:T(8,128)(2,1)}, bf16[64,14336]{1,0:T(8,128)(2,1)}, u32[]{:S(2)}, u32[]{:S(2)}) collective-permute-start(bf16[64,14336]{1,0:T(8,128)(2,1)} %copy-done.2), channel_id=1, source_target_pairs={{4,0},{6,2},{8,12},{10,14},{5,1},{7,3},{9,13},{11,15},{20,16},{22,... | collective-permute-start | bytes 5505032 | tf_op jit(solution)/shard_map/ppermute | solution.py:184
  53.7 41.6 %collective-permute-start.9 = (bf16[64,14336]{1,0:T(8,128)(2,1)}, bf16[64,14336]{1,0:T(8,128)(2,1)}, u32[]{:S(2)}, u32[]{:S(2)}) collective-permute-start(bf16[64,14336]{1,0:T(8,128)(2,1)} %copy-done.2), channel_id=1, source_target_pairs={{4,6},{6,4},{8,10},{10,8},{5,7},{7,5},{9,11},{11,9},{20,22},{22,20... | collective-permute-start | bytes 5505032 | tf_op jit(solution)/shard_map/ppermute | solution.py:184
  55.6 1.5 copy-start.4
  57.1 33.9 %copy-start.6 = (f32[512,2048]{1,0:T(8,128)S(1)}, f32[512,2048]{1,0:T(8,128)}, u32[]{:S(2)}) copy-start(f32[512,2048]{1,0:T(8,128)} %get-tuple-element.85) | copy-start | bytes 12582916
  94.6 26.0 %collective-permute-start.10 = (bf16[512,1024]{1,0:T(8,128)(2,1)S(1)}, bf16[512,1024]{1,0:T(8,128)(2,1)S(1)}, u32[]{:S(2)}, u32[]{:S(2)}) collective-permute-start(bf16[512,1024]{1,0:T(8,128)(2,1)S(1)} %add_convert_fusion.2), channel_id=1, source_target_pairs={{4,8},{6,10},{8,4},{10,6},{5,9},{7,11},{9,5},{11,7},{20,24},{22,26... | collective-permute-start | bytes 3145736 | tf_op jit(solution)/shard_map/ppermute | solution.py:184
  95.4 13.3 %copy-start.3 = (bf16[64,14336]{1,0:T(8,128)(2,1)S(1)}, bf16[64,14336]{1,0:T(8,128)(2,1)}, u32[]{:S(2)}) copy-start(bf16[64,14336]{1,0:T(8,128)(2,1)} %copy-done.2) | copy-start | bytes 5505028
  95.4 25.2 %collective-permute-start.11 = (bf16[64,5120]{1,0:T(8,128)(2,1)S(1)}, bf16[64,5120]{1,0:T(8,128)(2,1)S(1)}, u32[]{:S(2)}, u32[]{:S(2)}) collective-permute-start(bf16[64,5120]{1,0:T(8,128)(2,1)S(1)} %slice.34), channel_id=1, source_target_pairs={{4,6},{6,4},{8,10},{10,8},{5,7},{7,5},{9,11},{11,9},{20,22},{22,20... | collective-permute-start | bytes 1966088 | tf_op jit(solution)/shard_map/ppermute | solution.py:184
  96.2 41.9 %collective-permute-start.8 = (bf16[64,14336]{1,0:T(8,128)(2,1)}, bf16[64,14336]{1,0:T(8,128)(2,1)S(1)}, u32[]{:S(2)}, u32[]{:S(2)}) collective-permute-start(bf16[64,14336]{1,0:T(8,128)(2,1)} %collective-permute-done.4.refs_1_.refs_4_), channel_id=1, source_target_pairs={{0,2},{2,0},{12,14},{14,12},{1,3},{3,1},{13,15},{15,13},{16,18},{1... | collective-permute-start | bytes 5505032 | tf_op jit(solution)/shard_map/ppermute | solution.py:184
  99.3 42.8 %collective-permute-start.7 = (bf16[64,14336]{1,0:T(8,128)(2,1)S(1)}, bf16[64,14336]{1,0:T(8,128)(2,1)S(1)}, u32[]{:S(2)}, u32[]{:S(2)}) collective-permute-start(bf16[64,14336]{1,0:T(8,128)(2,1)S(1)} %collective-permute-done.5.refs_2_), channel_id=1, source_target_pairs={{4,0},{6,2},{8,12},{10,14},{5,1},{7,3},{9,13},{11,15},{20,16},{22,... | collective-permute-start | bytes 5505032 | tf_op jit(solution)/shard_map/ppermute | solution.py:184
  100.6 43.9 %collective-permute-start.14 = (bf16[64,14336]{1,0:T(8,128)(2,1)}, bf16[64,14336]{1,0:T(8,128)(2,1)S(1)}, u32[]{:S(2)}, u32[]{:S(2)}) collective-permute-start(bf16[64,14336]{1,0:T(8,128)(2,1)} %collective-permute-done.refs_3_), channel_id=1, source_target_pairs={{0,4},{2,6},{12,8},{14,10},{1,5},{3,7},{13,9},{15,11},{16,20},{18,... | collective-permute-start | bytes 5505032 | tf_op jit(solution)/shard_map/ppermute | solution.py:184
  121.2 1.7 copy-start.5
  121.2 23.3 %collective-permute-start.13 = (bf16[512,1024]{1,0:T(8,128)(2,1)S(1)}, bf16[512,1024]{1,0:T(8,128)(2,1)S(1)}, u32[]{:S(2)}, u32[]{:S(2)}) collective-permute-start(bf16[512,1024]{1,0:T(8,128)(2,1)S(1)} %get-tuple-element.135), channel_id=1, source_target_pairs={{4,6},{6,4},{8,10},{10,8},{5,7},{7,5},{9,11},{11,9},{20,22},{22,20... | collective-permute-start | bytes 3145736 | tf_op jit(solution)/shard_map/ppermute | solution.py:184
  122.2 46.6 %collective-permute-start.16 = (bf16[64,9216]{1,0:T(8,128)(2,1)S(1)}, bf16[64,9216]{1,0:T(8,128)(2,1)S(1)}, u32[]{:S(2)}, u32[]{:S(2)}) collective-permute-start(bf16[64,9216]{1,0:T(8,128)(2,1)S(1)} %slice.37), channel_id=1, source_target_pairs={{4,6},{6,4},{8,10},{10,8},{5,7},{7,5},{9,11},{11,9},{20,22},{22,20... | collective-permute-start | bytes 3538952 | tf_op jit(solution)/shard_map/ppermute | solution.py:184
  142.2 15.0 %collective-permute-start.12 = (bf16[64,5120]{1,0:T(8,128)(2,1)S(1)}, bf16[64,5120]{1,0:T(8,128)(2,1)S(1)}, u32[]{:S(2)}, u32[]{:S(2)}) collective-permute-start(bf16[64,5120]{1,0:T(8,128)(2,1)S(1)} %slice.35), channel_id=1, source_target_pairs={{0,2},{2,0},{12,14},{14,12},{1,3},{3,1},{13,15},{15,13},{16,18},{1... | collective-permute-start | bytes 1966088 | tf_op jit(solution)/shard_map/ppermute | solution.py:184
  144.8 24.0 %collective-permute-start.18 = (bf16[512,1024]{1,0:T(8,128)(2,1)S(1)}, bf16[512,1024]{1,0:T(8,128)(2,1)S(1)}, u32[]{:S(2)}, u32[]{:S(2)}) collective-permute-start(bf16[512,1024]{1,0:T(8,128)(2,1)S(1)} %add_convert_fusion.1), channel_id=1, source_target_pairs={{4,0},{6,2},{8,12},{10,14},{5,1},{7,3},{9,13},{11,15},{20,16},{22,... | collective-permute-start | bytes 3145736 | tf_op jit(solution)/shard_map/ppermute | solution.py:184
  146.1 22.7 %collective-permute-start.17 = (bf16[512,1024]{1,0:T(8,128)(2,1)S(1)}, bf16[512,1024]{1,0:T(8,128)(2,1)S(1)}, u32[]{:S(2)}, u32[]{:S(2)}) collective-permute-start(bf16[512,1024]{1,0:T(8,128)(2,1)S(1)} %add_convert_fusion.1), channel_id=1, source_target_pairs={{4,8},{6,10},{8,4},{10,6},{5,9},{7,11},{9,5},{11,7},{20,24},{22,26... | collective-permute-start | bytes 3145736 | tf_op jit(solution)/shard_map/ppermute | solution.py:184
  157.2 11.6 %collective-permute-start.15 = (bf16[64,4096]{1,0:T(8,128)(2,1)S(1)}, bf16[64,4096]{1,0:T(8,128)(2,1)S(1)}, u32[]{:S(2)}, u32[]{:S(2)}) collective-permute-start(bf16[64,4096]{1,0:T(8,128)(2,1)S(1)} %slice.36), channel_id=1, source_target_pairs={{0,2},{2,0},{12,14},{14,12},{1,3},{3,1},{13,15},{15,13},{16,18},{1... | collective-permute-start | bytes 1572872 | tf_op jit(solution)/shard_map/ppermute | solution.py:184
  168.8 14.8 %collective-permute-start.21 = (f32[320,1792]{1,0:T(8,128)S(1)}, f32[320,1792]{1,0:T(8,128)S(1)}, u32[]{:S(2)}, u32[]{:S(2)}) collective-permute-start(f32[320,1792]{1,0:T(8,128)S(1)} %rotate.9), channel_id=1, source_target_pairs={{0,1},{1,0},{2,3},{3,2},{4,5},{5,4},{6,7},{7,6},{8,9},{9,8},{10,11... | collective-permute-start | bytes 6881288 | tf_op jit(solution)/shard_map/ppermute | solution.py:146
  168.9 29.0 %collective-permute-start.19 = (bf16[512,1024]{1,0:T(8,128)(2,1)S(1)}, bf16[512,1024]{1,0:T(8,128)(2,1)S(1)}, u32[]{:S(2)}, u32[]{:S(2)}) collective-permute-start(bf16[512,1024]{1,0:T(8,128)(2,1)S(1)} %collective-permute-done.17.refs_8_), channel_id=1, source_target_pairs={{4,0},{6,2},{8,12},{10,14},{5,1},{7,3},{9,13},{11,15},{20,16},{22,... | collective-permute-start | bytes 3145736 | tf_op jit(solution)/shard_map/ppermute | solution.py:184
  170.2 13.4 %collective-permute-start.20 = (bf16[64,3072]{1,0:T(8,128)(2,1)S(1)}, bf16[64,3072]{1,0:T(8,128)(2,1)S(1)}, u32[]{:S(2)}, u32[]{:S(2)}) collective-permute-start(bf16[64,3072]{1,0:T(8,128)(2,1)S(1)} %slice.38), channel_id=1, source_target_pairs={{0,2},{2,0},{12,14},{14,12},{1,3},{3,1},{13,15},{15,13},{16,18},{1... | collective-permute-start | bytes 1179656 | tf_op jit(solution)/shard_map/ppermute | solution.py:184
  183.7 10.0 %collective-permute-start.22 = (bf16[64,2048]{1,0:T(8,128)(2,1)S(1)}, bf16[64,2048]{1,0:T(8,128)(2,1)S(1)}, u32[]{:S(2)}, u32[]{:S(2)}) collective-permute-start(bf16[64,2048]{1,0:T(8,128)(2,1)S(1)} %slice.39), channel_id=1, source_target_pairs={{0,2},{2,0},{12,14},{14,12},{1,3},{3,1},{13,15},{15,13},{16,18},{1... | collective-permute-start | bytes 786440 | tf_op jit(solution)/shard_map/ppermute | solution.py:184
  198.0 3.2 %collective-permute-start.23 = (f32[192,1792]{1,0:T(8,128)S(1)}, f32[192,1792]{1,0:T(8,128)S(1)}, u32[]{:S(2)}, u32[]{:S(2)}) collective-permute-start(f32[192,1792]{1,0:T(8,128)S(1)} %rotate.13.refs_4_), channel_id=1, source_target_pairs={{0,1},{1,0},{2,3},{3,2},{4,5},{5,4},{6,7},{7,6},{8,9},{9,8},{10,11... | collective-permute-start | bytes 4128776 | tf_op jit(solution)/shard_map/ppermute | solution.py:146
  201.2 9.4 %copy-start.1 = (bf16[512,1024]{1,0:T(8,128)(2,1)S(1)}, bf16[512,1024]{1,0:T(8,128)(2,1)}, u32[]{:S(2)}) copy-start(bf16[512,1024]{1,0:T(8,128)(2,1)} %param.5) | copy-start | bytes 3145732

commit v21 on v20

--- a/solution.py
+++ b/solution.py
@@ -7,8 +7,8 @@
 
 EX = 2
 LINE, PAIR = 4, 2
-DEEP = 1024
-VMEM = 22 << 20
+DEEP = 512
+VMEM = 16 << 20
 BF16, F32 = jnp.bfloat16, jnp.float32
 
 

time: 211 us -> 221 us (1.047)
  Pallas kernels: 77.2 us -> 95.3 us
  waiting for transfers between devices: 70.6 us -> 60.9 us
    pallas_call x7, Pallas kernels: 67.7 us -> 85.9 us  [rotate(): pl.pallas_call(lambda *refs: rotate_kernel([len(block) for block in block...]
    ppermute x22, waiting for transfers between devices: 67.7 us -> 58.1 us  [send(): return lax.ppermute(a, 'wide', perm)]
  transfers between devices with their start and end apart: 24 -> 24, of which waited for: 8 -> 6; matrix products, arithmetic and copies ran while one was open for 6% -> 6% of each run, Pallas kernels for 32% -> 39%
where the time goes in v21:
time: 221 us; the launch traced here: 219 us
  Pallas kernels  95.3 us (43%)
  waiting for transfers between devices  60.9 us (28%)
  starting transfers between devices  48.4 us (22%)
  matrix products  5.11 us (2%)
  other arithmetic  4.7 us (2%)
  local copies, waits for them, and re-layouts  4.52 us (2%)
    pallas_call x7, Pallas kernels, rotate(): pl.pallas_call(lambda *refs: rotate_kernel([len(block) for block in block...  85.9 us
    ppermute x22, waiting for transfers between devices, send(): return lax.ppermute(a, 'wide', perm)  58.1 us
    ppermute x22, starting transfers between devices, send(): return lax.ppermute(a, 'wide', perm)  48.3 us
    pallas_call x1, Pallas kernels, fit(): pl.pallas_call(lambda *refs: fit_kernel([len(halves) for halves in sums],...  9.42 us
    dot_general x1, matrix products, dot(): return jnp.dot(a, b, preferred_element_type=F32)  5.11 us
  transfers between devices with their start and end apart: 24, of which 6 were waited for; matrix products, arithmetic and copies ran while one was open for 6% of the time, Pallas kernels for 39%

profile of v21, /device:TPU:0, one launch (start us, length us, event | category | flops | bytes accessed | tf_op | source)
XLA Modules:
  0.0 219.5 jit_solution(6399977052838555796)
XLA Ops:
  0.9 5.8 %collective-permute-start.1 = (bf16[64,14336]{1,0:T(8,128)(2,1)}, bf16[64,14336]{1,0:T(8,128)(2,1)}, u32[]{:S(2)}, u32[]{:S(2)}) collective-permute-start(bf16[64,14336]{1,0:T(8,128)(2,1)} %refs_1_.3), channel_id=1, source_target_pairs={{0,4},{2,6},{4,0},{6,2},{8,12},{10,14},{12,8},{14,10},{1,5},{3,7},... | collective-permute-start | bytes 5505032 | tf_op jit(solution)/shard_map/ppermute | solution.py:184
  6.7 1.5 collective-permute-start
  8.2 2.7 %constant_dynamic-slice_fusion.1 = (bf16[1024,1024]{1,0:T(8,128)(2,1)S(1)}, bf16[1024,1024]{1,0:T(8,128)(2,1)S(1)}) fusion(bf16[1024,2048]{1,0:T(8,128)(2,1)} %param.7, s32[]{:T(128)S(6)} %select_n.48, s32[]{:T(128)S(6)} %select_n.49), kind=kLoop, calls=%fused_computation.13 | loop fusion | bytes 8388616 | tf_op jit(solution)/shard_map/dynamic_slice | solution.py:205
  10.9 5.1 %fusion.9 = (bf16[512,2048]{1,0:T(8,128)(2,1)}, f32[512,2048]{1,0:T(8,128)}) fusion(bf16[512,1024]{1,0:T(8,128)(2,1)S(1)} %copy-done, bf16[1024,1024]{1,0:T(8,128)(2,1)S(1)} %get-tuple-element.138, bf16[1024,1024]{1,0:T(8,128)(2,1)S(1)} %get-tuple-element.137), kind=kOutput, calls=%fused_computation.16 | convolution fusion | flops 2156920832 | bytes 11534336 | tf_op jit(solution)/shard_map/dot_general | solution.py:16
  16.0 3.3 %collective-permute-start.6 = (bf16[512,2048]{1,0:T(8,128)(2,1)}, bf16[512,2048]{1,0:T(8,128)(2,1)}, u32[]{:S(2)}, u32[]{:S(2)}) collective-permute-start(bf16[512,2048]{1,0:T(8,128)(2,1)} %get-tuple-element.139), channel_id=1, source_target_pairs={{0,4},{2,6},{12,8},{14,10},{1,5},{3,7},{13,9},{15,11},{16,20},{18,... | collective-permute-start | bytes 6291464 | tf_op jit(solution)/shard_map/ppermute | solution.py:184
  19.5 28.0 %collective-permute-done.1.refs_2_ = bf16[64,14336]{1,0:T(8,128)(2,1)} collective-permute-done((bf16[64,14336]{1,0:T(8,128)(2,1)}, bf16[64,14336]{1,0:T(8,128)(2,1)}, u32[]{:S(2)}, u32[]{:S(2)}) %collective-permute-start.1) | collective-permute-done | bytes 1835040 | tf_op jit(solution)/shard_map/ppermute | solution.py:184
  49.0 3.4 %collective-permute-start.3 = (bf16[64,14336]{1,0:T(8,128)(2,1)}, bf16[64,14336]{1,0:T(8,128)(2,1)}, u32[]{:S(2)}, u32[]{:S(2)}) collective-permute-start(bf16[64,14336]{1,0:T(8,128)(2,1)} %collective-permute-done.1.refs_2_), channel_id=1, source_target_pairs={{0,2},{2,0},{12,14},{14,12},{1,3},{3,1},{13,15},{15,13},{16,18},{1... | collective-permute-start | bytes 5505032 | tf_op jit(solution)/shard_map/ppermute | solution.py:184
  52.4 1.3 collective-permute-start.4
  53.7 1.9 collective-permute-start.9
  55.6 1.5 copy-done.4
  57.1 16.6 %rotate.7.refs_9_ = f32[192,1792]{1,0:T(8,128)S(1)} custom-call(s32[1]{0:T(128)} %bitcast.11.refs_0_.refs_1_, bf16[64,14336]{1,0:T(8,128)(2,1)S(1)} %copy-done.4, bf16[64,14336]{1,0:T(8,128)(2,1)} %collective-permute-done.1.refs_2_, bf16[64,14336]{1,0:T(8,128)(2,1)} %collective-permute-done.refs_3_, bf16[14336,1792]{1,0:T(8,128)(2,1)} %refs_7_.7), custom_call_target="tpu_custom_call" | custom-call | flops 344064 | bytes 1376256 | tf_op jit(solution)/shard_map/rotate/pallas_call | solution.py:125
  73.7 17.2 %collective-permute-done.6 = bf16[512,2048]{1,0:T(8,128)(2,1)} collective-permute-done((bf16[512,2048]{1,0:T(8,128)(2,1)}, bf16[512,2048]{1,0:T(8,128)(2,1)}, u32[]{:S(2)}, u32[]{:S(2)}) %collective-permute-start.6) | collective-permute-done | bytes 2097184 | tf_op jit(solution)/shard_map/ppermute | solution.py:184
  91.0 1.6 add_convert_fusion.2
  92.6 2.0 collective-permute-done.4.refs_1_.refs_4_
  96.2 3.1 %collective-permute-start.8 = (bf16[64,14336]{1,0:T(8,128)(2,1)}, bf16[64,14336]{1,0:T(8,128)(2,1)S(1)}, u32[]{:S(2)}, u32[]{:S(2)}) collective-permute-start(bf16[64,14336]{1,0:T(8,128)(2,1)} %collective-permute-done.4.refs_1_.refs_4_), channel_id=1, source_target_pairs={{0,2},{2,0},{12,14},{14,12},{1,3},{3,1},{13,15},{15,13},{16,18},{1... | collective-permute-start | bytes 5505032 | tf_op jit(solution)/shard_map/ppermute | solution.py:184
  99.3 1.3 collective-permute-start.7
  100.6 6.4 %collective-permute-start.14 = (bf16[64,14336]{1,0:T(8,128)(2,1)}, bf16[64,14336]{1,0:T(8,128)(2,1)S(1)}, u32[]{:S(2)}, u32[]{:S(2)}) collective-permute-start(bf16[64,14336]{1,0:T(8,128)(2,1)} %collective-permute-done.refs_3_), channel_id=1, source_target_pairs={{0,4},{2,6},{12,8},{14,10},{1,5},{3,7},{13,9},{15,11},{16,20},{18,... | collective-permute-start | bytes 5505032 | tf_op jit(solution)/shard_map/ppermute | solution.py:184
  107.0 1.7 convert_add_fusion.1
  108.7 15.7 %rotate.8.refs_10_ = f32[128,1792]{1,0:T(8,128)S(1)} custom-call(s32[1]{0:T(128)} %bitcast.11.refs_0_.refs_1_, bf16[64,14336]{1,0:T(8,128)(2,1)} %collective-permute-done.4.refs_1_.refs_4_, bf16[64,14336]{1,0:T(8,128)(2,1)S(1)} %copy-done.3, bf16[64,14336]{1,0:T(8,128)(2,1)} %collective-permute-done.3.refs_3_.refs_6_, ...), custom_call_target="tpu_custom_call" | custom-call | flops 229376 | bytes 917504 | tf_op jit(solution)/shard_map/rotate/pallas_call | solution.py:125
  126.7 18.9 %rotate.9 = f32[320,1792]{1,0:T(8,128)S(1)} custom-call(s32[1]{0:T(128)} %bitcast.11.refs_0_.refs_1_, bf16[64,14336]{1,0:T(8,128)(2,1)S(1)} %copy-done.5, bf16[64,14336]{1,0:T(8,128)(2,1)} %collective-permute-done.1.refs_2_, bf16[64,14336]{1,0:T(8,128)(2,1)} %collective-permute-done.refs_3_, bf16[64,14336]{1,0:T(8,128)(2,1)} %collective-permute-done.4.refs_1_.refs_4_, ...), custom_call_target="tpu_custom_call" | custom-call | flops 573440 | bytes 2293760 | tf_op jit(solution)/shard_map/rotate/pallas_call | solution.py:125
  145.7 2.8 %collective-permute-start.12 = (bf16[64,5120]{1,0:T(8,128)(2,1)S(1)}, bf16[64,5120]{1,0:T(8,128)(2,1)S(1)}, u32[]{:S(2)}, u32[]{:S(2)}) collective-permute-start(bf16[64,5120]{1,0:T(8,128)(2,1)S(1)} %slice.35), channel_id=1, source_target_pairs={{0,2},{2,0},{12,14},{14,12},{1,3},{3,1},{13,15},{15,13},{16,18},{1... | collective-permute-start | bytes 1966088 | tf_op jit(solution)/shard_map/ppermute | solution.py:184
  151.0 10.1 %collective-permute-done.12.refs_5_ = bf16[64,5120]{1,0:T(8,128)(2,1)S(1)} collective-permute-done((bf16[64,5120]{1,0:T(8,128)(2,1)S(1)}, bf16[64,5120]{1,0:T(8,128)(2,1)S(1)}, u32[]{:S(2)}, u32[]{:S(2)}) %collective-permute-start.12) | collective-permute-done | bytes 655392 | tf_op jit(solution)/shard_map/ppermute | solution.py:184
  161.1 2.3 %collective-permute-start.15 = (bf16[64,4096]{1,0:T(8,128)(2,1)S(1)}, bf16[64,4096]{1,0:T(8,128)(2,1)S(1)}, u32[]{:S(2)}, u32[]{:S(2)}) collective-permute-start(bf16[64,4096]{1,0:T(8,128)(2,1)S(1)} %slice.36), channel_id=1, source_target_pairs={{0,2},{2,0},{12,14},{14,12},{1,3},{3,1},{13,15},{15,13},{16,18},{1... | collective-permute-start | bytes 1572872 | tf_op jit(solution)/shard_map/ppermute | solution.py:184
  163.4 12.1 %rotate.10.refs_8_ = f32[192,1792]{1,0:T(8,128)S(1)} custom-call(s32[1]{0:T(128)} %bitcast.11.refs_0_.refs_1_, bf16[64,14336]{1,0:T(8,128)(2,1)S(1)} %collective-permute-done.7.refs_1_, bf16[64,14336]{1,0:T(8,128)(2,1)S(1)} %collective-permute-done.5.refs_2_, bf16[64,14336]{1,0:T(8,128)(2,1)S(1)} %collective-permute-done.8.refs_3_, ...), custom_call_target="tpu_custom_call" | custom-call | flops 344064 | bytes 1376256 | tf_op jit(solution)/shard_map/rotate/pallas_call | solution.py:125
  175.6 1.3 collective-permute-start.19
  176.9 3.5 %collective-permute-start.20 = (bf16[64,3072]{1,0:T(8,128)(2,1)S(1)}, bf16[64,3072]{1,0:T(8,128)(2,1)S(1)}, u32[]{:S(2)}, u32[]{:S(2)}) collective-permute-start(bf16[64,3072]{1,0:T(8,128)(2,1)S(1)} %slice.38), channel_id=1, source_target_pairs={{0,2},{2,0},{12,14},{14,12},{1,3},{3,1},{13,15},{15,13},{16,18},{1... | collective-permute-start | bytes 1179656 | tf_op jit(solution)/shard_map/ppermute | solution.py:184
  180.5 9.8 %rotate.11.refs_8_ = f32[192,1792]{1,0:T(8,128)S(1)} custom-call(s32[1]{0:T(128)} %bitcast.11.refs_0_.refs_1_, bf16[64,14336]{1,0:T(8,128)(2,1)S(1)} %collective-permute-done.7.refs_1_, bf16[64,14336]{1,0:T(8,128)(2,1)S(1)} %collective-permute-done.5.refs_2_, bf16[64,14336]{1,0:T(8,128)(2,1)S(1)} %collective-permute-done.8.refs_3_, ...), custom_call_target="tpu_custom_call" | custom-call | flops 344064 | bytes 1376256 | tf_op jit(solution)/shard_map/rotate/pallas_call | solution.py:125
  190.5 3.6 %collective-permute-start.22 = (bf16[64,2048]{1,0:T(8,128)(2,1)S(1)}, bf16[64,2048]{1,0:T(8,128)(2,1)S(1)}, u32[]{:S(2)}, u32[]{:S(2)}) collective-permute-start(bf16[64,2048]{1,0:T(8,128)(2,1)S(1)} %slice.39), channel_id=1, source_target_pairs={{0,2},{2,0},{12,14},{14,12},{1,3},{3,1},{13,15},{15,13},{16,18},{1... | collective-permute-start | bytes 786440 | tf_op jit(solution)/shard_map/ppermute | solution.py:184
  194.1 7.5 %rotate.12.refs_8_ = f32[192,1792]{1,0:T(8,128)S(1)} custom-call(s32[1]{0:T(128)} %bitcast.11.refs_0_.refs_1_, bf16[64,14336]{1,0:T(8,128)(2,1)S(1)} %collective-permute-done.7.refs_1_, bf16[64,14336]{1,0:T(8,128)(2,1)S(1)} %collective-permute-done.5.refs_2_, bf16[64,14336]{1,0:T(8,128)(2,1)S(1)} %collective-permute-done.8.refs_3_, ...), custom_call_target="tpu_custom_call" | custom-call | flops 344064 | bytes 1376256 | tf_op jit(solution)/shard_map/rotate/pallas_call | solution.py:125
  201.6 5.2 %rotate.13.refs_4_ = f32[192,1792]{1,0:T(8,128)S(1)} custom-call(s32[1]{0:T(128)} %bitcast.11.refs_0_.refs_1_, bf16[64,14336]{1,0:T(8,128)(2,1)S(1)} %collective-permute-done.7.refs_1_, bf16[64,14336]{1,0:T(8,128)(2,1)S(1)} %collective-permute-done.5.refs_2_, bf16[64,14336]{1,0:T(8,128)(2,1)S(1)} %collective-permute-done.8.refs_3_, ...), custom_call_target="tpu_custom_call" | custom-call | flops 344064 | bytes 1376256 | tf_op jit(solution)/shard_map/rotate/pallas_call | solution.py:125
  207.2 2.8 %collective-permute-done.23.refs_5_ = f32[192,1792]{1,0:T(8,128)S(1)} collective-permute-done((f32[192,1792]{1,0:T(8,128)S(1)}, f32[192,1792]{1,0:T(8,128)S(1)}, u32[]{:S(2)}, u32[]{:S(2)}) %collective-permute-start.23) | collective-permute-done | bytes 1376288 | tf_op jit(solution)/shard_map/ppermute | solution.py:146
  210.0 9.4 %fit.1 = f32[1792,2048]{1,0:T(8,128)} custom-call(s32[8]{0:T(128)S(1)} %stack.44.refs_0_, s32[1]{0:T(128)} %bitcast.11.refs_0_.refs_1_, s32[2]{0:T(128)S(1)} %pad_add_fusion.refs_2_, bf16[320,1792]{1,0:T(8,128)(2,1)S(1)} %add_convert_fusion.refs_3_, f32[192,1792]{1,0:T(8,128)S(1)} %rotate.13.refs_4_, f32[192,1792]{1,0:T(8,128)S(1)} %collective-permute-done.23.refs_5_, ...), custom_call_target="tpu_custom_call" | custom-call | flops 3758096384 | bytes 24117248 | tf_op jit(solution)/shard_map/fit/pallas_call | solution.py:64
  (54 shorter events, 9.5 us)
Async XLA Ops:
  0.0 10.9 %copy-start = (bf16[512,1024]{1,0:T(8,128)(2,1)S(1)}, bf16[512,1024]{1,0:T(8,128)(2,1)}, u32[]{:S(2)}) copy-start(bf16[512,1024]{1,0:T(8,128)(2,1)} %param.5) | copy-start | bytes 3145732
  0.0 19.4 %collective-permute-start.2 = (bf16[64,14336]{1,0:T(8,128)(2,1)}, bf16[64,14336]{1,0:T(8,128)(2,1)S(1)}, u32[]{:S(2)}, u32[]{:S(2)}) collective-permute-start(bf16[64,14336]{1,0:T(8,128)(2,1)} %refs_1_.3), channel_id=1, source_target_pairs={{4,8},{6,10},{8,4},{10,6},{5,9},{7,11},{9,5},{11,7},{20,24},{22,26... | collective-permute-start | bytes 5505032 | tf_op jit(solution)/shard_map/ppermute | solution.py:184
  0.9 46.6 %collective-permute-start.1 = (bf16[64,14336]{1,0:T(8,128)(2,1)}, bf16[64,14336]{1,0:T(8,128)(2,1)}, u32[]{:S(2)}, u32[]{:S(2)}) collective-permute-start(bf16[64,14336]{1,0:T(8,128)(2,1)} %refs_1_.3), channel_id=1, source_target_pairs={{0,4},{2,6},{4,0},{6,2},{8,12},{10,14},{12,8},{14,10},{1,5},{3,7},... | collective-permute-start | bytes 5505032 | tf_op jit(solution)/shard_map/ppermute | solution.py:184
  6.7 41.5 %collective-permute-start = (bf16[64,14336]{1,0:T(8,128)(2,1)}, bf16[64,14336]{1,0:T(8,128)(2,1)}, u32[]{:S(2)}, u32[]{:S(2)}) collective-permute-start(bf16[64,14336]{1,0:T(8,128)(2,1)} %refs_1_.3), channel_id=1, source_target_pairs={{0,2},{2,0},{4,6},{6,4},{8,10},{10,8},{12,14},{14,12},{1,3},{3,1},... | collective-permute-start | bytes 5505032 | tf_op jit(solution)/shard_map/ppermute | solution.py:184
  16.0 75.0 %collective-permute-start.6 = (bf16[512,2048]{1,0:T(8,128)(2,1)}, bf16[512,2048]{1,0:T(8,128)(2,1)}, u32[]{:S(2)}, u32[]{:S(2)}) collective-permute-start(bf16[512,2048]{1,0:T(8,128)(2,1)} %get-tuple-element.139), channel_id=1, source_target_pairs={{0,4},{2,6},{12,8},{14,10},{1,5},{3,7},{13,9},{15,11},{16,20},{18,... | collective-permute-start | bytes 6291464 | tf_op jit(solution)/shard_map/ppermute | solution.py:184
  19.5 28.8 %copy-start.2 = (bf16[64,14336]{1,0:T(8,128)(2,1)}, bf16[64,14336]{1,0:T(8,128)(2,1)S(1)}, u32[]{:S(2)}) copy-start(bf16[64,14336]{1,0:T(8,128)(2,1)S(1)} %collective-permute-done.2.refs_2_.refs_5_) | copy-start | bytes 5505028
  48.2 44.4 %collective-permute-start.5 = (bf16[64,14336]{1,0:T(8,128)(2,1)}, bf16[64,14336]{1,0:T(8,128)(2,1)S(1)}, u32[]{:S(2)}, u32[]{:S(2)}) collective-permute-start(bf16[64,14336]{1,0:T(8,128)(2,1)} %collective-permute-done.1.refs_2_), channel_id=1, source_target_pairs={{4,8},{6,10},{8,4},{10,6},{5,9},{7,11},{9,5},{11,7},{20,24},{22,26... | collective-permute-start | bytes 5505032 | tf_op jit(solution)/shard_map/ppermute | solution.py:184
  49.0 43.6 %collective-permute-start.3 = (bf16[64,14336]{1,0:T(8,128)(2,1)}, bf16[64,14336]{1,0:T(8,128)(2,1)}, u32[]{:S(2)}, u32[]{:S(2)}) collective-permute-start(bf16[64,14336]{1,0:T(8,128)(2,1)} %collective-permute-done.1.refs_2_), channel_id=1, source_target_pairs={{0,2},{2,0},{12,14},{14,12},{1,3},{3,1},{13,15},{15,13},{16,18},{1... | collective-permute-start | bytes 5505032 | tf_op jit(solution)/shard_map/ppermute | solution.py:184
  52.4 42.2 %collective-permute-start.4 = (bf16[64,14336]{1,0:T(8,128)(2,1)}, bf16[64,14336]{1,0:T(8,128)(2,1)}, u32[]{:S(2)}, u32[]{:S(2)}) collective-permute-start(bf16[64,14336]{1,0:T(8,128)(2,1)} %copy-done.2), channel_id=1, source_target_pairs={{4,0},{6,2},{8,12},{10,14},{5,1},{7,3},{9,13},{11,15},{20,16},{22,... | collective-permute-start | bytes 5505032 | tf_op jit(solution)/shard_map/ppermute | solution.py:184
  53.7 41.6 %collective-permute-start.9 = (bf16[64,14336]{1,0:T(8,128)(2,1)}, bf16[64,14336]{1,0:T(8,128)(2,1)}, u32[]{:S(2)}, u32[]{:S(2)}) collective-permute-start(bf16[64,14336]{1,0:T(8,128)(2,1)} %copy-done.2), channel_id=1, source_target_pairs={{4,6},{6,4},{8,10},{10,8},{5,7},{7,5},{9,11},{11,9},{20,22},{22,20... | collective-permute-start | bytes 5505032 | tf_op jit(solution)/shard_map/ppermute | solution.py:184
  55.6 1.5 copy-start.4
  57.1 33.9 %copy-start.6 = (f32[512,2048]{1,0:T(8,128)S(1)}, f32[512,2048]{1,0:T(8,128)}, u32[]{:S(2)}) copy-start(f32[512,2048]{1,0:T(8,128)} %get-tuple-element.85) | copy-start | bytes 12582916
  94.6 29.9 %collective-permute-start.10 = (bf16[512,1024]{1,0:T(8,128)(2,1)S(1)}, bf16[512,1024]{1,0:T(8,128)(2,1)S(1)}, u32[]{:S(2)}, u32[]{:S(2)}) collective-permute-start(bf16[512,1024]{1,0:T(8,128)(2,1)S(1)} %add_convert_fusion.2), channel_id=1, source_target_pairs={{4,8},{6,10},{8,4},{10,6},{5,9},{7,11},{9,5},{11,7},{20,24},{22,26... | collective-permute-start | bytes 3145736 | tf_op jit(solution)/shard_map/ppermute | solution.py:184
  95.4 13.3 %copy-start.3 = (bf16[64,14336]{1,0:T(8,128)(2,1)S(1)}, bf16[64,14336]{1,0:T(8,128)(2,1)}, u32[]{:S(2)}) copy-start(bf16[64,14336]{1,0:T(8,128)(2,1)} %copy-done.2) | copy-start | bytes 5505028
  95.4 29.0 %collective-permute-start.11 = (bf16[64,5120]{1,0:T(8,128)(2,1)S(1)}, bf16[64,5120]{1,0:T(8,128)(2,1)S(1)}, u32[]{:S(2)}, u32[]{:S(2)}) collective-permute-start(bf16[64,5120]{1,0:T(8,128)(2,1)S(1)} %slice.34), channel_id=1, source_target_pairs={{4,6},{6,4},{8,10},{10,8},{5,7},{7,5},{9,11},{11,9},{20,22},{22,20... | collective-permute-start | bytes 1966088 | tf_op jit(solution)/shard_map/ppermute | solution.py:184
  96.2 49.4 %collective-permute-start.8 = (bf16[64,14336]{1,0:T(8,128)(2,1)}, bf16[64,14336]{1,0:T(8,128)(2,1)S(1)}, u32[]{:S(2)}, u32[]{:S(2)}) collective-permute-start(bf16[64,14336]{1,0:T(8,128)(2,1)} %collective-permute-done.4.refs_1_.refs_4_), channel_id=1, source_target_pairs={{0,2},{2,0},{12,14},{14,12},{1,3},{3,1},{13,15},{15,13},{16,18},{1... | collective-permute-start | bytes 5505032 | tf_op jit(solution)/shard_map/ppermute | solution.py:184
  99.3 46.4 %collective-permute-start.7 = (bf16[64,14336]{1,0:T(8,128)(2,1)S(1)}, bf16[64,14336]{1,0:T(8,128)(2,1)S(1)}, u32[]{:S(2)}, u32[]{:S(2)}) collective-permute-start(bf16[64,14336]{1,0:T(8,128)(2,1)S(1)} %collective-permute-done.5.refs_2_), channel_id=1, source_target_pairs={{4,0},{6,2},{8,12},{10,14},{5,1},{7,3},{9,13},{11,15},{20,16},{22,... | collective-permute-start | bytes 5505032 | tf_op jit(solution)/shard_map/ppermute | solution.py:184
  100.6 47.9 %collective-permute-start.14 = (bf16[64,14336]{1,0:T(8,128)(2,1)}, bf16[64,14336]{1,0:T(8,128)(2,1)S(1)}, u32[]{:S(2)}, u32[]{:S(2)}) collective-permute-start(bf16[64,14336]{1,0:T(8,128)(2,1)} %collective-permute-done.refs_3_), channel_id=1, source_target_pairs={{0,4},{2,6},{12,8},{14,10},{1,5},{3,7},{13,9},{15,11},{16,20},{18,... | collective-permute-start | bytes 5505032 | tf_op jit(solution)/shard_map/ppermute | solution.py:184
  125.0 1.7 copy-start.5
  125.0 23.5 %collective-permute-start.13 = (bf16[512,1024]{1,0:T(8,128)(2,1)S(1)}, bf16[512,1024]{1,0:T(8,128)(2,1)S(1)}, u32[]{:S(2)}, u32[]{:S(2)}) collective-permute-start(bf16[512,1024]{1,0:T(8,128)(2,1)S(1)} %get-tuple-element.135), channel_id=1, source_target_pairs={{4,6},{6,4},{8,10},{10,8},{5,7},{7,5},{9,11},{11,9},{20,22},{22,20... | collective-permute-start | bytes 3145736 | tf_op jit(solution)/shard_map/ppermute | solution.py:184
  126.0 49.5 %collective-permute-start.16 = (bf16[64,9216]{1,0:T(8,128)(2,1)S(1)}, bf16[64,9216]{1,0:T(8,128)(2,1)S(1)}, u32[]{:S(2)}, u32[]{:S(2)}) collective-permute-start(bf16[64,9216]{1,0:T(8,128)(2,1)S(1)} %slice.37), channel_id=1, source_target_pairs={{4,6},{6,4},{8,10},{10,8},{5,7},{7,5},{9,11},{11,9},{20,22},{22,20... | collective-permute-start | bytes 3538952 | tf_op jit(solution)/shard_map/ppermute | solution.py:184
  145.7 15.3 %collective-permute-start.12 = (bf16[64,5120]{1,0:T(8,128)(2,1)S(1)}, bf16[64,5120]{1,0:T(8,128)(2,1)S(1)}, u32[]{:S(2)}, u32[]{:S(2)}) collective-permute-start(bf16[64,5120]{1,0:T(8,128)(2,1)S(1)} %slice.35), channel_id=1, source_target_pairs={{0,2},{2,0},{12,14},{14,12},{1,3},{3,1},{13,15},{15,13},{16,18},{1... | collective-permute-start | bytes 1966088 | tf_op jit(solution)/shard_map/ppermute | solution.py:184
  148.9 26.6 %collective-permute-start.18 = (bf16[512,1024]{1,0:T(8,128)(2,1)S(1)}, bf16[512,1024]{1,0:T(8,128)(2,1)S(1)}, u32[]{:S(2)}, u32[]{:S(2)}) collective-permute-start(bf16[512,1024]{1,0:T(8,128)(2,1)S(1)} %add_convert_fusion.1), channel_id=1, source_target_pairs={{4,0},{6,2},{8,12},{10,14},{5,1},{7,3},{9,13},{11,15},{20,16},{22,... | collective-permute-start | bytes 3145736 | tf_op jit(solution)/shard_map/ppermute | solution.py:184
  150.2 25.3 %collective-permute-start.17 = (bf16[512,1024]{1,0:T(8,128)(2,1)S(1)}, bf16[512,1024]{1,0:T(8,128)(2,1)S(1)}, u32[]{:S(2)}, u32[]{:S(2)}) collective-permute-start(bf16[512,1024]{1,0:T(8,128)(2,1)S(1)} %add_convert_fusion.1), channel_id=1, source_target_pairs={{4,8},{6,10},{8,4},{10,6},{5,9},{7,11},{9,5},{11,7},{20,24},{22,26... | collective-permute-start | bytes 3145736 | tf_op jit(solution)/shard_map/ppermute | solution.py:184
  161.1 14.4 %collective-permute-start.15 = (bf16[64,4096]{1,0:T(8,128)(2,1)S(1)}, bf16[64,4096]{1,0:T(8,128)(2,1)S(1)}, u32[]{:S(2)}, u32[]{:S(2)}) collective-permute-start(bf16[64,4096]{1,0:T(8,128)(2,1)S(1)} %slice.36), channel_id=1, source_target_pairs={{0,2},{2,0},{12,14},{14,12},{1,3},{3,1},{13,15},{15,13},{16,18},{1... | collective-permute-start | bytes 1572872 | tf_op jit(solution)/shard_map/ppermute | solution.py:184
  175.5 14.9 %collective-permute-start.21 = (f32[320,1792]{1,0:T(8,128)S(1)}, f32[320,1792]{1,0:T(8,128)S(1)}, u32[]{:S(2)}, u32[]{:S(2)}) collective-permute-start(f32[320,1792]{1,0:T(8,128)S(1)} %rotate.9), channel_id=1, source_target_pairs={{0,1},{1,0},{2,3},{3,2},{4,5},{5,4},{6,7},{7,6},{8,9},{9,8},{10,11... | collective-permute-start | bytes 6881288 | tf_op jit(solution)/shard_map/ppermute | solution.py:146
  175.6 31.2 %collective-permute-start.19 = (bf16[512,1024]{1,0:T(8,128)(2,1)S(1)}, bf16[512,1024]{1,0:T(8,128)(2,1)S(1)}, u32[]{:S(2)}, u32[]{:S(2)}) collective-permute-start(bf16[512,1024]{1,0:T(8,128)(2,1)S(1)} %collective-permute-done.17.refs_8_), channel_id=1, source_target_pairs={{4,0},{6,2},{8,12},{10,14},{5,1},{7,3},{9,13},{11,15},{20,16},{22,... | collective-permute-start | bytes 3145736 | tf_op jit(solution)/shard_map/ppermute | solution.py:184
  176.9 13.5 %collective-permute-start.20 = (bf16[64,3072]{1,0:T(8,128)(2,1)S(1)}, bf16[64,3072]{1,0:T(8,128)(2,1)S(1)}, u32[]{:S(2)}, u32[]{:S(2)}) collective-permute-start(bf16[64,3072]{1,0:T(8,128)(2,1)S(1)} %slice.38), channel_id=1, source_target_pairs={{0,2},{2,0},{12,14},{14,12},{1,3},{3,1},{13,15},{15,13},{16,18},{1... | collective-permute-start | bytes 1179656 | tf_op jit(solution)/shard_map/ppermute | solution.py:184
  190.5 11.1 %collective-permute-start.22 = (bf16[64,2048]{1,0:T(8,128)(2,1)S(1)}, bf16[64,2048]{1,0:T(8,128)(2,1)S(1)}, u32[]{:S(2)}, u32[]{:S(2)}) collective-permute-start(bf16[64,2048]{1,0:T(8,128)(2,1)S(1)} %slice.39), channel_id=1, source_target_pairs={{0,2},{2,0},{12,14},{14,12},{1,3},{3,1},{13,15},{15,13},{16,18},{1... | collective-permute-start | bytes 786440 | tf_op jit(solution)/shard_map/ppermute | solution.py:184
  206.8 3.2 %collective-permute-start.23 = (f32[192,1792]{1,0:T(8,128)S(1)}, f32[192,1792]{1,0:T(8,128)S(1)}, u32[]{:S(2)}, u32[]{:S(2)}) collective-permute-start(f32[192,1792]{1,0:T(8,128)S(1)} %rotate.13.refs_4_), channel_id=1, source_target_pairs={{0,1},{1,0},{2,3},{3,2},{4,5},{5,4},{6,7},{7,6},{8,9},{9,8},{10,11... | collective-permute-start | bytes 4128776 | tf_op jit(solution)/shard_map/ppermute | solution.py:146
  210.0 9.4 %copy-start.1 = (bf16[512,1024]{1,0:T(8,128)(2,1)S(1)}, bf16[512,1024]{1,0:T(8,128)(2,1)}, u32[]{:S(2)}) copy-start(bf16[512,1024]{1,0:T(8,128)(2,1)} %param.5) | copy-start | bytes 3145732

commit v22 on v21

--- a/solution.py
+++ b/solution.py
@@ -7,8 +7,8 @@
 
 EX = 2
 LINE, PAIR = 4, 2
-DEEP = 512
-VMEM = 16 << 20
+DEEP = 2048
+VMEM = 32 << 20
 BF16, F32 = jnp.bfloat16, jnp.float32
 
 

time: 221 us -> 214 us (0.968)
  Pallas kernels: 95.3 us -> 70.5 us
  waiting for transfers between devices: 60.9 us -> 80.4 us
    pallas_call x7, Pallas kernels: 85.9 us -> 61 us  [rotate(): pl.pallas_call(lambda *refs: rotate_kernel([len(block) for block in block...]
    ppermute x22, waiting for transfers between devices: 58.1 us -> 77.5 us  [send(): return lax.ppermute(a, 'wide', perm)]
  transfers between devices with their start and end apart: 24 -> 24, of which waited for: 6 -> 11; matrix products, arithmetic and copies ran while one was open for 6% -> 6% of each run, Pallas kernels for 39% -> 29%
where the time goes in v22:
time: 214 us
  waiting for transfers between devices  80.4 us (38%)
  Pallas kernels  70.5 us (33%)
  starting transfers between devices  48.1 us (22%)
  matrix products  5.11 us (2%)
  other arithmetic  4.59 us (2%)
  local copies, waits for them, and re-layouts  4.52 us (2%)
    ppermute x22, waiting for transfers between devices, send(): return lax.ppermute(a, 'wide', perm)  77.5 us
    pallas_call x7, Pallas kernels, rotate(): pl.pallas_call(lambda *refs: rotate_kernel([len(block) for block in block...  61 us
    ppermute x22, starting transfers between devices, send(): return lax.ppermute(a, 'wide', perm)  48 us
    pallas_call x1, Pallas kernels, fit(): pl.pallas_call(lambda *refs: fit_kernel([len(halves) for halves in sums],...  9.42 us
    dot_general x1, matrix products, dot(): return jnp.dot(a, b, preferred_element_type=F32)  5.11 us
  transfers between devices with their start and end apart: 24, of which 11 were waited for; matrix products, arithmetic and copies ran while one was open for 6% of the time, Pallas kernels for 29%

profile of v22, /device:TPU:0, one launch (start us, length us, event | category | flops | bytes accessed | tf_op | source)
XLA Modules:
  0.0 213.6 jit_solution(7015691585038988848)
XLA Ops:
  0.9 5.8 %collective-permute-start.1 = (bf16[64,14336]{1,0:T(8,128)(2,1)}, bf16[64,14336]{1,0:T(8,128)(2,1)}, u32[]{:S(2)}, u32[]{:S(2)}) collective-permute-start(bf16[64,14336]{1,0:T(8,128)(2,1)} %refs_1_.3), channel_id=1, source_target_pairs={{0,4},{2,6},{4,0},{6,2},{8,12},{10,14},{12,8},{14,10},{1,5},{3,7},... | collective-permute-start | bytes 5505032 | tf_op jit(solution)/shard_map/ppermute | solution.py:184
  8.2 2.7 %constant_dynamic-slice_fusion.1 = (bf16[1024,1024]{1,0:T(8,128)(2,1)S(1)}, bf16[1024,1024]{1,0:T(8,128)(2,1)S(1)}) fusion(bf16[1024,2048]{1,0:T(8,128)(2,1)} %param.7, s32[]{:T(128)S(6)} %select_n.48, s32[]{:T(128)S(6)} %select_n.49), kind=kLoop, calls=%fused_computation.13 | loop fusion | bytes 8388616 | tf_op jit(solution)/shard_map/dynamic_slice | solution.py:205
  10.9 5.1 %fusion.9 = (bf16[512,2048]{1,0:T(8,128)(2,1)}, f32[512,2048]{1,0:T(8,128)}) fusion(bf16[512,1024]{1,0:T(8,128)(2,1)S(1)} %copy-done, bf16[1024,1024]{1,0:T(8,128)(2,1)S(1)} %get-tuple-element.138, bf16[1024,1024]{1,0:T(8,128)(2,1)S(1)} %get-tuple-element.137), kind=kOutput, calls=%fused_computation.16 | convolution fusion | flops 2156920832 | bytes 11534336 | tf_op jit(solution)/shard_map/dot_general | solution.py:16
  16.0 3.3 %collective-permute-start.6 = (bf16[512,2048]{1,0:T(8,128)(2,1)}, bf16[512,2048]{1,0:T(8,128)(2,1)}, u32[]{:S(2)}, u32[]{:S(2)}) collective-permute-start(bf16[512,2048]{1,0:T(8,128)(2,1)} %get-tuple-element.139), channel_id=1, source_target_pairs={{0,4},{2,6},{12,8},{14,10},{1,5},{3,7},{13,9},{15,11},{16,20},{18,... | collective-permute-start | bytes 6291464 | tf_op jit(solution)/shard_map/ppermute | solution.py:184
  19.5 28.0 %collective-permute-done.1.refs_2_ = bf16[64,14336]{1,0:T(8,128)(2,1)} collective-permute-done((bf16[64,14336]{1,0:T(8,128)(2,1)}, bf16[64,14336]{1,0:T(8,128)(2,1)}, u32[]{:S(2)}, u32[]{:S(2)}) %collective-permute-start.1) | collective-permute-done | bytes 1835040 | tf_op jit(solution)/shard_map/ppermute | solution.py:184
  49.0 3.4 %collective-permute-start.3 = (bf16[64,14336]{1,0:T(8,128)(2,1)}, bf16[64,14336]{1,0:T(8,128)(2,1)}, u32[]{:S(2)}, u32[]{:S(2)}) collective-permute-start(bf16[64,14336]{1,0:T(8,128)(2,1)} %collective-permute-done.1.refs_2_), channel_id=1, source_target_pairs={{0,2},{2,0},{12,14},{14,12},{1,3},{3,1},{13,15},{15,13},{16,18},{1... | collective-permute-start | bytes 5505032 | tf_op jit(solution)/shard_map/ppermute | solution.py:184
  53.7 1.9 collective-permute-start.9
  57.1 10.3 %rotate.7.refs_9_ = f32[192,1792]{1,0:T(8,128)S(1)} custom-call(s32[1]{0:T(128)} %bitcast.11.refs_0_.refs_1_, bf16[64,14336]{1,0:T(8,128)(2,1)S(1)} %copy-done.4, bf16[64,14336]{1,0:T(8,128)(2,1)} %collective-permute-done.1.refs_2_, bf16[64,14336]{1,0:T(8,128)(2,1)} %collective-permute-done.refs_3_, bf16[14336,1792]{1,0:T(8,128)(2,1)} %refs_7_.7), custom_call_target="tpu_custom_call" | custom-call | flops 344064 | bytes 1376256 | tf_op jit(solution)/shard_map/rotate/pallas_call | solution.py:125
  67.4 23.5 %collective-permute-done.6 = bf16[512,2048]{1,0:T(8,128)(2,1)} collective-permute-done((bf16[512,2048]{1,0:T(8,128)(2,1)}, bf16[512,2048]{1,0:T(8,128)(2,1)}, u32[]{:S(2)}, u32[]{:S(2)}) %collective-permute-start.6) | collective-permute-done | bytes 2097184 | tf_op jit(solution)/shard_map/ppermute | solution.py:184
  91.0 1.6 add_convert_fusion.2
  92.6 2.0 collective-permute-done.4.refs_1_.refs_4_
  96.2 3.1 %collective-permute-start.8 = (bf16[64,14336]{1,0:T(8,128)(2,1)}, bf16[64,14336]{1,0:T(8,128)(2,1)S(1)}, u32[]{:S(2)}, u32[]{:S(2)}) collective-permute-start(bf16[64,14336]{1,0:T(8,128)(2,1)} %collective-permute-done.4.refs_1_.refs_4_), channel_id=1, source_target_pairs={{0,2},{2,0},{12,14},{14,12},{1,3},{3,1},{13,15},{15,13},{16,18},{1... | collective-permute-start | bytes 5505032 | tf_op jit(solution)/shard_map/ppermute | solution.py:184
  100.6 6.4 %collective-permute-start.14 = (bf16[64,14336]{1,0:T(8,128)(2,1)}, bf16[64,14336]{1,0:T(8,128)(2,1)S(1)}, u32[]{:S(2)}, u32[]{:S(2)}) collective-permute-start(bf16[64,14336]{1,0:T(8,128)(2,1)} %collective-permute-done.refs_3_), channel_id=1, source_target_pairs={{0,4},{2,6},{12,8},{14,10},{1,5},{3,7},{13,9},{15,11},{16,20},{18,... | collective-permute-start | bytes 5505032 | tf_op jit(solution)/shard_map/ppermute | solution.py:184
  107.0 1.7 convert_add_fusion.1
  108.7 9.3 %rotate.8.refs_10_ = f32[128,1792]{1,0:T(8,128)S(1)} custom-call(s32[1]{0:T(128)} %bitcast.11.refs_0_.refs_1_, bf16[64,14336]{1,0:T(8,128)(2,1)} %collective-permute-done.4.refs_1_.refs_4_, bf16[64,14336]{1,0:T(8,128)(2,1)S(1)} %copy-done.3, bf16[64,14336]{1,0:T(8,128)(2,1)} %collective-permute-done.3.refs_3_.refs_6_, ...), custom_call_target="tpu_custom_call" | custom-call | flops 229376 | bytes 917504 | tf_op jit(solution)/shard_map/rotate/pallas_call | solution.py:125
  120.3 15.3 %rotate.9 = f32[320,1792]{1,0:T(8,128)S(1)} custom-call(s32[1]{0:T(128)} %bitcast.11.refs_0_.refs_1_, bf16[64,14336]{1,0:T(8,128)(2,1)S(1)} %copy-done.5, bf16[64,14336]{1,0:T(8,128)(2,1)} %collective-permute-done.1.refs_2_, bf16[64,14336]{1,0:T(8,128)(2,1)} %collective-permute-done.refs_3_, bf16[64,14336]{1,0:T(8,128)(2,1)} %collective-permute-done.4.refs_1_.refs_4_, ...), custom_call_target="tpu_custom_call" | custom-call | flops 573440 | bytes 2293760 | tf_op jit(solution)/shard_map/rotate/pallas_call | solution.py:125
  135.6 1.7 collective-permute-done.8.refs_3_
  137.4 4.7 %collective-permute-done.7.refs_1_ = bf16[64,14336]{1,0:T(8,128)(2,1)S(1)} collective-permute-done((bf16[64,14336]{1,0:T(8,128)(2,1)S(1)}, bf16[64,14336]{1,0:T(8,128)(2,1)S(1)}, u32[]{:S(2)}, u32[]{:S(2)}) %collective-permute-start.7) | collective-permute-done | bytes 1835040 | tf_op jit(solution)/shard_map/ppermute | solution.py:184
  142.1 2.3 %collective-permute-start.12 = (bf16[64,4096]{1,0:T(8,128)(2,1)S(1)}, bf16[64,4096]{1,0:T(8,128)(2,1)S(1)}, u32[]{:S(2)}, u32[]{:S(2)}) collective-permute-start(bf16[64,4096]{1,0:T(8,128)(2,1)S(1)} %slice.35), channel_id=1, source_target_pairs={{0,2},{2,0},{12,14},{14,12},{1,3},{3,1},{13,15},{15,13},{16,18},{1... | collective-permute-start | bytes 1572872 | tf_op jit(solution)/shard_map/ppermute | solution.py:184
  146.9 7.4 %collective-permute-done.12.refs_5_ = bf16[64,4096]{1,0:T(8,128)(2,1)S(1)} collective-permute-done((bf16[64,4096]{1,0:T(8,128)(2,1)S(1)}, bf16[64,4096]{1,0:T(8,128)(2,1)S(1)}, u32[]{:S(2)}, u32[]{:S(2)}) %collective-permute-start.12) | collective-permute-done | bytes 524320 | tf_op jit(solution)/shard_map/ppermute | solution.py:184
  154.3 2.4 %collective-permute-start.15 = (bf16[64,4096]{1,0:T(8,128)(2,1)S(1)}, bf16[64,4096]{1,0:T(8,128)(2,1)S(1)}, u32[]{:S(2)}, u32[]{:S(2)}) collective-permute-start(bf16[64,4096]{1,0:T(8,128)(2,1)S(1)} %slice.36), channel_id=1, source_target_pairs={{0,2},{2,0},{12,14},{14,12},{1,3},{3,1},{13,15},{15,13},{16,18},{1... | collective-permute-start | bytes 1572872 | tf_op jit(solution)/shard_map/ppermute | solution.py:184
  156.7 7.1 %rotate.10.refs_8_ = f32[192,1792]{1,0:T(8,128)S(1)} custom-call(s32[1]{0:T(128)} %bitcast.11.refs_0_.refs_1_, bf16[64,14336]{1,0:T(8,128)(2,1)S(1)} %collective-permute-done.7.refs_1_, bf16[64,14336]{1,0:T(8,128)(2,1)S(1)} %collective-permute-done.5.refs_2_, bf16[64,14336]{1,0:T(8,128)(2,1)S(1)} %collective-permute-done.8.refs_3_, ...), custom_call_target="tpu_custom_call" | custom-call | flops 344064 | bytes 1376256 | tf_op jit(solution)/shard_map/rotate/pallas_call | solution.py:125
  163.8 1.7 collective-permute-done.15.refs_5_
  165.6 2.3 %collective-permute-done.18 = bf16[512,1024]{1,0:T(8,128)(2,1)S(1)} collective-permute-done((bf16[512,1024]{1,0:T(8,128)(2,1)S(1)}, bf16[512,1024]{1,0:T(8,128)(2,1)S(1)}, u32[]{:S(2)}, u32[]{:S(2)}) %collective-permute-start.18) | collective-permute-done | bytes 1048608 | tf_op jit(solution)/shard_map/ppermute | solution.py:184
  169.2 3.6 %collective-permute-start.20 = (bf16[64,4096]{1,0:T(8,128)(2,1)S(1)}, bf16[64,4096]{1,0:T(8,128)(2,1)S(1)}, u32[]{:S(2)}, u32[]{:S(2)}) collective-permute-start(bf16[64,4096]{1,0:T(8,128)(2,1)S(1)} %slice.38), channel_id=1, source_target_pairs={{0,2},{2,0},{12,14},{14,12},{1,3},{3,1},{13,15},{15,13},{16,18},{1... | collective-permute-start | bytes 1572872 | tf_op jit(solution)/shard_map/ppermute | solution.py:184
  172.8 7.1 %rotate.11.refs_8_ = f32[192,1792]{1,0:T(8,128)S(1)} custom-call(s32[1]{0:T(128)} %bitcast.11.refs_0_.refs_1_, bf16[64,14336]{1,0:T(8,128)(2,1)S(1)} %collective-permute-done.7.refs_1_, bf16[64,14336]{1,0:T(8,128)(2,1)S(1)} %collective-permute-done.5.refs_2_, bf16[64,14336]{1,0:T(8,128)(2,1)S(1)} %collective-permute-done.8.refs_3_, ...), custom_call_target="tpu_custom_call" | custom-call | flops 344064 | bytes 1376256 | tf_op jit(solution)/shard_map/rotate/pallas_call | solution.py:125
  180.1 5.3 %collective-permute-done.20.refs_5_ = bf16[64,4096]{1,0:T(8,128)(2,1)S(1)} collective-permute-done((bf16[64,4096]{1,0:T(8,128)(2,1)S(1)}, bf16[64,4096]{1,0:T(8,128)(2,1)S(1)}, u32[]{:S(2)}, u32[]{:S(2)}) %collective-permute-start.20) | collective-permute-done | bytes 524320 | tf_op jit(solution)/shard_map/ppermute | solution.py:184
  185.4 3.6 %collective-permute-start.22 = (bf16[64,2048]{1,0:T(8,128)(2,1)S(1)}, bf16[64,2048]{1,0:T(8,128)(2,1)S(1)}, u32[]{:S(2)}, u32[]{:S(2)}) collective-permute-start(bf16[64,2048]{1,0:T(8,128)(2,1)S(1)} %slice.39), channel_id=1, source_target_pairs={{0,2},{2,0},{12,14},{14,12},{1,3},{3,1},{13,15},{15,13},{16,18},{1... | collective-permute-start | bytes 786440 | tf_op jit(solution)/shard_map/ppermute | solution.py:184
  189.1 7.1 %rotate.12.refs_8_ = f32[192,1792]{1,0:T(8,128)S(1)} custom-call(s32[1]{0:T(128)} %bitcast.11.refs_0_.refs_1_, bf16[64,14336]{1,0:T(8,128)(2,1)S(1)} %collective-permute-done.7.refs_1_, bf16[64,14336]{1,0:T(8,128)(2,1)S(1)} %collective-permute-done.5.refs_2_, bf16[64,14336]{1,0:T(8,128)(2,1)S(1)} %collective-permute-done.8.refs_3_, ...), custom_call_target="tpu_custom_call" | custom-call | flops 344064 | bytes 1376256 | tf_op jit(solution)/shard_map/rotate/pallas_call | solution.py:125
  196.2 4.8 %rotate.13.refs_4_ = f32[192,1792]{1,0:T(8,128)S(1)} custom-call(s32[1]{0:T(128)} %bitcast.11.refs_0_.refs_1_, bf16[64,14336]{1,0:T(8,128)(2,1)S(1)} %collective-permute-done.7.refs_1_, bf16[64,14336]{1,0:T(8,128)(2,1)S(1)} %collective-permute-done.5.refs_2_, bf16[64,14336]{1,0:T(8,128)(2,1)S(1)} %collective-permute-done.8.refs_3_, ...), custom_call_target="tpu_custom_call" | custom-call | flops 344064 | bytes 1376256 | tf_op jit(solution)/shard_map/rotate/pallas_call | solution.py:125
  201.3 2.8 %collective-permute-done.23.refs_5_ = f32[192,1792]{1,0:T(8,128)S(1)} collective-permute-done((f32[192,1792]{1,0:T(8,128)S(1)}, f32[192,1792]{1,0:T(8,128)S(1)}, u32[]{:S(2)}, u32[]{:S(2)}) %collective-permute-start.23) | collective-permute-done | bytes 1376288 | tf_op jit(solution)/shard_map/ppermute | solution.py:146
  204.2 9.4 %fit.1 = f32[1792,2048]{1,0:T(8,128)} custom-call(s32[8]{0:T(128)S(1)} %stack.44.refs_0_, s32[1]{0:T(128)} %bitcast.11.refs_0_.refs_1_, s32[2]{0:T(128)S(1)} %pad_add_fusion.refs_2_, bf16[320,1792]{1,0:T(8,128)(2,1)S(1)} %add_convert_fusion.refs_3_, f32[192,1792]{1,0:T(8,128)S(1)} %rotate.13.refs_4_, f32[192,1792]{1,0:T(8,128)S(1)} %collective-permute-done.23.refs_5_, ...), custom_call_target="tpu_custom_call" | custom-call | flops 3758096384 | bytes 24117248 | tf_op jit(solution)/shard_map/fit/pallas_call | solution.py:64
  (54 shorter events, 16.2 us)
Async XLA Ops:
  0.0 10.9 %copy-start = (bf16[512,1024]{1,0:T(8,128)(2,1)S(1)}, bf16[512,1024]{1,0:T(8,128)(2,1)}, u32[]{:S(2)}) copy-start(bf16[512,1024]{1,0:T(8,128)(2,1)} %param.5) | copy-start | bytes 3145732
  0.0 19.4 %collective-permute-start.2 = (bf16[64,14336]{1,0:T(8,128)(2,1)}, bf16[64,14336]{1,0:T(8,128)(2,1)S(1)}, u32[]{:S(2)}, u32[]{:S(2)}) collective-permute-start(bf16[64,14336]{1,0:T(8,128)(2,1)} %refs_1_.3), channel_id=1, source_target_pairs={{4,8},{6,10},{8,4},{10,6},{5,9},{7,11},{9,5},{11,7},{20,24},{22,26... | collective-permute-start | bytes 5505032 | tf_op jit(solution)/shard_map/ppermute | solution.py:184
  0.9 46.6 %collective-permute-start.1 = (bf16[64,14336]{1,0:T(8,128)(2,1)}, bf16[64,14336]{1,0:T(8,128)(2,1)}, u32[]{:S(2)}, u32[]{:S(2)}) collective-permute-start(bf16[64,14336]{1,0:T(8,128)(2,1)} %refs_1_.3), channel_id=1, source_target_pairs={{0,4},{2,6},{4,0},{6,2},{8,12},{10,14},{12,8},{14,10},{1,5},{3,7},... | collective-permute-start | bytes 5505032 | tf_op jit(solution)/shard_map/ppermute | solution.py:184
  6.7 41.5 %collective-permute-start = (bf16[64,14336]{1,0:T(8,128)(2,1)}, bf16[64,14336]{1,0:T(8,128)(2,1)}, u32[]{:S(2)}, u32[]{:S(2)}) collective-permute-start(bf16[64,14336]{1,0:T(8,128)(2,1)} %refs_1_.3), channel_id=1, source_target_pairs={{0,2},{2,0},{4,6},{6,4},{8,10},{10,8},{12,14},{14,12},{1,3},{3,1},... | collective-permute-start | bytes 5505032 | tf_op jit(solution)/shard_map/ppermute | solution.py:184
  16.0 75.0 %collective-permute-start.6 = (bf16[512,2048]{1,0:T(8,128)(2,1)}, bf16[512,2048]{1,0:T(8,128)(2,1)}, u32[]{:S(2)}, u32[]{:S(2)}) collective-permute-start(bf16[512,2048]{1,0:T(8,128)(2,1)} %get-tuple-element.139), channel_id=1, source_target_pairs={{0,4},{2,6},{12,8},{14,10},{1,5},{3,7},{13,9},{15,11},{16,20},{18,... | collective-permute-start | bytes 6291464 | tf_op jit(solution)/shard_map/ppermute | solution.py:184
  19.5 28.8 %copy-start.2 = (bf16[64,14336]{1,0:T(8,128)(2,1)}, bf16[64,14336]{1,0:T(8,128)(2,1)S(1)}, u32[]{:S(2)}) copy-start(bf16[64,14336]{1,0:T(8,128)(2,1)S(1)} %collective-permute-done.2.refs_2_.refs_5_) | copy-start | bytes 5505028
  48.2 44.3 %collective-permute-start.5 = (bf16[64,14336]{1,0:T(8,128)(2,1)}, bf16[64,14336]{1,0:T(8,128)(2,1)S(1)}, u32[]{:S(2)}, u32[]{:S(2)}) collective-permute-start(bf16[64,14336]{1,0:T(8,128)(2,1)} %collective-permute-done.1.refs_2_), channel_id=1, source_target_pairs={{4,8},{6,10},{8,4},{10,6},{5,9},{7,11},{9,5},{11,7},{20,24},{22,26... | collective-permute-start | bytes 5505032 | tf_op jit(solution)/shard_map/ppermute | solution.py:184
  49.0 43.6 %collective-permute-start.3 = (bf16[64,14336]{1,0:T(8,128)(2,1)}, bf16[64,14336]{1,0:T(8,128)(2,1)}, u32[]{:S(2)}, u32[]{:S(2)}) collective-permute-start(bf16[64,14336]{1,0:T(8,128)(2,1)} %collective-permute-done.1.refs_2_), channel_id=1, source_target_pairs={{0,2},{2,0},{12,14},{14,12},{1,3},{3,1},{13,15},{15,13},{16,18},{1... | collective-permute-start | bytes 5505032 | tf_op jit(solution)/shard_map/ppermute | solution.py:184
  52.4 42.2 %collective-permute-start.4 = (bf16[64,14336]{1,0:T(8,128)(2,1)}, bf16[64,14336]{1,0:T(8,128)(2,1)}, u32[]{:S(2)}, u32[]{:S(2)}) collective-permute-start(bf16[64,14336]{1,0:T(8,128)(2,1)} %copy-done.2), channel_id=1, source_target_pairs={{4,0},{6,2},{8,12},{10,14},{5,1},{7,3},{9,13},{11,15},{20,16},{22,... | collective-permute-start | bytes 5505032 | tf_op jit(solution)/shard_map/ppermute | solution.py:184
  53.7 41.6 %collective-permute-start.9 = (bf16[64,14336]{1,0:T(8,128)(2,1)}, bf16[64,14336]{1,0:T(8,128)(2,1)}, u32[]{:S(2)}, u32[]{:S(2)}) collective-permute-start(bf16[64,14336]{1,0:T(8,128)(2,1)} %copy-done.2), channel_id=1, source_target_pairs={{4,6},{6,4},{8,10},{10,8},{5,7},{7,5},{9,11},{11,9},{20,22},{22,20... | collective-permute-start | bytes 5505032 | tf_op jit(solution)/shard_map/ppermute | solution.py:184
  55.6 1.5 copy-start.4
  57.1 33.9 %copy-start.6 = (f32[512,2048]{1,0:T(8,128)S(1)}, f32[512,2048]{1,0:T(8,128)}, u32[]{:S(2)}) copy-start(f32[512,2048]{1,0:T(8,128)} %get-tuple-element.85) | copy-start | bytes 12582916
  94.6 23.4 %collective-permute-start.10 = (bf16[512,1024]{1,0:T(8,128)(2,1)S(1)}, bf16[512,1024]{1,0:T(8,128)(2,1)S(1)}, u32[]{:S(2)}, u32[]{:S(2)}) collective-permute-start(bf16[512,1024]{1,0:T(8,128)(2,1)S(1)} %add_convert_fusion.2), channel_id=1, source_target_pairs={{4,8},{6,10},{8,4},{10,6},{5,9},{7,11},{9,5},{11,7},{20,24},{22,26... | collective-permute-start | bytes 3145736 | tf_op jit(solution)/shard_map/ppermute | solution.py:184
  95.4 13.3 %copy-start.3 = (bf16[64,14336]{1,0:T(8,128)(2,1)S(1)}, bf16[64,14336]{1,0:T(8,128)(2,1)}, u32[]{:S(2)}) copy-start(bf16[64,14336]{1,0:T(8,128)(2,1)} %copy-done.2) | copy-start | bytes 5505028
  95.4 22.6 %collective-permute-start.11 = (bf16[64,4096]{1,0:T(8,128)(2,1)S(1)}, bf16[64,4096]{1,0:T(8,128)(2,1)S(1)}, u32[]{:S(2)}, u32[]{:S(2)}) collective-permute-start(bf16[64,4096]{1,0:T(8,128)(2,1)S(1)} %slice.34), channel_id=1, source_target_pairs={{4,6},{6,4},{8,10},{10,8},{5,7},{7,5},{9,11},{11,9},{20,22},{22,20... | collective-permute-start | bytes 1572872 | tf_op jit(solution)/shard_map/ppermute | solution.py:184
  96.2 41.2 %collective-permute-start.8 = (bf16[64,14336]{1,0:T(8,128)(2,1)}, bf16[64,14336]{1,0:T(8,128)(2,1)S(1)}, u32[]{:S(2)}, u32[]{:S(2)}) collective-permute-start(bf16[64,14336]{1,0:T(8,128)(2,1)} %collective-permute-done.4.refs_1_.refs_4_), channel_id=1, source_target_pairs={{0,2},{2,0},{12,14},{14,12},{1,3},{3,1},{13,15},{15,13},{16,18},{1... | collective-permute-start | bytes 5505032 | tf_op jit(solution)/shard_map/ppermute | solution.py:184
  99.3 42.8 %collective-permute-start.7 = (bf16[64,14336]{1,0:T(8,128)(2,1)S(1)}, bf16[64,14336]{1,0:T(8,128)(2,1)S(1)}, u32[]{:S(2)}, u32[]{:S(2)}) collective-permute-start(bf16[64,14336]{1,0:T(8,128)(2,1)S(1)} %collective-permute-done.5.refs_2_), channel_id=1, source_target_pairs={{4,0},{6,2},{8,12},{10,14},{5,1},{7,3},{9,13},{11,15},{20,16},{22,... | collective-permute-start | bytes 5505032 | tf_op jit(solution)/shard_map/ppermute | solution.py:184
  100.6 43.9 %collective-permute-start.14 = (bf16[64,14336]{1,0:T(8,128)(2,1)}, bf16[64,14336]{1,0:T(8,128)(2,1)S(1)}, u32[]{:S(2)}, u32[]{:S(2)}) collective-permute-start(bf16[64,14336]{1,0:T(8,128)(2,1)} %collective-permute-done.refs_3_), channel_id=1, source_target_pairs={{0,4},{2,6},{12,8},{14,10},{1,5},{3,7},{13,9},{15,11},{16,20},{18,... | collective-permute-start | bytes 5505032 | tf_op jit(solution)/shard_map/ppermute | solution.py:184
  118.6 1.7 copy-start.5
  118.6 25.9 %collective-permute-start.13 = (bf16[512,1024]{1,0:T(8,128)(2,1)S(1)}, bf16[512,1024]{1,0:T(8,128)(2,1)S(1)}, u32[]{:S(2)}, u32[]{:S(2)}) collective-permute-start(bf16[512,1024]{1,0:T(8,128)(2,1)S(1)} %get-tuple-element.135), channel_id=1, source_target_pairs={{4,6},{6,4},{8,10},{10,8},{5,7},{7,5},{9,11},{11,9},{20,22},{22,20... | collective-permute-start | bytes 3145736 | tf_op jit(solution)/shard_map/ppermute | solution.py:184
  119.6 44.3 %collective-permute-start.16 = (bf16[64,10240]{1,0:T(8,128)(2,1)S(1)}, bf16[64,10240]{1,0:T(8,128)(2,1)S(1)}, u32[]{:S(2)}, u32[]{:S(2)}) collective-permute-start(bf16[64,10240]{1,0:T(8,128)(2,1)S(1)} %slice.37), channel_id=1, source_target_pairs={{4,6},{6,4},{8,10},{10,8},{5,7},{7,5},{9,11},{11,9},{20,22},{22,20... | collective-permute-start | bytes 3932168 | tf_op jit(solution)/shard_map/ppermute | solution.py:184
  142.1 12.2 %collective-permute-start.12 = (bf16[64,4096]{1,0:T(8,128)(2,1)S(1)}, bf16[64,4096]{1,0:T(8,128)(2,1)S(1)}, u32[]{:S(2)}, u32[]{:S(2)}) collective-permute-start(bf16[64,4096]{1,0:T(8,128)(2,1)S(1)} %slice.35), channel_id=1, source_target_pairs={{0,2},{2,0},{12,14},{14,12},{1,3},{3,1},{13,15},{15,13},{16,18},{1... | collective-permute-start | bytes 1572872 | tf_op jit(solution)/shard_map/ppermute | solution.py:184
  144.8 23.0 %collective-permute-start.18 = (bf16[512,1024]{1,0:T(8,128)(2,1)S(1)}, bf16[512,1024]{1,0:T(8,128)(2,1)S(1)}, u32[]{:S(2)}, u32[]{:S(2)}) collective-permute-start(bf16[512,1024]{1,0:T(8,128)(2,1)S(1)} %add_convert_fusion.1), channel_id=1, source_target_pairs={{4,0},{6,2},{8,12},{10,14},{5,1},{7,3},{9,13},{11,15},{20,16},{22,... | collective-permute-start | bytes 3145736 | tf_op jit(solution)/shard_map/ppermute | solution.py:184
  146.1 21.7 %collective-permute-start.17 = (bf16[512,1024]{1,0:T(8,128)(2,1)S(1)}, bf16[512,1024]{1,0:T(8,128)(2,1)S(1)}, u32[]{:S(2)}, u32[]{:S(2)}) collective-permute-start(bf16[512,1024]{1,0:T(8,128)(2,1)S(1)} %add_convert_fusion.1), channel_id=1, source_target_pairs={{4,8},{6,10},{8,4},{10,6},{5,9},{7,11},{9,5},{11,7},{20,24},{22,26... | collective-permute-start | bytes 3145736 | tf_op jit(solution)/shard_map/ppermute | solution.py:184
  154.3 11.2 %collective-permute-start.15 = (bf16[64,4096]{1,0:T(8,128)(2,1)S(1)}, bf16[64,4096]{1,0:T(8,128)(2,1)S(1)}, u32[]{:S(2)}, u32[]{:S(2)}) collective-permute-start(bf16[64,4096]{1,0:T(8,128)(2,1)S(1)} %slice.36), channel_id=1, source_target_pairs={{0,2},{2,0},{12,14},{14,12},{1,3},{3,1},{13,15},{15,13},{16,18},{1... | collective-permute-start | bytes 1572872 | tf_op jit(solution)/shard_map/ppermute | solution.py:184
  167.8 17.6 %collective-permute-start.21 = (f32[320,1792]{1,0:T(8,128)S(1)}, f32[320,1792]{1,0:T(8,128)S(1)}, u32[]{:S(2)}, u32[]{:S(2)}) collective-permute-start(f32[320,1792]{1,0:T(8,128)S(1)} %rotate.9), channel_id=1, source_target_pairs={{0,1},{1,0},{2,3},{3,2},{4,5},{5,4},{6,7},{7,6},{8,9},{9,8},{10,11... | collective-permute-start | bytes 6881288 | tf_op jit(solution)/shard_map/ppermute | solution.py:146
  167.8 33.1 %collective-permute-start.19 = (bf16[512,1024]{1,0:T(8,128)(2,1)S(1)}, bf16[512,1024]{1,0:T(8,128)(2,1)S(1)}, u32[]{:S(2)}, u32[]{:S(2)}) collective-permute-start(bf16[512,1024]{1,0:T(8,128)(2,1)S(1)} %collective-permute-done.17.refs_8_), channel_id=1, source_target_pairs={{4,0},{6,2},{8,12},{10,14},{5,1},{7,3},{9,13},{11,15},{20,16},{22,... | collective-permute-start | bytes 3145736 | tf_op jit(solution)/shard_map/ppermute | solution.py:184
  169.2 16.2 %collective-permute-start.20 = (bf16[64,4096]{1,0:T(8,128)(2,1)S(1)}, bf16[64,4096]{1,0:T(8,128)(2,1)S(1)}, u32[]{:S(2)}, u32[]{:S(2)}) collective-permute-start(bf16[64,4096]{1,0:T(8,128)(2,1)S(1)} %slice.38), channel_id=1, source_target_pairs={{0,2},{2,0},{12,14},{14,12},{1,3},{3,1},{13,15},{15,13},{16,18},{1... | collective-permute-start | bytes 1572872 | tf_op jit(solution)/shard_map/ppermute | solution.py:184
  185.4 10.8 %collective-permute-start.22 = (bf16[64,2048]{1,0:T(8,128)(2,1)S(1)}, bf16[64,2048]{1,0:T(8,128)(2,1)S(1)}, u32[]{:S(2)}, u32[]{:S(2)}) collective-permute-start(bf16[64,2048]{1,0:T(8,128)(2,1)S(1)} %slice.39), channel_id=1, source_target_pairs={{0,2},{2,0},{12,14},{14,12},{1,3},{3,1},{13,15},{15,13},{16,18},{1... | collective-permute-start | bytes 786440 | tf_op jit(solution)/shard_map/ppermute | solution.py:184
  201.0 3.2 %collective-permute-start.23 = (f32[192,1792]{1,0:T(8,128)S(1)}, f32[192,1792]{1,0:T(8,128)S(1)}, u32[]{:S(2)}, u32[]{:S(2)}) collective-permute-start(f32[192,1792]{1,0:T(8,128)S(1)} %rotate.13.refs_4_), channel_id=1, source_target_pairs={{0,1},{1,0},{2,3},{3,2},{4,5},{5,4},{6,7},{7,6},{8,9},{9,8},{10,11... | collective-permute-start | bytes 4128776 | tf_op jit(solution)/shard_map/ppermute | solution.py:146
  204.2 9.4 %copy-start.1 = (bf16[512,1024]{1,0:T(8,128)(2,1)S(1)}, bf16[512,1024]{1,0:T(8,128)(2,1)}, u32[]{:S(2)}) copy-start(bf16[512,1024]{1,0:T(8,128)(2,1)} %param.5) | copy-start | bytes 3145732
